TPU v7x, 32 devices: a whole 2x2x4 slice. The times are simulated.
32 devices in a mesh: group: 2 (over y), seq: 4 (over x, core), dom: 4 (over z).
Axes of the slice: x: 2, y: 2, z: 4, core: 2. Of those that a mesh axis runs over, the one named last changes fastest.
Arguments:
- q_nope: bfloat16 [32, 128, 128], P(('group', 'dom'), 'seq'), parts along dimension 0, may hold values from -6 to 6
- q_rope: bfloat16 [32, 128, 64], P(('group', 'dom'), 'seq'), parts along dimension 0, may hold values from -8 to 8
- w_uk: bfloat16 [128, 128, 512], P('seq'), may hold values from -0.5 to 0.5
- w_uv: bfloat16 [128, 512, 128], P('seq'), may hold values from -1.5 to 1.5
- prefix: bfloat16 [32768, 576], P(('group', 'seq')), parts along dimension 0, may hold values from -8 to 8
- private_caches: bfloat16 [32, 256, 576], P(('group', 'dom'), 'seq'), parts along dimension 0, may hold values from -8 to 8
- new_latent: bfloat16 [32, 576], P(('group', 'dom')), parts along dimension 0, may hold values from -6 to 6
- ancestors: int32 [32], P(('group', 'dom')), parts along dimension 0, may hold values from 0 to 15
- lengths: int32 [32], P('group'), parts along dimension 0, may hold values from 1 to 255
Outputs:
- head_values: bfloat16 [32, 128, 128], P(('group', 'dom'), 'seq'), parts along dimension 0
- new_caches: bfloat16 [32, 256, 576], P(('group', 'dom'), 'seq'), parts along dimension 0
There are 2 independent parts, one for each index of `group`. A program takes and returns all parts, laid end to end along the dimension named above; an argument that names none is the same for every part. Nothing has to cross between parts.
All inputs are finite; a program needn't handle non-finite values.
Results may differ from a plain program's by a relative error of at most 0.0085.
Values may be sent and summed in bfloat16 or wider, within the bound.
No kernel may reach another device: no remote copies, remote signals or barrier semaphores. Data moves between devices by JAX's collectives and lax.ppermute only.
A program may use at most 64 MiB of HBM per device.

v0:
```python
import jax
import jax.numpy as jnp
from jax import lax
from jax.sharding import PartitionSpec as P

ROPE = 64
NOPE = 128


masked_score = -1e30


def joined(part, axis, combine):
    gathered = jax.tree.map(lambda a: lax.all_gather(a, axis), part)

    def take(source):
        return jax.tree.map(lambda a: lax.dynamic_index_in_dim(a, source, 0, False), gathered)

    return lax.fori_loop(
        1, lax.axis_size(axis), lambda source, state: combine(state, take(source)), take(0)
    )


def merge_partials(left_part, right_part):
    left_max, left_sum, left_acc = left_part
    right_max, right_sum, right_acc = right_part
    largest = jnp.maximum(left_max, right_max)
    left_factor = jnp.exp(left_max - largest)
    right_factor = jnp.exp(right_max - largest)
    return (
        largest,
        left_sum * left_factor + right_sum * right_factor,
        left_acc * left_factor[..., None] + right_acc * right_factor[..., None],
    )


def on_device(q_nope, q_rope, w_uk, w_uv, prefix, private_caches, new_latent, ancestors, lengths):
    softmax_scale = (NOPE + ROPE) ** (-0.5)
    local_count = ancestors.shape[0]
    particle_total = lengths.shape[0]
    suffix_rows = private_caches.shape[1]
    latent_width = private_caches.shape[2]
    latent_rank = w_uv.shape[1]
    own_heads = w_uv.shape[0]
    seq_index = lax.axis_index("seq")
    portion = lax.all_gather(private_caches, "dom", axis=0, tiled=True)
    amount = portion.shape[0]
    picks = (ancestors[:, None] == jnp.arange(amount, dtype=jnp.int32)[None, :]).astype(
        jnp.bfloat16
    )
    gathered = jnp.dot(picks, portion.reshape(amount, -1), preferred_element_type=jnp.float32)
    migrated = gathered.astype(jnp.bfloat16).reshape(local_count, suffix_rows, latent_width)
    owners = ancestors[:, None] == jnp.arange(particle_total, dtype=jnp.int32)[None, :]
    new_lengths = jnp.sum(jnp.where(owners, lengths[None, :], 0), axis=1)
    positions = seq_index * suffix_rows + jnp.arange(suffix_rows, dtype=jnp.int32)
    writes = positions[None, :] == new_lengths[:, None]
    new_caches = jnp.where(writes[:, :, None], new_latent[:, None, :], migrated)
    query_latent = jnp.einsum(
        "phn,hnc->phc", q_nope, w_uk, preferred_element_type=jnp.float32
    ).astype(jnp.bfloat16)
    own_queries = jnp.concatenate([query_latent, q_rope], axis=2)
    all_queries = lax.all_gather(own_queries, "seq", axis=1, tiled=True)
    head_total = all_queries.shape[1]
    flat_queries = all_queries.reshape(local_count * head_total, latent_width)
    prefix_scores = (
        lax.dot_general(
            flat_queries, prefix, (((1,), (1,)), ((), ())), preferred_element_type=jnp.float32
        )
        * softmax_scale
    )
    prefix_max = jnp.max(prefix_scores, axis=1)
    prefix_weights = jnp.exp(prefix_scores - prefix_max[:, None])
    prefix_sum = jnp.sum(prefix_weights, axis=1)
    prefix_acc = jnp.dot(
        prefix_weights.astype(jnp.bfloat16),
        prefix[:, :latent_rank],
        preferred_element_type=jnp.float32,
    )
    prefix_part = (
        prefix_max.reshape(local_count, head_total),
        prefix_sum.reshape(local_count, head_total),
        prefix_acc.reshape(local_count, head_total, latent_rank),
    )
    suffix_scores = (
        jnp.einsum("phc,pkc->phk", all_queries, migrated, preferred_element_type=jnp.float32)
        * softmax_scale
    )
    visible = (positions[None, :] < new_lengths[:, None])[:, None, :]
    masked = jnp.where(visible, suffix_scores, masked_score)
    suffix_max = jnp.max(masked, axis=2)
    suffix_weights = jnp.where(visible, jnp.exp(masked - suffix_max[:, :, None]), 0.0)
    suffix_sum = jnp.sum(suffix_weights, axis=2)
    suffix_acc = jnp.einsum(
        "phk,pkc->phc",
        suffix_weights.astype(jnp.bfloat16),
        migrated[:, :, :latent_rank],
        preferred_element_type=jnp.float32,
    )
    local_part = merge_partials(prefix_part, (suffix_max, suffix_sum, suffix_acc))
    merged = joined(local_part, "seq", merge_partials)
    first_head = seq_index * own_heads
    denominator = lax.dynamic_slice_in_dim(merged[1], first_head, own_heads, 1)
    numerator = lax.dynamic_slice_in_dim(merged[2], first_head, own_heads, 1)
    latent_out = (numerator / denominator[:, :, None]).astype(jnp.bfloat16)
    head_values = jnp.einsum(
        "phc,hcv->phv", latent_out, w_uv, preferred_element_type=jnp.float32
    ).astype(jnp.bfloat16)
    return (head_values, new_caches)


def solution(mesh):
    placed = (
        P(("group", "dom"), "seq", None),
        P(("group", "dom"), "seq", None),
        P("seq", None, None),
        P("seq", None, None),
        P(("group", "seq"), None),
        P(("group", "dom"), "seq", None),
        P(("group", "dom"), None),
        P(("group", "dom")),
        P("group"),
    )
    return jax.shard_map(
        on_device,
        mesh=mesh,
        in_specs=placed,
        out_specs=(P(("group", "dom"), "seq", None), P(("group", "dom"), "seq", None)),
        check_vma=False,
    )
```

profile of v0, /device:TPU:0, one launch (start us, length us, event | category | flops | bytes accessed | tf_op | source)
XLA Modules:
  0.0 100.6 jit_solution(9597892583069278316)
XLA Ops:
  7.2 0.7 all-gather.4.cloned.1.call-update
  8.0 0.8 copy.29
  8.8 2.8 %fusion.12 = bf16[4,32,512]{2,0,1:T(4,128)(2,1)S(1)} fusion(bf16[32,128,512]{2,1,0:T(8,128)(2,1)} %param.13, bf16[4,32,128]{2,1,0:T(8,128)(2,1)S(1)} %copy-done), kind=kOutput, calls=%fused_computation.22 | convolution fusion | flops 16842752 | bytes 4358144 | tf_op jit(solution)/shard_map/phn,hnc->phc/dot_general | solution.py:58
  11.7 9.3 %all_gather.20 = bf16[4,128,576]{2,0,1:T(4,128)(2,1)S(1)} all-gather(bf16[4,32,576]{2,0,1:T(4,128)(2,1)S(1)} %pad_maximum_fusion), channel_id=1, replica_groups=mesh['group'=2,'seq'=4,'dom'=4] {'seq'}, dimensions={1}, use_global_device_ids=true | all-gather | bytes 737280 | tf_op jit(solution)/shard_map/all_gather | solution.py:62
  21.0 0.9 copy.30
  22.3 5.7 %multiply_reduce_fusion = (f32[512]{0:T(512)S(1)}, f32[512,4096]{1,0:T(8,128)S(1)}) fusion(bf16[4096,576]{0,1:T(8,128)(2,1)} %param.15, bf16[72,8,4,128]{3,2,1,0:T(4,128)(2,1)S(1)} %bitcast.74), kind=kOutput, calls=%fused_computation.10 | convolution fusion | flops 2420112896 | bytes 13699072 | tf_op jit(solution)/shard_map/dot_general | solution.py:66
  28.0 3.2 %copy-done.1 = f32[512,4096]{1,0:T(8,128)} copy-done((f32[512,4096]{1,0:T(8,128)}, f32[512,4096]{1,0:T(8,128)S(1)}, u32[]{:S(2)}) %copy-start.1) | copy-done | bytes 8388632
  31.2 2.5 %fusion.5 = f32[512,512]{1,0:T(8,128)S(1)} fusion(f32[512,4096]{1,0:T(8,128)S(1)} %get-tuple-element.216, bf16[4096,576]{0,1:T(8,128)(2,1)S(1)} %bitcast.73, f32[512]{0:T(512)S(1)} %get-tuple-element.215), kind=kOutput, calls=%fused_computation.13 | convolution fusion | flops 2153775104 | bytes 13633536 | tf_op jit(solution)/shard_map/dot_general | solution.py:74
  33.7 11.3 %all-gather.4.cloned.1.call-done = bf16[16,64,576]{2,1,0:T(8,128)(2,1)} async-done(((bf16[4,64,576]{2,1,0:T(8,128)(2,1)}), bf16[16,64,576]{2,1,0:T(8,128)(2,1)}) %all-gather.4.cloned.1.call-update) | async-done | bytes 1179664 | tf_op jit(solution)/shard_map/all_gather | solution.py:46
  45.0 2.7 %reshape.166 = bf16[16,36864]{1,0:T(8,128)(2,1)S(1)} reshape(bf16[16,64,576]{2,1,0:T(8,128)(2,1)} %all-gather.4.cloned.1.call-done) | data formatting | bytes 2359296 | tf_op jit(solution)/shard_map/reshape | solution.py:51
  48.5 0.4 fusion.36
  48.9 1.5 %fusion.10 = f32[4,128,512]{2,1,0:T(8,128)} fusion(f32[4,128,512]{2,1,0:T(8,128)S(1)} %bitcast.75, f32[4,128]{1,0:T(4,128)S(1)} %get-tuple-element.208, f32[4,128]{1,0:T(4,128)S(1)} %get-tuple-element.207, bf16[4,64,576]{2,1,0:T(8,128)(2,1)S(1)} %reshape.167, f32[4,128,64]{1,2,0:T(8,128)S(1)} %get-tuple-element.214, f32[4,128]{1,0:T(4,128)S(1)} %get-tuple-element.213, ...), kind=kOutput, calls=%fused_computation.18 | convolution fusion | flops 34439168 | bytes 2497024 | tf_op jit(solution)/shard_map/phk,pkc->phc/dot_general | solution.py:93
  50.4 4.9 %fusion.4 = f32[512]{0:T(512)S(1)} fusion(f32[512,4096]{1,0:T(8,128)} %copy-done.1, f32[512]{0:T(512)S(1)} %get-tuple-element.215), kind=kLoop, calls=%fused_computation.12 | loop fusion | flops 6290944 | bytes 8392704 | tf_op jit(solution)/shard_map/reduce_sum | solution.py:73
  55.4 5.2 %all_gather.22 = f32[4,4,128]{2,1,0:T(4,128)S(1)} all-gather(f32[1,4,128]{2,1,0:T(4,128)S(1)} %get-tuple-element.210), channel_id=1, replica_groups=mesh['group'=2,'seq'=4,'dom'=4] {'seq'}, dimensions={0}, use_global_device_ids=true | all-gather | bytes 10240 | tf_op jit(solution)/shard_map/all_gather | solution.py:14
  60.6 5.2 %all_gather.23 = f32[4,4,128]{2,1,0:T(4,128)S(1)} all-gather(f32[1,4,128]{2,1,0:T(4,128)S(1)} %get-tuple-element.209), channel_id=1, replica_groups=mesh['group'=2,'seq'=4,'dom'=4] {'seq'}, dimensions={0}, use_global_device_ids=true | all-gather | bytes 10240 | tf_op jit(solution)/shard_map/all_gather | solution.py:14
  65.8 0.8 broadcast_select_fusion
  66.6 17.5 %all-gather.6.cloned.1.call-done = f32[16,128,512]{2,1,0:T(8,128)} async-done(((f32[4,128,512]{2,1,0:T(8,128)}), f32[16,128,512]{2,1,0:T(8,128)}) %all-gather.6.cloned.1.call-update) | async-done | bytes 4194320 | tf_op jit(solution)/shard_map/all_gather | solution.py:14
  84.1 1.3 %slice.13 = f32[4,128,512]{2,1,0:T(8,128)S(1)} slice(f32[16,128,512]{2,1,0:T(8,128)} %all-gather.6.cloned.1.call-done), slice={[0:4], [0:128], [0:512]} | slice | bytes 2097152 | tf_op jit(solution)/shard_map/jit(dynamic_index_in_dim)/dynamic_slice | solution.py:17
  85.4 4.7 %while.19 = (s32[]{:T(128)}, f32[4,128]{1,0:T(4,128)S(1)}, f32[4,128]{1,0:T(4,128)S(1)}, f32[4,128,512]{2,1,0:T(8,128)S(1)}, f32[4,4,128]{2,1,0:T(4,128)S(1)}, /...) while((s32[]{:T(128)}, f32[4,128]{1,0:T(4,128)S(1)}, ...), condition=%wide.region_6.7_spmd, body=%wide.region_5.6_spmd.sunk | while | flops 789509 | bytes 3166359 | solution.py:19
  85.4 1.5 %fusion.45 = f32[4,128,512]{2,1,0:T(8,128)S(1)} fusion(f32[4,4,128,512]{3,2,1,0:T(8,128)} %get-tuple-element.294, s32[]{:T(128)S(6)} %select_n.51, f32[4,128,512]{2,1,0:T(8,128)S(1)} %get-tuple-element.281, f32[4,128]{1,0:T(4,128)S(1)} %get-tuple-element.266, f32[4,128]{1,0:T(4,128)S(1)} %get-tuple-element.267), kind=kLoop, calls=%fused_computation.1.clone.1 | loop fusion | flops 786432 | bytes 3149828 | tf_op jit(solution)/shard_map/while/body/eval_jaxpr/add | solution.py:33
  87.0 1.5 %fusion.45 = f32[4,128,512]{2,1,0:T(8,128)S(1)} fusion(f32[4,4,128,512]{3,2,1,0:T(8,128)} %get-tuple-element.294, s32[]{:T(128)S(6)} %select_n.51, f32[4,128,512]{2,1,0:T(8,128)S(1)} %get-tuple-element.281, f32[4,128]{1,0:T(4,128)S(1)} %get-tuple-element.266, f32[4,128]{1,0:T(4,128)S(1)} %get-tuple-element.267), kind=kLoop, calls=%fused_computation.1.clone.1 | loop fusion | flops 786432 | bytes 3149828 | tf_op jit(solution)/shard_map/while/body/eval_jaxpr/add | solution.py:33
  88.6 1.5 %fusion.45 = f32[4,128,512]{2,1,0:T(8,128)S(1)} fusion(f32[4,4,128,512]{3,2,1,0:T(8,128)} %get-tuple-element.294, s32[]{:T(128)S(6)} %select_n.51, f32[4,128,512]{2,1,0:T(8,128)S(1)} %get-tuple-element.281, f32[4,128]{1,0:T(4,128)S(1)} %get-tuple-element.266, f32[4,128]{1,0:T(4,128)S(1)} %get-tuple-element.267), kind=kLoop, calls=%fused_computation.1.clone.1 | loop fusion | flops 786432 | bytes 3149828 | tf_op jit(solution)/shard_map/while/body/eval_jaxpr/add | solution.py:33
  90.3 2.8 %fusion.13 = bf16[4,32,128]{2,0,1:T(4,128)(2,1)S(1)} fusion(bf16[32,512,128]{2,1,0:T(8,128)(2,1)} %param.14, bf16[4,32,512]{2,1,0:T(8,128)(2,1)S(1)} %divide_convert_fusion), kind=kOutput, calls=%fused_computation.24 | convolution fusion | flops 16793600 | bytes 4358144 | tf_op jit(solution)/shard_map/phc,hcv->phv/dot_general | solution.py:105
  93.1 0.6 copy.33
  (33 shorter events, 1.6 us)
Async XLA Ops:
  7.2 1.6 %copy-start = (bf16[4,32,128]{2,1,0:T(8,128)(2,1)S(1)}, bf16[4,32,128]{2,1,0:T(8,128)(2,1)}, u32[]{:S(2)}) copy-start(bf16[4,32,128]{2,1,0:T(8,128)(2,1)} %param.11) | copy-start | bytes 98308
  7.2 14.8 %copy-start.3 = (s32[4]{0:T(128)S(1)}, s32[4]{0:T(128)}, u32[]{:S(2)}) copy-start(s32[4]{0:T(128)} %param.18) | copy-start | bytes 52
  7.2 14.8 %copy-start.4 = (s32[16]{0:T(128)S(1)}, s32[16]{0:T(128)}, u32[]{:S(2)}) copy-start(s32[16]{0:T(128)} %param.19) | copy-start | bytes 196
  7.2 37.8 %all-gather.4.cloned.1.call-start = ((), (), s32[]{:S(2)}) async-start(), calls=%async_computation | async-start | bytes 1638400 | tf_op jit(solution)/shard_map/all_gather | solution.py:46
  7.9 76.1 %all-gather.6.cloned.1.call-start = ((), (), s32[]{:S(2)}) async-start(), calls=%async_computation.1 | async-start | bytes 5242880 | tf_op jit(solution)/shard_map/all_gather | solution.py:14
  21.0 10.2 %slice-start = ((s8[4718592]{0:T(1024)(128)(4,1)}), s8[524288]{0:T(1024)(128)(4,1)S(1)}, s32[]{:S(2)}) async-start(s8[4718592]{0:T(1024)(128)(4,1)} %bitcast.72), calls=%async_computation.2 | async-start | bytes 1048576
  22.3 9.0 %slice-start.1 = ((s8[4718592]{0:T(1024)(128)(4,1)}), s8[4194304]{0:T(1024)(128)(4,1)S(1)}, s32[]{:S(2)}) async-start(s8[4718592]{0:T(1024)(128)(4,1)} %bitcast.72), calls=%async_computation.3 | async-start | bytes 8388608
  28.0 3.2 %copy-start.1 = (f32[512,4096]{1,0:T(8,128)}, f32[512,4096]{1,0:T(8,128)S(1)}, u32[]{:S(2)}) copy-start(f32[512,4096]{1,0:T(8,128)S(1)} %get-tuple-element.216) | copy-start | bytes 25165828
  50.4 15.4 %copy-start.2 = (bf16[4,576]{1,0:T(4,128)(2,1)S(1)}, bf16[4,576]{1,0:T(4,128)(2,1)}, u32[]{:S(2)}) copy-start(bf16[4,576]{1,0:T(4,128)(2,1)} %param.17) | copy-start | bytes 13828
Sparse Core Ops, SparseCore 0:
  9.6 35.3 all-gather.3
  50.5 33.5 all-gather.5
where the time goes:
time: 101 us
  waiting for transfers between devices  29.5 us (29%)
  blocking collectives  19.7 us (20%)
  matrix products  16.1 us (16%)
  between operations  14.2 us (14%)
  other arithmetic  11 us (11%)
  local copies, waits for them, and re-layouts  10 us (10%)
    all_gather x1, waiting for transfers between devices, joined(): gathered = jax.tree.map(lambda a: lax.all_gather(a, axis), part)  17.5 us
    all_gather x1, waiting for transfers between devices, on_device(): portion = lax.all_gather(private_caches, 'dom', axis=0, tiled=True)  11.3 us
    all_gather x2, blocking collectives, joined(): gathered = jax.tree.map(lambda a: lax.all_gather(a, axis), part)  10.3 us
    all_gather x1, blocking collectives, on_device(): all_queries = lax.all_gather(own_queries, 'seq', axis=1, tiled=True)  9.33 us
    dot_general x1, matrix products, on_device(): lax.dot_general(flat_queries, prefix, (((1,), (1,)), ((), ())), preferred...  5.71 us
    reduce_sum x1, other arithmetic, on_device(): prefix_sum = jnp.sum(prefix_weights, axis=1)  4.88 us
    unnamed x16, local copies, waits for them, and re-layouts  4.67 us
    add x3, other arithmetic, merge_partials(): left_acc * left_factor[..., None] + right_acc * right_factor[..., None]  4.56 us
  transfers between devices with their start and end apart: 2, of which 2 were waited for; matrix products, arithmetic and copies ran while one was open for 19% of the time, Pallas kernels for 0%

commit v1 on v0

v1 whole, which is shorter than its diff:
```python
import functools
import math

import jax
import jax.numpy as jnp
from jax import lax
from jax.experimental import pallas as pl
from jax.experimental.pallas import tpu as pltpu
from jax.sharding import PartitionSpec as P

ROPE = 64
NOPE = 128
SCALE2 = (NOPE + ROPE) ** (-0.5) * math.log2(math.e)
HIDDEN = -1e30
LANES = 128
F32 = jnp.float32
BF16 = jnp.bfloat16
NT = (((1,), (1,)), ((), ()))

VMEM = pl.BlockSpec(memory_space=pltpu.VMEM)
SMEM = pl.BlockSpec(memory_space=pltpu.SMEM)
ANY = pl.BlockSpec(memory_space=pl.ANY)
PARAMS = pltpu.CompilerParams(vmem_limit_bytes=40 * 1024 * 1024)


def prefix_kernel(count, *refs):
    query_refs = refs[:count]
    prefix_hbm, acc_ref, max_ref, sum_ref, keys, sems = refs[count:]
    tiles, tile = keys.shape[0], keys.shape[1]
    rank = acc_ref.shape[1]

    def fetch(i):
        return pltpu.make_async_copy(
            prefix_hbm.at[pl.ds(i * tile, tile)], keys.at[i], sems.at[i]
        )

    for i in range(tiles):
        fetch(i).start()
    queries = jnp.concatenate([ref[...] for ref in query_refs], axis=0)
    for i in range(tiles):
        fetch(i).wait()
        scores = lax.dot_general(queries, keys[i], NT, preferred_element_type=F32) * SCALE2
        top = jnp.max(scores, axis=1, keepdims=True)
        if i > 0:
            top = jnp.maximum(top, largest)
        weights = jnp.exp2(scores - top)
        total = jnp.sum(weights, axis=1, keepdims=True)
        acc = jnp.dot(weights.astype(BF16), keys[i, :, :rank], preferred_element_type=F32)
        if i > 0:
            factor = jnp.exp2(largest - top)
            total = total + running * factor
            acc = acc + acc_ref[...] * factor
        largest, running = top, total
        acc_ref[...] = acc
    max_ref[...] = jnp.broadcast_to(largest, max_ref.shape)
    sum_ref[...] = jnp.broadcast_to(running, sum_ref.shape)


def prefix_attention(queries, prefix, rank, tiles=4):
    rows = sum(q.shape[0] for q in queries)
    tile = prefix.shape[0] // tiles
    stat = jax.ShapeDtypeStruct((rows, LANES), F32)
    return pl.pallas_call(
        functools.partial(prefix_kernel, len(queries)),
        out_shape=(jax.ShapeDtypeStruct((rows, rank), F32), stat, stat),
        in_specs=[VMEM] * len(queries) + [ANY],
        out_specs=(VMEM,) * 3,
        scratch_shapes=[
            pltpu.VMEM((tiles, tile, prefix.shape[1]), BF16),
            pltpu.SemaphoreType.DMA((tiles,)),
        ],
        compiler_params=PARAMS,
        name="prefix_attention",
    )(*queries, prefix)


def suffix_kernel(count, offsets, heads, *refs):
    anc, lens, place, fresh_ref = refs[:4]
    refs = refs[4:]
    query_refs, refs = refs[:count], refs[count:]
    stage_refs, refs = refs[: 3 * (count // 2)], refs[3 * (count // 2) :]
    block_refs, refs = refs[: len(offsets)], refs[len(offsets) :]
    cache_ref, refs = refs[0], refs[1:]
    out_refs, (moved, sems) = refs[:count], refs[count:]
    local, span, width = moved.shape
    rank = stage_refs[0].shape[1]

    for p in range(local):
        owner = lax.div(anc[p], local)
        slot = lax.rem(anc[p], local)
        for k, offset in enumerate(offsets):

            @pl.when(owner == place[1] + offset)
            def _():
                pltpu.make_async_copy(block_refs[k].at[slot], moved.at[p], sems.at[p]).start()

    for p in range(local):
        pltpu.make_async_copy(block_refs[0].at[0], moved.at[p], sems.at[p]).wait()

    start = place[0] * span
    ends = [lens[anc[p]] for p in range(local)]
    row_at = start + lax.broadcasted_iota(jnp.int32, (span, width), 0)
    for p in range(local):
        cache_ref[p] = jnp.where(row_at == ends[p], fresh_ref[pl.ds(p, 1), :], moved[p])

    keys = moved[...].reshape(local * span, width)
    half = 2 * heads * local
    shape = (half, local * span)
    row = lax.broadcasted_iota(jnp.int32, shape, 0)
    col = lax.broadcasted_iota(jnp.int32, shape, 1)
    row_of = lax.rem(lax.div(row, heads), local)
    at = start + lax.rem(col, span)
    col_of = lax.div(col, span)
    seen = jnp.zeros(shape, jnp.bool_)
    for p in range(local):
        seen = seen | ((row_of == p) & (col_of == p) & (at < ends[p]))
    lane = lax.broadcasted_iota(jnp.int32, (half, LANES), 1)
    for k in range(count // 2):
        queries = jnp.concatenate([query_refs[2 * k][...], query_refs[2 * k + 1][...]], axis=0)
        acc_ref, max_ref, sum_ref = stage_refs[3 * k : 3 * k + 3]
        scores = lax.dot_general(queries, keys, NT, preferred_element_type=F32) * SCALE2
        scores = jnp.where(seen, scores, HIDDEN)
        before = max_ref[:, 0:1]
        top = jnp.maximum(before, jnp.max(scores, axis=1, keepdims=True))
        weights = jnp.where(seen, jnp.exp2(scores - top), 0.0)
        factor = jnp.exp2(before - top)
        total = sum_ref[:, 0:1] * factor + jnp.sum(weights, axis=1, keepdims=True)
        acc = acc_ref[...] * factor + jnp.dot(
            weights.astype(BF16), keys[:, :rank], preferred_element_type=F32
        )
        level = top + jnp.log2(total)
        high = level.astype(BF16).astype(F32)
        middle = (level - high).astype(BF16).astype(F32)
        low = level - high - middle
        stats = jnp.where(lane == 0, high, jnp.where(lane == 1, middle, jnp.where(lane == 2, low, 0.0)))
        part = jnp.concatenate([(acc / total).astype(BF16), stats.astype(BF16)], axis=1)
        out_refs[2 * k][...] = part[: half // 2]
        out_refs[2 * k + 1][...] = part[half // 2 :]


def merge_kernel(count, *refs):
    part_refs, out_ref = refs[:count], refs[count]
    rank = out_ref.shape[1]
    levels = [jnp.sum(ref[:, rank:].astype(F32), axis=1, keepdims=True) for ref in part_refs]
    top = functools.reduce(jnp.maximum, levels)
    shares = [jnp.exp2(level - top) for level in levels]
    whole = functools.reduce(jnp.add, shares)
    acc = functools.reduce(
        jnp.add, [share * ref[:, :rank].astype(F32) for share, ref in zip(shares, part_refs)]
    )
    out_ref[...] = (acc / whole).astype(BF16)


def on_device(q_nope, q_rope, w_uk, w_uv, prefix, private_caches, new_latent, ancestors, lengths):
    local, heads = q_nope.shape[:2]
    span, width = private_caches.shape[1:]
    rank = w_uv.shape[1]
    seq_size, dom_size = lax.axis_size("seq"), lax.axis_size("dom")
    cores = 2 if seq_size % 2 == 0 else 1
    chips = seq_size // cores
    place = jnp.stack([lax.axis_index("seq"), lax.axis_index("dom")]).astype(jnp.int32)

    offsets, blocks = [0], [private_caches]
    left = right = private_caches
    for k in range(1, dom_size):
        right = lax.ppermute(right, "dom", [(i, i + 1) for i in range(k - 1, dom_size - 1)])
        left = lax.ppermute(left, "dom", [(i, i - 1) for i in range(1, dom_size - k + 1)])
        offsets += [-k, k]
        blocks += [right, left]

    query_latent = jnp.einsum("phn,hnc->phc", q_nope, w_uk, preferred_element_type=F32).astype(BF16)
    own = jnp.concatenate([query_latent, q_rope], axis=2).reshape(local * heads, width)

    def pairs(turn, flip):
        return [
            (x * cores + c, (x + turn) % chips * cores + (c ^ flip))
            for x in range(chips)
            for c in range(cores)
        ]

    routes = [(t, f) for t in range(chips) for f in range(cores)]
    queries = [own if r == (0, 0) else lax.ppermute(own, "seq", pairs(*r)) for r in routes]
    stages = []
    for k in range(0, len(routes), 2):
        stages += prefix_attention(queries[k : k + 2], prefix, rank)

    count = len(routes)
    rows = local * heads
    results = pl.pallas_call(
        functools.partial(suffix_kernel, count, tuple(offsets), heads),
        out_shape=(jax.ShapeDtypeStruct(private_caches.shape, BF16),)
        + (jax.ShapeDtypeStruct((rows, rank + LANES), BF16),) * count,
        in_specs=[SMEM] * 3 + [VMEM] * (1 + count + len(stages)) + [ANY] * len(blocks),
        out_specs=(VMEM,) * (1 + count),
        scratch_shapes=[
            pltpu.VMEM((local, span, width), BF16),
            pltpu.SemaphoreType.DMA((local,)),
        ],
        compiler_params=PARAMS,
        name="suffix_attention",
    )(ancestors, lengths, place, new_latent, *queries, *stages, *blocks)
    new_caches, parts = results[0], results[1:]

    parts = [
        part if r == (0, 0) else lax.ppermute(part, "seq", [(b, a) for a, b in pairs(*r)])
        for r, part in zip(routes, parts)
    ]
    latent_out = pl.pallas_call(
        functools.partial(merge_kernel, count),
        out_shape=jax.ShapeDtypeStruct((rows, rank), BF16),
        in_specs=[VMEM] * count,
        out_specs=VMEM,
        compiler_params=PARAMS,
        name="merge",
    )(*parts)
    head_values = jnp.einsum(
        "phc,hcv->phv", latent_out.reshape(local, heads, rank), w_uv, preferred_element_type=F32
    ).astype(BF16)
    return (head_values, new_caches)


def solution(mesh):
    placed = (
        P(("group", "dom"), "seq", None),
        P(("group", "dom"), "seq", None),
        P("seq", None, None),
        P("seq", None, None),
        P(("group", "seq"), None),
        P(("group", "dom"), "seq", None),
        P(("group", "dom"), None),
        P(("group", "dom")),
        P("group"),
    )
    return jax.shard_map(
        on_device,
        mesh=mesh,
        in_specs=placed,
        out_specs=(P(("group", "dom"), "seq", None), P(("group", "dom"), "seq", None)),
        check_vma=False,
    )
```

time: 101 us -> 68.5 us (0.68)
  blocking collectives: 19.7 us -> 0 us
  starting transfers between devices: 0.08 us -> 14.4 us
  between operations: 14.2 us -> 0.88 us
  Pallas kernels: 0 us -> 13.1 us
  matrix products: 16.1 us -> 3.49 us
  other arithmetic: 11 us -> 0.16 us
  waiting for transfers between devices: 29.5 us -> 24.9 us
    all_gather x2 -> x0, waiting for transfers between devices: 28.8 us -> none  [the longest x1 17.5 us: joined(): gathered = jax.tree.map(lambda a: lax.all_gather(a, axis), part)]
    ppermute x0 -> x12, waiting for transfers between devices: none -> 24.9 us  [the longest x3 11.7 us: on_device(): lax.ppermute(left, 'dom', [(i, i - 1) for i in range(1, dom_size - k + 1)])]
    all_gather x3 -> x0, blocking collectives: 19.7 us -> none  [the longest x2 10.3 us: joined(): gathered = jax.tree.map(lambda a: lax.all_gather(a, axis), part)]
    ppermute x0 -> x12, starting transfers between devices: none -> 14.4 us  [the longest x3 6.43 us: on_device(): lax.ppermute(right, 'dom', [(i, i + 1) for i in range(k - 1, dom_size - 1)])]
    pallas_call x0 -> x4, Pallas kernels: none -> 13.1 us  [the longest x2 9.8 us: prefix_attention(): pl.pallas_call(functools.partial(prefix_kernel, len(queries)), out_shape=...]
    dot_general x7 -> x2, matrix products: 16.1 us -> 3.49 us  [the longest x1 2.83 us: on_device(): jnp.einsum('phn,hnc->phc', q_nope, w_uk, preferred_element_type=F32)]
    unnamed x16 -> x21, local copies, waits for them, and re-layouts: 4.67 us -> 10.8 us
    reduce_sum x3 -> x0, other arithmetic: 5.18 us -> none  [the longest x1 4.88 us: on_device(): prefix_sum = jnp.sum(prefix_weights, axis=1)]
  transfers between devices with their start and end apart: 2 -> 12, of which waited for: 2 -> 5; matrix products, arithmetic and copies ran while one was open for 19% -> 16% of each run, Pallas kernels for 0% -> 14%
where the time goes in v1:
time: 68.5 us; the launch traced here: 67.8 us
  waiting for transfers between devices  24.9 us (36%)
  starting transfers between devices  14.4 us (21%)
  Pallas kernels  13.1 us (19%)
  local copies, waits for them, and re-layouts  10.8 us (16%)
  matrix products  3.49 us (5%)
  between operations  0.88 us (1%)
    ppermute x3, waiting for transfers between devices, on_device(): lax.ppermute(left, 'dom', [(i, i - 1) for i in range(1, dom_size - k + 1)])  11.7 us
    unnamed x21, local copies, waits for them, and re-layouts  10.8 us
    pallas_call x2, Pallas kernels, prefix_attention(): pl.pallas_call(functools.partial(prefix_kernel, len(queries)), out_shape=...  9.8 us
    ppermute x3, waiting for transfers between devices, on_device(): lax.ppermute(part, 'seq', [(b, a) for a, b in pairs(*r)])  7.25 us
    ppermute x3, starting transfers between devices, on_device(): lax.ppermute(right, 'dom', [(i, i + 1) for i in range(k - 1, dom_size - 1)])  6.43 us
    ppermute x3, waiting for transfers between devices, on_device(): lax.ppermute(right, 'dom', [(i, i + 1) for i in range(k - 1, dom_size - 1)])  5.95 us
    ppermute x3, starting transfers between devices, on_device(): lax.ppermute(left, 'dom', [(i, i - 1) for i in range(1, dom_size - k + 1)])  3.85 us
    pallas_call x1, Pallas kernels, on_device(): pl.pallas_call(functools.partial(suffix_kernel, count, tuple(offsets), he...  3.04 us
  transfers between devices with their start and end apart: 12, of which 5 were waited for; matrix products, arithmetic and copies ran while one was open for 16% of the time, Pallas kernels for 14%

profile of v1, /device:TPU:0, one launch (start us, length us, event | category | flops | bytes accessed | tf_op | source)
XLA Modules:
  0.0 67.8 jit_solution(352455248448891557)
XLA Ops:
  0.7 5.1 %collective-permute-start.3 = (bf16[4,64,576]{2,1,0:T(8,128)(2,1)}, bf16[4,64,576]{2,1,0:T(8,128)(2,1)S(1)}, u32[]{:S(2)}, u32[]{:S(2)}) collective-permute-start(bf16[4,64,576]{2,1,0:T(8,128)(2,1)} %refs_14_.1), channel_id=1, source_target_pairs={{0,1},{1,2},{2,3},{4,5},{5,6},{6,7},{8,9},{9,10},{10,11},{12,13},{... | collective-permute-start | bytes 884744 | tf_op jit(solution)/shard_map/ppermute | solution.py:166
  5.7 1.3 %collective-permute-start.4 = (bf16[4,64,576]{2,1,0:T(8,128)(2,1)}, bf16[4,64,576]{2,1,0:T(8,128)(2,1)S(1)}, u32[]{:S(2)}, u32[]{:S(2)}) collective-permute-start(bf16[4,64,576]{2,1,0:T(8,128)(2,1)} %refs_14_.1), channel_id=1, source_target_pairs={{1,0},{2,1},{3,2},{5,4},{6,5},{7,6},{9,8},{10,9},{11,10},{13,12},{... | collective-permute-start | bytes 884744 | tf_op jit(solution)/shard_map/ppermute | solution.py:167
  7.0 5.9 %collective-permute-done.3.refs_15_ = bf16[4,64,576]{2,1,0:T(8,128)(2,1)S(1)} collective-permute-done((bf16[4,64,576]{2,1,0:T(8,128)(2,1)}, bf16[4,64,576]{2,1,0:T(8,128)(2,1)S(1)}, u32[]{:S(2)}, u32[]{:S(2)}) %collective-permute-start.3) | collective-permute-done | bytes 294944 | tf_op jit(solution)/shard_map/ppermute | solution.py:166
  13.0 0.7 collective-permute-start.5
  13.7 3.4 %collective-permute-done.4.refs_16_ = bf16[4,64,576]{2,1,0:T(8,128)(2,1)S(1)} collective-permute-done((bf16[4,64,576]{2,1,0:T(8,128)(2,1)}, bf16[4,64,576]{2,1,0:T(8,128)(2,1)S(1)}, u32[]{:S(2)}, u32[]{:S(2)}) %collective-permute-start.4) | collective-permute-done | bytes 294944 | tf_op jit(solution)/shard_map/ppermute | solution.py:167
  17.0 1.3 %collective-permute-start.6 = (bf16[4,64,576]{2,1,0:T(8,128)(2,1)S(1)}, bf16[4,64,576]{2,1,0:T(8,128)(2,1)S(1)}, u32[]{:S(2)}, u32[]{:S(2)}) collective-permute-start(bf16[4,64,576]{2,1,0:T(8,128)(2,1)S(1)} %collective-permute-done.4.refs_16_), channel_id=1, source_target_pairs={{1,0},{2,1},{5,4},{6,5},{9,8},{10,9},{13,12},{14,13},{17,16},{18,1... | collective-permute-start | bytes 884744 | tf_op jit(solution)/shard_map/ppermute | solution.py:167
  18.3 0.7 %collective-permute-start.7 = (bf16[4,64,576]{2,1,0:T(8,128)(2,1)S(1)}, bf16[4,64,576]{2,1,0:T(8,128)(2,1)S(1)}, u32[]{:S(2)}, u32[]{:S(2)}) collective-permute-start(bf16[4,64,576]{2,1,0:T(8,128)(2,1)S(1)} %collective-permute-done.5.refs_17_), channel_id=1, source_target_pairs={{2,3},{6,7},{10,11},{14,15},{18,19},{22,23},{26,27},{30,31}} | collective-permute-start | bytes 884744 | tf_op jit(solution)/shard_map/ppermute | solution.py:166
  19.0 8.3 %collective-permute-done.6.refs_18_ = bf16[4,64,576]{2,1,0:T(8,128)(2,1)S(1)} collective-permute-done((bf16[4,64,576]{2,1,0:T(8,128)(2,1)S(1)}, bf16[4,64,576]{2,1,0:T(8,128)(2,1)S(1)}, u32[]{:S(2)}, u32[]{:S(2)}) %collective-permute-start.6) | collective-permute-done | bytes 294944 | tf_op jit(solution)/shard_map/ppermute | solution.py:167
  27.3 1.3 %collective-permute-start.8 = (bf16[4,64,576]{2,1,0:T(8,128)(2,1)S(1)}, bf16[4,64,576]{2,1,0:T(8,128)(2,1)S(1)}, u32[]{:S(2)}, u32[]{:S(2)}) collective-permute-start(bf16[4,64,576]{2,1,0:T(8,128)(2,1)S(1)} %collective-permute-done.6.refs_18_), channel_id=1, source_target_pairs={{1,0},{5,4},{9,8},{13,12},{17,16},{21,20},{25,24},{29,28}} | collective-permute-start | bytes 884744 | tf_op jit(solution)/shard_map/ppermute | solution.py:167
  28.6 2.8 %fusion = bf16[4,32,512]{2,0,1:T(4,128)(2,1)S(1)} fusion(bf16[32,128,512]{2,1,0:T(8,128)(2,1)} %param.11, bf16[4,32,128]{2,1,0:T(8,128)(2,1)S(1)} %copy-done), kind=kOutput, calls=%fused_computation.1 | convolution fusion | flops 16842752 | bytes 4358144 | tf_op jit(solution)/shard_map/phn,hnc->phc/dot_general | solution.py:171
  31.7 1.6 %collective-permute-start.1 = (bf16[128,576]{1,0:T(8,128)(2,1)S(1)}, bf16[128,576]{1,0:T(8,128)(2,1)S(1)}, u32[]{:S(2)}, u32[]{:S(2)}) collective-permute-start(bf16[128,576]{1,0:T(8,128)(2,1)S(1)} %bitcast.11), channel_id=1, source_target_pairs={{0,8},{4,12},{8,0},{12,4},{1,9},{5,13},{9,1},{13,5},{2,10},{6,14},... | collective-permute-start | bytes 442376 | tf_op jit(solution)/shard_map/ppermute | solution.py:182
  33.3 0.3 collective-permute-start.2
  33.6 7.6 %copy.14.refs_2_ = bf16[4096,576]{1,0:T(8,128)(2,1)} copy(bf16[4096,576]{0,1:T(8,128)(2,1)} %param.13) | data formatting | bytes 9437184 | tf_op args[4]
  41.3 2.5 %copy-done.1 = bf16[4096,576]{1,0:T(8,128)(2,1)S(1)} copy-done((bf16[4096,576]{1,0:T(8,128)(2,1)S(1)}, bf16[4096,576]{1,0:T(8,128)(2,1)}, u32[]{:S(2)}) %copy-start.1) | copy-done | bytes 4718616
  43.8 4.9 %prefix_attention.2 = (f32[256,512]{1,0:T(8,128)S(1)}, f32[256,128]{1,0:T(8,128)S(1)}, f32[256,128]{1,0:T(8,128)S(1)}) custom-call(bf16[128,576]{1,0:T(8,128)(2,1)S(1)} %bitcast.13, bf16[128,576]{1,0:T(8,128)(2,1)S(1)} %collective-permute-done.refs_1_.refs_5_, bf16[4096,576]{1,0:T(8,128)(2,1)S(1)} %copy-done.1), custom_call_target="tpu_custom_call" | custom-call | tf_op jit(solution)/shard_map/prefix_attention/pallas_call | solution.py:63
  48.7 4.9 %prefix_attention.3 = (f32[256,512]{1,0:T(8,128)S(1)}, f32[256,128]{1,0:T(8,128)S(1)}, f32[256,128]{1,0:T(8,128)S(1)}) custom-call(bf16[128,576]{1,0:T(8,128)(2,1)S(1)} %collective-permute-done.1.refs_0_.refs_6_, bf16[128,576]{1,0:T(8,128)(2,1)S(1)} %collective-permute-done.2.refs_1_.refs_7_, bf16[4096,576]{1,0:T(8,128)(2,1)S(1)} %copy-done.2), custom_call_target="tpu_custom_call" | custom-call | tf_op jit(solution)/shard_map/prefix_attention/pallas_call | solution.py:63
  53.7 3.0 %suffix_attention.1 = (bf16[4,64,576]{2,1,0:T(8,128)(2,1)}, bf16[128,640]{1,0:T(8,128)(2,1)S(1)}, bf16[128,640]{1,0:T(8,128)(2,1)S(1)}, bf16[128,640]{1,0:T(8,128)(2,1)S(1)}, bf16[128,640]{1,0:T(8,128)(2,1)S(1)}) custom-call(s32[4]{0:T(128)S(1)} %copy-done.5, s32[16]{0:T(128)S(1)} %copy-done.6, s32[2]{0:T(128)S(1)} %pad_add_fusion.refs_2_, ...), custom_call_target="tpu_custom_call" | custom-call | tf_op jit(solution)/shard_map/suffix_attention/pallas_call | solution.py:189
  56.7 1.6 %collective-permute-start.10 = (bf16[128,640]{1,0:T(8,128)(2,1)S(1)}, bf16[128,640]{1,0:T(8,128)(2,1)S(1)}, u32[]{:S(2)}, u32[]{:S(2)}) collective-permute-start(bf16[128,640]{1,0:T(8,128)(2,1)S(1)} %get-tuple-element.21), channel_id=1, source_target_pairs={{8,0},{12,4},{0,8},{4,12},{9,1},{13,5},{1,9},{5,13},{10,2},{14,6},... | collective-permute-start | bytes 491528 | tf_op jit(solution)/shard_map/ppermute | solution.py:205
  58.5 0.4 collective-permute-start.9
  59.0 4.9 %collective-permute-done.10.refs_2_ = bf16[128,640]{1,0:T(8,128)(2,1)S(1)} collective-permute-done((bf16[128,640]{1,0:T(8,128)(2,1)S(1)}, bf16[128,640]{1,0:T(8,128)(2,1)S(1)}, u32[]{:S(2)}, u32[]{:S(2)}) %collective-permute-start.10) | collective-permute-done | bytes 163872 | tf_op jit(solution)/shard_map/ppermute | solution.py:205
  63.8 2.4 %collective-permute-done.11.refs_3_ = bf16[128,640]{1,0:T(8,128)(2,1)S(1)} collective-permute-done((bf16[128,640]{1,0:T(8,128)(2,1)S(1)}, bf16[128,640]{1,0:T(8,128)(2,1)S(1)}, u32[]{:S(2)}, u32[]{:S(2)}) %collective-permute-start.11) | collective-permute-done | bytes 163872 | tf_op jit(solution)/shard_map/ppermute | solution.py:205
  66.2 0.3 merge.1
  66.5 0.7 fusion.1
  67.1 0.6 copy.17
  (30 shorter events, 0.5 us)
Async XLA Ops:
  0.6 28.0 %copy-start = (bf16[4,32,128]{2,1,0:T(8,128)(2,1)S(1)}, bf16[4,32,128]{2,1,0:T(8,128)(2,1)}, u32[]{:S(2)}) copy-start(bf16[4,32,128]{2,1,0:T(8,128)(2,1)} %param.9) | copy-start | bytes 98308
  0.6 30.8 %copy-start.8 = (bf16[4,32,64]{2,1,0:T(8,128)(2,1)S(1)}, bf16[4,32,64]{2,1,0:T(8,128)(2,1)}, u32[]{:S(2)}) copy-start(bf16[4,32,64]{2,1,0:T(8,128)(2,1)} %param.10) | copy-start | bytes 49156
  0.7 12.3 %collective-permute-start.3 = (bf16[4,64,576]{2,1,0:T(8,128)(2,1)}, bf16[4,64,576]{2,1,0:T(8,128)(2,1)S(1)}, u32[]{:S(2)}, u32[]{:S(2)}) collective-permute-start(bf16[4,64,576]{2,1,0:T(8,128)(2,1)} %refs_14_.1), channel_id=1, source_target_pairs={{0,1},{1,2},{2,3},{4,5},{5,6},{6,7},{8,9},{9,10},{10,11},{12,13},{... | collective-permute-start | bytes 884744 | tf_op jit(solution)/shard_map/ppermute | solution.py:166
  5.7 11.3 %collective-permute-start.4 = (bf16[4,64,576]{2,1,0:T(8,128)(2,1)}, bf16[4,64,576]{2,1,0:T(8,128)(2,1)S(1)}, u32[]{:S(2)}, u32[]{:S(2)}) collective-permute-start(bf16[4,64,576]{2,1,0:T(8,128)(2,1)} %refs_14_.1), channel_id=1, source_target_pairs={{1,0},{2,1},{3,2},{5,4},{6,5},{7,6},{9,8},{10,9},{11,10},{13,12},{... | collective-permute-start | bytes 884744 | tf_op jit(solution)/shard_map/ppermute | solution.py:167
  13.0 5.3 %collective-permute-start.5 = (bf16[4,64,576]{2,1,0:T(8,128)(2,1)S(1)}, bf16[4,64,576]{2,1,0:T(8,128)(2,1)S(1)}, u32[]{:S(2)}, u32[]{:S(2)}) collective-permute-start(bf16[4,64,576]{2,1,0:T(8,128)(2,1)S(1)} %collective-permute-done.3.refs_15_), channel_id=1, source_target_pairs={{1,2},{2,3},{5,6},{6,7},{9,10},{10,11},{13,14},{14,15},{17,18},{18... | collective-permute-start | bytes 884744 | tf_op jit(solution)/shard_map/ppermute | solution.py:166
  17.0 10.3 %collective-permute-start.6 = (bf16[4,64,576]{2,1,0:T(8,128)(2,1)S(1)}, bf16[4,64,576]{2,1,0:T(8,128)(2,1)S(1)}, u32[]{:S(2)}, u32[]{:S(2)}) collective-permute-start(bf16[4,64,576]{2,1,0:T(8,128)(2,1)S(1)} %collective-permute-done.4.refs_16_), channel_id=1, source_target_pairs={{1,0},{2,1},{5,4},{6,5},{9,8},{10,9},{13,12},{14,13},{17,16},{18,1... | collective-permute-start | bytes 884744 | tf_op jit(solution)/shard_map/ppermute | solution.py:167
  18.3 35.3 %collective-permute-start.7 = (bf16[4,64,576]{2,1,0:T(8,128)(2,1)S(1)}, bf16[4,64,576]{2,1,0:T(8,128)(2,1)S(1)}, u32[]{:S(2)}, u32[]{:S(2)}) collective-permute-start(bf16[4,64,576]{2,1,0:T(8,128)(2,1)S(1)} %collective-permute-done.5.refs_17_), channel_id=1, source_target_pairs={{2,3},{6,7},{10,11},{14,15},{18,19},{22,23},{26,27},{30,31}} | collective-permute-start | bytes 884744 | tf_op jit(solution)/shard_map/ppermute | solution.py:166
  27.3 26.3 %collective-permute-start.8 = (bf16[4,64,576]{2,1,0:T(8,128)(2,1)S(1)}, bf16[4,64,576]{2,1,0:T(8,128)(2,1)S(1)}, u32[]{:S(2)}, u32[]{:S(2)}) collective-permute-start(bf16[4,64,576]{2,1,0:T(8,128)(2,1)S(1)} %collective-permute-done.6.refs_18_), channel_id=1, source_target_pairs={{1,0},{5,4},{9,8},{13,12},{17,16},{21,20},{25,24},{29,28}} | collective-permute-start | bytes 884744 | tf_op jit(solution)/shard_map/ppermute | solution.py:167
  31.6 9.6 %collective-permute-start = (bf16[128,576]{1,0:T(8,128)(2,1)S(1)}, bf16[128,576]{1,0:T(8,128)(2,1)S(1)}, u32[]{:S(2)}, u32[]{:S(2)}) collective-permute-start(bf16[128,576]{1,0:T(8,128)(2,1)S(1)} %bitcast.10), channel_id=1, source_target_pairs={{0,4},{4,0},{8,12},{12,8},{1,5},{5,1},{9,13},{13,9},{2,6},{6,2},{1... | collective-permute-start | bytes 442376 | tf_op jit(solution)/shard_map/ppermute | solution.py:182
  31.7 17.0 %collective-permute-start.1 = (bf16[128,576]{1,0:T(8,128)(2,1)S(1)}, bf16[128,576]{1,0:T(8,128)(2,1)S(1)}, u32[]{:S(2)}, u32[]{:S(2)}) collective-permute-start(bf16[128,576]{1,0:T(8,128)(2,1)S(1)} %bitcast.11), channel_id=1, source_target_pairs={{0,8},{4,12},{8,0},{12,4},{1,9},{5,13},{9,1},{13,5},{2,10},{6,14},... | collective-permute-start | bytes 442376 | tf_op jit(solution)/shard_map/ppermute | solution.py:182
  33.3 15.4 %collective-permute-start.2 = (bf16[128,576]{1,0:T(8,128)(2,1)S(1)}, bf16[128,576]{1,0:T(8,128)(2,1)S(1)}, u32[]{:S(2)}, u32[]{:S(2)}) collective-permute-start(bf16[128,576]{1,0:T(8,128)(2,1)S(1)} %bitcast.12), channel_id=1, source_target_pairs={{0,12},{4,8},{8,4},{12,0},{1,13},{5,9},{9,5},{13,1},{2,14},{6,10},... | collective-permute-start | bytes 442376 | tf_op jit(solution)/shard_map/ppermute | solution.py:182
  41.3 2.5 %copy-start.1 = (bf16[4096,576]{1,0:T(8,128)(2,1)S(1)}, bf16[4096,576]{1,0:T(8,128)(2,1)}, u32[]{:S(2)}) copy-start(bf16[4096,576]{1,0:T(8,128)(2,1)} %copy.14.refs_2_) | copy-start | bytes 14155780
  43.8 5.0 %copy-start.2 = (bf16[4096,576]{1,0:T(8,128)(2,1)S(1)}, bf16[4096,576]{1,0:T(8,128)(2,1)}, u32[]{:S(2)}) copy-start(bf16[4096,576]{1,0:T(8,128)(2,1)} %copy.14.refs_2_) | copy-start | bytes 14155780
  43.8 9.9 %copy-start.3 = (bf16[4,64,576]{2,1,0:T(8,128)(2,1)S(1)}, bf16[4,64,576]{2,1,0:T(8,128)(2,1)}, u32[]{:S(2)}) copy-start(bf16[4,64,576]{2,1,0:T(8,128)(2,1)} %refs_14_.1) | copy-start | bytes 884740
  43.8 9.9 %copy-start.4 = (bf16[4,576]{1,0:T(4,128)(2,1)S(1)}, bf16[4,576]{1,0:T(4,128)(2,1)}, u32[]{:S(2)}) copy-start(bf16[4,576]{1,0:T(4,128)(2,1)} %refs_3_.1) | copy-start | bytes 13828
  43.8 9.9 %copy-start.5 = (s32[4]{0:T(128)S(1)}, s32[4]{0:T(128)}, u32[]{:S(2)}) copy-start(s32[4]{0:T(128)} %refs_0_.1) | copy-start | bytes 52
  43.8 9.9 %copy-start.6 = (s32[16]{0:T(128)S(1)}, s32[16]{0:T(128)}, u32[]{:S(2)}) copy-start(s32[16]{0:T(128)} %refs_1_.1) | copy-start | bytes 196
  48.7 17.8 %copy-start.7 = (bf16[32,512,128]{2,1,0:T(8,128)(2,1)S(1)}, bf16[32,512,128]{2,1,0:T(8,128)(2,1)}, u32[]{:S(2)}) copy-start(bf16[32,512,128]{2,1,0:T(8,128)(2,1)} %param.12) | copy-start | bytes 12582916
  56.7 7.1 %collective-permute-start.10 = (bf16[128,640]{1,0:T(8,128)(2,1)S(1)}, bf16[128,640]{1,0:T(8,128)(2,1)S(1)}, u32[]{:S(2)}, u32[]{:S(2)}) collective-permute-start(bf16[128,640]{1,0:T(8,128)(2,1)S(1)} %get-tuple-element.21), channel_id=1, source_target_pairs={{8,0},{12,4},{0,8},{4,12},{9,1},{13,5},{1,9},{5,13},{10,2},{14,6},... | collective-permute-start | bytes 491528 | tf_op jit(solution)/shard_map/ppermute | solution.py:205
  58.3 7.9 %collective-permute-start.11 = (bf16[128,640]{1,0:T(8,128)(2,1)S(1)}, bf16[128,640]{1,0:T(8,128)(2,1)S(1)}, u32[]{:S(2)}, u32[]{:S(2)}) collective-permute-start(bf16[128,640]{1,0:T(8,128)(2,1)S(1)} %get-tuple-element.22), channel_id=1, source_target_pairs={{12,0},{8,4},{4,8},{0,12},{13,1},{9,5},{5,9},{1,13},{14,2},{10,6},... | collective-permute-start | bytes 491528 | tf_op jit(solution)/shard_map/ppermute | solution.py:205
  58.5 7.7 %collective-permute-start.9 = (bf16[128,640]{1,0:T(8,128)(2,1)S(1)}, bf16[128,640]{1,0:T(8,128)(2,1)S(1)}, u32[]{:S(2)}, u32[]{:S(2)}) collective-permute-start(bf16[128,640]{1,0:T(8,128)(2,1)S(1)} %get-tuple-element.20), channel_id=1, source_target_pairs={{4,0},{0,4},{12,8},{8,12},{5,1},{1,5},{13,9},{9,13},{6,2},{2,6},{1... | collective-permute-start | bytes 491528 | tf_op jit(solution)/shard_map/ppermute | solution.py:205

commit v2 on v1

--- a/solution.py
+++ b/solution.py
@@ -20,32 +20,26 @@
 VMEM = pl.BlockSpec(memory_space=pltpu.VMEM)
 SMEM = pl.BlockSpec(memory_space=pltpu.SMEM)
 ANY = pl.BlockSpec(memory_space=pl.ANY)
-PARAMS = pltpu.CompilerParams(vmem_limit_bytes=40 * 1024 * 1024)
-
-
-def prefix_kernel(count, *refs):
+PARAMS = pltpu.CompilerParams(vmem_limit_bytes=24 * 1024 * 1024)
+
+
+def prefix_kernel(count, tiles, *refs):
     query_refs = refs[:count]
-    prefix_hbm, acc_ref, max_ref, sum_ref, keys, sems = refs[count:]
-    tiles, tile = keys.shape[0], keys.shape[1]
+    keys_ref, acc_ref, max_ref, sum_ref = refs[count:]
     rank = acc_ref.shape[1]
-
-    def fetch(i):
-        return pltpu.make_async_copy(
-            prefix_hbm.at[pl.ds(i * tile, tile)], keys.at[i], sems.at[i]
-        )
-
-    for i in range(tiles):
-        fetch(i).start()
+    tile = keys_ref.shape[1] // tiles
     queries = jnp.concatenate([ref[...] for ref in query_refs], axis=0)
     for i in range(tiles):
-        fetch(i).wait()
-        scores = lax.dot_general(queries, keys[i], NT, preferred_element_type=F32) * SCALE2
+        part = pl.ds(i * tile, tile)
+        scores = jnp.dot(queries, keys_ref[:, part], preferred_element_type=F32) * SCALE2
         top = jnp.max(scores, axis=1, keepdims=True)
         if i > 0:
             top = jnp.maximum(top, largest)
         weights = jnp.exp2(scores - top)
         total = jnp.sum(weights, axis=1, keepdims=True)
-        acc = jnp.dot(weights.astype(BF16), keys[i, :, :rank], preferred_element_type=F32)
+        acc = lax.dot_general(
+            weights.astype(BF16), keys_ref[:rank, part], NT, preferred_element_type=F32
+        )
         if i > 0:
             factor = jnp.exp2(largest - top)
             total = total + running * factor
@@ -56,65 +50,98 @@
     sum_ref[...] = jnp.broadcast_to(running, sum_ref.shape)
 
 
-def prefix_attention(queries, prefix, rank, tiles=4):
+def prefix_attention(queries, keys, rank, tiles=4):
     rows = sum(q.shape[0] for q in queries)
-    tile = prefix.shape[0] // tiles
+    width, length = keys.shape
     stat = jax.ShapeDtypeStruct((rows, LANES), F32)
     return pl.pallas_call(
-        functools.partial(prefix_kernel, len(queries)),
+        functools.partial(prefix_kernel, len(queries), tiles),
         out_shape=(jax.ShapeDtypeStruct((rows, rank), F32), stat, stat),
-        in_specs=[VMEM] * len(queries) + [ANY],
+        in_specs=[VMEM] * (len(queries) + 1),
         out_specs=(VMEM,) * 3,
-        scratch_shapes=[
-            pltpu.VMEM((tiles, tile, prefix.shape[1]), BF16),
-            pltpu.SemaphoreType.DMA((tiles,)),
-        ],
         compiler_params=PARAMS,
+        cost_estimate=pl.CostEstimate(
+            flops=2 * rows * length * (width + rank),
+            bytes_accessed=2 * width * length,
+            transcendentals=rows * length,
+        ),
         name="prefix_attention",
-    )(*queries, prefix)
-
-
-def suffix_kernel(count, offsets, heads, *refs):
+    )(*queries, keys)
+
+
+def start_copies(count, block_refs, picks, out_ref, sems):
+    for p, (which, slot) in enumerate(picks):
+        for k in range(count):
+
+            @pl.when(which == k)
+            def _():
+                pltpu.make_async_copy(block_refs[k].at[slot], out_ref.at[p], sems.at[p]).start()
+
+
+def wait_copies(block_refs, out_ref, sems):
+    for p in range(out_ref.shape[0]):
+        pltpu.make_async_copy(block_refs[0].at[0], out_ref.at[p], sems.at[p]).wait()
+
+
+def select_kernel(count, theirs, place, *refs):
+    block_refs, (_, out_ref, sems) = refs[:count], refs[count:]
+    local = out_ref.shape[0]
+    picks = []
+    for p in range(local):
+        ancestor = theirs[p]
+        picks.append((jnp.bitwise_xor(lax.div(ancestor, local), place[1]), lax.rem(ancestor, local)))
+    start_copies(count, block_refs, picks, out_ref, sems)
+    wait_copies(block_refs, out_ref, sems)
+
+
+def suffix_kernel(count, sources, inner, heads, *refs):
     anc, lens, place, fresh_ref = refs[:4]
     refs = refs[4:]
     query_refs, refs = refs[:count], refs[count:]
     stage_refs, refs = refs[: 3 * (count // 2)], refs[3 * (count // 2) :]
-    block_refs, refs = refs[: len(offsets)], refs[len(offsets) :]
+    block_refs, refs = refs[:sources], refs[sources:]
     cache_ref, refs = refs[0], refs[1:]
     out_refs, (moved, sems) = refs[:count], refs[count:]
     local, span, width = moved.shape
     rank = stage_refs[0].shape[1]
 
+    picks = []
     for p in range(local):
         owner = lax.div(anc[p], local)
         slot = lax.rem(anc[p], local)
-        for k, offset in enumerate(offsets):
-
-            @pl.when(owner == place[1] + offset)
-            def _():
-                pltpu.make_async_copy(block_refs[k].at[slot], moved.at[p], sems.at[p]).start()
-
-    for p in range(local):
-        pltpu.make_async_copy(block_refs[0].at[0], moved.at[p], sems.at[p]).wait()
-
+        if inner:
+            far = (place[1] == 0) | (place[1] == 3)
+            far = far & (owner != place[1])
+            which = jnp.where(far, sources - 1, jnp.bitwise_xor(owner, place[1]))
+            slot = jnp.where(far, p, slot)
+        else:
+            which = lax.rem(place[1] - owner + sources, sources)
+        picks.append((which, slot))
+    start_copies(sources, block_refs, picks, moved, sems)
+
+    cols, half = local * span, 2 * heads * local
     start = place[0] * span
     ends = [lens[anc[p]] for p in range(local)]
+    col = lax.broadcasted_iota(jnp.int32, (1, cols), 1)
+    row = lax.broadcasted_iota(jnp.int32, (half, 1), 0)
+    col_of = jnp.zeros_like(col)
+    row_of = jnp.zeros_like(row)
+    limit = jnp.full_like(col, ends[0] - start)
+    for p in range(1, local):
+        col_of = col_of + (col >= p * span).astype(jnp.int32)
+        limit = jnp.where(col >= p * span, ends[p] - start + p * span, limit)
+    for k in range(2):
+        for p in range(local):
+            row_of = jnp.where(row >= (k * local + p) * heads, p, row_of)
+    col_of = jnp.where(col < limit, col_of, -1)
+    seen = row_of == col_of
+    lane = lax.broadcasted_iota(jnp.int32, (half, LANES), 1)
     row_at = start + lax.broadcasted_iota(jnp.int32, (span, width), 0)
+
+    wait_copies(block_refs, moved, sems)
     for p in range(local):
         cache_ref[p] = jnp.where(row_at == ends[p], fresh_ref[pl.ds(p, 1), :], moved[p])
-
-    keys = moved[...].reshape(local * span, width)
-    half = 2 * heads * local
-    shape = (half, local * span)
-    row = lax.broadcasted_iota(jnp.int32, shape, 0)
-    col = lax.broadcasted_iota(jnp.int32, shape, 1)
-    row_of = lax.rem(lax.div(row, heads), local)
-    at = start + lax.rem(col, span)
-    col_of = lax.div(col, span)
-    seen = jnp.zeros(shape, jnp.bool_)
-    for p in range(local):
-        seen = seen | ((row_of == p) & (col_of == p) & (at < ends[p]))
-    lane = lax.broadcasted_iota(jnp.int32, (half, LANES), 1)
+    keys = moved[...].reshape(cols, width)
     for k in range(count // 2):
         queries = jnp.concatenate([query_refs[2 * k][...], query_refs[2 * k + 1][...]], axis=0)
         acc_ref, max_ref, sum_ref = stage_refs[3 * k : 3 * k + 3]
@@ -133,7 +160,7 @@
         middle = (level - high).astype(BF16).astype(F32)
         low = level - high - middle
         stats = jnp.where(lane == 0, high, jnp.where(lane == 1, middle, jnp.where(lane == 2, low, 0.0)))
-        part = jnp.concatenate([(acc / total).astype(BF16), stats.astype(BF16)], axis=1)
+        part = jnp.concatenate([(acc * (1.0 / total)).astype(BF16), stats.astype(BF16)], axis=1)
         out_refs[2 * k][...] = part[: half // 2]
         out_refs[2 * k + 1][...] = part[half // 2 :]
 
@@ -160,13 +187,18 @@
     chips = seq_size // cores
     place = jnp.stack([lax.axis_index("seq"), lax.axis_index("dom")]).astype(jnp.int32)
 
-    offsets, blocks = [0], [private_caches]
-    left = right = private_caches
-    for k in range(1, dom_size):
-        right = lax.ppermute(right, "dom", [(i, i + 1) for i in range(k - 1, dom_size - 1)])
-        left = lax.ppermute(left, "dom", [(i, i - 1) for i in range(1, dom_size - k + 1)])
-        offsets += [-k, k]
-        blocks += [right, left]
+    inner = dom_size == 4
+    if inner:
+        far = lax.ppermute(private_caches, "dom", [(1, 2), (2, 1)])
+        near = lax.ppermute(private_caches, "dom", [(0, 1), (3, 2)])
+        middle = lax.ppermute(private_caches, "dom", [(0, 2), (3, 1)])
+        theirs = lax.ppermute(ancestors, "dom", [(0, 1), (3, 2)])
+        blocks = [private_caches, near, middle, far]
+    else:
+        blocks = [private_caches] + [
+            lax.ppermute(private_caches, "dom", [(i, (i + k) % dom_size) for i in range(dom_size)])
+            for k in range(1, dom_size)
+        ]
 
     query_latent = jnp.einsum("phn,hnc->phc", q_nope, w_uk, preferred_element_type=F32).astype(BF16)
     own = jnp.concatenate([query_latent, q_rope], axis=2).reshape(local * heads, width)
@@ -180,14 +212,26 @@
 
     routes = [(t, f) for t in range(chips) for f in range(cores)]
     queries = [own if r == (0, 0) else lax.ppermute(own, "seq", pairs(*r)) for r in routes]
+    keys = prefix.T
     stages = []
     for k in range(0, len(routes), 2):
-        stages += prefix_attention(queries[k : k + 2], prefix, rank)
+        stages += prefix_attention(queries[k : k + 2], keys, rank)
+        if inner and k == 0:
+            chosen = pl.pallas_call(
+                functools.partial(select_kernel, len(blocks)),
+                out_shape=jax.ShapeDtypeStruct(private_caches.shape, BF16),
+                in_specs=[SMEM] * 2 + [ANY] * (len(blocks) + 1),
+                out_specs=ANY,
+                scratch_shapes=[pltpu.SemaphoreType.DMA((local,))],
+                compiler_params=PARAMS,
+                name="select",
+            )(theirs, place, *blocks, stages[1])
+            blocks.append(lax.ppermute(chosen, "dom", [(1, 0), (2, 3)]))
 
     count = len(routes)
     rows = local * heads
     results = pl.pallas_call(
-        functools.partial(suffix_kernel, count, tuple(offsets), heads),
+        functools.partial(suffix_kernel, count, len(blocks), inner, heads),
         out_shape=(jax.ShapeDtypeStruct(private_caches.shape, BF16),)
         + (jax.ShapeDtypeStruct((rows, rank + LANES), BF16),) * count,
         in_specs=[SMEM] * 3 + [VMEM] * (1 + count + len(stages)) + [ANY] * len(blocks),

time: 68.5 us -> 63.1 us (0.921)
  local copies, waits for them, and re-layouts: 10.8 us -> 3.85 us
  starting transfers between devices: 14.4 us -> 15.8 us
  waiting for transfers between devices: 24.9 us -> 26.1 us
    unnamed x21 -> x16, local copies, waits for them, and re-layouts: 10.8 us -> 3.83 us
    ppermute x6 -> x5, starting transfers between devices: 10.3 us -> 11.9 us  [the longest x1 7.22 us: on_device(): middle = lax.ppermute(private_caches, 'dom', [(0, 2), (3, 1)])]
    ppermute x6 -> x5, waiting for transfers between devices: 17.6 us -> 18.3 us  [the longest x1 11.6 us: on_device(): theirs = lax.ppermute(ancestors, 'dom', [(0, 1), (3, 2)])]
    pallas_call x3 -> x4, Pallas kernels: 12.8 us -> 12.2 us  [the longest x2 7.89 us: prefix_attention(): pl.pallas_call(functools.partial(prefix_kernel, len(queries), tiles), out...]
  transfers between devices with their start and end apart: 12 -> 11, of which waited for: 5 -> 4; matrix products, arithmetic and copies ran while one was open for 16% -> 0% of each run, Pallas kernels for 14% -> 14%
where the time goes in v2:
time: 63.1 us; the launch traced here: 62.8 us
  waiting for transfers between devices  26.1 us (41%)
  starting transfers between devices  15.8 us (25%)
  Pallas kernels  12.5 us (20%)
  local copies, waits for them, and re-layouts  3.85 us (6%)
  matrix products  3.51 us (6%)
  between operations  0.86 us (1%)
    ppermute x1, waiting for transfers between devices, on_device(): theirs = lax.ppermute(ancestors, 'dom', [(0, 1), (3, 2)])  11.6 us
    pallas_call x2, Pallas kernels, prefix_attention(): pl.pallas_call(functools.partial(prefix_kernel, len(queries), tiles), out...  7.89 us
    ppermute x3, waiting for transfers between devices, on_device(): lax.ppermute(part, 'seq', [(b, a) for a, b in pairs(*r)])  7.81 us
    ppermute x1, starting transfers between devices, on_device(): middle = lax.ppermute(private_caches, 'dom', [(0, 2), (3, 1)])  7.22 us
    ppermute x1, waiting for transfers between devices, on_device(): blocks.append(lax.ppermute(chosen, 'dom', [(1, 0), (2, 3)]))  6.69 us
    unnamed x16, local copies, waits for them, and re-layouts  3.83 us
    pallas_call x1, Pallas kernels, on_device(): pl.pallas_call(functools.partial(suffix_kernel, count, len(blocks), inner...  3.22 us
    dot_general x1, matrix products, on_device(): jnp.einsum('phn,hnc->phc', q_nope, w_uk, preferred_element_type=F32)  2.84 us
  transfers between devices with their start and end apart: 11, of which 4 were waited for; matrix products, arithmetic and copies ran while one was open for 0% of the time, Pallas kernels for 14%

profile of v2, /device:TPU:0, one launch (start us, length us, event | category | flops | bytes accessed | tf_op | source)
XLA Modules:
  0.0 62.8 jit_solution(13087391701484521252)
XLA Ops:
  0.7 0.8 %copy.12 = bf16[4,32,64]{2,0,1:T(4,128)(2,1)S(1)} copy(bf16[4,32,64]{2,1,0:T(8,128)(2,1)} %param.10) | data formatting | bytes 32768 | tf_op args[1]
  1.5 2.8 %fusion = bf16[4,32,512]{2,0,1:T(4,128)(2,1)S(1)} fusion(bf16[32,128,512]{2,1,0:T(8,128)(2,1)} %param.11, bf16[4,32,128]{2,1,0:T(8,128)(2,1)S(1)} %copy-done), kind=kOutput, calls=%fused_computation.1 | convolution fusion | flops 16842752 | bytes 4358144 | tf_op jit(solution)/shard_map/phn,hnc->phc/dot_general | solution.py:203
  4.5 0.5 collective-permute-start
  5.0 0.7 %collective-permute-start.5 = (bf16[4,64,576]{2,1,0:T(8,128)(2,1)S(1)}, bf16[4,64,576]{2,1,0:T(8,128)(2,1)S(1)}, u32[]{:S(2)}, u32[]{:S(2)}) collective-permute-start(bf16[4,64,576]{2,1,0:T(8,128)(2,1)S(1)} %copy-done.1), channel_id=1, source_target_pairs={{1,2},{2,1},{5,6},{6,5},{9,10},{10,9},{13,14},{14,13},{17,18},{18,... | collective-permute-start | bytes 884744 | tf_op jit(solution)/shard_map/ppermute | solution.py:192
  5.7 7.2 %collective-permute-start.4 = (bf16[4,64,576]{2,1,0:T(8,128)(2,1)S(1)}, bf16[4,64,576]{2,1,0:T(8,128)(2,1)S(1)}, u32[]{:S(2)}, u32[]{:S(2)}) collective-permute-start(bf16[4,64,576]{2,1,0:T(8,128)(2,1)S(1)} %copy-done.1), channel_id=1, source_target_pairs={{0,2},{3,1},{4,6},{7,5},{8,10},{11,9},{12,14},{15,13},{16,18},{19,... | collective-permute-start | bytes 884744 | tf_op jit(solution)/shard_map/ppermute | solution.py:194
  12.9 1.4 %collective-permute-start.3 = (bf16[4,64,576]{2,1,0:T(8,128)(2,1)S(1)}, bf16[4,64,576]{2,1,0:T(8,128)(2,1)S(1)}, u32[]{:S(2)}, u32[]{:S(2)}) collective-permute-start(bf16[4,64,576]{2,1,0:T(8,128)(2,1)S(1)} %copy-done.1), channel_id=1, source_target_pairs={{0,1},{3,2},{4,5},{7,6},{8,9},{11,10},{12,13},{15,14},{16,17},{19,... | collective-permute-start | bytes 884744 | tf_op jit(solution)/shard_map/ppermute | solution.py:193
  14.3 1.3 %collective-permute-start.6 = (s32[4]{0:T(128)S(1)}, s32[4]{0:T(128)S(1)}, u32[]{:S(2)}, u32[]{:S(2)}) collective-permute-start(s32[4]{0:T(128)S(1)} %copy-done.3), channel_id=1, source_target_pairs={{0,1},{3,2},{4,5},{7,6},{8,9},{11,10},{12,13},{15,14},{16,17},{19,... | collective-permute-start | bytes 56 | tf_op jit(solution)/shard_map/ppermute | solution.py:195
  15.7 11.6 %collective-permute-done.6.theirs = s32[4]{0:T(128)S(1)} collective-permute-done((s32[4]{0:T(128)S(1)}, s32[4]{0:T(128)S(1)}, u32[]{:S(2)}, u32[]{:S(2)}) %collective-permute-start.6) | collective-permute-done | bytes 48 | tf_op jit(solution)/shard_map/ppermute | solution.py:195
  27.3 0.5 collective-permute-start.2
  27.8 1.0 %collective-permute-start.1 = (bf16[128,576]{1,0:T(8,128)(2,1)S(1)}, bf16[128,576]{1,0:T(8,128)(2,1)S(1)}, u32[]{:S(2)}, u32[]{:S(2)}) collective-permute-start(bf16[128,576]{1,0:T(8,128)(2,1)S(1)} %bitcast.13), channel_id=1, source_target_pairs={{0,8},{4,12},{8,0},{12,4},{1,9},{5,13},{9,1},{13,5},{2,10},{6,14},... | collective-permute-start | bytes 442376 | tf_op jit(solution)/shard_map/ppermute | solution.py:214
  28.8 2.3 %copy-done.5 = bf16[4096,576]{0,1:T(8,128)(2,1)S(1)} copy-done((bf16[4096,576]{0,1:T(8,128)(2,1)S(1)}, bf16[4096,576]{0,1:T(8,128)(2,1)}, u32[]{:S(2)}) %copy-start.5) | copy-done | bytes 4718616
  31.2 3.9 %prefix_attention.2 = (f32[256,512]{1,0:T(8,128)S(1)}, f32[256,128]{1,0:T(8,128)S(1)}, f32[256,128]{1,0:T(8,128)S(1)}) custom-call(bf16[128,576]{1,0:T(8,128)(2,1)S(1)} %bitcast.14, bf16[128,576]{1,0:T(8,128)(2,1)S(1)} %collective-permute-done.refs_1_.refs_5_, bf16[576,4096]{1,0:T(8,128)(2,1)S(1)} %bitcast.17), custom_call_target="tpu_custom_call" | custom-call | flops 2281701376 | bytes 4718592 | tf_op jit(solution)/shard_map/prefix_attention/pallas_call | solution.py:57
  35.1 1.1 %select.1 = bf16[4,64,576]{2,1,0:T(8,128)(2,1)S(1)} custom-call(s32[4]{0:T(128)S(1)} %collective-permute-done.6.theirs, s32[2]{0:T(128)S(1)} %pad_add_fusion.place.refs_2_, bf16[4,64,576]{2,1,0:T(8,128)(2,1)S(1)} %copy-done.1, bf16[4,64,576]{2,1,0:T(8,128)(2,1)S(1)} %collective-permute-done.3.refs_1_.refs_15_, ...), custom_call_target="tpu_custom_call" | custom-call | tf_op jit(solution)/shard_map/select/pallas_call | solution.py:220
  36.3 1.3 %collective-permute-start.7 = (bf16[4,64,576]{2,1,0:T(8,128)(2,1)S(1)}, bf16[4,64,576]{2,1,0:T(8,128)(2,1)S(1)}, u32[]{:S(2)}, u32[]{:S(2)}) collective-permute-start(bf16[4,64,576]{2,1,0:T(8,128)(2,1)S(1)} %select.1), channel_id=1, source_target_pairs={{1,0},{2,3},{5,4},{6,7},{9,8},{10,11},{13,12},{14,15},{17,16},{18,... | collective-permute-start | bytes 884744 | tf_op jit(solution)/shard_map/ppermute | solution.py:229
  37.6 3.9 %prefix_attention.3 = (f32[256,512]{1,0:T(8,128)S(1)}, f32[256,128]{1,0:T(8,128)S(1)}, f32[256,128]{1,0:T(8,128)S(1)}) custom-call(bf16[128,576]{1,0:T(8,128)(2,1)S(1)} %collective-permute-done.1.refs_0_.refs_6_, bf16[128,576]{1,0:T(8,128)(2,1)S(1)} %collective-permute-done.2.refs_1_.refs_7_, bf16[576,4096]{1,0:T(8,128)(2,1)S(1)} %bitcast.18), custom_call_target="tpu_custom_call" | custom-call | flops 2281701376 | bytes 4718592 | tf_op jit(solution)/shard_map/prefix_attention/pallas_call | solution.py:57
  41.6 6.7 %collective-permute-done.7.refs_18_ = bf16[4,64,576]{2,1,0:T(8,128)(2,1)S(1)} collective-permute-done((bf16[4,64,576]{2,1,0:T(8,128)(2,1)S(1)}, bf16[4,64,576]{2,1,0:T(8,128)(2,1)S(1)}, u32[]{:S(2)}, u32[]{:S(2)}) %collective-permute-start.7) | collective-permute-done | bytes 294944 | tf_op jit(solution)/shard_map/ppermute | solution.py:229
  48.3 3.2 %suffix_attention.1 = (bf16[4,64,576]{2,1,0:T(8,128)(2,1)}, bf16[128,640]{1,0:T(8,128)(2,1)S(1)}, bf16[128,640]{1,0:T(8,128)(2,1)S(1)}, bf16[128,640]{1,0:T(8,128)(2,1)S(1)}, bf16[128,640]{1,0:T(8,128)(2,1)S(1)}) custom-call(s32[4]{0:T(128)S(1)} %copy-done.3, s32[16]{0:T(128)S(1)} %copy-done.4, s32[2]{0:T(128)S(1)} %pad_add_fusion.place.refs_2_, ...), custom_call_target="tpu_custom_call" | custom-call | tf_op jit(solution)/shard_map/suffix_attention/pallas_call | solution.py:233
  51.6 1.6 %collective-permute-start.9 = (bf16[128,640]{1,0:T(8,128)(2,1)S(1)}, bf16[128,640]{1,0:T(8,128)(2,1)S(1)}, u32[]{:S(2)}, u32[]{:S(2)}) collective-permute-start(bf16[128,640]{1,0:T(8,128)(2,1)S(1)} %get-tuple-element.21), channel_id=1, source_target_pairs={{8,0},{12,4},{0,8},{4,12},{9,1},{13,5},{1,9},{5,13},{10,2},{14,6},... | collective-permute-start | bytes 491528 | tf_op jit(solution)/shard_map/ppermute | solution.py:249
  53.1 0.3 collective-permute-start.10
  53.4 5.2 %collective-permute-done.9.refs_2_ = bf16[128,640]{1,0:T(8,128)(2,1)S(1)} collective-permute-done((bf16[128,640]{1,0:T(8,128)(2,1)S(1)}, bf16[128,640]{1,0:T(8,128)(2,1)S(1)}, u32[]{:S(2)}, u32[]{:S(2)}) %collective-permute-start.9) | collective-permute-done | bytes 163872 | tf_op jit(solution)/shard_map/ppermute | solution.py:249
  58.6 2.6 %collective-permute-done.10.refs_3_ = bf16[128,640]{1,0:T(8,128)(2,1)S(1)} collective-permute-done((bf16[128,640]{1,0:T(8,128)(2,1)S(1)}, bf16[128,640]{1,0:T(8,128)(2,1)S(1)}, u32[]{:S(2)}, u32[]{:S(2)}) %collective-permute-start.10) | collective-permute-done | bytes 163872 | tf_op jit(solution)/shard_map/ppermute | solution.py:249
  61.2 0.3 merge.1
  61.5 0.7 %fusion.1 = bf16[4,32,128]{2,0,1:T(4,128)(2,1)S(1)} fusion(bf16[32,512,128]{2,1,0:T(8,128)(2,1)S(1)} %copy-done.6, bf16[4,32,512]{2,1,0:T(8,128)(2,1)S(1)} %bitcast.16), kind=kOutput, calls=%fused_computation.3 | convolution fusion | flops 16793600 | bytes 4358144 | tf_op jit(solution)/shard_map/phc,hcv->phv/dot_general | solution.py:260
  62.2 0.6 %copy.15 = bf16[4,32,128]{2,1,0:T(8,128)(2,1)} copy(bf16[4,32,128]{2,0,1:T(4,128)(2,1)S(1)} %fusion.1) | data formatting | bytes 65536
  (24 shorter events, 0.3 us)
Async XLA Ops:
  0.6 0.9 %copy-start = (bf16[4,32,128]{2,1,0:T(8,128)(2,1)S(1)}, bf16[4,32,128]{2,1,0:T(8,128)(2,1)}, u32[]{:S(2)}) copy-start(bf16[4,32,128]{2,1,0:T(8,128)(2,1)} %param.9) | copy-start | bytes 98308
  0.6 4.3 %copy-start.1 = (bf16[4,64,576]{2,1,0:T(8,128)(2,1)S(1)}, bf16[4,64,576]{2,1,0:T(8,128)(2,1)}, u32[]{:S(2)}) copy-start(bf16[4,64,576]{2,1,0:T(8,128)(2,1)} %refs_14_.1) | copy-start | bytes 884740
  0.7 13.6 %copy-start.3 = (s32[4]{0:T(128)S(1)}, s32[4]{0:T(128)}, u32[]{:S(2)}) copy-start(s32[4]{0:T(128)} %refs_0_.3) | copy-start | bytes 52
  4.5 23.3 %collective-permute-start = (bf16[128,576]{1,0:T(8,128)(2,1)S(1)}, bf16[128,576]{1,0:T(8,128)(2,1)S(1)}, u32[]{:S(2)}, u32[]{:S(2)}) collective-permute-start(bf16[128,576]{1,0:T(8,128)(2,1)S(1)} %bitcast.11), channel_id=1, source_target_pairs={{0,4},{4,0},{8,12},{12,8},{1,5},{5,1},{9,13},{13,9},{2,6},{6,2},{1... | collective-permute-start | bytes 442376 | tf_op jit(solution)/shard_map/ppermute | solution.py:214
  5.0 30.1 %collective-permute-start.5 = (bf16[4,64,576]{2,1,0:T(8,128)(2,1)S(1)}, bf16[4,64,576]{2,1,0:T(8,128)(2,1)S(1)}, u32[]{:S(2)}, u32[]{:S(2)}) collective-permute-start(bf16[4,64,576]{2,1,0:T(8,128)(2,1)S(1)} %copy-done.1), channel_id=1, source_target_pairs={{1,2},{2,1},{5,6},{6,5},{9,10},{10,9},{13,14},{14,13},{17,18},{18,... | collective-permute-start | bytes 884744 | tf_op jit(solution)/shard_map/ppermute | solution.py:192
  5.7 29.5 %collective-permute-start.4 = (bf16[4,64,576]{2,1,0:T(8,128)(2,1)S(1)}, bf16[4,64,576]{2,1,0:T(8,128)(2,1)S(1)}, u32[]{:S(2)}, u32[]{:S(2)}) collective-permute-start(bf16[4,64,576]{2,1,0:T(8,128)(2,1)S(1)} %copy-done.1), channel_id=1, source_target_pairs={{0,2},{3,1},{4,6},{7,5},{8,10},{11,9},{12,14},{15,13},{16,18},{19,... | collective-permute-start | bytes 884744 | tf_op jit(solution)/shard_map/ppermute | solution.py:194
  12.9 22.2 %collective-permute-start.3 = (bf16[4,64,576]{2,1,0:T(8,128)(2,1)S(1)}, bf16[4,64,576]{2,1,0:T(8,128)(2,1)S(1)}, u32[]{:S(2)}, u32[]{:S(2)}) collective-permute-start(bf16[4,64,576]{2,1,0:T(8,128)(2,1)S(1)} %copy-done.1), channel_id=1, source_target_pairs={{0,1},{3,2},{4,5},{7,6},{8,9},{11,10},{12,13},{15,14},{16,17},{19,... | collective-permute-start | bytes 884744 | tf_op jit(solution)/shard_map/ppermute | solution.py:193
  14.3 13.0 %collective-permute-start.6 = (s32[4]{0:T(128)S(1)}, s32[4]{0:T(128)S(1)}, u32[]{:S(2)}, u32[]{:S(2)}) collective-permute-start(s32[4]{0:T(128)S(1)} %copy-done.3), channel_id=1, source_target_pairs={{0,1},{3,2},{4,5},{7,6},{8,9},{11,10},{12,13},{15,14},{16,17},{19,... | collective-permute-start | bytes 56 | tf_op jit(solution)/shard_map/ppermute | solution.py:195
  27.3 10.3 %collective-permute-start.2 = (bf16[128,576]{1,0:T(8,128)(2,1)S(1)}, bf16[128,576]{1,0:T(8,128)(2,1)S(1)}, u32[]{:S(2)}, u32[]{:S(2)}) collective-permute-start(bf16[128,576]{1,0:T(8,128)(2,1)S(1)} %bitcast.12), channel_id=1, source_target_pairs={{0,12},{4,8},{8,4},{12,0},{1,13},{5,9},{9,5},{13,1},{2,14},{6,10},... | collective-permute-start | bytes 442376 | tf_op jit(solution)/shard_map/ppermute | solution.py:214
  27.8 9.8 %collective-permute-start.1 = (bf16[128,576]{1,0:T(8,128)(2,1)S(1)}, bf16[128,576]{1,0:T(8,128)(2,1)S(1)}, u32[]{:S(2)}, u32[]{:S(2)}) collective-permute-start(bf16[128,576]{1,0:T(8,128)(2,1)S(1)} %bitcast.13), channel_id=1, source_target_pairs={{0,8},{4,12},{8,0},{12,4},{1,9},{5,13},{9,1},{13,5},{2,10},{6,14},... | collective-permute-start | bytes 442376 | tf_op jit(solution)/shard_map/ppermute | solution.py:214
  28.8 2.3 %copy-start.5 = (bf16[4096,576]{0,1:T(8,128)(2,1)S(1)}, bf16[4096,576]{0,1:T(8,128)(2,1)}, u32[]{:S(2)}) copy-start(bf16[4096,576]{0,1:T(8,128)(2,1)} %param.13) | copy-start | bytes 14155780
  36.2 12.0 %copy-start.2 = (bf16[4,576]{1,0:T(4,128)(2,1)S(1)}, bf16[4,576]{1,0:T(4,128)(2,1)}, u32[]{:S(2)}) copy-start(bf16[4,576]{1,0:T(4,128)(2,1)} %refs_3_.1) | copy-start | bytes 13828
  36.3 12.0 %copy-start.4 = (s32[16]{0:T(128)S(1)}, s32[16]{0:T(128)}, u32[]{:S(2)}) copy-start(s32[16]{0:T(128)} %refs_1_.1) | copy-start | bytes 196
  36.3 12.0 %collective-permute-start.7 = (bf16[4,64,576]{2,1,0:T(8,128)(2,1)S(1)}, bf16[4,64,576]{2,1,0:T(8,128)(2,1)S(1)}, u32[]{:S(2)}, u32[]{:S(2)}) collective-permute-start(bf16[4,64,576]{2,1,0:T(8,128)(2,1)S(1)} %select.1), channel_id=1, source_target_pairs={{1,0},{2,3},{5,4},{6,7},{9,8},{10,11},{13,12},{14,15},{17,16},{18,... | collective-permute-start | bytes 884744 | tf_op jit(solution)/shard_map/ppermute | solution.py:229
  41.5 20.0 %copy-start.6 = (bf16[32,512,128]{2,1,0:T(8,128)(2,1)S(1)}, bf16[32,512,128]{2,1,0:T(8,128)(2,1)}, u32[]{:S(2)}) copy-start(bf16[32,512,128]{2,1,0:T(8,128)(2,1)} %param.12) | copy-start | bytes 12582916
  51.5 1.9 %collective-permute-start.8 = (bf16[128,640]{1,0:T(8,128)(2,1)S(1)}, bf16[128,640]{1,0:T(8,128)(2,1)S(1)}, u32[]{:S(2)}, u32[]{:S(2)}) collective-permute-start(bf16[128,640]{1,0:T(8,128)(2,1)S(1)} %get-tuple-element.20), channel_id=1, source_target_pairs={{4,0},{0,4},{12,8},{8,12},{5,1},{1,5},{13,9},{9,13},{6,2},{2,6},{1... | collective-permute-start | bytes 491528 | tf_op jit(solution)/shard_map/ppermute | solution.py:249
  51.6 7.1 %collective-permute-start.9 = (bf16[128,640]{1,0:T(8,128)(2,1)S(1)}, bf16[128,640]{1,0:T(8,128)(2,1)S(1)}, u32[]{:S(2)}, u32[]{:S(2)}) collective-permute-start(bf16[128,640]{1,0:T(8,128)(2,1)S(1)} %get-tuple-element.21), channel_id=1, source_target_pairs={{8,0},{12,4},{0,8},{4,12},{9,1},{13,5},{1,9},{5,13},{10,2},{14,6},... | collective-permute-start | bytes 491528 | tf_op jit(solution)/shard_map/ppermute | solution.py:249
  53.1 8.1 %collective-permute-start.10 = (bf16[128,640]{1,0:T(8,128)(2,1)S(1)}, bf16[128,640]{1,0:T(8,128)(2,1)S(1)}, u32[]{:S(2)}, u32[]{:S(2)}) collective-permute-start(bf16[128,640]{1,0:T(8,128)(2,1)S(1)} %get-tuple-element.22), channel_id=1, source_target_pairs={{12,0},{8,4},{4,8},{0,12},{13,1},{9,5},{5,9},{1,13},{14,2},{10,6},... | collective-permute-start | bytes 491528 | tf_op jit(solution)/shard_map/ppermute | solution.py:249

commit v3 on v2

--- a/solution.py
+++ b/solution.py
@@ -20,7 +20,7 @@
 VMEM = pl.BlockSpec(memory_space=pltpu.VMEM)
 SMEM = pl.BlockSpec(memory_space=pltpu.SMEM)
 ANY = pl.BlockSpec(memory_space=pl.ANY)
-PARAMS = pltpu.CompilerParams(vmem_limit_bytes=24 * 1024 * 1024)
+PARAMS = pltpu.CompilerParams(vmem_limit_bytes=40 * 1024 * 1024)
 
 
 def prefix_kernel(count, tiles, *refs):
@@ -83,25 +83,14 @@
         pltpu.make_async_copy(block_refs[0].at[0], out_ref.at[p], sems.at[p]).wait()
 
 
-def select_kernel(count, theirs, place, *refs):
-    block_refs, (_, out_ref, sems) = refs[:count], refs[count:]
-    local = out_ref.shape[0]
-    picks = []
-    for p in range(local):
-        ancestor = theirs[p]
-        picks.append((jnp.bitwise_xor(lax.div(ancestor, local), place[1]), lax.rem(ancestor, local)))
-    start_copies(count, block_refs, picks, out_ref, sems)
-    wait_copies(block_refs, out_ref, sems)
-
-
-def suffix_kernel(count, sources, inner, heads, *refs):
+def suffix_kernel(count, sources, line, heads, *refs):
     anc, lens, place, fresh_ref = refs[:4]
     refs = refs[4:]
     query_refs, refs = refs[:count], refs[count:]
     stage_refs, refs = refs[: 3 * (count // 2)], refs[3 * (count // 2) :]
     block_refs, refs = refs[:sources], refs[sources:]
     cache_ref, refs = refs[0], refs[1:]
-    out_refs, (moved, sems) = refs[:count], refs[count:]
+    keep_ref, give_ref, moved, sems = refs
     local, span, width = moved.shape
     rank = stage_refs[0].shape[1]
 
@@ -109,11 +98,10 @@
     for p in range(local):
         owner = lax.div(anc[p], local)
         slot = lax.rem(anc[p], local)
-        if inner:
-            far = (place[1] == 0) | (place[1] == 3)
-            far = far & (owner != place[1])
-            which = jnp.where(far, sources - 1, jnp.bitwise_xor(owner, place[1]))
-            slot = jnp.where(far, p, slot)
+        if line:
+            apart = jnp.bitwise_xor(owner, place[1])
+            ends_line = (place[1] == 0) | (place[1] == 3)
+            which = jnp.where(ends_line & (apart > 1), apart + 2, apart)
         else:
             which = lax.rem(place[1] - owner + sources, sources)
         picks.append((which, slot))
@@ -135,7 +123,6 @@
             row_of = jnp.where(row >= (k * local + p) * heads, p, row_of)
     col_of = jnp.where(col < limit, col_of, -1)
     seen = row_of == col_of
-    lane = lax.broadcasted_iota(jnp.int32, (half, LANES), 1)
     row_at = start + lax.broadcasted_iota(jnp.int32, (span, width), 0)
 
     wait_copies(block_refs, moved, sems)
@@ -156,26 +143,43 @@
             weights.astype(BF16), keys[:, :rank], preferred_element_type=F32
         )
         level = top + jnp.log2(total)
-        high = level.astype(BF16).astype(F32)
-        middle = (level - high).astype(BF16).astype(F32)
-        low = level - high - middle
-        stats = jnp.where(lane == 0, high, jnp.where(lane == 1, middle, jnp.where(lane == 2, low, 0.0)))
-        part = jnp.concatenate([(acc * (1.0 / total)).astype(BF16), stats.astype(BF16)], axis=1)
-        out_refs[2 * k][...] = part[: half // 2]
-        out_refs[2 * k + 1][...] = part[half // 2 :]
-
-
-def merge_kernel(count, *refs):
-    part_refs, out_ref = refs[:count], refs[count]
-    rank = out_ref.shape[1]
-    levels = [jnp.sum(ref[:, rank:].astype(F32), axis=1, keepdims=True) for ref in part_refs]
+        part = packed(acc * (1.0 / total), level)
+        keep_ref[pl.ds(k * half // 2, half // 2)] = part[: half // 2]
+        give_ref[pl.ds(k * half // 2, half // 2)] = part[half // 2 :]
+
+
+def packed(values, level):
+    rows = values.shape[0]
+    lane = lax.broadcasted_iota(jnp.int32, (rows, LANES), 1)
+    high = level.astype(BF16).astype(F32)
+    middle = (level - high).astype(BF16).astype(F32)
+    low = level - high - middle
+    stats = jnp.where(lane == 0, high, jnp.where(lane == 1, middle, jnp.where(lane == 2, low, 0.0)))
+    return jnp.concatenate([values.astype(BF16), stats.astype(BF16)], axis=1)
+
+
+def merged(parts, rank):
+    levels = [jnp.sum(part[:, rank:].astype(F32), axis=1, keepdims=True) for part in parts]
     top = functools.reduce(jnp.maximum, levels)
     shares = [jnp.exp2(level - top) for level in levels]
     whole = functools.reduce(jnp.add, shares)
     acc = functools.reduce(
-        jnp.add, [share * ref[:, :rank].astype(F32) for share, ref in zip(shares, part_refs)]
+        jnp.add, [share * part[:, :rank].astype(F32) for share, part in zip(shares, parts)]
     )
-    out_ref[...] = (acc / whole).astype(BF16)
+    return acc * (1.0 / whole), top + jnp.log2(whole)
+
+
+def chip_kernel(chips, keep_ref, got_ref, *out_refs):
+    rows, rank = out_refs[0].shape[0], out_refs[0].shape[1] - LANES
+    for t in reversed(range(chips)):
+        part = pl.ds(t * rows, rows)
+        out_refs[t][...] = packed(*merged([keep_ref[part], got_ref[part]], rank))
+
+
+def final_kernel(*refs):
+    out_ref = refs[-1]
+    values, _ = merged([ref[...] for ref in refs[:-1]], out_ref.shape[1])
+    out_ref[...] = values.astype(BF16)
 
 
 def on_device(q_nope, q_rope, w_uk, w_uv, prefix, private_caches, new_latent, ancestors, lengths):
@@ -187,13 +191,10 @@
     chips = seq_size // cores
     place = jnp.stack([lax.axis_index("seq"), lax.axis_index("dom")]).astype(jnp.int32)
 
-    inner = dom_size == 4
-    if inner:
+    line = dom_size == 4
+    if line:
+        near = lax.ppermute(private_caches, "dom", [(0, 1), (1, 0), (2, 3), (3, 2)])
         far = lax.ppermute(private_caches, "dom", [(1, 2), (2, 1)])
-        near = lax.ppermute(private_caches, "dom", [(0, 1), (3, 2)])
-        middle = lax.ppermute(private_caches, "dom", [(0, 2), (3, 1)])
-        theirs = lax.ppermute(ancestors, "dom", [(0, 1), (3, 2)])
-        blocks = [private_caches, near, middle, far]
     else:
         blocks = [private_caches] + [
             lax.ppermute(private_caches, "dom", [(i, (i + k) % dom_size) for i in range(dom_size)])
@@ -213,29 +214,27 @@
     routes = [(t, f) for t in range(chips) for f in range(cores)]
     queries = [own if r == (0, 0) else lax.ppermute(own, "seq", pairs(*r)) for r in routes]
     keys = prefix.T
+    if line:
+        near, far, queries[1] = lax.optimization_barrier((near, far, queries[1]))
+        inner_middle = lax.ppermute(near, "dom", [(1, 2), (2, 1)])
+        outer_middle = lax.ppermute(far, "dom", [(1, 0), (2, 3)])
     stages = []
     for k in range(0, len(routes), 2):
         stages += prefix_attention(queries[k : k + 2], keys, rank)
-        if inner and k == 0:
-            chosen = pl.pallas_call(
-                functools.partial(select_kernel, len(blocks)),
-                out_shape=jax.ShapeDtypeStruct(private_caches.shape, BF16),
-                in_specs=[SMEM] * 2 + [ANY] * (len(blocks) + 1),
-                out_specs=ANY,
-                scratch_shapes=[pltpu.SemaphoreType.DMA((local,))],
-                compiler_params=PARAMS,
-                name="select",
-            )(theirs, place, *blocks, stages[1])
-            blocks.append(lax.ppermute(chosen, "dom", [(1, 0), (2, 3)]))
+        if line and k == 0:
+            inner_middle, stages[1] = lax.optimization_barrier((inner_middle, stages[1]))
+            outer_far = lax.ppermute(inner_middle, "dom", [(1, 0), (2, 3)])
+    if line:
+        blocks = [private_caches, near, inner_middle, far, outer_middle, outer_far]
 
     count = len(routes)
     rows = local * heads
-    results = pl.pallas_call(
-        functools.partial(suffix_kernel, count, len(blocks), inner, heads),
-        out_shape=(jax.ShapeDtypeStruct(private_caches.shape, BF16),)
-        + (jax.ShapeDtypeStruct((rows, rank + LANES), BF16),) * count,
+    packed_rows = jax.ShapeDtypeStruct((chips * rows, rank + LANES), BF16)
+    new_caches, keep, give = pl.pallas_call(
+        functools.partial(suffix_kernel, count, len(blocks), line, heads),
+        out_shape=(jax.ShapeDtypeStruct(private_caches.shape, BF16), packed_rows, packed_rows),
         in_specs=[SMEM] * 3 + [VMEM] * (1 + count + len(stages)) + [ANY] * len(blocks),
-        out_specs=(VMEM,) * (1 + count),
+        out_specs=(VMEM,) * 3,
         scratch_shapes=[
             pltpu.VMEM((local, span, width), BF16),
             pltpu.SemaphoreType.DMA((local,)),
@@ -243,16 +242,23 @@
         compiler_params=PARAMS,
         name="suffix_attention",
     )(ancestors, lengths, place, new_latent, *queries, *stages, *blocks)
-    new_caches, parts = results[0], results[1:]
-
-    parts = [
-        part if r == (0, 0) else lax.ppermute(part, "seq", [(b, a) for a, b in pairs(*r)])
-        for r, part in zip(routes, parts)
+
+    got = lax.ppermute(give, "seq", pairs(0, 1))
+    parts = pl.pallas_call(
+        functools.partial(chip_kernel, chips),
+        out_shape=[jax.ShapeDtypeStruct((rows, rank + LANES), BF16)] * chips,
+        in_specs=[VMEM] * 2,
+        out_specs=[VMEM] * chips,
+        compiler_params=PARAMS,
+        name="chip_merge",
+    )(keep, got)
+    parts = [parts[0]] + [
+        lax.ppermute(parts[t], "seq", [(b, a) for a, b in pairs(t, 0)]) for t in range(1, chips)
     ]
     latent_out = pl.pallas_call(
-        functools.partial(merge_kernel, count),
+        final_kernel,
         out_shape=jax.ShapeDtypeStruct((rows, rank), BF16),
-        in_specs=[VMEM] * count,
+        in_specs=[VMEM] * chips,
         out_specs=VMEM,
         compiler_params=PARAMS,
         name="merge",

time: 63.1 us -> 52.1 us (0.83)
  starting transfers between devices: 15.8 us -> 9.43 us
  waiting for transfers between devices: 26.1 us -> 23.3 us
  Pallas kernels: 12.5 us -> 11.6 us
  local copies, waits for them, and re-layouts: 3.85 us -> 3.04 us
    ppermute x7 -> x6, starting transfers between devices: 13.1 us -> 6.89 us  [the longest x1 3.09 us: on_device(): near = lax.ppermute(private_caches, 'dom', [(0, 1), (1, 0), (2, 3), (3, 2)])]
    ppermute x7 -> x6, waiting for transfers between devices: 26.1 us -> 21.9 us  [the longest x1 7.62 us: on_device(): outer_far = lax.ppermute(inner_middle, 'dom', [(1, 0), (2, 3)])]
    ppermute x3, waiting for transfers between devices: 0.01 us -> 1.39 us  [on_device(): lax.ppermute(own, 'seq', pairs(*r))]
    pallas_call x3, Pallas kernels: 4.58 us -> 3.71 us  [the longest x1 3.26 us: on_device(): pl.pallas_call(functools.partial(suffix_kernel, count, len(blocks), line,...]
    unnamed x16 -> x18, local copies, waits for them, and re-layouts: 3.83 us -> 3.02 us
  transfers between devices with their start and end apart: 11 -> 10, of which waited for: 4 -> 6; matrix products, arithmetic and copies ran while one was open for 0% -> 6% of each run, Pallas kernels for 14% -> 15%
where the time goes in v3:
time: 52.1 us; the launch traced here: 51.8 us
  waiting for transfers between devices  23.3 us (45%)
  Pallas kernels  11.6 us (22%)
  starting transfers between devices  9.43 us (18%)
  matrix products  3.49 us (7%)
  local copies, waits for them, and re-layouts  3.04 us (6%)
  between operations  0.83 us (2%)
    pallas_call x2, Pallas kernels, prefix_attention(): pl.pallas_call(functools.partial(prefix_kernel, len(queries), tiles), out...  7.87 us
    ppermute x1, waiting for transfers between devices, on_device(): outer_far = lax.ppermute(inner_middle, 'dom', [(1, 0), (2, 3)])  7.62 us
    ppermute x1, waiting for transfers between devices, on_device(): lax.ppermute(parts[t], 'seq', [(b, a) for a, b in pairs(t, 0)])  5.82 us
    ppermute x1, waiting for transfers between devices, on_device(): outer_middle = lax.ppermute(far, 'dom', [(1, 0), (2, 3)])  4.04 us
    pallas_call x1, Pallas kernels, on_device(): pl.pallas_call(functools.partial(suffix_kernel, count, len(blocks), line,...  3.26 us
    ppermute x1, starting transfers between devices, on_device(): near = lax.ppermute(private_caches, 'dom', [(0, 1), (1, 0), (2, 3), (3, 2)])  3.09 us
    unnamed x18, local copies, waits for them, and re-layouts  3.02 us
    dot_general x1, matrix products, on_device(): jnp.einsum('phn,hnc->phc', q_nope, w_uk, preferred_element_type=F32)  2.83 us
  transfers between devices with their start and end apart: 10, of which 6 were waited for; matrix products, arithmetic and copies ran while one was open for 6% of the time, Pallas kernels for 15%

profile of v3, /device:TPU:0, one launch (start us, length us, event | category | flops | bytes accessed | tf_op | source)
XLA Modules:
  0.0 51.8 jit_solution(16848124737522472779)
XLA Ops:
  0.7 3.1 %collective-permute-start = (bf16[4,64,576]{2,1,0:T(8,128)(2,1)}, bf16[4,64,576]{2,1,0:T(8,128)(2,1)S(1)}, u32[]{:S(2)}, u32[]{:S(2)}) collective-permute-start(bf16[4,64,576]{2,1,0:T(8,128)(2,1)} %refs_14_.1), channel_id=1, source_target_pairs={{0,1},{1,0},{2,3},{3,2},{4,5},{5,4},{6,7},{7,6},{8,9},{9,8},{10,11... | collective-permute-start | bytes 884744 | tf_op jit(solution)/shard_map/ppermute | solution.py:196
  3.7 0.7 %collective-permute-start.1 = (bf16[4,64,576]{2,1,0:T(8,128)(2,1)}, bf16[4,64,576]{2,1,0:T(8,128)(2,1)S(1)}, u32[]{:S(2)}, u32[]{:S(2)}) collective-permute-start(bf16[4,64,576]{2,1,0:T(8,128)(2,1)} %refs_14_.1), channel_id=1, source_target_pairs={{1,2},{2,1},{5,6},{6,5},{9,10},{10,9},{13,14},{14,13},{17,18},{18,... | collective-permute-start | bytes 884744 | tf_op jit(solution)/shard_map/ppermute | solution.py:197
  4.4 2.8 %fusion = bf16[4,32,512]{2,0,1:T(4,128)(2,1)S(1)} fusion(bf16[32,128,512]{2,1,0:T(8,128)(2,1)} %param.11, bf16[4,32,128]{2,1,0:T(8,128)(2,1)S(1)} %copy-done), kind=kOutput, calls=%fused_computation.1 | convolution fusion | flops 16842752 | bytes 4358144 | tf_op jit(solution)/shard_map/phn,hnc->phc/dot_general | solution.py:204
  7.3 0.1 pad_maximum_fusion
  7.5 1.4 %collective-permute-done.2.refs_1_.refs_5_ = bf16[128,576]{1,0:T(8,128)(2,1)S(1)} collective-permute-done((bf16[128,576]{1,0:T(8,128)(2,1)S(1)}, bf16[128,576]{1,0:T(8,128)(2,1)S(1)}, u32[]{:S(2)}, u32[]{:S(2)}) %collective-permute-start.2) | collective-permute-done | bytes 147488 | tf_op jit(solution)/shard_map/ppermute | solution.py:215
  8.9 2.8 %collective-permute-done.refs_15_ = bf16[4,64,576]{2,1,0:T(8,128)(2,1)S(1)} collective-permute-done((bf16[4,64,576]{2,1,0:T(8,128)(2,1)}, bf16[4,64,576]{2,1,0:T(8,128)(2,1)S(1)}, u32[]{:S(2)}, u32[]{:S(2)}) %collective-permute-start) | collective-permute-done | bytes 294944 | tf_op jit(solution)/shard_map/ppermute | solution.py:196
  11.7 0.7 %collective-permute-start.5 = (bf16[4,64,576]{2,1,0:T(8,128)(2,1)S(1)}, bf16[4,64,576]{2,1,0:T(8,128)(2,1)S(1)}, u32[]{:S(2)}, u32[]{:S(2)}) collective-permute-start(bf16[4,64,576]{2,1,0:T(8,128)(2,1)S(1)} %collective-permute-done.refs_15_), channel_id=1, source_target_pairs={{1,2},{2,1},{5,6},{6,5},{9,10},{10,9},{13,14},{14,13},{17,18},{18,... | collective-permute-start | bytes 884744 | tf_op jit(solution)/shard_map/ppermute | solution.py:219
  12.3 0.3 collective-permute-start.4
  12.6 1.5 %collective-permute-start.3 = (bf16[128,576]{1,0:T(8,128)(2,1)S(1)}, bf16[128,576]{1,0:T(8,128)(2,1)S(1)}, u32[]{:S(2)}, u32[]{:S(2)}) collective-permute-start(bf16[128,576]{1,0:T(8,128)(2,1)S(1)} %bitcast.13), channel_id=1, source_target_pairs={{0,8},{4,12},{8,0},{12,4},{1,9},{5,13},{9,1},{13,5},{2,10},{6,14},... | collective-permute-start | bytes 442376 | tf_op jit(solution)/shard_map/ppermute | solution.py:215
  14.1 1.3 %collective-permute-start.6 = (bf16[4,64,576]{2,1,0:T(8,128)(2,1)S(1)}, bf16[4,64,576]{2,1,0:T(8,128)(2,1)S(1)}, u32[]{:S(2)}, u32[]{:S(2)}) collective-permute-start(bf16[4,64,576]{2,1,0:T(8,128)(2,1)S(1)} %collective-permute-done.1.refs_17_), channel_id=1, source_target_pairs={{1,0},{2,3},{5,4},{6,7},{9,8},{10,11},{13,12},{14,15},{17,16},{18,... | collective-permute-start | bytes 884744 | tf_op jit(solution)/shard_map/ppermute | solution.py:220
  15.4 2.3 %copy-done.5 = bf16[4096,576]{0,1:T(8,128)(2,1)S(1)} copy-done((bf16[4096,576]{0,1:T(8,128)(2,1)S(1)}, bf16[4096,576]{0,1:T(8,128)(2,1)}, u32[]{:S(2)}) %copy-start.5) | copy-done | bytes 4718616
  17.8 3.9 %prefix_attention.2 = (f32[256,512]{1,0:T(8,128)S(1)}, f32[256,128]{1,0:T(8,128)S(1)}, f32[256,128]{1,0:T(8,128)S(1)}) custom-call(bf16[128,576]{1,0:T(8,128)(2,1)S(1)} %bitcast.14, bf16[128,576]{1,0:T(8,128)(2,1)S(1)} %collective-permute-done.2.refs_1_.refs_5_, bf16[576,4096]{1,0:T(8,128)(2,1)S(1)} %bitcast.17), custom_call_target="tpu_custom_call" | custom-call | flops 2281701376 | bytes 4718592 | tf_op jit(solution)/shard_map/prefix_attention/pallas_call | solution.py:57
  21.7 1.3 %collective-permute-start.7 = (bf16[4,64,576]{2,1,0:T(8,128)(2,1)S(1)}, bf16[4,64,576]{2,1,0:T(8,128)(2,1)S(1)}, u32[]{:S(2)}, u32[]{:S(2)}) collective-permute-start(bf16[4,64,576]{2,1,0:T(8,128)(2,1)S(1)} %collective-permute-done.5.refs_16_), channel_id=1, source_target_pairs={{1,0},{2,3},{5,4},{6,7},{9,8},{10,11},{13,12},{14,15},{17,16},{18,... | collective-permute-start | bytes 884744 | tf_op jit(solution)/shard_map/ppermute | solution.py:226
  23.1 3.9 %prefix_attention.3 = (f32[256,512]{1,0:T(8,128)S(1)}, f32[256,128]{1,0:T(8,128)S(1)}, f32[256,128]{1,0:T(8,128)S(1)}) custom-call(bf16[128,576]{1,0:T(8,128)(2,1)S(1)} %collective-permute-done.3.refs_0_.refs_6_, bf16[128,576]{1,0:T(8,128)(2,1)S(1)} %collective-permute-done.4.refs_1_.refs_7_, bf16[576,4096]{1,0:T(8,128)(2,1)S(1)} %bitcast.18), custom_call_target="tpu_custom_call" | custom-call | flops 2281701376 | bytes 4718592 | tf_op jit(solution)/shard_map/prefix_attention/pallas_call | solution.py:57
  27.1 4.0 %collective-permute-done.6.refs_18_ = bf16[4,64,576]{2,1,0:T(8,128)(2,1)S(1)} collective-permute-done((bf16[4,64,576]{2,1,0:T(8,128)(2,1)S(1)}, bf16[4,64,576]{2,1,0:T(8,128)(2,1)S(1)}, u32[]{:S(2)}, u32[]{:S(2)}) %collective-permute-start.6) | collective-permute-done | bytes 294944 | tf_op jit(solution)/shard_map/ppermute | solution.py:220
  31.1 7.6 %collective-permute-done.7.refs_19_ = bf16[4,64,576]{2,1,0:T(8,128)(2,1)S(1)} collective-permute-done((bf16[4,64,576]{2,1,0:T(8,128)(2,1)S(1)}, bf16[4,64,576]{2,1,0:T(8,128)(2,1)S(1)}, u32[]{:S(2)}, u32[]{:S(2)}) %collective-permute-start.7) | collective-permute-done | bytes 294944 | tf_op jit(solution)/shard_map/ppermute | solution.py:226
  38.8 3.3 %suffix_attention.1 = (bf16[4,64,576]{2,1,0:T(8,128)(2,1)}, bf16[256,640]{1,0:T(8,128)(2,1)S(1)}, bf16[256,640]{1,0:T(8,128)(2,1)S(1)}) custom-call(s32[4]{0:T(128)S(1)} %copy-done.3, s32[16]{0:T(128)S(1)} %copy-done.4, s32[2]{0:T(128)S(1)} %pad_add_fusion.refs_2_, bf16[4,576]{1,0:T(4,128)(2,1)S(1)} %copy-done.2, bf16[128,576]{1,0:T(8,128)(2,1)S(1)} %bitcast.15, ...), custom_call_target="tpu_custom_call" | custom-call | tf_op jit(solution)/shard_map/suffix_attention/pallas_call | solution.py:233
  42.1 1.6 %collective-permute-done.8.got_ref = bf16[256,640]{1,0:T(8,128)(2,1)S(1)} collective-permute-done((bf16[256,640]{1,0:T(8,128)(2,1)S(1)}, bf16[256,640]{1,0:T(8,128)(2,1)S(1)}, u32[]{:S(2)}, u32[]{:S(2)}) %collective-permute-start.8) | collective-permute-done | bytes 327712 | tf_op jit(solution)/shard_map/ppermute | solution.py:246
  43.7 0.3 chip_merge.1
  44.0 0.5 collective-permute-start.9
  44.5 5.8 %collective-permute-done.9.refs_1_ = bf16[128,640]{1,0:T(8,128)(2,1)S(1)} collective-permute-done((bf16[128,640]{1,0:T(8,128)(2,1)S(1)}, bf16[128,640]{1,0:T(8,128)(2,1)S(1)}, u32[]{:S(2)}, u32[]{:S(2)}) %collective-permute-start.9) | collective-permute-done | bytes 163872 | tf_op jit(solution)/shard_map/ppermute | solution.py:256
  50.3 0.2 merge.1
  50.5 0.7 %fusion.1 = bf16[4,32,128]{2,0,1:T(4,128)(2,1)S(1)} fusion(bf16[32,512,128]{2,1,0:T(8,128)(2,1)S(1)} %copy-done.6, bf16[4,32,512]{2,1,0:T(8,128)(2,1)S(1)} %bitcast.16), kind=kOutput, calls=%fused_computation.3 | convolution fusion | flops 16793600 | bytes 4358144 | tf_op jit(solution)/shard_map/phc,hcv->phv/dot_general | solution.py:266
  51.2 0.6 %copy.15 = bf16[4,32,128]{2,1,0:T(8,128)(2,1)} copy(bf16[4,32,128]{2,0,1:T(4,128)(2,1)S(1)} %fusion.1) | data formatting | bytes 65536
  (24 shorter events, 0.3 us)
Async XLA Ops:
  0.6 3.8 %copy-start = (bf16[4,32,128]{2,1,0:T(8,128)(2,1)S(1)}, bf16[4,32,128]{2,1,0:T(8,128)(2,1)}, u32[]{:S(2)}) copy-start(bf16[4,32,128]{2,1,0:T(8,128)(2,1)} %param.9) | copy-start | bytes 98308
  0.6 6.6 %copy-start.7 = (bf16[4,32,64]{2,1,0:T(8,128)(2,1)S(1)}, bf16[4,32,64]{2,1,0:T(8,128)(2,1)}, u32[]{:S(2)}) copy-start(bf16[4,32,64]{2,1,0:T(8,128)(2,1)} %param.10) | copy-start | bytes 49156
  0.7 11.0 %collective-permute-start = (bf16[4,64,576]{2,1,0:T(8,128)(2,1)}, bf16[4,64,576]{2,1,0:T(8,128)(2,1)S(1)}, u32[]{:S(2)}, u32[]{:S(2)}) collective-permute-start(bf16[4,64,576]{2,1,0:T(8,128)(2,1)} %refs_14_.1), channel_id=1, source_target_pairs={{0,1},{1,0},{2,3},{3,2},{4,5},{5,4},{6,7},{7,6},{8,9},{9,8},{10,11... | collective-permute-start | bytes 884744 | tf_op jit(solution)/shard_map/ppermute | solution.py:196
  3.7 7.9 %collective-permute-start.1 = (bf16[4,64,576]{2,1,0:T(8,128)(2,1)}, bf16[4,64,576]{2,1,0:T(8,128)(2,1)S(1)}, u32[]{:S(2)}, u32[]{:S(2)}) collective-permute-start(bf16[4,64,576]{2,1,0:T(8,128)(2,1)} %refs_14_.1), channel_id=1, source_target_pairs={{1,2},{2,1},{5,6},{6,5},{9,10},{10,9},{13,14},{14,13},{17,18},{18,... | collective-permute-start | bytes 884744 | tf_op jit(solution)/shard_map/ppermute | solution.py:197
  7.4 1.5 %collective-permute-start.2 = (bf16[128,576]{1,0:T(8,128)(2,1)S(1)}, bf16[128,576]{1,0:T(8,128)(2,1)S(1)}, u32[]{:S(2)}, u32[]{:S(2)}) collective-permute-start(bf16[128,576]{1,0:T(8,128)(2,1)S(1)} %bitcast.11), channel_id=1, source_target_pairs={{0,4},{4,0},{8,12},{12,8},{1,5},{5,1},{9,13},{13,9},{2,6},{6,2},{1... | collective-permute-start | bytes 442376 | tf_op jit(solution)/shard_map/ppermute | solution.py:215
  11.7 10.1 %collective-permute-start.5 = (bf16[4,64,576]{2,1,0:T(8,128)(2,1)S(1)}, bf16[4,64,576]{2,1,0:T(8,128)(2,1)S(1)}, u32[]{:S(2)}, u32[]{:S(2)}) collective-permute-start(bf16[4,64,576]{2,1,0:T(8,128)(2,1)S(1)} %collective-permute-done.refs_15_), channel_id=1, source_target_pairs={{1,2},{2,1},{5,6},{6,5},{9,10},{10,9},{13,14},{14,13},{17,18},{18,... | collective-permute-start | bytes 884744 | tf_op jit(solution)/shard_map/ppermute | solution.py:219
  12.3 10.8 %collective-permute-start.4 = (bf16[128,576]{1,0:T(8,128)(2,1)S(1)}, bf16[128,576]{1,0:T(8,128)(2,1)S(1)}, u32[]{:S(2)}, u32[]{:S(2)}) collective-permute-start(bf16[128,576]{1,0:T(8,128)(2,1)S(1)} %bitcast.12), channel_id=1, source_target_pairs={{0,12},{4,8},{8,4},{12,0},{1,13},{5,9},{9,5},{13,1},{2,14},{6,10},... | collective-permute-start | bytes 442376 | tf_op jit(solution)/shard_map/ppermute | solution.py:215
  12.6 10.5 %collective-permute-start.3 = (bf16[128,576]{1,0:T(8,128)(2,1)S(1)}, bf16[128,576]{1,0:T(8,128)(2,1)S(1)}, u32[]{:S(2)}, u32[]{:S(2)}) collective-permute-start(bf16[128,576]{1,0:T(8,128)(2,1)S(1)} %bitcast.13), channel_id=1, source_target_pairs={{0,8},{4,12},{8,0},{12,4},{1,9},{5,13},{9,1},{13,5},{2,10},{6,14},... | collective-permute-start | bytes 442376 | tf_op jit(solution)/shard_map/ppermute | solution.py:215
  14.1 17.0 %collective-permute-start.6 = (bf16[4,64,576]{2,1,0:T(8,128)(2,1)S(1)}, bf16[4,64,576]{2,1,0:T(8,128)(2,1)S(1)}, u32[]{:S(2)}, u32[]{:S(2)}) collective-permute-start(bf16[4,64,576]{2,1,0:T(8,128)(2,1)S(1)} %collective-permute-done.1.refs_17_), channel_id=1, source_target_pairs={{1,0},{2,3},{5,4},{6,7},{9,8},{10,11},{13,12},{14,15},{17,16},{18,... | collective-permute-start | bytes 884744 | tf_op jit(solution)/shard_map/ppermute | solution.py:220
  15.4 2.3 %copy-start.5 = (bf16[4096,576]{0,1:T(8,128)(2,1)S(1)}, bf16[4096,576]{0,1:T(8,128)(2,1)}, u32[]{:S(2)}) copy-start(bf16[4096,576]{0,1:T(8,128)(2,1)} %param.13) | copy-start | bytes 14155780
  21.7 17.0 %collective-permute-start.7 = (bf16[4,64,576]{2,1,0:T(8,128)(2,1)S(1)}, bf16[4,64,576]{2,1,0:T(8,128)(2,1)S(1)}, u32[]{:S(2)}, u32[]{:S(2)}) collective-permute-start(bf16[4,64,576]{2,1,0:T(8,128)(2,1)S(1)} %collective-permute-done.5.refs_16_), channel_id=1, source_target_pairs={{1,0},{2,3},{5,4},{6,7},{9,8},{10,11},{13,12},{14,15},{17,16},{18,... | collective-permute-start | bytes 884744 | tf_op jit(solution)/shard_map/ppermute | solution.py:226
  23.1 15.6 %copy-start.1 = (bf16[4,64,576]{2,1,0:T(8,128)(2,1)S(1)}, bf16[4,64,576]{2,1,0:T(8,128)(2,1)}, u32[]{:S(2)}) copy-start(bf16[4,64,576]{2,1,0:T(8,128)(2,1)} %refs_14_.1) | copy-start | bytes 884740
  23.1 15.6 %copy-start.2 = (bf16[4,576]{1,0:T(4,128)(2,1)S(1)}, bf16[4,576]{1,0:T(4,128)(2,1)}, u32[]{:S(2)}) copy-start(bf16[4,576]{1,0:T(4,128)(2,1)} %refs_3_.1) | copy-start | bytes 13828
  23.1 15.6 %copy-start.3 = (s32[4]{0:T(128)S(1)}, s32[4]{0:T(128)}, u32[]{:S(2)}) copy-start(s32[4]{0:T(128)} %refs_0_.1) | copy-start | bytes 52
  23.1 15.6 %copy-start.4 = (s32[16]{0:T(128)S(1)}, s32[16]{0:T(128)}, u32[]{:S(2)}) copy-start(s32[16]{0:T(128)} %refs_1_.1) | copy-start | bytes 196
  27.1 23.4 %copy-start.6 = (bf16[32,512,128]{2,1,0:T(8,128)(2,1)S(1)}, bf16[32,512,128]{2,1,0:T(8,128)(2,1)}, u32[]{:S(2)}) copy-start(bf16[32,512,128]{2,1,0:T(8,128)(2,1)} %param.12) | copy-start | bytes 12582916
  42.0 1.7 %collective-permute-start.8 = (bf16[256,640]{1,0:T(8,128)(2,1)S(1)}, bf16[256,640]{1,0:T(8,128)(2,1)S(1)}, u32[]{:S(2)}, u32[]{:S(2)}) collective-permute-start(bf16[256,640]{1,0:T(8,128)(2,1)S(1)} %get-tuple-element.30), channel_id=1, source_target_pairs={{0,4},{4,0},{8,12},{12,8},{1,5},{5,1},{9,13},{13,9},{2,6},{6,2},{1... | collective-permute-start | bytes 983048 | tf_op jit(solution)/shard_map/ppermute | solution.py:246
  44.0 6.3 %collective-permute-start.9 = (bf16[128,640]{1,0:T(8,128)(2,1)S(1)}, bf16[128,640]{1,0:T(8,128)(2,1)S(1)}, u32[]{:S(2)}, u32[]{:S(2)}) collective-permute-start(bf16[128,640]{1,0:T(8,128)(2,1)S(1)} %get-tuple-element.32), channel_id=1, source_target_pairs={{8,0},{12,4},{0,8},{4,12},{9,1},{13,5},{1,9},{5,13},{10,2},{14,6},... | collective-permute-start | bytes 491528 | tf_op jit(solution)/shard_map/ppermute | solution.py:256

commit v4 on v3

v4 whole, which is shorter than its diff:
```python
import functools
import math

import jax
import jax.numpy as jnp
from jax import lax
from jax.experimental import pallas as pl
from jax.experimental.pallas import tpu as pltpu
from jax.sharding import PartitionSpec as P

ROPE = 64
NOPE = 128
SCALE2 = (NOPE + ROPE) ** (-0.5) * math.log2(math.e)
HIDDEN = -1e30
LANES = 128
F32 = jnp.float32
BF16 = jnp.bfloat16
NT = (((1,), (1,)), ((), ()))

VMEM = pl.BlockSpec(memory_space=pltpu.VMEM)
SMEM = pl.BlockSpec(memory_space=pltpu.SMEM)
ANY = pl.BlockSpec(memory_space=pl.ANY)
HBM = pl.BlockSpec(memory_space=pltpu.HBM)
PARAMS = pltpu.CompilerParams(vmem_limit_bytes=40 * 1024 * 1024)
STREAM = pltpu.CompilerParams(vmem_limit_bytes=51 * 1024 * 1024)


def shape(dims, dtype=BF16):
    return jax.ShapeDtypeStruct(dims, dtype)


def pack_kernel(rank, cache_ref, out_ref):
    local, span, width = cache_ref.shape
    for p in range(local):
        out_ref[pl.ds(p * span, span)] = cache_ref[p, :, :rank]
    rope = jnp.concatenate([cache_ref[p, :, rank:] for p in range(local)], axis=1)
    tail = out_ref.shape[0] - local * span
    out_ref[pl.ds(local * span, tail)] = jnp.concatenate(
        [rope[i : i + tail] for i in range(0, span, tail)], axis=1
    )


def project_kernel(
    pieces, nope_ref, rope_ref, w_hbm, own_ref, nope, turned, w_ref, sems
):
    local, heads = nope_ref.shape[:2]
    rank = w_ref.shape[2]
    piece = heads // pieces
    fetches = [
        pltpu.make_async_copy(
            w_hbm.at[pl.ds(i * piece, piece)], w_ref.at[pl.ds(i * piece, piece)], sems.at[i]
        )
        for i in range(pieces)
    ]
    for fetch in fetches:
        fetch.start()
    for p in range(local):
        nope[pl.ds(p, heads, stride=local), :] = nope_ref[p].astype(F32)
        wide = rope_ref[p].astype(F32)
        wide = jnp.concatenate([wide, jnp.zeros((heads, LANES - wide.shape[1]), F32)], axis=1)
        turned[pl.ds(p, heads, stride=local), :] = wide
    width = nope.shape[1]
    first = lax.broadcasted_iota(jnp.int32, (2 * local, width), 0) < local

    def pair(h):
        two = nope[pl.ds(h * local, 2 * local), :]
        left = jnp.concatenate([jnp.where(first, two, 0.0), jnp.where(first, 0.0, two)], axis=1)
        weights = w_ref[pl.ds(h, 2)].reshape(2 * width, rank)
        return jnp.dot(left.astype(BF16), weights, preferred_element_type=F32)

    own_ref[:, rank:] = turned[:, : rope_ref.shape[2]].astype(BF16)
    for h in range(0, heads, 4):
        if h % piece == 0:
            fetches[h // piece].wait()
        own_ref[pl.ds(h * local, 4 * local), :rank] = jnp.concatenate(
            [pair(i) for i in (h, h + 2)], axis=0
        ).astype(BF16)


def prefix_kernel(count, tiles, *refs):
    query_refs = refs[:count]
    keys_hbm, acc_ref, max_ref, sum_ref, keys_ref, sems = refs[count:]
    rank = acc_ref.shape[1]
    tile = keys_ref.shape[1] // tiles

    def fetch(i):
        part = pl.ds(i * tile, tile)
        return pltpu.make_async_copy(keys_hbm.at[:, part], keys_ref.at[:, part], sems.at[i])

    for i in range(tiles):
        fetch(i).start()
    queries = jnp.concatenate([ref[...] for ref in query_refs], axis=0)
    for i in range(tiles):
        part = pl.ds(i * tile, tile)
        fetch(i).wait()
        scores = jnp.dot(queries, keys_ref[:, part], preferred_element_type=F32) * SCALE2
        top = jnp.max(scores, axis=1, keepdims=True)
        if i > 0:
            top = jnp.maximum(top, largest)
        weights = jnp.exp2(scores - top)
        total = jnp.sum(weights, axis=1, keepdims=True)
        acc = lax.dot_general(
            weights.astype(BF16), keys_ref[:rank, part], NT, preferred_element_type=F32
        )
        if i > 0:
            factor = jnp.exp2(largest - top)
            total = total + running * factor
            acc = acc + acc_ref[...] * factor
        largest, running = top, total
        acc_ref[...] = acc
    max_ref[...] = jnp.broadcast_to(largest, max_ref.shape)
    sum_ref[...] = jnp.broadcast_to(running, sum_ref.shape)


def prefix_attention(queries, keys, rank, tiles=4):
    rows = sum(q.shape[0] for q in queries)
    width, length = keys.shape
    stat = shape((rows, LANES), F32)
    return pl.pallas_call(
        functools.partial(prefix_kernel, len(queries), tiles),
        out_shape=(shape((rows, rank), F32), stat, stat),
        in_specs=[VMEM] * len(queries) + [HBM],
        out_specs=(VMEM,) * 3,
        scratch_shapes=[pltpu.VMEM(keys.shape, BF16), pltpu.SemaphoreType.DMA((tiles,))],
        compiler_params=STREAM,
        cost_estimate=pl.CostEstimate(
            flops=2 * rows * length * (width + rank),
            bytes_accessed=2 * width * length,
            transcendentals=rows * length,
        ),
        name="prefix_attention",
    )(*queries, keys)


def packed(values, level):
    rows = values.shape[0]
    lane = lax.broadcasted_iota(jnp.int32, (rows, LANES), 1)
    high = level.astype(BF16).astype(F32)
    middle = (level - high).astype(BF16).astype(F32)
    low = level - high - middle
    stats = jnp.where(lane == 0, high, jnp.where(lane == 1, middle, jnp.where(lane == 2, low, 0.0)))
    return jnp.concatenate([values.astype(BF16), stats.astype(BF16)], axis=1)


def merged(parts, rank):
    levels = [jnp.sum(part[:, rank:].astype(F32), axis=1, keepdims=True) for part in parts]
    top = functools.reduce(jnp.maximum, levels)
    shares = [jnp.exp2(level - top) for level in levels]
    whole = functools.reduce(jnp.add, shares)
    acc = functools.reduce(
        jnp.add, [share * part[:, :rank].astype(F32) for share, part in zip(shares, parts)]
    )
    return acc * (1.0 / whole), top + jnp.log2(whole)


def attend_suffix(refs, latents, ropes, ends, start, span, keep_ref, give_ref):
    local = len(ends)
    first_ref, second_ref, acc_ref, max_ref, sum_ref = refs
    rows, rank = acc_ref.shape
    half, cols = rows // 2, local * span
    col = lax.broadcasted_iota(jnp.int32, (1, cols), 1)
    col_of = jnp.zeros_like(col)
    limit = jnp.full_like(col, ends[0] - start)
    for p in range(1, local):
        col_of = col_of + (col >= p * span).astype(jnp.int32)
        limit = jnp.where(col >= p * span, ends[p] - start + p * span, limit)
    col_of = jnp.where(col < limit, col_of, -1)
    row_of = lax.rem(lax.broadcasted_iota(jnp.int32, (rows, 1), 0), local)
    seen = row_of == col_of

    queries = jnp.concatenate([first_ref[...], second_ref[...]], axis=0)
    scores = lax.dot_general(queries[:, :rank], latents, NT, preferred_element_type=F32)
    scores = scores + lax.dot_general(queries[:, rank:], ropes, NT, preferred_element_type=F32)
    scores = jnp.where(seen, scores * SCALE2, HIDDEN)
    before = max_ref[:, 0:1]
    top = jnp.maximum(before, jnp.max(scores, axis=1, keepdims=True))
    weights = jnp.where(seen, jnp.exp2(scores - top), 0.0)
    factor = jnp.exp2(before - top)
    total = sum_ref[:, 0:1] * factor + jnp.sum(weights, axis=1, keepdims=True)
    acc = acc_ref[...] * factor + jnp.dot(weights.astype(BF16), latents, preferred_element_type=F32)
    part = packed(acc * (1.0 / total), top + jnp.log2(total))
    keep_ref[...] = part[:half]
    give_ref[...] = part[half:]


def far_kernel(stages, sources, line, *refs):
    anc, lens, place = refs[:3]
    refs = refs[3:]
    stage_refs, refs = refs[: 5 * stages], refs[5 * stages :]
    block_refs, refs = refs[:sources], refs[sources:]
    moved_ref, rope_ref, refs = refs[0], refs[1], refs[2:]
    keep_refs, give_refs = refs[:stages], refs[stages : 2 * stages]
    folded, sems = refs[2 * stages :]
    local, tail, rank = folded.shape
    span = moved_ref.shape[0] // local
    rope = rope_ref.shape[1]

    def copies(p, k, slot):
        return (
            pltpu.make_async_copy(
                block_refs[k].at[pl.ds(pl.multiple_of(slot * span, span), span)],
                moved_ref.at[pl.ds(p * span, span)],
                sems.at[p],
            ),
            pltpu.make_async_copy(
                block_refs[k].at[pl.ds(local * span, tail)], folded.at[p], sems.at[local + p]
            ),
        )

    slots = []
    for p in range(local):
        owner = lax.div(anc[p], local)
        slots.append(lax.rem(anc[p], local))
        if line:
            apart = jnp.bitwise_xor(owner, place[1])
            at_end = (place[1] == 0) | (place[1] == 3)
            which = jnp.where(at_end & (apart > 1), apart + 2, apart)
        else:
            which = lax.rem(place[1] - owner + sources, sources)
        for k in range(sources):

            @pl.when(which == k)
            def _():
                for copy in copies(p, k, slots[p]):
                    copy.start()

    for p in range(local):
        for copy in copies(p, 0, 0):
            copy.wait()

    for p in range(local):
        for i in range(span // tail):
            from_slot = [
                folded[p, :, (i * local + q) * rope : (i * local + q + 1) * rope] for q in range(local)
            ]
            picked = from_slot[0]
            for q in range(1, local):
                picked = jnp.where(slots[p] == q, from_slot[q], picked)
            rope_ref[pl.ds(p * span + i * tail, tail)] = picked

    ends = [lens[anc[p]] for p in range(local)]
    for k in range(stages):
        attend_suffix(
            stage_refs[5 * k : 5 * k + 5],
            moved_ref[...],
            rope_ref[...],
            ends,
            place[0] * span,
            span,
            keep_refs[k],
            give_refs[k],
        )


def near_kernel(anc, lens, place, fresh_ref, *refs):
    stage_refs = refs[:5]
    moved_ref, rope_ref, cache_ref, keep_ref, give_ref = refs[5:]
    local, span, width = cache_ref.shape
    rank = moved_ref.shape[1]
    start = place[0] * span
    ends = [lens[anc[p]] for p in range(local)]
    attend_suffix(
        stage_refs, moved_ref[...], rope_ref[...], ends, start, span, keep_ref, give_ref
    )
    for p in range(local):
        at = start + lax.broadcasted_iota(jnp.int32, (span, 1), 0) == ends[p]
        part = pl.ds(p * span, span)
        cache_ref[p, :, :rank] = jnp.where(at, fresh_ref[pl.ds(p, 1), :rank], moved_ref[part])
        cache_ref[p, :, rank:] = jnp.where(at, fresh_ref[pl.ds(p, 1), rank:], rope_ref[part])


def chip_kernel(count, *refs):
    for k in range(count):
        out_ref = refs[2 * count + k]
        rank = out_ref.shape[1] - LANES
        out_ref[...] = packed(*merged([refs[k][...], refs[count + k][...]], rank))


def chip_merge(keep, got):
    return pl.pallas_call(
        functools.partial(chip_kernel, len(keep)),
        out_shape=[shape(k.shape) for k in keep],
        in_specs=[VMEM] * (2 * len(keep)),
        out_specs=[VMEM] * len(keep),
        compiler_params=PARAMS,
        name="chip_merge",
    )(*keep, *got)


def final_kernel(count, *refs):
    part_refs, (w_ref, out_ref, values) = refs[:count], refs[count:]
    heads, rank, reach = w_ref.shape
    local = out_ref.shape[0]
    latent = merged([ref[...] for ref in part_refs], rank)[0].astype(BF16)
    first = lax.broadcasted_iota(jnp.int32, (2 * local, reach), 0) < local
    for h in range(0, heads, 2):
        two = latent[h * local : (h + 2) * local]
        here = jnp.dot(two, w_ref[h], preferred_element_type=F32)
        there = jnp.dot(two, w_ref[h + 1], preferred_element_type=F32)
        values[pl.ds(h * local, 2 * local), :] = jnp.where(first, here, there)
    for p in range(local):
        out_ref[p] = values[pl.ds(p, heads, stride=local), :].astype(BF16)


def on_device(q_nope, q_rope, w_uk, w_uv, prefix, private_caches, new_latent, ancestors, lengths):
    local, heads, nope = q_nope.shape
    span, width = private_caches.shape[1:]
    rank, reach = w_uv.shape[1:]
    rope = width - rank
    rows = local * heads
    seq_size, dom_size = lax.axis_size("seq"), lax.axis_size("dom")
    cores = 2
    chips = seq_size // cores
    place = jnp.stack([lax.axis_index("seq"), lax.axis_index("dom")]).astype(jnp.int32)
    tail = span * local * rope // rank

    block = pl.pallas_call(
        functools.partial(pack_kernel, rank),
        out_shape=shape((local * span + tail, rank)),
        in_specs=[VMEM],
        out_specs=VMEM,
        compiler_params=PARAMS,
        name="pack",
    )(private_caches)
    line = dom_size == 4
    if line:
        near = lax.ppermute(block, "dom", [(0, 1), (1, 0), (2, 3), (3, 2)])
        far = lax.ppermute(block, "dom", [(1, 2), (2, 1)])
    else:
        blocks = [block] + [
            lax.ppermute(block, "dom", [(i, (i + k) % dom_size) for i in range(dom_size)])
            for k in range(1, dom_size)
        ]

    pieces = math.gcd(heads // 4, 4)
    own = pl.pallas_call(
        functools.partial(project_kernel, pieces),
        out_shape=shape((rows, width)),
        in_specs=[VMEM] * 2 + [HBM],
        out_specs=VMEM,
        scratch_shapes=[
            pltpu.VMEM((rows, nope), F32),
            pltpu.VMEM((rows, LANES), F32),
            pltpu.VMEM(w_uk.shape, BF16),
            pltpu.SemaphoreType.DMA((pieces,)),
        ],
        compiler_params=STREAM,
        name="project",
    )(q_nope, q_rope, w_uk)
    keys = prefix.T

    def pairs(turn, flip):
        return [
            (x * cores + c, (x + turn) % chips * cores + (c ^ flip))
            for x in range(chips)
            for c in range(cores)
        ]

    def back(turn, flip):
        return [(b, a) for a, b in pairs(turn, flip)]

    routes = [(t, f) for t in range(chips) for f in range(cores)]
    queries = [own if r == (0, 0) else lax.ppermute(own, "seq", pairs(*r)) for r in routes]
    if line:
        near, far, queries[1] = lax.optimization_barrier((near, far, queries[1]))
        inner_middle = lax.ppermute(near, "dom", [(1, 2), (2, 1)])
        outer_middle = lax.ppermute(far, "dom", [(1, 0), (2, 3)])
    stages = []
    for t in range(chips):
        stage = [*queries[2 * t : 2 * t + 2], *prefix_attention(queries[2 * t : 2 * t + 2], keys, rank)]
        stages.append(stage)
        if line and t == 0:
            inner_middle, stage[3] = lax.optimization_barrier((inner_middle, stage[3]))
            outer_far = lax.ppermute(inner_middle, "dom", [(1, 0), (2, 3)])
    if line:
        blocks = [block, near, inner_middle, far, outer_middle, outer_far]

    part = shape((rows, rank + LANES))
    others = chips - 1
    far_results = pl.pallas_call(
        functools.partial(far_kernel, others, len(blocks), line),
        out_shape=[shape((local * span, rank)), shape((local * span, rope))] + [part] * (2 * others),
        in_specs=[SMEM] * 3 + [VMEM] * (5 * others) + [ANY] * len(blocks),
        out_specs=[VMEM] * (2 + 2 * others),
        scratch_shapes=[
            pltpu.VMEM((local, tail, rank), BF16),
            pltpu.SemaphoreType.DMA((2 * local,)),
        ],
        compiler_params=PARAMS,
        name="suffix_far",
    )(ancestors, lengths, place, *[a for stage in stages[1:] for a in stage], *blocks)
    moved, moved_rope = far_results[:2]
    keep, give = far_results[2 : 2 + others], far_results[2 + others :]
    sums = chip_merge(keep, [lax.ppermute(g, "seq", pairs(0, 1)) for g in give])
    parts = [lax.ppermute(s, "seq", back(t, 0)) for t, s in enumerate(sums, 1)]

    new_caches, keep, give = pl.pallas_call(
        near_kernel,
        out_shape=[shape(private_caches.shape), part, part],
        in_specs=[SMEM] * 3 + [VMEM] * 8,
        out_specs=[VMEM] * 3,
        compiler_params=PARAMS,
        name="suffix_near",
    )(ancestors, lengths, place, new_latent, *stages[0], moved, moved_rope)
    parts += chip_merge([keep], [lax.ppermute(give, "seq", pairs(0, 1))])

    head_values = pl.pallas_call(
        functools.partial(final_kernel, chips),
        out_shape=shape((local, heads, reach)),
        in_specs=[VMEM] * (chips + 1),
        out_specs=VMEM,
        scratch_shapes=[pltpu.VMEM((rows, reach), F32)],
        compiler_params=PARAMS,
        name="final",
    )(*parts, w_uv)
    return (head_values, new_caches)


def solution(mesh):
    placed = (
        P(("group", "dom"), "seq", None),
        P(("group", "dom"), "seq", None),
        P("seq", None, None),
        P("seq", None, None),
        P(("group", "seq"), None),
        P(("group", "dom"), "seq", None),
        P(("group", "dom"), None),
        P(("group", "dom")),
        P("group"),
    )
    return jax.shard_map(
        on_device,
        mesh=mesh,
        in_specs=placed,
        out_specs=(P(("group", "dom"), "seq", None), P(("group", "dom"), "seq", None)),
        check_vma=False,
    )
```

time: 52.1 us -> 49.2 us (0.944)
  waiting for transfers between devices: 23.3 us -> 13.2 us
  Pallas kernels: 11.6 us -> 19.7 us
  matrix products: 3.49 us -> 0 us
  starting transfers between devices: 9.43 us -> 12.6 us
  local copies, waits for them, and re-layouts: 3.04 us -> 2.5 us
    pallas_call x3 -> x7, Pallas kernels: 3.71 us -> 8.37 us  [the longest x1 2.46 us: on_device(): pl.pallas_call(functools.partial(project_kernel, pieces), out_shape=shape...]
    ppermute x1, waiting for transfers between devices: 4.04 us -> 0.01 us  [on_device(): outer_middle = lax.ppermute(far, 'dom', [(1, 0), (2, 3)])]
    pallas_call x2, Pallas kernels: 7.87 us -> 11.4 us  [prefix_attention(): pl.pallas_call(functools.partial(prefix_kernel, len(queries), tiles), out...]
    dot_general x2 -> x0, matrix products: 3.49 us -> none  [the longest x1 2.83 us: on_device(): jnp.einsum('phn,hnc->phc', q_nope, w_uk, preferred_element_type=F32)]
    ppermute x4 -> x5, waiting for transfers between devices: 10.2 us -> 6.76 us  [the longest x1 5.17 us: on_device(): parts = [lax.ppermute(s, 'seq', back(t, 0)) for t, s in enumerate(sums, 1)]]
    ppermute x4 -> x5, starting transfers between devices: 4.32 us -> 7.63 us  [the longest x1 5.89 us: on_device(): near = lax.ppermute(block, 'dom', [(0, 1), (1, 0), (2, 3), (3, 2)])]
    ppermute x1, waiting for transfers between devices: 7.62 us -> 5.01 us  [on_device(): outer_far = lax.ppermute(inner_middle, 'dom', [(1, 0), (2, 3)])]
    unnamed x18 -> x14, local copies, waits for them, and re-layouts: 3.02 us -> 2.5 us
  transfers between devices with their start and end apart: 10 -> 11, of which waited for: 6 -> 6; matrix products, arithmetic and copies ran while one was open for 6% -> 0% of each run, Pallas kernels for 15% -> 33%
where the time goes in v4:
time: 49.2 us; the launch traced here: 48.9 us
  Pallas kernels  19.7 us (40%)
  waiting for transfers between devices  13.2 us (27%)
  starting transfers between devices  12.6 us (26%)
  local copies, waits for them, and re-layouts  2.5 us (5%)
  between operations  0.77 us (2%)
    pallas_call x2, Pallas kernels, prefix_attention(): pl.pallas_call(functools.partial(prefix_kernel, len(queries), tiles), out...  11.4 us
    ppermute x1, starting transfers between devices, on_device(): near = lax.ppermute(block, 'dom', [(0, 1), (1, 0), (2, 3), (3, 2)])  5.89 us
    ppermute x1, waiting for transfers between devices, on_device(): parts = [lax.ppermute(s, 'seq', back(t, 0)) for t, s in enumerate(sums, 1)]  5.17 us
    ppermute x1, waiting for transfers between devices, on_device(): outer_far = lax.ppermute(inner_middle, 'dom', [(1, 0), (2, 3)])  5.01 us
    unnamed x14, local copies, waits for them, and re-layouts  2.5 us
    pallas_call x1, Pallas kernels, on_device(): pl.pallas_call(functools.partial(project_kernel, pieces), out_shape=shape...  2.46 us
    pallas_call x1, Pallas kernels, on_device(): pl.pallas_call(functools.partial(far_kernel, others, len(blocks), line),...  2.32 us
    pallas_call x1, Pallas kernels, on_device(): pl.pallas_call(near_kernel, out_shape=[shape(private_caches.shape), part,...  1.76 us
  transfers between devices with their start and end apart: 11, of which 6 were waited for; matrix products, arithmetic and copies ran while one was open for 0% of the time, Pallas kernels for 33%

profile of v4, /device:TPU:0, one launch (start us, length us, event | category | flops | bytes accessed | tf_op | source)
XLA Modules:
  0.0 48.9 jit_solution(17344491659668883969)
XLA Ops:
  0.6 1.0 %copy-done.1 = bf16[4,64,576]{2,1,0:T(8,128)(2,1)S(1)} copy-done((bf16[4,64,576]{2,1,0:T(8,128)(2,1)S(1)}, bf16[4,64,576]{2,1,0:T(8,128)(2,1)}, u32[]{:S(2)}) %copy-start.1) | copy-done | bytes 294936
  1.7 0.7 %collective-permute-start.3 = (bf16[288,512]{1,0:T(8,128)(2,1)S(1)}, bf16[288,512]{1,0:T(8,128)(2,1)S(1)}, u32[]{:S(2)}, u32[]{:S(2)}) collective-permute-start(bf16[288,512]{1,0:T(8,128)(2,1)S(1)} %pack.1.refs_8_), channel_id=1, source_target_pairs={{1,2},{2,1},{5,6},{6,5},{9,10},{10,9},{13,14},{14,13},{17,18},{18,... | collective-permute-start | bytes 884744 | tf_op jit(solution)/shard_map/ppermute | solution.py:328
  2.4 5.9 %collective-permute-start.2 = (bf16[288,512]{1,0:T(8,128)(2,1)S(1)}, bf16[288,512]{1,0:T(8,128)(2,1)S(1)}, u32[]{:S(2)}, u32[]{:S(2)}) collective-permute-start(bf16[288,512]{1,0:T(8,128)(2,1)S(1)} %pack.1.refs_8_), channel_id=1, source_target_pairs={{0,1},{1,0},{2,3},{3,2},{4,5},{5,4},{6,7},{7,6},{8,9},{9,8},{10,11... | collective-permute-start | bytes 884744 | tf_op jit(solution)/shard_map/ppermute | solution.py:327
  8.3 0.8 %copy-done.2 = bf16[4,32,128]{2,1,0:T(8,128)(2,1)S(1)} copy-done((bf16[4,32,128]{2,1,0:T(8,128)(2,1)S(1)}, bf16[4,32,128]{2,1,0:T(8,128)(2,1)}, u32[]{:S(2)}) %copy-start.2) | copy-done | bytes 32792
  9.0 0.8 %copy-done.3 = bf16[4,32,64]{2,1,0:T(8,128)(2,1)S(1)} copy-done((bf16[4,32,64]{2,1,0:T(8,128)(2,1)S(1)}, bf16[4,32,64]{2,1,0:T(8,128)(2,1)}, u32[]{:S(2)}) %copy-start.3) | copy-done | bytes 16408
  9.8 2.5 %project.1.refs_0_ = bf16[128,576]{1,0:T(8,128)(2,1)S(1)} custom-call(bf16[4,32,128]{2,1,0:T(8,128)(2,1)S(1)} %copy-done.2, bf16[4,32,64]{2,1,0:T(8,128)(2,1)S(1)} %copy-done.3, bf16[32,128,512]{2,1,0:T(8,128)(2,1)} %w_hbm.1), custom_call_target="tpu_custom_call" | custom-call | tf_op jit(solution)/shard_map/project/pallas_call | solution.py:336
  12.3 1.4 %collective-permute-done.4.refs_1_ = bf16[128,576]{1,0:T(8,128)(2,1)S(1)} collective-permute-done((bf16[128,576]{1,0:T(8,128)(2,1)S(1)}, bf16[128,576]{1,0:T(8,128)(2,1)S(1)}, u32[]{:S(2)}, u32[]{:S(2)}) %collective-permute-start.4) | collective-permute-done | bytes 147488 | tf_op jit(solution)/shard_map/ppermute | solution.py:363
  13.7 1.3 %collective-permute-done.2.refs_9_ = bf16[288,512]{1,0:T(8,128)(2,1)S(1)} collective-permute-done((bf16[288,512]{1,0:T(8,128)(2,1)S(1)}, bf16[288,512]{1,0:T(8,128)(2,1)S(1)}, u32[]{:S(2)}, u32[]{:S(2)}) %collective-permute-start.2) | collective-permute-done | bytes 294944 | tf_op jit(solution)/shard_map/ppermute | solution.py:327
  15.0 0.7 %collective-permute-start.5 = (bf16[288,512]{1,0:T(8,128)(2,1)S(1)}, bf16[288,512]{1,0:T(8,128)(2,1)S(1)}, u32[]{:S(2)}, u32[]{:S(2)}) collective-permute-start(bf16[288,512]{1,0:T(8,128)(2,1)S(1)} %collective-permute-done.2.refs_9_), channel_id=1, source_target_pairs={{1,2},{2,1},{5,6},{6,5},{9,10},{10,9},{13,14},{14,13},{17,18},{18,... | collective-permute-start | bytes 884744 | tf_op jit(solution)/shard_map/ppermute | solution.py:366
  15.8 1.5 %collective-permute-start = (bf16[128,576]{1,0:T(8,128)(2,1)S(1)}, bf16[128,576]{1,0:T(8,128)(2,1)S(1)}, u32[]{:S(2)}, u32[]{:S(2)}) collective-permute-start(bf16[128,576]{1,0:T(8,128)(2,1)S(1)} %project.1.refs_0_), channel_id=1, source_target_pairs={{0,8},{4,12},{8,0},{12,4},{1,9},{5,13},{9,1},{13,5},{2,10},{6,14},... | collective-permute-start | bytes 442376 | tf_op jit(solution)/shard_map/ppermute | solution.py:363
  17.3 1.3 %collective-permute-start.6 = (bf16[288,512]{1,0:T(8,128)(2,1)S(1)}, bf16[288,512]{1,0:T(8,128)(2,1)S(1)}, u32[]{:S(2)}, u32[]{:S(2)}) collective-permute-start(bf16[288,512]{1,0:T(8,128)(2,1)S(1)} %collective-permute-done.3.refs_11_), channel_id=1, source_target_pairs={{1,0},{2,3},{5,4},{6,7},{9,8},{10,11},{13,12},{14,15},{17,16},{18,... | collective-permute-start | bytes 884744 | tf_op jit(solution)/shard_map/ppermute | solution.py:367
  18.6 5.7 %prefix_attention.3 = (f32[256,512]{1,0:T(8,128)S(1)}, f32[256,128]{1,0:T(8,128)S(1)}, f32[256,128]{1,0:T(8,128)S(1)}) custom-call(bf16[128,576]{1,0:T(8,128)(2,1)S(1)} %project.1.refs_0_, bf16[128,576]{1,0:T(8,128)(2,1)S(1)} %collective-permute-done.4.refs_1_, bf16[576,4096]{1,0:T(8,128)(2,1)} %bitcast.3), custom_call_target="tpu_custom_call" | custom-call | flops 2281701376 | bytes 4718592 | tf_op jit(solution)/shard_map/prefix_attention/pallas_call | solution.py:119
  24.3 1.3 %collective-permute-start.7 = (bf16[288,512]{1,0:T(8,128)(2,1)S(1)}, bf16[288,512]{1,0:T(8,128)(2,1)S(1)}, u32[]{:S(2)}, u32[]{:S(2)}) collective-permute-start(bf16[288,512]{1,0:T(8,128)(2,1)S(1)} %collective-permute-done.5.refs_10_), channel_id=1, source_target_pairs={{1,0},{2,3},{5,4},{6,7},{9,8},{10,11},{13,12},{14,15},{17,16},{18,... | collective-permute-start | bytes 884744 | tf_op jit(solution)/shard_map/ppermute | solution.py:374
  25.7 5.7 %prefix_attention.2 = (f32[256,512]{1,0:T(8,128)S(1)}, f32[256,128]{1,0:T(8,128)S(1)}, f32[256,128]{1,0:T(8,128)S(1)}) custom-call(bf16[128,576]{1,0:T(8,128)(2,1)S(1)} %collective-permute-done.refs_0_.refs_3_, bf16[128,576]{1,0:T(8,128)(2,1)S(1)} %collective-permute-done.1.refs_1_.refs_4_, bf16[576,4096]{1,0:T(8,128)(2,1)} %bitcast.4), custom_call_target="tpu_custom_call" | custom-call | flops 2281701376 | bytes 4718592 | tf_op jit(solution)/shard_map/prefix_attention/pallas_call | solution.py:119
  31.4 5.0 %collective-permute-done.7.refs_13_ = bf16[288,512]{1,0:T(8,128)(2,1)S(1)} collective-permute-done((bf16[288,512]{1,0:T(8,128)(2,1)S(1)}, bf16[288,512]{1,0:T(8,128)(2,1)S(1)}, u32[]{:S(2)}, u32[]{:S(2)}) %collective-permute-start.7) | collective-permute-done | bytes 294944 | tf_op jit(solution)/shard_map/ppermute | solution.py:374
  36.5 2.3 %suffix_far.1 = (bf16[256,512]{1,0:T(8,128)(2,1)S(1)}, bf16[256,64]{1,0:T(8,128)(2,1)S(1)}, bf16[128,640]{1,0:T(8,128)(2,1)S(1)}, bf16[128,640]{1,0:T(8,128)(2,1)S(1)}) custom-call(s32[4]{0:T(128)S(1)} %copy-done.5, s32[16]{0:T(128)S(1)} %copy-done.6, s32[2]{0:T(128)S(1)} %pad_add_fusion.refs_2_.place, ...), custom_call_target="tpu_custom_call" | custom-call | tf_op jit(solution)/shard_map/suffix_far/pallas_call | solution.py:380
  38.9 1.8 %suffix_near.1 = (bf16[4,64,576]{2,1,0:T(8,128)(2,1)}, bf16[128,640]{1,0:T(8,128)(2,1)S(1)}, bf16[128,640]{1,0:T(8,128)(2,1)S(1)}) custom-call(s32[4]{0:T(128)S(1)} %copy-done.5, s32[16]{0:T(128)S(1)} %copy-done.6, s32[2]{0:T(128)S(1)} %pad_add_fusion.refs_2_.place, bf16[4,576]{1,0:T(4,128)(2,1)S(1)} %copy-done.4, bf16[128,576]{1,0:T(8,128)(2,1)S(1)} %project.1.refs_0_, ...), custom_call_target="tpu_custom_call" | custom-call | tf_op jit(solution)/shard_map/suffix_near/pallas_call | solution.py:397
  40.6 0.5 collective-permute-start.10
  41.1 0.2 chip_merge.2
  41.3 0.5 %collective-permute-start.9 = (bf16[128,640]{1,0:T(8,128)(2,1)S(1)}, bf16[128,640]{1,0:T(8,128)(2,1)S(1)}, u32[]{:S(2)}, u32[]{:S(2)}) collective-permute-start(bf16[128,640]{1,0:T(8,128)(2,1)S(1)} %chip_merge.2), channel_id=1, source_target_pairs={{8,0},{12,4},{0,8},{4,12},{9,1},{13,5},{1,9},{5,13},{10,2},{14,6},... | collective-permute-start | bytes 491528 | tf_op jit(solution)/shard_map/ppermute | solution.py:395
  41.8 0.3 collective-permute-done.10.refs_1_
  42.2 0.2 chip_merge.3.refs_1_
  42.4 5.2 %collective-permute-done.9.refs_0_ = bf16[128,640]{1,0:T(8,128)(2,1)S(1)} collective-permute-done((bf16[128,640]{1,0:T(8,128)(2,1)S(1)}, bf16[128,640]{1,0:T(8,128)(2,1)S(1)}, u32[]{:S(2)}, u32[]{:S(2)}) %collective-permute-start.9) | collective-permute-done | bytes 163872 | tf_op jit(solution)/shard_map/ppermute | solution.py:395
  47.5 1.4 %final.1 = bf16[4,32,128]{2,1,0:T(8,128)(2,1)} custom-call(bf16[128,640]{1,0:T(8,128)(2,1)S(1)} %collective-permute-done.9.refs_0_, bf16[128,640]{1,0:T(8,128)(2,1)S(1)} %chip_merge.3.refs_1_, bf16[32,512,128]{2,1,0:T(8,128)(2,1)S(1)} %copy-done), custom_call_target="tpu_custom_call" | custom-call | tf_op jit(solution)/shard_map/final/pallas_call | solution.py:407
  (22 shorter events, 0.5 us)
Async XLA Ops:
  0.6 1.0 %copy-start.1 = (bf16[4,64,576]{2,1,0:T(8,128)(2,1)S(1)}, bf16[4,64,576]{2,1,0:T(8,128)(2,1)}, u32[]{:S(2)}) copy-start(bf16[4,64,576]{2,1,0:T(8,128)(2,1)} %cache_ref.1) | copy-start | bytes 884740
  1.7 12.0 %collective-permute-start.3 = (bf16[288,512]{1,0:T(8,128)(2,1)S(1)}, bf16[288,512]{1,0:T(8,128)(2,1)S(1)}, u32[]{:S(2)}, u32[]{:S(2)}) collective-permute-start(bf16[288,512]{1,0:T(8,128)(2,1)S(1)} %pack.1.refs_8_), channel_id=1, source_target_pairs={{1,2},{2,1},{5,6},{6,5},{9,10},{10,9},{13,14},{14,13},{17,18},{18,... | collective-permute-start | bytes 884744 | tf_op jit(solution)/shard_map/ppermute | solution.py:328
  2.4 12.6 %collective-permute-start.2 = (bf16[288,512]{1,0:T(8,128)(2,1)S(1)}, bf16[288,512]{1,0:T(8,128)(2,1)S(1)}, u32[]{:S(2)}, u32[]{:S(2)}) collective-permute-start(bf16[288,512]{1,0:T(8,128)(2,1)S(1)} %pack.1.refs_8_), channel_id=1, source_target_pairs={{0,1},{1,0},{2,3},{3,2},{4,5},{5,4},{6,7},{7,6},{8,9},{9,8},{10,11... | collective-permute-start | bytes 884744 | tf_op jit(solution)/shard_map/ppermute | solution.py:327
  8.3 0.8 %copy-start.2 = (bf16[4,32,128]{2,1,0:T(8,128)(2,1)S(1)}, bf16[4,32,128]{2,1,0:T(8,128)(2,1)}, u32[]{:S(2)}) copy-start(bf16[4,32,128]{2,1,0:T(8,128)(2,1)} %nope_ref.1) | copy-start | bytes 98308
  9.0 0.8 %copy-start.3 = (bf16[4,32,64]{2,1,0:T(8,128)(2,1)S(1)}, bf16[4,32,64]{2,1,0:T(8,128)(2,1)}, u32[]{:S(2)}) copy-start(bf16[4,32,64]{2,1,0:T(8,128)(2,1)} %rope_ref.1) | copy-start | bytes 49156
  12.2 1.5 %collective-permute-start.4 = (bf16[128,576]{1,0:T(8,128)(2,1)S(1)}, bf16[128,576]{1,0:T(8,128)(2,1)S(1)}, u32[]{:S(2)}, u32[]{:S(2)}) collective-permute-start(bf16[128,576]{1,0:T(8,128)(2,1)S(1)} %project.1.refs_0_), channel_id=1, source_target_pairs={{0,4},{4,0},{8,12},{12,8},{1,5},{5,1},{9,13},{13,9},{2,6},{6,2},{1... | collective-permute-start | bytes 442376 | tf_op jit(solution)/shard_map/ppermute | solution.py:363
  15.0 9.3 %collective-permute-start.5 = (bf16[288,512]{1,0:T(8,128)(2,1)S(1)}, bf16[288,512]{1,0:T(8,128)(2,1)S(1)}, u32[]{:S(2)}, u32[]{:S(2)}) collective-permute-start(bf16[288,512]{1,0:T(8,128)(2,1)S(1)} %collective-permute-done.2.refs_9_), channel_id=1, source_target_pairs={{1,2},{2,1},{5,6},{6,5},{9,10},{10,9},{13,14},{14,13},{17,18},{18,... | collective-permute-start | bytes 884744 | tf_op jit(solution)/shard_map/ppermute | solution.py:366
  15.7 10.0 %collective-permute-start.1 = (bf16[128,576]{1,0:T(8,128)(2,1)S(1)}, bf16[128,576]{1,0:T(8,128)(2,1)S(1)}, u32[]{:S(2)}, u32[]{:S(2)}) collective-permute-start(bf16[128,576]{1,0:T(8,128)(2,1)S(1)} %project.1.refs_0_), channel_id=1, source_target_pairs={{0,12},{4,8},{8,4},{12,0},{1,13},{5,9},{9,5},{13,1},{2,14},{6,10},... | collective-permute-start | bytes 442376 | tf_op jit(solution)/shard_map/ppermute | solution.py:363
  15.8 10.0 %collective-permute-start = (bf16[128,576]{1,0:T(8,128)(2,1)S(1)}, bf16[128,576]{1,0:T(8,128)(2,1)S(1)}, u32[]{:S(2)}, u32[]{:S(2)}) collective-permute-start(bf16[128,576]{1,0:T(8,128)(2,1)S(1)} %project.1.refs_0_), channel_id=1, source_target_pairs={{0,8},{4,12},{8,0},{12,4},{1,9},{5,13},{9,1},{13,5},{2,10},{6,14},... | collective-permute-start | bytes 442376 | tf_op jit(solution)/shard_map/ppermute | solution.py:363
  17.3 14.1 %collective-permute-start.6 = (bf16[288,512]{1,0:T(8,128)(2,1)S(1)}, bf16[288,512]{1,0:T(8,128)(2,1)S(1)}, u32[]{:S(2)}, u32[]{:S(2)}) collective-permute-start(bf16[288,512]{1,0:T(8,128)(2,1)S(1)} %collective-permute-done.3.refs_11_), channel_id=1, source_target_pairs={{1,0},{2,3},{5,4},{6,7},{9,8},{10,11},{13,12},{14,15},{17,16},{18,... | collective-permute-start | bytes 884744 | tf_op jit(solution)/shard_map/ppermute | solution.py:367
  24.3 12.2 %collective-permute-start.7 = (bf16[288,512]{1,0:T(8,128)(2,1)S(1)}, bf16[288,512]{1,0:T(8,128)(2,1)S(1)}, u32[]{:S(2)}, u32[]{:S(2)}) collective-permute-start(bf16[288,512]{1,0:T(8,128)(2,1)S(1)} %collective-permute-done.5.refs_10_), channel_id=1, source_target_pairs={{1,0},{2,3},{5,4},{6,7},{9,8},{10,11},{13,12},{14,15},{17,16},{18,... | collective-permute-start | bytes 884744 | tf_op jit(solution)/shard_map/ppermute | solution.py:374
  25.7 10.8 %copy-start.5 = (s32[4]{0:T(128)S(1)}, s32[4]{0:T(128)}, u32[]{:S(2)}) copy-start(s32[4]{0:T(128)} %anc.1) | copy-start | bytes 52
  25.7 10.8 %copy-start.6 = (s32[16]{0:T(128)S(1)}, s32[16]{0:T(128)}, u32[]{:S(2)}) copy-start(s32[16]{0:T(128)} %lens.1) | copy-start | bytes 196
  25.7 13.2 %copy-start.4 = (bf16[4,576]{1,0:T(4,128)(2,1)S(1)}, bf16[4,576]{1,0:T(4,128)(2,1)}, u32[]{:S(2)}) copy-start(bf16[4,576]{1,0:T(4,128)(2,1)} %fresh_ref.1) | copy-start | bytes 13828
  31.4 16.1 %copy-start = (bf16[32,512,128]{2,1,0:T(8,128)(2,1)S(1)}, bf16[32,512,128]{2,1,0:T(8,128)(2,1)}, u32[]{:S(2)}) copy-start(bf16[32,512,128]{2,1,0:T(8,128)(2,1)} %refs_2_.1) | copy-start | bytes 12582916
  38.8 2.3 %collective-permute-start.8 = (bf16[128,640]{1,0:T(8,128)(2,1)S(1)}, bf16[128,640]{1,0:T(8,128)(2,1)S(1)}, u32[]{:S(2)}, u32[]{:S(2)}) collective-permute-start(bf16[128,640]{1,0:T(8,128)(2,1)S(1)} %get-tuple-element.29), channel_id=1, source_target_pairs={{0,4},{4,0},{8,12},{12,8},{1,5},{5,1},{9,13},{13,9},{2,6},{6,2},{1... | collective-permute-start | bytes 491528 | tf_op jit(solution)/shard_map/ppermute | solution.py:394
  40.6 1.5 %collective-permute-start.10 = (bf16[128,640]{1,0:T(8,128)(2,1)S(1)}, bf16[128,640]{1,0:T(8,128)(2,1)S(1)}, u32[]{:S(2)}, u32[]{:S(2)}) collective-permute-start(bf16[128,640]{1,0:T(8,128)(2,1)S(1)} %get-tuple-element.36), channel_id=1, source_target_pairs={{0,4},{4,0},{8,12},{12,8},{1,5},{5,1},{9,13},{13,9},{2,6},{6,2},{1... | collective-permute-start | bytes 491528 | tf_op jit(solution)/shard_map/ppermute | solution.py:405
  41.3 6.2 %collective-permute-start.9 = (bf16[128,640]{1,0:T(8,128)(2,1)S(1)}, bf16[128,640]{1,0:T(8,128)(2,1)S(1)}, u32[]{:S(2)}, u32[]{:S(2)}) collective-permute-start(bf16[128,640]{1,0:T(8,128)(2,1)S(1)} %chip_merge.2), channel_id=1, source_target_pairs={{8,0},{12,4},{0,8},{4,12},{9,1},{13,5},{1,9},{5,13},{10,2},{14,6},... | collective-permute-start | bytes 491528 | tf_op jit(solution)/shard_map/ppermute | solution.py:395

commit v5 on v4

v5 whole, which is shorter than its diff:
```python
import functools
import math

import jax
import jax.numpy as jnp
from jax import lax
from jax.experimental import pallas as pl
from jax.experimental.pallas import tpu as pltpu
from jax.sharding import PartitionSpec as P

ROPE = 64
NOPE = 128
SCALE2 = (NOPE + ROPE) ** (-0.5) * math.log2(math.e)
HIDDEN = -1e30
LANES = 128
F32 = jnp.float32
BF16 = jnp.bfloat16
NT = (((1,), (1,)), ((), ()))

VMEM = pl.BlockSpec(memory_space=pltpu.VMEM)
SMEM = pl.BlockSpec(memory_space=pltpu.SMEM)
ANY = pl.BlockSpec(memory_space=pl.ANY)
HBM = pl.BlockSpec(memory_space=pltpu.HBM)
PARAMS = pltpu.CompilerParams(vmem_limit_bytes=40 * 1024 * 1024)
STREAM = pltpu.CompilerParams(vmem_limit_bytes=51 * 1024 * 1024)


def shape(dims, dtype=BF16):
    return jax.ShapeDtypeStruct(dims, dtype)


def pack_kernel(rank, cache_ref, out_ref):
    local, span, width = cache_ref.shape
    half = out_ref.shape[0] // 2
    some = span // 2
    tail = half - local * some
    rope = jnp.concatenate([cache_ref[p, :, rank:] for p in range(local)], axis=1)
    for h in range(2):
        for p in range(local):
            out_ref[pl.ds(h * half + p * some, some)] = cache_ref[p, pl.ds(h * some, some), :rank]
        out_ref[pl.ds(h * half + local * some, tail)] = jnp.concatenate(
            [rope[h * some + i : h * some + i + tail] for i in range(0, some, tail)], axis=1
        )


def project_kernel(pieces, local, nope_ref, rope_ref, w_hbm, own_ref, w_ref, sems):
    heads, _, rank = w_ref.shape
    piece = heads // pieces
    fetches = [
        pltpu.make_async_copy(
            w_hbm.at[pl.ds(i * piece, piece)], w_ref.at[pl.ds(i * piece, piece)], sems.at[i]
        )
        for i in range(pieces)
    ]
    for fetch in fetches[:2]:
        fetch.start()
    nope = nope_ref[...].astype(F32)
    width = nope.shape[1]
    first = lax.broadcasted_iota(jnp.int32, (2 * local, width), 0) < local

    def pair(h):
        two = nope[h * local : (h + 2) * local]
        left = jnp.concatenate([jnp.where(first, two, 0.0), jnp.where(first, 0.0, two)], axis=1)
        weights = w_ref[pl.ds(h, 2)].reshape(2 * width, rank)
        return jnp.dot(left.astype(BF16), weights, preferred_element_type=F32)

    own_ref[:, rank:] = rope_ref[...]
    for h in range(0, heads, 4):
        if h % piece == 0:
            at = h // piece
            fetches[at].wait()
            if at + 2 < pieces:
                fetches[at + 2].start()
        own_ref[pl.ds(h * local, 4 * local), :rank] = jnp.concatenate(
            [pair(i) for i in (h, h + 2)], axis=0
        ).astype(BF16)


def prefix_kernel(count, tiles, *refs):
    query_refs = refs[:count]
    keys_hbm, out_ref, max_ref, sum_ref, *give_ref, acc_ref, keys_ref, sems = refs[count:]
    rank = acc_ref.shape[1]
    parts = [pl.ds(begin, end - begin) for begin, end in zip(tiles, tiles[1:])]
    fetches = [
        pltpu.make_async_copy(keys_hbm.at[:, part], keys_ref.at[:, part], sems.at[i])
        for i, part in enumerate(parts)
    ]
    for fetch in fetches[:2]:
        fetch.start()
    queries = jnp.concatenate([ref[...] for ref in query_refs], axis=0)
    for i, part in enumerate(parts):
        fetches[i].wait()
        if i + 2 < len(parts):
            fetches[i + 2].start()
        scores = jnp.dot(queries, keys_ref[:, part], preferred_element_type=F32) * SCALE2
        top = jnp.max(scores, axis=1, keepdims=True)
        if i > 0:
            top = jnp.maximum(top, largest)
        weights = jnp.exp2(scores - top)
        total = jnp.sum(weights, axis=1, keepdims=True)
        acc = lax.dot_general(
            weights.astype(BF16), keys_ref[:rank, part], NT, preferred_element_type=F32
        )
        if i > 0:
            factor = jnp.exp2(largest - top)
            total = total + running * factor
            acc = acc + acc_ref[...] * factor
        largest, running = top, total
        if i < len(parts) - 1:
            acc_ref[...] = acc
    kept = out_ref.shape[0]
    out_ref[...] = acc[:kept]
    max_ref[...] = jnp.broadcast_to(largest[:kept], max_ref.shape)
    sum_ref[...] = jnp.broadcast_to(running[:kept], sum_ref.shape)
    if give_ref:
        level = largest[kept:] + jnp.log2(running[kept:])
        give_ref[0][...] = packed(acc[kept:] * (1.0 / running[kept:]), level)


def prefix_attention(queries, keys, rank, give):
    rows = sum(q.shape[0] for q in queries)
    kept = queries[0].shape[0] if give else rows
    width, length = keys.shape
    tiles = [0, length // 8] + [length * i // 4 for i in range(1, 5)]
    out = [shape((kept, rank), F32)] + [shape((kept, LANES), F32)] * 2
    if give:
        out.append(shape((rows - kept, rank + LANES)))
    return pl.pallas_call(
        functools.partial(prefix_kernel, len(queries), tiles),
        out_shape=out,
        in_specs=[VMEM] * len(queries) + [HBM],
        out_specs=[VMEM] * len(out),
        scratch_shapes=[
            pltpu.VMEM((rows, rank), F32),
            pltpu.VMEM(keys.shape, BF16),
            pltpu.SemaphoreType.DMA((len(tiles) - 1,)),
        ],
        compiler_params=STREAM,
        name="prefix_attention",
    )(*queries, keys)


def packed(values, level):
    rows = values.shape[0]
    lane = lax.broadcasted_iota(jnp.int32, (rows, LANES), 1)
    high = level.astype(BF16).astype(F32)
    middle = (level - high).astype(BF16).astype(F32)
    low = level - high - middle
    stats = jnp.where(lane == 0, high, jnp.where(lane == 1, middle, jnp.where(lane == 2, low, 0.0)))
    return jnp.concatenate([values.astype(BF16), stats.astype(BF16)], axis=1)


def merged(parts, rank):
    levels = [jnp.sum(part[:, rank:].astype(F32), axis=1, keepdims=True) for part in parts]
    top = functools.reduce(jnp.maximum, levels)
    shares = [jnp.exp2(level - top) for level in levels]
    whole = functools.reduce(jnp.add, shares)
    acc = functools.reduce(
        jnp.add, [share * part[:, :rank].astype(F32) for share, part in zip(shares, parts)]
    )
    return acc * (1.0 / whole), top + jnp.log2(whole)


def visible(rows, ends, starts, span):
    local = len(ends)
    cols = len(starts) * local * span
    col = lax.broadcasted_iota(jnp.int32, (1, cols), 1)
    col_of = jnp.zeros_like(col)
    limit = jnp.full_like(col, ends[0] - starts[0])
    for at in range(1, len(starts) * local):
        begin, p = at * span, at % local
        later = col >= begin
        col_of = jnp.where(later, p, col_of)
        limit = jnp.where(later, ends[p] - starts[at // local] + begin, limit)
    col_of = jnp.where(col < limit, col_of, -1)
    row_of = lax.rem(lax.broadcasted_iota(jnp.int32, (rows, 1), 0), local)
    return row_of == col_of


def attend(queries, keys, seen, rank, known):
    scores = lax.dot_general(queries, keys, NT, preferred_element_type=F32)
    scores = jnp.where(seen, scores * SCALE2, HIDDEN)
    top = jnp.max(scores, axis=1, keepdims=True)
    for level, _, _ in known:
        top = jnp.maximum(top, level)
    weights = jnp.where(seen, jnp.exp2(scores - top), 0.0)
    total = jnp.sum(weights, axis=1, keepdims=True)
    acc = jnp.dot(weights.astype(BF16), keys[:, :rank], preferred_element_type=F32)
    for level, mass, part in known:
        factor = jnp.exp2(level - top)
        total = total + mass * factor
        acc = acc + part * factor
    return packed(acc * (1.0 / total), top + jnp.log2(total))


def far_kernel(stages, sources, line, *refs):
    anc, lens, place = refs[:3]
    refs = refs[3:]
    stage_refs, refs = refs[: 5 * stages], refs[5 * stages :]
    count = max(ref for source in sources for ref, _ in source) + 1
    block_refs, refs = refs[:count], refs[count:]
    moved_ref, refs = refs[0], refs[1:]
    keep_refs, give_refs = refs[:stages], refs[stages : 2 * stages]
    folded, sems = refs[2 * stages :]
    local, _, tail, rank = folded.shape
    span = moved_ref.shape[0] // local
    some = span // 2
    rope = moved_ref.shape[1] - rank

    def copies(p, source, slot):
        found = []
        for h, (ref, base) in enumerate(source):
            at = pl.multiple_of(base + slot * some, 16)
            there = moved_ref.at[pl.ds(p * span + h * some, some), pl.ds(0, rank)]
            found.append((block_refs[ref].at[pl.ds(at, some)], there))
            found.append((block_refs[ref].at[pl.ds(base + local * some, tail)], folded.at[p, h]))
        return [pltpu.make_async_copy(a, b, sems.at[4 * p + i]) for i, (a, b) in enumerate(found)]

    slots = []
    for p in range(local):
        owner = lax.div(anc[p], local)
        slots.append(lax.rem(anc[p], local))
        if line:
            apart = jnp.bitwise_xor(owner, place[1])
            at_end = (place[1] == 0) | (place[1] == 3)
            which = jnp.where(at_end & (apart > 1), apart + 2, apart)
        else:
            which = lax.rem(place[1] - owner + len(sources), len(sources))
        for k, source in enumerate(sources):

            @pl.when(which == k)
            def _():
                for copy in copies(p, source, slots[p]):
                    copy.start()

    for p in range(local):
        for copy in copies(p, sources[0], 0):
            copy.wait()

    for p in range(local):
        for h in range(2):
            for i in range(some // tail):
                choices = [
                    folded[p, h, :, (i * local + q) * rope : (i * local + q + 1) * rope]
                    for q in range(local)
                ]
                picked = choices[0]
                for q in range(1, local):
                    picked = jnp.where(slots[p] == q, choices[q], picked)
                moved_ref[pl.ds(p * span + h * some + i * tail, tail), rank:] = picked

    ends = [lens[anc[p]] for p in range(local)]
    for k in range(stages):
        first_ref, second_ref, acc_ref, max_ref, sum_ref = stage_refs[5 * k : 5 * k + 5]
        queries = jnp.concatenate([first_ref[...], second_ref[...]], axis=0)
        seen = visible(queries.shape[0], ends, [place[0] * span], span)
        known = [(max_ref[:, 0:1], sum_ref[:, 0:1], acc_ref[...])]
        part = attend(queries, moved_ref[...], seen, rank, known)
        rows = first_ref.shape[0]
        keep_refs[k][...] = part[:rows]
        give_refs[k][...] = part[rows:]


def near_kernel(anc, lens, place, fresh_ref, *refs):
    query_ref, acc_ref, max_ref, sum_ref, got_ref, moved_ref, other_ref, cache_ref, part_ref = refs
    local, span, width = cache_ref.shape
    rank = acc_ref.shape[1]
    start, other = place[0] * span, jnp.bitwise_xor(place[0], 1) * span
    ends = [lens[anc[p]] for p in range(local)]
    keys = jnp.concatenate([moved_ref[...], other_ref[...]], axis=0)
    seen = visible(query_ref.shape[0], ends, [start, other], span)
    level = jnp.sum(got_ref[:, rank:].astype(F32), axis=1, keepdims=True)
    known = [
        (max_ref[:, 0:1], sum_ref[:, 0:1], acc_ref[...]),
        (level, 1.0, got_ref[:, :rank].astype(F32)),
    ]
    part_ref[...] = attend(query_ref[...], keys, seen, rank, known)
    for p in range(local):
        at = start + lax.broadcasted_iota(jnp.int32, (span, 1), 0) == ends[p]
        cache_ref[p] = jnp.where(at, fresh_ref[pl.ds(p, 1), :], moved_ref[pl.ds(p * span, span)])


def chip_kernel(count, *refs):
    for k in range(count):
        out_ref = refs[2 * count + k]
        rank = out_ref.shape[1] - LANES
        out_ref[...] = packed(*merged([refs[k][...], refs[count + k][...]], rank))


def chip_merge(keep, got):
    return pl.pallas_call(
        functools.partial(chip_kernel, len(keep)),
        out_shape=[shape(k.shape) for k in keep],
        in_specs=[VMEM] * (2 * len(keep)),
        out_specs=[VMEM] * len(keep),
        compiler_params=PARAMS,
        name="chip_merge",
    )(*keep, *got)


def final_kernel(count, *refs):
    part_refs, (w_ref, out_ref, values) = refs[:count], refs[count:]
    heads, rank, reach = w_ref.shape
    local = out_ref.shape[0]
    latent = merged([ref[...] for ref in part_refs], rank)[0].astype(BF16)
    first = lax.broadcasted_iota(jnp.int32, (2 * local, reach), 0) < local
    for h in range(0, heads, 2):
        two = latent[h * local : (h + 2) * local]
        here = jnp.dot(two, w_ref[h], preferred_element_type=F32)
        there = jnp.dot(two, w_ref[h + 1], preferred_element_type=F32)
        values[pl.ds(h * local, 2 * local), :] = jnp.where(first, here, there)
    for p in range(local):
        out_ref[p] = values[pl.ds(p, heads, stride=local), :].astype(BF16)


def after_kernel(_, value_ref, out_ref):
    out_ref[...] = value_ref[...]


def after(token, value):
    return pl.pallas_call(
        after_kernel,
        out_shape=shape(value.shape, value.dtype),
        in_specs=[ANY, VMEM],
        out_specs=VMEM,
        compiler_params=PARAMS,
        name="after",
    )(token, value)


def on_device(q_nope, q_rope, w_uk, w_uv, prefix, private_caches, new_latent, ancestors, lengths):
    local, heads, nope = q_nope.shape
    span, width = private_caches.shape[1:]
    rank, reach = w_uv.shape[1:]
    rope = width - rank
    rows = local * heads
    seq_size, dom_size = lax.axis_size("seq"), lax.axis_size("dom")
    cores = 2
    chips = seq_size // cores
    place = jnp.stack([lax.axis_index("seq"), lax.axis_index("dom")]).astype(jnp.int32)
    tail = span * local * rope // rank

    block = pl.pallas_call(
        functools.partial(pack_kernel, rank),
        out_shape=shape((local * span + tail, rank)),
        in_specs=[VMEM],
        out_specs=VMEM,
        compiler_params=PARAMS,
        name="pack",
    )(private_caches)
    nope_rows, rope_rows = (jnp.swapaxes(q, 0, 1).reshape(rows, -1) for q in (q_nope, q_rope))
    line = dom_size == 4
    if line:
        near = lax.ppermute(block, "dom", [(0, 1), (1, 0), (2, 3), (3, 2)])
        far = lax.ppermute(block, "dom", [(1, 2), (2, 1)])
    else:
        blocks = [block] + [
            lax.ppermute(block, "dom", [(i, (i + k) % dom_size) for i in range(dom_size)])
            for k in range(1, dom_size)
        ]

    pieces = math.gcd(heads // 4, 4)
    own = pl.pallas_call(
        functools.partial(project_kernel, pieces, local),
        out_shape=shape((rows, width)),
        in_specs=[VMEM] * 2 + [HBM],
        out_specs=VMEM,
        scratch_shapes=[pltpu.VMEM(w_uk.shape, BF16), pltpu.SemaphoreType.DMA((pieces,))],
        compiler_params=STREAM,
        name="project",
    )(nope_rows, rope_rows, w_uk)
    keys = prefix.T

    def pairs(turn, flip):
        return [
            (x * cores + c, (x + turn) % chips * cores + (c ^ flip))
            for x in range(chips)
            for c in range(cores)
        ]

    def back(turn, flip):
        return [(b, a) for a, b in pairs(turn, flip)]

    routes = [(t, f) for t in range(chips) for f in range(cores)]
    queries = [own if r == (0, 0) else lax.ppermute(own, "seq", pairs(*r)) for r in routes]
    stages = []
    half = block.shape[0] // 2
    for t in range(chips):
        asked = queries[2 * t : 2 * t + 2]
        stage = [*asked, *prefix_attention(asked, keys, rank, t == 0)]
        stages.append(stage)
        if line and t == 0:
            near, far, stage[3] = lax.optimization_barrier((near, far, stage[3]))
            outer = lax.ppermute(far, "dom", [(1, 0), (2, 3)])
            second = [
                lax.ppermute(piece, "dom", [(1, 2), (2, 1)])
                for piece in (near[: half + 16], near[half:])
            ]
        if t == 0:
            given = lax.ppermute(stage.pop(), "seq", pairs(0, 1))
    if line:
        third = []
        for piece in second:
            piece, stages[-1][3] = lax.optimization_barrier((piece, stages[-1][3]))
            third.append(lax.ppermute(piece, "dom", [(1, 0), (2, 3)]))
            stages[-1][3] = after(piece, stages[-1][3])
    if line:
        blocks = [block, near, far, outer, *second, *third]
        whole = [((i, 0), (i, half)) for i in range(4)]
        halves = [((i, 0), (i + 1, 0)) for i in (4, 6)]
        sources = (whole[0], whole[1], halves[0], whole[2], whole[3], halves[1])
    else:
        sources = tuple(((i, 0), (i, half)) for i in range(dom_size))

    part = shape((rows, rank + LANES))
    others = chips - 1
    far_results = pl.pallas_call(
        functools.partial(far_kernel, others, sources, line),
        out_shape=[shape((local * span, width))] + [part] * (2 * others),
        in_specs=[SMEM] * 3 + [VMEM] * (5 * others) + [ANY] * len(blocks),
        out_specs=[VMEM] * (1 + 2 * others),
        scratch_shapes=[
            pltpu.VMEM((local, 2, tail // 2, rank), BF16),
            pltpu.SemaphoreType.DMA((4 * local,)),
        ],
        compiler_params=PARAMS,
        name="suffix_far",
    )(ancestors, lengths, place, *[a for stage in stages[1:] for a in stage], *blocks)
    moved = far_results[0]
    keep, give = far_results[1 : 1 + others], far_results[1 + others :]
    sums = chip_merge(keep, [lax.ppermute(g, "seq", pairs(0, 1)) for g in give])
    parts = [lax.ppermute(s, "seq", back(t, 0)) for t, s in enumerate(sums, 1)]
    other = lax.ppermute(moved, "seq", pairs(0, 1))

    moved, _ = lax.optimization_barrier((moved, sums[0]))
    query, _, acc, level, mass = stages[0]
    new_caches, own_part = pl.pallas_call(
        near_kernel,
        out_shape=[shape(private_caches.shape), part],
        in_specs=[SMEM] * 3 + [VMEM] * 8,
        out_specs=[VMEM] * 2,
        compiler_params=PARAMS,
        name="suffix_near",
    )(ancestors, lengths, place, new_latent, query, acc, level, mass, given, moved, other)
    parts.append(own_part)

    head_values = pl.pallas_call(
        functools.partial(final_kernel, chips),
        out_shape=shape((local, heads, reach)),
        in_specs=[VMEM] * (chips + 1),
        out_specs=VMEM,
        scratch_shapes=[pltpu.VMEM((rows, reach), F32)],
        compiler_params=PARAMS,
        name="final",
    )(*parts, w_uv)
    return (head_values, new_caches)


def solution(mesh):
    placed = (
        P(("group", "dom"), "seq", None),
        P(("group", "dom"), "seq", None),
        P("seq", None, None),
        P("seq", None, None),
        P(("group", "seq"), None),
        P(("group", "dom"), "seq", None),
        P(("group", "dom"), None),
        P(("group", "dom")),
        P("group"),
    )
    return jax.shard_map(
        on_device,
        mesh=mesh,
        in_specs=placed,
        out_specs=(P(("group", "dom"), "seq", None), P(("group", "dom"), "seq", None)),
        check_vma=False,
    )
```

time: 49.2 us -> 59.9 us (1.22)
  waiting for transfers between devices: 13.2 us -> 19.8 us
  starting transfers between devices: 12.6 us -> 16 us
    ppermute x3, waiting for transfers between devices: 1.44 us -> 7.59 us  [on_device(): lax.ppermute(own, 'seq', pairs(*r))]
    ppermute x4 -> x7, waiting for transfers between devices: 5.33 us -> 8.2 us  [the longest x2 8.19 us: on_device(): third.append(lax.ppermute(piece, 'dom', [(1, 0), (2, 3)]))]
    ppermute x4 -> x7, starting transfers between devices: 3.73 us -> 5.92 us  [the longest x2 2.58 us: on_device(): third.append(lax.ppermute(piece, 'dom', [(1, 0), (2, 3)]))]
    ppermute x1, waiting for transfers between devices: 5.17 us -> 3.15 us  [on_device(): parts = [lax.ppermute(s, 'seq', back(t, 0)) for t, s in enumerate(sums, 1)]]
    transpose x0 -> x2, local copies, waits for them, and re-layouts: none -> 1.55 us  [on_device(): jnp.swapaxes(q, 0, 1).reshape(rows, -1)]
    unnamed x14 -> x12, local copies, waits for them, and re-layouts: 2.5 us -> 1 us
    ppermute x1, waiting for transfers between devices: 1.28 us -> 0.01 us  [on_device(): near = lax.ppermute(block, 'dom', [(0, 1), (1, 0), (2, 3), (3, 2)])]
    ppermute x1, starting transfers between devices: 0.51 us -> 1.55 us  [on_device(): parts = [lax.ppermute(s, 'seq', back(t, 0)) for t, s in enumerate(sums, 1)]]
  transfers between devices with their start and end apart: 11 -> 14, of which waited for: 6 -> 6; matrix products, arithmetic and copies ran while one was open for 0% -> 3% of each run, Pallas kernels for 33% -> 28%
where the time goes in v5:
time: 59.9 us; the launch traced here: 59.3 us
  Pallas kernels  20 us (33%)
  waiting for transfers between devices  19.8 us (33%)
  starting transfers between devices  16 us (27%)
  local copies, waits for them, and re-layouts  2.57 us (4%)
  between operations  0.87 us (1%)
    pallas_call x2, Pallas kernels, prefix_attention(): pl.pallas_call(functools.partial(prefix_kernel, len(queries), tiles), out...  11.5 us
    ppermute x2, waiting for transfers between devices, on_device(): third.append(lax.ppermute(piece, 'dom', [(1, 0), (2, 3)]))  8.19 us
    ppermute x3, waiting for transfers between devices, on_device(): lax.ppermute(own, 'seq', pairs(*r))  7.59 us
    ppermute x1, starting transfers between devices, on_device(): near = lax.ppermute(block, 'dom', [(0, 1), (1, 0), (2, 3), (3, 2)])  5.89 us
    ppermute x1, waiting for transfers between devices, on_device(): parts = [lax.ppermute(s, 'seq', back(t, 0)) for t, s in enumerate(sums, 1)]  3.15 us
    pallas_call x1, Pallas kernels, on_device(): pl.pallas_call(functools.partial(project_kernel, pieces, local), out_shap...  3.11 us
    ppermute x2, starting transfers between devices, on_device(): third.append(lax.ppermute(piece, 'dom', [(1, 0), (2, 3)]))  2.58 us
    pallas_call x1, Pallas kernels, on_device(): pl.pallas_call(functools.partial(far_kernel, others, sources, line), out_...  2.11 us
  transfers between devices with their start and end apart: 14, of which 6 were waited for; matrix products, arithmetic and copies ran while one was open for 3% of the time, Pallas kernels for 28%

profile of v5, /device:TPU:0, one launch (start us, length us, event | category | flops | bytes accessed | tf_op | source)
XLA Modules:
  0.0 59.3 jit_solution(7497631829946776867)
XLA Ops:
  0.6 1.0 %copy-done.1 = bf16[4,64,576]{2,1,0:T(8,128)(2,1)S(1)} copy-done((bf16[4,64,576]{2,1,0:T(8,128)(2,1)S(1)}, bf16[4,64,576]{2,1,0:T(8,128)(2,1)}, u32[]{:S(2)}) %copy-start.1) | copy-done | bytes 294936
  1.7 0.7 %collective-permute-start.3 = (bf16[288,512]{1,0:T(8,128)(2,1)S(1)}, bf16[288,512]{1,0:T(8,128)(2,1)S(1)}, u32[]{:S(2)}, u32[]{:S(2)}) collective-permute-start(bf16[288,512]{1,0:T(8,128)(2,1)S(1)} %pack.1.refs_8_), channel_id=1, source_target_pairs={{1,2},{2,1},{5,6},{6,5},{9,10},{10,9},{13,14},{14,13},{17,18},{18,... | collective-permute-start | bytes 884744 | tf_op jit(solution)/shard_map/ppermute | solution.py:355
  2.4 5.9 %collective-permute-start.2 = (bf16[288,512]{1,0:T(8,128)(2,1)S(1)}, bf16[288,512]{1,0:T(8,128)(2,1)S(1)}, u32[]{:S(2)}, u32[]{:S(2)}) collective-permute-start(bf16[288,512]{1,0:T(8,128)(2,1)S(1)} %pack.1.refs_8_), channel_id=1, source_target_pairs={{0,1},{1,0},{2,3},{3,2},{4,5},{5,4},{6,7},{7,6},{8,9},{9,8},{10,11... | collective-permute-start | bytes 884744 | tf_op jit(solution)/shard_map/ppermute | solution.py:354
  8.3 0.8 %copy.11 = bf16[32,4,128]{2,1,0:T(4,128)(2,1)S(1)} copy(bf16[32,4,128]{2,0,1:T(8,128)(2,1)} %bitcast.11) | data formatting | bytes 65536 | tf_op jit(solution)/shard_map/transpose | solution.py:351
  9.0 0.8 %copy.12 = bf16[32,4,64]{2,1,0:T(4,128)(2,1)S(1)} copy(bf16[32,4,64]{2,0,1:T(8,128)(2,1)} %bitcast.12) | data formatting | bytes 32768 | tf_op jit(solution)/shard_map/transpose | solution.py:351
  9.8 3.1 %project.1.refs_0_ = bf16[128,576]{1,0:T(8,128)(2,1)S(1)} custom-call(bf16[128,128]{1,0:T(8,128)(2,1)S(1)} %bitcast.7, bf16[128,64]{1,0:T(8,128)(2,1)S(1)} %bitcast.8, bf16[32,128,512]{2,1,0:T(8,128)(2,1)} %w_hbm.1), custom_call_target="tpu_custom_call" | custom-call | tf_op jit(solution)/shard_map/project/pallas_call | solution.py:363
  13.0 1.4 %collective-permute-done.4.refs_1_ = bf16[128,576]{1,0:T(8,128)(2,1)S(1)} collective-permute-done((bf16[128,576]{1,0:T(8,128)(2,1)S(1)}, bf16[128,576]{1,0:T(8,128)(2,1)S(1)}, u32[]{:S(2)}, u32[]{:S(2)}) %collective-permute-start.4) | collective-permute-done | bytes 147488 | tf_op jit(solution)/shard_map/ppermute | solution.py:385
  14.4 5.8 %prefix_attention.3 = (f32[128,512]{1,0:T(8,128)S(1)}, f32[128,128]{1,0:T(8,128)S(1)}, f32[128,128]{1,0:T(8,128)S(1)}, bf16[128,640]{1,0:T(8,128)(2,1)S(1)}) custom-call(bf16[128,576]{1,0:T(8,128)(2,1)S(1)} %project.1.refs_0_, bf16[128,576]{1,0:T(8,128)(2,1)S(1)} %collective-permute-done.4.refs_1_, bf16[576,4096]{1,0:T(8,128)(2,1)} %bitcast.9), custom_call_target="tpu_custom_call" | custom-call | tf_op jit(solution)/shard_map/prefix_attention/pallas_call | solution.py:128
  20.2 0.8 %collective-permute-start.6 = (bf16[160,512]{1,0:T(8,128)(2,1)S(1)}, bf16[160,512]{1,0:T(8,128)(2,1)S(1)}, u32[]{:S(2)}, u32[]{:S(2)}) collective-permute-start(bf16[160,512]{1,0:T(8,128)(2,1)S(1)} %slice.7), channel_id=1, source_target_pairs={{1,2},{2,1},{5,6},{6,5},{9,10},{10,9},{13,14},{14,13},{17,18},{18,... | collective-permute-start | bytes 491528 | tf_op jit(solution)/shard_map/ppermute | solution.py:396
  21.0 1.3 %collective-permute-start.1 = (bf16[128,576]{1,0:T(8,128)(2,1)S(1)}, bf16[128,576]{1,0:T(8,128)(2,1)S(1)}, u32[]{:S(2)}, u32[]{:S(2)}) collective-permute-start(bf16[128,576]{1,0:T(8,128)(2,1)S(1)} %project.1.refs_0_), channel_id=1, source_target_pairs={{0,12},{4,8},{8,4},{12,0},{1,13},{5,9},{9,5},{13,1},{2,14},{6,10},... | collective-permute-start | bytes 442376 | tf_op jit(solution)/shard_map/ppermute | solution.py:385
  22.9 0.7 %collective-permute-start.5 = (bf16[144,512]{1,0:T(8,128)(2,1)S(1)}, bf16[144,512]{1,0:T(8,128)(2,1)S(1)}, u32[]{:S(2)}, u32[]{:S(2)}) collective-permute-start(bf16[144,512]{1,0:T(8,128)(2,1)S(1)} %slice.6), channel_id=1, source_target_pairs={{1,2},{2,1},{5,6},{6,5},{9,10},{10,9},{13,14},{14,13},{17,18},{18,... | collective-permute-start | bytes 442376 | tf_op jit(solution)/shard_map/ppermute | solution.py:396
  23.6 1.3 %collective-permute-start.7 = (bf16[288,512]{1,0:T(8,128)(2,1)S(1)}, bf16[288,512]{1,0:T(8,128)(2,1)S(1)}, u32[]{:S(2)}, u32[]{:S(2)}) collective-permute-start(bf16[288,512]{1,0:T(8,128)(2,1)S(1)} %collective-permute-done.3.refs_10_), channel_id=1, source_target_pairs={{1,0},{2,3},{5,4},{6,7},{9,8},{10,11},{13,12},{14,15},{17,16},{18,... | collective-permute-start | bytes 884744 | tf_op jit(solution)/shard_map/ppermute | solution.py:394
  24.9 2.4 %collective-permute-done.1.refs_1_.refs_4_ = bf16[128,576]{1,0:T(8,128)(2,1)S(1)} collective-permute-done((bf16[128,576]{1,0:T(8,128)(2,1)S(1)}, bf16[128,576]{1,0:T(8,128)(2,1)S(1)}, u32[]{:S(2)}, u32[]{:S(2)}) %collective-permute-start.1) | collective-permute-done | bytes 147488 | tf_op jit(solution)/shard_map/ppermute | solution.py:385
  27.3 3.8 %collective-permute-done.refs_0_.refs_3_ = bf16[128,576]{1,0:T(8,128)(2,1)S(1)} collective-permute-done((bf16[128,576]{1,0:T(8,128)(2,1)S(1)}, bf16[128,576]{1,0:T(8,128)(2,1)S(1)}, u32[]{:S(2)}, u32[]{:S(2)}) %collective-permute-start) | collective-permute-done | bytes 147488 | tf_op jit(solution)/shard_map/ppermute | solution.py:385
  31.1 5.8 %prefix_attention.2 = (f32[256,512]{1,0:T(8,128)S(1)}, f32[256,128]{1,0:T(8,128)S(1)}, f32[256,128]{1,0:T(8,128)S(1)}) custom-call(bf16[128,576]{1,0:T(8,128)(2,1)S(1)} %collective-permute-done.refs_0_.refs_3_, bf16[128,576]{1,0:T(8,128)(2,1)S(1)} %collective-permute-done.1.refs_1_.refs_4_, bf16[576,4096]{1,0:T(8,128)(2,1)} %bitcast.10), custom_call_target="tpu_custom_call" | custom-call | tf_op jit(solution)/shard_map/prefix_attention/pallas_call | solution.py:128
  36.9 1.3 %collective-permute-start.8 = (bf16[160,512]{1,0:T(8,128)(2,1)S(1)}, bf16[160,512]{1,0:T(8,128)(2,1)S(1)}, u32[]{:S(2)}, u32[]{:S(2)}) collective-permute-start(bf16[160,512]{1,0:T(8,128)(2,1)S(1)} %collective-permute-done.6._.refs_12_), channel_id=1, source_target_pairs={{1,0},{2,3},{5,4},{6,7},{9,8},{10,11},{13,12},{14,15},{17,16},{18,... | collective-permute-start | bytes 491528 | tf_op jit(solution)/shard_map/ppermute | solution.py:405
  38.2 1.3 %collective-permute-start.9 = (bf16[144,512]{1,0:T(8,128)(2,1)S(1)}, bf16[144,512]{1,0:T(8,128)(2,1)S(1)}, u32[]{:S(2)}, u32[]{:S(2)}) collective-permute-start(bf16[144,512]{1,0:T(8,128)(2,1)S(1)} %collective-permute-done.5._.refs_13_), channel_id=1, source_target_pairs={{1,0},{2,3},{5,4},{6,7},{9,8},{10,11},{13,12},{14,15},{17,16},{18,... | collective-permute-start | bytes 442376 | tf_op jit(solution)/shard_map/ppermute | solution.py:405
  39.6 8.2 %collective-permute-done.9.refs_15_ = bf16[144,512]{1,0:T(8,128)(2,1)S(1)} collective-permute-done((bf16[144,512]{1,0:T(8,128)(2,1)S(1)}, bf16[144,512]{1,0:T(8,128)(2,1)S(1)}, u32[]{:S(2)}, u32[]{:S(2)}) %collective-permute-start.9) | collective-permute-done | bytes 147488 | tf_op jit(solution)/shard_map/ppermute | solution.py:405
  47.8 2.1 %suffix_far.1 = (bf16[256,576]{1,0:T(8,128)(2,1)S(1)}, bf16[128,640]{1,0:T(8,128)(2,1)S(1)}, bf16[128,640]{1,0:T(8,128)(2,1)S(1)}) custom-call(s32[4]{0:T(128)S(1)} %copy-done.3, s32[16]{0:T(128)S(1)} %copy-done.4, s32[2]{0:T(128)S(1)} %pad_add_fusion.refs_2_.place, bf16[128,576]{1,0:T(8,128)(2,1)S(1)} %collective-permute-done.refs_0_.refs_3_, ...), custom_call_target="tpu_custom_call" | custom-call | tf_op jit(solution)/shard_map/suffix_far/pallas_call | solution.py:417
  50.6 0.8 %collective-permute-done.10.refs_1_ = bf16[128,640]{1,0:T(8,128)(2,1)S(1)} collective-permute-done((bf16[128,640]{1,0:T(8,128)(2,1)S(1)}, bf16[128,640]{1,0:T(8,128)(2,1)S(1)}, u32[]{:S(2)}, u32[]{:S(2)}) %collective-permute-start.10) | collective-permute-done | bytes 163872 | tf_op jit(solution)/shard_map/ppermute | solution.py:431
  51.6 1.6 %collective-permute-start.11 = (bf16[128,640]{1,0:T(8,128)(2,1)S(1)}, bf16[128,640]{1,0:T(8,128)(2,1)S(1)}, u32[]{:S(2)}, u32[]{:S(2)}) collective-permute-start(bf16[128,640]{1,0:T(8,128)(2,1)S(1)} %chip_merge.1), channel_id=1, source_target_pairs={{8,0},{12,4},{0,8},{4,12},{9,1},{13,5},{1,9},{5,13},{10,2},{14,6},... | collective-permute-start | bytes 491528 | tf_op jit(solution)/shard_map/ppermute | solution.py:432
  53.2 1.6 %suffix_near.1 = (bf16[4,64,576]{2,1,0:T(8,128)(2,1)}, bf16[128,640]{1,0:T(8,128)(2,1)S(1)}) custom-call(s32[4]{0:T(128)S(1)} %copy-done.3, s32[16]{0:T(128)S(1)} %copy-done.4, s32[2]{0:T(128)S(1)} %pad_add_fusion.refs_2_.place, bf16[4,576]{1,0:T(4,128)(2,1)S(1)} %copy-done.2, bf16[128,576]{1,0:T(8,128)(2,1)S(1)} %project.1.refs_0_, ...), custom_call_target="tpu_custom_call" | custom-call | tf_op jit(solution)/shard_map/suffix_near/pallas_call | solution.py:437
  54.8 3.2 %collective-permute-done.11.refs_0_ = bf16[128,640]{1,0:T(8,128)(2,1)S(1)} collective-permute-done((bf16[128,640]{1,0:T(8,128)(2,1)S(1)}, bf16[128,640]{1,0:T(8,128)(2,1)S(1)}, u32[]{:S(2)}, u32[]{:S(2)}) %collective-permute-start.11) | collective-permute-done | bytes 163872 | tf_op jit(solution)/shard_map/ppermute | solution.py:432
  57.9 1.4 %final.1 = bf16[4,32,128]{2,1,0:T(8,128)(2,1)} custom-call(bf16[128,640]{1,0:T(8,128)(2,1)S(1)} %collective-permute-done.11.refs_0_, bf16[128,640]{1,0:T(8,128)(2,1)S(1)} %get-tuple-element.40.refs_1_, bf16[32,512,128]{2,1,0:T(8,128)(2,1)S(1)} %copy-done), custom_call_target="tpu_custom_call" | custom-call | tf_op jit(solution)/shard_map/final/pallas_call | solution.py:447
  (31 shorter events, 1.7 us)
Async XLA Ops:
  0.6 1.0 %copy-start.1 = (bf16[4,64,576]{2,1,0:T(8,128)(2,1)S(1)}, bf16[4,64,576]{2,1,0:T(8,128)(2,1)}, u32[]{:S(2)}) copy-start(bf16[4,64,576]{2,1,0:T(8,128)(2,1)} %cache_ref.1) | copy-start | bytes 884740
  1.7 18.5 %collective-permute-start.3 = (bf16[288,512]{1,0:T(8,128)(2,1)S(1)}, bf16[288,512]{1,0:T(8,128)(2,1)S(1)}, u32[]{:S(2)}, u32[]{:S(2)}) collective-permute-start(bf16[288,512]{1,0:T(8,128)(2,1)S(1)} %pack.1.refs_8_), channel_id=1, source_target_pairs={{1,2},{2,1},{5,6},{6,5},{9,10},{10,9},{13,14},{14,13},{17,18},{18,... | collective-permute-start | bytes 884744 | tf_op jit(solution)/shard_map/ppermute | solution.py:355
  2.4 17.8 %collective-permute-start.2 = (bf16[288,512]{1,0:T(8,128)(2,1)S(1)}, bf16[288,512]{1,0:T(8,128)(2,1)S(1)}, u32[]{:S(2)}, u32[]{:S(2)}) collective-permute-start(bf16[288,512]{1,0:T(8,128)(2,1)S(1)} %pack.1.refs_8_), channel_id=1, source_target_pairs={{0,1},{1,0},{2,3},{3,2},{4,5},{5,4},{6,7},{7,6},{8,9},{9,8},{10,11... | collective-permute-start | bytes 884744 | tf_op jit(solution)/shard_map/ppermute | solution.py:354
  12.9 1.5 %collective-permute-start.4 = (bf16[128,576]{1,0:T(8,128)(2,1)S(1)}, bf16[128,576]{1,0:T(8,128)(2,1)S(1)}, u32[]{:S(2)}, u32[]{:S(2)}) collective-permute-start(bf16[128,576]{1,0:T(8,128)(2,1)S(1)} %project.1.refs_0_), channel_id=1, source_target_pairs={{0,4},{4,0},{8,12},{12,8},{1,5},{5,1},{9,13},{13,9},{2,6},{6,2},{1... | collective-permute-start | bytes 442376 | tf_op jit(solution)/shard_map/ppermute | solution.py:385
  20.2 18.1 %copy-start.5 = (bf16[128,640]{1,0:T(8,128)(2,1)}, bf16[128,640]{1,0:T(8,128)(2,1)S(1)}, u32[]{:S(2)}) copy-start(bf16[128,640]{1,0:T(8,128)(2,1)S(1)} %get-tuple-element.37) | copy-start | bytes 491524
  20.2 27.7 %copy-start.3 = (s32[4]{0:T(128)S(1)}, s32[4]{0:T(128)}, u32[]{:S(2)}) copy-start(s32[4]{0:T(128)} %anc.1) | copy-start | bytes 52
  20.2 27.7 %copy-start.4 = (s32[16]{0:T(128)S(1)}, s32[16]{0:T(128)}, u32[]{:S(2)}) copy-start(s32[16]{0:T(128)} %lens.1) | copy-start | bytes 196
  20.2 16.7 %collective-permute-start.6 = (bf16[160,512]{1,0:T(8,128)(2,1)S(1)}, bf16[160,512]{1,0:T(8,128)(2,1)S(1)}, u32[]{:S(2)}, u32[]{:S(2)}) collective-permute-start(bf16[160,512]{1,0:T(8,128)(2,1)S(1)} %slice.7), channel_id=1, source_target_pairs={{1,2},{2,1},{5,6},{6,5},{9,10},{10,9},{13,14},{14,13},{17,18},{18,... | collective-permute-start | bytes 491528 | tf_op jit(solution)/shard_map/ppermute | solution.py:396
  21.0 6.2 %collective-permute-start.1 = (bf16[128,576]{1,0:T(8,128)(2,1)S(1)}, bf16[128,576]{1,0:T(8,128)(2,1)S(1)}, u32[]{:S(2)}, u32[]{:S(2)}) collective-permute-start(bf16[128,576]{1,0:T(8,128)(2,1)S(1)} %project.1.refs_0_), channel_id=1, source_target_pairs={{0,12},{4,8},{8,4},{12,0},{1,13},{5,9},{9,5},{13,1},{2,14},{6,10},... | collective-permute-start | bytes 442376 | tf_op jit(solution)/shard_map/ppermute | solution.py:385
  22.3 8.8 %collective-permute-start = (bf16[128,576]{1,0:T(8,128)(2,1)S(1)}, bf16[128,576]{1,0:T(8,128)(2,1)S(1)}, u32[]{:S(2)}, u32[]{:S(2)}) collective-permute-start(bf16[128,576]{1,0:T(8,128)(2,1)S(1)} %project.1.refs_0_), channel_id=1, source_target_pairs={{0,8},{4,12},{8,0},{12,4},{1,9},{5,13},{9,1},{13,5},{2,10},{6,14},... | collective-permute-start | bytes 442376 | tf_op jit(solution)/shard_map/ppermute | solution.py:385
  22.9 30.3 %copy-start.2 = (bf16[4,576]{1,0:T(4,128)(2,1)S(1)}, bf16[4,576]{1,0:T(4,128)(2,1)}, u32[]{:S(2)}) copy-start(bf16[4,576]{1,0:T(4,128)(2,1)} %fresh_ref.1) | copy-start | bytes 13828
  22.9 15.3 %collective-permute-start.5 = (bf16[144,512]{1,0:T(8,128)(2,1)S(1)}, bf16[144,512]{1,0:T(8,128)(2,1)S(1)}, u32[]{:S(2)}, u32[]{:S(2)}) collective-permute-start(bf16[144,512]{1,0:T(8,128)(2,1)S(1)} %slice.6), channel_id=1, source_target_pairs={{1,2},{2,1},{5,6},{6,5},{9,10},{10,9},{13,14},{14,13},{17,18},{18,... | collective-permute-start | bytes 442376 | tf_op jit(solution)/shard_map/ppermute | solution.py:396
  23.6 16.0 %collective-permute-start.7 = (bf16[288,512]{1,0:T(8,128)(2,1)S(1)}, bf16[288,512]{1,0:T(8,128)(2,1)S(1)}, u32[]{:S(2)}, u32[]{:S(2)}) collective-permute-start(bf16[288,512]{1,0:T(8,128)(2,1)S(1)} %collective-permute-done.3.refs_10_), channel_id=1, source_target_pairs={{1,0},{2,3},{5,4},{6,7},{9,8},{10,11},{13,12},{14,15},{17,16},{18,... | collective-permute-start | bytes 884744 | tf_op jit(solution)/shard_map/ppermute | solution.py:394
  36.9 10.9 %collective-permute-start.8 = (bf16[160,512]{1,0:T(8,128)(2,1)S(1)}, bf16[160,512]{1,0:T(8,128)(2,1)S(1)}, u32[]{:S(2)}, u32[]{:S(2)}) collective-permute-start(bf16[160,512]{1,0:T(8,128)(2,1)S(1)} %collective-permute-done.6._.refs_12_), channel_id=1, source_target_pairs={{1,0},{2,3},{5,4},{6,7},{9,8},{10,11},{13,12},{14,15},{17,16},{18,... | collective-permute-start | bytes 491528 | tf_op jit(solution)/shard_map/ppermute | solution.py:405
  38.2 9.6 %collective-permute-start.9 = (bf16[144,512]{1,0:T(8,128)(2,1)S(1)}, bf16[144,512]{1,0:T(8,128)(2,1)S(1)}, u32[]{:S(2)}, u32[]{:S(2)}) collective-permute-start(bf16[144,512]{1,0:T(8,128)(2,1)S(1)} %collective-permute-done.5._.refs_13_), channel_id=1, source_target_pairs={{1,0},{2,3},{5,4},{6,7},{9,8},{10,11},{13,12},{14,15},{17,16},{18,... | collective-permute-start | bytes 442376 | tf_op jit(solution)/shard_map/ppermute | solution.py:405
  39.5 18.4 %copy-start = (bf16[32,512,128]{2,1,0:T(8,128)(2,1)S(1)}, bf16[32,512,128]{2,1,0:T(8,128)(2,1)}, u32[]{:S(2)}) copy-start(bf16[32,512,128]{2,1,0:T(8,128)(2,1)} %refs_2_.1) | copy-start | bytes 12582916
  50.0 1.5 %collective-permute-start.10 = (bf16[128,640]{1,0:T(8,128)(2,1)S(1)}, bf16[128,640]{1,0:T(8,128)(2,1)S(1)}, u32[]{:S(2)}, u32[]{:S(2)}) collective-permute-start(bf16[128,640]{1,0:T(8,128)(2,1)S(1)} %get-tuple-element.33), channel_id=1, source_target_pairs={{0,4},{4,0},{8,12},{12,8},{1,5},{5,1},{9,13},{13,9},{2,6},{6,2},{1... | collective-permute-start | bytes 491528 | tf_op jit(solution)/shard_map/ppermute | solution.py:431
  50.0 3.1 %collective-permute-start.13 = (bf16[256,576]{1,0:T(8,128)(2,1)S(1)}, bf16[256,576]{1,0:T(8,128)(2,1)S(1)}, u32[]{:S(2)}, u32[]{:S(2)}) collective-permute-start(bf16[256,576]{1,0:T(8,128)(2,1)S(1)} %get-tuple-element.39.refs_5_), channel_id=1, source_target_pairs={{0,4},{4,0},{8,12},{12,8},{1,5},{5,1},{9,13},{13,9},{2,6},{6,2},{1... | collective-permute-start | bytes 884744 | tf_op jit(solution)/shard_map/ppermute | solution.py:433
  50.5 2.6 %collective-permute-start.12 = (bf16[128,640]{1,0:T(8,128)(2,1)}, bf16[128,640]{1,0:T(8,128)(2,1)S(1)}, u32[]{:S(2)}, u32[]{:S(2)}) collective-permute-start(bf16[128,640]{1,0:T(8,128)(2,1)} %copy-done.5), channel_id=1, source_target_pairs={{0,4},{4,0},{8,12},{12,8},{1,5},{5,1},{9,13},{13,9},{2,6},{6,2},{1... | collective-permute-start | bytes 491528 | tf_op jit(solution)/shard_map/ppermute | solution.py:400
  51.6 6.3 %collective-permute-start.11 = (bf16[128,640]{1,0:T(8,128)(2,1)S(1)}, bf16[128,640]{1,0:T(8,128)(2,1)S(1)}, u32[]{:S(2)}, u32[]{:S(2)}) collective-permute-start(bf16[128,640]{1,0:T(8,128)(2,1)S(1)} %chip_merge.1), channel_id=1, source_target_pairs={{8,0},{12,4},{0,8},{4,12},{9,1},{13,5},{1,9},{5,13},{10,2},{14,6},... | collective-permute-start | bytes 491528 | tf_op jit(solution)/shard_map/ppermute | solution.py:432

commit v6 on v5

--- a/solution.py
+++ b/solution.py
@@ -31,19 +31,18 @@
 
 def pack_kernel(rank, cache_ref, out_ref):
     local, span, width = cache_ref.shape
-    half = out_ref.shape[0] // 2
-    some = span // 2
-    tail = half - local * some
+    for p in range(local):
+        out_ref[pl.ds(p * span, span)] = cache_ref[p, :, :rank]
     rope = jnp.concatenate([cache_ref[p, :, rank:] for p in range(local)], axis=1)
-    for h in range(2):
-        for p in range(local):
-            out_ref[pl.ds(h * half + p * some, some)] = cache_ref[p, pl.ds(h * some, some), :rank]
-        out_ref[pl.ds(h * half + local * some, tail)] = jnp.concatenate(
-            [rope[h * some + i : h * some + i + tail] for i in range(0, some, tail)], axis=1
-        )
-
-
-def project_kernel(pieces, local, nope_ref, rope_ref, w_hbm, own_ref, w_ref, sems):
+    tail = out_ref.shape[0] - local * span
+    out_ref[pl.ds(local * span, tail)] = jnp.concatenate(
+        [rope[i : i + tail] for i in range(0, span, tail)], axis=1
+    )
+
+
+def project_kernel(
+    pieces, local, nope_ref, rope_ref, w_hbm, own_ref, w_ref, sems
+):
     heads, _, rank = w_ref.shape
     piece = heads // pieces
     fetches = [
@@ -52,7 +51,7 @@
         )
         for i in range(pieces)
     ]
-    for fetch in fetches[:2]:
+    for fetch in fetches:
         fetch.start()
     nope = nope_ref[...].astype(F32)
     width = nope.shape[1]
@@ -67,10 +66,7 @@
     own_ref[:, rank:] = rope_ref[...]
     for h in range(0, heads, 4):
         if h % piece == 0:
-            at = h // piece
-            fetches[at].wait()
-            if at + 2 < pieces:
-                fetches[at + 2].start()
+            fetches[h // piece].wait()
         own_ref[pl.ds(h * local, 4 * local), :rank] = jnp.concatenate(
             [pair(i) for i in (h, h + 2)], axis=0
         ).astype(BF16)
@@ -80,33 +76,39 @@
     query_refs = refs[:count]
     keys_hbm, out_ref, max_ref, sum_ref, *give_ref, acc_ref, keys_ref, sems = refs[count:]
     rank = acc_ref.shape[1]
-    parts = [pl.ds(begin, end - begin) for begin, end in zip(tiles, tiles[1:])]
+    tile = keys_ref.shape[1] // tiles
+    parts = [pl.ds(i * tile, tile) for i in range(tiles)]
     fetches = [
         pltpu.make_async_copy(keys_hbm.at[:, part], keys_ref.at[:, part], sems.at[i])
         for i, part in enumerate(parts)
     ]
-    for fetch in fetches[:2]:
+    for fetch in fetches:
         fetch.start()
     queries = jnp.concatenate([ref[...] for ref in query_refs], axis=0)
-    for i, part in enumerate(parts):
+
+    def score(i):
         fetches[i].wait()
-        if i + 2 < len(parts):
-            fetches[i + 2].start()
-        scores = jnp.dot(queries, keys_ref[:, part], preferred_element_type=F32) * SCALE2
+        return jnp.dot(queries, keys_ref[:, parts[i]], preferred_element_type=F32) * SCALE2
+
+    ahead = score(0)
+    for i in range(tiles):
+        scores = ahead
+        if i + 1 < tiles:
+            ahead = score(i + 1)
         top = jnp.max(scores, axis=1, keepdims=True)
         if i > 0:
             top = jnp.maximum(top, largest)
         weights = jnp.exp2(scores - top)
         total = jnp.sum(weights, axis=1, keepdims=True)
         acc = lax.dot_general(
-            weights.astype(BF16), keys_ref[:rank, part], NT, preferred_element_type=F32
+            weights.astype(BF16), keys_ref[:rank, parts[i]], NT, preferred_element_type=F32
         )
         if i > 0:
             factor = jnp.exp2(largest - top)
             total = total + running * factor
             acc = acc + acc_ref[...] * factor
         largest, running = top, total
-        if i < len(parts) - 1:
+        if i < tiles - 1:
             acc_ref[...] = acc
     kept = out_ref.shape[0]
     out_ref[...] = acc[:kept]
@@ -117,11 +119,10 @@
         give_ref[0][...] = packed(acc[kept:] * (1.0 / running[kept:]), level)
 
 
-def prefix_attention(queries, keys, rank, give):
+def prefix_attention(queries, keys, rank, give, tiles=4):
     rows = sum(q.shape[0] for q in queries)
     kept = queries[0].shape[0] if give else rows
     width, length = keys.shape
-    tiles = [0, length // 8] + [length * i // 4 for i in range(1, 5)]
     out = [shape((kept, rank), F32)] + [shape((kept, LANES), F32)] * 2
     if give:
         out.append(shape((rows - kept, rank + LANES)))
@@ -133,9 +134,14 @@
         scratch_shapes=[
             pltpu.VMEM((rows, rank), F32),
             pltpu.VMEM(keys.shape, BF16),
-            pltpu.SemaphoreType.DMA((len(tiles) - 1,)),
+            pltpu.SemaphoreType.DMA((tiles,)),
         ],
         compiler_params=STREAM,
+        cost_estimate=None if give else pl.CostEstimate(
+            flops=2 * rows * length * (width + rank),
+            bytes_accessed=2 * width * length,
+            transcendentals=rows * length,
+        ),
         name="prefix_attention",
     )(*queries, keys)
 
@@ -197,24 +203,23 @@
     anc, lens, place = refs[:3]
     refs = refs[3:]
     stage_refs, refs = refs[: 5 * stages], refs[5 * stages :]
-    count = max(ref for source in sources for ref, _ in source) + 1
-    block_refs, refs = refs[:count], refs[count:]
+    block_refs, refs = refs[:sources], refs[sources:]
     moved_ref, refs = refs[0], refs[1:]
     keep_refs, give_refs = refs[:stages], refs[stages : 2 * stages]
     folded, sems = refs[2 * stages :]
-    local, _, tail, rank = folded.shape
+    local, tail, rank = folded.shape
     span = moved_ref.shape[0] // local
-    some = span // 2
     rope = moved_ref.shape[1] - rank
 
-    def copies(p, source, slot):
-        found = []
-        for h, (ref, base) in enumerate(source):
-            at = pl.multiple_of(base + slot * some, 16)
-            there = moved_ref.at[pl.ds(p * span + h * some, some), pl.ds(0, rank)]
-            found.append((block_refs[ref].at[pl.ds(at, some)], there))
-            found.append((block_refs[ref].at[pl.ds(base + local * some, tail)], folded.at[p, h]))
-        return [pltpu.make_async_copy(a, b, sems.at[4 * p + i]) for i, (a, b) in enumerate(found)]
+    def copies(p, k, slot):
+        at = pl.multiple_of(slot * span, span)
+        there = moved_ref.at[pl.ds(p * span, span), pl.ds(0, rank)]
+        return (
+            pltpu.make_async_copy(block_refs[k].at[pl.ds(at, span)], there, sems.at[2 * p]),
+            pltpu.make_async_copy(
+                block_refs[k].at[pl.ds(local * span, tail)], folded.at[p], sems.at[2 * p + 1]
+            ),
+        )
 
     slots = []
     for p in range(local):
@@ -225,29 +230,27 @@
             at_end = (place[1] == 0) | (place[1] == 3)
             which = jnp.where(at_end & (apart > 1), apart + 2, apart)
         else:
-            which = lax.rem(place[1] - owner + len(sources), len(sources))
-        for k, source in enumerate(sources):
+            which = lax.rem(place[1] - owner + sources, sources)
+        for k in range(sources):
 
             @pl.when(which == k)
             def _():
-                for copy in copies(p, source, slots[p]):
+                for copy in copies(p, k, slots[p]):
                     copy.start()
 
     for p in range(local):
-        for copy in copies(p, sources[0], 0):
+        for copy in copies(p, 0, 0):
             copy.wait()
 
     for p in range(local):
-        for h in range(2):
-            for i in range(some // tail):
-                choices = [
-                    folded[p, h, :, (i * local + q) * rope : (i * local + q + 1) * rope]
-                    for q in range(local)
-                ]
-                picked = choices[0]
-                for q in range(1, local):
-                    picked = jnp.where(slots[p] == q, choices[q], picked)
-                moved_ref[pl.ds(p * span + h * some + i * tail, tail), rank:] = picked
+        for i in range(span // tail):
+            choices = [
+                folded[p, :, (i * local + q) * rope : (i * local + q + 1) * rope] for q in range(local)
+            ]
+            picked = choices[0]
+            for q in range(1, local):
+                picked = jnp.where(slots[p] == q, choices[q], picked)
+            moved_ref[pl.ds(p * span + i * tail, tail), rank:] = picked
 
     ends = [lens[anc[p]] for p in range(local)]
     for k in range(stages):
@@ -306,26 +309,11 @@
     first = lax.broadcasted_iota(jnp.int32, (2 * local, reach), 0) < local
     for h in range(0, heads, 2):
         two = latent[h * local : (h + 2) * local]
-        here = jnp.dot(two, w_ref[h], preferred_element_type=F32)
-        there = jnp.dot(two, w_ref[h + 1], preferred_element_type=F32)
-        values[pl.ds(h * local, 2 * local), :] = jnp.where(first, here, there)
+        weights = jnp.concatenate([w_ref[h], w_ref[h + 1]], axis=1)
+        both = jnp.dot(two, weights, preferred_element_type=F32)
+        values[pl.ds(h * local, 2 * local), :] = jnp.where(first, both[:, :reach], both[:, reach:])
     for p in range(local):
         out_ref[p] = values[pl.ds(p, heads, stride=local), :].astype(BF16)
-
-
-def after_kernel(_, value_ref, out_ref):
-    out_ref[...] = value_ref[...]
-
-
-def after(token, value):
-    return pl.pallas_call(
-        after_kernel,
-        out_shape=shape(value.shape, value.dtype),
-        in_specs=[ANY, VMEM],
-        out_specs=VMEM,
-        compiler_params=PARAMS,
-        name="after",
-    )(token, value)
 
 
 def on_device(q_nope, q_rope, w_uk, w_uv, prefix, private_caches, new_latent, ancestors, lengths):
@@ -370,6 +358,9 @@
         name="project",
     )(nope_rows, rope_rows, w_uk)
     keys = prefix.T
+    if line:
+        sent, own = lax.optimization_barrier((block, own))
+        inner_middle = lax.ppermute(sent, "dom", [(0, 2), (3, 1)])
 
     def pairs(turn, flip):
         return [
@@ -383,45 +374,32 @@
 
     routes = [(t, f) for t in range(chips) for f in range(cores)]
     queries = [own if r == (0, 0) else lax.ppermute(own, "seq", pairs(*r)) for r in routes]
+    if line:
+        near, far, queries[1] = lax.optimization_barrier((near, far, queries[1]))
+        outer_middle = lax.ppermute(far, "dom", [(1, 0), (2, 3)])
     stages = []
-    half = block.shape[0] // 2
     for t in range(chips):
         asked = queries[2 * t : 2 * t + 2]
         stage = [*asked, *prefix_attention(asked, keys, rank, t == 0)]
         stages.append(stage)
-        if line and t == 0:
-            near, far, stage[3] = lax.optimization_barrier((near, far, stage[3]))
-            outer = lax.ppermute(far, "dom", [(1, 0), (2, 3)])
-            second = [
-                lax.ppermute(piece, "dom", [(1, 2), (2, 1)])
-                for piece in (near[: half + 16], near[half:])
-            ]
         if t == 0:
             given = lax.ppermute(stage.pop(), "seq", pairs(0, 1))
+        if line and t == 0:
+            inner_middle, stage[3] = lax.optimization_barrier((inner_middle, stage[3]))
+            outer_far = lax.ppermute(inner_middle, "dom", [(1, 0), (2, 3)])
     if line:
-        third = []
-        for piece in second:
-            piece, stages[-1][3] = lax.optimization_barrier((piece, stages[-1][3]))
-            third.append(lax.ppermute(piece, "dom", [(1, 0), (2, 3)]))
-            stages[-1][3] = after(piece, stages[-1][3])
-    if line:
-        blocks = [block, near, far, outer, *second, *third]
-        whole = [((i, 0), (i, half)) for i in range(4)]
-        halves = [((i, 0), (i + 1, 0)) for i in (4, 6)]
-        sources = (whole[0], whole[1], halves[0], whole[2], whole[3], halves[1])
-    else:
-        sources = tuple(((i, 0), (i, half)) for i in range(dom_size))
+        blocks = [block, near, inner_middle, far, outer_middle, outer_far]
 
     part = shape((rows, rank + LANES))
     others = chips - 1
     far_results = pl.pallas_call(
-        functools.partial(far_kernel, others, sources, line),
+        functools.partial(far_kernel, others, len(blocks), line),
         out_shape=[shape((local * span, width))] + [part] * (2 * others),
         in_specs=[SMEM] * 3 + [VMEM] * (5 * others) + [ANY] * len(blocks),
         out_specs=[VMEM] * (1 + 2 * others),
         scratch_shapes=[
-            pltpu.VMEM((local, 2, tail // 2, rank), BF16),
-            pltpu.SemaphoreType.DMA((4 * local,)),
+            pltpu.VMEM((local, tail, rank), BF16),
+            pltpu.SemaphoreType.DMA((2 * local,)),
         ],
         compiler_params=PARAMS,
         name="suffix_far",

time: 59.9 us -> 45.8 us (0.76)
  waiting for transfers between devices: 19.8 us -> 9 us
  Pallas kernels: 20 us -> 17.8 us
  starting transfers between devices: 16 us -> 15.3 us
    ppermute x3, waiting for transfers between devices: 7.59 us -> 0.01 us  [on_device(): lax.ppermute(own, 'seq', pairs(*r))]
    ppermute x5 -> x3, waiting for transfers between devices: 8.2 us -> 4.21 us  [the longest x1 4.2 us: on_device(): outer_far = lax.ppermute(inner_middle, 'dom', [(1, 0), (2, 3)])]
    pallas_call x2, Pallas kernels: 11.5 us -> 10.2 us  [prefix_attention(): pl.pallas_call(functools.partial(prefix_kernel, len(queries), tiles), out...]
    ppermute x3, starting transfers between devices: 1.93 us -> 2.94 us  [on_device(): lax.ppermute(own, 'seq', pairs(*r))]
    ppermute x5 -> x3, starting transfers between devices: 5.35 us -> 4.4 us  [the longest x1 1.82 us: on_device(): inner_middle = lax.ppermute(sent, 'dom', [(0, 2), (3, 1)])]
    ppermute x1, waiting for transfers between devices: 3.15 us -> 3.97 us  [on_device(): parts = [lax.ppermute(s, 'seq', back(t, 0)) for t, s in enumerate(sums, 1)]]
    ppermute x1, starting transfers between devices: 1.55 us -> 0.75 us  [on_device(): parts = [lax.ppermute(s, 'seq', back(t, 0)) for t, s in enumerate(sums, 1)]]
    pallas_call x1, Pallas kernels: 3.11 us -> 2.46 us  [on_device(): pl.pallas_call(functools.partial(project_kernel, pieces, local), out_shap...]
  transfers between devices with their start and end apart: 14 -> 12, of which waited for: 6 -> 3; matrix products, arithmetic and copies ran while one was open for 3% -> 4% of each run, Pallas kernels for 28% -> 32%
where the time goes in v6:
time: 45.8 us; the launch traced here: 45.5 us
  Pallas kernels  17.8 us (39%)
  starting transfers between devices  15.3 us (33%)
  waiting for transfers between devices  9 us (20%)
  local copies, waits for them, and re-layouts  2.54 us (6%)
  between operations  0.78 us (2%)
    pallas_call x2, Pallas kernels, prefix_attention(): pl.pallas_call(functools.partial(prefix_kernel, len(queries), tiles), out...  10.2 us
    ppermute x1, starting transfers between devices, on_device(): near = lax.ppermute(block, 'dom', [(0, 1), (1, 0), (2, 3), (3, 2)])  5.89 us
    ppermute x1, waiting for transfers between devices, on_device(): outer_far = lax.ppermute(inner_middle, 'dom', [(1, 0), (2, 3)])  4.2 us
    ppermute x1, waiting for transfers between devices, on_device(): parts = [lax.ppermute(s, 'seq', back(t, 0)) for t, s in enumerate(sums, 1)]  3.97 us
    ppermute x3, starting transfers between devices, on_device(): lax.ppermute(own, 'seq', pairs(*r))  2.94 us
    pallas_call x1, Pallas kernels, on_device(): pl.pallas_call(functools.partial(project_kernel, pieces, local), out_shap...  2.46 us
    pallas_call x1, Pallas kernels, on_device(): pl.pallas_call(functools.partial(far_kernel, others, len(blocks), line),...  1.96 us
    ppermute x1, starting transfers between devices, on_device(): inner_middle = lax.ppermute(sent, 'dom', [(0, 2), (3, 1)])  1.82 us
  transfers between devices with their start and end apart: 12, of which 3 were waited for; matrix products, arithmetic and copies ran while one was open for 4% of the time, Pallas kernels for 32%

profile of v6, /device:TPU:0, one launch (start us, length us, event | category | flops | bytes accessed | tf_op | source)
XLA Modules:
  0.0 45.5 jit_solution(15327144467841075483)
XLA Ops:
  0.6 1.0 %copy-done.1 = bf16[4,64,576]{2,1,0:T(8,128)(2,1)S(1)} copy-done((bf16[4,64,576]{2,1,0:T(8,128)(2,1)S(1)}, bf16[4,64,576]{2,1,0:T(8,128)(2,1)}, u32[]{:S(2)}) %copy-start.1) | copy-done | bytes 294936
  1.7 0.7 %collective-permute-start.3 = (bf16[288,512]{1,0:T(8,128)(2,1)S(1)}, bf16[288,512]{1,0:T(8,128)(2,1)S(1)}, u32[]{:S(2)}, u32[]{:S(2)}) collective-permute-start(bf16[288,512]{1,0:T(8,128)(2,1)S(1)} %pack.1.refs_8_), channel_id=1, source_target_pairs={{1,2},{2,1},{5,6},{6,5},{9,10},{10,9},{13,14},{14,13},{17,18},{18,... | collective-permute-start | bytes 884744 | tf_op jit(solution)/shard_map/ppermute | solution.py:343
  2.4 5.9 %collective-permute-start.2 = (bf16[288,512]{1,0:T(8,128)(2,1)S(1)}, bf16[288,512]{1,0:T(8,128)(2,1)S(1)}, u32[]{:S(2)}, u32[]{:S(2)}) collective-permute-start(bf16[288,512]{1,0:T(8,128)(2,1)S(1)} %pack.1.refs_8_), channel_id=1, source_target_pairs={{0,1},{1,0},{2,3},{3,2},{4,5},{5,4},{6,7},{7,6},{8,9},{9,8},{10,11... | collective-permute-start | bytes 884744 | tf_op jit(solution)/shard_map/ppermute | solution.py:342
  8.3 0.8 %copy.11 = bf16[32,4,128]{2,1,0:T(4,128)(2,1)S(1)} copy(bf16[32,4,128]{2,0,1:T(8,128)(2,1)} %bitcast.11) | data formatting | bytes 65536 | tf_op jit(solution)/shard_map/transpose | solution.py:339
  9.0 0.8 %copy.12 = bf16[32,4,64]{2,1,0:T(4,128)(2,1)S(1)} copy(bf16[32,4,64]{2,0,1:T(8,128)(2,1)} %bitcast.12) | data formatting | bytes 32768 | tf_op jit(solution)/shard_map/transpose | solution.py:339
  9.8 2.5 %project.1.refs_0_ = bf16[128,576]{1,0:T(8,128)(2,1)S(1)} custom-call(bf16[128,128]{1,0:T(8,128)(2,1)S(1)} %bitcast.7, bf16[128,64]{1,0:T(8,128)(2,1)S(1)} %bitcast.8, bf16[32,128,512]{2,1,0:T(8,128)(2,1)} %w_hbm.1), custom_call_target="tpu_custom_call" | custom-call | tf_op jit(solution)/shard_map/project/pallas_call | solution.py:351
  12.3 1.8 %collective-permute-start.5 = (bf16[288,512]{1,0:T(8,128)(2,1)S(1)}, bf16[288,512]{1,0:T(8,128)(2,1)S(1)}, u32[]{:S(2)}, u32[]{:S(2)}) collective-permute-start(bf16[288,512]{1,0:T(8,128)(2,1)S(1)} %pack.1.refs_8_), channel_id=1, source_target_pairs={{0,2},{3,1},{4,6},{7,5},{8,10},{11,9},{12,14},{15,13},{16,18},{19,... | collective-permute-start | bytes 884744 | tf_op jit(solution)/shard_map/ppermute | solution.py:363
  14.2 1.6 %collective-permute-start.1 = (bf16[128,576]{1,0:T(8,128)(2,1)S(1)}, bf16[128,576]{1,0:T(8,128)(2,1)S(1)}, u32[]{:S(2)}, u32[]{:S(2)}) collective-permute-start(bf16[128,576]{1,0:T(8,128)(2,1)S(1)} %project.1.refs_0_), channel_id=1, source_target_pairs={{0,12},{4,8},{8,4},{12,0},{1,13},{5,9},{9,5},{13,1},{2,14},{6,10},... | collective-permute-start | bytes 442376 | tf_op jit(solution)/shard_map/ppermute | solution.py:376
  15.8 1.3 %collective-permute-start = (bf16[128,576]{1,0:T(8,128)(2,1)S(1)}, bf16[128,576]{1,0:T(8,128)(2,1)S(1)}, u32[]{:S(2)}, u32[]{:S(2)}) collective-permute-start(bf16[128,576]{1,0:T(8,128)(2,1)S(1)} %project.1.refs_0_), channel_id=1, source_target_pairs={{0,8},{4,12},{8,0},{12,4},{1,9},{5,13},{9,1},{13,5},{2,10},{6,14},... | collective-permute-start | bytes 442376 | tf_op jit(solution)/shard_map/ppermute | solution.py:376
  17.1 1.3 %collective-permute-start.6 = (bf16[288,512]{1,0:T(8,128)(2,1)S(1)}, bf16[288,512]{1,0:T(8,128)(2,1)S(1)}, u32[]{:S(2)}, u32[]{:S(2)}) collective-permute-start(bf16[288,512]{1,0:T(8,128)(2,1)S(1)} %collective-permute-done.3.refs_11_), channel_id=1, source_target_pairs={{1,0},{2,3},{5,4},{6,7},{9,8},{10,11},{13,12},{14,15},{17,16},{18,... | collective-permute-start | bytes 884744 | tf_op jit(solution)/shard_map/ppermute | solution.py:379
  18.4 5.1 %prefix_attention.3 = (f32[128,512]{1,0:T(8,128)S(1)}, f32[128,128]{1,0:T(8,128)S(1)}, f32[128,128]{1,0:T(8,128)S(1)}, bf16[128,640]{1,0:T(8,128)(2,1)S(1)}) custom-call(bf16[128,576]{1,0:T(8,128)(2,1)S(1)} %project.1.refs_0_, bf16[128,576]{1,0:T(8,128)(2,1)S(1)} %collective-permute-done.4.refs_1_, bf16[576,4096]{1,0:T(8,128)(2,1)} %bitcast.9), custom_call_target="tpu_custom_call" | custom-call | tf_op jit(solution)/shard_map/prefix_attention/pallas_call | solution.py:129
  23.5 1.3 %collective-permute-start.7 = (bf16[288,512]{1,0:T(8,128)(2,1)S(1)}, bf16[288,512]{1,0:T(8,128)(2,1)S(1)}, u32[]{:S(2)}, u32[]{:S(2)}) collective-permute-start(bf16[288,512]{1,0:T(8,128)(2,1)S(1)} %collective-permute-done.5.refs_10_), channel_id=1, source_target_pairs={{1,0},{2,3},{5,4},{6,7},{9,8},{10,11},{13,12},{14,15},{17,16},{18,... | collective-permute-start | bytes 884744 | tf_op jit(solution)/shard_map/ppermute | solution.py:389
  24.8 0.1 pad_add_fusion.refs_2_.place
  24.9 5.1 %prefix_attention.2 = (f32[256,512]{1,0:T(8,128)S(1)}, f32[256,128]{1,0:T(8,128)S(1)}, f32[256,128]{1,0:T(8,128)S(1)}) custom-call(bf16[128,576]{1,0:T(8,128)(2,1)S(1)} %collective-permute-done.refs_0_.refs_3_, bf16[128,576]{1,0:T(8,128)(2,1)S(1)} %collective-permute-done.1.refs_1_.refs_4_, bf16[576,4096]{1,0:T(8,128)(2,1)} %bitcast.10), custom_call_target="tpu_custom_call" | custom-call | flops 2281701376 | bytes 4718592 | tf_op jit(solution)/shard_map/prefix_attention/pallas_call | solution.py:129
  30.0 4.2 %collective-permute-done.7.refs_13_ = bf16[288,512]{1,0:T(8,128)(2,1)S(1)} collective-permute-done((bf16[288,512]{1,0:T(8,128)(2,1)S(1)}, bf16[288,512]{1,0:T(8,128)(2,1)S(1)}, u32[]{:S(2)}, u32[]{:S(2)}) %collective-permute-start.7) | collective-permute-done | bytes 294944 | tf_op jit(solution)/shard_map/ppermute | solution.py:389
  34.2 2.0 %suffix_far.1 = (bf16[256,576]{1,0:T(8,128)(2,1)S(1)}, bf16[128,640]{1,0:T(8,128)(2,1)S(1)}, bf16[128,640]{1,0:T(8,128)(2,1)S(1)}) custom-call(s32[4]{0:T(128)S(1)} %copy-done.3, s32[16]{0:T(128)S(1)} %copy-done.4, s32[2]{0:T(128)S(1)} %pad_add_fusion.refs_2_.place, bf16[128,576]{1,0:T(8,128)(2,1)S(1)} %collective-permute-done.refs_0_.refs_3_, ...), custom_call_target="tpu_custom_call" | custom-call | tf_op jit(solution)/shard_map/suffix_far/pallas_call | solution.py:395
  36.2 0.5 %collective-permute-start.11 = (bf16[256,576]{1,0:T(8,128)(2,1)S(1)}, bf16[256,576]{1,0:T(8,128)(2,1)S(1)}, u32[]{:S(2)}, u32[]{:S(2)}) collective-permute-start(bf16[256,576]{1,0:T(8,128)(2,1)S(1)} %get-tuple-element.39.refs_5_), channel_id=1, source_target_pairs={{0,4},{4,0},{8,12},{12,8},{1,5},{5,1},{9,13},{13,9},{2,6},{6,2},{1... | collective-permute-start | bytes 884744 | tf_op jit(solution)/shard_map/ppermute | solution.py:411
  36.7 0.1 collective-permute-start.10
  36.8 0.8 %collective-permute-done.8.refs_1_ = bf16[128,640]{1,0:T(8,128)(2,1)S(1)} collective-permute-done((bf16[128,640]{1,0:T(8,128)(2,1)S(1)}, bf16[128,640]{1,0:T(8,128)(2,1)S(1)}, u32[]{:S(2)}, u32[]{:S(2)}) %collective-permute-start.8) | collective-permute-done | bytes 163872 | tf_op jit(solution)/shard_map/ppermute | solution.py:409
  37.6 0.2 chip_merge.1
  37.8 0.7 %collective-permute-start.9 = (bf16[128,640]{1,0:T(8,128)(2,1)S(1)}, bf16[128,640]{1,0:T(8,128)(2,1)S(1)}, u32[]{:S(2)}, u32[]{:S(2)}) collective-permute-start(bf16[128,640]{1,0:T(8,128)(2,1)S(1)} %chip_merge.1), channel_id=1, source_target_pairs={{8,0},{12,4},{0,8},{4,12},{9,1},{13,5},{1,9},{5,13},{10,2},{14,6},... | collective-permute-start | bytes 491528 | tf_op jit(solution)/shard_map/ppermute | solution.py:410
  38.6 1.6 %suffix_near.1 = (bf16[4,64,576]{2,1,0:T(8,128)(2,1)}, bf16[128,640]{1,0:T(8,128)(2,1)S(1)}) custom-call(s32[4]{0:T(128)S(1)} %copy-done.3, s32[16]{0:T(128)S(1)} %copy-done.4, s32[2]{0:T(128)S(1)} %pad_add_fusion.refs_2_.place, bf16[4,576]{1,0:T(4,128)(2,1)S(1)} %copy-done.2, bf16[128,576]{1,0:T(8,128)(2,1)S(1)} %project.1.refs_0_, ...), custom_call_target="tpu_custom_call" | custom-call | tf_op jit(solution)/shard_map/suffix_near/pallas_call | solution.py:415
  40.2 4.0 %collective-permute-done.9.refs_0_ = bf16[128,640]{1,0:T(8,128)(2,1)S(1)} collective-permute-done((bf16[128,640]{1,0:T(8,128)(2,1)S(1)}, bf16[128,640]{1,0:T(8,128)(2,1)S(1)}, u32[]{:S(2)}, u32[]{:S(2)}) %collective-permute-start.9) | collective-permute-done | bytes 163872 | tf_op jit(solution)/shard_map/ppermute | solution.py:410
  44.1 1.4 %final.1 = bf16[4,32,128]{2,1,0:T(8,128)(2,1)} custom-call(bf16[128,640]{1,0:T(8,128)(2,1)S(1)} %collective-permute-done.9.refs_0_, bf16[128,640]{1,0:T(8,128)(2,1)S(1)} %get-tuple-element.40.refs_1_, bf16[32,512,128]{2,1,0:T(8,128)(2,1)S(1)} %copy-done), custom_call_target="tpu_custom_call" | custom-call | tf_op jit(solution)/shard_map/final/pallas_call | solution.py:425
  (21 shorter events, 0.3 us)
Async XLA Ops:
  0.6 1.0 %copy-start.1 = (bf16[4,64,576]{2,1,0:T(8,128)(2,1)S(1)}, bf16[4,64,576]{2,1,0:T(8,128)(2,1)}, u32[]{:S(2)}) copy-start(bf16[4,64,576]{2,1,0:T(8,128)(2,1)} %cache_ref.1) | copy-start | bytes 884740
  1.7 15.4 %collective-permute-start.3 = (bf16[288,512]{1,0:T(8,128)(2,1)S(1)}, bf16[288,512]{1,0:T(8,128)(2,1)S(1)}, u32[]{:S(2)}, u32[]{:S(2)}) collective-permute-start(bf16[288,512]{1,0:T(8,128)(2,1)S(1)} %pack.1.refs_8_), channel_id=1, source_target_pairs={{1,2},{2,1},{5,6},{6,5},{9,10},{10,9},{13,14},{14,13},{17,18},{18,... | collective-permute-start | bytes 884744 | tf_op jit(solution)/shard_map/ppermute | solution.py:343
  2.4 14.7 %collective-permute-start.2 = (bf16[288,512]{1,0:T(8,128)(2,1)S(1)}, bf16[288,512]{1,0:T(8,128)(2,1)S(1)}, u32[]{:S(2)}, u32[]{:S(2)}) collective-permute-start(bf16[288,512]{1,0:T(8,128)(2,1)S(1)} %pack.1.refs_8_), channel_id=1, source_target_pairs={{0,1},{1,0},{2,3},{3,2},{4,5},{5,4},{6,7},{7,6},{8,9},{9,8},{10,11... | collective-permute-start | bytes 884744 | tf_op jit(solution)/shard_map/ppermute | solution.py:342
  12.3 11.2 %collective-permute-start.5 = (bf16[288,512]{1,0:T(8,128)(2,1)S(1)}, bf16[288,512]{1,0:T(8,128)(2,1)S(1)}, u32[]{:S(2)}, u32[]{:S(2)}) collective-permute-start(bf16[288,512]{1,0:T(8,128)(2,1)S(1)} %pack.1.refs_8_), channel_id=1, source_target_pairs={{0,2},{3,1},{4,6},{7,5},{8,10},{11,9},{12,14},{15,13},{16,18},{19,... | collective-permute-start | bytes 884744 | tf_op jit(solution)/shard_map/ppermute | solution.py:363
  14.1 1.7 %collective-permute-start.4 = (bf16[128,576]{1,0:T(8,128)(2,1)S(1)}, bf16[128,576]{1,0:T(8,128)(2,1)S(1)}, u32[]{:S(2)}, u32[]{:S(2)}) collective-permute-start(bf16[128,576]{1,0:T(8,128)(2,1)S(1)} %project.1.refs_0_), channel_id=1, source_target_pairs={{0,4},{4,0},{8,12},{12,8},{1,5},{5,1},{9,13},{13,9},{2,6},{6,2},{1... | collective-permute-start | bytes 442376 | tf_op jit(solution)/shard_map/ppermute | solution.py:376
  14.2 10.7 %collective-permute-start.1 = (bf16[128,576]{1,0:T(8,128)(2,1)S(1)}, bf16[128,576]{1,0:T(8,128)(2,1)S(1)}, u32[]{:S(2)}, u32[]{:S(2)}) collective-permute-start(bf16[128,576]{1,0:T(8,128)(2,1)S(1)} %project.1.refs_0_), channel_id=1, source_target_pairs={{0,12},{4,8},{8,4},{12,0},{1,13},{5,9},{9,5},{13,1},{2,14},{6,10},... | collective-permute-start | bytes 442376 | tf_op jit(solution)/shard_map/ppermute | solution.py:376
  15.8 9.1 %collective-permute-start = (bf16[128,576]{1,0:T(8,128)(2,1)S(1)}, bf16[128,576]{1,0:T(8,128)(2,1)S(1)}, u32[]{:S(2)}, u32[]{:S(2)}) collective-permute-start(bf16[128,576]{1,0:T(8,128)(2,1)S(1)} %project.1.refs_0_), channel_id=1, source_target_pairs={{0,8},{4,12},{8,0},{12,4},{1,9},{5,13},{9,1},{13,5},{2,10},{6,14},... | collective-permute-start | bytes 442376 | tf_op jit(solution)/shard_map/ppermute | solution.py:376
  17.1 12.9 %collective-permute-start.6 = (bf16[288,512]{1,0:T(8,128)(2,1)S(1)}, bf16[288,512]{1,0:T(8,128)(2,1)S(1)}, u32[]{:S(2)}, u32[]{:S(2)}) collective-permute-start(bf16[288,512]{1,0:T(8,128)(2,1)S(1)} %collective-permute-done.3.refs_11_), channel_id=1, source_target_pairs={{1,0},{2,3},{5,4},{6,7},{9,8},{10,11},{13,12},{14,15},{17,16},{18,... | collective-permute-start | bytes 884744 | tf_op jit(solution)/shard_map/ppermute | solution.py:379
  23.5 10.7 %collective-permute-start.7 = (bf16[288,512]{1,0:T(8,128)(2,1)S(1)}, bf16[288,512]{1,0:T(8,128)(2,1)S(1)}, u32[]{:S(2)}, u32[]{:S(2)}) collective-permute-start(bf16[288,512]{1,0:T(8,128)(2,1)S(1)} %collective-permute-done.5.refs_10_), channel_id=1, source_target_pairs={{1,0},{2,3},{5,4},{6,7},{9,8},{10,11},{13,12},{14,15},{17,16},{18,... | collective-permute-start | bytes 884744 | tf_op jit(solution)/shard_map/ppermute | solution.py:389
  24.9 9.3 %copy-start.3 = (s32[4]{0:T(128)S(1)}, s32[4]{0:T(128)}, u32[]{:S(2)}) copy-start(s32[4]{0:T(128)} %anc.1) | copy-start | bytes 52
  24.9 9.3 %copy-start.4 = (s32[16]{0:T(128)S(1)}, s32[16]{0:T(128)}, u32[]{:S(2)}) copy-start(s32[16]{0:T(128)} %lens.1) | copy-start | bytes 196
  24.9 13.7 %copy-start.2 = (bf16[4,576]{1,0:T(4,128)(2,1)S(1)}, bf16[4,576]{1,0:T(4,128)(2,1)}, u32[]{:S(2)}) copy-start(bf16[4,576]{1,0:T(4,128)(2,1)} %fresh_ref.1) | copy-start | bytes 13828
  29.9 14.2 %copy-start = (bf16[32,512,128]{2,1,0:T(8,128)(2,1)S(1)}, bf16[32,512,128]{2,1,0:T(8,128)(2,1)}, u32[]{:S(2)}) copy-start(bf16[32,512,128]{2,1,0:T(8,128)(2,1)} %refs_2_.1) | copy-start | bytes 12582916
  36.1 1.5 %collective-permute-start.8 = (bf16[128,640]{1,0:T(8,128)(2,1)S(1)}, bf16[128,640]{1,0:T(8,128)(2,1)S(1)}, u32[]{:S(2)}, u32[]{:S(2)}) collective-permute-start(bf16[128,640]{1,0:T(8,128)(2,1)S(1)} %get-tuple-element.33), channel_id=1, source_target_pairs={{0,4},{4,0},{8,12},{12,8},{1,5},{5,1},{9,13},{13,9},{2,6},{6,2},{1... | collective-permute-start | bytes 491528 | tf_op jit(solution)/shard_map/ppermute | solution.py:409
  36.2 2.3 %collective-permute-start.11 = (bf16[256,576]{1,0:T(8,128)(2,1)S(1)}, bf16[256,576]{1,0:T(8,128)(2,1)S(1)}, u32[]{:S(2)}, u32[]{:S(2)}) collective-permute-start(bf16[256,576]{1,0:T(8,128)(2,1)S(1)} %get-tuple-element.39.refs_5_), channel_id=1, source_target_pairs={{0,4},{4,0},{8,12},{12,8},{1,5},{5,1},{9,13},{13,9},{2,6},{6,2},{1... | collective-permute-start | bytes 884744 | tf_op jit(solution)/shard_map/ppermute | solution.py:411
  36.7 1.8 %collective-permute-start.10 = (bf16[128,640]{1,0:T(8,128)(2,1)S(1)}, bf16[128,640]{1,0:T(8,128)(2,1)S(1)}, u32[]{:S(2)}, u32[]{:S(2)}) collective-permute-start(bf16[128,640]{1,0:T(8,128)(2,1)S(1)} %get-tuple-element.37), channel_id=1, source_target_pairs={{0,4},{4,0},{8,12},{12,8},{1,5},{5,1},{9,13},{13,9},{2,6},{6,2},{1... | collective-permute-start | bytes 491528 | tf_op jit(solution)/shard_map/ppermute | solution.py:386
  37.8 6.3 %collective-permute-start.9 = (bf16[128,640]{1,0:T(8,128)(2,1)S(1)}, bf16[128,640]{1,0:T(8,128)(2,1)S(1)}, u32[]{:S(2)}, u32[]{:S(2)}) collective-permute-start(bf16[128,640]{1,0:T(8,128)(2,1)S(1)} %chip_merge.1), channel_id=1, source_target_pairs={{8,0},{12,4},{0,8},{4,12},{9,1},{13,5},{1,9},{5,13},{10,2},{14,6},... | collective-permute-start | bytes 491528 | tf_op jit(solution)/shard_map/ppermute | solution.py:410

commit v7 on v6

--- a/solution.py
+++ b/solution.py
@@ -29,7 +29,7 @@
     return jax.ShapeDtypeStruct(dims, dtype)
 
 
-def pack_kernel(rank, cache_ref, out_ref):
+def pack_kernel(rank, anc, cache_ref, out_ref, ext_ref):
     local, span, width = cache_ref.shape
     for p in range(local):
         out_ref[pl.ds(p * span, span)] = cache_ref[p, :, :rank]
@@ -38,6 +38,13 @@
     out_ref[pl.ds(local * span, tail)] = jnp.concatenate(
         [rope[i : i + tail] for i in range(0, span, tail)], axis=1
     )
+    whole = out_ref.shape[0]
+    ext_ref[pl.ds(0, whole)] = out_ref[...]
+    lane = lax.broadcasted_iota(jnp.int32, (ext_ref.shape[0] - whole, rank), 1)
+    names = jnp.zeros(lane.shape, F32)
+    for p in range(local):
+        names = jnp.where(lane == p, anc[p].astype(F32), names)
+    ext_ref[pl.ds(whole, ext_ref.shape[0] - whole)] = names.astype(BF16)
 
 
 def project_kernel(
@@ -199,6 +206,60 @@
     return packed(acc * (1.0 / total), top + jnp.log2(total))
 
 
+def gather_blocks(block_refs, picks, latents_ref, folded, sems):
+    local, tail, rank = folded.shape
+    span = latents_ref.shape[0] // local
+
+    def copies(p, k, slot):
+        at = pl.multiple_of(slot * span, span)
+        return (
+            pltpu.make_async_copy(
+                block_refs[k].at[pl.ds(at, span)],
+                latents_ref.at[pl.ds(p * span, span), pl.ds(0, rank)],
+                sems.at[2 * p],
+            ),
+            pltpu.make_async_copy(
+                block_refs[k].at[pl.ds(local * span, tail)], folded.at[p], sems.at[2 * p + 1]
+            ),
+        )
+
+    for p, (which, slot) in enumerate(picks):
+        for k in range(len(block_refs)):
+
+            @pl.when(which == k)
+            def _():
+                for copy in copies(p, k, slot):
+                    copy.start()
+
+    for p in range(local):
+        for copy in copies(p, 0, 0):
+            copy.wait()
+
+
+def rope_rows(folded, p, i, slot, rope):
+    local = folded.shape[0]
+    choices = [folded[p, :, (i * local + q) * rope : (i * local + q + 1) * rope] for q in range(local)]
+    picked = choices[0]
+    for q in range(1, local):
+        picked = jnp.where(slot == q, choices[q], picked)
+    return picked
+
+
+def select_kernel(rope, theirs, place, *refs):
+    block_refs, (_, out_ref, folded, sems) = refs[:-4], refs[-4:]
+    local, tail, rank = folded.shape
+    span = (out_ref.shape[0] - tail) // local
+    picks = []
+    for p in range(local):
+        owner = lax.div(theirs[p], local)
+        picks.append((jnp.bitwise_xor(owner, place[1]), lax.rem(theirs[p], local)))
+    gather_blocks(block_refs, picks, out_ref.at[pl.ds(0, local * span)], folded, sems)
+    rows = [
+        rope_rows(folded, p, i, picks[p][1], rope) for i in range(span // tail) for p in range(local)
+    ]
+    out_ref[pl.ds(local * span, tail)] = jnp.concatenate(rows, axis=1)
+
+
 def far_kernel(stages, sources, line, *refs):
     anc, lens, place = refs[:3]
     refs = refs[3:]
@@ -211,46 +272,23 @@
     span = moved_ref.shape[0] // local
     rope = moved_ref.shape[1] - rank
 
-    def copies(p, k, slot):
-        at = pl.multiple_of(slot * span, span)
-        there = moved_ref.at[pl.ds(p * span, span), pl.ds(0, rank)]
-        return (
-            pltpu.make_async_copy(block_refs[k].at[pl.ds(at, span)], there, sems.at[2 * p]),
-            pltpu.make_async_copy(
-                block_refs[k].at[pl.ds(local * span, tail)], folded.at[p], sems.at[2 * p + 1]
-            ),
-        )
-
-    slots = []
-    for p in range(local):
-        owner = lax.div(anc[p], local)
-        slots.append(lax.rem(anc[p], local))
+    picks = []
+    for p in range(local):
+        owner, slot = lax.div(anc[p], local), lax.rem(anc[p], local)
         if line:
-            apart = jnp.bitwise_xor(owner, place[1])
-            at_end = (place[1] == 0) | (place[1] == 3)
-            which = jnp.where(at_end & (apart > 1), apart + 2, apart)
+            which = jnp.bitwise_xor(owner, place[1])
+            chosen = ((place[1] == 0) | (place[1] == 3)) & (which != 0)
+            which = jnp.where(chosen, sources - 1, which)
+            slot = jnp.where(chosen, p, slot)
         else:
             which = lax.rem(place[1] - owner + sources, sources)
-        for k in range(sources):
-
-            @pl.when(which == k)
-            def _():
-                for copy in copies(p, k, slots[p]):
-                    copy.start()
-
-    for p in range(local):
-        for copy in copies(p, 0, 0):
-            copy.wait()
-
+        picks.append((which, slot))
+    gather_blocks(block_refs, picks, moved_ref, folded, sems)
     for p in range(local):
         for i in range(span // tail):
-            choices = [
-                folded[p, :, (i * local + q) * rope : (i * local + q + 1) * rope] for q in range(local)
-            ]
-            picked = choices[0]
-            for q in range(1, local):
-                picked = jnp.where(slots[p] == q, choices[q], picked)
-            moved_ref[pl.ds(p * span + i * tail, tail), rank:] = picked
+            moved_ref[pl.ds(p * span + i * tail, tail), rank:] = rope_rows(
+                folded, p, i, picks[p][1], rope
+            )
 
     ends = [lens[anc[p]] for p in range(local)]
     for k in range(stages):
@@ -328,19 +366,20 @@
     place = jnp.stack([lax.axis_index("seq"), lax.axis_index("dom")]).astype(jnp.int32)
     tail = span * local * rope // rank
 
-    block = pl.pallas_call(
+    whole = local * span + tail
+    block, extended = pl.pallas_call(
         functools.partial(pack_kernel, rank),
-        out_shape=shape((local * span + tail, rank)),
-        in_specs=[VMEM],
-        out_specs=VMEM,
+        out_shape=(shape((whole, rank)), shape((whole + 16, rank))),
+        in_specs=[SMEM, VMEM],
+        out_specs=(VMEM,) * 2,
         compiler_params=PARAMS,
         name="pack",
-    )(private_caches)
+    )(ancestors, private_caches)
     nope_rows, rope_rows = (jnp.swapaxes(q, 0, 1).reshape(rows, -1) for q in (q_nope, q_rope))
     line = dom_size == 4
     if line:
-        near = lax.ppermute(block, "dom", [(0, 1), (1, 0), (2, 3), (3, 2)])
         far = lax.ppermute(block, "dom", [(1, 2), (2, 1)])
+        near = lax.ppermute(extended, "dom", [(0, 1), (3, 2)])
     else:
         blocks = [block] + [
             lax.ppermute(block, "dom", [(i, (i + k) % dom_size) for i in range(dom_size)])
@@ -360,7 +399,7 @@
     keys = prefix.T
     if line:
         sent, own = lax.optimization_barrier((block, own))
-        inner_middle = lax.ppermute(sent, "dom", [(0, 2), (3, 1)])
+        middle = lax.ppermute(sent, "dom", [(0, 2), (3, 1)])
 
     def pairs(turn, flip):
         return [
@@ -375,8 +414,7 @@
     routes = [(t, f) for t in range(chips) for f in range(cores)]
     queries = [own if r == (0, 0) else lax.ppermute(own, "seq", pairs(*r)) for r in routes]
     if line:
-        near, far, queries[1] = lax.optimization_barrier((near, far, queries[1]))
-        outer_middle = lax.ppermute(far, "dom", [(1, 0), (2, 3)])
+        far, queries[1] = lax.optimization_barrier((far, queries[1]))
     stages = []
     for t in range(chips):
         asked = queries[2 * t : 2 * t + 2]
@@ -385,10 +423,21 @@
         if t == 0:
             given = lax.ppermute(stage.pop(), "seq", pairs(0, 1))
         if line and t == 0:
-            inner_middle, stage[3] = lax.optimization_barrier((inner_middle, stage[3]))
-            outer_far = lax.ppermute(inner_middle, "dom", [(1, 0), (2, 3)])
-    if line:
-        blocks = [block, near, inner_middle, far, outer_middle, outer_far]
+            blocks = [block, near, middle, far]
+            theirs = near[whole, :local].astype(F32).astype(jnp.int32)
+            chosen = pl.pallas_call(
+                functools.partial(select_kernel, rope),
+                out_shape=shape((whole, rank)),
+                in_specs=[SMEM] * 2 + [ANY] * 5,
+                out_specs=VMEM,
+                scratch_shapes=[
+                    pltpu.VMEM((local, tail, rank), BF16),
+                    pltpu.SemaphoreType.DMA((2 * local,)),
+                ],
+                compiler_params=PARAMS,
+                name="select",
+            )(theirs, place, *blocks, stage[3])
+            blocks.append(lax.ppermute(chosen, "dom", [(1, 0), (2, 3)]))
 
     part = shape((rows, rank + LANES))
     others = chips - 1

time: 45.8 us -> 49.2 us (1.074)
  Pallas kernels: 17.8 us -> 19.8 us
  waiting for transfers between devices: 9 us -> 10.4 us
  starting transfers between devices: 15.3 us -> 14.5 us
  local copies, waits for them, and re-layouts: 2.54 us -> 3.2 us
    pallas_call x1 -> x2, Pallas kernels: 0.08 us -> 2.13 us  [the longest x1 1.52 us: on_device(): pl.pallas_call(functools.partial(select_kernel, rope), out_shape=shape((w...]
    ppermute x4 -> x3, waiting for transfers between devices: 4.21 us -> 5.47 us  [the longest x1 4.77 us: on_device(): blocks.append(lax.ppermute(chosen, 'dom', [(1, 0), (2, 3)]))]
    ppermute x3, starting transfers between devices: 2.94 us -> 2.23 us  [on_device(): lax.ppermute(own, 'seq', pairs(*r))]
    unnamed x10 -> x12, local copies, waits for them, and re-layouts: 0.98 us -> 1.65 us
    ppermute x4 -> x3, starting transfers between devices: 10.3 us -> 10.3 us  [the longest x1 4.94 us: on_device(): near = lax.ppermute(extended, 'dom', [(0, 1), (3, 2)])]
  transfers between devices with their start and end apart: 12 -> 11, of which waited for: 3 -> 4; matrix products, arithmetic and copies ran while one was open for 4% -> 3% of each run, Pallas kernels for 32% -> 33%
where the time goes in v7:
time: 49.2 us; the launch traced here: 48.8 us
  Pallas kernels  19.8 us (40%)
  starting transfers between devices  14.5 us (29%)
  waiting for transfers between devices  10.4 us (21%)
  local copies, waits for them, and re-layouts  3.2 us (7%)
  between operations  0.81 us (2%)
    pallas_call x2, Pallas kernels, prefix_attention(): pl.pallas_call(functools.partial(prefix_kernel, len(queries), tiles), out...  10.1 us
    ppermute x1, starting transfers between devices, on_device(): near = lax.ppermute(extended, 'dom', [(0, 1), (3, 2)])  4.94 us
    ppermute x1, waiting for transfers between devices, on_device(): blocks.append(lax.ppermute(chosen, 'dom', [(1, 0), (2, 3)]))  4.77 us
    ppermute x1, waiting for transfers between devices, on_device(): parts = [lax.ppermute(s, 'seq', back(t, 0)) for t, s in enumerate(sums, 1)]  4.11 us
    ppermute x1, starting transfers between devices, on_device(): middle = lax.ppermute(sent, 'dom', [(0, 2), (3, 1)])  3.97 us
    pallas_call x1, Pallas kernels, on_device(): pl.pallas_call(functools.partial(project_kernel, pieces, local), out_shap...  2.46 us
    ppermute x3, starting transfers between devices, on_device(): lax.ppermute(own, 'seq', pairs(*r))  2.23 us
    pallas_call x1, Pallas kernels, on_device(): pl.pallas_call(functools.partial(far_kernel, others, len(blocks), line),...  1.92 us
  transfers between devices with their start and end apart: 11, of which 4 were waited for; matrix products, arithmetic and copies ran while one was open for 3% of the time, Pallas kernels for 33%

profile of v7, /device:TPU:0, one launch (start us, length us, event | category | flops | bytes accessed | tf_op | source)
XLA Modules:
  0.0 48.8 jit_solution(6847487825994690143)
XLA Ops:
  0.6 1.0 %copy-done.1 = bf16[4,64,576]{2,1,0:T(8,128)(2,1)S(1)} copy-done((bf16[4,64,576]{2,1,0:T(8,128)(2,1)S(1)}, bf16[4,64,576]{2,1,0:T(8,128)(2,1)}, u32[]{:S(2)}) %copy-start.1) | copy-done | bytes 294936
  1.6 0.7 %copy-done.3 = s32[4]{0:T(128)S(1)} copy-done((s32[4]{0:T(128)S(1)}, s32[4]{0:T(128)}, u32[]{:S(2)}) %copy-start.3) | copy-done | bytes 40
  2.3 0.6 %pack.1 = (bf16[288,512]{1,0:T(8,128)(2,1)S(1)}, bf16[304,512]{1,0:T(8,128)(2,1)S(1)}) custom-call(s32[4]{0:T(128)S(1)} %copy-done.3, bf16[4,64,576]{2,1,0:T(8,128)(2,1)S(1)} %copy-done.1), custom_call_target="tpu_custom_call" | custom-call | tf_op jit(solution)/shard_map/pack/pallas_call | solution.py:370
  2.9 4.9 %collective-permute-start.2 = (bf16[304,512]{1,0:T(8,128)(2,1)S(1)}, bf16[304,512]{1,0:T(8,128)(2,1)S(1)}, u32[]{:S(2)}, u32[]{:S(2)}) collective-permute-start(bf16[304,512]{1,0:T(8,128)(2,1)S(1)} %get-tuple-element.26), channel_id=1, source_target_pairs={{0,1},{3,2},{4,5},{7,6},{8,9},{11,10},{12,13},{15,14},{16,17},{19,... | collective-permute-start | bytes 933896 | tf_op jit(solution)/shard_map/ppermute | solution.py:382
  7.8 0.7 %collective-permute-start.4 = (bf16[288,512]{1,0:T(8,128)(2,1)S(1)}, bf16[288,512]{1,0:T(8,128)(2,1)S(1)}, u32[]{:S(2)}, u32[]{:S(2)}) collective-permute-start(bf16[288,512]{1,0:T(8,128)(2,1)S(1)} %get-tuple-element.27.refs_0_.refs_8_), channel_id=1, source_target_pairs={{1,2},{2,1},{5,6},{6,5},{9,10},{10,9},{13,14},{14,13},{17,18},{18,... | collective-permute-start | bytes 884744 | tf_op jit(solution)/shard_map/ppermute | solution.py:381
  8.5 0.8 %copy.11 = bf16[32,4,128]{2,1,0:T(4,128)(2,1)S(1)} copy(bf16[32,4,128]{2,0,1:T(8,128)(2,1)} %bitcast.13) | data formatting | bytes 65536 | tf_op jit(solution)/shard_map/transpose | solution.py:378
  9.3 0.8 %copy.12 = bf16[32,4,64]{2,1,0:T(4,128)(2,1)S(1)} copy(bf16[32,4,64]{2,0,1:T(8,128)(2,1)} %bitcast.14) | data formatting | bytes 32768 | tf_op jit(solution)/shard_map/transpose | solution.py:378
  10.1 2.5 %project.1.refs_0_ = bf16[128,576]{1,0:T(8,128)(2,1)S(1)} custom-call(bf16[128,128]{1,0:T(8,128)(2,1)S(1)} %bitcast.9, bf16[128,64]{1,0:T(8,128)(2,1)S(1)} %bitcast.10, bf16[32,128,512]{2,1,0:T(8,128)(2,1)} %w_hbm.1), custom_call_target="tpu_custom_call" | custom-call | tf_op jit(solution)/shard_map/project/pallas_call | solution.py:390
  12.6 1.6 %collective-permute-start.1 = (bf16[128,576]{1,0:T(8,128)(2,1)S(1)}, bf16[128,576]{1,0:T(8,128)(2,1)S(1)}, u32[]{:S(2)}, u32[]{:S(2)}) collective-permute-start(bf16[128,576]{1,0:T(8,128)(2,1)S(1)} %project.1.refs_0_), channel_id=1, source_target_pairs={{0,12},{4,8},{8,4},{12,0},{1,13},{5,9},{9,5},{13,1},{2,14},{6,10},... | collective-permute-start | bytes 442376 | tf_op jit(solution)/shard_map/ppermute | solution.py:415
  14.2 4.0 %collective-permute-start.3 = (bf16[288,512]{1,0:T(8,128)(2,1)S(1)}, bf16[288,512]{1,0:T(8,128)(2,1)S(1)}, u32[]{:S(2)}, u32[]{:S(2)}) collective-permute-start(bf16[288,512]{1,0:T(8,128)(2,1)S(1)} %get-tuple-element.27.refs_0_.refs_8_), channel_id=1, source_target_pairs={{0,2},{3,1},{4,6},{7,5},{8,10},{11,9},{12,14},{15,13},{16,18},{19,... | collective-permute-start | bytes 884744 | tf_op jit(solution)/shard_map/ppermute | solution.py:402
  18.3 0.5 %collective-permute-start = (bf16[128,576]{1,0:T(8,128)(2,1)S(1)}, bf16[128,576]{1,0:T(8,128)(2,1)S(1)}, u32[]{:S(2)}, u32[]{:S(2)}) collective-permute-start(bf16[128,576]{1,0:T(8,128)(2,1)S(1)} %project.1.refs_0_), channel_id=1, source_target_pairs={{0,8},{4,12},{8,0},{12,4},{1,9},{5,13},{9,1},{13,5},{2,10},{6,14},... | collective-permute-start | bytes 442376 | tf_op jit(solution)/shard_map/ppermute | solution.py:415
  18.8 5.1 %prefix_attention.3 = (f32[128,512]{1,0:T(8,128)S(1)}, f32[128,128]{1,0:T(8,128)S(1)}, f32[128,128]{1,0:T(8,128)S(1)}, bf16[128,640]{1,0:T(8,128)(2,1)S(1)}) custom-call(bf16[128,576]{1,0:T(8,128)(2,1)S(1)} %project.1.refs_0_, bf16[128,576]{1,0:T(8,128)(2,1)S(1)} %collective-permute-done.5.refs_1_, bf16[576,4096]{1,0:T(8,128)(2,1)} %bitcast.11), custom_call_target="tpu_custom_call" | custom-call | tf_op jit(solution)/shard_map/prefix_attention/pallas_call | solution.py:136
  24.0 0.7 %collective-permute-done.3.refs_2_.refs_10_ = bf16[288,512]{1,0:T(8,128)(2,1)S(1)} collective-permute-done((bf16[288,512]{1,0:T(8,128)(2,1)S(1)}, bf16[288,512]{1,0:T(8,128)(2,1)S(1)}, u32[]{:S(2)}, u32[]{:S(2)}) %collective-permute-start.3) | collective-permute-done | bytes 294944 | tf_op jit(solution)/shard_map/ppermute | solution.py:402
  24.7 1.5 %select.1 = bf16[288,512]{1,0:T(8,128)(2,1)S(1)} custom-call(s32[4]{0:T(128)S(1)} %fusion.1.theirs, s32[2]{0:T(128)S(1)} %pad_add_fusion.place.refs_2_, bf16[288,512]{1,0:T(8,128)(2,1)S(1)} %get-tuple-element.27.refs_0_.refs_8_, bf16[304,512]{1,0:T(8,128)(2,1)S(1)} %collective-permute-done.2.refs_1_.refs_9_, ...), custom_call_target="tpu_custom_call" | custom-call | tf_op jit(solution)/shard_map/select/pallas_call | solution.py:428
  26.2 1.4 %collective-permute-start.6 = (bf16[288,512]{1,0:T(8,128)(2,1)S(1)}, bf16[288,512]{1,0:T(8,128)(2,1)S(1)}, u32[]{:S(2)}, u32[]{:S(2)}) collective-permute-start(bf16[288,512]{1,0:T(8,128)(2,1)S(1)} %select.1), channel_id=1, source_target_pairs={{1,0},{2,3},{5,4},{6,7},{9,8},{10,11},{13,12},{14,15},{17,16},{18,... | collective-permute-start | bytes 884744 | tf_op jit(solution)/shard_map/ppermute | solution.py:440
  27.7 5.0 %prefix_attention.2 = (f32[256,512]{1,0:T(8,128)S(1)}, f32[256,128]{1,0:T(8,128)S(1)}, f32[256,128]{1,0:T(8,128)S(1)}) custom-call(bf16[128,576]{1,0:T(8,128)(2,1)S(1)} %collective-permute-done.refs_0_.refs_3_, bf16[128,576]{1,0:T(8,128)(2,1)S(1)} %collective-permute-done.1.refs_1_.refs_4_, bf16[576,4096]{1,0:T(8,128)(2,1)} %bitcast.12), custom_call_target="tpu_custom_call" | custom-call | flops 2281701376 | bytes 4718592 | tf_op jit(solution)/shard_map/prefix_attention/pallas_call | solution.py:136
  32.7 4.8 %collective-permute-done.6.refs_12_ = bf16[288,512]{1,0:T(8,128)(2,1)S(1)} collective-permute-done((bf16[288,512]{1,0:T(8,128)(2,1)S(1)}, bf16[288,512]{1,0:T(8,128)(2,1)S(1)}, u32[]{:S(2)}, u32[]{:S(2)}) %collective-permute-start.6) | collective-permute-done | bytes 294944 | tf_op jit(solution)/shard_map/ppermute | solution.py:440
  37.5 1.9 %suffix_far.1 = (bf16[256,576]{1,0:T(8,128)(2,1)S(1)}, bf16[128,640]{1,0:T(8,128)(2,1)S(1)}, bf16[128,640]{1,0:T(8,128)(2,1)S(1)}) custom-call(s32[4]{0:T(128)S(1)} %copy-done.4, s32[16]{0:T(128)S(1)} %copy-done.5, s32[2]{0:T(128)S(1)} %pad_add_fusion.place.refs_2_, bf16[128,576]{1,0:T(8,128)(2,1)S(1)} %collective-permute-done.refs_0_.refs_3_, ...), custom_call_target="tpu_custom_call" | custom-call | tf_op jit(solution)/shard_map/suffix_far/pallas_call | solution.py:444
  39.5 0.5 %collective-permute-start.10 = (bf16[256,576]{1,0:T(8,128)(2,1)S(1)}, bf16[256,576]{1,0:T(8,128)(2,1)S(1)}, u32[]{:S(2)}, u32[]{:S(2)}) collective-permute-start(bf16[256,576]{1,0:T(8,128)(2,1)S(1)} %get-tuple-element.37.refs_5_), channel_id=1, source_target_pairs={{0,4},{4,0},{8,12},{12,8},{1,5},{5,1},{9,13},{13,9},{2,6},{6,2},{1... | collective-permute-start | bytes 884744 | tf_op jit(solution)/shard_map/ppermute | solution.py:460
  40.1 0.8 %collective-permute-done.7.refs_1_ = bf16[128,640]{1,0:T(8,128)(2,1)S(1)} collective-permute-done((bf16[128,640]{1,0:T(8,128)(2,1)S(1)}, bf16[128,640]{1,0:T(8,128)(2,1)S(1)}, u32[]{:S(2)}, u32[]{:S(2)}) %collective-permute-start.7) | collective-permute-done | bytes 163872 | tf_op jit(solution)/shard_map/ppermute | solution.py:458
  41.1 0.6 %collective-permute-start.8 = (bf16[128,640]{1,0:T(8,128)(2,1)S(1)}, bf16[128,640]{1,0:T(8,128)(2,1)S(1)}, u32[]{:S(2)}, u32[]{:S(2)}) collective-permute-start(bf16[128,640]{1,0:T(8,128)(2,1)S(1)} %chip_merge.1), channel_id=1, source_target_pairs={{8,0},{12,4},{0,8},{4,12},{9,1},{13,5},{1,9},{5,13},{10,2},{14,6},... | collective-permute-start | bytes 491528 | tf_op jit(solution)/shard_map/ppermute | solution.py:459
  41.7 1.6 %suffix_near.1 = (bf16[4,64,576]{2,1,0:T(8,128)(2,1)}, bf16[128,640]{1,0:T(8,128)(2,1)S(1)}) custom-call(s32[4]{0:T(128)S(1)} %copy-done.4, s32[16]{0:T(128)S(1)} %copy-done.5, s32[2]{0:T(128)S(1)} %pad_add_fusion.place.refs_2_, bf16[4,576]{1,0:T(4,128)(2,1)S(1)} %copy-done.2, bf16[128,576]{1,0:T(8,128)(2,1)S(1)} %project.1.refs_0_, ...), custom_call_target="tpu_custom_call" | custom-call | tf_op jit(solution)/shard_map/suffix_near/pallas_call | solution.py:464
  43.3 4.1 %collective-permute-done.8.refs_0_ = bf16[128,640]{1,0:T(8,128)(2,1)S(1)} collective-permute-done((bf16[128,640]{1,0:T(8,128)(2,1)S(1)}, bf16[128,640]{1,0:T(8,128)(2,1)S(1)}, u32[]{:S(2)}, u32[]{:S(2)}) %collective-permute-start.8) | collective-permute-done | bytes 163872 | tf_op jit(solution)/shard_map/ppermute | solution.py:459
  47.4 1.4 %final.1 = bf16[4,32,128]{2,1,0:T(8,128)(2,1)} custom-call(bf16[128,640]{1,0:T(8,128)(2,1)S(1)} %collective-permute-done.8.refs_0_, bf16[128,640]{1,0:T(8,128)(2,1)S(1)} %get-tuple-element.38.refs_1_, bf16[32,512,128]{2,1,0:T(8,128)(2,1)S(1)} %copy-done), custom_call_target="tpu_custom_call" | custom-call | tf_op jit(solution)/shard_map/final/pallas_call | solution.py:474
  (23 shorter events, 0.5 us)
Async XLA Ops:
  0.6 1.0 %copy-start.1 = (bf16[4,64,576]{2,1,0:T(8,128)(2,1)S(1)}, bf16[4,64,576]{2,1,0:T(8,128)(2,1)}, u32[]{:S(2)}) copy-start(bf16[4,64,576]{2,1,0:T(8,128)(2,1)} %cache_ref.1) | copy-start | bytes 884740
  1.6 0.7 %copy-start.3 = (s32[4]{0:T(128)S(1)}, s32[4]{0:T(128)}, u32[]{:S(2)}) copy-start(s32[4]{0:T(128)} %anc.3) | copy-start | bytes 52
  2.9 21.1 %collective-permute-start.2 = (bf16[304,512]{1,0:T(8,128)(2,1)S(1)}, bf16[304,512]{1,0:T(8,128)(2,1)S(1)}, u32[]{:S(2)}, u32[]{:S(2)}) collective-permute-start(bf16[304,512]{1,0:T(8,128)(2,1)S(1)} %get-tuple-element.26), channel_id=1, source_target_pairs={{0,1},{3,2},{4,5},{7,6},{8,9},{11,10},{12,13},{15,14},{16,17},{19,... | collective-permute-start | bytes 933896 | tf_op jit(solution)/shard_map/ppermute | solution.py:382
  7.8 11.0 %collective-permute-start.4 = (bf16[288,512]{1,0:T(8,128)(2,1)S(1)}, bf16[288,512]{1,0:T(8,128)(2,1)S(1)}, u32[]{:S(2)}, u32[]{:S(2)}) collective-permute-start(bf16[288,512]{1,0:T(8,128)(2,1)S(1)} %get-tuple-element.27.refs_0_.refs_8_), channel_id=1, source_target_pairs={{1,2},{2,1},{5,6},{6,5},{9,10},{10,9},{13,14},{14,13},{17,18},{18,... | collective-permute-start | bytes 884744 | tf_op jit(solution)/shard_map/ppermute | solution.py:381
  12.5 5.7 %collective-permute-start.5 = (bf16[128,576]{1,0:T(8,128)(2,1)S(1)}, bf16[128,576]{1,0:T(8,128)(2,1)S(1)}, u32[]{:S(2)}, u32[]{:S(2)}) collective-permute-start(bf16[128,576]{1,0:T(8,128)(2,1)S(1)} %project.1.refs_0_), channel_id=1, source_target_pairs={{0,4},{4,0},{8,12},{12,8},{1,5},{5,1},{9,13},{13,9},{2,6},{6,2},{1... | collective-permute-start | bytes 442376 | tf_op jit(solution)/shard_map/ppermute | solution.py:415
  12.6 15.0 %collective-permute-start.1 = (bf16[128,576]{1,0:T(8,128)(2,1)S(1)}, bf16[128,576]{1,0:T(8,128)(2,1)S(1)}, u32[]{:S(2)}, u32[]{:S(2)}) collective-permute-start(bf16[128,576]{1,0:T(8,128)(2,1)S(1)} %project.1.refs_0_), channel_id=1, source_target_pairs={{0,12},{4,8},{8,4},{12,0},{1,13},{5,9},{9,5},{13,1},{2,14},{6,10},... | collective-permute-start | bytes 442376 | tf_op jit(solution)/shard_map/ppermute | solution.py:415
  14.2 10.4 %collective-permute-start.3 = (bf16[288,512]{1,0:T(8,128)(2,1)S(1)}, bf16[288,512]{1,0:T(8,128)(2,1)S(1)}, u32[]{:S(2)}, u32[]{:S(2)}) collective-permute-start(bf16[288,512]{1,0:T(8,128)(2,1)S(1)} %get-tuple-element.27.refs_0_.refs_8_), channel_id=1, source_target_pairs={{0,2},{3,1},{4,6},{7,5},{8,10},{11,9},{12,14},{15,13},{16,18},{19,... | collective-permute-start | bytes 884744 | tf_op jit(solution)/shard_map/ppermute | solution.py:402
  18.3 9.4 %collective-permute-start = (bf16[128,576]{1,0:T(8,128)(2,1)S(1)}, bf16[128,576]{1,0:T(8,128)(2,1)S(1)}, u32[]{:S(2)}, u32[]{:S(2)}) collective-permute-start(bf16[128,576]{1,0:T(8,128)(2,1)S(1)} %project.1.refs_0_), channel_id=1, source_target_pairs={{0,8},{4,12},{8,0},{12,4},{1,9},{5,13},{9,1},{13,5},{2,10},{6,14},... | collective-permute-start | bytes 442376 | tf_op jit(solution)/shard_map/ppermute | solution.py:415
  26.2 11.3 %copy-start.4 = (s32[4]{0:T(128)S(1)}, s32[4]{0:T(128)}, u32[]{:S(2)}) copy-start(s32[4]{0:T(128)} %anc.3) | copy-start | bytes 52
  26.2 11.3 %copy-start.5 = (s32[16]{0:T(128)S(1)}, s32[16]{0:T(128)}, u32[]{:S(2)}) copy-start(s32[16]{0:T(128)} %lens.1) | copy-start | bytes 196
  26.2 15.5 %copy-start.2 = (bf16[4,576]{1,0:T(4,128)(2,1)S(1)}, bf16[4,576]{1,0:T(4,128)(2,1)}, u32[]{:S(2)}) copy-start(bf16[4,576]{1,0:T(4,128)(2,1)} %fresh_ref.1) | copy-start | bytes 13828
  26.2 11.3 %collective-permute-start.6 = (bf16[288,512]{1,0:T(8,128)(2,1)S(1)}, bf16[288,512]{1,0:T(8,128)(2,1)S(1)}, u32[]{:S(2)}, u32[]{:S(2)}) collective-permute-start(bf16[288,512]{1,0:T(8,128)(2,1)S(1)} %select.1), channel_id=1, source_target_pairs={{1,0},{2,3},{5,4},{6,7},{9,8},{10,11},{13,12},{14,15},{17,16},{18,... | collective-permute-start | bytes 884744 | tf_op jit(solution)/shard_map/ppermute | solution.py:440
  32.7 14.7 %copy-start = (bf16[32,512,128]{2,1,0:T(8,128)(2,1)S(1)}, bf16[32,512,128]{2,1,0:T(8,128)(2,1)}, u32[]{:S(2)}) copy-start(bf16[32,512,128]{2,1,0:T(8,128)(2,1)} %refs_2_.1) | copy-start | bytes 12582916
  39.5 1.5 %collective-permute-start.7 = (bf16[128,640]{1,0:T(8,128)(2,1)S(1)}, bf16[128,640]{1,0:T(8,128)(2,1)S(1)}, u32[]{:S(2)}, u32[]{:S(2)}) collective-permute-start(bf16[128,640]{1,0:T(8,128)(2,1)S(1)} %get-tuple-element.32), channel_id=1, source_target_pairs={{0,4},{4,0},{8,12},{12,8},{1,5},{5,1},{9,13},{13,9},{2,6},{6,2},{1... | collective-permute-start | bytes 491528 | tf_op jit(solution)/shard_map/ppermute | solution.py:458
  39.5 2.2 %collective-permute-start.10 = (bf16[256,576]{1,0:T(8,128)(2,1)S(1)}, bf16[256,576]{1,0:T(8,128)(2,1)S(1)}, u32[]{:S(2)}, u32[]{:S(2)}) collective-permute-start(bf16[256,576]{1,0:T(8,128)(2,1)S(1)} %get-tuple-element.37.refs_5_), channel_id=1, source_target_pairs={{0,4},{4,0},{8,12},{12,8},{1,5},{5,1},{9,13},{13,9},{2,6},{6,2},{1... | collective-permute-start | bytes 884744 | tf_op jit(solution)/shard_map/ppermute | solution.py:460
  40.0 1.7 %collective-permute-start.9 = (bf16[128,640]{1,0:T(8,128)(2,1)S(1)}, bf16[128,640]{1,0:T(8,128)(2,1)S(1)}, u32[]{:S(2)}, u32[]{:S(2)}) collective-permute-start(bf16[128,640]{1,0:T(8,128)(2,1)S(1)} %get-tuple-element.35), channel_id=1, source_target_pairs={{0,4},{4,0},{8,12},{12,8},{1,5},{5,1},{9,13},{13,9},{2,6},{6,2},{1... | collective-permute-start | bytes 491528 | tf_op jit(solution)/shard_map/ppermute | solution.py:424
  41.1 6.3 %collective-permute-start.8 = (bf16[128,640]{1,0:T(8,128)(2,1)S(1)}, bf16[128,640]{1,0:T(8,128)(2,1)S(1)}, u32[]{:S(2)}, u32[]{:S(2)}) collective-permute-start(bf16[128,640]{1,0:T(8,128)(2,1)S(1)} %chip_merge.1), channel_id=1, source_target_pairs={{8,0},{12,4},{0,8},{4,12},{9,1},{13,5},{1,9},{5,13},{10,2},{14,6},... | collective-permute-start | bytes 491528 | tf_op jit(solution)/shard_map/ppermute | solution.py:459

commit v8 on v6

--- a/solution.py
+++ b/solution.py
@@ -30,14 +30,14 @@
 
 
 def pack_kernel(rank, cache_ref, out_ref):
-    local, span, width = cache_ref.shape
-    for p in range(local):
-        out_ref[pl.ds(p * span, span)] = cache_ref[p, :, :rank]
-    rope = jnp.concatenate([cache_ref[p, :, rank:] for p in range(local)], axis=1)
-    tail = out_ref.shape[0] - local * span
-    out_ref[pl.ds(local * span, tail)] = jnp.concatenate(
-        [rope[i : i + tail] for i in range(0, span, tail)], axis=1
-    )
+    local, span, _ = cache_ref.shape
+    some = span // 2
+    for p in range(local):
+        part = pl.ds(p * some, some)
+        first, second = cache_ref[p, :some], cache_ref[p, some:]
+        out_ref[part, :rank] = first[:, :rank]
+        out_ref[part, rank : 2 * rank] = second[:, :rank]
+        out_ref[part, 2 * rank :] = jnp.concatenate([first[:, rank:], second[:, rank:]], axis=1)
 
 
 def project_kernel(
@@ -199,6 +199,42 @@
     return packed(acc * (1.0 / total), top + jnp.log2(total))
 
 
+def gather_blocks(block_refs, picks, out_ref, sems):
+    some = out_ref.shape[0] // len(picks)
+
+    def copy(p, k, slot):
+        return pltpu.make_async_copy(
+            block_refs[k].at[pl.ds(pl.multiple_of(slot * some, some), some)],
+            out_ref.at[pl.ds(p * some, some)],
+            sems.at[p],
+        )
+
+    for p, (which, slot) in enumerate(picks):
+        for k in range(len(block_refs)):
+
+            @pl.when(which == k)
+            def _():
+                copy(p, k, slot).start()
+
+    for p in range(len(picks)):
+        copy(p, 0, 0).wait()
+
+
+def at_end(place):
+    return (place[1] == 0) | (place[1] == 3)
+
+
+def select_kernel(theirs, place, *refs):
+    block_refs, (_, out_ref, sems) = refs[:-3], refs[-3:]
+    local = sems.shape[0]
+    picks = []
+    for p in range(local):
+        apart = jnp.bitwise_xor(lax.div(theirs[p], local), place[1])
+        which = jnp.where(at_end(place), 0, jnp.maximum(apart - 1, 0))
+        picks.append((which, jnp.where(at_end(place), p, lax.rem(theirs[p], local))))
+    gather_blocks(block_refs, picks, out_ref, sems)
+
+
 def far_kernel(stages, sources, line, *refs):
     anc, lens, place = refs[:3]
     refs = refs[3:]
@@ -206,51 +242,30 @@
     block_refs, refs = refs[:sources], refs[sources:]
     moved_ref, refs = refs[0], refs[1:]
     keep_refs, give_refs = refs[:stages], refs[stages : 2 * stages]
-    folded, sems = refs[2 * stages :]
-    local, tail, rank = folded.shape
-    span = moved_ref.shape[0] // local
-    rope = moved_ref.shape[1] - rank
-
-    def copies(p, k, slot):
-        at = pl.multiple_of(slot * span, span)
-        there = moved_ref.at[pl.ds(p * span, span), pl.ds(0, rank)]
-        return (
-            pltpu.make_async_copy(block_refs[k].at[pl.ds(at, span)], there, sems.at[2 * p]),
-            pltpu.make_async_copy(
-                block_refs[k].at[pl.ds(local * span, tail)], folded.at[p], sems.at[2 * p + 1]
-            ),
-        )
-
-    slots = []
-    for p in range(local):
-        owner = lax.div(anc[p], local)
-        slots.append(lax.rem(anc[p], local))
+    raw, sems = refs[2 * stages :]
+    local = sems.shape[0]
+    some = raw.shape[0] // local
+    span, width = 2 * some, moved_ref.shape[1]
+    rank = stage_refs[2].shape[1]
+
+    picks = []
+    for p in range(local):
+        owner, slot = lax.div(anc[p], local), lax.rem(anc[p], local)
         if line:
-            apart = jnp.bitwise_xor(owner, place[1])
-            at_end = (place[1] == 0) | (place[1] == 3)
-            which = jnp.where(at_end & (apart > 1), apart + 2, apart)
+            which = jnp.bitwise_xor(owner, place[1])
+            chosen = at_end(place) & (which != 0)
+            which = jnp.where(chosen, 1, which)
+            slot = jnp.where(chosen, p, slot)
         else:
             which = lax.rem(place[1] - owner + sources, sources)
-        for k in range(sources):
-
-            @pl.when(which == k)
-            def _():
-                for copy in copies(p, k, slots[p]):
-                    copy.start()
-
-    for p in range(local):
-        for copy in copies(p, 0, 0):
-            copy.wait()
-
-    for p in range(local):
-        for i in range(span // tail):
-            choices = [
-                folded[p, :, (i * local + q) * rope : (i * local + q + 1) * rope] for q in range(local)
-            ]
-            picked = choices[0]
-            for q in range(1, local):
-                picked = jnp.where(slots[p] == q, choices[q], picked)
-            moved_ref[pl.ds(p * span + i * tail, tail), rank:] = picked
+        picks.append((which, slot))
+    gather_blocks(block_refs, picks, raw, sems)
+    for p in range(local):
+        for h in range(2):
+            part, rows = pl.ds(p * some, some), pl.ds(p * span + h * some, some)
+            rope = 2 * rank + h * (width - rank)
+            moved_ref[rows, :rank] = raw[part, h * rank : (h + 1) * rank]
+            moved_ref[rows, rank:] = raw[part, rope : rope + width - rank]
 
     ends = [lens[anc[p]] for p in range(local)]
     for k in range(stages):
@@ -320,17 +335,14 @@
     local, heads, nope = q_nope.shape
     span, width = private_caches.shape[1:]
     rank, reach = w_uv.shape[1:]
-    rope = width - rank
     rows = local * heads
     seq_size, dom_size = lax.axis_size("seq"), lax.axis_size("dom")
     cores = 2
     chips = seq_size // cores
     place = jnp.stack([lax.axis_index("seq"), lax.axis_index("dom")]).astype(jnp.int32)
-    tail = span * local * rope // rank
-
     block = pl.pallas_call(
         functools.partial(pack_kernel, rank),
-        out_shape=shape((local * span + tail, rank)),
+        out_shape=shape((local * span // 2, 2 * width)),
         in_specs=[VMEM],
         out_specs=VMEM,
         compiler_params=PARAMS,
@@ -339,14 +351,17 @@
     nope_rows, rope_rows = (jnp.swapaxes(q, 0, 1).reshape(rows, -1) for q in (q_nope, q_rope))
     line = dom_size == 4
     if line:
-        near = lax.ppermute(block, "dom", [(0, 1), (1, 0), (2, 3), (3, 2)])
         far = lax.ppermute(block, "dom", [(1, 2), (2, 1)])
+        swap = [(0, 1), (1, 0), (2, 3), (3, 2)]
+        theirs = lax.ppermute(ancestors, "dom", swap)
     else:
         blocks = [block] + [
             lax.ppermute(block, "dom", [(i, (i + k) % dom_size) for i in range(dom_size)])
             for k in range(1, dom_size)
         ]
 
+    if line:
+        theirs, nope_rows = lax.optimization_barrier((theirs, nope_rows))
     pieces = math.gcd(heads // 4, 4)
     own = pl.pallas_call(
         functools.partial(project_kernel, pieces, local),
@@ -360,7 +375,7 @@
     keys = prefix.T
     if line:
         sent, own = lax.optimization_barrier((block, own))
-        inner_middle = lax.ppermute(sent, "dom", [(0, 2), (3, 1)])
+        middle = lax.ppermute(sent, "dom", [(0, 2), (3, 1)])
 
     def pairs(turn, flip):
         return [
@@ -375,8 +390,7 @@
     routes = [(t, f) for t in range(chips) for f in range(cores)]
     queries = [own if r == (0, 0) else lax.ppermute(own, "seq", pairs(*r)) for r in routes]
     if line:
-        near, far, queries[1] = lax.optimization_barrier((near, far, queries[1]))
-        outer_middle = lax.ppermute(far, "dom", [(1, 0), (2, 3)])
+        far, queries[1] = lax.optimization_barrier((far, queries[1]))
     stages = []
     for t in range(chips):
         asked = queries[2 * t : 2 * t + 2]
@@ -385,10 +399,17 @@
         if t == 0:
             given = lax.ppermute(stage.pop(), "seq", pairs(0, 1))
         if line and t == 0:
-            inner_middle, stage[3] = lax.optimization_barrier((inner_middle, stage[3]))
-            outer_far = lax.ppermute(inner_middle, "dom", [(1, 0), (2, 3)])
-    if line:
-        blocks = [block, near, inner_middle, far, outer_middle, outer_far]
+            chosen = pl.pallas_call(
+                select_kernel,
+                out_shape=shape(block.shape),
+                in_specs=[SMEM] * 2 + [ANY] * 4,
+                out_specs=VMEM,
+                scratch_shapes=[pltpu.SemaphoreType.DMA((local,))],
+                compiler_params=PARAMS,
+                cost_estimate=pl.CostEstimate(flops=0, bytes_accessed=0, transcendentals=0),
+                name="select",
+            )(theirs, place, block, middle, far, stage[3])
+            blocks = [block, lax.ppermute(chosen, "dom", swap), middle, far]
 
     part = shape((rows, rank + LANES))
     others = chips - 1
@@ -398,8 +419,8 @@
         in_specs=[SMEM] * 3 + [VMEM] * (5 * others) + [ANY] * len(blocks),
         out_specs=[VMEM] * (1 + 2 * others),
         scratch_shapes=[
-            pltpu.VMEM((local, tail, rank), BF16),
-            pltpu.SemaphoreType.DMA((2 * local,)),
+            pltpu.VMEM(block.shape, BF16),
+            pltpu.SemaphoreType.DMA((local,)),
         ],
         compiler_params=PARAMS,
         name="suffix_far",

time: 45.8 us -> 44 us (0.961)
  waiting for transfers between devices: 9 us -> 5.28 us
  Pallas kernels: 17.8 us -> 18.8 us
  starting transfers between devices: 15.3 us -> 16.2 us
    ppermute x4 -> x3, waiting for transfers between devices: 4.21 us -> 1.3 us  [the longest x1 1.29 us: on_device(): blocks = [block, lax.ppermute(chosen, 'dom', swap), middle, far]]
    pallas_call x0 -> x1, Pallas kernels: none -> 1.04 us  [on_device(): pl.pallas_call(select_kernel, out_shape=shape(block.shape), in_specs=[SME...]
    ppermute x1, waiting for transfers between devices: 3.97 us -> 3.16 us  [on_device(): parts = [lax.ppermute(s, 'seq', back(t, 0)) for t, s in enumerate(sums, 1)]]
    ppermute x1, starting transfers between devices: 0.75 us -> 1.55 us  [on_device(): parts = [lax.ppermute(s, 'seq', back(t, 0)) for t, s in enumerate(sums, 1)]]
    ppermute x4 -> x3, starting transfers between devices: 10.3 us -> 11.1 us  [the longest x1 5.75 us: on_device(): middle = lax.ppermute(sent, 'dom', [(0, 2), (3, 1)])]
    ppermute x3, starting transfers between devices: 2.94 us -> 2.21 us  [on_device(): lax.ppermute(own, 'seq', pairs(*r))]
  transfers between devices with their start and end apart: 12 -> 11, of which waited for: 3 -> 3; matrix products, arithmetic and copies ran while one was open for 4% -> 4% of each run, Pallas kernels for 32% -> 36%
where the time goes in v8:
time: 44 us; the launch traced here: 43.7 us
  Pallas kernels  18.8 us (43%)
  starting transfers between devices  16.2 us (37%)
  waiting for transfers between devices  5.28 us (12%)
  local copies, waits for them, and re-layouts  2.55 us (6%)
  between operations  0.77 us (2%)
    pallas_call x2, Pallas kernels, prefix_attention(): pl.pallas_call(functools.partial(prefix_kernel, len(queries), tiles), out...  10.3 us
    ppermute x1, starting transfers between devices, on_device(): middle = lax.ppermute(sent, 'dom', [(0, 2), (3, 1)])  5.75 us
    ppermute x1, waiting for transfers between devices, on_device(): parts = [lax.ppermute(s, 'seq', back(t, 0)) for t, s in enumerate(sums, 1)]  3.16 us
    ppermute x1, starting transfers between devices, on_device(): theirs = lax.ppermute(ancestors, 'dom', swap)  3.09 us
    pallas_call x1, Pallas kernels, on_device(): pl.pallas_call(functools.partial(project_kernel, pieces, local), out_shap...  2.46 us
    ppermute x1, starting transfers between devices, on_device(): blocks = [block, lax.ppermute(chosen, 'dom', swap), middle, far]  2.24 us
    ppermute x3, starting transfers between devices, on_device(): lax.ppermute(own, 'seq', pairs(*r))  2.21 us
    pallas_call x1, Pallas kernels, on_device(): pl.pallas_call(functools.partial(far_kernel, others, len(blocks), line),...  1.83 us
  transfers between devices with their start and end apart: 11, of which 3 were waited for; matrix products, arithmetic and copies ran while one was open for 4% of the time, Pallas kernels for 36%

profile of v8, /device:TPU:0, one launch (start us, length us, event | category | flops | bytes accessed | tf_op | source)
XLA Modules:
  0.0 43.7 jit_solution(12859349891248512676)
XLA Ops:
  0.6 3.1 %collective-permute-start = (s32[4]{0:T(128)}, s32[4]{0:T(128)S(1)}, u32[]{:S(2)}, u32[]{:S(2)}) collective-permute-start(s32[4]{0:T(128)} %anc.1), channel_id=1, source_target_pairs={{0,1},{1,0},{2,3},{3,2},{4,5},{5,4},{6,7},{7,6},{8,9},{9,8},{10,11... | collective-permute-start | bytes 56 | tf_op jit(solution)/shard_map/ppermute | solution.py:356
  3.7 1.0 %copy-done.1 = bf16[4,64,576]{2,1,0:T(8,128)(2,1)S(1)} copy-done((bf16[4,64,576]{2,1,0:T(8,128)(2,1)S(1)}, bf16[4,64,576]{2,1,0:T(8,128)(2,1)}, u32[]{:S(2)}) %copy-start.1) | copy-done | bytes 294936
  4.7 0.1 pack.1.refs_0_.refs_8_
  4.8 0.7 %collective-permute-start.4 = (bf16[128,1152]{1,0:T(8,128)(2,1)S(1)}, bf16[128,1152]{1,0:T(8,128)(2,1)S(1)}, u32[]{:S(2)}, u32[]{:S(2)}) collective-permute-start(bf16[128,1152]{1,0:T(8,128)(2,1)S(1)} %pack.1.refs_0_.refs_8_), channel_id=1, source_target_pairs={{1,2},{2,1},{5,6},{6,5},{9,10},{10,9},{13,14},{14,13},{17,18},{18,... | collective-permute-start | bytes 884744 | tf_op jit(solution)/shard_map/ppermute | solution.py:354
  5.5 0.8 %copy.11 = bf16[32,4,128]{2,1,0:T(4,128)(2,1)S(1)} copy(bf16[32,4,128]{2,0,1:T(8,128)(2,1)} %bitcast.11) | data formatting | bytes 65536 | tf_op jit(solution)/shard_map/transpose | solution.py:351
  6.2 0.8 %copy.12 = bf16[32,4,64]{2,1,0:T(4,128)(2,1)S(1)} copy(bf16[32,4,64]{2,0,1:T(8,128)(2,1)} %bitcast.12) | data formatting | bytes 32768 | tf_op jit(solution)/shard_map/transpose | solution.py:351
  7.0 2.5 %project.1.refs_0_ = bf16[128,576]{1,0:T(8,128)(2,1)S(1)} custom-call(bf16[128,128]{1,0:T(8,128)(2,1)S(1)} %bitcast.7, bf16[128,64]{1,0:T(8,128)(2,1)S(1)} %bitcast.8, bf16[32,128,512]{2,1,0:T(8,128)(2,1)} %w_hbm.1), custom_call_target="tpu_custom_call" | custom-call | tf_op jit(solution)/shard_map/project/pallas_call | solution.py:366
  9.5 5.8 %collective-permute-start.3 = (bf16[128,1152]{1,0:T(8,128)(2,1)S(1)}, bf16[128,1152]{1,0:T(8,128)(2,1)S(1)}, u32[]{:S(2)}, u32[]{:S(2)}) collective-permute-start(bf16[128,1152]{1,0:T(8,128)(2,1)S(1)} %pack.1.refs_0_.refs_8_), channel_id=1, source_target_pairs={{0,2},{3,1},{4,6},{7,5},{8,10},{11,9},{12,14},{15,13},{16,18},{19,... | collective-permute-start | bytes 884744 | tf_op jit(solution)/shard_map/ppermute | solution.py:378
  15.3 1.6 %collective-permute-start.2 = (bf16[128,576]{1,0:T(8,128)(2,1)S(1)}, bf16[128,576]{1,0:T(8,128)(2,1)S(1)}, u32[]{:S(2)}, u32[]{:S(2)}) collective-permute-start(bf16[128,576]{1,0:T(8,128)(2,1)S(1)} %project.1.refs_0_), channel_id=1, source_target_pairs={{0,12},{4,8},{8,4},{12,0},{1,13},{5,9},{9,5},{13,1},{2,14},{6,10},... | collective-permute-start | bytes 442376 | tf_op jit(solution)/shard_map/ppermute | solution.py:391
  16.9 0.5 %collective-permute-start.1 = (bf16[128,576]{1,0:T(8,128)(2,1)S(1)}, bf16[128,576]{1,0:T(8,128)(2,1)S(1)}, u32[]{:S(2)}, u32[]{:S(2)}) collective-permute-start(bf16[128,576]{1,0:T(8,128)(2,1)S(1)} %project.1.refs_0_), channel_id=1, source_target_pairs={{0,8},{4,12},{8,0},{12,4},{1,9},{5,13},{9,1},{13,5},{2,10},{6,14},... | collective-permute-start | bytes 442376 | tf_op jit(solution)/shard_map/ppermute | solution.py:391
  17.6 5.1 %prefix_attention.3 = (f32[128,512]{1,0:T(8,128)S(1)}, f32[128,128]{1,0:T(8,128)S(1)}, f32[128,128]{1,0:T(8,128)S(1)}, bf16[128,640]{1,0:T(8,128)(2,1)S(1)}) custom-call(bf16[128,576]{1,0:T(8,128)(2,1)S(1)} %project.1.refs_0_, bf16[128,576]{1,0:T(8,128)(2,1)S(1)} %collective-permute-done.5.refs_1_, bf16[576,4096]{1,0:T(8,128)(2,1)} %bitcast.9), custom_call_target="tpu_custom_call" | custom-call | tf_op jit(solution)/shard_map/prefix_attention/pallas_call | solution.py:129
  22.7 1.0 %select.1 = bf16[128,1152]{1,0:T(8,128)(2,1)S(1)} custom-call(s32[4]{0:T(128)S(1)} %collective-permute-done.theirs, s32[2]{0:T(128)S(1)} %pad_add_fusion.place.refs_2_, bf16[128,1152]{1,0:T(8,128)(2,1)S(1)} %pack.1.refs_0_.refs_8_, bf16[128,1152]{1,0:T(8,128)(2,1)S(1)} %collective-permute-done.3.refs_1_.refs_10_, ...), custom_call_target="tpu_custom_call" | custom-call | tf_op jit(solution)/shard_map/select/pallas_call | solution.py:402
  23.8 2.2 %collective-permute-start.6 = (bf16[128,1152]{1,0:T(8,128)(2,1)S(1)}, bf16[128,1152]{1,0:T(8,128)(2,1)S(1)}, u32[]{:S(2)}, u32[]{:S(2)}) collective-permute-start(bf16[128,1152]{1,0:T(8,128)(2,1)S(1)} %select.1), channel_id=1, source_target_pairs={{0,1},{1,0},{2,3},{3,2},{4,5},{5,4},{6,7},{7,6},{8,9},{9,8},{10,11... | collective-permute-start | bytes 884744 | tf_op jit(solution)/shard_map/ppermute | solution.py:412
  26.0 5.2 %prefix_attention.2 = (f32[256,512]{1,0:T(8,128)S(1)}, f32[256,128]{1,0:T(8,128)S(1)}, f32[256,128]{1,0:T(8,128)S(1)}) custom-call(bf16[128,576]{1,0:T(8,128)(2,1)S(1)} %collective-permute-done.1.refs_0_.refs_3_, bf16[128,576]{1,0:T(8,128)(2,1)S(1)} %collective-permute-done.2.refs_1_.refs_4_, bf16[576,4096]{1,0:T(8,128)(2,1)} %bitcast.10), custom_call_target="tpu_custom_call" | custom-call | flops 2281701376 | bytes 4718592 | tf_op jit(solution)/shard_map/prefix_attention/pallas_call | solution.py:129
  31.2 1.3 %collective-permute-done.6.refs_9_ = bf16[128,1152]{1,0:T(8,128)(2,1)S(1)} collective-permute-done((bf16[128,1152]{1,0:T(8,128)(2,1)S(1)}, bf16[128,1152]{1,0:T(8,128)(2,1)S(1)}, u32[]{:S(2)}, u32[]{:S(2)}) %collective-permute-start.6) | collective-permute-done | bytes 294944 | tf_op jit(solution)/shard_map/ppermute | solution.py:412
  32.5 1.8 %suffix_far.1 = (bf16[256,576]{1,0:T(8,128)(2,1)S(1)}, bf16[128,640]{1,0:T(8,128)(2,1)S(1)}, bf16[128,640]{1,0:T(8,128)(2,1)S(1)}) custom-call(s32[4]{0:T(128)S(1)} %copy-done.3, s32[16]{0:T(128)S(1)} %copy-done.4, s32[2]{0:T(128)S(1)} %pad_add_fusion.place.refs_2_, bf16[128,576]{1,0:T(8,128)(2,1)S(1)} %collective-permute-done.1.refs_0_.refs_3_, ...), custom_call_target="tpu_custom_call" | custom-call | tf_op jit(solution)/shard_map/suffix_far/pallas_call | solution.py:416
  34.4 0.5 %collective-permute-start.10 = (bf16[256,576]{1,0:T(8,128)(2,1)S(1)}, bf16[256,576]{1,0:T(8,128)(2,1)S(1)}, u32[]{:S(2)}, u32[]{:S(2)}) collective-permute-start(bf16[256,576]{1,0:T(8,128)(2,1)S(1)} %get-tuple-element.37.refs_5_), channel_id=1, source_target_pairs={{0,4},{4,0},{8,12},{12,8},{1,5},{5,1},{9,13},{13,9},{2,6},{6,2},{1... | collective-permute-start | bytes 884744 | tf_op jit(solution)/shard_map/ppermute | solution.py:432
  34.9 0.1 collective-permute-start.9
  35.0 0.8 %collective-permute-done.7.refs_1_ = bf16[128,640]{1,0:T(8,128)(2,1)S(1)} collective-permute-done((bf16[128,640]{1,0:T(8,128)(2,1)S(1)}, bf16[128,640]{1,0:T(8,128)(2,1)S(1)}, u32[]{:S(2)}, u32[]{:S(2)}) %collective-permute-start.7) | collective-permute-done | bytes 163872 | tf_op jit(solution)/shard_map/ppermute | solution.py:430
  35.8 0.2 chip_merge.1
  36.0 1.6 %collective-permute-start.8 = (bf16[128,640]{1,0:T(8,128)(2,1)S(1)}, bf16[128,640]{1,0:T(8,128)(2,1)S(1)}, u32[]{:S(2)}, u32[]{:S(2)}) collective-permute-start(bf16[128,640]{1,0:T(8,128)(2,1)S(1)} %chip_merge.1), channel_id=1, source_target_pairs={{8,0},{12,4},{0,8},{4,12},{9,1},{13,5},{1,9},{5,13},{10,2},{14,6},... | collective-permute-start | bytes 491528 | tf_op jit(solution)/shard_map/ppermute | solution.py:431
  37.6 1.6 %suffix_near.1 = (bf16[4,64,576]{2,1,0:T(8,128)(2,1)}, bf16[128,640]{1,0:T(8,128)(2,1)S(1)}) custom-call(s32[4]{0:T(128)S(1)} %copy-done.3, s32[16]{0:T(128)S(1)} %copy-done.4, s32[2]{0:T(128)S(1)} %pad_add_fusion.place.refs_2_, bf16[4,576]{1,0:T(4,128)(2,1)S(1)} %copy-done.2, bf16[128,576]{1,0:T(8,128)(2,1)S(1)} %project.1.refs_0_, ...), custom_call_target="tpu_custom_call" | custom-call | tf_op jit(solution)/shard_map/suffix_near/pallas_call | solution.py:436
  39.2 3.2 %collective-permute-done.8.refs_0_ = bf16[128,640]{1,0:T(8,128)(2,1)S(1)} collective-permute-done((bf16[128,640]{1,0:T(8,128)(2,1)S(1)}, bf16[128,640]{1,0:T(8,128)(2,1)S(1)}, u32[]{:S(2)}, u32[]{:S(2)}) %collective-permute-start.8) | collective-permute-done | bytes 163872 | tf_op jit(solution)/shard_map/ppermute | solution.py:431
  42.3 1.3 %final.1 = bf16[4,32,128]{2,1,0:T(8,128)(2,1)} custom-call(bf16[128,640]{1,0:T(8,128)(2,1)S(1)} %collective-permute-done.8.refs_0_, bf16[128,640]{1,0:T(8,128)(2,1)S(1)} %get-tuple-element.38.refs_1_, bf16[32,512,128]{2,1,0:T(8,128)(2,1)S(1)} %copy-done), custom_call_target="tpu_custom_call" | custom-call | tf_op jit(solution)/shard_map/final/pallas_call | solution.py:446
  (20 shorter events, 0.3 us)
Async XLA Ops:
  0.6 6.4 %collective-permute-start = (s32[4]{0:T(128)}, s32[4]{0:T(128)S(1)}, u32[]{:S(2)}, u32[]{:S(2)}) collective-permute-start(s32[4]{0:T(128)} %anc.1), channel_id=1, source_target_pairs={{0,1},{1,0},{2,3},{3,2},{4,5},{5,4},{6,7},{7,6},{8,9},{9,8},{10,11... | collective-permute-start | bytes 56 | tf_op jit(solution)/shard_map/ppermute | solution.py:356
  3.7 1.0 %copy-start.1 = (bf16[4,64,576]{2,1,0:T(8,128)(2,1)S(1)}, bf16[4,64,576]{2,1,0:T(8,128)(2,1)}, u32[]{:S(2)}) copy-start(bf16[4,64,576]{2,1,0:T(8,128)(2,1)} %cache_ref.1) | copy-start | bytes 884740
  4.8 12.8 %collective-permute-start.4 = (bf16[128,1152]{1,0:T(8,128)(2,1)S(1)}, bf16[128,1152]{1,0:T(8,128)(2,1)S(1)}, u32[]{:S(2)}, u32[]{:S(2)}) collective-permute-start(bf16[128,1152]{1,0:T(8,128)(2,1)S(1)} %pack.1.refs_0_.refs_8_), channel_id=1, source_target_pairs={{1,2},{2,1},{5,6},{6,5},{9,10},{10,9},{13,14},{14,13},{17,18},{18,... | collective-permute-start | bytes 884744 | tf_op jit(solution)/shard_map/ppermute | solution.py:354
  9.5 13.2 %collective-permute-start.3 = (bf16[128,1152]{1,0:T(8,128)(2,1)S(1)}, bf16[128,1152]{1,0:T(8,128)(2,1)S(1)}, u32[]{:S(2)}, u32[]{:S(2)}) collective-permute-start(bf16[128,1152]{1,0:T(8,128)(2,1)S(1)} %pack.1.refs_0_.refs_8_), channel_id=1, source_target_pairs={{0,2},{3,1},{4,6},{7,5},{8,10},{11,9},{12,14},{15,13},{16,18},{19,... | collective-permute-start | bytes 884744 | tf_op jit(solution)/shard_map/ppermute | solution.py:378
  15.3 2.3 %collective-permute-start.5 = (bf16[128,576]{1,0:T(8,128)(2,1)S(1)}, bf16[128,576]{1,0:T(8,128)(2,1)S(1)}, u32[]{:S(2)}, u32[]{:S(2)}) collective-permute-start(bf16[128,576]{1,0:T(8,128)(2,1)S(1)} %project.1.refs_0_), channel_id=1, source_target_pairs={{0,4},{4,0},{8,12},{12,8},{1,5},{5,1},{9,13},{13,9},{2,6},{6,2},{1... | collective-permute-start | bytes 442376 | tf_op jit(solution)/shard_map/ppermute | solution.py:391
  15.3 10.7 %collective-permute-start.2 = (bf16[128,576]{1,0:T(8,128)(2,1)S(1)}, bf16[128,576]{1,0:T(8,128)(2,1)S(1)}, u32[]{:S(2)}, u32[]{:S(2)}) collective-permute-start(bf16[128,576]{1,0:T(8,128)(2,1)S(1)} %project.1.refs_0_), channel_id=1, source_target_pairs={{0,12},{4,8},{8,4},{12,0},{1,13},{5,9},{9,5},{13,1},{2,14},{6,10},... | collective-permute-start | bytes 442376 | tf_op jit(solution)/shard_map/ppermute | solution.py:391
  16.9 9.1 %collective-permute-start.1 = (bf16[128,576]{1,0:T(8,128)(2,1)S(1)}, bf16[128,576]{1,0:T(8,128)(2,1)S(1)}, u32[]{:S(2)}, u32[]{:S(2)}) collective-permute-start(bf16[128,576]{1,0:T(8,128)(2,1)S(1)} %project.1.refs_0_), channel_id=1, source_target_pairs={{0,8},{4,12},{8,0},{12,4},{1,9},{5,13},{9,1},{13,5},{2,10},{6,14},... | collective-permute-start | bytes 442376 | tf_op jit(solution)/shard_map/ppermute | solution.py:391
  23.7 8.8 %copy-start.3 = (s32[4]{0:T(128)S(1)}, s32[4]{0:T(128)}, u32[]{:S(2)}) copy-start(s32[4]{0:T(128)} %anc.1) | copy-start | bytes 52
  23.7 8.8 %copy-start.4 = (s32[16]{0:T(128)S(1)}, s32[16]{0:T(128)}, u32[]{:S(2)}) copy-start(s32[16]{0:T(128)} %lens.1) | copy-start | bytes 196
  23.8 13.8 %copy-start.2 = (bf16[4,576]{1,0:T(4,128)(2,1)S(1)}, bf16[4,576]{1,0:T(4,128)(2,1)}, u32[]{:S(2)}) copy-start(bf16[4,576]{1,0:T(4,128)(2,1)} %fresh_ref.1) | copy-start | bytes 13828
  23.8 8.8 %collective-permute-start.6 = (bf16[128,1152]{1,0:T(8,128)(2,1)S(1)}, bf16[128,1152]{1,0:T(8,128)(2,1)S(1)}, u32[]{:S(2)}, u32[]{:S(2)}) collective-permute-start(bf16[128,1152]{1,0:T(8,128)(2,1)S(1)} %select.1), channel_id=1, source_target_pairs={{0,1},{1,0},{2,3},{3,2},{4,5},{5,4},{6,7},{7,6},{8,9},{9,8},{10,11... | collective-permute-start | bytes 884744 | tf_op jit(solution)/shard_map/ppermute | solution.py:412
  26.0 16.3 %copy-start = (bf16[32,512,128]{2,1,0:T(8,128)(2,1)S(1)}, bf16[32,512,128]{2,1,0:T(8,128)(2,1)}, u32[]{:S(2)}) copy-start(bf16[32,512,128]{2,1,0:T(8,128)(2,1)} %refs_2_.1) | copy-start | bytes 12582916
  34.4 1.5 %collective-permute-start.7 = (bf16[128,640]{1,0:T(8,128)(2,1)S(1)}, bf16[128,640]{1,0:T(8,128)(2,1)S(1)}, u32[]{:S(2)}, u32[]{:S(2)}) collective-permute-start(bf16[128,640]{1,0:T(8,128)(2,1)S(1)} %get-tuple-element.32), channel_id=1, source_target_pairs={{0,4},{4,0},{8,12},{12,8},{1,5},{5,1},{9,13},{13,9},{2,6},{6,2},{1... | collective-permute-start | bytes 491528 | tf_op jit(solution)/shard_map/ppermute | solution.py:430
  34.4 3.1 %collective-permute-start.10 = (bf16[256,576]{1,0:T(8,128)(2,1)S(1)}, bf16[256,576]{1,0:T(8,128)(2,1)S(1)}, u32[]{:S(2)}, u32[]{:S(2)}) collective-permute-start(bf16[256,576]{1,0:T(8,128)(2,1)S(1)} %get-tuple-element.37.refs_5_), channel_id=1, source_target_pairs={{0,4},{4,0},{8,12},{12,8},{1,5},{5,1},{9,13},{13,9},{2,6},{6,2},{1... | collective-permute-start | bytes 884744 | tf_op jit(solution)/shard_map/ppermute | solution.py:432
  34.9 2.6 %collective-permute-start.9 = (bf16[128,640]{1,0:T(8,128)(2,1)S(1)}, bf16[128,640]{1,0:T(8,128)(2,1)S(1)}, u32[]{:S(2)}, u32[]{:S(2)}) collective-permute-start(bf16[128,640]{1,0:T(8,128)(2,1)S(1)} %get-tuple-element.35), channel_id=1, source_target_pairs={{0,4},{4,0},{8,12},{12,8},{1,5},{5,1},{9,13},{13,9},{2,6},{6,2},{1... | collective-permute-start | bytes 491528 | tf_op jit(solution)/shard_map/ppermute | solution.py:400
  36.0 6.3 %collective-permute-start.8 = (bf16[128,640]{1,0:T(8,128)(2,1)S(1)}, bf16[128,640]{1,0:T(8,128)(2,1)S(1)}, u32[]{:S(2)}, u32[]{:S(2)}) collective-permute-start(bf16[128,640]{1,0:T(8,128)(2,1)S(1)} %chip_merge.1), channel_id=1, source_target_pairs={{8,0},{12,4},{0,8},{4,12},{9,1},{13,5},{1,9},{5,13},{10,2},{14,6},... | collective-permute-start | bytes 491528 | tf_op jit(solution)/shard_map/ppermute | solution.py:431

commit v9 on v8

--- a/solution.py
+++ b/solution.py
@@ -353,7 +353,8 @@
     if line:
         far = lax.ppermute(block, "dom", [(1, 2), (2, 1)])
         swap = [(0, 1), (1, 0), (2, 3), (3, 2)]
-        theirs = lax.ppermute(ancestors, "dom", swap)
+        block, named = lax.optimization_barrier((block, ancestors))
+        theirs = lax.ppermute(named, "dom", swap)
     else:
         blocks = [block] + [
             lax.ppermute(block, "dom", [(i, (i + k) % dom_size) for i in range(dom_size)])

time: 44 us -> 45 us (1.023)
  waiting for transfers between devices: 5.28 us -> 6.38 us
    ppermute x1, starting transfers between devices: 3.09 us -> 5.89 us  [on_device(): theirs = lax.ppermute(named, 'dom', swap)]
    ppermute x1, starting transfers between devices: 5.75 us -> 3.83 us  [on_device(): middle = lax.ppermute(sent, 'dom', [(0, 2), (3, 1)])]
    ppermute x1, starting transfers between devices: 2.24 us -> 1.23 us  [on_device(): blocks = [block, lax.ppermute(chosen, 'dom', swap), middle, far]]
    ppermute x1, waiting for transfers between devices: 1.29 us -> 1.9 us  [on_device(): blocks = [block, lax.ppermute(chosen, 'dom', swap), middle, far]]
  transfers between devices with their start and end apart: 11 -> 11, of which waited for: 3 -> 5; matrix products, arithmetic and copies ran while one was open for 4% -> 4% of each run, Pallas kernels for 36% -> 35%
where the time goes in v9:
time: 45 us; the launch traced here: 44.7 us
  Pallas kernels  18.8 us (42%)
  starting transfers between devices  16 us (36%)
  waiting for transfers between devices  6.38 us (14%)
  local copies, waits for them, and re-layouts  2.54 us (6%)
  between operations  0.77 us (2%)
    pallas_call x2, Pallas kernels, prefix_attention(): pl.pallas_call(functools.partial(prefix_kernel, len(queries), tiles), out...  10.3 us
    ppermute x1, starting transfers between devices, on_device(): theirs = lax.ppermute(named, 'dom', swap)  5.89 us
    ppermute x1, starting transfers between devices, on_device(): middle = lax.ppermute(sent, 'dom', [(0, 2), (3, 1)])  3.83 us
    ppermute x1, waiting for transfers between devices, on_device(): parts = [lax.ppermute(s, 'seq', back(t, 0)) for t, s in enumerate(sums, 1)]  3.14 us
    pallas_call x1, Pallas kernels, on_device(): pl.pallas_call(functools.partial(project_kernel, pieces, local), out_shap...  2.46 us
    ppermute x3, starting transfers between devices, on_device(): lax.ppermute(own, 'seq', pairs(*r))  2.21 us
    ppermute x1, waiting for transfers between devices, on_device(): blocks = [block, lax.ppermute(chosen, 'dom', swap), middle, far]  1.9 us
    pallas_call x1, Pallas kernels, on_device(): pl.pallas_call(functools.partial(far_kernel, others, len(blocks), line),...  1.83 us
  transfers between devices with their start and end apart: 11, of which 5 were waited for; matrix products, arithmetic and copies ran while one was open for 4% of the time, Pallas kernels for 35%

profile of v9, /device:TPU:0, one launch (start us, length us, event | category | flops | bytes accessed | tf_op | source)
XLA Modules:
  0.0 44.7 jit_solution(5348469112719593779)
XLA Ops:
  0.6 1.0 %copy-done.1 = bf16[4,64,576]{2,1,0:T(8,128)(2,1)S(1)} copy-done((bf16[4,64,576]{2,1,0:T(8,128)(2,1)S(1)}, bf16[4,64,576]{2,1,0:T(8,128)(2,1)}, u32[]{:S(2)}) %copy-start.1) | copy-done | bytes 294936
  1.7 0.7 %collective-permute-start.4 = (bf16[128,1152]{1,0:T(8,128)(2,1)S(1)}, bf16[128,1152]{1,0:T(8,128)(2,1)S(1)}, u32[]{:S(2)}, u32[]{:S(2)}) collective-permute-start(bf16[128,1152]{1,0:T(8,128)(2,1)S(1)} %pack.1.refs_0_.refs_8_), channel_id=1, source_target_pairs={{1,2},{2,1},{5,6},{6,5},{9,10},{10,9},{13,14},{14,13},{17,18},{18,... | collective-permute-start | bytes 884744 | tf_op jit(solution)/shard_map/ppermute | solution.py:354
  2.4 5.9 %collective-permute-start = (s32[4]{0:T(128)}, s32[4]{0:T(128)S(1)}, u32[]{:S(2)}, u32[]{:S(2)}) collective-permute-start(s32[4]{0:T(128)} %anc.1), channel_id=1, source_target_pairs={{0,1},{1,0},{2,3},{3,2},{4,5},{5,4},{6,7},{7,6},{8,9},{9,8},{10,11... | collective-permute-start | bytes 56 | tf_op jit(solution)/shard_map/ppermute | solution.py:357
  8.3 0.8 %copy.11 = bf16[32,4,128]{2,1,0:T(4,128)(2,1)S(1)} copy(bf16[32,4,128]{2,0,1:T(8,128)(2,1)} %bitcast.11) | data formatting | bytes 65536 | tf_op jit(solution)/shard_map/transpose | solution.py:351
  9.0 0.8 %copy.12 = bf16[32,4,64]{2,1,0:T(4,128)(2,1)S(1)} copy(bf16[32,4,64]{2,0,1:T(8,128)(2,1)} %bitcast.12) | data formatting | bytes 32768 | tf_op jit(solution)/shard_map/transpose | solution.py:351
  9.8 0.1 collective-permute-done.theirs
  9.9 2.5 %project.1.refs_0_ = bf16[128,576]{1,0:T(8,128)(2,1)S(1)} custom-call(bf16[128,128]{1,0:T(8,128)(2,1)S(1)} %bitcast.7, bf16[128,64]{1,0:T(8,128)(2,1)S(1)} %bitcast.8, bf16[32,128,512]{2,1,0:T(8,128)(2,1)} %w_hbm.1), custom_call_target="tpu_custom_call" | custom-call | tf_op jit(solution)/shard_map/project/pallas_call | solution.py:367
  12.4 3.8 %collective-permute-start.3 = (bf16[128,1152]{1,0:T(8,128)(2,1)S(1)}, bf16[128,1152]{1,0:T(8,128)(2,1)S(1)}, u32[]{:S(2)}, u32[]{:S(2)}) collective-permute-start(bf16[128,1152]{1,0:T(8,128)(2,1)S(1)} %pack.1.refs_0_.refs_8_), channel_id=1, source_target_pairs={{0,2},{3,1},{4,6},{7,5},{8,10},{11,9},{12,14},{15,13},{16,18},{19,... | collective-permute-start | bytes 884744 | tf_op jit(solution)/shard_map/ppermute | solution.py:379
  16.3 1.6 %collective-permute-start.2 = (bf16[128,576]{1,0:T(8,128)(2,1)S(1)}, bf16[128,576]{1,0:T(8,128)(2,1)S(1)}, u32[]{:S(2)}, u32[]{:S(2)}) collective-permute-start(bf16[128,576]{1,0:T(8,128)(2,1)S(1)} %project.1.refs_0_), channel_id=1, source_target_pairs={{0,12},{4,8},{8,4},{12,0},{1,13},{5,9},{9,5},{13,1},{2,14},{6,10},... | collective-permute-start | bytes 442376 | tf_op jit(solution)/shard_map/ppermute | solution.py:392
  17.9 0.5 %collective-permute-start.1 = (bf16[128,576]{1,0:T(8,128)(2,1)S(1)}, bf16[128,576]{1,0:T(8,128)(2,1)S(1)}, u32[]{:S(2)}, u32[]{:S(2)}) collective-permute-start(bf16[128,576]{1,0:T(8,128)(2,1)S(1)} %project.1.refs_0_), channel_id=1, source_target_pairs={{0,8},{4,12},{8,0},{12,4},{1,9},{5,13},{9,1},{13,5},{2,10},{6,14},... | collective-permute-start | bytes 442376 | tf_op jit(solution)/shard_map/ppermute | solution.py:392
  18.5 5.1 %prefix_attention.3 = (f32[128,512]{1,0:T(8,128)S(1)}, f32[128,128]{1,0:T(8,128)S(1)}, f32[128,128]{1,0:T(8,128)S(1)}, bf16[128,640]{1,0:T(8,128)(2,1)S(1)}) custom-call(bf16[128,576]{1,0:T(8,128)(2,1)S(1)} %project.1.refs_0_, bf16[128,576]{1,0:T(8,128)(2,1)S(1)} %collective-permute-done.5.refs_1_, bf16[576,4096]{1,0:T(8,128)(2,1)} %bitcast.9), custom_call_target="tpu_custom_call" | custom-call | tf_op jit(solution)/shard_map/prefix_attention/pallas_call | solution.py:129
  23.6 1.0 %select.1 = bf16[128,1152]{1,0:T(8,128)(2,1)S(1)} custom-call(s32[4]{0:T(128)S(1)} %collective-permute-done.theirs, s32[2]{0:T(128)S(1)} %pad_add_fusion.place.refs_2_, bf16[128,1152]{1,0:T(8,128)(2,1)S(1)} %pack.1.refs_0_.refs_8_, bf16[128,1152]{1,0:T(8,128)(2,1)S(1)} %collective-permute-done.3.refs_1_.refs_10_, ...), custom_call_target="tpu_custom_call" | custom-call | tf_op jit(solution)/shard_map/select/pallas_call | solution.py:403
  24.7 1.2 %collective-permute-start.6 = (bf16[128,1152]{1,0:T(8,128)(2,1)S(1)}, bf16[128,1152]{1,0:T(8,128)(2,1)S(1)}, u32[]{:S(2)}, u32[]{:S(2)}) collective-permute-start(bf16[128,1152]{1,0:T(8,128)(2,1)S(1)} %select.1), channel_id=1, source_target_pairs={{0,1},{1,0},{2,3},{3,2},{4,5},{5,4},{6,7},{7,6},{8,9},{9,8},{10,11... | collective-permute-start | bytes 884744 | tf_op jit(solution)/shard_map/ppermute | solution.py:413
  26.0 0.4 collective-permute-done.1.refs_0_.refs_3_
  26.4 5.2 %prefix_attention.2 = (f32[256,512]{1,0:T(8,128)S(1)}, f32[256,128]{1,0:T(8,128)S(1)}, f32[256,128]{1,0:T(8,128)S(1)}) custom-call(bf16[128,576]{1,0:T(8,128)(2,1)S(1)} %collective-permute-done.1.refs_0_.refs_3_, bf16[128,576]{1,0:T(8,128)(2,1)S(1)} %collective-permute-done.2.refs_1_.refs_4_, bf16[576,4096]{1,0:T(8,128)(2,1)} %bitcast.10), custom_call_target="tpu_custom_call" | custom-call | flops 2281701376 | bytes 4718592 | tf_op jit(solution)/shard_map/prefix_attention/pallas_call | solution.py:129
  31.6 1.9 %collective-permute-done.6.refs_9_ = bf16[128,1152]{1,0:T(8,128)(2,1)S(1)} collective-permute-done((bf16[128,1152]{1,0:T(8,128)(2,1)S(1)}, bf16[128,1152]{1,0:T(8,128)(2,1)S(1)}, u32[]{:S(2)}, u32[]{:S(2)}) %collective-permute-start.6) | collective-permute-done | bytes 294944 | tf_op jit(solution)/shard_map/ppermute | solution.py:413
  33.5 1.8 %suffix_far.1 = (bf16[256,576]{1,0:T(8,128)(2,1)S(1)}, bf16[128,640]{1,0:T(8,128)(2,1)S(1)}, bf16[128,640]{1,0:T(8,128)(2,1)S(1)}) custom-call(s32[4]{0:T(128)S(1)} %copy-done.3, s32[16]{0:T(128)S(1)} %copy-done.4, s32[2]{0:T(128)S(1)} %pad_add_fusion.place.refs_2_, bf16[128,576]{1,0:T(8,128)(2,1)S(1)} %collective-permute-done.1.refs_0_.refs_3_, ...), custom_call_target="tpu_custom_call" | custom-call | tf_op jit(solution)/shard_map/suffix_far/pallas_call | solution.py:417
  35.4 0.5 %collective-permute-start.10 = (bf16[256,576]{1,0:T(8,128)(2,1)S(1)}, bf16[256,576]{1,0:T(8,128)(2,1)S(1)}, u32[]{:S(2)}, u32[]{:S(2)}) collective-permute-start(bf16[256,576]{1,0:T(8,128)(2,1)S(1)} %get-tuple-element.41.refs_5_), channel_id=1, source_target_pairs={{0,4},{4,0},{8,12},{12,8},{1,5},{5,1},{9,13},{13,9},{2,6},{6,2},{1... | collective-permute-start | bytes 884744 | tf_op jit(solution)/shard_map/ppermute | solution.py:433
  36.0 0.8 %collective-permute-done.7.refs_1_ = bf16[128,640]{1,0:T(8,128)(2,1)S(1)} collective-permute-done((bf16[128,640]{1,0:T(8,128)(2,1)S(1)}, bf16[128,640]{1,0:T(8,128)(2,1)S(1)}, u32[]{:S(2)}, u32[]{:S(2)}) %collective-permute-start.7) | collective-permute-done | bytes 163872 | tf_op jit(solution)/shard_map/ppermute | solution.py:431
  36.8 0.2 chip_merge.1
  37.0 1.6 %collective-permute-start.8 = (bf16[128,640]{1,0:T(8,128)(2,1)S(1)}, bf16[128,640]{1,0:T(8,128)(2,1)S(1)}, u32[]{:S(2)}, u32[]{:S(2)}) collective-permute-start(bf16[128,640]{1,0:T(8,128)(2,1)S(1)} %chip_merge.1), channel_id=1, source_target_pairs={{8,0},{12,4},{0,8},{4,12},{9,1},{13,5},{1,9},{5,13},{10,2},{14,6},... | collective-permute-start | bytes 491528 | tf_op jit(solution)/shard_map/ppermute | solution.py:432
  38.6 1.6 %suffix_near.1 = (bf16[4,64,576]{2,1,0:T(8,128)(2,1)}, bf16[128,640]{1,0:T(8,128)(2,1)S(1)}) custom-call(s32[4]{0:T(128)S(1)} %copy-done.3, s32[16]{0:T(128)S(1)} %copy-done.4, s32[2]{0:T(128)S(1)} %pad_add_fusion.place.refs_2_, bf16[4,576]{1,0:T(4,128)(2,1)S(1)} %copy-done.2, bf16[128,576]{1,0:T(8,128)(2,1)S(1)} %project.1.refs_0_, ...), custom_call_target="tpu_custom_call" | custom-call | tf_op jit(solution)/shard_map/suffix_near/pallas_call | solution.py:437
  40.2 3.1 %collective-permute-done.8.refs_0_ = bf16[128,640]{1,0:T(8,128)(2,1)S(1)} collective-permute-done((bf16[128,640]{1,0:T(8,128)(2,1)S(1)}, bf16[128,640]{1,0:T(8,128)(2,1)S(1)}, u32[]{:S(2)}, u32[]{:S(2)}) %collective-permute-start.8) | collective-permute-done | bytes 163872 | tf_op jit(solution)/shard_map/ppermute | solution.py:432
  43.3 1.3 %final.1 = bf16[4,32,128]{2,1,0:T(8,128)(2,1)} custom-call(bf16[128,640]{1,0:T(8,128)(2,1)S(1)} %collective-permute-done.8.refs_0_, bf16[128,640]{1,0:T(8,128)(2,1)S(1)} %get-tuple-element.42.refs_1_, bf16[32,512,128]{2,1,0:T(8,128)(2,1)S(1)} %copy-done), custom_call_target="tpu_custom_call" | custom-call | tf_op jit(solution)/shard_map/final/pallas_call | solution.py:447
  (20 shorter events, 0.4 us)
Async XLA Ops:
  0.6 1.0 %copy-start.1 = (bf16[4,64,576]{2,1,0:T(8,128)(2,1)S(1)}, bf16[4,64,576]{2,1,0:T(8,128)(2,1)}, u32[]{:S(2)}) copy-start(bf16[4,64,576]{2,1,0:T(8,128)(2,1)} %cache_ref.1) | copy-start | bytes 884740
  1.7 16.8 %collective-permute-start.4 = (bf16[128,1152]{1,0:T(8,128)(2,1)S(1)}, bf16[128,1152]{1,0:T(8,128)(2,1)S(1)}, u32[]{:S(2)}, u32[]{:S(2)}) collective-permute-start(bf16[128,1152]{1,0:T(8,128)(2,1)S(1)} %pack.1.refs_0_.refs_8_), channel_id=1, source_target_pairs={{1,2},{2,1},{5,6},{6,5},{9,10},{10,9},{13,14},{14,13},{17,18},{18,... | collective-permute-start | bytes 884744 | tf_op jit(solution)/shard_map/ppermute | solution.py:354
  2.4 7.6 %collective-permute-start = (s32[4]{0:T(128)}, s32[4]{0:T(128)S(1)}, u32[]{:S(2)}, u32[]{:S(2)}) collective-permute-start(s32[4]{0:T(128)} %anc.1), channel_id=1, source_target_pairs={{0,1},{1,0},{2,3},{3,2},{4,5},{5,4},{6,7},{7,6},{8,9},{9,8},{10,11... | collective-permute-start | bytes 56 | tf_op jit(solution)/shard_map/ppermute | solution.py:357
  12.4 11.3 %collective-permute-start.3 = (bf16[128,1152]{1,0:T(8,128)(2,1)S(1)}, bf16[128,1152]{1,0:T(8,128)(2,1)S(1)}, u32[]{:S(2)}, u32[]{:S(2)}) collective-permute-start(bf16[128,1152]{1,0:T(8,128)(2,1)S(1)} %pack.1.refs_0_.refs_8_), channel_id=1, source_target_pairs={{0,2},{3,1},{4,6},{7,5},{8,10},{11,9},{12,14},{15,13},{16,18},{19,... | collective-permute-start | bytes 884744 | tf_op jit(solution)/shard_map/ppermute | solution.py:379
  16.2 2.3 %collective-permute-start.5 = (bf16[128,576]{1,0:T(8,128)(2,1)S(1)}, bf16[128,576]{1,0:T(8,128)(2,1)S(1)}, u32[]{:S(2)}, u32[]{:S(2)}) collective-permute-start(bf16[128,576]{1,0:T(8,128)(2,1)S(1)} %project.1.refs_0_), channel_id=1, source_target_pairs={{0,4},{4,0},{8,12},{12,8},{1,5},{5,1},{9,13},{13,9},{2,6},{6,2},{1... | collective-permute-start | bytes 442376 | tf_op jit(solution)/shard_map/ppermute | solution.py:392
  16.3 9.7 %collective-permute-start.2 = (bf16[128,576]{1,0:T(8,128)(2,1)S(1)}, bf16[128,576]{1,0:T(8,128)(2,1)S(1)}, u32[]{:S(2)}, u32[]{:S(2)}) collective-permute-start(bf16[128,576]{1,0:T(8,128)(2,1)S(1)} %project.1.refs_0_), channel_id=1, source_target_pairs={{0,12},{4,8},{8,4},{12,0},{1,13},{5,9},{9,5},{13,1},{2,14},{6,10},... | collective-permute-start | bytes 442376 | tf_op jit(solution)/shard_map/ppermute | solution.py:392
  17.9 8.5 %collective-permute-start.1 = (bf16[128,576]{1,0:T(8,128)(2,1)S(1)}, bf16[128,576]{1,0:T(8,128)(2,1)S(1)}, u32[]{:S(2)}, u32[]{:S(2)}) collective-permute-start(bf16[128,576]{1,0:T(8,128)(2,1)S(1)} %project.1.refs_0_), channel_id=1, source_target_pairs={{0,8},{4,12},{8,0},{12,4},{1,9},{5,13},{9,1},{13,5},{2,10},{6,14},... | collective-permute-start | bytes 442376 | tf_op jit(solution)/shard_map/ppermute | solution.py:392
  24.7 8.8 %copy-start.3 = (s32[4]{0:T(128)S(1)}, s32[4]{0:T(128)}, u32[]{:S(2)}) copy-start(s32[4]{0:T(128)} %anc.1) | copy-start | bytes 52
  24.7 8.8 %copy-start.4 = (s32[16]{0:T(128)S(1)}, s32[16]{0:T(128)}, u32[]{:S(2)}) copy-start(s32[16]{0:T(128)} %lens.1) | copy-start | bytes 196
  24.7 13.8 %copy-start.2 = (bf16[4,576]{1,0:T(4,128)(2,1)S(1)}, bf16[4,576]{1,0:T(4,128)(2,1)}, u32[]{:S(2)}) copy-start(bf16[4,576]{1,0:T(4,128)(2,1)} %fresh_ref.1) | copy-start | bytes 13828
  24.7 8.8 %collective-permute-start.6 = (bf16[128,1152]{1,0:T(8,128)(2,1)S(1)}, bf16[128,1152]{1,0:T(8,128)(2,1)S(1)}, u32[]{:S(2)}, u32[]{:S(2)}) collective-permute-start(bf16[128,1152]{1,0:T(8,128)(2,1)S(1)} %select.1), channel_id=1, source_target_pairs={{0,1},{1,0},{2,3},{3,2},{4,5},{5,4},{6,7},{7,6},{8,9},{9,8},{10,11... | collective-permute-start | bytes 884744 | tf_op jit(solution)/shard_map/ppermute | solution.py:413
  26.4 16.9 %copy-start = (bf16[32,512,128]{2,1,0:T(8,128)(2,1)S(1)}, bf16[32,512,128]{2,1,0:T(8,128)(2,1)}, u32[]{:S(2)}) copy-start(bf16[32,512,128]{2,1,0:T(8,128)(2,1)} %refs_2_.1) | copy-start | bytes 12582916
  35.3 1.5 %collective-permute-start.7 = (bf16[128,640]{1,0:T(8,128)(2,1)S(1)}, bf16[128,640]{1,0:T(8,128)(2,1)S(1)}, u32[]{:S(2)}, u32[]{:S(2)}) collective-permute-start(bf16[128,640]{1,0:T(8,128)(2,1)S(1)} %get-tuple-element.36), channel_id=1, source_target_pairs={{0,4},{4,0},{8,12},{12,8},{1,5},{5,1},{9,13},{13,9},{2,6},{6,2},{1... | collective-permute-start | bytes 491528 | tf_op jit(solution)/shard_map/ppermute | solution.py:431
  35.4 3.2 %collective-permute-start.10 = (bf16[256,576]{1,0:T(8,128)(2,1)S(1)}, bf16[256,576]{1,0:T(8,128)(2,1)S(1)}, u32[]{:S(2)}, u32[]{:S(2)}) collective-permute-start(bf16[256,576]{1,0:T(8,128)(2,1)S(1)} %get-tuple-element.41.refs_5_), channel_id=1, source_target_pairs={{0,4},{4,0},{8,12},{12,8},{1,5},{5,1},{9,13},{13,9},{2,6},{6,2},{1... | collective-permute-start | bytes 884744 | tf_op jit(solution)/shard_map/ppermute | solution.py:433
  35.9 2.7 %collective-permute-start.9 = (bf16[128,640]{1,0:T(8,128)(2,1)S(1)}, bf16[128,640]{1,0:T(8,128)(2,1)S(1)}, u32[]{:S(2)}, u32[]{:S(2)}) collective-permute-start(bf16[128,640]{1,0:T(8,128)(2,1)S(1)} %get-tuple-element.39), channel_id=1, source_target_pairs={{0,4},{4,0},{8,12},{12,8},{1,5},{5,1},{9,13},{13,9},{2,6},{6,2},{1... | collective-permute-start | bytes 491528 | tf_op jit(solution)/shard_map/ppermute | solution.py:401
  37.0 6.3 %collective-permute-start.8 = (bf16[128,640]{1,0:T(8,128)(2,1)S(1)}, bf16[128,640]{1,0:T(8,128)(2,1)S(1)}, u32[]{:S(2)}, u32[]{:S(2)}) collective-permute-start(bf16[128,640]{1,0:T(8,128)(2,1)S(1)} %chip_merge.1), channel_id=1, source_target_pairs={{8,0},{12,4},{0,8},{4,12},{9,1},{13,5},{1,9},{5,13},{10,2},{14,6},... | collective-permute-start | bytes 491528 | tf_op jit(solution)/shard_map/ppermute | solution.py:432

commit v10 on v8

--- a/solution.py
+++ b/solution.py
@@ -137,10 +137,10 @@
             pltpu.SemaphoreType.DMA((tiles,)),
         ],
         compiler_params=STREAM,
-        cost_estimate=None if give else pl.CostEstimate(
-            flops=2 * rows * length * (width + rank),
-            bytes_accessed=2 * width * length,
-            transcendentals=rows * length,
+        cost_estimate=pl.CostEstimate(
+            flops=0 if give else 2 * rows * length * (width + rank),
+            bytes_accessed=0 if give else 2 * width * length,
+            transcendentals=0 if give else rows * length,
         ),
         name="prefix_attention",
     )(*queries, keys)
@@ -353,15 +353,14 @@
     if line:
         far = lax.ppermute(block, "dom", [(1, 2), (2, 1)])
         swap = [(0, 1), (1, 0), (2, 3), (3, 2)]
-        theirs = lax.ppermute(ancestors, "dom", swap)
+        middle = lax.ppermute(block, "dom", [(0, 2), (3, 1)])
+        theirs = lax.ppermute(ancestors, "dom", [(0, 1), (3, 2)])
     else:
         blocks = [block] + [
             lax.ppermute(block, "dom", [(i, (i + k) % dom_size) for i in range(dom_size)])
             for k in range(1, dom_size)
         ]
 
-    if line:
-        theirs, nope_rows = lax.optimization_barrier((theirs, nope_rows))
     pieces = math.gcd(heads // 4, 4)
     own = pl.pallas_call(
         functools.partial(project_kernel, pieces, local),
@@ -373,9 +372,6 @@
         name="project",
     )(nope_rows, rope_rows, w_uk)
     keys = prefix.T
-    if line:
-        sent, own = lax.optimization_barrier((block, own))
-        middle = lax.ppermute(sent, "dom", [(0, 2), (3, 1)])
 
     def pairs(turn, flip):
         return [

time: 44 us -> 45.6 us (1.036)
  starting transfers between devices: 16.2 us -> 18.1 us
    ppermute x1, starting transfers between devices: 2.24 us -> 3.98 us  [on_device(): blocks = [block, lax.ppermute(chosen, 'dom', swap), middle, far]]
  transfers between devices with their start and end apart: 11 -> 11, of which waited for: 3 -> 3; matrix products, arithmetic and copies ran while one was open for 4% -> 4% of each run, Pallas kernels for 36% -> 35%
where the time goes in v10:
time: 45.6 us; the launch traced here: 45.2 us
  Pallas kernels  18.9 us (41%)
  starting transfers between devices  18.1 us (40%)
  waiting for transfers between devices  4.87 us (11%)
  local copies, waits for them, and re-layouts  2.54 us (6%)
  between operations  0.78 us (2%)
    pallas_call x2, Pallas kernels, prefix_attention(): pl.pallas_call(functools.partial(prefix_kernel, len(queries), tiles), out...  10.3 us
    ppermute x1, starting transfers between devices, on_device(): middle = lax.ppermute(block, 'dom', [(0, 2), (3, 1)])  7.64 us
    ppermute x1, starting transfers between devices, on_device(): blocks = [block, lax.ppermute(chosen, 'dom', swap), middle, far]  3.98 us
    ppermute x1, waiting for transfers between devices, on_device(): parts = [lax.ppermute(s, 'seq', back(t, 0)) for t, s in enumerate(sums, 1)]  3.15 us
    pallas_call x1, Pallas kernels, on_device(): pl.pallas_call(functools.partial(project_kernel, pieces, local), out_shap...  2.46 us
    ppermute x3, starting transfers between devices, on_device(): lax.ppermute(own, 'seq', pairs(*r))  2.21 us
    pallas_call x1, Pallas kernels, on_device(): pl.pallas_call(functools.partial(far_kernel, others, len(blocks), line),...  1.83 us
    pallas_call x1, Pallas kernels, on_device(): pl.pallas_call(near_kernel, out_shape=[shape(private_caches.shape), part]...  1.59 us
  transfers between devices with their start and end apart: 11, of which 3 were waited for; matrix products, arithmetic and copies ran while one was open for 4% of the time, Pallas kernels for 35%

profile of v10, /device:TPU:0, one launch (start us, length us, event | category | flops | bytes accessed | tf_op | source)
XLA Modules:
  0.0 45.2 jit_solution(10415433611515914063)
XLA Ops:
  0.6 1.0 %copy-done.1 = bf16[4,64,576]{2,1,0:T(8,128)(2,1)S(1)} copy-done((bf16[4,64,576]{2,1,0:T(8,128)(2,1)S(1)}, bf16[4,64,576]{2,1,0:T(8,128)(2,1)}, u32[]{:S(2)}) %copy-start.1) | copy-done | bytes 294936
  1.6 0.1 pack.1.refs_0_.refs_8_
  1.7 0.7 %collective-permute-start.4 = (bf16[128,1152]{1,0:T(8,128)(2,1)S(1)}, bf16[128,1152]{1,0:T(8,128)(2,1)S(1)}, u32[]{:S(2)}, u32[]{:S(2)}) collective-permute-start(bf16[128,1152]{1,0:T(8,128)(2,1)S(1)} %pack.1.refs_0_.refs_8_), channel_id=1, source_target_pairs={{1,2},{2,1},{5,6},{6,5},{9,10},{10,9},{13,14},{14,13},{17,18},{18,... | collective-permute-start | bytes 884744 | tf_op jit(solution)/shard_map/ppermute | solution.py:354
  2.4 7.6 %collective-permute-start.3 = (bf16[128,1152]{1,0:T(8,128)(2,1)S(1)}, bf16[128,1152]{1,0:T(8,128)(2,1)S(1)}, u32[]{:S(2)}, u32[]{:S(2)}) collective-permute-start(bf16[128,1152]{1,0:T(8,128)(2,1)S(1)} %pack.1.refs_0_.refs_8_), channel_id=1, source_target_pairs={{0,2},{3,1},{4,6},{7,5},{8,10},{11,9},{12,14},{15,13},{16,18},{19,... | collective-permute-start | bytes 884744 | tf_op jit(solution)/shard_map/ppermute | solution.py:356
  10.0 0.8 %copy.11 = bf16[32,4,128]{2,1,0:T(4,128)(2,1)S(1)} copy(bf16[32,4,128]{2,0,1:T(8,128)(2,1)} %bitcast.11) | data formatting | bytes 65536 | tf_op jit(solution)/shard_map/transpose | solution.py:351
  10.8 0.8 %copy.12 = bf16[32,4,64]{2,1,0:T(4,128)(2,1)S(1)} copy(bf16[32,4,64]{2,0,1:T(8,128)(2,1)} %bitcast.12) | data formatting | bytes 32768 | tf_op jit(solution)/shard_map/transpose | solution.py:351
  11.6 2.5 %project.1.refs_0_ = bf16[128,576]{1,0:T(8,128)(2,1)S(1)} custom-call(bf16[128,128]{1,0:T(8,128)(2,1)S(1)} %bitcast.7, bf16[128,64]{1,0:T(8,128)(2,1)S(1)} %bitcast.8, bf16[32,128,512]{2,1,0:T(8,128)(2,1)} %w_hbm.1), custom_call_target="tpu_custom_call" | custom-call | tf_op jit(solution)/shard_map/project/pallas_call | solution.py:365
  14.1 1.6 %collective-permute-start.1 = (bf16[128,576]{1,0:T(8,128)(2,1)S(1)}, bf16[128,576]{1,0:T(8,128)(2,1)S(1)}, u32[]{:S(2)}, u32[]{:S(2)}) collective-permute-start(bf16[128,576]{1,0:T(8,128)(2,1)S(1)} %project.1.refs_0_), channel_id=1, source_target_pairs={{0,12},{4,8},{8,4},{12,0},{1,13},{5,9},{9,5},{13,1},{2,14},{6,10},... | collective-permute-start | bytes 442376 | tf_op jit(solution)/shard_map/ppermute | solution.py:387
  15.7 0.5 %collective-permute-start = (bf16[128,576]{1,0:T(8,128)(2,1)S(1)}, bf16[128,576]{1,0:T(8,128)(2,1)S(1)}, u32[]{:S(2)}, u32[]{:S(2)}) collective-permute-start(bf16[128,576]{1,0:T(8,128)(2,1)S(1)} %project.1.refs_0_), channel_id=1, source_target_pairs={{0,8},{4,12},{8,0},{12,4},{1,9},{5,13},{9,1},{13,5},{2,10},{6,14},... | collective-permute-start | bytes 442376 | tf_op jit(solution)/shard_map/ppermute | solution.py:387
  16.3 1.4 %collective-permute-start.2 = (s32[4]{0:T(128)S(1)}, s32[4]{0:T(128)S(1)}, u32[]{:S(2)}, u32[]{:S(2)}) collective-permute-start(s32[4]{0:T(128)S(1)} %copy-done.3), channel_id=1, source_target_pairs={{0,1},{3,2},{4,5},{7,6},{8,9},{11,10},{12,13},{15,14},{16,17},{19,... | collective-permute-start | bytes 56 | tf_op jit(solution)/shard_map/ppermute | solution.py:357
  17.7 5.1 %prefix_attention.3 = (f32[128,512]{1,0:T(8,128)S(1)}, f32[128,128]{1,0:T(8,128)S(1)}, f32[128,128]{1,0:T(8,128)S(1)}, bf16[128,640]{1,0:T(8,128)(2,1)S(1)}) custom-call(bf16[128,576]{1,0:T(8,128)(2,1)S(1)} %project.1.refs_0_, bf16[128,576]{1,0:T(8,128)(2,1)S(1)} %collective-permute-done.5.refs_1_, bf16[576,4096]{1,0:T(8,128)(2,1)} %bitcast.9), custom_call_target="tpu_custom_call" | custom-call | tf_op jit(solution)/shard_map/prefix_attention/pallas_call | solution.py:129
  22.9 1.0 %select.1 = bf16[128,1152]{1,0:T(8,128)(2,1)S(1)} custom-call(s32[4]{0:T(128)S(1)} %collective-permute-done.2.theirs, s32[2]{0:T(128)S(1)} %pad_add_fusion.place.refs_2_, bf16[128,1152]{1,0:T(8,128)(2,1)S(1)} %pack.1.refs_0_.refs_8_, bf16[128,1152]{1,0:T(8,128)(2,1)S(1)} %collective-permute-done.3.refs_1_.refs_10_, ...), custom_call_target="tpu_custom_call" | custom-call | tf_op jit(solution)/shard_map/select/pallas_call | solution.py:398
  24.0 4.0 %collective-permute-start.6 = (bf16[128,1152]{1,0:T(8,128)(2,1)S(1)}, bf16[128,1152]{1,0:T(8,128)(2,1)S(1)}, u32[]{:S(2)}, u32[]{:S(2)}) collective-permute-start(bf16[128,1152]{1,0:T(8,128)(2,1)S(1)} %select.1), channel_id=1, source_target_pairs={{0,1},{1,0},{2,3},{3,2},{4,5},{5,4},{6,7},{7,6},{8,9},{9,8},{10,11... | collective-permute-start | bytes 884744 | tf_op jit(solution)/shard_map/ppermute | solution.py:408
  28.0 5.2 %prefix_attention.2 = (f32[256,512]{1,0:T(8,128)S(1)}, f32[256,128]{1,0:T(8,128)S(1)}, f32[256,128]{1,0:T(8,128)S(1)}) custom-call(bf16[128,576]{1,0:T(8,128)(2,1)S(1)} %collective-permute-done.refs_0_.refs_3_, bf16[128,576]{1,0:T(8,128)(2,1)S(1)} %collective-permute-done.1.refs_1_.refs_4_, bf16[576,4096]{1,0:T(8,128)(2,1)} %bitcast.10), custom_call_target="tpu_custom_call" | custom-call | flops 2281701376 | bytes 4718592 | tf_op jit(solution)/shard_map/prefix_attention/pallas_call | solution.py:129
  33.2 0.9 %collective-permute-done.6.refs_9_ = bf16[128,1152]{1,0:T(8,128)(2,1)S(1)} collective-permute-done((bf16[128,1152]{1,0:T(8,128)(2,1)S(1)}, bf16[128,1152]{1,0:T(8,128)(2,1)S(1)}, u32[]{:S(2)}, u32[]{:S(2)}) %collective-permute-start.6) | collective-permute-done | bytes 294944 | tf_op jit(solution)/shard_map/ppermute | solution.py:408
  34.1 1.8 %suffix_far.1 = (bf16[256,576]{1,0:T(8,128)(2,1)S(1)}, bf16[128,640]{1,0:T(8,128)(2,1)S(1)}, bf16[128,640]{1,0:T(8,128)(2,1)S(1)}) custom-call(s32[4]{0:T(128)S(1)} %copy-done.3, s32[16]{0:T(128)S(1)} %copy-done.4, s32[2]{0:T(128)S(1)} %pad_add_fusion.place.refs_2_, bf16[128,576]{1,0:T(8,128)(2,1)S(1)} %collective-permute-done.refs_0_.refs_3_, ...), custom_call_target="tpu_custom_call" | custom-call | tf_op jit(solution)/shard_map/suffix_far/pallas_call | solution.py:412
  36.0 0.5 %collective-permute-start.10 = (bf16[256,576]{1,0:T(8,128)(2,1)S(1)}, bf16[256,576]{1,0:T(8,128)(2,1)S(1)}, u32[]{:S(2)}, u32[]{:S(2)}) collective-permute-start(bf16[256,576]{1,0:T(8,128)(2,1)S(1)} %get-tuple-element.29.refs_5_), channel_id=1, source_target_pairs={{0,4},{4,0},{8,12},{12,8},{1,5},{5,1},{9,13},{13,9},{2,6},{6,2},{1... | collective-permute-start | bytes 884744 | tf_op jit(solution)/shard_map/ppermute | solution.py:428
  36.5 0.1 collective-permute-start.9
  36.6 0.8 %collective-permute-done.7.refs_1_ = bf16[128,640]{1,0:T(8,128)(2,1)S(1)} collective-permute-done((bf16[128,640]{1,0:T(8,128)(2,1)S(1)}, bf16[128,640]{1,0:T(8,128)(2,1)S(1)}, u32[]{:S(2)}, u32[]{:S(2)}) %collective-permute-start.7) | collective-permute-done | bytes 163872 | tf_op jit(solution)/shard_map/ppermute | solution.py:426
  37.4 0.2 chip_merge.1
  37.6 1.6 %collective-permute-start.8 = (bf16[128,640]{1,0:T(8,128)(2,1)S(1)}, bf16[128,640]{1,0:T(8,128)(2,1)S(1)}, u32[]{:S(2)}, u32[]{:S(2)}) collective-permute-start(bf16[128,640]{1,0:T(8,128)(2,1)S(1)} %chip_merge.1), channel_id=1, source_target_pairs={{8,0},{12,4},{0,8},{4,12},{9,1},{13,5},{1,9},{5,13},{10,2},{14,6},... | collective-permute-start | bytes 491528 | tf_op jit(solution)/shard_map/ppermute | solution.py:427
  39.1 1.6 %suffix_near.1 = (bf16[4,64,576]{2,1,0:T(8,128)(2,1)}, bf16[128,640]{1,0:T(8,128)(2,1)S(1)}) custom-call(s32[4]{0:T(128)S(1)} %copy-done.3, s32[16]{0:T(128)S(1)} %copy-done.4, s32[2]{0:T(128)S(1)} %pad_add_fusion.place.refs_2_, bf16[4,576]{1,0:T(4,128)(2,1)S(1)} %copy-done.2, bf16[128,576]{1,0:T(8,128)(2,1)S(1)} %project.1.refs_0_, ...), custom_call_target="tpu_custom_call" | custom-call | tf_op jit(solution)/shard_map/suffix_near/pallas_call | solution.py:432
  40.7 3.1 %collective-permute-done.8.refs_0_ = bf16[128,640]{1,0:T(8,128)(2,1)S(1)} collective-permute-done((bf16[128,640]{1,0:T(8,128)(2,1)S(1)}, bf16[128,640]{1,0:T(8,128)(2,1)S(1)}, u32[]{:S(2)}, u32[]{:S(2)}) %collective-permute-start.8) | collective-permute-done | bytes 163872 | tf_op jit(solution)/shard_map/ppermute | solution.py:427
  43.9 1.3 %final.1 = bf16[4,32,128]{2,1,0:T(8,128)(2,1)} custom-call(bf16[128,640]{1,0:T(8,128)(2,1)S(1)} %collective-permute-done.8.refs_0_, bf16[128,640]{1,0:T(8,128)(2,1)S(1)} %get-tuple-element.30.refs_1_, bf16[32,512,128]{2,1,0:T(8,128)(2,1)S(1)} %copy-done), custom_call_target="tpu_custom_call" | custom-call | tf_op jit(solution)/shard_map/final/pallas_call | solution.py:442
  (20 shorter events, 0.3 us)
Async XLA Ops:
  0.6 1.0 %copy-start.1 = (bf16[4,64,576]{2,1,0:T(8,128)(2,1)S(1)}, bf16[4,64,576]{2,1,0:T(8,128)(2,1)}, u32[]{:S(2)}) copy-start(bf16[4,64,576]{2,1,0:T(8,128)(2,1)} %cache_ref.1) | copy-start | bytes 884740
  1.6 14.7 %copy-start.3 = (s32[4]{0:T(128)S(1)}, s32[4]{0:T(128)}, u32[]{:S(2)}) copy-start(s32[4]{0:T(128)} %anc.1) | copy-start | bytes 52
  1.7 16.1 %collective-permute-start.4 = (bf16[128,1152]{1,0:T(8,128)(2,1)S(1)}, bf16[128,1152]{1,0:T(8,128)(2,1)S(1)}, u32[]{:S(2)}, u32[]{:S(2)}) collective-permute-start(bf16[128,1152]{1,0:T(8,128)(2,1)S(1)} %pack.1.refs_0_.refs_8_), channel_id=1, source_target_pairs={{1,2},{2,1},{5,6},{6,5},{9,10},{10,9},{13,14},{14,13},{17,18},{18,... | collective-permute-start | bytes 884744 | tf_op jit(solution)/shard_map/ppermute | solution.py:354
  2.4 20.5 %collective-permute-start.3 = (bf16[128,1152]{1,0:T(8,128)(2,1)S(1)}, bf16[128,1152]{1,0:T(8,128)(2,1)S(1)}, u32[]{:S(2)}, u32[]{:S(2)}) collective-permute-start(bf16[128,1152]{1,0:T(8,128)(2,1)S(1)} %pack.1.refs_0_.refs_8_), channel_id=1, source_target_pairs={{0,2},{3,1},{4,6},{7,5},{8,10},{11,9},{12,14},{15,13},{16,18},{19,... | collective-permute-start | bytes 884744 | tf_op jit(solution)/shard_map/ppermute | solution.py:356
  14.0 2.3 %collective-permute-start.5 = (bf16[128,576]{1,0:T(8,128)(2,1)S(1)}, bf16[128,576]{1,0:T(8,128)(2,1)S(1)}, u32[]{:S(2)}, u32[]{:S(2)}) collective-permute-start(bf16[128,576]{1,0:T(8,128)(2,1)S(1)} %project.1.refs_0_), channel_id=1, source_target_pairs={{0,4},{4,0},{8,12},{12,8},{1,5},{5,1},{9,13},{13,9},{2,6},{6,2},{1... | collective-permute-start | bytes 442376 | tf_op jit(solution)/shard_map/ppermute | solution.py:387
  14.1 13.8 %collective-permute-start.1 = (bf16[128,576]{1,0:T(8,128)(2,1)S(1)}, bf16[128,576]{1,0:T(8,128)(2,1)S(1)}, u32[]{:S(2)}, u32[]{:S(2)}) collective-permute-start(bf16[128,576]{1,0:T(8,128)(2,1)S(1)} %project.1.refs_0_), channel_id=1, source_target_pairs={{0,12},{4,8},{8,4},{12,0},{1,13},{5,9},{9,5},{13,1},{2,14},{6,10},... | collective-permute-start | bytes 442376 | tf_op jit(solution)/shard_map/ppermute | solution.py:387
  15.7 12.2 %collective-permute-start = (bf16[128,576]{1,0:T(8,128)(2,1)S(1)}, bf16[128,576]{1,0:T(8,128)(2,1)S(1)}, u32[]{:S(2)}, u32[]{:S(2)}) collective-permute-start(bf16[128,576]{1,0:T(8,128)(2,1)S(1)} %project.1.refs_0_), channel_id=1, source_target_pairs={{0,8},{4,12},{8,0},{12,4},{1,9},{5,13},{9,1},{13,5},{2,10},{6,14},... | collective-permute-start | bytes 442376 | tf_op jit(solution)/shard_map/ppermute | solution.py:387
  16.3 6.5 %collective-permute-start.2 = (s32[4]{0:T(128)S(1)}, s32[4]{0:T(128)S(1)}, u32[]{:S(2)}, u32[]{:S(2)}) collective-permute-start(s32[4]{0:T(128)S(1)} %copy-done.3), channel_id=1, source_target_pairs={{0,1},{3,2},{4,5},{7,6},{8,9},{11,10},{12,13},{15,14},{16,17},{19,... | collective-permute-start | bytes 56 | tf_op jit(solution)/shard_map/ppermute | solution.py:357
  23.9 10.1 %copy-start.4 = (s32[16]{0:T(128)S(1)}, s32[16]{0:T(128)}, u32[]{:S(2)}) copy-start(s32[16]{0:T(128)} %lens.1) | copy-start | bytes 196
  23.9 15.2 %copy-start.2 = (bf16[4,576]{1,0:T(4,128)(2,1)S(1)}, bf16[4,576]{1,0:T(4,128)(2,1)}, u32[]{:S(2)}) copy-start(bf16[4,576]{1,0:T(4,128)(2,1)} %fresh_ref.1) | copy-start | bytes 13828
  24.0 10.1 %collective-permute-start.6 = (bf16[128,1152]{1,0:T(8,128)(2,1)S(1)}, bf16[128,1152]{1,0:T(8,128)(2,1)S(1)}, u32[]{:S(2)}, u32[]{:S(2)}) collective-permute-start(bf16[128,1152]{1,0:T(8,128)(2,1)S(1)} %select.1), channel_id=1, source_target_pairs={{0,1},{1,0},{2,3},{3,2},{4,5},{5,4},{6,7},{7,6},{8,9},{9,8},{10,11... | collective-permute-start | bytes 884744 | tf_op jit(solution)/shard_map/ppermute | solution.py:408
  27.9 15.9 %copy-start = (bf16[32,512,128]{2,1,0:T(8,128)(2,1)S(1)}, bf16[32,512,128]{2,1,0:T(8,128)(2,1)}, u32[]{:S(2)}) copy-start(bf16[32,512,128]{2,1,0:T(8,128)(2,1)} %refs_2_.1) | copy-start | bytes 12582916
  35.9 1.5 %collective-permute-start.7 = (bf16[128,640]{1,0:T(8,128)(2,1)S(1)}, bf16[128,640]{1,0:T(8,128)(2,1)S(1)}, u32[]{:S(2)}, u32[]{:S(2)}) collective-permute-start(bf16[128,640]{1,0:T(8,128)(2,1)S(1)} %get-tuple-element.24), channel_id=1, source_target_pairs={{0,4},{4,0},{8,12},{12,8},{1,5},{5,1},{9,13},{13,9},{2,6},{6,2},{1... | collective-permute-start | bytes 491528 | tf_op jit(solution)/shard_map/ppermute | solution.py:426
  36.0 3.2 %collective-permute-start.10 = (bf16[256,576]{1,0:T(8,128)(2,1)S(1)}, bf16[256,576]{1,0:T(8,128)(2,1)S(1)}, u32[]{:S(2)}, u32[]{:S(2)}) collective-permute-start(bf16[256,576]{1,0:T(8,128)(2,1)S(1)} %get-tuple-element.29.refs_5_), channel_id=1, source_target_pairs={{0,4},{4,0},{8,12},{12,8},{1,5},{5,1},{9,13},{13,9},{2,6},{6,2},{1... | collective-permute-start | bytes 884744 | tf_op jit(solution)/shard_map/ppermute | solution.py:428
  36.5 2.7 %collective-permute-start.9 = (bf16[128,640]{1,0:T(8,128)(2,1)S(1)}, bf16[128,640]{1,0:T(8,128)(2,1)S(1)}, u32[]{:S(2)}, u32[]{:S(2)}) collective-permute-start(bf16[128,640]{1,0:T(8,128)(2,1)S(1)} %get-tuple-element.27), channel_id=1, source_target_pairs={{0,4},{4,0},{8,12},{12,8},{1,5},{5,1},{9,13},{13,9},{2,6},{6,2},{1... | collective-permute-start | bytes 491528 | tf_op jit(solution)/shard_map/ppermute | solution.py:396
  37.6 6.3 %collective-permute-start.8 = (bf16[128,640]{1,0:T(8,128)(2,1)S(1)}, bf16[128,640]{1,0:T(8,128)(2,1)S(1)}, u32[]{:S(2)}, u32[]{:S(2)}) collective-permute-start(bf16[128,640]{1,0:T(8,128)(2,1)S(1)} %chip_merge.1), channel_id=1, source_target_pairs={{8,0},{12,4},{0,8},{4,12},{9,1},{13,5},{1,9},{5,13},{10,2},{14,6},... | collective-permute-start | bytes 491528 | tf_op jit(solution)/shard_map/ppermute | solution.py:427

commit v11 on v10

--- a/solution.py
+++ b/solution.py
@@ -385,8 +385,6 @@
 
     routes = [(t, f) for t in range(chips) for f in range(cores)]
     queries = [own if r == (0, 0) else lax.ppermute(own, "seq", pairs(*r)) for r in routes]
-    if line:
-        far, queries[1] = lax.optimization_barrier((far, queries[1]))
     stages = []
     for t in range(chips):
         asked = queries[2 * t : 2 * t + 2]

time: 45.6 us -> 44.1 us (0.967)
  starting transfers between devices: 18.1 us -> 14.2 us
  waiting for transfers between devices: 4.87 us -> 7.38 us
    ppermute x1, starting transfers between devices: 3.98 us -> 0.07 us  [on_device(): blocks = [block, lax.ppermute(chosen, 'dom', swap), middle, far]]
    ppermute x1, waiting for transfers between devices: 0.9 us -> 3.23 us  [on_device(): blocks = [block, lax.ppermute(chosen, 'dom', swap), middle, far]]
  transfers between devices with their start and end apart: 11 -> 11, of which waited for: 3 -> 4; matrix products, arithmetic and copies ran while one was open for 4% -> 4% of each run, Pallas kernels for 35% -> 36%
where the time goes in v11:
time: 44.1 us; the launch traced here: 43.8 us
  Pallas kernels  18.8 us (43%)
  starting transfers between devices  14.2 us (32%)
  waiting for transfers between devices  7.38 us (17%)
  local copies, waits for them, and re-layouts  2.54 us (6%)
  between operations  0.8 us (2%)
    pallas_call x2, Pallas kernels, prefix_attention(): pl.pallas_call(functools.partial(prefix_kernel, len(queries), tiles), out...  10.3 us
    ppermute x1, starting transfers between devices, on_device(): middle = lax.ppermute(block, 'dom', [(0, 2), (3, 1)])  7.64 us
    ppermute x1, waiting for transfers between devices, on_device(): blocks = [block, lax.ppermute(chosen, 'dom', swap), middle, far]  3.23 us
    ppermute x1, waiting for transfers between devices, on_device(): parts = [lax.ppermute(s, 'seq', back(t, 0)) for t, s in enumerate(sums, 1)]  3.17 us
    pallas_call x1, Pallas kernels, on_device(): pl.pallas_call(functools.partial(project_kernel, pieces, local), out_shap...  2.46 us
    ppermute x3, starting transfers between devices, on_device(): lax.ppermute(own, 'seq', pairs(*r))  2.21 us
    pallas_call x1, Pallas kernels, on_device(): pl.pallas_call(functools.partial(far_kernel, others, len(blocks), line),...  1.83 us
    pallas_call x1, Pallas kernels, on_device(): pl.pallas_call(near_kernel, out_shape=[shape(private_caches.shape), part]...  1.59 us
  transfers between devices with their start and end apart: 11, of which 4 were waited for; matrix products, arithmetic and copies ran while one was open for 4% of the time, Pallas kernels for 36%

profile of v11, /device:TPU:0, one launch (start us, length us, event | category | flops | bytes accessed | tf_op | source)
XLA Modules:
  0.0 43.8 jit_solution(6605071251689406204)
XLA Ops:
  0.6 1.0 %copy-done.1 = bf16[4,64,576]{2,1,0:T(8,128)(2,1)S(1)} copy-done((bf16[4,64,576]{2,1,0:T(8,128)(2,1)S(1)}, bf16[4,64,576]{2,1,0:T(8,128)(2,1)}, u32[]{:S(2)}) %copy-start.1) | copy-done | bytes 294936
  1.6 0.1 pack.1.refs_0_.refs_8_
  1.7 0.7 %collective-permute-start.4 = (bf16[128,1152]{1,0:T(8,128)(2,1)S(1)}, bf16[128,1152]{1,0:T(8,128)(2,1)S(1)}, u32[]{:S(2)}, u32[]{:S(2)}) collective-permute-start(bf16[128,1152]{1,0:T(8,128)(2,1)S(1)} %pack.1.refs_0_.refs_8_), channel_id=1, source_target_pairs={{1,2},{2,1},{5,6},{6,5},{9,10},{10,9},{13,14},{14,13},{17,18},{18,... | collective-permute-start | bytes 884744 | tf_op jit(solution)/shard_map/ppermute | solution.py:354
  2.4 7.6 %collective-permute-start.3 = (bf16[128,1152]{1,0:T(8,128)(2,1)S(1)}, bf16[128,1152]{1,0:T(8,128)(2,1)S(1)}, u32[]{:S(2)}, u32[]{:S(2)}) collective-permute-start(bf16[128,1152]{1,0:T(8,128)(2,1)S(1)} %pack.1.refs_0_.refs_8_), channel_id=1, source_target_pairs={{0,2},{3,1},{4,6},{7,5},{8,10},{11,9},{12,14},{15,13},{16,18},{19,... | collective-permute-start | bytes 884744 | tf_op jit(solution)/shard_map/ppermute | solution.py:356
  10.0 0.8 %copy.11 = bf16[32,4,128]{2,1,0:T(4,128)(2,1)S(1)} copy(bf16[32,4,128]{2,0,1:T(8,128)(2,1)} %bitcast.11) | data formatting | bytes 65536 | tf_op jit(solution)/shard_map/transpose | solution.py:351
  10.8 0.8 %copy.12 = bf16[32,4,64]{2,1,0:T(4,128)(2,1)S(1)} copy(bf16[32,4,64]{2,0,1:T(8,128)(2,1)} %bitcast.12) | data formatting | bytes 32768 | tf_op jit(solution)/shard_map/transpose | solution.py:351
  11.6 2.5 %project.1.refs_0_ = bf16[128,576]{1,0:T(8,128)(2,1)S(1)} custom-call(bf16[128,128]{1,0:T(8,128)(2,1)S(1)} %bitcast.7, bf16[128,64]{1,0:T(8,128)(2,1)S(1)} %bitcast.8, bf16[32,128,512]{2,1,0:T(8,128)(2,1)} %w_hbm.1), custom_call_target="tpu_custom_call" | custom-call | tf_op jit(solution)/shard_map/project/pallas_call | solution.py:365
  14.1 1.6 %collective-permute-start.1 = (bf16[128,576]{1,0:T(8,128)(2,1)S(1)}, bf16[128,576]{1,0:T(8,128)(2,1)S(1)}, u32[]{:S(2)}, u32[]{:S(2)}) collective-permute-start(bf16[128,576]{1,0:T(8,128)(2,1)S(1)} %project.1.refs_0_), channel_id=1, source_target_pairs={{0,12},{4,8},{8,4},{12,0},{1,13},{5,9},{9,5},{13,1},{2,14},{6,10},... | collective-permute-start | bytes 442376 | tf_op jit(solution)/shard_map/ppermute | solution.py:387
  15.7 0.5 %collective-permute-start = (bf16[128,576]{1,0:T(8,128)(2,1)S(1)}, bf16[128,576]{1,0:T(8,128)(2,1)S(1)}, u32[]{:S(2)}, u32[]{:S(2)}) collective-permute-start(bf16[128,576]{1,0:T(8,128)(2,1)S(1)} %project.1.refs_0_), channel_id=1, source_target_pairs={{0,8},{4,12},{8,0},{12,4},{1,9},{5,13},{9,1},{13,5},{2,10},{6,14},... | collective-permute-start | bytes 442376 | tf_op jit(solution)/shard_map/ppermute | solution.py:387
  16.3 1.4 %collective-permute-start.2 = (s32[4]{0:T(128)S(1)}, s32[4]{0:T(128)S(1)}, u32[]{:S(2)}, u32[]{:S(2)}) collective-permute-start(s32[4]{0:T(128)S(1)} %copy-done.3), channel_id=1, source_target_pairs={{0,1},{3,2},{4,5},{7,6},{8,9},{11,10},{12,13},{15,14},{16,17},{19,... | collective-permute-start | bytes 56 | tf_op jit(solution)/shard_map/ppermute | solution.py:357
  17.7 5.1 %prefix_attention.3 = (f32[128,512]{1,0:T(8,128)S(1)}, f32[128,128]{1,0:T(8,128)S(1)}, f32[128,128]{1,0:T(8,128)S(1)}, bf16[128,640]{1,0:T(8,128)(2,1)S(1)}) custom-call(bf16[128,576]{1,0:T(8,128)(2,1)S(1)} %project.1.refs_0_, bf16[128,576]{1,0:T(8,128)(2,1)S(1)} %collective-permute-done.5.refs_1_, bf16[576,4096]{1,0:T(8,128)(2,1)} %bitcast.9), custom_call_target="tpu_custom_call" | custom-call | tf_op jit(solution)/shard_map/prefix_attention/pallas_call | solution.py:129
  22.9 1.0 %select.1 = bf16[128,1152]{1,0:T(8,128)(2,1)S(1)} custom-call(s32[4]{0:T(128)S(1)} %collective-permute-done.2.theirs, s32[2]{0:T(128)S(1)} %pad_add_fusion.place.refs_2_, bf16[128,1152]{1,0:T(8,128)(2,1)S(1)} %pack.1.refs_0_.refs_8_, bf16[128,1152]{1,0:T(8,128)(2,1)S(1)} %collective-permute-done.3.refs_1_.refs_10_, ...), custom_call_target="tpu_custom_call" | custom-call | tf_op jit(solution)/shard_map/select/pallas_call | solution.py:396
  24.0 0.2 collective-permute-done.refs_0_.refs_3_
  24.2 5.2 %prefix_attention.2 = (f32[256,512]{1,0:T(8,128)S(1)}, f32[256,128]{1,0:T(8,128)S(1)}, f32[256,128]{1,0:T(8,128)S(1)}) custom-call(bf16[128,576]{1,0:T(8,128)(2,1)S(1)} %collective-permute-done.refs_0_.refs_3_, bf16[128,576]{1,0:T(8,128)(2,1)S(1)} %collective-permute-done.1.refs_1_.refs_4_, bf16[576,4096]{1,0:T(8,128)(2,1)} %bitcast.10), custom_call_target="tpu_custom_call" | custom-call | flops 2281701376 | bytes 4718592 | tf_op jit(solution)/shard_map/prefix_attention/pallas_call | solution.py:129
  29.4 3.2 %collective-permute-done.6.refs_9_ = bf16[128,1152]{1,0:T(8,128)(2,1)S(1)} collective-permute-done((bf16[128,1152]{1,0:T(8,128)(2,1)S(1)}, bf16[128,1152]{1,0:T(8,128)(2,1)S(1)}, u32[]{:S(2)}, u32[]{:S(2)}) %collective-permute-start.6) | collective-permute-done | bytes 294944 | tf_op jit(solution)/shard_map/ppermute | solution.py:406
  32.6 1.8 %suffix_far.1 = (bf16[256,576]{1,0:T(8,128)(2,1)S(1)}, bf16[128,640]{1,0:T(8,128)(2,1)S(1)}, bf16[128,640]{1,0:T(8,128)(2,1)S(1)}) custom-call(s32[4]{0:T(128)S(1)} %copy-done.3, s32[16]{0:T(128)S(1)} %copy-done.4, s32[2]{0:T(128)S(1)} %pad_add_fusion.place.refs_2_, bf16[128,576]{1,0:T(8,128)(2,1)S(1)} %collective-permute-done.refs_0_.refs_3_, ...), custom_call_target="tpu_custom_call" | custom-call | tf_op jit(solution)/shard_map/suffix_far/pallas_call | solution.py:410
  34.5 0.5 %collective-permute-start.10 = (bf16[256,576]{1,0:T(8,128)(2,1)S(1)}, bf16[256,576]{1,0:T(8,128)(2,1)S(1)}, u32[]{:S(2)}, u32[]{:S(2)}) collective-permute-start(bf16[256,576]{1,0:T(8,128)(2,1)S(1)} %get-tuple-element.25.refs_5_), channel_id=1, source_target_pairs={{0,4},{4,0},{8,12},{12,8},{1,5},{5,1},{9,13},{13,9},{2,6},{6,2},{1... | collective-permute-start | bytes 884744 | tf_op jit(solution)/shard_map/ppermute | solution.py:426
  35.0 0.1 collective-permute-start.9
  35.1 0.8 %collective-permute-done.7.refs_1_ = bf16[128,640]{1,0:T(8,128)(2,1)S(1)} collective-permute-done((bf16[128,640]{1,0:T(8,128)(2,1)S(1)}, bf16[128,640]{1,0:T(8,128)(2,1)S(1)}, u32[]{:S(2)}, u32[]{:S(2)}) %collective-permute-start.7) | collective-permute-done | bytes 163872 | tf_op jit(solution)/shard_map/ppermute | solution.py:424
  35.9 0.2 chip_merge.1
  36.1 1.5 %collective-permute-start.8 = (bf16[128,640]{1,0:T(8,128)(2,1)S(1)}, bf16[128,640]{1,0:T(8,128)(2,1)S(1)}, u32[]{:S(2)}, u32[]{:S(2)}) collective-permute-start(bf16[128,640]{1,0:T(8,128)(2,1)S(1)} %chip_merge.1), channel_id=1, source_target_pairs={{8,0},{12,4},{0,8},{4,12},{9,1},{13,5},{1,9},{5,13},{10,2},{14,6},... | collective-permute-start | bytes 491528 | tf_op jit(solution)/shard_map/ppermute | solution.py:425
  37.7 1.6 %suffix_near.1 = (bf16[4,64,576]{2,1,0:T(8,128)(2,1)}, bf16[128,640]{1,0:T(8,128)(2,1)S(1)}) custom-call(s32[4]{0:T(128)S(1)} %copy-done.3, s32[16]{0:T(128)S(1)} %copy-done.4, s32[2]{0:T(128)S(1)} %pad_add_fusion.place.refs_2_, bf16[4,576]{1,0:T(4,128)(2,1)S(1)} %copy-done.2, bf16[128,576]{1,0:T(8,128)(2,1)S(1)} %project.1.refs_0_, ...), custom_call_target="tpu_custom_call" | custom-call | tf_op jit(solution)/shard_map/suffix_near/pallas_call | solution.py:430
  39.3 3.2 %collective-permute-done.8.refs_0_ = bf16[128,640]{1,0:T(8,128)(2,1)S(1)} collective-permute-done((bf16[128,640]{1,0:T(8,128)(2,1)S(1)}, bf16[128,640]{1,0:T(8,128)(2,1)S(1)}, u32[]{:S(2)}, u32[]{:S(2)}) %collective-permute-start.8) | collective-permute-done | bytes 163872 | tf_op jit(solution)/shard_map/ppermute | solution.py:425
  42.4 1.3 %final.1 = bf16[4,32,128]{2,1,0:T(8,128)(2,1)} custom-call(bf16[128,640]{1,0:T(8,128)(2,1)S(1)} %collective-permute-done.8.refs_0_, bf16[128,640]{1,0:T(8,128)(2,1)S(1)} %get-tuple-element.26.refs_1_, bf16[32,512,128]{2,1,0:T(8,128)(2,1)S(1)} %copy-done), custom_call_target="tpu_custom_call" | custom-call | tf_op jit(solution)/shard_map/final/pallas_call | solution.py:440
  (20 shorter events, 0.3 us)
Async XLA Ops:
  0.6 1.0 %copy-start.1 = (bf16[4,64,576]{2,1,0:T(8,128)(2,1)S(1)}, bf16[4,64,576]{2,1,0:T(8,128)(2,1)}, u32[]{:S(2)}) copy-start(bf16[4,64,576]{2,1,0:T(8,128)(2,1)} %cache_ref.1) | copy-start | bytes 884740
  1.6 14.7 %copy-start.3 = (s32[4]{0:T(128)S(1)}, s32[4]{0:T(128)}, u32[]{:S(2)}) copy-start(s32[4]{0:T(128)} %anc.1) | copy-start | bytes 52
  1.7 21.2 %collective-permute-start.4 = (bf16[128,1152]{1,0:T(8,128)(2,1)S(1)}, bf16[128,1152]{1,0:T(8,128)(2,1)S(1)}, u32[]{:S(2)}, u32[]{:S(2)}) collective-permute-start(bf16[128,1152]{1,0:T(8,128)(2,1)S(1)} %pack.1.refs_0_.refs_8_), channel_id=1, source_target_pairs={{1,2},{2,1},{5,6},{6,5},{9,10},{10,9},{13,14},{14,13},{17,18},{18,... | collective-permute-start | bytes 884744 | tf_op jit(solution)/shard_map/ppermute | solution.py:354
  2.4 20.5 %collective-permute-start.3 = (bf16[128,1152]{1,0:T(8,128)(2,1)S(1)}, bf16[128,1152]{1,0:T(8,128)(2,1)S(1)}, u32[]{:S(2)}, u32[]{:S(2)}) collective-permute-start(bf16[128,1152]{1,0:T(8,128)(2,1)S(1)} %pack.1.refs_0_.refs_8_), channel_id=1, source_target_pairs={{0,2},{3,1},{4,6},{7,5},{8,10},{11,9},{12,14},{15,13},{16,18},{19,... | collective-permute-start | bytes 884744 | tf_op jit(solution)/shard_map/ppermute | solution.py:356
  14.0 2.3 %collective-permute-start.5 = (bf16[128,576]{1,0:T(8,128)(2,1)S(1)}, bf16[128,576]{1,0:T(8,128)(2,1)S(1)}, u32[]{:S(2)}, u32[]{:S(2)}) collective-permute-start(bf16[128,576]{1,0:T(8,128)(2,1)S(1)} %project.1.refs_0_), channel_id=1, source_target_pairs={{0,4},{4,0},{8,12},{12,8},{1,5},{5,1},{9,13},{13,9},{2,6},{6,2},{1... | collective-permute-start | bytes 442376 | tf_op jit(solution)/shard_map/ppermute | solution.py:387
  14.1 9.9 %collective-permute-start.1 = (bf16[128,576]{1,0:T(8,128)(2,1)S(1)}, bf16[128,576]{1,0:T(8,128)(2,1)S(1)}, u32[]{:S(2)}, u32[]{:S(2)}) collective-permute-start(bf16[128,576]{1,0:T(8,128)(2,1)S(1)} %project.1.refs_0_), channel_id=1, source_target_pairs={{0,12},{4,8},{8,4},{12,0},{1,13},{5,9},{9,5},{13,1},{2,14},{6,10},... | collective-permute-start | bytes 442376 | tf_op jit(solution)/shard_map/ppermute | solution.py:387
  15.7 8.5 %collective-permute-start = (bf16[128,576]{1,0:T(8,128)(2,1)S(1)}, bf16[128,576]{1,0:T(8,128)(2,1)S(1)}, u32[]{:S(2)}, u32[]{:S(2)}) collective-permute-start(bf16[128,576]{1,0:T(8,128)(2,1)S(1)} %project.1.refs_0_), channel_id=1, source_target_pairs={{0,8},{4,12},{8,0},{12,4},{1,9},{5,13},{9,1},{13,5},{2,10},{6,14},... | collective-permute-start | bytes 442376 | tf_op jit(solution)/shard_map/ppermute | solution.py:387
  16.3 6.5 %collective-permute-start.2 = (s32[4]{0:T(128)S(1)}, s32[4]{0:T(128)S(1)}, u32[]{:S(2)}, u32[]{:S(2)}) collective-permute-start(s32[4]{0:T(128)S(1)} %copy-done.3), channel_id=1, source_target_pairs={{0,1},{3,2},{4,5},{7,6},{8,9},{11,10},{12,13},{15,14},{16,17},{19,... | collective-permute-start | bytes 56 | tf_op jit(solution)/shard_map/ppermute | solution.py:357
  23.9 8.7 %copy-start.4 = (s32[16]{0:T(128)S(1)}, s32[16]{0:T(128)}, u32[]{:S(2)}) copy-start(s32[16]{0:T(128)} %lens.1) | copy-start | bytes 196
  23.9 13.7 %copy-start.2 = (bf16[4,576]{1,0:T(4,128)(2,1)S(1)}, bf16[4,576]{1,0:T(4,128)(2,1)}, u32[]{:S(2)}) copy-start(bf16[4,576]{1,0:T(4,128)(2,1)} %fresh_ref.1) | copy-start | bytes 13828
  24.0 8.7 %collective-permute-start.6 = (bf16[128,1152]{1,0:T(8,128)(2,1)S(1)}, bf16[128,1152]{1,0:T(8,128)(2,1)S(1)}, u32[]{:S(2)}, u32[]{:S(2)}) collective-permute-start(bf16[128,1152]{1,0:T(8,128)(2,1)S(1)} %select.1), channel_id=1, source_target_pairs={{0,1},{1,0},{2,3},{3,2},{4,5},{5,4},{6,7},{7,6},{8,9},{9,8},{10,11... | collective-permute-start | bytes 884744 | tf_op jit(solution)/shard_map/ppermute | solution.py:406
  24.2 18.2 %copy-start = (bf16[32,512,128]{2,1,0:T(8,128)(2,1)S(1)}, bf16[32,512,128]{2,1,0:T(8,128)(2,1)}, u32[]{:S(2)}) copy-start(bf16[32,512,128]{2,1,0:T(8,128)(2,1)} %refs_2_.1) | copy-start | bytes 12582916
  34.5 1.5 %collective-permute-start.7 = (bf16[128,640]{1,0:T(8,128)(2,1)S(1)}, bf16[128,640]{1,0:T(8,128)(2,1)S(1)}, u32[]{:S(2)}, u32[]{:S(2)}) collective-permute-start(bf16[128,640]{1,0:T(8,128)(2,1)S(1)} %get-tuple-element.20), channel_id=1, source_target_pairs={{0,4},{4,0},{8,12},{12,8},{1,5},{5,1},{9,13},{13,9},{2,6},{6,2},{1... | collective-permute-start | bytes 491528 | tf_op jit(solution)/shard_map/ppermute | solution.py:424
  34.5 3.1 %collective-permute-start.10 = (bf16[256,576]{1,0:T(8,128)(2,1)S(1)}, bf16[256,576]{1,0:T(8,128)(2,1)S(1)}, u32[]{:S(2)}, u32[]{:S(2)}) collective-permute-start(bf16[256,576]{1,0:T(8,128)(2,1)S(1)} %get-tuple-element.25.refs_5_), channel_id=1, source_target_pairs={{0,4},{4,0},{8,12},{12,8},{1,5},{5,1},{9,13},{13,9},{2,6},{6,2},{1... | collective-permute-start | bytes 884744 | tf_op jit(solution)/shard_map/ppermute | solution.py:426
  35.0 2.6 %collective-permute-start.9 = (bf16[128,640]{1,0:T(8,128)(2,1)S(1)}, bf16[128,640]{1,0:T(8,128)(2,1)S(1)}, u32[]{:S(2)}, u32[]{:S(2)}) collective-permute-start(bf16[128,640]{1,0:T(8,128)(2,1)S(1)} %get-tuple-element.23), channel_id=1, source_target_pairs={{0,4},{4,0},{8,12},{12,8},{1,5},{5,1},{9,13},{13,9},{2,6},{6,2},{1... | collective-permute-start | bytes 491528 | tf_op jit(solution)/shard_map/ppermute | solution.py:394
  36.1 6.3 %collective-permute-start.8 = (bf16[128,640]{1,0:T(8,128)(2,1)S(1)}, bf16[128,640]{1,0:T(8,128)(2,1)S(1)}, u32[]{:S(2)}, u32[]{:S(2)}) collective-permute-start(bf16[128,640]{1,0:T(8,128)(2,1)S(1)} %chip_merge.1), channel_id=1, source_target_pairs={{8,0},{12,4},{0,8},{4,12},{9,1},{13,5},{1,9},{5,13},{10,2},{14,6},... | collective-permute-start | bytes 491528 | tf_op jit(solution)/shard_map/ppermute | solution.py:425

commit v12 on v11

--- a/solution.py
+++ b/solution.py
@@ -40,9 +40,7 @@
         out_ref[part, 2 * rank :] = jnp.concatenate([first[:, rank:], second[:, rank:]], axis=1)
 
 
-def project_kernel(
-    pieces, local, nope_ref, rope_ref, w_hbm, own_ref, w_ref, sems
-):
+def project_kernel(pieces, local, asked_ref, w_hbm, own_ref, w_ref, sems):
     heads, _, rank = w_ref.shape
     piece = heads // pieces
     fetches = [
@@ -53,8 +51,8 @@
     ]
     for fetch in fetches:
         fetch.start()
-    nope = nope_ref[...].astype(F32)
-    width = nope.shape[1]
+    width = w_ref.shape[1]
+    nope = asked_ref[:, :width].astype(F32)
     first = lax.broadcasted_iota(jnp.int32, (2 * local, width), 0) < local
 
     def pair(h):
@@ -63,7 +61,7 @@
         weights = w_ref[pl.ds(h, 2)].reshape(2 * width, rank)
         return jnp.dot(left.astype(BF16), weights, preferred_element_type=F32)
 
-    own_ref[:, rank:] = rope_ref[...]
+    own_ref[:, rank:] = asked_ref[:, width:]
     for h in range(0, heads, 4):
         if h % piece == 0:
             fetches[h // piece].wait()
@@ -230,7 +228,7 @@
     picks = []
     for p in range(local):
         apart = jnp.bitwise_xor(lax.div(theirs[p], local), place[1])
-        which = jnp.where(at_end(place), 0, jnp.maximum(apart - 1, 0))
+        which = jnp.where(at_end(place) | (apart < 2), 0, 4 - apart)
         picks.append((which, jnp.where(at_end(place), p, lax.rem(theirs[p], local))))
     gather_blocks(block_refs, picks, out_ref, sems)
 
@@ -348,12 +346,12 @@
         compiler_params=PARAMS,
         name="pack",
     )(private_caches)
-    nope_rows, rope_rows = (jnp.swapaxes(q, 0, 1).reshape(rows, -1) for q in (q_nope, q_rope))
+    asked_rows = jnp.swapaxes(jnp.concatenate([q_nope, q_rope], axis=2), 0, 1).reshape(rows, -1)
     line = dom_size == 4
     if line:
-        far = lax.ppermute(block, "dom", [(1, 2), (2, 1)])
         swap = [(0, 1), (1, 0), (2, 3), (3, 2)]
         middle = lax.ppermute(block, "dom", [(0, 2), (3, 1)])
+        far = lax.ppermute(block, "dom", [(1, 2), (2, 1)])
         theirs = lax.ppermute(ancestors, "dom", [(0, 1), (3, 2)])
     else:
         blocks = [block] + [
@@ -365,12 +363,12 @@
     own = pl.pallas_call(
         functools.partial(project_kernel, pieces, local),
         out_shape=shape((rows, width)),
-        in_specs=[VMEM] * 2 + [HBM],
+        in_specs=[VMEM, HBM],
         out_specs=VMEM,
         scratch_shapes=[pltpu.VMEM(w_uk.shape, BF16), pltpu.SemaphoreType.DMA((pieces,))],
         compiler_params=STREAM,
         name="project",
-    )(nope_rows, rope_rows, w_uk)
+    )(asked_rows, w_uk)
     keys = prefix.T
 
     def pairs(turn, flip):
@@ -402,7 +400,7 @@
                 compiler_params=PARAMS,
                 cost_estimate=pl.CostEstimate(flops=0, bytes_accessed=0, transcendentals=0),
                 name="select",
-            )(theirs, place, block, middle, far, stage[3])
+            )(theirs, place, block, far, middle, stage[3])
             blocks = [block, lax.ppermute(chosen, "dom", swap), middle, far]
 
     part = shape((rows, rank + LANES))

time: 44.1 us -> 43.2 us (0.980)
  local copies, waits for them, and re-layouts: 2.54 us -> 1.08 us
  other arithmetic: 0.07 us -> 0.86 us
  waiting for transfers between devices: 7.38 us -> 6.82 us
    ppermute x1, starting transfers between devices: 7.64 us -> 5.95 us  [on_device(): middle = lax.ppermute(block, 'dom', [(0, 2), (3, 1)])]
    ppermute x1, starting transfers between devices: 1.38 us -> 3.06 us  [on_device(): theirs = lax.ppermute(ancestors, 'dom', [(0, 1), (3, 2)])]
    transpose x2 -> x1, local copies, waits for them, and re-layouts: 1.56 us -> 0.05 us  [on_device(): jnp.swapaxes(jnp.concatenate([q_nope, q_rope], axis=2), 0, 1)]
    transpose x0 -> x1, other arithmetic: none -> 0.79 us  [on_device(): jnp.swapaxes(jnp.concatenate([q_nope, q_rope], axis=2), 0, 1)]
  transfers between devices with their start and end apart: 11 -> 11, of which waited for: 4 -> 3; matrix products, arithmetic and copies ran while one was open for 4% -> 2% of each run, Pallas kernels for 36% -> 36%
where the time goes in v12:
time: 43.2 us; the launch traced here: 42.9 us
  Pallas kernels  18.9 us (44%)
  starting transfers between devices  14.5 us (34%)
  waiting for transfers between devices  6.82 us (16%)
  local copies, waits for them, and re-layouts  1.08 us (2%)
  other arithmetic  0.86 us (2%)
  between operations  0.79 us (2%)
    pallas_call x2, Pallas kernels, prefix_attention(): pl.pallas_call(functools.partial(prefix_kernel, len(queries), tiles), out...  10.3 us
    ppermute x1, starting transfers between devices, on_device(): middle = lax.ppermute(block, 'dom', [(0, 2), (3, 1)])  5.95 us
    ppermute x1, waiting for transfers between devices, on_device(): parts = [lax.ppermute(s, 'seq', back(t, 0)) for t, s in enumerate(sums, 1)]  3.15 us
    ppermute x1, starting transfers between devices, on_device(): theirs = lax.ppermute(ancestors, 'dom', [(0, 1), (3, 2)])  3.06 us
    ppermute x1, waiting for transfers between devices, on_device(): blocks = [block, lax.ppermute(chosen, 'dom', swap), middle, far]  2.85 us
    pallas_call x1, Pallas kernels, on_device(): pl.pallas_call(functools.partial(project_kernel, pieces, local), out_shap...  2.46 us
    ppermute x3, starting transfers between devices, on_device(): lax.ppermute(own, 'seq', pairs(*r))  2.21 us
    pallas_call x1, Pallas kernels, on_device(): pl.pallas_call(functools.partial(far_kernel, others, len(blocks), line),...  1.83 us
  transfers between devices with their start and end apart: 11, of which 3 were waited for; matrix products, arithmetic and copies ran while one was open for 2% of the time, Pallas kernels for 36%

profile of v12, /device:TPU:0, one launch (start us, length us, event | category | flops | bytes accessed | tf_op | source)
XLA Modules:
  0.0 42.9 jit_solution(16103121618394374451)
XLA Ops:
  0.6 1.0 %copy-done.1 = bf16[4,64,576]{2,1,0:T(8,128)(2,1)S(1)} copy-done((bf16[4,64,576]{2,1,0:T(8,128)(2,1)S(1)}, bf16[4,64,576]{2,1,0:T(8,128)(2,1)}, u32[]{:S(2)}) %copy-start.1) | copy-done | bytes 294936
  1.6 0.1 pack.1.refs_0_.refs_8_
  1.7 6.0 %collective-permute-start.4 = (bf16[128,1152]{1,0:T(8,128)(2,1)S(1)}, bf16[128,1152]{1,0:T(8,128)(2,1)S(1)}, u32[]{:S(2)}, u32[]{:S(2)}) collective-permute-start(bf16[128,1152]{1,0:T(8,128)(2,1)S(1)} %pack.1.refs_0_.refs_8_), channel_id=1, source_target_pairs={{0,2},{3,1},{4,6},{7,5},{8,10},{11,9},{12,14},{15,13},{16,18},{19,... | collective-permute-start | bytes 884744 | tf_op jit(solution)/shard_map/ppermute | solution.py:353
  7.6 0.7 %collective-permute-start.3 = (bf16[128,1152]{1,0:T(8,128)(2,1)S(1)}, bf16[128,1152]{1,0:T(8,128)(2,1)S(1)}, u32[]{:S(2)}, u32[]{:S(2)}) collective-permute-start(bf16[128,1152]{1,0:T(8,128)(2,1)S(1)} %pack.1.refs_0_.refs_8_), channel_id=1, source_target_pairs={{1,2},{2,1},{5,6},{6,5},{9,10},{10,9},{13,14},{14,13},{17,18},{18,... | collective-permute-start | bytes 884744 | tf_op jit(solution)/shard_map/ppermute | solution.py:354
  8.3 0.8 %maximum_bitcast_fusion = bf16[32,4,192]{2,0,1:T(8,128)(2,1)S(1)} fusion(bf16[4,32,64]{2,1,0:T(8,128)(2,1)} %param.10, bf16[4,32,128]{2,1,0:T(8,128)(2,1)} %param.9), kind=kLoop, calls=%fused_computation | loop fusion | flops 98304 | bytes 98304 | tf_op jit(solution)/shard_map/transpose | solution.py:349
  9.2 2.5 %project.1.refs_0_ = bf16[128,576]{1,0:T(8,128)(2,1)S(1)} custom-call(bf16[128,192]{1,0:T(8,128)(2,1)S(1)} %reshape.7.asked_ref, bf16[32,128,512]{2,1,0:T(8,128)(2,1)} %w_hbm.1), custom_call_target="tpu_custom_call" | custom-call | tf_op jit(solution)/shard_map/project/pallas_call | solution.py:363
  11.8 1.6 %collective-permute-start.1 = (bf16[128,576]{1,0:T(8,128)(2,1)S(1)}, bf16[128,576]{1,0:T(8,128)(2,1)S(1)}, u32[]{:S(2)}, u32[]{:S(2)}) collective-permute-start(bf16[128,576]{1,0:T(8,128)(2,1)S(1)} %project.1.refs_0_), channel_id=1, source_target_pairs={{0,12},{4,8},{8,4},{12,0},{1,13},{5,9},{9,5},{13,1},{2,14},{6,10},... | collective-permute-start | bytes 442376 | tf_op jit(solution)/shard_map/ppermute | solution.py:385
  13.4 0.5 %collective-permute-start = (bf16[128,576]{1,0:T(8,128)(2,1)S(1)}, bf16[128,576]{1,0:T(8,128)(2,1)S(1)}, u32[]{:S(2)}, u32[]{:S(2)}) collective-permute-start(bf16[128,576]{1,0:T(8,128)(2,1)S(1)} %project.1.refs_0_), channel_id=1, source_target_pairs={{0,8},{4,12},{8,0},{12,4},{1,9},{5,13},{9,1},{13,5},{2,10},{6,14},... | collective-permute-start | bytes 442376 | tf_op jit(solution)/shard_map/ppermute | solution.py:385
  13.9 0.1 pad_add_fusion.place.refs_2_
  14.0 3.1 %collective-permute-start.2 = (s32[4]{0:T(128)S(1)}, s32[4]{0:T(128)S(1)}, u32[]{:S(2)}, u32[]{:S(2)}) collective-permute-start(s32[4]{0:T(128)S(1)} %copy-done.3), channel_id=1, source_target_pairs={{0,1},{3,2},{4,5},{7,6},{8,9},{11,10},{12,13},{15,14},{16,17},{19,... | collective-permute-start | bytes 56 | tf_op jit(solution)/shard_map/ppermute | solution.py:355
  17.1 5.1 %prefix_attention.3 = (f32[128,512]{1,0:T(8,128)S(1)}, f32[128,128]{1,0:T(8,128)S(1)}, f32[128,128]{1,0:T(8,128)S(1)}, bf16[128,640]{1,0:T(8,128)(2,1)S(1)}) custom-call(bf16[128,576]{1,0:T(8,128)(2,1)S(1)} %project.1.refs_0_, bf16[128,576]{1,0:T(8,128)(2,1)S(1)} %collective-permute-done.5.refs_1_, bf16[576,4096]{1,0:T(8,128)(2,1)} %bitcast.5), custom_call_target="tpu_custom_call" | custom-call | tf_op jit(solution)/shard_map/prefix_attention/pallas_call | solution.py:127
  22.2 1.0 %select.1 = bf16[128,1152]{1,0:T(8,128)(2,1)S(1)} custom-call(s32[4]{0:T(128)S(1)} %collective-permute-done.2.theirs, s32[2]{0:T(128)S(1)} %pad_add_fusion.place.refs_2_, bf16[128,1152]{1,0:T(8,128)(2,1)S(1)} %pack.1.refs_0_.refs_8_, bf16[128,1152]{1,0:T(8,128)(2,1)S(1)} %collective-permute-done.3.refs_1_.refs_11_, ...), custom_call_target="tpu_custom_call" | custom-call | tf_op jit(solution)/shard_map/select/pallas_call | solution.py:394
  23.3 0.4 collective-permute-start.6
  23.7 5.2 %prefix_attention.2 = (f32[256,512]{1,0:T(8,128)S(1)}, f32[256,128]{1,0:T(8,128)S(1)}, f32[256,128]{1,0:T(8,128)S(1)}) custom-call(bf16[128,576]{1,0:T(8,128)(2,1)S(1)} %collective-permute-done.refs_0_.refs_3_, bf16[128,576]{1,0:T(8,128)(2,1)S(1)} %collective-permute-done.1.refs_1_.refs_4_, bf16[576,4096]{1,0:T(8,128)(2,1)} %bitcast.6), custom_call_target="tpu_custom_call" | custom-call | flops 2281701376 | bytes 4718592 | tf_op jit(solution)/shard_map/prefix_attention/pallas_call | solution.py:127
  28.9 2.8 %collective-permute-done.6.refs_9_ = bf16[128,1152]{1,0:T(8,128)(2,1)S(1)} collective-permute-done((bf16[128,1152]{1,0:T(8,128)(2,1)S(1)}, bf16[128,1152]{1,0:T(8,128)(2,1)S(1)}, u32[]{:S(2)}, u32[]{:S(2)}) %collective-permute-start.6) | collective-permute-done | bytes 294944 | tf_op jit(solution)/shard_map/ppermute | solution.py:404
  31.8 1.8 %suffix_far.1 = (bf16[256,576]{1,0:T(8,128)(2,1)S(1)}, bf16[128,640]{1,0:T(8,128)(2,1)S(1)}, bf16[128,640]{1,0:T(8,128)(2,1)S(1)}) custom-call(s32[4]{0:T(128)S(1)} %copy-done.3, s32[16]{0:T(128)S(1)} %copy-done.4, s32[2]{0:T(128)S(1)} %pad_add_fusion.place.refs_2_, bf16[128,576]{1,0:T(8,128)(2,1)S(1)} %collective-permute-done.refs_0_.refs_3_, ...), custom_call_target="tpu_custom_call" | custom-call | tf_op jit(solution)/shard_map/suffix_far/pallas_call | solution.py:408
  33.7 0.5 %collective-permute-start.10 = (bf16[256,576]{1,0:T(8,128)(2,1)S(1)}, bf16[256,576]{1,0:T(8,128)(2,1)S(1)}, u32[]{:S(2)}, u32[]{:S(2)}) collective-permute-start(bf16[256,576]{1,0:T(8,128)(2,1)S(1)} %get-tuple-element.25.refs_5_), channel_id=1, source_target_pairs={{0,4},{4,0},{8,12},{12,8},{1,5},{5,1},{9,13},{13,9},{2,6},{6,2},{1... | collective-permute-start | bytes 884744 | tf_op jit(solution)/shard_map/ppermute | solution.py:424
  34.2 0.1 collective-permute-start.9
  34.3 0.8 %collective-permute-done.7.refs_1_ = bf16[128,640]{1,0:T(8,128)(2,1)S(1)} collective-permute-done((bf16[128,640]{1,0:T(8,128)(2,1)S(1)}, bf16[128,640]{1,0:T(8,128)(2,1)S(1)}, u32[]{:S(2)}, u32[]{:S(2)}) %collective-permute-start.7) | collective-permute-done | bytes 163872 | tf_op jit(solution)/shard_map/ppermute | solution.py:422
  35.1 0.2 chip_merge.1
  35.3 1.6 %collective-permute-start.8 = (bf16[128,640]{1,0:T(8,128)(2,1)S(1)}, bf16[128,640]{1,0:T(8,128)(2,1)S(1)}, u32[]{:S(2)}, u32[]{:S(2)}) collective-permute-start(bf16[128,640]{1,0:T(8,128)(2,1)S(1)} %chip_merge.1), channel_id=1, source_target_pairs={{8,0},{12,4},{0,8},{4,12},{9,1},{13,5},{1,9},{5,13},{10,2},{14,6},... | collective-permute-start | bytes 491528 | tf_op jit(solution)/shard_map/ppermute | solution.py:423
  36.8 1.6 %suffix_near.1 = (bf16[4,64,576]{2,1,0:T(8,128)(2,1)}, bf16[128,640]{1,0:T(8,128)(2,1)S(1)}) custom-call(s32[4]{0:T(128)S(1)} %copy-done.3, s32[16]{0:T(128)S(1)} %copy-done.4, s32[2]{0:T(128)S(1)} %pad_add_fusion.place.refs_2_, bf16[4,576]{1,0:T(4,128)(2,1)S(1)} %copy-done.2, bf16[128,576]{1,0:T(8,128)(2,1)S(1)} %project.1.refs_0_, ...), custom_call_target="tpu_custom_call" | custom-call | tf_op jit(solution)/shard_map/suffix_near/pallas_call | solution.py:428
  38.4 3.2 %collective-permute-done.8.refs_0_ = bf16[128,640]{1,0:T(8,128)(2,1)S(1)} collective-permute-done((bf16[128,640]{1,0:T(8,128)(2,1)S(1)}, bf16[128,640]{1,0:T(8,128)(2,1)S(1)}, u32[]{:S(2)}, u32[]{:S(2)}) %collective-permute-start.8) | collective-permute-done | bytes 163872 | tf_op jit(solution)/shard_map/ppermute | solution.py:423
  41.6 1.3 %final.1 = bf16[4,32,128]{2,1,0:T(8,128)(2,1)} custom-call(bf16[128,640]{1,0:T(8,128)(2,1)S(1)} %collective-permute-done.8.refs_0_, bf16[128,640]{1,0:T(8,128)(2,1)S(1)} %get-tuple-element.26.refs_1_, bf16[32,512,128]{2,1,0:T(8,128)(2,1)S(1)} %copy-done), custom_call_target="tpu_custom_call" | custom-call | tf_op jit(solution)/shard_map/final/pallas_call | solution.py:438
  (21 shorter events, 0.3 us)
Async XLA Ops:
  0.6 1.0 %copy-start.1 = (bf16[4,64,576]{2,1,0:T(8,128)(2,1)S(1)}, bf16[4,64,576]{2,1,0:T(8,128)(2,1)}, u32[]{:S(2)}) copy-start(bf16[4,64,576]{2,1,0:T(8,128)(2,1)} %cache_ref.1) | copy-start | bytes 884740
  1.6 12.4 %copy-start.3 = (s32[4]{0:T(128)S(1)}, s32[4]{0:T(128)}, u32[]{:S(2)}) copy-start(s32[4]{0:T(128)} %anc.1) | copy-start | bytes 52
  1.7 20.5 %collective-permute-start.4 = (bf16[128,1152]{1,0:T(8,128)(2,1)S(1)}, bf16[128,1152]{1,0:T(8,128)(2,1)S(1)}, u32[]{:S(2)}, u32[]{:S(2)}) collective-permute-start(bf16[128,1152]{1,0:T(8,128)(2,1)S(1)} %pack.1.refs_0_.refs_8_), channel_id=1, source_target_pairs={{0,2},{3,1},{4,6},{7,5},{8,10},{11,9},{12,14},{15,13},{16,18},{19,... | collective-permute-start | bytes 884744 | tf_op jit(solution)/shard_map/ppermute | solution.py:353
  7.6 14.6 %collective-permute-start.3 = (bf16[128,1152]{1,0:T(8,128)(2,1)S(1)}, bf16[128,1152]{1,0:T(8,128)(2,1)S(1)}, u32[]{:S(2)}, u32[]{:S(2)}) collective-permute-start(bf16[128,1152]{1,0:T(8,128)(2,1)S(1)} %pack.1.refs_0_.refs_8_), channel_id=1, source_target_pairs={{1,2},{2,1},{5,6},{6,5},{9,10},{10,9},{13,14},{14,13},{17,18},{18,... | collective-permute-start | bytes 884744 | tf_op jit(solution)/shard_map/ppermute | solution.py:354
  11.7 2.3 %collective-permute-start.5 = (bf16[128,576]{1,0:T(8,128)(2,1)S(1)}, bf16[128,576]{1,0:T(8,128)(2,1)S(1)}, u32[]{:S(2)}, u32[]{:S(2)}) collective-permute-start(bf16[128,576]{1,0:T(8,128)(2,1)S(1)} %project.1.refs_0_), channel_id=1, source_target_pairs={{0,4},{4,0},{8,12},{12,8},{1,5},{5,1},{9,13},{13,9},{2,6},{6,2},{1... | collective-permute-start | bytes 442376 | tf_op jit(solution)/shard_map/ppermute | solution.py:385
  11.8 11.9 %collective-permute-start.1 = (bf16[128,576]{1,0:T(8,128)(2,1)S(1)}, bf16[128,576]{1,0:T(8,128)(2,1)S(1)}, u32[]{:S(2)}, u32[]{:S(2)}) collective-permute-start(bf16[128,576]{1,0:T(8,128)(2,1)S(1)} %project.1.refs_0_), channel_id=1, source_target_pairs={{0,12},{4,8},{8,4},{12,0},{1,13},{5,9},{9,5},{13,1},{2,14},{6,10},... | collective-permute-start | bytes 442376 | tf_op jit(solution)/shard_map/ppermute | solution.py:385
  13.4 10.3 %collective-permute-start = (bf16[128,576]{1,0:T(8,128)(2,1)S(1)}, bf16[128,576]{1,0:T(8,128)(2,1)S(1)}, u32[]{:S(2)}, u32[]{:S(2)}) collective-permute-start(bf16[128,576]{1,0:T(8,128)(2,1)S(1)} %project.1.refs_0_), channel_id=1, source_target_pairs={{0,8},{4,12},{8,0},{12,4},{1,9},{5,13},{9,1},{13,5},{2,10},{6,14},... | collective-permute-start | bytes 442376 | tf_op jit(solution)/shard_map/ppermute | solution.py:385
  14.0 8.2 %collective-permute-start.2 = (s32[4]{0:T(128)S(1)}, s32[4]{0:T(128)S(1)}, u32[]{:S(2)}, u32[]{:S(2)}) collective-permute-start(s32[4]{0:T(128)S(1)} %copy-done.3), channel_id=1, source_target_pairs={{0,1},{3,2},{4,5},{7,6},{8,9},{11,10},{12,13},{15,14},{16,17},{19,... | collective-permute-start | bytes 56 | tf_op jit(solution)/shard_map/ppermute | solution.py:355
  23.3 8.5 %copy-start.4 = (s32[16]{0:T(128)S(1)}, s32[16]{0:T(128)}, u32[]{:S(2)}) copy-start(s32[16]{0:T(128)} %lens.1) | copy-start | bytes 196
  23.3 13.6 %copy-start.2 = (bf16[4,576]{1,0:T(4,128)(2,1)S(1)}, bf16[4,576]{1,0:T(4,128)(2,1)}, u32[]{:S(2)}) copy-start(bf16[4,576]{1,0:T(4,128)(2,1)} %fresh_ref.1) | copy-start | bytes 13828
  23.3 8.5 %collective-permute-start.6 = (bf16[128,1152]{1,0:T(8,128)(2,1)S(1)}, bf16[128,1152]{1,0:T(8,128)(2,1)S(1)}, u32[]{:S(2)}, u32[]{:S(2)}) collective-permute-start(bf16[128,1152]{1,0:T(8,128)(2,1)S(1)} %select.1), channel_id=1, source_target_pairs={{0,1},{1,0},{2,3},{3,2},{4,5},{5,4},{6,7},{7,6},{8,9},{9,8},{10,11... | collective-permute-start | bytes 884744 | tf_op jit(solution)/shard_map/ppermute | solution.py:404
  23.7 17.9 %copy-start = (bf16[32,512,128]{2,1,0:T(8,128)(2,1)S(1)}, bf16[32,512,128]{2,1,0:T(8,128)(2,1)}, u32[]{:S(2)}) copy-start(bf16[32,512,128]{2,1,0:T(8,128)(2,1)} %refs_2_.1) | copy-start | bytes 12582916
  33.6 1.5 %collective-permute-start.7 = (bf16[128,640]{1,0:T(8,128)(2,1)S(1)}, bf16[128,640]{1,0:T(8,128)(2,1)S(1)}, u32[]{:S(2)}, u32[]{:S(2)}) collective-permute-start(bf16[128,640]{1,0:T(8,128)(2,1)S(1)} %get-tuple-element.20), channel_id=1, source_target_pairs={{0,4},{4,0},{8,12},{12,8},{1,5},{5,1},{9,13},{13,9},{2,6},{6,2},{1... | collective-permute-start | bytes 491528 | tf_op jit(solution)/shard_map/ppermute | solution.py:422
  33.7 3.1 %collective-permute-start.10 = (bf16[256,576]{1,0:T(8,128)(2,1)S(1)}, bf16[256,576]{1,0:T(8,128)(2,1)S(1)}, u32[]{:S(2)}, u32[]{:S(2)}) collective-permute-start(bf16[256,576]{1,0:T(8,128)(2,1)S(1)} %get-tuple-element.25.refs_5_), channel_id=1, source_target_pairs={{0,4},{4,0},{8,12},{12,8},{1,5},{5,1},{9,13},{13,9},{2,6},{6,2},{1... | collective-permute-start | bytes 884744 | tf_op jit(solution)/shard_map/ppermute | solution.py:424
  34.2 2.6 %collective-permute-start.9 = (bf16[128,640]{1,0:T(8,128)(2,1)S(1)}, bf16[128,640]{1,0:T(8,128)(2,1)S(1)}, u32[]{:S(2)}, u32[]{:S(2)}) collective-permute-start(bf16[128,640]{1,0:T(8,128)(2,1)S(1)} %get-tuple-element.23), channel_id=1, source_target_pairs={{0,4},{4,0},{8,12},{12,8},{1,5},{5,1},{9,13},{13,9},{2,6},{6,2},{1... | collective-permute-start | bytes 491528 | tf_op jit(solution)/shard_map/ppermute | solution.py:392
  35.3 6.3 %collective-permute-start.8 = (bf16[128,640]{1,0:T(8,128)(2,1)S(1)}, bf16[128,640]{1,0:T(8,128)(2,1)S(1)}, u32[]{:S(2)}, u32[]{:S(2)}) collective-permute-start(bf16[128,640]{1,0:T(8,128)(2,1)S(1)} %chip_merge.1), channel_id=1, source_target_pairs={{8,0},{12,4},{0,8},{4,12},{9,1},{13,5},{1,9},{5,13},{10,2},{14,6},... | collective-permute-start | bytes 491528 | tf_op jit(solution)/shard_map/ppermute | solution.py:423

commit v13 on v12

--- a/solution.py
+++ b/solution.py
@@ -352,7 +352,6 @@
         swap = [(0, 1), (1, 0), (2, 3), (3, 2)]
         middle = lax.ppermute(block, "dom", [(0, 2), (3, 1)])
         far = lax.ppermute(block, "dom", [(1, 2), (2, 1)])
-        theirs = lax.ppermute(ancestors, "dom", [(0, 1), (3, 2)])
     else:
         blocks = [block] + [
             lax.ppermute(block, "dom", [(i, (i + k) % dom_size) for i in range(dom_size)])
@@ -391,6 +390,8 @@
         if t == 0:
             given = lax.ppermute(stage.pop(), "seq", pairs(0, 1))
         if line and t == 0:
+            named, stage[3] = lax.optimization_barrier((ancestors, stage[3]))
+            theirs = lax.ppermute(named, "dom", [(0, 1), (3, 2)])
             chosen = pl.pallas_call(
                 select_kernel,
                 out_shape=shape(block.shape),

time: 43.2 us -> 44.1 us (1.021)
  starting transfers between devices: 14.5 us -> 16.4 us
  waiting for transfers between devices: 6.82 us -> 5.85 us
    ppermute x1, waiting for transfers between devices: 2.85 us -> 0.59 us  [on_device(): blocks = [block, lax.ppermute(chosen, 'dom', swap), middle, far]]
    ppermute x1, starting transfers between devices: 0.41 us -> 2.31 us  [on_device(): blocks = [block, lax.ppermute(chosen, 'dom', swap), middle, far]]
    ppermute x1, waiting for transfers between devices: 0.01 us -> 1.28 us  [on_device(): theirs = lax.ppermute(named, 'dom', [(0, 1), (3, 2)])]
  transfers between devices with their start and end apart: 11 -> 11, of which waited for: 3 -> 4; matrix products, arithmetic and copies ran while one was open for 2% -> 2% of each run, Pallas kernels for 36% -> 36%
where the time goes in v13:
time: 44.1 us; the launch traced here: 43.8 us
  Pallas kernels  18.8 us (43%)
  starting transfers between devices  16.4 us (37%)
  waiting for transfers between devices  5.85 us (13%)
  local copies, waits for them, and re-layouts  1.08 us (2%)
  other arithmetic  0.86 us (2%)
  between operations  0.78 us (2%)
    pallas_call x2, Pallas kernels, prefix_attention(): pl.pallas_call(functools.partial(prefix_kernel, len(queries), tiles), out...  10.3 us
    ppermute x1, starting transfers between devices, on_device(): middle = lax.ppermute(block, 'dom', [(0, 2), (3, 1)])  5.95 us
    ppermute x1, waiting for transfers between devices, on_device(): parts = [lax.ppermute(s, 'seq', back(t, 0)) for t, s in enumerate(sums, 1)]  3.16 us
    ppermute x1, starting transfers between devices, on_device(): theirs = lax.ppermute(named, 'dom', [(0, 1), (3, 2)])  3.06 us
    pallas_call x1, Pallas kernels, on_device(): pl.pallas_call(functools.partial(project_kernel, pieces, local), out_shap...  2.46 us
    ppermute x1, starting transfers between devices, on_device(): blocks = [block, lax.ppermute(chosen, 'dom', swap), middle, far]  2.31 us
    ppermute x3, starting transfers between devices, on_device(): lax.ppermute(own, 'seq', pairs(*r))  2.21 us
    pallas_call x1, Pallas kernels, on_device(): pl.pallas_call(functools.partial(far_kernel, others, len(blocks), line),...  1.82 us
  transfers between devices with their start and end apart: 11, of which 4 were waited for; matrix products, arithmetic and copies ran while one was open for 2% of the time, Pallas kernels for 36%

profile of v13, /device:TPU:0, one launch (start us, length us, event | category | flops | bytes accessed | tf_op | source)
XLA Modules:
  0.0 43.8 jit_solution(15782327558365190849)
XLA Ops:
  0.6 1.0 %copy-done.1 = bf16[4,64,576]{2,1,0:T(8,128)(2,1)S(1)} copy-done((bf16[4,64,576]{2,1,0:T(8,128)(2,1)S(1)}, bf16[4,64,576]{2,1,0:T(8,128)(2,1)}, u32[]{:S(2)}) %copy-start.1) | copy-done | bytes 294936
  1.6 0.1 pack.1.refs_0_.refs_8_
  1.7 6.0 %collective-permute-start.5 = (bf16[128,1152]{1,0:T(8,128)(2,1)S(1)}, bf16[128,1152]{1,0:T(8,128)(2,1)S(1)}, u32[]{:S(2)}, u32[]{:S(2)}) collective-permute-start(bf16[128,1152]{1,0:T(8,128)(2,1)S(1)} %pack.1.refs_0_.refs_8_), channel_id=1, source_target_pairs={{0,2},{3,1},{4,6},{7,5},{8,10},{11,9},{12,14},{15,13},{16,18},{19,... | collective-permute-start | bytes 884744 | tf_op jit(solution)/shard_map/ppermute | solution.py:353
  7.6 0.7 %collective-permute-start.4 = (bf16[128,1152]{1,0:T(8,128)(2,1)S(1)}, bf16[128,1152]{1,0:T(8,128)(2,1)S(1)}, u32[]{:S(2)}, u32[]{:S(2)}) collective-permute-start(bf16[128,1152]{1,0:T(8,128)(2,1)S(1)} %pack.1.refs_0_.refs_8_), channel_id=1, source_target_pairs={{1,2},{2,1},{5,6},{6,5},{9,10},{10,9},{13,14},{14,13},{17,18},{18,... | collective-permute-start | bytes 884744 | tf_op jit(solution)/shard_map/ppermute | solution.py:354
  8.3 0.8 %maximum_bitcast_fusion = bf16[32,4,192]{2,0,1:T(8,128)(2,1)S(1)} fusion(bf16[4,32,64]{2,1,0:T(8,128)(2,1)} %param.10, bf16[4,32,128]{2,1,0:T(8,128)(2,1)} %param.9), kind=kLoop, calls=%fused_computation | loop fusion | flops 98304 | bytes 98304 | tf_op jit(solution)/shard_map/transpose | solution.py:349
  9.2 2.5 %project.1.refs_0_ = bf16[128,576]{1,0:T(8,128)(2,1)S(1)} custom-call(bf16[128,192]{1,0:T(8,128)(2,1)S(1)} %reshape.7.asked_ref, bf16[32,128,512]{2,1,0:T(8,128)(2,1)} %w_hbm.1), custom_call_target="tpu_custom_call" | custom-call | tf_op jit(solution)/shard_map/project/pallas_call | solution.py:362
  11.8 1.6 %collective-permute-start.1 = (bf16[128,576]{1,0:T(8,128)(2,1)S(1)}, bf16[128,576]{1,0:T(8,128)(2,1)S(1)}, u32[]{:S(2)}, u32[]{:S(2)}) collective-permute-start(bf16[128,576]{1,0:T(8,128)(2,1)S(1)} %project.1.refs_0_), channel_id=1, source_target_pairs={{0,12},{4,8},{8,4},{12,0},{1,13},{5,9},{9,5},{13,1},{2,14},{6,10},... | collective-permute-start | bytes 442376 | tf_op jit(solution)/shard_map/ppermute | solution.py:384
  13.4 0.5 %collective-permute-start = (bf16[128,576]{1,0:T(8,128)(2,1)S(1)}, bf16[128,576]{1,0:T(8,128)(2,1)S(1)}, u32[]{:S(2)}, u32[]{:S(2)}) collective-permute-start(bf16[128,576]{1,0:T(8,128)(2,1)S(1)} %project.1.refs_0_), channel_id=1, source_target_pairs={{0,8},{4,12},{8,0},{12,4},{1,9},{5,13},{9,1},{13,5},{2,10},{6,14},... | collective-permute-start | bytes 442376 | tf_op jit(solution)/shard_map/ppermute | solution.py:384
  14.0 5.1 %prefix_attention.3 = (f32[128,512]{1,0:T(8,128)S(1)}, f32[128,128]{1,0:T(8,128)S(1)}, f32[128,128]{1,0:T(8,128)S(1)}, bf16[128,640]{1,0:T(8,128)(2,1)S(1)}) custom-call(bf16[128,576]{1,0:T(8,128)(2,1)S(1)} %project.1.refs_0_, bf16[128,576]{1,0:T(8,128)(2,1)S(1)} %collective-permute-done.2.refs_1_, bf16[576,4096]{1,0:T(8,128)(2,1)} %bitcast.5), custom_call_target="tpu_custom_call" | custom-call | tf_op jit(solution)/shard_map/prefix_attention/pallas_call | solution.py:127
  19.1 3.1 %collective-permute-start.3 = (s32[4]{0:T(128)S(1)}, s32[4]{0:T(128)S(1)}, u32[]{:S(2)}, u32[]{:S(2)}) collective-permute-start(s32[4]{0:T(128)S(1)} %copy-done.3), channel_id=1, source_target_pairs={{0,1},{3,2},{4,5},{7,6},{8,9},{11,10},{12,13},{15,14},{16,17},{19,... | collective-permute-start | bytes 56 | tf_op jit(solution)/shard_map/ppermute | solution.py:394
  22.2 1.3 %collective-permute-done.3.theirs = s32[4]{0:T(128)S(1)} collective-permute-done((s32[4]{0:T(128)S(1)}, s32[4]{0:T(128)S(1)}, u32[]{:S(2)}, u32[]{:S(2)}) %collective-permute-start.3) | collective-permute-done | bytes 48 | tf_op jit(solution)/shard_map/ppermute | solution.py:394
  23.5 1.0 %select.1 = bf16[128,1152]{1,0:T(8,128)(2,1)S(1)} custom-call(s32[4]{0:T(128)S(1)} %collective-permute-done.3.theirs, s32[2]{0:T(128)S(1)} %pad_add_fusion.place.refs_2_, bf16[128,1152]{1,0:T(8,128)(2,1)S(1)} %pack.1.refs_0_.refs_8_, bf16[128,1152]{1,0:T(8,128)(2,1)S(1)} %collective-permute-done.4.refs_1_.refs_11_, ...), custom_call_target="tpu_custom_call" | custom-call | tf_op jit(solution)/shard_map/select/pallas_call | solution.py:395
  24.6 2.3 %collective-permute-start.6 = (bf16[128,1152]{1,0:T(8,128)(2,1)S(1)}, bf16[128,1152]{1,0:T(8,128)(2,1)S(1)}, u32[]{:S(2)}, u32[]{:S(2)}) collective-permute-start(bf16[128,1152]{1,0:T(8,128)(2,1)S(1)} %select.1), channel_id=1, source_target_pairs={{0,1},{1,0},{2,3},{3,2},{4,5},{5,4},{6,7},{7,6},{8,9},{9,8},{10,11... | collective-permute-start | bytes 884744 | tf_op jit(solution)/shard_map/ppermute | solution.py:405
  26.9 5.2 %prefix_attention.2 = (f32[256,512]{1,0:T(8,128)S(1)}, f32[256,128]{1,0:T(8,128)S(1)}, f32[256,128]{1,0:T(8,128)S(1)}) custom-call(bf16[128,576]{1,0:T(8,128)(2,1)S(1)} %collective-permute-done.refs_0_.refs_3_, bf16[128,576]{1,0:T(8,128)(2,1)S(1)} %collective-permute-done.1.refs_1_.refs_4_, bf16[576,4096]{1,0:T(8,128)(2,1)} %bitcast.6), custom_call_target="tpu_custom_call" | custom-call | flops 2281701376 | bytes 4718592 | tf_op jit(solution)/shard_map/prefix_attention/pallas_call | solution.py:127
  32.1 0.6 %collective-permute-done.6.refs_9_ = bf16[128,1152]{1,0:T(8,128)(2,1)S(1)} collective-permute-done((bf16[128,1152]{1,0:T(8,128)(2,1)S(1)}, bf16[128,1152]{1,0:T(8,128)(2,1)S(1)}, u32[]{:S(2)}, u32[]{:S(2)}) %collective-permute-start.6) | collective-permute-done | bytes 294944 | tf_op jit(solution)/shard_map/ppermute | solution.py:405
  32.7 1.8 %suffix_far.1 = (bf16[256,576]{1,0:T(8,128)(2,1)S(1)}, bf16[128,640]{1,0:T(8,128)(2,1)S(1)}, bf16[128,640]{1,0:T(8,128)(2,1)S(1)}) custom-call(s32[4]{0:T(128)S(1)} %copy-done.3, s32[16]{0:T(128)S(1)} %copy-done.4, s32[2]{0:T(128)S(1)} %pad_add_fusion.place.refs_2_, bf16[128,576]{1,0:T(8,128)(2,1)S(1)} %collective-permute-done.refs_0_.refs_3_, ...), custom_call_target="tpu_custom_call" | custom-call | tf_op jit(solution)/shard_map/suffix_far/pallas_call | solution.py:409
  34.6 0.5 %collective-permute-start.10 = (bf16[256,576]{1,0:T(8,128)(2,1)S(1)}, bf16[256,576]{1,0:T(8,128)(2,1)S(1)}, u32[]{:S(2)}, u32[]{:S(2)}) collective-permute-start(bf16[256,576]{1,0:T(8,128)(2,1)S(1)} %get-tuple-element.29.refs_5_), channel_id=1, source_target_pairs={{0,4},{4,0},{8,12},{12,8},{1,5},{5,1},{9,13},{13,9},{2,6},{6,2},{1... | collective-permute-start | bytes 884744 | tf_op jit(solution)/shard_map/ppermute | solution.py:425
  35.1 0.1 collective-permute-start.9
  35.2 0.8 %collective-permute-done.7.refs_1_ = bf16[128,640]{1,0:T(8,128)(2,1)S(1)} collective-permute-done((bf16[128,640]{1,0:T(8,128)(2,1)S(1)}, bf16[128,640]{1,0:T(8,128)(2,1)S(1)}, u32[]{:S(2)}, u32[]{:S(2)}) %collective-permute-start.7) | collective-permute-done | bytes 163872 | tf_op jit(solution)/shard_map/ppermute | solution.py:423
  36.0 0.2 chip_merge.1
  36.2 1.6 %collective-permute-start.8 = (bf16[128,640]{1,0:T(8,128)(2,1)S(1)}, bf16[128,640]{1,0:T(8,128)(2,1)S(1)}, u32[]{:S(2)}, u32[]{:S(2)}) collective-permute-start(bf16[128,640]{1,0:T(8,128)(2,1)S(1)} %chip_merge.1), channel_id=1, source_target_pairs={{8,0},{12,4},{0,8},{4,12},{9,1},{13,5},{1,9},{5,13},{10,2},{14,6},... | collective-permute-start | bytes 491528 | tf_op jit(solution)/shard_map/ppermute | solution.py:424
  37.7 1.6 %suffix_near.1 = (bf16[4,64,576]{2,1,0:T(8,128)(2,1)}, bf16[128,640]{1,0:T(8,128)(2,1)S(1)}) custom-call(s32[4]{0:T(128)S(1)} %copy-done.3, s32[16]{0:T(128)S(1)} %copy-done.4, s32[2]{0:T(128)S(1)} %pad_add_fusion.place.refs_2_, bf16[4,576]{1,0:T(4,128)(2,1)S(1)} %copy-done.2, bf16[128,576]{1,0:T(8,128)(2,1)S(1)} %project.1.refs_0_, ...), custom_call_target="tpu_custom_call" | custom-call | tf_op jit(solution)/shard_map/suffix_near/pallas_call | solution.py:429
  39.3 3.2 %collective-permute-done.8.refs_0_ = bf16[128,640]{1,0:T(8,128)(2,1)S(1)} collective-permute-done((bf16[128,640]{1,0:T(8,128)(2,1)S(1)}, bf16[128,640]{1,0:T(8,128)(2,1)S(1)}, u32[]{:S(2)}, u32[]{:S(2)}) %collective-permute-start.8) | collective-permute-done | bytes 163872 | tf_op jit(solution)/shard_map/ppermute | solution.py:424
  42.5 1.3 %final.1 = bf16[4,32,128]{2,1,0:T(8,128)(2,1)} custom-call(bf16[128,640]{1,0:T(8,128)(2,1)S(1)} %collective-permute-done.8.refs_0_, bf16[128,640]{1,0:T(8,128)(2,1)S(1)} %get-tuple-element.30.refs_1_, bf16[32,512,128]{2,1,0:T(8,128)(2,1)S(1)} %copy-done), custom_call_target="tpu_custom_call" | custom-call | tf_op jit(solution)/shard_map/final/pallas_call | solution.py:439
  (21 shorter events, 0.4 us)
Async XLA Ops:
  0.6 1.0 %copy-start.1 = (bf16[4,64,576]{2,1,0:T(8,128)(2,1)S(1)}, bf16[4,64,576]{2,1,0:T(8,128)(2,1)}, u32[]{:S(2)}) copy-start(bf16[4,64,576]{2,1,0:T(8,128)(2,1)} %cache_ref.1) | copy-start | bytes 884740
  1.7 21.8 %collective-permute-start.5 = (bf16[128,1152]{1,0:T(8,128)(2,1)S(1)}, bf16[128,1152]{1,0:T(8,128)(2,1)S(1)}, u32[]{:S(2)}, u32[]{:S(2)}) collective-permute-start(bf16[128,1152]{1,0:T(8,128)(2,1)S(1)} %pack.1.refs_0_.refs_8_), channel_id=1, source_target_pairs={{0,2},{3,1},{4,6},{7,5},{8,10},{11,9},{12,14},{15,13},{16,18},{19,... | collective-permute-start | bytes 884744 | tf_op jit(solution)/shard_map/ppermute | solution.py:353
  7.6 15.8 %collective-permute-start.4 = (bf16[128,1152]{1,0:T(8,128)(2,1)S(1)}, bf16[128,1152]{1,0:T(8,128)(2,1)S(1)}, u32[]{:S(2)}, u32[]{:S(2)}) collective-permute-start(bf16[128,1152]{1,0:T(8,128)(2,1)S(1)} %pack.1.refs_0_.refs_8_), channel_id=1, source_target_pairs={{1,2},{2,1},{5,6},{6,5},{9,10},{10,9},{13,14},{14,13},{17,18},{18,... | collective-permute-start | bytes 884744 | tf_op jit(solution)/shard_map/ppermute | solution.py:354
  9.2 9.9 %copy-start.3 = (s32[4]{0:T(128)S(1)}, s32[4]{0:T(128)}, u32[]{:S(2)}) copy-start(s32[4]{0:T(128)} %anc.1) | copy-start | bytes 52
  11.7 2.3 %collective-permute-start.2 = (bf16[128,576]{1,0:T(8,128)(2,1)S(1)}, bf16[128,576]{1,0:T(8,128)(2,1)S(1)}, u32[]{:S(2)}, u32[]{:S(2)}) collective-permute-start(bf16[128,576]{1,0:T(8,128)(2,1)S(1)} %project.1.refs_0_), channel_id=1, source_target_pairs={{0,4},{4,0},{8,12},{12,8},{1,5},{5,1},{9,13},{13,9},{2,6},{6,2},{1... | collective-permute-start | bytes 442376 | tf_op jit(solution)/shard_map/ppermute | solution.py:384
  11.8 15.1 %collective-permute-start.1 = (bf16[128,576]{1,0:T(8,128)(2,1)S(1)}, bf16[128,576]{1,0:T(8,128)(2,1)S(1)}, u32[]{:S(2)}, u32[]{:S(2)}) collective-permute-start(bf16[128,576]{1,0:T(8,128)(2,1)S(1)} %project.1.refs_0_), channel_id=1, source_target_pairs={{0,12},{4,8},{8,4},{12,0},{1,13},{5,9},{9,5},{13,1},{2,14},{6,10},... | collective-permute-start | bytes 442376 | tf_op jit(solution)/shard_map/ppermute | solution.py:384
  13.4 13.5 %collective-permute-start = (bf16[128,576]{1,0:T(8,128)(2,1)S(1)}, bf16[128,576]{1,0:T(8,128)(2,1)S(1)}, u32[]{:S(2)}, u32[]{:S(2)}) collective-permute-start(bf16[128,576]{1,0:T(8,128)(2,1)S(1)} %project.1.refs_0_), channel_id=1, source_target_pairs={{0,8},{4,12},{8,0},{12,4},{1,9},{5,13},{9,1},{13,5},{2,10},{6,14},... | collective-permute-start | bytes 442376 | tf_op jit(solution)/shard_map/ppermute | solution.py:384
  19.1 4.3 %collective-permute-start.3 = (s32[4]{0:T(128)S(1)}, s32[4]{0:T(128)S(1)}, u32[]{:S(2)}, u32[]{:S(2)}) collective-permute-start(s32[4]{0:T(128)S(1)} %copy-done.3), channel_id=1, source_target_pairs={{0,1},{3,2},{4,5},{7,6},{8,9},{11,10},{12,13},{15,14},{16,17},{19,... | collective-permute-start | bytes 56 | tf_op jit(solution)/shard_map/ppermute | solution.py:394
  24.5 8.1 %copy-start.4 = (s32[16]{0:T(128)S(1)}, s32[16]{0:T(128)}, u32[]{:S(2)}) copy-start(s32[16]{0:T(128)} %lens.1) | copy-start | bytes 196
  24.5 13.2 %copy-start.2 = (bf16[4,576]{1,0:T(4,128)(2,1)S(1)}, bf16[4,576]{1,0:T(4,128)(2,1)}, u32[]{:S(2)}) copy-start(bf16[4,576]{1,0:T(4,128)(2,1)} %fresh_ref.1) | copy-start | bytes 13828
  24.6 8.1 %collective-permute-start.6 = (bf16[128,1152]{1,0:T(8,128)(2,1)S(1)}, bf16[128,1152]{1,0:T(8,128)(2,1)S(1)}, u32[]{:S(2)}, u32[]{:S(2)}) collective-permute-start(bf16[128,1152]{1,0:T(8,128)(2,1)S(1)} %select.1), channel_id=1, source_target_pairs={{0,1},{1,0},{2,3},{3,2},{4,5},{5,4},{6,7},{7,6},{8,9},{9,8},{10,11... | collective-permute-start | bytes 884744 | tf_op jit(solution)/shard_map/ppermute | solution.py:405
  26.9 15.6 %copy-start = (bf16[32,512,128]{2,1,0:T(8,128)(2,1)S(1)}, bf16[32,512,128]{2,1,0:T(8,128)(2,1)}, u32[]{:S(2)}) copy-start(bf16[32,512,128]{2,1,0:T(8,128)(2,1)} %refs_2_.1) | copy-start | bytes 12582916
  34.5 1.5 %collective-permute-start.7 = (bf16[128,640]{1,0:T(8,128)(2,1)S(1)}, bf16[128,640]{1,0:T(8,128)(2,1)S(1)}, u32[]{:S(2)}, u32[]{:S(2)}) collective-permute-start(bf16[128,640]{1,0:T(8,128)(2,1)S(1)} %get-tuple-element.24), channel_id=1, source_target_pairs={{0,4},{4,0},{8,12},{12,8},{1,5},{5,1},{9,13},{13,9},{2,6},{6,2},{1... | collective-permute-start | bytes 491528 | tf_op jit(solution)/shard_map/ppermute | solution.py:423
  34.6 3.1 %collective-permute-start.10 = (bf16[256,576]{1,0:T(8,128)(2,1)S(1)}, bf16[256,576]{1,0:T(8,128)(2,1)S(1)}, u32[]{:S(2)}, u32[]{:S(2)}) collective-permute-start(bf16[256,576]{1,0:T(8,128)(2,1)S(1)} %get-tuple-element.29.refs_5_), channel_id=1, source_target_pairs={{0,4},{4,0},{8,12},{12,8},{1,5},{5,1},{9,13},{13,9},{2,6},{6,2},{1... | collective-permute-start | bytes 884744 | tf_op jit(solution)/shard_map/ppermute | solution.py:425
  35.1 2.6 %collective-permute-start.9 = (bf16[128,640]{1,0:T(8,128)(2,1)S(1)}, bf16[128,640]{1,0:T(8,128)(2,1)S(1)}, u32[]{:S(2)}, u32[]{:S(2)}) collective-permute-start(bf16[128,640]{1,0:T(8,128)(2,1)S(1)} %get-tuple-element.27), channel_id=1, source_target_pairs={{0,4},{4,0},{8,12},{12,8},{1,5},{5,1},{9,13},{13,9},{2,6},{6,2},{1... | collective-permute-start | bytes 491528 | tf_op jit(solution)/shard_map/ppermute | solution.py:391
  36.2 6.3 %collective-permute-start.8 = (bf16[128,640]{1,0:T(8,128)(2,1)S(1)}, bf16[128,640]{1,0:T(8,128)(2,1)S(1)}, u32[]{:S(2)}, u32[]{:S(2)}) collective-permute-start(bf16[128,640]{1,0:T(8,128)(2,1)S(1)} %chip_merge.1), channel_id=1, source_target_pairs={{8,0},{12,4},{0,8},{4,12},{9,1},{13,5},{1,9},{5,13},{10,2},{14,6},... | collective-permute-start | bytes 491528 | tf_op jit(solution)/shard_map/ppermute | solution.py:424

commit v14 on v12

--- a/solution.py
+++ b/solution.py
@@ -22,7 +22,8 @@
 ANY = pl.BlockSpec(memory_space=pl.ANY)
 HBM = pl.BlockSpec(memory_space=pltpu.HBM)
 PARAMS = pltpu.CompilerParams(vmem_limit_bytes=40 * 1024 * 1024)
-STREAM = pltpu.CompilerParams(vmem_limit_bytes=51 * 1024 * 1024)
+PACK = 8_000_000_000
+PROJECT = 8_000_000_000
 
 
 def shape(dims, dtype=BF16):
@@ -40,17 +41,8 @@
         out_ref[part, 2 * rank :] = jnp.concatenate([first[:, rank:], second[:, rank:]], axis=1)
 
 
-def project_kernel(pieces, local, asked_ref, w_hbm, own_ref, w_ref, sems):
+def project_kernel(local, asked_ref, w_ref, own_ref):
     heads, _, rank = w_ref.shape
-    piece = heads // pieces
-    fetches = [
-        pltpu.make_async_copy(
-            w_hbm.at[pl.ds(i * piece, piece)], w_ref.at[pl.ds(i * piece, piece)], sems.at[i]
-        )
-        for i in range(pieces)
-    ]
-    for fetch in fetches:
-        fetch.start()
     width = w_ref.shape[1]
     nope = asked_ref[:, :width].astype(F32)
     first = lax.broadcasted_iota(jnp.int32, (2 * local, width), 0) < local
@@ -63,8 +55,6 @@
 
     own_ref[:, rank:] = asked_ref[:, width:]
     for h in range(0, heads, 4):
-        if h % piece == 0:
-            fetches[h // piece].wait()
         own_ref[pl.ds(h * local, 4 * local), :rank] = jnp.concatenate(
             [pair(i) for i in (h, h + 2)], axis=0
         ).astype(BF16)
@@ -72,20 +62,13 @@
 
 def prefix_kernel(count, tiles, *refs):
     query_refs = refs[:count]
-    keys_hbm, out_ref, max_ref, sum_ref, *give_ref, acc_ref, keys_ref, sems = refs[count:]
+    keys_ref, out_ref, max_ref, sum_ref, *give_ref, acc_ref = refs[count:]
     rank = acc_ref.shape[1]
     tile = keys_ref.shape[1] // tiles
     parts = [pl.ds(i * tile, tile) for i in range(tiles)]
-    fetches = [
-        pltpu.make_async_copy(keys_hbm.at[:, part], keys_ref.at[:, part], sems.at[i])
-        for i, part in enumerate(parts)
-    ]
-    for fetch in fetches:
-        fetch.start()
     queries = jnp.concatenate([ref[...] for ref in query_refs], axis=0)
 
     def score(i):
-        fetches[i].wait()
         return jnp.dot(queries, keys_ref[:, parts[i]], preferred_element_type=F32) * SCALE2
 
     ahead = score(0)
@@ -127,14 +110,10 @@
     return pl.pallas_call(
         functools.partial(prefix_kernel, len(queries), tiles),
         out_shape=out,
-        in_specs=[VMEM] * len(queries) + [HBM],
+        in_specs=[VMEM] * (len(queries) + 1),
         out_specs=[VMEM] * len(out),
-        scratch_shapes=[
-            pltpu.VMEM((rows, rank), F32),
-            pltpu.VMEM(keys.shape, BF16),
-            pltpu.SemaphoreType.DMA((tiles,)),
-        ],
-        compiler_params=STREAM,
+        scratch_shapes=[pltpu.VMEM((rows, rank), F32)],
+        compiler_params=PARAMS,
         cost_estimate=pl.CostEstimate(
             flops=0 if give else 2 * rows * length * (width + rank),
             bytes_accessed=0 if give else 2 * width * length,
@@ -344,6 +323,7 @@
         in_specs=[VMEM],
         out_specs=VMEM,
         compiler_params=PARAMS,
+        cost_estimate=pl.CostEstimate(flops=PACK, bytes_accessed=0, transcendentals=0),
         name="pack",
     )(private_caches)
     asked_rows = jnp.swapaxes(jnp.concatenate([q_nope, q_rope], axis=2), 0, 1).reshape(rows, -1)
@@ -359,14 +339,13 @@
             for k in range(1, dom_size)
         ]
 
-    pieces = math.gcd(heads // 4, 4)
     own = pl.pallas_call(
-        functools.partial(project_kernel, pieces, local),
+        functools.partial(project_kernel, local),
         out_shape=shape((rows, width)),
-        in_specs=[VMEM, HBM],
+        in_specs=[VMEM] * 2,
         out_specs=VMEM,
-        scratch_shapes=[pltpu.VMEM(w_uk.shape, BF16), pltpu.SemaphoreType.DMA((pieces,))],
-        compiler_params=STREAM,
+        compiler_params=PARAMS,
+        cost_estimate=pl.CostEstimate(flops=PROJECT, bytes_accessed=0, transcendentals=0),
         name="project",
     )(asked_rows, w_uk)
     keys = prefix.T

time: 43.2 us -> 43.4 us (level)
  local copies, waits for them, and re-layouts: 1.08 us -> 7.94 us
  Pallas kernels: 18.9 us -> 13.3 us
  other arithmetic: 0.86 us -> 0.09 us
    unnamed x10 -> x20, local copies, waits for them, and re-layouts: 0.99 us -> 7.84 us
    pallas_call x2, Pallas kernels: 10.3 us -> 6.57 us  [prefix_attention(): pl.pallas_call(functools.partial(prefix_kernel, len(queries), tiles), out...]
    pallas_call x1, Pallas kernels: 2.46 us -> 0.64 us  [on_device(): pl.pallas_call(functools.partial(project_kernel, local), out_shape=shape(...]
    transpose x1, other arithmetic: 0.79 us -> 0.01 us  [on_device(): jnp.swapaxes(jnp.concatenate([q_nope, q_rope], axis=2), 0, 1)]
  transfers between devices with their start and end apart: 11 -> 11, of which waited for: 3 -> 3; matrix products, arithmetic and copies ran while one was open for 2% -> 0% of each run, Pallas kernels for 36% -> 23%
where the time goes in v14:
time: 43.4 us; the launch traced here: 43 us
  starting transfers between devices  14.3 us (33%)
  Pallas kernels  13.3 us (31%)
  local copies, waits for them, and re-layouts  7.94 us (18%)
  waiting for transfers between devices  6.57 us (15%)
  between operations  0.82 us (2%)
    unnamed x20, local copies, waits for them, and re-layouts  7.84 us
    pallas_call x2, Pallas kernels, prefix_attention(): pl.pallas_call(functools.partial(prefix_kernel, len(queries), tiles), out...  6.57 us
    ppermute x1, starting transfers between devices, on_device(): middle = lax.ppermute(block, 'dom', [(0, 2), (3, 1)])  5.95 us
    ppermute x1, waiting for transfers between devices, on_device(): parts = [lax.ppermute(s, 'seq', back(t, 0)) for t, s in enumerate(sums, 1)]  3.16 us
    ppermute x1, starting transfers between devices, on_device(): theirs = lax.ppermute(ancestors, 'dom', [(0, 1), (3, 2)])  3.06 us
    ppermute x1, waiting for transfers between devices, on_device(): blocks = [block, lax.ppermute(chosen, 'dom', swap), middle, far]  2.59 us
    ppermute x3, starting transfers between devices, on_device(): lax.ppermute(own, 'seq', pairs(*r))  2.15 us
    pallas_call x1, Pallas kernels, on_device(): pl.pallas_call(functools.partial(far_kernel, others, len(blocks), line),...  1.83 us
  transfers between devices with their start and end apart: 11, of which 3 were waited for; matrix products, arithmetic and copies ran while one was open for 0% of the time, Pallas kernels for 23%

profile of v14, /device:TPU:0, one launch (start us, length us, event | category | flops | bytes accessed | tf_op | source)
XLA Modules:
  0.0 43.0 jit_solution(4337982787404335182)
XLA Ops:
  0.6 1.0 %copy-done.7 = bf16[4,64,576]{2,1,0:T(8,128)(2,1)S(1)} copy-done((bf16[4,64,576]{2,1,0:T(8,128)(2,1)S(1)}, bf16[4,64,576]{2,1,0:T(8,128)(2,1)}, u32[]{:S(2)}) %copy-start.7) | copy-done | bytes 294936
  1.7 6.0 %collective-permute-start.4 = (bf16[128,1152]{1,0:T(8,128)(2,1)S(1)}, bf16[128,1152]{1,0:T(8,128)(2,1)S(1)}, u32[]{:S(2)}, u32[]{:S(2)}) collective-permute-start(bf16[128,1152]{1,0:T(8,128)(2,1)S(1)} %pack.1.refs_0_.refs_8_), channel_id=1, source_target_pairs={{0,2},{3,1},{4,6},{7,5},{8,10},{11,9},{12,14},{15,13},{16,18},{19,... | collective-permute-start | bytes 884744 | tf_op jit(solution)/shard_map/ppermute | solution.py:333
  7.6 0.7 %collective-permute-start.3 = (bf16[128,1152]{1,0:T(8,128)(2,1)S(1)}, bf16[128,1152]{1,0:T(8,128)(2,1)S(1)}, u32[]{:S(2)}, u32[]{:S(2)}) collective-permute-start(bf16[128,1152]{1,0:T(8,128)(2,1)S(1)} %pack.1.refs_0_.refs_8_), channel_id=1, source_target_pairs={{1,2},{2,1},{5,6},{6,5},{9,10},{10,9},{13,14},{14,13},{17,18},{18,... | collective-permute-start | bytes 884744 | tf_op jit(solution)/shard_map/ppermute | solution.py:334
  8.5 2.2 %copy-done.6 = bf16[32,128,512]{2,1,0:T(8,128)(2,1)S(1)} copy-done((bf16[32,128,512]{2,1,0:T(8,128)(2,1)S(1)}, bf16[32,128,512]{2,1,0:T(8,128)(2,1)}, u32[]{:S(2)}) %copy-start.6) | copy-done | bytes 4194328
  10.7 0.6 %project.1.refs_0_ = bf16[128,576]{1,0:T(8,128)(2,1)S(1)} custom-call(bf16[128,192]{1,0:T(8,128)(2,1)S(1)} %reshape.7.asked_ref, bf16[32,128,512]{2,1,0:T(8,128)(2,1)S(1)} %copy-done.6), custom_call_target="tpu_custom_call" | custom-call | flops 8000000000 | tf_op jit(solution)/shard_map/project/pallas_call | solution.py:342
  11.3 1.6 %collective-permute-start.1 = (bf16[128,576]{1,0:T(8,128)(2,1)S(1)}, bf16[128,576]{1,0:T(8,128)(2,1)S(1)}, u32[]{:S(2)}, u32[]{:S(2)}) collective-permute-start(bf16[128,576]{1,0:T(8,128)(2,1)S(1)} %project.1.refs_0_), channel_id=1, source_target_pairs={{0,12},{4,8},{8,4},{12,0},{1,13},{5,9},{9,5},{13,1},{2,14},{6,10},... | collective-permute-start | bytes 442376 | tf_op jit(solution)/shard_map/ppermute | solution.py:364
  12.9 0.5 %collective-permute-start = (bf16[128,576]{1,0:T(8,128)(2,1)S(1)}, bf16[128,576]{1,0:T(8,128)(2,1)S(1)}, u32[]{:S(2)}, u32[]{:S(2)}) collective-permute-start(bf16[128,576]{1,0:T(8,128)(2,1)S(1)} %project.1.refs_0_), channel_id=1, source_target_pairs={{0,8},{4,12},{8,0},{12,4},{1,9},{5,13},{9,1},{13,5},{2,10},{6,14},... | collective-permute-start | bytes 442376 | tf_op jit(solution)/shard_map/ppermute | solution.py:364
  13.6 3.1 %collective-permute-start.2 = (s32[4]{0:T(128)S(1)}, s32[4]{0:T(128)S(1)}, u32[]{:S(2)}, u32[]{:S(2)}) collective-permute-start(s32[4]{0:T(128)S(1)} %copy-done.4), channel_id=1, source_target_pairs={{0,1},{3,2},{4,5},{7,6},{8,9},{11,10},{12,13},{15,14},{16,17},{19,... | collective-permute-start | bytes 56 | tf_op jit(solution)/shard_map/ppermute | solution.py:335
  16.6 2.3 %copy-done = bf16[4096,576]{0,1:T(8,128)(2,1)S(1)} copy-done((bf16[4096,576]{0,1:T(8,128)(2,1)S(1)}, bf16[4096,576]{0,1:T(8,128)(2,1)}, u32[]{:S(2)}) %copy-start) | copy-done | bytes 4718616
  19.0 3.3 %prefix_attention.3 = (f32[128,512]{1,0:T(8,128)S(1)}, f32[128,128]{1,0:T(8,128)S(1)}, f32[128,128]{1,0:T(8,128)S(1)}, bf16[128,640]{1,0:T(8,128)(2,1)S(1)}) custom-call(bf16[128,576]{1,0:T(8,128)(2,1)S(1)} %project.1.refs_0_, bf16[128,576]{1,0:T(8,128)(2,1)S(1)} %collective-permute-done.5.refs_1_, bf16[576,4096]{1,0:T(8,128)(2,1)S(1)} %bitcast.5), custom_call_target="tpu_custom_call" | custom-call | tf_op jit(solution)/shard_map/prefix_attention/pallas_call | solution.py:110
  22.3 1.0 %select.1 = bf16[128,1152]{1,0:T(8,128)(2,1)S(1)} custom-call(s32[4]{0:T(128)S(1)} %collective-permute-done.2.theirs, s32[2]{0:T(128)S(1)} %pad_add_fusion.place.refs_2_, bf16[128,1152]{1,0:T(8,128)(2,1)S(1)} %pack.1.refs_0_.refs_8_, bf16[128,1152]{1,0:T(8,128)(2,1)S(1)} %collective-permute-done.3.refs_1_.refs_11_, ...), custom_call_target="tpu_custom_call" | custom-call | tf_op jit(solution)/shard_map/select/pallas_call | solution.py:373
  23.4 0.3 collective-permute-start.6
  23.7 2.3 %copy-done.1 = bf16[4096,576]{0,1:T(8,128)(2,1)S(1)} copy-done((bf16[4096,576]{0,1:T(8,128)(2,1)S(1)}, bf16[4096,576]{0,1:T(8,128)(2,1)}, u32[]{:S(2)}) %copy-start.1) | copy-done | bytes 4718616
  26.0 3.2 %prefix_attention.2 = (f32[256,512]{1,0:T(8,128)S(1)}, f32[256,128]{1,0:T(8,128)S(1)}, f32[256,128]{1,0:T(8,128)S(1)}) custom-call(bf16[128,576]{1,0:T(8,128)(2,1)S(1)} %collective-permute-done.refs_0_.refs_3_, bf16[128,576]{1,0:T(8,128)(2,1)S(1)} %collective-permute-done.1.refs_1_.refs_4_, bf16[576,4096]{1,0:T(8,128)(2,1)S(1)} %bitcast.6), custom_call_target="tpu_custom_call" | custom-call | flops 2281701376 | bytes 4718592 | tf_op jit(solution)/shard_map/prefix_attention/pallas_call | solution.py:110
  29.3 2.6 %collective-permute-done.6.refs_9_ = bf16[128,1152]{1,0:T(8,128)(2,1)S(1)} collective-permute-done((bf16[128,1152]{1,0:T(8,128)(2,1)S(1)}, bf16[128,1152]{1,0:T(8,128)(2,1)S(1)}, u32[]{:S(2)}, u32[]{:S(2)}) %collective-permute-start.6) | collective-permute-done | bytes 294944 | tf_op jit(solution)/shard_map/ppermute | solution.py:383
  31.9 1.8 %suffix_far.1 = (bf16[256,576]{1,0:T(8,128)(2,1)S(1)}, bf16[128,640]{1,0:T(8,128)(2,1)S(1)}, bf16[128,640]{1,0:T(8,128)(2,1)S(1)}) custom-call(s32[4]{0:T(128)S(1)} %copy-done.4, s32[16]{0:T(128)S(1)} %copy-done.5, s32[2]{0:T(128)S(1)} %pad_add_fusion.place.refs_2_, bf16[128,576]{1,0:T(8,128)(2,1)S(1)} %collective-permute-done.refs_0_.refs_3_, ...), custom_call_target="tpu_custom_call" | custom-call | tf_op jit(solution)/shard_map/suffix_far/pallas_call | solution.py:387
  33.8 0.5 %collective-permute-start.10 = (bf16[256,576]{1,0:T(8,128)(2,1)S(1)}, bf16[256,576]{1,0:T(8,128)(2,1)S(1)}, u32[]{:S(2)}, u32[]{:S(2)}) collective-permute-start(bf16[256,576]{1,0:T(8,128)(2,1)S(1)} %get-tuple-element.25.refs_5_), channel_id=1, source_target_pairs={{0,4},{4,0},{8,12},{12,8},{1,5},{5,1},{9,13},{13,9},{2,6},{6,2},{1... | collective-permute-start | bytes 884744 | tf_op jit(solution)/shard_map/ppermute | solution.py:403
  34.3 0.1 collective-permute-start.9
  34.4 0.8 %collective-permute-done.7.refs_1_ = bf16[128,640]{1,0:T(8,128)(2,1)S(1)} collective-permute-done((bf16[128,640]{1,0:T(8,128)(2,1)S(1)}, bf16[128,640]{1,0:T(8,128)(2,1)S(1)}, u32[]{:S(2)}, u32[]{:S(2)}) %collective-permute-start.7) | collective-permute-done | bytes 163872 | tf_op jit(solution)/shard_map/ppermute | solution.py:401
  35.2 0.2 chip_merge.1
  35.4 1.6 %collective-permute-start.8 = (bf16[128,640]{1,0:T(8,128)(2,1)S(1)}, bf16[128,640]{1,0:T(8,128)(2,1)S(1)}, u32[]{:S(2)}, u32[]{:S(2)}) collective-permute-start(bf16[128,640]{1,0:T(8,128)(2,1)S(1)} %chip_merge.1), channel_id=1, source_target_pairs={{8,0},{12,4},{0,8},{4,12},{9,1},{13,5},{1,9},{5,13},{10,2},{14,6},... | collective-permute-start | bytes 491528 | tf_op jit(solution)/shard_map/ppermute | solution.py:402
  36.9 1.6 %suffix_near.1 = (bf16[4,64,576]{2,1,0:T(8,128)(2,1)}, bf16[128,640]{1,0:T(8,128)(2,1)S(1)}) custom-call(s32[4]{0:T(128)S(1)} %copy-done.4, s32[16]{0:T(128)S(1)} %copy-done.5, s32[2]{0:T(128)S(1)} %pad_add_fusion.place.refs_2_, bf16[4,576]{1,0:T(4,128)(2,1)S(1)} %copy-done.3, bf16[128,576]{1,0:T(8,128)(2,1)S(1)} %project.1.refs_0_, ...), custom_call_target="tpu_custom_call" | custom-call | tf_op jit(solution)/shard_map/suffix_near/pallas_call | solution.py:407
  38.5 3.2 %collective-permute-done.8.refs_0_ = bf16[128,640]{1,0:T(8,128)(2,1)S(1)} collective-permute-done((bf16[128,640]{1,0:T(8,128)(2,1)S(1)}, bf16[128,640]{1,0:T(8,128)(2,1)S(1)}, u32[]{:S(2)}, u32[]{:S(2)}) %collective-permute-start.8) | collective-permute-done | bytes 163872 | tf_op jit(solution)/shard_map/ppermute | solution.py:402
  41.7 1.3 %final.1 = bf16[4,32,128]{2,1,0:T(8,128)(2,1)} custom-call(bf16[128,640]{1,0:T(8,128)(2,1)S(1)} %collective-permute-done.8.refs_0_, bf16[128,640]{1,0:T(8,128)(2,1)S(1)} %get-tuple-element.26.refs_1_, bf16[32,512,128]{2,1,0:T(8,128)(2,1)S(1)} %copy-done.2), custom_call_target="tpu_custom_call" | custom-call | tf_op jit(solution)/shard_map/final/pallas_call | solution.py:417
  (31 shorter events, 0.4 us)
Async XLA Ops:
  0.6 1.0 %copy-start.7 = (bf16[4,64,576]{2,1,0:T(8,128)(2,1)S(1)}, bf16[4,64,576]{2,1,0:T(8,128)(2,1)}, u32[]{:S(2)}) copy-start(bf16[4,64,576]{2,1,0:T(8,128)(2,1)} %cache_ref.1) | copy-start | bytes 884740
  1.6 6.7 %copy-start.8 = (bf16[4,32,64]{2,1,0:T(8,128)(2,1)S(1)}, bf16[4,32,64]{2,1,0:T(8,128)(2,1)}, u32[]{:S(2)}) copy-start(bf16[4,32,64]{2,1,0:T(8,128)(2,1)} %param.10) | copy-start | bytes 49156
  1.6 6.7 %copy-start.9 = (bf16[4,32,128]{2,1,0:T(8,128)(2,1)S(1)}, bf16[4,32,128]{2,1,0:T(8,128)(2,1)}, u32[]{:S(2)}) copy-start(bf16[4,32,128]{2,1,0:T(8,128)(2,1)} %param.9) | copy-start | bytes 98308
  1.7 20.6 %collective-permute-start.4 = (bf16[128,1152]{1,0:T(8,128)(2,1)S(1)}, bf16[128,1152]{1,0:T(8,128)(2,1)S(1)}, u32[]{:S(2)}, u32[]{:S(2)}) collective-permute-start(bf16[128,1152]{1,0:T(8,128)(2,1)S(1)} %pack.1.refs_0_.refs_8_), channel_id=1, source_target_pairs={{0,2},{3,1},{4,6},{7,5},{8,10},{11,9},{12,14},{15,13},{16,18},{19,... | collective-permute-start | bytes 884744 | tf_op jit(solution)/shard_map/ppermute | solution.py:333
  7.6 14.7 %collective-permute-start.3 = (bf16[128,1152]{1,0:T(8,128)(2,1)S(1)}, bf16[128,1152]{1,0:T(8,128)(2,1)S(1)}, u32[]{:S(2)}, u32[]{:S(2)}) collective-permute-start(bf16[128,1152]{1,0:T(8,128)(2,1)S(1)} %pack.1.refs_0_.refs_8_), channel_id=1, source_target_pairs={{1,2},{2,1},{5,6},{6,5},{9,10},{10,9},{13,14},{14,13},{17,18},{18,... | collective-permute-start | bytes 884744 | tf_op jit(solution)/shard_map/ppermute | solution.py:334
  8.5 2.2 %copy-start.6 = (bf16[32,128,512]{2,1,0:T(8,128)(2,1)S(1)}, bf16[32,128,512]{2,1,0:T(8,128)(2,1)}, u32[]{:S(2)}) copy-start(bf16[32,128,512]{2,1,0:T(8,128)(2,1)} %w_ref.1) | copy-start | bytes 12582916
  10.7 2.9 %copy-start.4 = (s32[4]{0:T(128)S(1)}, s32[4]{0:T(128)}, u32[]{:S(2)}) copy-start(s32[4]{0:T(128)} %anc.1) | copy-start | bytes 52
  11.3 2.2 %collective-permute-start.5 = (bf16[128,576]{1,0:T(8,128)(2,1)S(1)}, bf16[128,576]{1,0:T(8,128)(2,1)S(1)}, u32[]{:S(2)}, u32[]{:S(2)}) collective-permute-start(bf16[128,576]{1,0:T(8,128)(2,1)S(1)} %project.1.refs_0_), channel_id=1, source_target_pairs={{0,4},{4,0},{8,12},{12,8},{1,5},{5,1},{9,13},{13,9},{2,6},{6,2},{1... | collective-permute-start | bytes 442376 | tf_op jit(solution)/shard_map/ppermute | solution.py:364
  11.3 12.4 %collective-permute-start.1 = (bf16[128,576]{1,0:T(8,128)(2,1)S(1)}, bf16[128,576]{1,0:T(8,128)(2,1)S(1)}, u32[]{:S(2)}, u32[]{:S(2)}) collective-permute-start(bf16[128,576]{1,0:T(8,128)(2,1)S(1)} %project.1.refs_0_), channel_id=1, source_target_pairs={{0,12},{4,8},{8,4},{12,0},{1,13},{5,9},{9,5},{13,1},{2,14},{6,10},... | collective-permute-start | bytes 442376 | tf_op jit(solution)/shard_map/ppermute | solution.py:364
  12.9 10.7 %collective-permute-start = (bf16[128,576]{1,0:T(8,128)(2,1)S(1)}, bf16[128,576]{1,0:T(8,128)(2,1)S(1)}, u32[]{:S(2)}, u32[]{:S(2)}) collective-permute-start(bf16[128,576]{1,0:T(8,128)(2,1)S(1)} %project.1.refs_0_), channel_id=1, source_target_pairs={{0,8},{4,12},{8,0},{12,4},{1,9},{5,13},{9,1},{13,5},{2,10},{6,14},... | collective-permute-start | bytes 442376 | tf_op jit(solution)/shard_map/ppermute | solution.py:364
  13.6 8.7 %collective-permute-start.2 = (s32[4]{0:T(128)S(1)}, s32[4]{0:T(128)S(1)}, u32[]{:S(2)}, u32[]{:S(2)}) collective-permute-start(s32[4]{0:T(128)S(1)} %copy-done.4), channel_id=1, source_target_pairs={{0,1},{3,2},{4,5},{7,6},{8,9},{11,10},{12,13},{15,14},{16,17},{19,... | collective-permute-start | bytes 56 | tf_op jit(solution)/shard_map/ppermute | solution.py:335
  16.6 2.3 %copy-start = (bf16[4096,576]{0,1:T(8,128)(2,1)S(1)}, bf16[4096,576]{0,1:T(8,128)(2,1)}, u32[]{:S(2)}) copy-start(bf16[4096,576]{0,1:T(8,128)(2,1)} %param.13) | copy-start | bytes 14155780
  22.3 9.6 %copy-start.5 = (s32[16]{0:T(128)S(1)}, s32[16]{0:T(128)}, u32[]{:S(2)}) copy-start(s32[16]{0:T(128)} %lens.1) | copy-start | bytes 196
  22.3 14.6 %copy-start.3 = (bf16[4,576]{1,0:T(4,128)(2,1)S(1)}, bf16[4,576]{1,0:T(4,128)(2,1)}, u32[]{:S(2)}) copy-start(bf16[4,576]{1,0:T(4,128)(2,1)} %fresh_ref.1) | copy-start | bytes 13828
  23.4 8.5 %collective-permute-start.6 = (bf16[128,1152]{1,0:T(8,128)(2,1)S(1)}, bf16[128,1152]{1,0:T(8,128)(2,1)S(1)}, u32[]{:S(2)}, u32[]{:S(2)}) collective-permute-start(bf16[128,1152]{1,0:T(8,128)(2,1)S(1)} %select.1), channel_id=1, source_target_pairs={{0,1},{1,0},{2,3},{3,2},{4,5},{5,4},{6,7},{7,6},{8,9},{9,8},{10,11... | collective-permute-start | bytes 884744 | tf_op jit(solution)/shard_map/ppermute | solution.py:383
  23.7 2.3 %copy-start.1 = (bf16[4096,576]{0,1:T(8,128)(2,1)S(1)}, bf16[4096,576]{0,1:T(8,128)(2,1)}, u32[]{:S(2)}) copy-start(bf16[4096,576]{0,1:T(8,128)(2,1)} %param.13) | copy-start | bytes 14155780
  26.0 15.7 %copy-start.2 = (bf16[32,512,128]{2,1,0:T(8,128)(2,1)S(1)}, bf16[32,512,128]{2,1,0:T(8,128)(2,1)}, u32[]{:S(2)}) copy-start(bf16[32,512,128]{2,1,0:T(8,128)(2,1)} %refs_2_.1) | copy-start | bytes 12582916
  33.7 1.5 %collective-permute-start.7 = (bf16[128,640]{1,0:T(8,128)(2,1)S(1)}, bf16[128,640]{1,0:T(8,128)(2,1)S(1)}, u32[]{:S(2)}, u32[]{:S(2)}) collective-permute-start(bf16[128,640]{1,0:T(8,128)(2,1)S(1)} %get-tuple-element.20), channel_id=1, source_target_pairs={{0,4},{4,0},{8,12},{12,8},{1,5},{5,1},{9,13},{13,9},{2,6},{6,2},{1... | collective-permute-start | bytes 491528 | tf_op jit(solution)/shard_map/ppermute | solution.py:401
  33.8 3.1 %collective-permute-start.10 = (bf16[256,576]{1,0:T(8,128)(2,1)S(1)}, bf16[256,576]{1,0:T(8,128)(2,1)S(1)}, u32[]{:S(2)}, u32[]{:S(2)}) collective-permute-start(bf16[256,576]{1,0:T(8,128)(2,1)S(1)} %get-tuple-element.25.refs_5_), channel_id=1, source_target_pairs={{0,4},{4,0},{8,12},{12,8},{1,5},{5,1},{9,13},{13,9},{2,6},{6,2},{1... | collective-permute-start | bytes 884744 | tf_op jit(solution)/shard_map/ppermute | solution.py:403
  34.3 2.6 %collective-permute-start.9 = (bf16[128,640]{1,0:T(8,128)(2,1)S(1)}, bf16[128,640]{1,0:T(8,128)(2,1)S(1)}, u32[]{:S(2)}, u32[]{:S(2)}) collective-permute-start(bf16[128,640]{1,0:T(8,128)(2,1)S(1)} %get-tuple-element.23), channel_id=1, source_target_pairs={{0,4},{4,0},{8,12},{12,8},{1,5},{5,1},{9,13},{13,9},{2,6},{6,2},{1... | collective-permute-start | bytes 491528 | tf_op jit(solution)/shard_map/ppermute | solution.py:371
  35.4 6.3 %collective-permute-start.8 = (bf16[128,640]{1,0:T(8,128)(2,1)S(1)}, bf16[128,640]{1,0:T(8,128)(2,1)S(1)}, u32[]{:S(2)}, u32[]{:S(2)}) collective-permute-start(bf16[128,640]{1,0:T(8,128)(2,1)S(1)} %chip_merge.1), channel_id=1, source_target_pairs={{8,0},{12,4},{0,8},{4,12},{9,1},{13,5},{1,9},{5,13},{10,2},{14,6},... | collective-permute-start | bytes 491528 | tf_op jit(solution)/shard_map/ppermute | solution.py:402

commit v15 on v14

--- a/solution.py
+++ b/solution.py
@@ -41,10 +41,10 @@
         out_ref[part, 2 * rank :] = jnp.concatenate([first[:, rank:], second[:, rank:]], axis=1)
 
 
-def project_kernel(local, asked_ref, w_ref, own_ref):
+def project_kernel(local, nope_ref, rope_ref, w_ref, own_ref):
     heads, _, rank = w_ref.shape
-    width = w_ref.shape[1]
-    nope = asked_ref[:, :width].astype(F32)
+    nope = nope_ref[...].astype(F32)
+    width = nope.shape[1]
     first = lax.broadcasted_iota(jnp.int32, (2 * local, width), 0) < local
 
     def pair(h):
@@ -53,7 +53,7 @@
         weights = w_ref[pl.ds(h, 2)].reshape(2 * width, rank)
         return jnp.dot(left.astype(BF16), weights, preferred_element_type=F32)
 
-    own_ref[:, rank:] = asked_ref[:, width:]
+    own_ref[:, rank:] = rope_ref[...]
     for h in range(0, heads, 4):
         own_ref[pl.ds(h * local, 4 * local), :rank] = jnp.concatenate(
             [pair(i) for i in (h, h + 2)], axis=0
@@ -197,24 +197,26 @@
         copy(p, 0, 0).wait()
 
 
-def at_end(place):
-    return (place[1] == 0) | (place[1] == 3)
-
-
-def select_kernel(theirs, place, *refs):
+def at_end(dom):
+    return (dom == 0) | (dom == 3)
+
+
+def select_kernel(theirs, *refs):
+    dom = lax.axis_index("dom")
     block_refs, (_, out_ref, sems) = refs[:-3], refs[-3:]
     local = sems.shape[0]
     picks = []
     for p in range(local):
-        apart = jnp.bitwise_xor(lax.div(theirs[p], local), place[1])
-        which = jnp.where(at_end(place) | (apart < 2), 0, 4 - apart)
-        picks.append((which, jnp.where(at_end(place), p, lax.rem(theirs[p], local))))
+        apart = jnp.bitwise_xor(lax.div(theirs[p], local), dom)
+        which = jnp.where(at_end(dom), 0, jnp.maximum(apart - 1, 0))
+        picks.append((which, jnp.where(at_end(dom), p, lax.rem(theirs[p], local))))
     gather_blocks(block_refs, picks, out_ref, sems)
 
 
 def far_kernel(stages, sources, line, *refs):
-    anc, lens, place = refs[:3]
-    refs = refs[3:]
+    anc, lens = refs[:2]
+    refs = refs[2:]
+    seq, dom = lax.axis_index("seq"), lax.axis_index("dom")
     stage_refs, refs = refs[: 5 * stages], refs[5 * stages :]
     block_refs, refs = refs[:sources], refs[sources:]
     moved_ref, refs = refs[0], refs[1:]
@@ -229,12 +231,12 @@
     for p in range(local):
         owner, slot = lax.div(anc[p], local), lax.rem(anc[p], local)
         if line:
-            which = jnp.bitwise_xor(owner, place[1])
-            chosen = at_end(place) & (which != 0)
+            which = jnp.bitwise_xor(owner, dom)
+            chosen = at_end(dom) & (which != 0)
             which = jnp.where(chosen, 1, which)
             slot = jnp.where(chosen, p, slot)
         else:
-            which = lax.rem(place[1] - owner + sources, sources)
+            which = lax.rem(dom - owner + sources, sources)
         picks.append((which, slot))
     gather_blocks(block_refs, picks, raw, sems)
     for p in range(local):
@@ -248,7 +250,7 @@
     for k in range(stages):
         first_ref, second_ref, acc_ref, max_ref, sum_ref = stage_refs[5 * k : 5 * k + 5]
         queries = jnp.concatenate([first_ref[...], second_ref[...]], axis=0)
-        seen = visible(queries.shape[0], ends, [place[0] * span], span)
+        seen = visible(queries.shape[0], ends, [seq * span], span)
         known = [(max_ref[:, 0:1], sum_ref[:, 0:1], acc_ref[...])]
         part = attend(queries, moved_ref[...], seen, rank, known)
         rows = first_ref.shape[0]
@@ -256,11 +258,12 @@
         give_refs[k][...] = part[rows:]
 
 
-def near_kernel(anc, lens, place, fresh_ref, *refs):
+def near_kernel(anc, lens, fresh_ref, *refs):
+    seq = lax.axis_index("seq")
     query_ref, acc_ref, max_ref, sum_ref, got_ref, moved_ref, other_ref, cache_ref, part_ref = refs
     local, span, width = cache_ref.shape
     rank = acc_ref.shape[1]
-    start, other = place[0] * span, jnp.bitwise_xor(place[0], 1) * span
+    start, other = seq * span, jnp.bitwise_xor(seq, 1) * span
     ends = [lens[anc[p]] for p in range(local)]
     keys = jnp.concatenate([moved_ref[...], other_ref[...]], axis=0)
     seen = visible(query_ref.shape[0], ends, [start, other], span)
@@ -316,7 +319,6 @@
     seq_size, dom_size = lax.axis_size("seq"), lax.axis_size("dom")
     cores = 2
     chips = seq_size // cores
-    place = jnp.stack([lax.axis_index("seq"), lax.axis_index("dom")]).astype(jnp.int32)
     block = pl.pallas_call(
         functools.partial(pack_kernel, rank),
         out_shape=shape((local * span // 2, 2 * width)),
@@ -326,7 +328,7 @@
         cost_estimate=pl.CostEstimate(flops=PACK, bytes_accessed=0, transcendentals=0),
         name="pack",
     )(private_caches)
-    asked_rows = jnp.swapaxes(jnp.concatenate([q_nope, q_rope], axis=2), 0, 1).reshape(rows, -1)
+    nope_rows, rope_rows = (jnp.swapaxes(q, 0, 1).reshape(rows, -1) for q in (q_nope, q_rope))
     line = dom_size == 4
     if line:
         swap = [(0, 1), (1, 0), (2, 3), (3, 2)]
@@ -342,12 +344,12 @@
     own = pl.pallas_call(
         functools.partial(project_kernel, local),
         out_shape=shape((rows, width)),
-        in_specs=[VMEM] * 2,
+        in_specs=[VMEM] * 3,
         out_specs=VMEM,
         compiler_params=PARAMS,
         cost_estimate=pl.CostEstimate(flops=PROJECT, bytes_accessed=0, transcendentals=0),
         name="project",
-    )(asked_rows, w_uk)
+    )(nope_rows, rope_rows, w_uk)
     keys = prefix.T
 
     def pairs(turn, flip):
@@ -373,13 +375,13 @@
             chosen = pl.pallas_call(
                 select_kernel,
                 out_shape=shape(block.shape),
-                in_specs=[SMEM] * 2 + [ANY] * 4,
+                in_specs=[SMEM] + [ANY] * 4,
                 out_specs=VMEM,
                 scratch_shapes=[pltpu.SemaphoreType.DMA((local,))],
                 compiler_params=PARAMS,
                 cost_estimate=pl.CostEstimate(flops=0, bytes_accessed=0, transcendentals=0),
                 name="select",
-            )(theirs, place, block, far, middle, stage[3])
+            )(theirs, block, middle, far, stage[3])
             blocks = [block, lax.ppermute(chosen, "dom", swap), middle, far]
 
     part = shape((rows, rank + LANES))
@@ -387,7 +389,7 @@
     far_results = pl.pallas_call(
         functools.partial(far_kernel, others, len(blocks), line),
         out_shape=[shape((local * span, width))] + [part] * (2 * others),
-        in_specs=[SMEM] * 3 + [VMEM] * (5 * others) + [ANY] * len(blocks),
+        in_specs=[SMEM] * 2 + [VMEM] * (5 * others) + [ANY] * len(blocks),
         out_specs=[VMEM] * (1 + 2 * others),
         scratch_shapes=[
             pltpu.VMEM(block.shape, BF16),
@@ -395,7 +397,7 @@
         ],
         compiler_params=PARAMS,
         name="suffix_far",
-    )(ancestors, lengths, place, *[a for stage in stages[1:] for a in stage], *blocks)
+    )(ancestors, lengths, *[a for stage in stages[1:] for a in stage], *blocks)
     moved = far_results[0]
     keep, give = far_results[1 : 1 + others], far_results[1 + others :]
     sums = chip_merge(keep, [lax.ppermute(g, "seq", pairs(0, 1)) for g in give])
@@ -407,11 +409,11 @@
     new_caches, own_part = pl.pallas_call(
         near_kernel,
         out_shape=[shape(private_caches.shape), part],
-        in_specs=[SMEM] * 3 + [VMEM] * 8,
+        in_specs=[SMEM] * 2 + [VMEM] * 8,
         out_specs=[VMEM] * 2,
         compiler_params=PARAMS,
         name="suffix_near",
-    )(ancestors, lengths, place, new_latent, query, acc, level, mass, given, moved, other)
+    )(ancestors, lengths, new_latent, query, acc, level, mass, given, moved, other)
     parts.append(own_part)
 
     head_values = pl.pallas_call(

time: 43.4 us -> 40.7 us (0.938)
  local copies, waits for them, and re-layouts: 7.94 us -> 1.2 us
  starting transfers between devices: 14.3 us -> 18.3 us
    unnamed x20, local copies, waits for them, and re-layouts: 7.84 us -> 1.16 us
    ppermute x1, starting transfers between devices: 0.29 us -> 4.03 us  [on_device(): blocks = [block, lax.ppermute(chosen, 'dom', swap), middle, far]]
    ppermute x1, starting transfers between devices: 5.95 us -> 7.77 us  [on_device(): middle = lax.ppermute(block, 'dom', [(0, 2), (3, 1)])]
    ppermute x1, starting transfers between devices: 3.06 us -> 1.38 us  [on_device(): theirs = lax.ppermute(ancestors, 'dom', [(0, 1), (3, 2)])]
  transfers between devices with their start and end apart: 11 -> 11, of which waited for: 3 -> 3; matrix products, arithmetic and copies ran while one was open for 0% -> 0% of each run, Pallas kernels for 23% -> 25%
where the time goes in v15:
time: 40.7 us; the launch traced here: 40.5 us
  starting transfers between devices  18.3 us (45%)
  Pallas kernels  13.3 us (33%)
  waiting for transfers between devices  6.85 us (17%)
  local copies, waits for them, and re-layouts  1.2 us (3%)
  between operations  0.86 us (2%)
    ppermute x1, starting transfers between devices, on_device(): middle = lax.ppermute(block, 'dom', [(0, 2), (3, 1)])  7.77 us
    pallas_call x2, Pallas kernels, prefix_attention(): pl.pallas_call(functools.partial(prefix_kernel, len(queries), tiles), out...  6.58 us
    ppermute x1, starting transfers between devices, on_device(): blocks = [block, lax.ppermute(chosen, 'dom', swap), middle, far]  4.03 us
    ppermute x1, waiting for transfers between devices, on_device(): parts = [lax.ppermute(s, 'seq', back(t, 0)) for t, s in enumerate(sums, 1)]  3.16 us
    ppermute x1, waiting for transfers between devices, on_device(): blocks = [block, lax.ppermute(chosen, 'dom', swap), middle, far]  2.86 us
    ppermute x3, starting transfers between devices, on_device(): lax.ppermute(own, 'seq', pairs(*r))  2.15 us
    pallas_call x1, Pallas kernels, on_device(): pl.pallas_call(functools.partial(far_kernel, others, len(blocks), line),...  1.82 us
    pallas_call x1, Pallas kernels, on_device(): pl.pallas_call(near_kernel, out_shape=[shape(private_caches.shape), part]...  1.58 us
  transfers between devices with their start and end apart: 11, of which 3 were waited for; matrix products, arithmetic and copies ran while one was open for 0% of the time, Pallas kernels for 25%

profile of v15, /device:TPU:0, one launch (start us, length us, event | category | flops | bytes accessed | tf_op | source)
XLA Modules:
  0.0 40.5 jit_solution(9280980197242250021)
XLA Ops:
  0.7 1.1 %copy-done.5 = bf16[4,64,576]{2,1,0:T(8,128)(2,1)S(1)} copy-done((bf16[4,64,576]{2,1,0:T(8,128)(2,1)S(1)}, bf16[4,64,576]{2,1,0:T(8,128)(2,1)}, u32[]{:S(2)}) %copy-start.5) | copy-done | bytes 294936
  1.8 0.1 pack.1.refs_0_.refs_7_
  1.8 0.8 %collective-permute-start.4 = (bf16[128,1152]{1,0:T(8,128)(2,1)S(1)}, bf16[128,1152]{1,0:T(8,128)(2,1)S(1)}, u32[]{:S(2)}, u32[]{:S(2)}) collective-permute-start(bf16[128,1152]{1,0:T(8,128)(2,1)S(1)} %pack.1.refs_0_.refs_7_), channel_id=1, source_target_pairs={{1,2},{2,1},{5,6},{6,5},{9,10},{10,9},{13,14},{14,13},{17,18},{18,... | collective-permute-start | bytes 884744 | tf_op jit(solution)/shard_map/ppermute | solution.py:336
  2.7 7.8 %collective-permute-start.3 = (bf16[128,1152]{1,0:T(8,128)(2,1)S(1)}, bf16[128,1152]{1,0:T(8,128)(2,1)S(1)}, u32[]{:S(2)}, u32[]{:S(2)}) collective-permute-start(bf16[128,1152]{1,0:T(8,128)(2,1)S(1)} %pack.1.refs_0_.refs_7_), channel_id=1, source_target_pairs={{0,2},{3,1},{4,6},{7,5},{8,10},{11,9},{12,14},{15,13},{16,18},{19,... | collective-permute-start | bytes 884744 | tf_op jit(solution)/shard_map/ppermute | solution.py:335
  10.5 0.6 %project.1.refs_0_ = bf16[128,576]{1,0:T(8,128)(2,1)S(1)} custom-call(bf16[128,128]{1,0:T(8,128)(2,1)S(1)} %bitcast.9, bf16[128,64]{1,0:T(8,128)(2,1)S(1)} %bitcast.10, bf16[32,128,512]{2,1,0:T(8,128)(2,1)S(1)} %copy-done.4), custom_call_target="tpu_custom_call" | custom-call | flops 8000000000 | tf_op jit(solution)/shard_map/project/pallas_call | solution.py:344
  11.2 0.0 collective-permute-start.5
  11.2 1.6 %collective-permute-start.1 = (bf16[128,576]{1,0:T(8,128)(2,1)S(1)}, bf16[128,576]{1,0:T(8,128)(2,1)S(1)}, u32[]{:S(2)}, u32[]{:S(2)}) collective-permute-start(bf16[128,576]{1,0:T(8,128)(2,1)S(1)} %project.1.refs_0_), channel_id=1, source_target_pairs={{0,12},{4,8},{8,4},{12,0},{1,13},{5,9},{9,5},{13,1},{2,14},{6,10},... | collective-permute-start | bytes 442376 | tf_op jit(solution)/shard_map/ppermute | solution.py:366
  12.8 0.5 %collective-permute-start = (bf16[128,576]{1,0:T(8,128)(2,1)S(1)}, bf16[128,576]{1,0:T(8,128)(2,1)S(1)}, u32[]{:S(2)}, u32[]{:S(2)}) collective-permute-start(bf16[128,576]{1,0:T(8,128)(2,1)S(1)} %project.1.refs_0_), channel_id=1, source_target_pairs={{0,8},{4,12},{8,0},{12,4},{1,9},{5,13},{9,1},{13,5},{2,10},{6,14},... | collective-permute-start | bytes 442376 | tf_op jit(solution)/shard_map/ppermute | solution.py:366
  13.4 1.4 %collective-permute-start.2 = (s32[4]{0:T(128)S(1)}, s32[4]{0:T(128)S(1)}, u32[]{:S(2)}, u32[]{:S(2)}) collective-permute-start(s32[4]{0:T(128)S(1)} %copy-done.2), channel_id=1, source_target_pairs={{0,1},{3,2},{4,5},{7,6},{8,9},{11,10},{12,13},{15,14},{16,17},{19,... | collective-permute-start | bytes 56 | tf_op jit(solution)/shard_map/ppermute | solution.py:337
  14.8 3.3 %prefix_attention.3 = (f32[128,512]{1,0:T(8,128)S(1)}, f32[128,128]{1,0:T(8,128)S(1)}, f32[128,128]{1,0:T(8,128)S(1)}, bf16[128,640]{1,0:T(8,128)(2,1)S(1)}) custom-call(bf16[128,576]{1,0:T(8,128)(2,1)S(1)} %project.1.refs_0_, bf16[128,576]{1,0:T(8,128)(2,1)S(1)} %collective-permute-done.5.refs_1_, bf16[576,4096]{1,0:T(8,128)(2,1)S(1)} %bitcast.7), custom_call_target="tpu_custom_call" | custom-call | tf_op jit(solution)/shard_map/prefix_attention/pallas_call | solution.py:110
  18.1 1.0 %select.1 = bf16[128,1152]{1,0:T(8,128)(2,1)S(1)} custom-call(s32[4]{0:T(128)S(1)} %collective-permute-done.2.theirs, bf16[128,1152]{1,0:T(8,128)(2,1)S(1)} %pack.1.refs_0_.refs_7_, bf16[128,1152]{1,0:T(8,128)(2,1)S(1)} %collective-permute-done.3.refs_1_.refs_9_, bf16[128,1152]{1,0:T(8,128)(2,1)S(1)} %collective-permute-done.4.refs_2_.refs_10_, ...), custom_call_target="tpu_custom_call" | custom-call | tf_op jit(solution)/shard_map/select/pallas_call | solution.py:375
  19.2 4.0 %collective-permute-start.6 = (bf16[128,1152]{1,0:T(8,128)(2,1)S(1)}, bf16[128,1152]{1,0:T(8,128)(2,1)S(1)}, u32[]{:S(2)}, u32[]{:S(2)}) collective-permute-start(bf16[128,1152]{1,0:T(8,128)(2,1)S(1)} %select.1), channel_id=1, source_target_pairs={{0,1},{1,0},{2,3},{3,2},{4,5},{5,4},{6,7},{7,6},{8,9},{9,8},{10,11... | collective-permute-start | bytes 884744 | tf_op jit(solution)/shard_map/ppermute | solution.py:385
  23.2 3.3 %prefix_attention.2 = (f32[256,512]{1,0:T(8,128)S(1)}, f32[256,128]{1,0:T(8,128)S(1)}, f32[256,128]{1,0:T(8,128)S(1)}) custom-call(bf16[128,576]{1,0:T(8,128)(2,1)S(1)} %collective-permute-done.refs_0_.refs_2_, bf16[128,576]{1,0:T(8,128)(2,1)S(1)} %collective-permute-done.1.refs_1_.refs_3_, bf16[576,4096]{1,0:T(8,128)(2,1)S(1)} %bitcast.8), custom_call_target="tpu_custom_call" | custom-call | flops 2281701376 | bytes 4718592 | tf_op jit(solution)/shard_map/prefix_attention/pallas_call | solution.py:110
  26.5 2.9 %collective-permute-done.6.refs_8_ = bf16[128,1152]{1,0:T(8,128)(2,1)S(1)} collective-permute-done((bf16[128,1152]{1,0:T(8,128)(2,1)S(1)}, bf16[128,1152]{1,0:T(8,128)(2,1)S(1)}, u32[]{:S(2)}, u32[]{:S(2)}) %collective-permute-start.6) | collective-permute-done | bytes 294944 | tf_op jit(solution)/shard_map/ppermute | solution.py:385
  29.4 1.8 %suffix_far.1 = (bf16[256,576]{1,0:T(8,128)(2,1)S(1)}, bf16[128,640]{1,0:T(8,128)(2,1)S(1)}, bf16[128,640]{1,0:T(8,128)(2,1)S(1)}) custom-call(s32[4]{0:T(128)S(1)} %copy-done.2, s32[16]{0:T(128)S(1)} %copy-done.3, bf16[128,576]{1,0:T(8,128)(2,1)S(1)} %collective-permute-done.refs_0_.refs_2_, bf16[128,576]{1,0:T(8,128)(2,1)S(1)} %collective-permute-done.1.refs_1_.refs_3_, ...), custom_call_target="tpu_custom_call" | custom-call | tf_op jit(solution)/shard_map/suffix_far/pallas_call | solution.py:389
  31.2 0.1 collective-permute-start.7
  31.3 0.5 %collective-permute-start.10 = (bf16[256,576]{1,0:T(8,128)(2,1)S(1)}, bf16[256,576]{1,0:T(8,128)(2,1)S(1)}, u32[]{:S(2)}, u32[]{:S(2)}) collective-permute-start(bf16[256,576]{1,0:T(8,128)(2,1)S(1)} %get-tuple-element.25.refs_5_), channel_id=1, source_target_pairs={{0,4},{4,0},{8,12},{12,8},{1,5},{5,1},{9,13},{13,9},{2,6},{6,2},{1... | collective-permute-start | bytes 884744 | tf_op jit(solution)/shard_map/ppermute | solution.py:405
  31.8 0.1 collective-permute-start.9
  31.9 0.8 %collective-permute-done.7.refs_1_ = bf16[128,640]{1,0:T(8,128)(2,1)S(1)} collective-permute-done((bf16[128,640]{1,0:T(8,128)(2,1)S(1)}, bf16[128,640]{1,0:T(8,128)(2,1)S(1)}, u32[]{:S(2)}, u32[]{:S(2)}) %collective-permute-start.7) | collective-permute-done | bytes 163872 | tf_op jit(solution)/shard_map/ppermute | solution.py:403
  32.7 0.2 chip_merge.1
  32.9 1.6 %collective-permute-start.8 = (bf16[128,640]{1,0:T(8,128)(2,1)S(1)}, bf16[128,640]{1,0:T(8,128)(2,1)S(1)}, u32[]{:S(2)}, u32[]{:S(2)}) collective-permute-start(bf16[128,640]{1,0:T(8,128)(2,1)S(1)} %chip_merge.1), channel_id=1, source_target_pairs={{8,0},{12,4},{0,8},{4,12},{9,1},{13,5},{1,9},{5,13},{10,2},{14,6},... | collective-permute-start | bytes 491528 | tf_op jit(solution)/shard_map/ppermute | solution.py:404
  34.4 1.6 %suffix_near.1 = (bf16[4,64,576]{2,1,0:T(8,128)(2,1)}, bf16[128,640]{1,0:T(8,128)(2,1)S(1)}) custom-call(s32[4]{0:T(128)S(1)} %copy-done.2, s32[16]{0:T(128)S(1)} %copy-done.3, bf16[4,576]{1,0:T(4,128)(2,1)S(1)} %copy-done.1, bf16[128,576]{1,0:T(8,128)(2,1)S(1)} %project.1.refs_0_, f32[128,512]{1,0:T(8,128)S(1)} %get-tuple-element.21.refs_1_, ...), custom_call_target="tpu_custom_call" | custom-call | tf_op jit(solution)/shard_map/suffix_near/pallas_call | solution.py:409
  36.0 3.2 %collective-permute-done.8.refs_0_ = bf16[128,640]{1,0:T(8,128)(2,1)S(1)} collective-permute-done((bf16[128,640]{1,0:T(8,128)(2,1)S(1)}, bf16[128,640]{1,0:T(8,128)(2,1)S(1)}, u32[]{:S(2)}, u32[]{:S(2)}) %collective-permute-start.8) | collective-permute-done | bytes 163872 | tf_op jit(solution)/shard_map/ppermute | solution.py:404
  39.2 1.3 %final.1 = bf16[4,32,128]{2,1,0:T(8,128)(2,1)} custom-call(bf16[128,640]{1,0:T(8,128)(2,1)S(1)} %collective-permute-done.8.refs_0_, bf16[128,640]{1,0:T(8,128)(2,1)S(1)} %get-tuple-element.26.refs_1_, bf16[32,512,128]{2,1,0:T(8,128)(2,1)S(1)} %copy-done), custom_call_target="tpu_custom_call" | custom-call | tf_op jit(solution)/shard_map/final/pallas_call | solution.py:419
  (30 shorter events, 0.1 us)
Async XLA Ops:
  0.6 9.9 %copy-start.4 = (bf16[32,128,512]{2,1,0:T(8,128)(2,1)S(1)}, bf16[32,128,512]{2,1,0:T(8,128)(2,1)}, u32[]{:S(2)}) copy-start(bf16[32,128,512]{2,1,0:T(8,128)(2,1)} %w_ref.1) | copy-start | bytes 12582916
  0.6 1.1 %copy-start.5 = (bf16[4,64,576]{2,1,0:T(8,128)(2,1)S(1)}, bf16[4,64,576]{2,1,0:T(8,128)(2,1)}, u32[]{:S(2)}) copy-start(bf16[4,64,576]{2,1,0:T(8,128)(2,1)} %cache_ref.1) | copy-start | bytes 884740
  1.8 8.7 %copy-start.6 = (bf16[4,32,128]{2,1,0:T(8,128)(2,1)S(1)}, bf16[4,32,128]{2,1,0:T(8,128)(2,1)}, u32[]{:S(2)}) copy-start(bf16[4,32,128]{2,1,0:T(8,128)(2,1)} %param.9) | copy-start | bytes 98308
  1.8 8.7 %copy-start.7 = (bf16[4,32,64]{2,1,0:T(8,128)(2,1)S(1)}, bf16[4,32,64]{2,1,0:T(8,128)(2,1)}, u32[]{:S(2)}) copy-start(bf16[4,32,64]{2,1,0:T(8,128)(2,1)} %param.10) | copy-start | bytes 49156
  1.8 13.0 %slice-start = ((s8[4718592]{0:T(1024)(128)(4,1)}), s8[4194304]{0:T(1024)(128)(4,1)S(1)}, s32[]{:S(2)}) async-start(s8[4718592]{0:T(1024)(128)(4,1)} %bitcast.5), calls=%async_computation | async-start | bytes 8388608
  1.8 16.3 %collective-permute-start.4 = (bf16[128,1152]{1,0:T(8,128)(2,1)S(1)}, bf16[128,1152]{1,0:T(8,128)(2,1)S(1)}, u32[]{:S(2)}, u32[]{:S(2)}) collective-permute-start(bf16[128,1152]{1,0:T(8,128)(2,1)S(1)} %pack.1.refs_0_.refs_7_), channel_id=1, source_target_pairs={{1,2},{2,1},{5,6},{6,5},{9,10},{10,9},{13,14},{14,13},{17,18},{18,... | collective-permute-start | bytes 884744 | tf_op jit(solution)/shard_map/ppermute | solution.py:336
  2.7 15.5 %collective-permute-start.3 = (bf16[128,1152]{1,0:T(8,128)(2,1)S(1)}, bf16[128,1152]{1,0:T(8,128)(2,1)S(1)}, u32[]{:S(2)}, u32[]{:S(2)}) collective-permute-start(bf16[128,1152]{1,0:T(8,128)(2,1)S(1)} %pack.1.refs_0_.refs_7_), channel_id=1, source_target_pairs={{0,2},{3,1},{4,6},{7,5},{8,10},{11,9},{12,14},{15,13},{16,18},{19,... | collective-permute-start | bytes 884744 | tf_op jit(solution)/shard_map/ppermute | solution.py:335
  10.5 4.3 %slice-start.1 = ((s8[4718592]{0:T(1024)(128)(4,1)}), s8[524288]{0:T(1024)(128)(4,1)S(1)}, s32[]{:S(2)}) async-start(s8[4718592]{0:T(1024)(128)(4,1)} %bitcast.5), calls=%async_computation.1 | async-start | bytes 1048576
  10.5 2.8 %copy-start.2 = (s32[4]{0:T(128)S(1)}, s32[4]{0:T(128)}, u32[]{:S(2)}) copy-start(s32[4]{0:T(128)} %anc.1) | copy-start | bytes 52
  11.2 2.2 %collective-permute-start.5 = (bf16[128,576]{1,0:T(8,128)(2,1)S(1)}, bf16[128,576]{1,0:T(8,128)(2,1)S(1)}, u32[]{:S(2)}, u32[]{:S(2)}) collective-permute-start(bf16[128,576]{1,0:T(8,128)(2,1)S(1)} %project.1.refs_0_), channel_id=1, source_target_pairs={{0,4},{4,0},{8,12},{12,8},{1,5},{5,1},{9,13},{13,9},{2,6},{6,2},{1... | collective-permute-start | bytes 442376 | tf_op jit(solution)/shard_map/ppermute | solution.py:366
  11.2 12.0 %collective-permute-start.1 = (bf16[128,576]{1,0:T(8,128)(2,1)S(1)}, bf16[128,576]{1,0:T(8,128)(2,1)S(1)}, u32[]{:S(2)}, u32[]{:S(2)}) collective-permute-start(bf16[128,576]{1,0:T(8,128)(2,1)S(1)} %project.1.refs_0_), channel_id=1, source_target_pairs={{0,12},{4,8},{8,4},{12,0},{1,13},{5,9},{9,5},{13,1},{2,14},{6,10},... | collective-permute-start | bytes 442376 | tf_op jit(solution)/shard_map/ppermute | solution.py:366
  12.8 10.4 %collective-permute-start = (bf16[128,576]{1,0:T(8,128)(2,1)S(1)}, bf16[128,576]{1,0:T(8,128)(2,1)S(1)}, u32[]{:S(2)}, u32[]{:S(2)}) collective-permute-start(bf16[128,576]{1,0:T(8,128)(2,1)S(1)} %project.1.refs_0_), channel_id=1, source_target_pairs={{0,8},{4,12},{8,0},{12,4},{1,9},{5,13},{9,1},{13,5},{2,10},{6,14},... | collective-permute-start | bytes 442376 | tf_op jit(solution)/shard_map/ppermute | solution.py:366
  13.4 4.7 %collective-permute-start.2 = (s32[4]{0:T(128)S(1)}, s32[4]{0:T(128)S(1)}, u32[]{:S(2)}, u32[]{:S(2)}) collective-permute-start(s32[4]{0:T(128)S(1)} %copy-done.2), channel_id=1, source_target_pairs={{0,1},{3,2},{4,5},{7,6},{8,9},{11,10},{12,13},{15,14},{16,17},{19,... | collective-permute-start | bytes 56 | tf_op jit(solution)/shard_map/ppermute | solution.py:337
  19.2 10.2 %copy-start.3 = (s32[16]{0:T(128)S(1)}, s32[16]{0:T(128)}, u32[]{:S(2)}) copy-start(s32[16]{0:T(128)} %lens.1) | copy-start | bytes 196
  19.2 15.2 %copy-start.1 = (bf16[4,576]{1,0:T(4,128)(2,1)S(1)}, bf16[4,576]{1,0:T(4,128)(2,1)}, u32[]{:S(2)}) copy-start(bf16[4,576]{1,0:T(4,128)(2,1)} %fresh_ref.1) | copy-start | bytes 13828
  19.2 10.2 %collective-permute-start.6 = (bf16[128,1152]{1,0:T(8,128)(2,1)S(1)}, bf16[128,1152]{1,0:T(8,128)(2,1)S(1)}, u32[]{:S(2)}, u32[]{:S(2)}) collective-permute-start(bf16[128,1152]{1,0:T(8,128)(2,1)S(1)} %select.1), channel_id=1, source_target_pairs={{0,1},{1,0},{2,3},{3,2},{4,5},{5,4},{6,7},{7,6},{8,9},{9,8},{10,11... | collective-permute-start | bytes 884744 | tf_op jit(solution)/shard_map/ppermute | solution.py:385
  23.2 15.9 %copy-start = (bf16[32,512,128]{2,1,0:T(8,128)(2,1)S(1)}, bf16[32,512,128]{2,1,0:T(8,128)(2,1)}, u32[]{:S(2)}) copy-start(bf16[32,512,128]{2,1,0:T(8,128)(2,1)} %refs_2_.1) | copy-start | bytes 12582916
  31.2 1.5 %collective-permute-start.7 = (bf16[128,640]{1,0:T(8,128)(2,1)S(1)}, bf16[128,640]{1,0:T(8,128)(2,1)S(1)}, u32[]{:S(2)}, u32[]{:S(2)}) collective-permute-start(bf16[128,640]{1,0:T(8,128)(2,1)S(1)} %get-tuple-element.20), channel_id=1, source_target_pairs={{0,4},{4,0},{8,12},{12,8},{1,5},{5,1},{9,13},{13,9},{2,6},{6,2},{1... | collective-permute-start | bytes 491528 | tf_op jit(solution)/shard_map/ppermute | solution.py:403
  31.3 3.1 %collective-permute-start.10 = (bf16[256,576]{1,0:T(8,128)(2,1)S(1)}, bf16[256,576]{1,0:T(8,128)(2,1)S(1)}, u32[]{:S(2)}, u32[]{:S(2)}) collective-permute-start(bf16[256,576]{1,0:T(8,128)(2,1)S(1)} %get-tuple-element.25.refs_5_), channel_id=1, source_target_pairs={{0,4},{4,0},{8,12},{12,8},{1,5},{5,1},{9,13},{13,9},{2,6},{6,2},{1... | collective-permute-start | bytes 884744 | tf_op jit(solution)/shard_map/ppermute | solution.py:405
  31.8 2.6 %collective-permute-start.9 = (bf16[128,640]{1,0:T(8,128)(2,1)S(1)}, bf16[128,640]{1,0:T(8,128)(2,1)S(1)}, u32[]{:S(2)}, u32[]{:S(2)}) collective-permute-start(bf16[128,640]{1,0:T(8,128)(2,1)S(1)} %get-tuple-element.23), channel_id=1, source_target_pairs={{0,4},{4,0},{8,12},{12,8},{1,5},{5,1},{9,13},{13,9},{2,6},{6,2},{1... | collective-permute-start | bytes 491528 | tf_op jit(solution)/shard_map/ppermute | solution.py:373
  32.9 6.3 %collective-permute-start.8 = (bf16[128,640]{1,0:T(8,128)(2,1)S(1)}, bf16[128,640]{1,0:T(8,128)(2,1)S(1)}, u32[]{:S(2)}, u32[]{:S(2)}) collective-permute-start(bf16[128,640]{1,0:T(8,128)(2,1)S(1)} %chip_merge.1), channel_id=1, source_target_pairs={{8,0},{12,4},{0,8},{4,12},{9,1},{13,5},{1,9},{5,13},{10,2},{14,6},... | collective-permute-start | bytes 491528 | tf_op jit(solution)/shard_map/ppermute | solution.py:404

commit v16 on v15

--- a/solution.py
+++ b/solution.py
@@ -22,6 +22,7 @@
 ANY = pl.BlockSpec(memory_space=pl.ANY)
 HBM = pl.BlockSpec(memory_space=pltpu.HBM)
 PARAMS = pltpu.CompilerParams(vmem_limit_bytes=40 * 1024 * 1024)
+NO_COST = pl.CostEstimate(flops=0, bytes_accessed=0, transcendentals=0)
 PACK = 8_000_000_000
 PROJECT = 8_000_000_000
 
@@ -176,86 +177,104 @@
     return packed(acc * (1.0 / total), top + jnp.log2(total))
 
 
-def gather_blocks(block_refs, picks, out_ref, sems):
-    some = out_ref.shape[0] // len(picks)
-
-    def copy(p, k, slot):
-        return pltpu.make_async_copy(
-            block_refs[k].at[pl.ds(pl.multiple_of(slot * some, some), some)],
-            out_ref.at[pl.ds(p * some, some)],
-            sems.at[p],
-        )
-
-    for p, (which, slot) in enumerate(picks):
-        for k in range(len(block_refs)):
+def at_end(dom):
+    return (dom == 0) | (dom == 3)
+
+
+def gather_kernel(line, chosen, names, *refs):
+    block_refs, out_ref = refs[:-1], refs[-1]
+    if chosen:
+        block_refs = block_refs[:-1]
+    dom = lax.axis_index("dom")
+    local = names.shape[0]
+    some = out_ref.shape[0] // local
+    for p in range(local):
+        owner, slot = lax.div(names[p], local), lax.rem(names[p], local)
+        if line:
+            apart = jnp.bitwise_xor(owner, dom)
+            which = jnp.where(at_end(dom), 0, jnp.maximum(apart - 1, 0))
+            if chosen:
+                slot = jnp.where(at_end(dom), p, slot)
+        else:
+            which = lax.rem(dom - owner + len(block_refs), len(block_refs))
+        rows = pl.ds(pl.multiple_of(slot * some, some), some)
+        for k, block_ref in enumerate(block_refs):
 
             @pl.when(which == k)
             def _():
-                copy(p, k, slot).start()
-
-    for p in range(len(picks)):
-        copy(p, 0, 0).wait()
-
-
-def at_end(dom):
-    return (dom == 0) | (dom == 3)
-
-
-def select_kernel(theirs, *refs):
+                out_ref[pl.ds(p * some, some)] = block_ref[rows]
+
+
+def gathered(names, blocks, line, token=None):
+    token = [] if token is None else [token]
+    return pl.pallas_call(
+        functools.partial(gather_kernel, line, bool(token)),
+        out_shape=shape(blocks[0].shape),
+        in_specs=[SMEM] + [VMEM] * len(blocks) + [ANY] * len(token),
+        out_specs=VMEM,
+        compiler_params=PARAMS,
+        cost_estimate=NO_COST,
+        name="gather",
+    )(names, *blocks, *token)
+
+
+def far_part(anc, lens, query_ref, stage_refs, part, keys):
+    acc_ref, max_ref, sum_ref = stage_refs
+    local = anc.shape[0]
+    span, rank = keys.shape[0] // local, acc_ref.shape[1]
+    ends = [lens[anc[p]] for p in range(local)]
+    seen = visible(query_ref.shape[0], ends, [lax.axis_index("seq") * span], span)
+    known = [(max_ref[part, 0:1], sum_ref[part, 0:1], acc_ref[part])]
+    return attend(query_ref[...], keys, seen, rank, known)
+
+
+def give_kernel(stages, line, anc, lens, *refs):
+    stage_refs, refs = refs[: 4 * stages], refs[4 * stages :]
+    early_ref, late_ref, moved_ref, give_refs = refs[0], refs[1], refs[2], refs[3:]
     dom = lax.axis_index("dom")
-    block_refs, (_, out_ref, sems) = refs[:-3], refs[-3:]
-    local = sems.shape[0]
-    picks = []
+    local = anc.shape[0]
+    some = early_ref.shape[0] // local
+    span, width = 2 * some, moved_ref.shape[1]
+    rank = stage_refs[1].shape[1]
+
+    def place(p, value):
+        for h in range(2):
+            rows, rope = pl.ds(p * span + h * some, some), 2 * rank + h * (width - rank)
+            moved_ref[rows, :rank] = value[:, h * rank : (h + 1) * rank]
+            moved_ref[rows, rank:] = value[:, rope : rope + width - rank]
+
     for p in range(local):
-        apart = jnp.bitwise_xor(lax.div(theirs[p], local), dom)
-        which = jnp.where(at_end(dom), 0, jnp.maximum(apart - 1, 0))
-        picks.append((which, jnp.where(at_end(dom), p, lax.rem(theirs[p], local))))
-    gather_blocks(block_refs, picks, out_ref, sems)
-
-
-def far_kernel(stages, sources, line, *refs):
-    anc, lens = refs[:2]
-    refs = refs[2:]
-    seq, dom = lax.axis_index("seq"), lax.axis_index("dom")
-    stage_refs, refs = refs[: 5 * stages], refs[5 * stages :]
-    block_refs, refs = refs[:sources], refs[sources:]
-    moved_ref, refs = refs[0], refs[1:]
-    keep_refs, give_refs = refs[:stages], refs[stages : 2 * stages]
-    raw, sems = refs[2 * stages :]
-    local = sems.shape[0]
-    some = raw.shape[0] // local
-    span, width = 2 * some, moved_ref.shape[1]
-    rank = stage_refs[2].shape[1]
-
-    picks = []
-    for p in range(local):
-        owner, slot = lax.div(anc[p], local), lax.rem(anc[p], local)
         if line:
-            which = jnp.bitwise_xor(owner, dom)
-            chosen = at_end(dom) & (which != 0)
-            which = jnp.where(chosen, 1, which)
-            slot = jnp.where(chosen, p, slot)
+            owner, slot = lax.div(anc[p], local), lax.rem(anc[p], local)
+            apart = jnp.bitwise_xor(owner, dom)
+            late = jnp.where(at_end(dom), apart != 0, apart == 1)
+            slot = jnp.where(at_end(dom), p, slot)
+            rows = pl.ds(pl.multiple_of(slot * some, some), some)
+
+            @pl.when(late)
+            def _():
+                place(p, late_ref[rows])
+
+            @pl.when(jnp.logical_not(late))
+            def _():
+                place(p, early_ref[pl.ds(p * some, some)])
+
         else:
-            which = lax.rem(dom - owner + sources, sources)
-        picks.append((which, slot))
-    gather_blocks(block_refs, picks, raw, sems)
-    for p in range(local):
-        for h in range(2):
-            part, rows = pl.ds(p * some, some), pl.ds(p * span + h * some, some)
-            rope = 2 * rank + h * (width - rank)
-            moved_ref[rows, :rank] = raw[part, h * rank : (h + 1) * rank]
-            moved_ref[rows, rank:] = raw[part, rope : rope + width - rank]
-
-    ends = [lens[anc[p]] for p in range(local)]
+            place(p, early_ref[pl.ds(p * some, some)])
+
     for k in range(stages):
-        first_ref, second_ref, acc_ref, max_ref, sum_ref = stage_refs[5 * k : 5 * k + 5]
-        queries = jnp.concatenate([first_ref[...], second_ref[...]], axis=0)
-        seen = visible(queries.shape[0], ends, [seq * span], span)
-        known = [(max_ref[:, 0:1], sum_ref[:, 0:1], acc_ref[...])]
-        part = attend(queries, moved_ref[...], seen, rank, known)
-        rows = first_ref.shape[0]
-        keep_refs[k][...] = part[:rows]
-        give_refs[k][...] = part[rows:]
+        query_ref, *partial = stage_refs[4 * k : 4 * k + 4]
+        rows = query_ref.shape[0]
+        give_refs[k][...] = far_part(anc, lens, query_ref, partial, pl.ds(rows, rows), moved_ref[...])
+
+
+def keep_kernel(stages, anc, lens, *refs):
+    stage_refs, refs = refs[: 4 * stages], refs[4 * stages :]
+    moved_ref, keep_refs = refs[0], refs[1:]
+    for k in range(stages):
+        query_ref, *partial = stage_refs[4 * k : 4 * k + 4]
+        rows = query_ref.shape[0]
+        keep_refs[k][...] = far_part(anc, lens, query_ref, partial, pl.ds(0, rows), moved_ref[...])
 
 
 def near_kernel(anc, lens, fresh_ref, *refs):
@@ -372,34 +391,32 @@
         if t == 0:
             given = lax.ppermute(stage.pop(), "seq", pairs(0, 1))
         if line and t == 0:
-            chosen = pl.pallas_call(
-                select_kernel,
-                out_shape=shape(block.shape),
-                in_specs=[SMEM] + [ANY] * 4,
-                out_specs=VMEM,
-                scratch_shapes=[pltpu.SemaphoreType.DMA((local,))],
-                compiler_params=PARAMS,
-                cost_estimate=pl.CostEstimate(flops=0, bytes_accessed=0, transcendentals=0),
-                name="select",
-            )(theirs, block, middle, far, stage[3])
-            blocks = [block, lax.ppermute(chosen, "dom", swap), middle, far]
+            chosen = gathered(theirs, [block, middle, far], line, stage[3])
+            late = lax.ppermute(chosen, "dom", swap)
+            early = gathered(ancestors, [block, middle, far], line)
+    if not line:
+        early = late = gathered(ancestors, blocks, line)
 
     part = shape((rows, rank + LANES))
     others = chips - 1
-    far_results = pl.pallas_call(
-        functools.partial(far_kernel, others, len(blocks), line),
-        out_shape=[shape((local * span, width))] + [part] * (2 * others),
-        in_specs=[SMEM] * 2 + [VMEM] * (5 * others) + [ANY] * len(blocks),
-        out_specs=[VMEM] * (1 + 2 * others),
-        scratch_shapes=[
-            pltpu.VMEM(block.shape, BF16),
-            pltpu.SemaphoreType.DMA((local,)),
-        ],
-        compiler_params=PARAMS,
-        name="suffix_far",
-    )(ancestors, lengths, *[a for stage in stages[1:] for a in stage], *blocks)
-    moved = far_results[0]
-    keep, give = far_results[1 : 1 + others], far_results[1 + others :]
+    giving = [a for stage in stages[1:] for a in stage[1:]]
+    keeping = [a for stage in stages[1:] for a in (stage[0], *stage[2:])]
+    moved, *give = pl.pallas_call(
+        functools.partial(give_kernel, others, line),
+        out_shape=[shape((local * span, width))] + [part] * others,
+        in_specs=[SMEM] * 2 + [VMEM] * (len(giving) + 2),
+        out_specs=[VMEM] * (1 + others),
+        compiler_params=PARAMS,
+        name="suffix_give",
+    )(ancestors, lengths, *giving, early, late)
+    keep = pl.pallas_call(
+        functools.partial(keep_kernel, others),
+        out_shape=[part] * others,
+        in_specs=[SMEM] * 2 + [VMEM] * (len(keeping) + 1),
+        out_specs=[VMEM] * others,
+        compiler_params=PARAMS,
+        name="suffix_keep",
+    )(ancestors, lengths, *keeping, moved)
     sums = chip_merge(keep, [lax.ppermute(g, "seq", pairs(0, 1)) for g in give])
     parts = [lax.ppermute(s, "seq", back(t, 0)) for t, s in enumerate(sums, 1)]
     other = lax.ppermute(moved, "seq", pairs(0, 1))

time: 40.7 us -> 40.6 us (level)
  waiting for transfers between devices: 6.85 us -> 5.66 us
  Pallas kernels: 13.3 us -> 14.3 us
    pallas_call x2 -> x4, Pallas kernels: 2.87 us -> 3.92 us  [the longest x1 1.45 us: on_device(): pl.pallas_call(functools.partial(give_kernel, others, line), out_shape=[s...]
    ppermute x1, waiting for transfers between devices: 0.81 us -> 0.01 us  [on_device(): sums = chip_merge(keep, [lax.ppermute(g, 'seq', pairs(0, 1)) for g in give])]
    ppermute x1, waiting for transfers between devices: 2.86 us -> 2.18 us  [on_device(): late = lax.ppermute(chosen, 'dom', swap)]
  transfers between devices with their start and end apart: 11 -> 11, of which waited for: 3 -> 2; matrix products, arithmetic and copies ran while one was open for 0% -> 0% of each run, Pallas kernels for 25% -> 28%
where the time goes in v16:
time: 40.6 us; the launch traced here: 40.4 us
  starting transfers between devices  18.3 us (45%)
  Pallas kernels  14.3 us (35%)
  waiting for transfers between devices  5.66 us (14%)
  local copies, waits for them, and re-layouts  1.2 us (3%)
  between operations  0.88 us (2%)
    ppermute x1, starting transfers between devices, on_device(): middle = lax.ppermute(block, 'dom', [(0, 2), (3, 1)])  7.77 us
    pallas_call x2, Pallas kernels, prefix_attention(): pl.pallas_call(functools.partial(prefix_kernel, len(queries), tiles), out...  6.57 us
    ppermute x1, starting transfers between devices, on_device(): late = lax.ppermute(chosen, 'dom', swap)  4.03 us
    ppermute x1, waiting for transfers between devices, on_device(): parts = [lax.ppermute(s, 'seq', back(t, 0)) for t, s in enumerate(sums, 1)]  3.46 us
    ppermute x1, waiting for transfers between devices, on_device(): late = lax.ppermute(chosen, 'dom', swap)  2.18 us
    ppermute x3, starting transfers between devices, on_device(): lax.ppermute(own, 'seq', pairs(*r))  2.15 us
    pallas_call x1, Pallas kernels, on_device(): pl.pallas_call(near_kernel, out_shape=[shape(private_caches.shape), part]...  1.59 us
    ppermute x1, starting transfers between devices, on_device(): parts = [lax.ppermute(s, 'seq', back(t, 0)) for t, s in enumerate(sums, 1)]  1.56 us
  transfers between devices with their start and end apart: 11, of which 2 were waited for; matrix products, arithmetic and copies ran while one was open for 0% of the time, Pallas kernels for 28%

profile of v16, /device:TPU:0, one launch (start us, length us, event | category | flops | bytes accessed | tf_op | source)
XLA Modules:
  0.0 40.4 jit_solution(13790067228344812668)
XLA Ops:
  0.7 1.1 %copy-done.5 = bf16[4,64,576]{2,1,0:T(8,128)(2,1)S(1)} copy-done((bf16[4,64,576]{2,1,0:T(8,128)(2,1)S(1)}, bf16[4,64,576]{2,1,0:T(8,128)(2,1)}, u32[]{:S(2)}) %copy-start.5) | copy-done | bytes 294936
  1.8 0.1 pack.1.refs_0_
  1.8 0.8 %collective-permute-start.3 = (bf16[128,1152]{1,0:T(8,128)(2,1)S(1)}, bf16[128,1152]{1,0:T(8,128)(2,1)S(1)}, u32[]{:S(2)}, u32[]{:S(2)}) collective-permute-start(bf16[128,1152]{1,0:T(8,128)(2,1)S(1)} %pack.1.refs_0_), channel_id=1, source_target_pairs={{1,2},{2,1},{5,6},{6,5},{9,10},{10,9},{13,14},{14,13},{17,18},{18,... | collective-permute-start | bytes 884744 | tf_op jit(solution)/shard_map/ppermute | solution.py:355
  2.7 7.8 %collective-permute-start.2 = (bf16[128,1152]{1,0:T(8,128)(2,1)S(1)}, bf16[128,1152]{1,0:T(8,128)(2,1)S(1)}, u32[]{:S(2)}, u32[]{:S(2)}) collective-permute-start(bf16[128,1152]{1,0:T(8,128)(2,1)S(1)} %pack.1.refs_0_), channel_id=1, source_target_pairs={{0,2},{3,1},{4,6},{7,5},{8,10},{11,9},{12,14},{15,13},{16,18},{19,... | collective-permute-start | bytes 884744 | tf_op jit(solution)/shard_map/ppermute | solution.py:354
  10.5 0.6 %project.1.refs_0_ = bf16[128,576]{1,0:T(8,128)(2,1)S(1)} custom-call(bf16[128,128]{1,0:T(8,128)(2,1)S(1)} %bitcast.9, bf16[128,64]{1,0:T(8,128)(2,1)S(1)} %bitcast.10, bf16[32,128,512]{2,1,0:T(8,128)(2,1)S(1)} %copy-done.4), custom_call_target="tpu_custom_call" | custom-call | flops 8000000000 | tf_op jit(solution)/shard_map/project/pallas_call | solution.py:363
  11.2 1.6 %collective-permute-start.1 = (bf16[128,576]{1,0:T(8,128)(2,1)S(1)}, bf16[128,576]{1,0:T(8,128)(2,1)S(1)}, u32[]{:S(2)}, u32[]{:S(2)}) collective-permute-start(bf16[128,576]{1,0:T(8,128)(2,1)S(1)} %project.1.refs_0_), channel_id=1, source_target_pairs={{0,12},{4,8},{8,4},{12,0},{1,13},{5,9},{9,5},{13,1},{2,14},{6,10},... | collective-permute-start | bytes 442376 | tf_op jit(solution)/shard_map/ppermute | solution.py:385
  12.8 0.5 %collective-permute-start = (bf16[128,576]{1,0:T(8,128)(2,1)S(1)}, bf16[128,576]{1,0:T(8,128)(2,1)S(1)}, u32[]{:S(2)}, u32[]{:S(2)}) collective-permute-start(bf16[128,576]{1,0:T(8,128)(2,1)S(1)} %project.1.refs_0_), channel_id=1, source_target_pairs={{0,8},{4,12},{8,0},{12,4},{1,9},{5,13},{9,1},{13,5},{2,10},{6,14},... | collective-permute-start | bytes 442376 | tf_op jit(solution)/shard_map/ppermute | solution.py:385
  13.4 1.4 %collective-permute-start.4 = (s32[4]{0:T(128)S(1)}, s32[4]{0:T(128)S(1)}, u32[]{:S(2)}, u32[]{:S(2)}) collective-permute-start(s32[4]{0:T(128)S(1)} %copy-done.1), channel_id=1, source_target_pairs={{0,1},{3,2},{4,5},{7,6},{8,9},{11,10},{12,13},{15,14},{16,17},{19,... | collective-permute-start | bytes 56 | tf_op jit(solution)/shard_map/ppermute | solution.py:356
  14.8 3.3 %prefix_attention.3 = (f32[128,512]{1,0:T(8,128)S(1)}, f32[128,128]{1,0:T(8,128)S(1)}, f32[128,128]{1,0:T(8,128)S(1)}, bf16[128,640]{1,0:T(8,128)(2,1)S(1)}) custom-call(bf16[128,576]{1,0:T(8,128)(2,1)S(1)} %project.1.refs_0_, bf16[128,576]{1,0:T(8,128)(2,1)S(1)} %collective-permute-done.5.refs_1_, bf16[576,4096]{1,0:T(8,128)(2,1)S(1)} %bitcast.7), custom_call_target="tpu_custom_call" | custom-call | tf_op jit(solution)/shard_map/prefix_attention/pallas_call | solution.py:111
  18.1 0.7 %gather.3 = bf16[128,1152]{1,0:T(8,128)(2,1)S(1)} custom-call(s32[4]{0:T(128)S(1)} %collective-permute-done.4.names, bf16[128,1152]{1,0:T(8,128)(2,1)S(1)} %pack.1.refs_0_, bf16[128,1152]{1,0:T(8,128)(2,1)S(1)} %collective-permute-done.2.refs_1_, bf16[128,1152]{1,0:T(8,128)(2,1)S(1)} %collective-permute-done.3.refs_2_, ...), custom_call_target="tpu_custom_call" | custom-call | tf_op jit(solution)/shard_map/gather/pallas_call | solution.py:210
  18.8 4.0 %collective-permute-start.6 = (bf16[128,1152]{1,0:T(8,128)(2,1)S(1)}, bf16[128,1152]{1,0:T(8,128)(2,1)S(1)}, u32[]{:S(2)}, u32[]{:S(2)}) collective-permute-start(bf16[128,1152]{1,0:T(8,128)(2,1)S(1)} %gather.3), channel_id=1, source_target_pairs={{0,1},{1,0},{2,3},{3,2},{4,5},{5,4},{6,7},{7,6},{8,9},{9,8},{10,11... | collective-permute-start | bytes 884744 | tf_op jit(solution)/shard_map/ppermute | solution.py:395
  22.8 3.3 %prefix_attention.2 = (f32[256,512]{1,0:T(8,128)S(1)}, f32[256,128]{1,0:T(8,128)S(1)}, f32[256,128]{1,0:T(8,128)S(1)}) custom-call(bf16[128,576]{1,0:T(8,128)(2,1)S(1)} %collective-permute-done.refs_0_, bf16[128,576]{1,0:T(8,128)(2,1)S(1)} %collective-permute-done.1.refs_1_.refs_0_, bf16[576,4096]{1,0:T(8,128)(2,1)S(1)} %bitcast.8), custom_call_target="tpu_custom_call" | custom-call | flops 2281701376 | bytes 4718592 | tf_op jit(solution)/shard_map/prefix_attention/pallas_call | solution.py:111
  26.1 0.7 %gather.2.refs_4_ = bf16[128,1152]{1,0:T(8,128)(2,1)S(1)} custom-call(s32[4]{0:T(128)S(1)} %copy-done.1, bf16[128,1152]{1,0:T(8,128)(2,1)S(1)} %pack.1.refs_0_, bf16[128,1152]{1,0:T(8,128)(2,1)S(1)} %collective-permute-done.2.refs_1_, bf16[128,1152]{1,0:T(8,128)(2,1)S(1)} %collective-permute-done.3.refs_2_), custom_call_target="tpu_custom_call" | custom-call | tf_op jit(solution)/shard_map/gather/pallas_call | solution.py:210
  26.8 2.2 %collective-permute-done.6.refs_5_ = bf16[128,1152]{1,0:T(8,128)(2,1)S(1)} collective-permute-done((bf16[128,1152]{1,0:T(8,128)(2,1)S(1)}, bf16[128,1152]{1,0:T(8,128)(2,1)S(1)}, u32[]{:S(2)}, u32[]{:S(2)}) %collective-permute-start.6) | collective-permute-done | bytes 294944 | tf_op jit(solution)/shard_map/ppermute | solution.py:395
  29.0 1.5 %suffix_give.1 = (bf16[256,576]{1,0:T(8,128)(2,1)S(1)}, bf16[128,640]{1,0:T(8,128)(2,1)S(1)}) custom-call(s32[4]{0:T(128)S(1)} %copy-done.1, s32[16]{0:T(128)S(1)} %copy-done.3, bf16[128,576]{1,0:T(8,128)(2,1)S(1)} %collective-permute-done.1.refs_1_.refs_0_, f32[256,512]{1,0:T(8,128)S(1)} %get-tuple-element.14.refs_1_, ...), custom_call_target="tpu_custom_call" | custom-call | tf_op jit(solution)/shard_map/suffix_give/pallas_call | solution.py:404
  30.4 0.1 collective-permute-start.7
  30.5 0.5 %collective-permute-start.10 = (bf16[256,576]{1,0:T(8,128)(2,1)S(1)}, bf16[256,576]{1,0:T(8,128)(2,1)S(1)}, u32[]{:S(2)}, u32[]{:S(2)}) collective-permute-start(bf16[256,576]{1,0:T(8,128)(2,1)S(1)} %get-tuple-element.23.refs_4_.refs_5_), channel_id=1, source_target_pairs={{0,4},{4,0},{8,12},{12,8},{1,5},{5,1},{9,13},{13,9},{2,6},{6,2},{1... | collective-permute-start | bytes 884744 | tf_op jit(solution)/shard_map/ppermute | solution.py:422
  31.0 0.1 collective-permute-start.9
  31.1 1.1 %suffix_keep.1.refs_0_ = bf16[128,640]{1,0:T(8,128)(2,1)S(1)} custom-call(s32[4]{0:T(128)S(1)} %copy-done.1, s32[16]{0:T(128)S(1)} %copy-done.3, bf16[128,576]{1,0:T(8,128)(2,1)S(1)} %collective-permute-done.refs_0_, f32[256,512]{1,0:T(8,128)S(1)} %get-tuple-element.14.refs_1_, f32[256,128]{1,0:T(8,128)S(1)} %get-tuple-element.15.refs_2_, ...), custom_call_target="tpu_custom_call" | custom-call | tf_op jit(solution)/shard_map/suffix_keep/pallas_call | solution.py:412
  32.3 0.2 chip_merge.1
  32.5 1.6 %collective-permute-start.8 = (bf16[128,640]{1,0:T(8,128)(2,1)S(1)}, bf16[128,640]{1,0:T(8,128)(2,1)S(1)}, u32[]{:S(2)}, u32[]{:S(2)}) collective-permute-start(bf16[128,640]{1,0:T(8,128)(2,1)S(1)} %chip_merge.1), channel_id=1, source_target_pairs={{8,0},{12,4},{0,8},{4,12},{9,1},{13,5},{1,9},{5,13},{10,2},{14,6},... | collective-permute-start | bytes 491528 | tf_op jit(solution)/shard_map/ppermute | solution.py:421
  34.0 1.6 %suffix_near.1 = (bf16[4,64,576]{2,1,0:T(8,128)(2,1)}, bf16[128,640]{1,0:T(8,128)(2,1)S(1)}) custom-call(s32[4]{0:T(128)S(1)} %copy-done.1, s32[16]{0:T(128)S(1)} %copy-done.3, bf16[4,576]{1,0:T(4,128)(2,1)S(1)} %copy-done.2, bf16[128,576]{1,0:T(8,128)(2,1)S(1)} %project.1.refs_0_, f32[128,512]{1,0:T(8,128)S(1)} %get-tuple-element.20.refs_1_, ...), custom_call_target="tpu_custom_call" | custom-call | tf_op jit(solution)/shard_map/suffix_near/pallas_call | solution.py:426
  35.6 3.5 %collective-permute-done.8.refs_0_ = bf16[128,640]{1,0:T(8,128)(2,1)S(1)} collective-permute-done((bf16[128,640]{1,0:T(8,128)(2,1)S(1)}, bf16[128,640]{1,0:T(8,128)(2,1)S(1)}, u32[]{:S(2)}, u32[]{:S(2)}) %collective-permute-start.8) | collective-permute-done | bytes 163872 | tf_op jit(solution)/shard_map/ppermute | solution.py:421
  39.1 1.4 %final.1 = bf16[4,32,128]{2,1,0:T(8,128)(2,1)} custom-call(bf16[128,640]{1,0:T(8,128)(2,1)S(1)} %collective-permute-done.8.refs_0_, bf16[128,640]{1,0:T(8,128)(2,1)S(1)} %get-tuple-element.24.refs_1_, bf16[32,512,128]{2,1,0:T(8,128)(2,1)S(1)} %copy-done), custom_call_target="tpu_custom_call" | custom-call | tf_op jit(solution)/shard_map/final/pallas_call | solution.py:436
  (32 shorter events, 0.1 us)
Async XLA Ops:
  0.6 9.9 %copy-start.4 = (bf16[32,128,512]{2,1,0:T(8,128)(2,1)S(1)}, bf16[32,128,512]{2,1,0:T(8,128)(2,1)}, u32[]{:S(2)}) copy-start(bf16[32,128,512]{2,1,0:T(8,128)(2,1)} %w_ref.1) | copy-start | bytes 12582916
  0.6 1.1 %copy-start.5 = (bf16[4,64,576]{2,1,0:T(8,128)(2,1)S(1)}, bf16[4,64,576]{2,1,0:T(8,128)(2,1)}, u32[]{:S(2)}) copy-start(bf16[4,64,576]{2,1,0:T(8,128)(2,1)} %cache_ref.1) | copy-start | bytes 884740
  1.8 8.7 %copy-start.6 = (bf16[4,32,128]{2,1,0:T(8,128)(2,1)S(1)}, bf16[4,32,128]{2,1,0:T(8,128)(2,1)}, u32[]{:S(2)}) copy-start(bf16[4,32,128]{2,1,0:T(8,128)(2,1)} %param.9) | copy-start | bytes 98308
  1.8 8.7 %copy-start.7 = (bf16[4,32,64]{2,1,0:T(8,128)(2,1)S(1)}, bf16[4,32,64]{2,1,0:T(8,128)(2,1)}, u32[]{:S(2)}) copy-start(bf16[4,32,64]{2,1,0:T(8,128)(2,1)} %param.10) | copy-start | bytes 49156
  1.8 13.0 %slice-start = ((s8[4718592]{0:T(1024)(128)(4,1)}), s8[4194304]{0:T(1024)(128)(4,1)S(1)}, s32[]{:S(2)}) async-start(s8[4718592]{0:T(1024)(128)(4,1)} %bitcast.5), calls=%async_computation | async-start | bytes 8388608
  1.8 16.3 %collective-permute-start.3 = (bf16[128,1152]{1,0:T(8,128)(2,1)S(1)}, bf16[128,1152]{1,0:T(8,128)(2,1)S(1)}, u32[]{:S(2)}, u32[]{:S(2)}) collective-permute-start(bf16[128,1152]{1,0:T(8,128)(2,1)S(1)} %pack.1.refs_0_), channel_id=1, source_target_pairs={{1,2},{2,1},{5,6},{6,5},{9,10},{10,9},{13,14},{14,13},{17,18},{18,... | collective-permute-start | bytes 884744 | tf_op jit(solution)/shard_map/ppermute | solution.py:355
  2.7 15.5 %collective-permute-start.2 = (bf16[128,1152]{1,0:T(8,128)(2,1)S(1)}, bf16[128,1152]{1,0:T(8,128)(2,1)S(1)}, u32[]{:S(2)}, u32[]{:S(2)}) collective-permute-start(bf16[128,1152]{1,0:T(8,128)(2,1)S(1)} %pack.1.refs_0_), channel_id=1, source_target_pairs={{0,2},{3,1},{4,6},{7,5},{8,10},{11,9},{12,14},{15,13},{16,18},{19,... | collective-permute-start | bytes 884744 | tf_op jit(solution)/shard_map/ppermute | solution.py:354
  10.5 4.3 %slice-start.1 = ((s8[4718592]{0:T(1024)(128)(4,1)}), s8[524288]{0:T(1024)(128)(4,1)S(1)}, s32[]{:S(2)}) async-start(s8[4718592]{0:T(1024)(128)(4,1)} %bitcast.5), calls=%async_computation.1 | async-start | bytes 1048576
  10.5 2.8 %copy-start.1 = (s32[4]{0:T(128)S(1)}, s32[4]{0:T(128)}, u32[]{:S(2)}) copy-start(s32[4]{0:T(128)} %anc.5) | copy-start | bytes 52
  11.2 2.2 %collective-permute-start.5 = (bf16[128,576]{1,0:T(8,128)(2,1)S(1)}, bf16[128,576]{1,0:T(8,128)(2,1)S(1)}, u32[]{:S(2)}, u32[]{:S(2)}) collective-permute-start(bf16[128,576]{1,0:T(8,128)(2,1)S(1)} %project.1.refs_0_), channel_id=1, source_target_pairs={{0,4},{4,0},{8,12},{12,8},{1,5},{5,1},{9,13},{13,9},{2,6},{6,2},{1... | collective-permute-start | bytes 442376 | tf_op jit(solution)/shard_map/ppermute | solution.py:385
  11.2 11.6 %collective-permute-start.1 = (bf16[128,576]{1,0:T(8,128)(2,1)S(1)}, bf16[128,576]{1,0:T(8,128)(2,1)S(1)}, u32[]{:S(2)}, u32[]{:S(2)}) collective-permute-start(bf16[128,576]{1,0:T(8,128)(2,1)S(1)} %project.1.refs_0_), channel_id=1, source_target_pairs={{0,12},{4,8},{8,4},{12,0},{1,13},{5,9},{9,5},{13,1},{2,14},{6,10},... | collective-permute-start | bytes 442376 | tf_op jit(solution)/shard_map/ppermute | solution.py:385
  12.8 10.0 %collective-permute-start = (bf16[128,576]{1,0:T(8,128)(2,1)S(1)}, bf16[128,576]{1,0:T(8,128)(2,1)S(1)}, u32[]{:S(2)}, u32[]{:S(2)}) collective-permute-start(bf16[128,576]{1,0:T(8,128)(2,1)S(1)} %project.1.refs_0_), channel_id=1, source_target_pairs={{0,8},{4,12},{8,0},{12,4},{1,9},{5,13},{9,1},{13,5},{2,10},{6,14},... | collective-permute-start | bytes 442376 | tf_op jit(solution)/shard_map/ppermute | solution.py:385
  13.4 4.7 %collective-permute-start.4 = (s32[4]{0:T(128)S(1)}, s32[4]{0:T(128)S(1)}, u32[]{:S(2)}, u32[]{:S(2)}) collective-permute-start(s32[4]{0:T(128)S(1)} %copy-done.1), channel_id=1, source_target_pairs={{0,1},{3,2},{4,5},{7,6},{8,9},{11,10},{12,13},{15,14},{16,17},{19,... | collective-permute-start | bytes 56 | tf_op jit(solution)/shard_map/ppermute | solution.py:356
  18.8 10.2 %copy-start.3 = (s32[16]{0:T(128)S(1)}, s32[16]{0:T(128)}, u32[]{:S(2)}) copy-start(s32[16]{0:T(128)} %lens.5) | copy-start | bytes 196
  18.8 10.2 %collective-permute-start.6 = (bf16[128,1152]{1,0:T(8,128)(2,1)S(1)}, bf16[128,1152]{1,0:T(8,128)(2,1)S(1)}, u32[]{:S(2)}, u32[]{:S(2)}) collective-permute-start(bf16[128,1152]{1,0:T(8,128)(2,1)S(1)} %gather.3), channel_id=1, source_target_pairs={{0,1},{1,0},{2,3},{3,2},{4,5},{5,4},{6,7},{7,6},{8,9},{9,8},{10,11... | collective-permute-start | bytes 884744 | tf_op jit(solution)/shard_map/ppermute | solution.py:395
  26.1 7.9 %copy-start.2 = (bf16[4,576]{1,0:T(4,128)(2,1)S(1)}, bf16[4,576]{1,0:T(4,128)(2,1)}, u32[]{:S(2)}) copy-start(bf16[4,576]{1,0:T(4,128)(2,1)} %fresh_ref.1) | copy-start | bytes 13828
  26.1 13.0 %copy-start = (bf16[32,512,128]{2,1,0:T(8,128)(2,1)S(1)}, bf16[32,512,128]{2,1,0:T(8,128)(2,1)}, u32[]{:S(2)}) copy-start(bf16[32,512,128]{2,1,0:T(8,128)(2,1)} %refs_2_.1) | copy-start | bytes 12582916
  30.4 1.8 %collective-permute-start.7 = (bf16[128,640]{1,0:T(8,128)(2,1)S(1)}, bf16[128,640]{1,0:T(8,128)(2,1)S(1)}, u32[]{:S(2)}, u32[]{:S(2)}) collective-permute-start(bf16[128,640]{1,0:T(8,128)(2,1)S(1)} %get-tuple-element.19), channel_id=1, source_target_pairs={{0,4},{4,0},{8,12},{12,8},{1,5},{5,1},{9,13},{13,9},{2,6},{6,2},{1... | collective-permute-start | bytes 491528 | tf_op jit(solution)/shard_map/ppermute | solution.py:420
  30.5 3.5 %collective-permute-start.10 = (bf16[256,576]{1,0:T(8,128)(2,1)S(1)}, bf16[256,576]{1,0:T(8,128)(2,1)S(1)}, u32[]{:S(2)}, u32[]{:S(2)}) collective-permute-start(bf16[256,576]{1,0:T(8,128)(2,1)S(1)} %get-tuple-element.23.refs_4_.refs_5_), channel_id=1, source_target_pairs={{0,4},{4,0},{8,12},{12,8},{1,5},{5,1},{9,13},{13,9},{2,6},{6,2},{1... | collective-permute-start | bytes 884744 | tf_op jit(solution)/shard_map/ppermute | solution.py:422
  31.0 3.0 %collective-permute-start.9 = (bf16[128,640]{1,0:T(8,128)(2,1)S(1)}, bf16[128,640]{1,0:T(8,128)(2,1)S(1)}, u32[]{:S(2)}, u32[]{:S(2)}) collective-permute-start(bf16[128,640]{1,0:T(8,128)(2,1)S(1)} %get-tuple-element.22), channel_id=1, source_target_pairs={{0,4},{4,0},{8,12},{12,8},{1,5},{5,1},{9,13},{13,9},{2,6},{6,2},{1... | collective-permute-start | bytes 491528 | tf_op jit(solution)/shard_map/ppermute | solution.py:392
  32.5 6.6 %collective-permute-start.8 = (bf16[128,640]{1,0:T(8,128)(2,1)S(1)}, bf16[128,640]{1,0:T(8,128)(2,1)S(1)}, u32[]{:S(2)}, u32[]{:S(2)}) collective-permute-start(bf16[128,640]{1,0:T(8,128)(2,1)S(1)} %chip_merge.1), channel_id=1, source_target_pairs={{8,0},{12,4},{0,8},{4,12},{9,1},{13,5},{1,9},{5,13},{10,2},{14,6},... | collective-permute-start | bytes 491528 | tf_op jit(solution)/shard_map/ppermute | solution.py:421

commit v17 on v16

--- a/solution.py
+++ b/solution.py
@@ -134,15 +134,23 @@
     return jnp.concatenate([values.astype(BF16), stats.astype(BF16)], axis=1)
 
 
-def merged(parts, rank):
-    levels = [jnp.sum(part[:, rank:].astype(F32), axis=1, keepdims=True) for part in parts]
+def unpacked(part):
+    rank = part.shape[1] - LANES
+    return part[:, :rank].astype(F32), jnp.sum(part[:, rank:].astype(F32), axis=1, keepdims=True)
+
+
+def merged(parts):
+    levels = [level for _, level in parts]
     top = functools.reduce(jnp.maximum, levels)
     shares = [jnp.exp2(level - top) for level in levels]
     whole = functools.reduce(jnp.add, shares)
-    acc = functools.reduce(
-        jnp.add, [share * part[:, :rank].astype(F32) for share, part in zip(shares, parts)]
-    )
+    acc = functools.reduce(jnp.add, [share * values for share, (values, _) in zip(shares, parts)])
     return acc * (1.0 / whole), top + jnp.log2(whole)
+
+
+def diagonal(rows, lanes):
+    row = lax.broadcasted_iota(jnp.int32, (rows, lanes), 0)
+    return row == lax.broadcasted_iota(jnp.int32, (rows, lanes), 1)
 
 
 def visible(rows, ends, starts, span):
@@ -174,7 +182,7 @@
         factor = jnp.exp2(level - top)
         total = total + mass * factor
         acc = acc + part * factor
-    return packed(acc * (1.0 / total), top + jnp.log2(total))
+    return acc * (1.0 / total), top + jnp.log2(total)
 
 
 def at_end(dom):
@@ -225,7 +233,7 @@
     ends = [lens[anc[p]] for p in range(local)]
     seen = visible(query_ref.shape[0], ends, [lax.axis_index("seq") * span], span)
     known = [(max_ref[part, 0:1], sum_ref[part, 0:1], acc_ref[part])]
-    return attend(query_ref[...], keys, seen, rank, known)
+    return packed(*attend(query_ref[...], keys, seen, rank, known))
 
 
 def give_kernel(stages, line, anc, lens, *refs):
@@ -279,7 +287,7 @@
 
 def near_kernel(anc, lens, fresh_ref, *refs):
     seq = lax.axis_index("seq")
-    query_ref, acc_ref, max_ref, sum_ref, got_ref, moved_ref, other_ref, cache_ref, part_ref = refs
+    query_ref, acc_ref, max_ref, sum_ref, got_ref, moved_ref, other_ref, cache_ref, value_ref, level_ref = refs
     local, span, width = cache_ref.shape
     rank = acc_ref.shape[1]
     start, other = seq * span, jnp.bitwise_xor(seq, 1) * span
@@ -291,7 +299,9 @@
         (max_ref[:, 0:1], sum_ref[:, 0:1], acc_ref[...]),
         (level, 1.0, got_ref[:, :rank].astype(F32)),
     ]
-    part_ref[...] = attend(query_ref[...], keys, seen, rank, known)
+    values, level = attend(query_ref[...], keys, seen, rank, known)
+    value_ref[...] = values
+    level_ref[...] = jnp.broadcast_to(level, level_ref.shape)
     for p in range(local):
         at = start + lax.broadcasted_iota(jnp.int32, (span, 1), 0) == ends[p]
         cache_ref[p] = jnp.where(at, fresh_ref[pl.ds(p, 1), :], moved_ref[pl.ds(p * span, span)])
@@ -299,27 +309,35 @@
 
 def chip_kernel(count, *refs):
     for k in range(count):
-        out_ref = refs[2 * count + k]
-        rank = out_ref.shape[1] - LANES
-        out_ref[...] = packed(*merged([refs[k][...], refs[count + k][...]], rank))
+        value_ref, level_ref = refs[2 * count + 2 * k : 2 * count + 2 * k + 2]
+        values, level = merged([unpacked(refs[k][...]), unpacked(refs[count + k][...])])
+        value_ref[...] = values.astype(BF16)
+        kept = jnp.where(diagonal(values.shape[0], level_ref.shape[1]), level, 0.0)
+        level_ref[...] = jnp.broadcast_to(jnp.sum(kept, axis=0, keepdims=True), level_ref.shape)
 
 
 def chip_merge(keep, got):
+    rows, rank = keep[0].shape[0], keep[0].shape[1] - LANES
     return pl.pallas_call(
         functools.partial(chip_kernel, len(keep)),
-        out_shape=[shape(k.shape) for k in keep],
+        out_shape=[shape((rows, rank)), shape((8, max(rows, LANES)), F32)] * len(keep),
         in_specs=[VMEM] * (2 * len(keep)),
-        out_specs=[VMEM] * len(keep),
+        out_specs=[VMEM] * (2 * len(keep)),
         compiler_params=PARAMS,
         name="chip_merge",
     )(*keep, *got)
 
 
 def final_kernel(count, *refs):
-    part_refs, (w_ref, out_ref, values) = refs[:count], refs[count:]
+    part_refs, (value_ref, level_ref, w_ref, out_ref, values) = refs[: 2 * count], refs[2 * count :]
     heads, rank, reach = w_ref.shape
     local = out_ref.shape[0]
-    latent = merged([ref[...] for ref in part_refs], rank)[0].astype(BF16)
+    parts = [(value_ref[...], level_ref[:, 0:1])]
+    for k in range(count):
+        row = part_refs[2 * k + 1][0:1]
+        kept = jnp.where(diagonal(value_ref.shape[0], row.shape[1]), row, 0.0)
+        parts.append((part_refs[2 * k][...].astype(F32), jnp.sum(kept, axis=1, keepdims=True)))
+    latent = merged(parts)[0].astype(BF16)
     first = lax.broadcasted_iota(jnp.int32, (2 * local, reach), 0) < local
     for h in range(0, heads, 2):
         two = latent[h * local : (h + 2) * local]
@@ -418,25 +436,25 @@
         name="suffix_keep",
     )(ancestors, lengths, *keeping, moved)
     sums = chip_merge(keep, [lax.ppermute(g, "seq", pairs(0, 1)) for g in give])
-    parts = [lax.ppermute(s, "seq", back(t, 0)) for t, s in enumerate(sums, 1)]
+    parts = [lax.ppermute(s, "seq", back(1 + i // 2, 0)) for i, s in enumerate(sums)]
     other = lax.ppermute(moved, "seq", pairs(0, 1))
 
     moved, _ = lax.optimization_barrier((moved, sums[0]))
     query, _, acc, level, mass = stages[0]
-    new_caches, own_part = pl.pallas_call(
+    new_caches, *own_part = pl.pallas_call(
         near_kernel,
-        out_shape=[shape(private_caches.shape), part],
+        out_shape=[shape(private_caches.shape), shape((rows, rank), F32), shape((rows, LANES), F32)],
         in_specs=[SMEM] * 2 + [VMEM] * 8,
-        out_specs=[VMEM] * 2,
+        out_specs=[VMEM] * 3,
         compiler_params=PARAMS,
         name="suffix_near",
     )(ancestors, lengths, new_latent, query, acc, level, mass, given, moved, other)
-    parts.append(own_part)
+    parts += own_part
 
     head_values = pl.pallas_call(
-        functools.partial(final_kernel, chips),
+        functools.partial(final_kernel, others),
         out_shape=shape((local, heads, reach)),
-        in_specs=[VMEM] * (chips + 1),
+        in_specs=[VMEM] * (2 * chips + 1),
         out_specs=VMEM,
         scratch_shapes=[pltpu.VMEM((rows, reach), F32)],
         compiler_params=PARAMS,

time: 40.6 us -> 40.3 us (level)
  waiting for transfers between devices: 5.66 us -> 4.21 us
  Pallas kernels: 14.3 us -> 15 us
  starting transfers between devices: 18.3 us -> 18.9 us
    ppermute x1 -> x2, waiting for transfers between devices: 3.46 us -> 1.88 us  [on_device(): lax.ppermute(s, 'seq', back(1 + i // 2, 0))]
    pallas_call x2, Pallas kernels: 2.94 us -> 3.62 us  [the longest x1 1.89 us: on_device(): pl.pallas_call(near_kernel, out_shape=[shape(private_caches.shape), shape...]
    ppermute x1 -> x2, starting transfers between devices: 1.56 us -> 2.09 us  [on_device(): lax.ppermute(s, 'seq', back(1 + i // 2, 0))]
    ppermute x1, starting transfers between devices: 0.07 us -> 0.5 us  [on_device(): sums = chip_merge(keep, [lax.ppermute(g, 'seq', pairs(0, 1)) for g in give])]
    ppermute x1, starting transfers between devices: 0.5 us -> 0.07 us  [on_device(): other = lax.ppermute(moved, 'seq', pairs(0, 1))]
  transfers between devices with their start and end apart: 11 -> 12, of which waited for: 2 -> 3; matrix products, arithmetic and copies ran while one was open for 0% -> 0% of each run, Pallas kernels for 28% -> 29%
where the time goes in v17:
time: 40.3 us; the launch traced here: 40.2 us
  starting transfers between devices  18.9 us (47%)
  Pallas kernels  15 us (37%)
  waiting for transfers between devices  4.21 us (10%)
  local copies, waits for them, and re-layouts  1.2 us (3%)
  between operations  0.88 us (2%)
    ppermute x1, starting transfers between devices, on_device(): middle = lax.ppermute(block, 'dom', [(0, 2), (3, 1)])  7.77 us
    pallas_call x2, Pallas kernels, prefix_attention(): pl.pallas_call(functools.partial(prefix_kernel, len(queries), tiles), out...  6.58 us
    ppermute x1, starting transfers between devices, on_device(): late = lax.ppermute(chosen, 'dom', swap)  4.02 us
    ppermute x1, waiting for transfers between devices, on_device(): late = lax.ppermute(chosen, 'dom', swap)  2.18 us
    ppermute x3, starting transfers between devices, on_device(): lax.ppermute(own, 'seq', pairs(*r))  2.15 us
    ppermute x2, starting transfers between devices, on_device(): lax.ppermute(s, 'seq', back(1 + i // 2, 0))  2.09 us
    pallas_call x1, Pallas kernels, on_device(): pl.pallas_call(near_kernel, out_shape=[shape(private_caches.shape), shape...  1.89 us
    ppermute x2, waiting for transfers between devices, on_device(): lax.ppermute(s, 'seq', back(1 + i // 2, 0))  1.88 us
  transfers between devices with their start and end apart: 12, of which 3 were waited for; matrix products, arithmetic and copies ran while one was open for 0% of the time, Pallas kernels for 29%

profile of v17, /device:TPU:0, one launch (start us, length us, event | category | flops | bytes accessed | tf_op | source)
XLA Modules:
  0.0 40.2 jit_solution(405452437005479629)
XLA Ops:
  0.7 1.1 %copy-done.5 = bf16[4,64,576]{2,1,0:T(8,128)(2,1)S(1)} copy-done((bf16[4,64,576]{2,1,0:T(8,128)(2,1)S(1)}, bf16[4,64,576]{2,1,0:T(8,128)(2,1)}, u32[]{:S(2)}) %copy-start.5) | copy-done | bytes 294936
  1.8 0.8 %collective-permute-start.3 = (bf16[128,1152]{1,0:T(8,128)(2,1)S(1)}, bf16[128,1152]{1,0:T(8,128)(2,1)S(1)}, u32[]{:S(2)}, u32[]{:S(2)}) collective-permute-start(bf16[128,1152]{1,0:T(8,128)(2,1)S(1)} %pack.1.refs_0_), channel_id=1, source_target_pairs={{1,2},{2,1},{5,6},{6,5},{9,10},{10,9},{13,14},{14,13},{17,18},{18,... | collective-permute-start | bytes 884744 | tf_op jit(solution)/shard_map/ppermute | solution.py:373
  2.7 7.8 %collective-permute-start.2 = (bf16[128,1152]{1,0:T(8,128)(2,1)S(1)}, bf16[128,1152]{1,0:T(8,128)(2,1)S(1)}, u32[]{:S(2)}, u32[]{:S(2)}) collective-permute-start(bf16[128,1152]{1,0:T(8,128)(2,1)S(1)} %pack.1.refs_0_), channel_id=1, source_target_pairs={{0,2},{3,1},{4,6},{7,5},{8,10},{11,9},{12,14},{15,13},{16,18},{19,... | collective-permute-start | bytes 884744 | tf_op jit(solution)/shard_map/ppermute | solution.py:372
  10.5 0.6 %project.1.refs_0_ = bf16[128,576]{1,0:T(8,128)(2,1)S(1)} custom-call(bf16[128,128]{1,0:T(8,128)(2,1)S(1)} %bitcast.9, bf16[128,64]{1,0:T(8,128)(2,1)S(1)} %bitcast.10, bf16[32,128,512]{2,1,0:T(8,128)(2,1)S(1)} %copy-done.4), custom_call_target="tpu_custom_call" | custom-call | flops 8000000000 | tf_op jit(solution)/shard_map/project/pallas_call | solution.py:381
  11.2 1.6 %collective-permute-start.1 = (bf16[128,576]{1,0:T(8,128)(2,1)S(1)}, bf16[128,576]{1,0:T(8,128)(2,1)S(1)}, u32[]{:S(2)}, u32[]{:S(2)}) collective-permute-start(bf16[128,576]{1,0:T(8,128)(2,1)S(1)} %project.1.refs_0_), channel_id=1, source_target_pairs={{0,12},{4,8},{8,4},{12,0},{1,13},{5,9},{9,5},{13,1},{2,14},{6,10},... | collective-permute-start | bytes 442376 | tf_op jit(solution)/shard_map/ppermute | solution.py:403
  12.8 0.5 %collective-permute-start = (bf16[128,576]{1,0:T(8,128)(2,1)S(1)}, bf16[128,576]{1,0:T(8,128)(2,1)S(1)}, u32[]{:S(2)}, u32[]{:S(2)}) collective-permute-start(bf16[128,576]{1,0:T(8,128)(2,1)S(1)} %project.1.refs_0_), channel_id=1, source_target_pairs={{0,8},{4,12},{8,0},{12,4},{1,9},{5,13},{9,1},{13,5},{2,10},{6,14},... | collective-permute-start | bytes 442376 | tf_op jit(solution)/shard_map/ppermute | solution.py:403
  13.4 1.4 %collective-permute-start.4 = (s32[4]{0:T(128)S(1)}, s32[4]{0:T(128)S(1)}, u32[]{:S(2)}, u32[]{:S(2)}) collective-permute-start(s32[4]{0:T(128)S(1)} %copy-done.1), channel_id=1, source_target_pairs={{0,1},{3,2},{4,5},{7,6},{8,9},{11,10},{12,13},{15,14},{16,17},{19,... | collective-permute-start | bytes 56 | tf_op jit(solution)/shard_map/ppermute | solution.py:374
  14.8 3.3 %prefix_attention.3 = (f32[128,512]{1,0:T(8,128)S(1)}, f32[128,128]{1,0:T(8,128)S(1)}, f32[128,128]{1,0:T(8,128)S(1)}, bf16[128,640]{1,0:T(8,128)(2,1)S(1)}) custom-call(bf16[128,576]{1,0:T(8,128)(2,1)S(1)} %project.1.refs_0_, bf16[128,576]{1,0:T(8,128)(2,1)S(1)} %collective-permute-done.5.refs_1_, bf16[576,4096]{1,0:T(8,128)(2,1)S(1)} %bitcast.7), custom_call_target="tpu_custom_call" | custom-call | tf_op jit(solution)/shard_map/prefix_attention/pallas_call | solution.py:111
  18.1 0.7 %gather.3 = bf16[128,1152]{1,0:T(8,128)(2,1)S(1)} custom-call(s32[4]{0:T(128)S(1)} %collective-permute-done.4.names, bf16[128,1152]{1,0:T(8,128)(2,1)S(1)} %pack.1.refs_0_, bf16[128,1152]{1,0:T(8,128)(2,1)S(1)} %collective-permute-done.2.refs_1_, bf16[128,1152]{1,0:T(8,128)(2,1)S(1)} %collective-permute-done.3.refs_2_, ...), custom_call_target="tpu_custom_call" | custom-call | tf_op jit(solution)/shard_map/gather/pallas_call | solution.py:218
  18.8 4.0 %collective-permute-start.6 = (bf16[128,1152]{1,0:T(8,128)(2,1)S(1)}, bf16[128,1152]{1,0:T(8,128)(2,1)S(1)}, u32[]{:S(2)}, u32[]{:S(2)}) collective-permute-start(bf16[128,1152]{1,0:T(8,128)(2,1)S(1)} %gather.3), channel_id=1, source_target_pairs={{0,1},{1,0},{2,3},{3,2},{4,5},{5,4},{6,7},{7,6},{8,9},{9,8},{10,11... | collective-permute-start | bytes 884744 | tf_op jit(solution)/shard_map/ppermute | solution.py:413
  22.8 3.3 %prefix_attention.2 = (f32[256,512]{1,0:T(8,128)S(1)}, f32[256,128]{1,0:T(8,128)S(1)}, f32[256,128]{1,0:T(8,128)S(1)}) custom-call(bf16[128,576]{1,0:T(8,128)(2,1)S(1)} %collective-permute-done.refs_0_, bf16[128,576]{1,0:T(8,128)(2,1)S(1)} %collective-permute-done.1.refs_1_.refs_0_, bf16[576,4096]{1,0:T(8,128)(2,1)S(1)} %bitcast.8), custom_call_target="tpu_custom_call" | custom-call | flops 2281701376 | bytes 4718592 | tf_op jit(solution)/shard_map/prefix_attention/pallas_call | solution.py:111
  26.1 0.7 %gather.2.refs_4_ = bf16[128,1152]{1,0:T(8,128)(2,1)S(1)} custom-call(s32[4]{0:T(128)S(1)} %copy-done.1, bf16[128,1152]{1,0:T(8,128)(2,1)S(1)} %pack.1.refs_0_, bf16[128,1152]{1,0:T(8,128)(2,1)S(1)} %collective-permute-done.2.refs_1_, bf16[128,1152]{1,0:T(8,128)(2,1)S(1)} %collective-permute-done.3.refs_2_), custom_call_target="tpu_custom_call" | custom-call | tf_op jit(solution)/shard_map/gather/pallas_call | solution.py:218
  26.8 2.2 %collective-permute-done.6.refs_5_ = bf16[128,1152]{1,0:T(8,128)(2,1)S(1)} collective-permute-done((bf16[128,1152]{1,0:T(8,128)(2,1)S(1)}, bf16[128,1152]{1,0:T(8,128)(2,1)S(1)}, u32[]{:S(2)}, u32[]{:S(2)}) %collective-permute-start.6) | collective-permute-done | bytes 294944 | tf_op jit(solution)/shard_map/ppermute | solution.py:413
  29.0 1.5 %suffix_give.1 = (bf16[256,576]{1,0:T(8,128)(2,1)S(1)}, bf16[128,640]{1,0:T(8,128)(2,1)S(1)}) custom-call(s32[4]{0:T(128)S(1)} %copy-done.1, s32[16]{0:T(128)S(1)} %copy-done.3, bf16[128,576]{1,0:T(8,128)(2,1)S(1)} %collective-permute-done.1.refs_1_.refs_0_, f32[256,512]{1,0:T(8,128)S(1)} %get-tuple-element.17.refs_1_, ...), custom_call_target="tpu_custom_call" | custom-call | tf_op jit(solution)/shard_map/suffix_give/pallas_call | solution.py:422
  30.5 0.5 %collective-permute-start.7 = (bf16[128,640]{1,0:T(8,128)(2,1)S(1)}, bf16[128,640]{1,0:T(8,128)(2,1)S(1)}, u32[]{:S(2)}, u32[]{:S(2)}) collective-permute-start(bf16[128,640]{1,0:T(8,128)(2,1)S(1)} %get-tuple-element.22), channel_id=1, source_target_pairs={{0,4},{4,0},{8,12},{12,8},{1,5},{5,1},{9,13},{13,9},{2,6},{6,2},{1... | collective-permute-start | bytes 491528 | tf_op jit(solution)/shard_map/ppermute | solution.py:438
  31.0 0.1 collective-permute-start.10
  31.1 1.1 %suffix_keep.1.refs_0_ = bf16[128,640]{1,0:T(8,128)(2,1)S(1)} custom-call(s32[4]{0:T(128)S(1)} %copy-done.1, s32[16]{0:T(128)S(1)} %copy-done.3, bf16[128,576]{1,0:T(8,128)(2,1)S(1)} %collective-permute-done.refs_0_, f32[256,512]{1,0:T(8,128)S(1)} %get-tuple-element.17.refs_1_, f32[256,128]{1,0:T(8,128)S(1)} %get-tuple-element.18.refs_2_, ...), custom_call_target="tpu_custom_call" | custom-call | tf_op jit(solution)/shard_map/suffix_keep/pallas_call | solution.py:430
  32.2 0.1 collective-permute-done.7.refs_1_
  32.4 0.2 chip_merge.1
  32.5 1.6 %collective-permute-start.8 = (bf16[128,512]{1,0:T(8,128)(2,1)S(1)}, bf16[128,512]{1,0:T(8,128)(2,1)S(1)}, u32[]{:S(2)}, u32[]{:S(2)}) collective-permute-start(bf16[128,512]{1,0:T(8,128)(2,1)S(1)} %get-tuple-element.23), channel_id=1, source_target_pairs={{8,0},{12,4},{0,8},{4,12},{9,1},{13,5},{1,9},{5,13},{10,2},{14,6},... | collective-permute-start | bytes 393224 | tf_op jit(solution)/shard_map/ppermute | solution.py:439
  34.1 0.5 %collective-permute-start.9 = (f32[8,128]{1,0:T(8,128)S(1)}, f32[8,128]{1,0:T(8,128)S(1)}, u32[]{:S(2)}, u32[]{:S(2)}) collective-permute-start(f32[8,128]{1,0:T(8,128)S(1)} %get-tuple-element.24), channel_id=1, source_target_pairs={{8,0},{12,4},{0,8},{4,12},{9,1},{13,5},{1,9},{5,13},{10,2},{14,6},... | collective-permute-start | bytes 12296 | tf_op jit(solution)/shard_map/ppermute | solution.py:439
  34.7 1.9 %suffix_near.1 = (bf16[4,64,576]{2,1,0:T(8,128)(2,1)}, f32[128,512]{1,0:T(8,128)S(1)}, f32[128,128]{1,0:T(8,128)S(1)}) custom-call(s32[4]{0:T(128)S(1)} %copy-done.1, s32[16]{0:T(128)S(1)} %copy-done.3, bf16[4,576]{1,0:T(4,128)(2,1)S(1)} %copy-done.2, bf16[128,576]{1,0:T(8,128)(2,1)S(1)} %project.1.refs_0_, f32[128,512]{1,0:T(8,128)S(1)} %get-tuple-element.25.refs_1_, ...), custom_call_target="tpu_custom_call" | custom-call | tf_op jit(solution)/shard_map/suffix_near/pallas_call | solution.py:444
  36.5 1.9 %collective-permute-done.9.refs_1_ = f32[8,128]{1,0:T(8,128)S(1)} collective-permute-done((f32[8,128]{1,0:T(8,128)S(1)}, f32[8,128]{1,0:T(8,128)S(1)}, u32[]{:S(2)}, u32[]{:S(2)}) %collective-permute-start.9) | collective-permute-done | bytes 4128 | tf_op jit(solution)/shard_map/ppermute | solution.py:439
  38.4 1.7 %final.1 = bf16[4,32,128]{2,1,0:T(8,128)(2,1)} custom-call(bf16[128,512]{1,0:T(8,128)(2,1)S(1)} %collective-permute-done.8.refs_0_, f32[8,128]{1,0:T(8,128)S(1)} %collective-permute-done.9.refs_1_, f32[128,512]{1,0:T(8,128)S(1)} %get-tuple-element.29.refs_2_, f32[128,128]{1,0:T(8,128)S(1)} %get-tuple-element.30.refs_3_, bf16[32,512,128]{2,1,0:T(8,128)(2,1)S(1)} %copy-done), custom_call_target="tpu_custom_call" | custom-call | tf_op jit(solution)/shard_map/final/pallas_call | solution.py:454
  (34 shorter events, 0.3 us)
Async XLA Ops:
  0.6 9.9 %copy-start.4 = (bf16[32,128,512]{2,1,0:T(8,128)(2,1)S(1)}, bf16[32,128,512]{2,1,0:T(8,128)(2,1)}, u32[]{:S(2)}) copy-start(bf16[32,128,512]{2,1,0:T(8,128)(2,1)} %w_ref.1) | copy-start | bytes 12582916
  0.6 1.1 %copy-start.5 = (bf16[4,64,576]{2,1,0:T(8,128)(2,1)S(1)}, bf16[4,64,576]{2,1,0:T(8,128)(2,1)}, u32[]{:S(2)}) copy-start(bf16[4,64,576]{2,1,0:T(8,128)(2,1)} %cache_ref.1) | copy-start | bytes 884740
  1.8 8.7 %copy-start.6 = (bf16[4,32,128]{2,1,0:T(8,128)(2,1)S(1)}, bf16[4,32,128]{2,1,0:T(8,128)(2,1)}, u32[]{:S(2)}) copy-start(bf16[4,32,128]{2,1,0:T(8,128)(2,1)} %param.9) | copy-start | bytes 98308
  1.8 8.7 %copy-start.7 = (bf16[4,32,64]{2,1,0:T(8,128)(2,1)S(1)}, bf16[4,32,64]{2,1,0:T(8,128)(2,1)}, u32[]{:S(2)}) copy-start(bf16[4,32,64]{2,1,0:T(8,128)(2,1)} %param.10) | copy-start | bytes 49156
  1.8 13.0 %slice-start = ((s8[4718592]{0:T(1024)(128)(4,1)}), s8[4194304]{0:T(1024)(128)(4,1)S(1)}, s32[]{:S(2)}) async-start(s8[4718592]{0:T(1024)(128)(4,1)} %bitcast.5), calls=%async_computation | async-start | bytes 8388608
  1.8 16.3 %collective-permute-start.3 = (bf16[128,1152]{1,0:T(8,128)(2,1)S(1)}, bf16[128,1152]{1,0:T(8,128)(2,1)S(1)}, u32[]{:S(2)}, u32[]{:S(2)}) collective-permute-start(bf16[128,1152]{1,0:T(8,128)(2,1)S(1)} %pack.1.refs_0_), channel_id=1, source_target_pairs={{1,2},{2,1},{5,6},{6,5},{9,10},{10,9},{13,14},{14,13},{17,18},{18,... | collective-permute-start | bytes 884744 | tf_op jit(solution)/shard_map/ppermute | solution.py:373
  2.7 15.5 %collective-permute-start.2 = (bf16[128,1152]{1,0:T(8,128)(2,1)S(1)}, bf16[128,1152]{1,0:T(8,128)(2,1)S(1)}, u32[]{:S(2)}, u32[]{:S(2)}) collective-permute-start(bf16[128,1152]{1,0:T(8,128)(2,1)S(1)} %pack.1.refs_0_), channel_id=1, source_target_pairs={{0,2},{3,1},{4,6},{7,5},{8,10},{11,9},{12,14},{15,13},{16,18},{19,... | collective-permute-start | bytes 884744 | tf_op jit(solution)/shard_map/ppermute | solution.py:372
  10.5 4.3 %slice-start.1 = ((s8[4718592]{0:T(1024)(128)(4,1)}), s8[524288]{0:T(1024)(128)(4,1)S(1)}, s32[]{:S(2)}) async-start(s8[4718592]{0:T(1024)(128)(4,1)} %bitcast.5), calls=%async_computation.1 | async-start | bytes 1048576
  10.5 2.8 %copy-start.1 = (s32[4]{0:T(128)S(1)}, s32[4]{0:T(128)}, u32[]{:S(2)}) copy-start(s32[4]{0:T(128)} %anc.5) | copy-start | bytes 52
  11.2 2.2 %collective-permute-start.5 = (bf16[128,576]{1,0:T(8,128)(2,1)S(1)}, bf16[128,576]{1,0:T(8,128)(2,1)S(1)}, u32[]{:S(2)}, u32[]{:S(2)}) collective-permute-start(bf16[128,576]{1,0:T(8,128)(2,1)S(1)} %project.1.refs_0_), channel_id=1, source_target_pairs={{0,4},{4,0},{8,12},{12,8},{1,5},{5,1},{9,13},{13,9},{2,6},{6,2},{1... | collective-permute-start | bytes 442376 | tf_op jit(solution)/shard_map/ppermute | solution.py:403
  11.2 11.6 %collective-permute-start.1 = (bf16[128,576]{1,0:T(8,128)(2,1)S(1)}, bf16[128,576]{1,0:T(8,128)(2,1)S(1)}, u32[]{:S(2)}, u32[]{:S(2)}) collective-permute-start(bf16[128,576]{1,0:T(8,128)(2,1)S(1)} %project.1.refs_0_), channel_id=1, source_target_pairs={{0,12},{4,8},{8,4},{12,0},{1,13},{5,9},{9,5},{13,1},{2,14},{6,10},... | collective-permute-start | bytes 442376 | tf_op jit(solution)/shard_map/ppermute | solution.py:403
  12.8 10.0 %collective-permute-start = (bf16[128,576]{1,0:T(8,128)(2,1)S(1)}, bf16[128,576]{1,0:T(8,128)(2,1)S(1)}, u32[]{:S(2)}, u32[]{:S(2)}) collective-permute-start(bf16[128,576]{1,0:T(8,128)(2,1)S(1)} %project.1.refs_0_), channel_id=1, source_target_pairs={{0,8},{4,12},{8,0},{12,4},{1,9},{5,13},{9,1},{13,5},{2,10},{6,14},... | collective-permute-start | bytes 442376 | tf_op jit(solution)/shard_map/ppermute | solution.py:403
  13.4 4.8 %collective-permute-start.4 = (s32[4]{0:T(128)S(1)}, s32[4]{0:T(128)S(1)}, u32[]{:S(2)}, u32[]{:S(2)}) collective-permute-start(s32[4]{0:T(128)S(1)} %copy-done.1), channel_id=1, source_target_pairs={{0,1},{3,2},{4,5},{7,6},{8,9},{11,10},{12,13},{15,14},{16,17},{19,... | collective-permute-start | bytes 56 | tf_op jit(solution)/shard_map/ppermute | solution.py:374
  18.8 10.2 %copy-start.3 = (s32[16]{0:T(128)S(1)}, s32[16]{0:T(128)}, u32[]{:S(2)}) copy-start(s32[16]{0:T(128)} %lens.5) | copy-start | bytes 196
  18.8 10.2 %collective-permute-start.6 = (bf16[128,1152]{1,0:T(8,128)(2,1)S(1)}, bf16[128,1152]{1,0:T(8,128)(2,1)S(1)}, u32[]{:S(2)}, u32[]{:S(2)}) collective-permute-start(bf16[128,1152]{1,0:T(8,128)(2,1)S(1)} %gather.3), channel_id=1, source_target_pairs={{0,1},{1,0},{2,3},{3,2},{4,5},{5,4},{6,7},{7,6},{8,9},{9,8},{10,11... | collective-permute-start | bytes 884744 | tf_op jit(solution)/shard_map/ppermute | solution.py:413
  26.1 8.5 %copy-start.2 = (bf16[4,576]{1,0:T(4,128)(2,1)S(1)}, bf16[4,576]{1,0:T(4,128)(2,1)}, u32[]{:S(2)}) copy-start(bf16[4,576]{1,0:T(4,128)(2,1)} %fresh_ref.1) | copy-start | bytes 13828
  26.1 12.3 %copy-start = (bf16[32,512,128]{2,1,0:T(8,128)(2,1)S(1)}, bf16[32,512,128]{2,1,0:T(8,128)(2,1)}, u32[]{:S(2)}) copy-start(bf16[32,512,128]{2,1,0:T(8,128)(2,1)} %refs_4_.1) | copy-start | bytes 12582916
  30.4 4.2 %collective-permute-start.11 = (bf16[256,576]{1,0:T(8,128)(2,1)S(1)}, bf16[256,576]{1,0:T(8,128)(2,1)S(1)}, u32[]{:S(2)}, u32[]{:S(2)}) collective-permute-start(bf16[256,576]{1,0:T(8,128)(2,1)S(1)} %get-tuple-element.28.refs_4_.refs_5_), channel_id=1, source_target_pairs={{0,4},{4,0},{8,12},{12,8},{1,5},{5,1},{9,13},{13,9},{2,6},{6,2},{1... | collective-permute-start | bytes 884744 | tf_op jit(solution)/shard_map/ppermute | solution.py:440
  30.5 1.9 %collective-permute-start.7 = (bf16[128,640]{1,0:T(8,128)(2,1)S(1)}, bf16[128,640]{1,0:T(8,128)(2,1)S(1)}, u32[]{:S(2)}, u32[]{:S(2)}) collective-permute-start(bf16[128,640]{1,0:T(8,128)(2,1)S(1)} %get-tuple-element.22), channel_id=1, source_target_pairs={{0,4},{4,0},{8,12},{12,8},{1,5},{5,1},{9,13},{13,9},{2,6},{6,2},{1... | collective-permute-start | bytes 491528 | tf_op jit(solution)/shard_map/ppermute | solution.py:438
  31.0 3.6 %collective-permute-start.10 = (bf16[128,640]{1,0:T(8,128)(2,1)S(1)}, bf16[128,640]{1,0:T(8,128)(2,1)S(1)}, u32[]{:S(2)}, u32[]{:S(2)}) collective-permute-start(bf16[128,640]{1,0:T(8,128)(2,1)S(1)} %get-tuple-element.27), channel_id=1, source_target_pairs={{0,4},{4,0},{8,12},{12,8},{1,5},{5,1},{9,13},{13,9},{2,6},{6,2},{1... | collective-permute-start | bytes 491528 | tf_op jit(solution)/shard_map/ppermute | solution.py:410
  32.5 5.9 %collective-permute-start.8 = (bf16[128,512]{1,0:T(8,128)(2,1)S(1)}, bf16[128,512]{1,0:T(8,128)(2,1)S(1)}, u32[]{:S(2)}, u32[]{:S(2)}) collective-permute-start(bf16[128,512]{1,0:T(8,128)(2,1)S(1)} %get-tuple-element.23), channel_id=1, source_target_pairs={{8,0},{12,4},{0,8},{4,12},{9,1},{13,5},{1,9},{5,13},{10,2},{14,6},... | collective-permute-start | bytes 393224 | tf_op jit(solution)/shard_map/ppermute | solution.py:439
  34.1 4.3 %collective-permute-start.9 = (f32[8,128]{1,0:T(8,128)S(1)}, f32[8,128]{1,0:T(8,128)S(1)}, u32[]{:S(2)}, u32[]{:S(2)}) collective-permute-start(f32[8,128]{1,0:T(8,128)S(1)} %get-tuple-element.24), channel_id=1, source_target_pairs={{8,0},{12,4},{0,8},{4,12},{9,1},{13,5},{1,9},{5,13},{10,2},{14,6},... | collective-permute-start | bytes 12296 | tf_op jit(solution)/shard_map/ppermute | solution.py:439

commit v18 on v17

--- a/solution.py
+++ b/solution.py
@@ -148,6 +148,10 @@
     return acc * (1.0 / whole), top + jnp.log2(whole)
 
 
+def column(stat):
+    return jnp.max(stat, axis=1, keepdims=True)
+
+
 def diagonal(rows, lanes):
     row = lax.broadcasted_iota(jnp.int32, (rows, lanes), 0)
     return row == lax.broadcasted_iota(jnp.int32, (rows, lanes), 1)
@@ -232,7 +236,7 @@
     span, rank = keys.shape[0] // local, acc_ref.shape[1]
     ends = [lens[anc[p]] for p in range(local)]
     seen = visible(query_ref.shape[0], ends, [lax.axis_index("seq") * span], span)
-    known = [(max_ref[part, 0:1], sum_ref[part, 0:1], acc_ref[part])]
+    known = [(column(max_ref[part]), column(sum_ref[part]), acc_ref[part])]
     return packed(*attend(query_ref[...], keys, seen, rank, known))
 
 
@@ -296,11 +300,11 @@
     seen = visible(query_ref.shape[0], ends, [start, other], span)
     level = jnp.sum(got_ref[:, rank:].astype(F32), axis=1, keepdims=True)
     known = [
-        (max_ref[:, 0:1], sum_ref[:, 0:1], acc_ref[...]),
+        (column(max_ref[...]), column(sum_ref[...]), acc_ref[...]),
         (level, 1.0, got_ref[:, :rank].astype(F32)),
     ]
     values, level = attend(query_ref[...], keys, seen, rank, known)
-    value_ref[...] = values
+    value_ref[...] = values.astype(BF16)
     level_ref[...] = jnp.broadcast_to(level, level_ref.shape)
     for p in range(local):
         at = start + lax.broadcasted_iota(jnp.int32, (span, 1), 0) == ends[p]
@@ -332,7 +336,7 @@
     part_refs, (value_ref, level_ref, w_ref, out_ref, values) = refs[: 2 * count], refs[2 * count :]
     heads, rank, reach = w_ref.shape
     local = out_ref.shape[0]
-    parts = [(value_ref[...], level_ref[:, 0:1])]
+    parts = [(value_ref[...].astype(F32), column(level_ref[...]))]
     for k in range(count):
         row = part_refs[2 * k + 1][0:1]
         kept = jnp.where(diagonal(value_ref.shape[0], row.shape[1]), row, 0.0)
@@ -443,7 +447,7 @@
     query, _, acc, level, mass = stages[0]
     new_caches, *own_part = pl.pallas_call(
         near_kernel,
-        out_shape=[shape(private_caches.shape), shape((rows, rank), F32), shape((rows, LANES), F32)],
+        out_shape=[shape(private_caches.shape), shape((rows, rank)), shape((rows, LANES), F32)],
         in_specs=[SMEM] * 2 + [VMEM] * 8,
         out_specs=[VMEM] * 3,
         compiler_params=PARAMS,

time: 40.3 us -> 39.7 us (0.985)
  Pallas kernels: 15 us -> 14.2 us
where the time goes in v18:
time: 39.7 us; the launch traced here: 39.6 us
  starting transfers between devices  18.9 us (48%)
  Pallas kernels  14.2 us (36%)
  waiting for transfers between devices  4.45 us (11%)
  local copies, waits for them, and re-layouts  1.2 us (3%)
  between operations  0.88 us (2%)
    ppermute x1, starting transfers between devices, on_device(): middle = lax.ppermute(block, 'dom', [(0, 2), (3, 1)])  7.77 us
    pallas_call x2, Pallas kernels, prefix_attention(): pl.pallas_call(functools.partial(prefix_kernel, len(queries), tiles), out...  6.58 us
    ppermute x1, starting transfers between devices, on_device(): late = lax.ppermute(chosen, 'dom', swap)  4.02 us
    ppermute x1, waiting for transfers between devices, on_device(): late = lax.ppermute(chosen, 'dom', swap)  2.18 us
    ppermute x3, starting transfers between devices, on_device(): lax.ppermute(own, 'seq', pairs(*r))  2.15 us
    ppermute x2, starting transfers between devices, on_device(): lax.ppermute(s, 'seq', back(1 + i // 2, 0))  2.09 us
    ppermute x2, waiting for transfers between devices, on_device(): lax.ppermute(s, 'seq', back(1 + i // 2, 0))  2.02 us
    pallas_call x1, Pallas kernels, on_device(): pl.pallas_call(near_kernel, out_shape=[shape(private_caches.shape), shape...  1.65 us
  transfers between devices with their start and end apart: 12, of which 3 were waited for; matrix products, arithmetic and copies ran while one was open for 0% of the time, Pallas kernels for 29%

profile of v18, /device:TPU:0, one launch (start us, length us, event | category | flops | bytes accessed | tf_op | source)
XLA Modules:
  0.0 39.6 jit_solution(11816834077352209403)
XLA Ops:
  0.7 1.1 %copy-done.5 = bf16[4,64,576]{2,1,0:T(8,128)(2,1)S(1)} copy-done((bf16[4,64,576]{2,1,0:T(8,128)(2,1)S(1)}, bf16[4,64,576]{2,1,0:T(8,128)(2,1)}, u32[]{:S(2)}) %copy-start.5) | copy-done | bytes 294936
  1.8 0.8 %collective-permute-start.3 = (bf16[128,1152]{1,0:T(8,128)(2,1)S(1)}, bf16[128,1152]{1,0:T(8,128)(2,1)S(1)}, u32[]{:S(2)}, u32[]{:S(2)}) collective-permute-start(bf16[128,1152]{1,0:T(8,128)(2,1)S(1)} %pack.1.refs_0_), channel_id=1, source_target_pairs={{1,2},{2,1},{5,6},{6,5},{9,10},{10,9},{13,14},{14,13},{17,18},{18,... | collective-permute-start | bytes 884744 | tf_op jit(solution)/shard_map/ppermute | solution.py:377
  2.7 7.8 %collective-permute-start.2 = (bf16[128,1152]{1,0:T(8,128)(2,1)S(1)}, bf16[128,1152]{1,0:T(8,128)(2,1)S(1)}, u32[]{:S(2)}, u32[]{:S(2)}) collective-permute-start(bf16[128,1152]{1,0:T(8,128)(2,1)S(1)} %pack.1.refs_0_), channel_id=1, source_target_pairs={{0,2},{3,1},{4,6},{7,5},{8,10},{11,9},{12,14},{15,13},{16,18},{19,... | collective-permute-start | bytes 884744 | tf_op jit(solution)/shard_map/ppermute | solution.py:376
  10.5 0.6 %project.1.refs_0_ = bf16[128,576]{1,0:T(8,128)(2,1)S(1)} custom-call(bf16[128,128]{1,0:T(8,128)(2,1)S(1)} %bitcast.9, bf16[128,64]{1,0:T(8,128)(2,1)S(1)} %bitcast.10, bf16[32,128,512]{2,1,0:T(8,128)(2,1)S(1)} %copy-done.4), custom_call_target="tpu_custom_call" | custom-call | flops 8000000000 | tf_op jit(solution)/shard_map/project/pallas_call | solution.py:385
  11.2 1.6 %collective-permute-start.1 = (bf16[128,576]{1,0:T(8,128)(2,1)S(1)}, bf16[128,576]{1,0:T(8,128)(2,1)S(1)}, u32[]{:S(2)}, u32[]{:S(2)}) collective-permute-start(bf16[128,576]{1,0:T(8,128)(2,1)S(1)} %project.1.refs_0_), channel_id=1, source_target_pairs={{0,12},{4,8},{8,4},{12,0},{1,13},{5,9},{9,5},{13,1},{2,14},{6,10},... | collective-permute-start | bytes 442376 | tf_op jit(solution)/shard_map/ppermute | solution.py:407
  12.8 0.5 %collective-permute-start = (bf16[128,576]{1,0:T(8,128)(2,1)S(1)}, bf16[128,576]{1,0:T(8,128)(2,1)S(1)}, u32[]{:S(2)}, u32[]{:S(2)}) collective-permute-start(bf16[128,576]{1,0:T(8,128)(2,1)S(1)} %project.1.refs_0_), channel_id=1, source_target_pairs={{0,8},{4,12},{8,0},{12,4},{1,9},{5,13},{9,1},{13,5},{2,10},{6,14},... | collective-permute-start | bytes 442376 | tf_op jit(solution)/shard_map/ppermute | solution.py:407
  13.4 1.4 %collective-permute-start.4 = (s32[4]{0:T(128)S(1)}, s32[4]{0:T(128)S(1)}, u32[]{:S(2)}, u32[]{:S(2)}) collective-permute-start(s32[4]{0:T(128)S(1)} %copy-done.1), channel_id=1, source_target_pairs={{0,1},{3,2},{4,5},{7,6},{8,9},{11,10},{12,13},{15,14},{16,17},{19,... | collective-permute-start | bytes 56 | tf_op jit(solution)/shard_map/ppermute | solution.py:378
  14.8 3.3 %prefix_attention.3 = (f32[128,512]{1,0:T(8,128)S(1)}, f32[128,128]{1,0:T(8,128)S(1)}, f32[128,128]{1,0:T(8,128)S(1)}, bf16[128,640]{1,0:T(8,128)(2,1)S(1)}) custom-call(bf16[128,576]{1,0:T(8,128)(2,1)S(1)} %project.1.refs_0_, bf16[128,576]{1,0:T(8,128)(2,1)S(1)} %collective-permute-done.5.refs_1_, bf16[576,4096]{1,0:T(8,128)(2,1)S(1)} %bitcast.7), custom_call_target="tpu_custom_call" | custom-call | tf_op jit(solution)/shard_map/prefix_attention/pallas_call | solution.py:111
  18.1 0.7 %gather.3 = bf16[128,1152]{1,0:T(8,128)(2,1)S(1)} custom-call(s32[4]{0:T(128)S(1)} %collective-permute-done.4.names, bf16[128,1152]{1,0:T(8,128)(2,1)S(1)} %pack.1.refs_0_, bf16[128,1152]{1,0:T(8,128)(2,1)S(1)} %collective-permute-done.2.refs_1_, bf16[128,1152]{1,0:T(8,128)(2,1)S(1)} %collective-permute-done.3.refs_2_, ...), custom_call_target="tpu_custom_call" | custom-call | tf_op jit(solution)/shard_map/gather/pallas_call | solution.py:222
  18.8 4.0 %collective-permute-start.6 = (bf16[128,1152]{1,0:T(8,128)(2,1)S(1)}, bf16[128,1152]{1,0:T(8,128)(2,1)S(1)}, u32[]{:S(2)}, u32[]{:S(2)}) collective-permute-start(bf16[128,1152]{1,0:T(8,128)(2,1)S(1)} %gather.3), channel_id=1, source_target_pairs={{0,1},{1,0},{2,3},{3,2},{4,5},{5,4},{6,7},{7,6},{8,9},{9,8},{10,11... | collective-permute-start | bytes 884744 | tf_op jit(solution)/shard_map/ppermute | solution.py:417
  22.8 3.3 %prefix_attention.2 = (f32[256,512]{1,0:T(8,128)S(1)}, f32[256,128]{1,0:T(8,128)S(1)}, f32[256,128]{1,0:T(8,128)S(1)}) custom-call(bf16[128,576]{1,0:T(8,128)(2,1)S(1)} %collective-permute-done.refs_0_, bf16[128,576]{1,0:T(8,128)(2,1)S(1)} %collective-permute-done.1.refs_1_.refs_0_, bf16[576,4096]{1,0:T(8,128)(2,1)S(1)} %bitcast.8), custom_call_target="tpu_custom_call" | custom-call | flops 2281701376 | bytes 4718592 | tf_op jit(solution)/shard_map/prefix_attention/pallas_call | solution.py:111
  26.1 0.7 %gather.2.refs_4_ = bf16[128,1152]{1,0:T(8,128)(2,1)S(1)} custom-call(s32[4]{0:T(128)S(1)} %copy-done.1, bf16[128,1152]{1,0:T(8,128)(2,1)S(1)} %pack.1.refs_0_, bf16[128,1152]{1,0:T(8,128)(2,1)S(1)} %collective-permute-done.2.refs_1_, bf16[128,1152]{1,0:T(8,128)(2,1)S(1)} %collective-permute-done.3.refs_2_), custom_call_target="tpu_custom_call" | custom-call | tf_op jit(solution)/shard_map/gather/pallas_call | solution.py:222
  26.8 2.2 %collective-permute-done.6.refs_5_ = bf16[128,1152]{1,0:T(8,128)(2,1)S(1)} collective-permute-done((bf16[128,1152]{1,0:T(8,128)(2,1)S(1)}, bf16[128,1152]{1,0:T(8,128)(2,1)S(1)}, u32[]{:S(2)}, u32[]{:S(2)}) %collective-permute-start.6) | collective-permute-done | bytes 294944 | tf_op jit(solution)/shard_map/ppermute | solution.py:417
  29.0 1.4 %suffix_give.1 = (bf16[256,576]{1,0:T(8,128)(2,1)S(1)}, bf16[128,640]{1,0:T(8,128)(2,1)S(1)}) custom-call(s32[4]{0:T(128)S(1)} %copy-done.1, s32[16]{0:T(128)S(1)} %copy-done.3, bf16[128,576]{1,0:T(8,128)(2,1)S(1)} %collective-permute-done.1.refs_1_.refs_0_, f32[256,512]{1,0:T(8,128)S(1)} %get-tuple-element.17.refs_1_, ...), custom_call_target="tpu_custom_call" | custom-call | tf_op jit(solution)/shard_map/suffix_give/pallas_call | solution.py:426
  30.4 0.5 %collective-permute-start.7 = (bf16[128,640]{1,0:T(8,128)(2,1)S(1)}, bf16[128,640]{1,0:T(8,128)(2,1)S(1)}, u32[]{:S(2)}, u32[]{:S(2)}) collective-permute-start(bf16[128,640]{1,0:T(8,128)(2,1)S(1)} %get-tuple-element.22), channel_id=1, source_target_pairs={{0,4},{4,0},{8,12},{12,8},{1,5},{5,1},{9,13},{13,9},{2,6},{6,2},{1... | collective-permute-start | bytes 491528 | tf_op jit(solution)/shard_map/ppermute | solution.py:442
  30.9 0.1 collective-permute-start.10
  31.0 1.0 %suffix_keep.1.refs_0_ = bf16[128,640]{1,0:T(8,128)(2,1)S(1)} custom-call(s32[4]{0:T(128)S(1)} %copy-done.1, s32[16]{0:T(128)S(1)} %copy-done.3, bf16[128,576]{1,0:T(8,128)(2,1)S(1)} %collective-permute-done.refs_0_, f32[256,512]{1,0:T(8,128)S(1)} %get-tuple-element.17.refs_1_, f32[256,128]{1,0:T(8,128)S(1)} %get-tuple-element.18.refs_2_, ...), custom_call_target="tpu_custom_call" | custom-call | tf_op jit(solution)/shard_map/suffix_keep/pallas_call | solution.py:434
  32.0 0.2 collective-permute-done.7.refs_1_
  32.3 0.2 chip_merge.1
  32.5 1.6 %collective-permute-start.8 = (bf16[128,512]{1,0:T(8,128)(2,1)S(1)}, bf16[128,512]{1,0:T(8,128)(2,1)S(1)}, u32[]{:S(2)}, u32[]{:S(2)}) collective-permute-start(bf16[128,512]{1,0:T(8,128)(2,1)S(1)} %get-tuple-element.23), channel_id=1, source_target_pairs={{8,0},{12,4},{0,8},{4,12},{9,1},{13,5},{1,9},{5,13},{10,2},{14,6},... | collective-permute-start | bytes 393224 | tf_op jit(solution)/shard_map/ppermute | solution.py:443
  34.0 0.5 %collective-permute-start.9 = (f32[8,128]{1,0:T(8,128)S(1)}, f32[8,128]{1,0:T(8,128)S(1)}, u32[]{:S(2)}, u32[]{:S(2)}) collective-permute-start(f32[8,128]{1,0:T(8,128)S(1)} %get-tuple-element.24), channel_id=1, source_target_pairs={{8,0},{12,4},{0,8},{4,12},{9,1},{13,5},{1,9},{5,13},{10,2},{14,6},... | collective-permute-start | bytes 12296 | tf_op jit(solution)/shard_map/ppermute | solution.py:443
  34.6 1.6 %suffix_near.1 = (bf16[4,64,576]{2,1,0:T(8,128)(2,1)}, bf16[128,512]{1,0:T(8,128)(2,1)S(1)}, f32[128,128]{1,0:T(8,128)S(1)}) custom-call(s32[4]{0:T(128)S(1)} %copy-done.1, s32[16]{0:T(128)S(1)} %copy-done.3, bf16[4,576]{1,0:T(4,128)(2,1)S(1)} %copy-done.2, bf16[128,576]{1,0:T(8,128)(2,1)S(1)} %project.1.refs_0_, f32[128,512]{1,0:T(8,128)S(1)} %get-tuple-element.25.refs_1_, ...), custom_call_target="tpu_custom_call" | custom-call | tf_op jit(solution)/shard_map/suffix_near/pallas_call | solution.py:448
  36.2 2.0 %collective-permute-done.9.refs_1_ = f32[8,128]{1,0:T(8,128)S(1)} collective-permute-done((f32[8,128]{1,0:T(8,128)S(1)}, f32[8,128]{1,0:T(8,128)S(1)}, u32[]{:S(2)}, u32[]{:S(2)}) %collective-permute-start.9) | collective-permute-done | bytes 4128 | tf_op jit(solution)/shard_map/ppermute | solution.py:443
  38.2 1.4 %final.1 = bf16[4,32,128]{2,1,0:T(8,128)(2,1)} custom-call(bf16[128,512]{1,0:T(8,128)(2,1)S(1)} %collective-permute-done.8.refs_0_, f32[8,128]{1,0:T(8,128)S(1)} %collective-permute-done.9.refs_1_, bf16[128,512]{1,0:T(8,128)(2,1)S(1)} %get-tuple-element.29.refs_2_, f32[128,128]{1,0:T(8,128)S(1)} %get-tuple-element.30.refs_3_, bf16[32,512,128]{2,1,0:T(8,128)(2,1)S(1)} %copy-done), custom_call_target="tpu_custom_call" | custom-call | tf_op jit(solution)/shard_map/final/pallas_call | solution.py:458
  (34 shorter events, 0.3 us)
Async XLA Ops:
  0.6 9.9 %copy-start.4 = (bf16[32,128,512]{2,1,0:T(8,128)(2,1)S(1)}, bf16[32,128,512]{2,1,0:T(8,128)(2,1)}, u32[]{:S(2)}) copy-start(bf16[32,128,512]{2,1,0:T(8,128)(2,1)} %w_ref.1) | copy-start | bytes 12582916
  0.6 1.1 %copy-start.5 = (bf16[4,64,576]{2,1,0:T(8,128)(2,1)S(1)}, bf16[4,64,576]{2,1,0:T(8,128)(2,1)}, u32[]{:S(2)}) copy-start(bf16[4,64,576]{2,1,0:T(8,128)(2,1)} %cache_ref.1) | copy-start | bytes 884740
  1.8 8.7 %copy-start.6 = (bf16[4,32,128]{2,1,0:T(8,128)(2,1)S(1)}, bf16[4,32,128]{2,1,0:T(8,128)(2,1)}, u32[]{:S(2)}) copy-start(bf16[4,32,128]{2,1,0:T(8,128)(2,1)} %param.9) | copy-start | bytes 98308
  1.8 8.7 %copy-start.7 = (bf16[4,32,64]{2,1,0:T(8,128)(2,1)S(1)}, bf16[4,32,64]{2,1,0:T(8,128)(2,1)}, u32[]{:S(2)}) copy-start(bf16[4,32,64]{2,1,0:T(8,128)(2,1)} %param.10) | copy-start | bytes 49156
  1.8 13.0 %slice-start = ((s8[4718592]{0:T(1024)(128)(4,1)}), s8[4194304]{0:T(1024)(128)(4,1)S(1)}, s32[]{:S(2)}) async-start(s8[4718592]{0:T(1024)(128)(4,1)} %bitcast.5), calls=%async_computation | async-start | bytes 8388608
  1.8 16.3 %collective-permute-start.3 = (bf16[128,1152]{1,0:T(8,128)(2,1)S(1)}, bf16[128,1152]{1,0:T(8,128)(2,1)S(1)}, u32[]{:S(2)}, u32[]{:S(2)}) collective-permute-start(bf16[128,1152]{1,0:T(8,128)(2,1)S(1)} %pack.1.refs_0_), channel_id=1, source_target_pairs={{1,2},{2,1},{5,6},{6,5},{9,10},{10,9},{13,14},{14,13},{17,18},{18,... | collective-permute-start | bytes 884744 | tf_op jit(solution)/shard_map/ppermute | solution.py:377
  2.7 15.5 %collective-permute-start.2 = (bf16[128,1152]{1,0:T(8,128)(2,1)S(1)}, bf16[128,1152]{1,0:T(8,128)(2,1)S(1)}, u32[]{:S(2)}, u32[]{:S(2)}) collective-permute-start(bf16[128,1152]{1,0:T(8,128)(2,1)S(1)} %pack.1.refs_0_), channel_id=1, source_target_pairs={{0,2},{3,1},{4,6},{7,5},{8,10},{11,9},{12,14},{15,13},{16,18},{19,... | collective-permute-start | bytes 884744 | tf_op jit(solution)/shard_map/ppermute | solution.py:376
  10.5 4.3 %slice-start.1 = ((s8[4718592]{0:T(1024)(128)(4,1)}), s8[524288]{0:T(1024)(128)(4,1)S(1)}, s32[]{:S(2)}) async-start(s8[4718592]{0:T(1024)(128)(4,1)} %bitcast.5), calls=%async_computation.1 | async-start | bytes 1048576
  10.5 2.8 %copy-start.1 = (s32[4]{0:T(128)S(1)}, s32[4]{0:T(128)}, u32[]{:S(2)}) copy-start(s32[4]{0:T(128)} %anc.5) | copy-start | bytes 52
  11.2 2.2 %collective-permute-start.5 = (bf16[128,576]{1,0:T(8,128)(2,1)S(1)}, bf16[128,576]{1,0:T(8,128)(2,1)S(1)}, u32[]{:S(2)}, u32[]{:S(2)}) collective-permute-start(bf16[128,576]{1,0:T(8,128)(2,1)S(1)} %project.1.refs_0_), channel_id=1, source_target_pairs={{0,4},{4,0},{8,12},{12,8},{1,5},{5,1},{9,13},{13,9},{2,6},{6,2},{1... | collective-permute-start | bytes 442376 | tf_op jit(solution)/shard_map/ppermute | solution.py:407
  11.2 11.6 %collective-permute-start.1 = (bf16[128,576]{1,0:T(8,128)(2,1)S(1)}, bf16[128,576]{1,0:T(8,128)(2,1)S(1)}, u32[]{:S(2)}, u32[]{:S(2)}) collective-permute-start(bf16[128,576]{1,0:T(8,128)(2,1)S(1)} %project.1.refs_0_), channel_id=1, source_target_pairs={{0,12},{4,8},{8,4},{12,0},{1,13},{5,9},{9,5},{13,1},{2,14},{6,10},... | collective-permute-start | bytes 442376 | tf_op jit(solution)/shard_map/ppermute | solution.py:407
  12.8 10.0 %collective-permute-start = (bf16[128,576]{1,0:T(8,128)(2,1)S(1)}, bf16[128,576]{1,0:T(8,128)(2,1)S(1)}, u32[]{:S(2)}, u32[]{:S(2)}) collective-permute-start(bf16[128,576]{1,0:T(8,128)(2,1)S(1)} %project.1.refs_0_), channel_id=1, source_target_pairs={{0,8},{4,12},{8,0},{12,4},{1,9},{5,13},{9,1},{13,5},{2,10},{6,14},... | collective-permute-start | bytes 442376 | tf_op jit(solution)/shard_map/ppermute | solution.py:407
  13.4 4.8 %collective-permute-start.4 = (s32[4]{0:T(128)S(1)}, s32[4]{0:T(128)S(1)}, u32[]{:S(2)}, u32[]{:S(2)}) collective-permute-start(s32[4]{0:T(128)S(1)} %copy-done.1), channel_id=1, source_target_pairs={{0,1},{3,2},{4,5},{7,6},{8,9},{11,10},{12,13},{15,14},{16,17},{19,... | collective-permute-start | bytes 56 | tf_op jit(solution)/shard_map/ppermute | solution.py:378
  18.8 10.2 %copy-start.3 = (s32[16]{0:T(128)S(1)}, s32[16]{0:T(128)}, u32[]{:S(2)}) copy-start(s32[16]{0:T(128)} %lens.5) | copy-start | bytes 196
  18.8 10.2 %collective-permute-start.6 = (bf16[128,1152]{1,0:T(8,128)(2,1)S(1)}, bf16[128,1152]{1,0:T(8,128)(2,1)S(1)}, u32[]{:S(2)}, u32[]{:S(2)}) collective-permute-start(bf16[128,1152]{1,0:T(8,128)(2,1)S(1)} %gather.3), channel_id=1, source_target_pairs={{0,1},{1,0},{2,3},{3,2},{4,5},{5,4},{6,7},{7,6},{8,9},{9,8},{10,11... | collective-permute-start | bytes 884744 | tf_op jit(solution)/shard_map/ppermute | solution.py:417
  26.1 8.4 %copy-start.2 = (bf16[4,576]{1,0:T(4,128)(2,1)S(1)}, bf16[4,576]{1,0:T(4,128)(2,1)}, u32[]{:S(2)}) copy-start(bf16[4,576]{1,0:T(4,128)(2,1)} %fresh_ref.1) | copy-start | bytes 13828
  26.1 12.1 %copy-start = (bf16[32,512,128]{2,1,0:T(8,128)(2,1)S(1)}, bf16[32,512,128]{2,1,0:T(8,128)(2,1)}, u32[]{:S(2)}) copy-start(bf16[32,512,128]{2,1,0:T(8,128)(2,1)} %refs_4_.1) | copy-start | bytes 12582916
  30.3 4.2 %collective-permute-start.11 = (bf16[256,576]{1,0:T(8,128)(2,1)S(1)}, bf16[256,576]{1,0:T(8,128)(2,1)S(1)}, u32[]{:S(2)}, u32[]{:S(2)}) collective-permute-start(bf16[256,576]{1,0:T(8,128)(2,1)S(1)} %get-tuple-element.28.refs_4_.refs_5_), channel_id=1, source_target_pairs={{0,4},{4,0},{8,12},{12,8},{1,5},{5,1},{9,13},{13,9},{2,6},{6,2},{1... | collective-permute-start | bytes 884744 | tf_op jit(solution)/shard_map/ppermute | solution.py:444
  30.4 1.9 %collective-permute-start.7 = (bf16[128,640]{1,0:T(8,128)(2,1)S(1)}, bf16[128,640]{1,0:T(8,128)(2,1)S(1)}, u32[]{:S(2)}, u32[]{:S(2)}) collective-permute-start(bf16[128,640]{1,0:T(8,128)(2,1)S(1)} %get-tuple-element.22), channel_id=1, source_target_pairs={{0,4},{4,0},{8,12},{12,8},{1,5},{5,1},{9,13},{13,9},{2,6},{6,2},{1... | collective-permute-start | bytes 491528 | tf_op jit(solution)/shard_map/ppermute | solution.py:442
  30.9 3.6 %collective-permute-start.10 = (bf16[128,640]{1,0:T(8,128)(2,1)S(1)}, bf16[128,640]{1,0:T(8,128)(2,1)S(1)}, u32[]{:S(2)}, u32[]{:S(2)}) collective-permute-start(bf16[128,640]{1,0:T(8,128)(2,1)S(1)} %get-tuple-element.27), channel_id=1, source_target_pairs={{0,4},{4,0},{8,12},{12,8},{1,5},{5,1},{9,13},{13,9},{2,6},{6,2},{1... | collective-permute-start | bytes 491528 | tf_op jit(solution)/shard_map/ppermute | solution.py:414
  32.5 5.8 %collective-permute-start.8 = (bf16[128,512]{1,0:T(8,128)(2,1)S(1)}, bf16[128,512]{1,0:T(8,128)(2,1)S(1)}, u32[]{:S(2)}, u32[]{:S(2)}) collective-permute-start(bf16[128,512]{1,0:T(8,128)(2,1)S(1)} %get-tuple-element.23), channel_id=1, source_target_pairs={{8,0},{12,4},{0,8},{4,12},{9,1},{13,5},{1,9},{5,13},{10,2},{14,6},... | collective-permute-start | bytes 393224 | tf_op jit(solution)/shard_map/ppermute | solution.py:443
  34.0 4.2 %collective-permute-start.9 = (f32[8,128]{1,0:T(8,128)S(1)}, f32[8,128]{1,0:T(8,128)S(1)}, u32[]{:S(2)}, u32[]{:S(2)}) collective-permute-start(f32[8,128]{1,0:T(8,128)S(1)} %get-tuple-element.24), channel_id=1, source_target_pairs={{8,0},{12,4},{0,8},{4,12},{9,1},{13,5},{1,9},{5,13},{10,2},{14,6},... | collective-permute-start | bytes 12296 | tf_op jit(solution)/shard_map/ppermute | solution.py:443

commit v19 on v18

--- a/solution.py
+++ b/solution.py
@@ -23,6 +23,8 @@
 HBM = pl.BlockSpec(memory_space=pltpu.HBM)
 PARAMS = pltpu.CompilerParams(vmem_limit_bytes=40 * 1024 * 1024)
 NO_COST = pl.CostEstimate(flops=0, bytes_accessed=0, transcendentals=0)
+FOLD = 4
+PAD = 32
 PACK = 8_000_000_000
 PROJECT = 8_000_000_000
 
@@ -31,18 +33,22 @@
     return jax.ShapeDtypeStruct(dims, dtype)
 
 
-def pack_kernel(rank, cache_ref, out_ref):
+def pack_kernel(rank, cache_ref, out_ref, *part_refs):
     local, span, _ = cache_ref.shape
-    some = span // 2
+    piece = span // FOLD
     for p in range(local):
-        part = pl.ds(p * some, some)
-        first, second = cache_ref[p, :some], cache_ref[p, some:]
-        out_ref[part, :rank] = first[:, :rank]
-        out_ref[part, rank : 2 * rank] = second[:, :rank]
-        out_ref[part, 2 * rank :] = jnp.concatenate([first[:, rank:], second[:, rank:]], axis=1)
-
-
-def project_kernel(local, nope_ref, rope_ref, w_ref, own_ref):
+        part = pl.ds(p * piece, piece)
+        pieces = [cache_ref[p, q * piece : (q + 1) * piece] for q in range(FOLD)]
+        row = jnp.concatenate([x[:, :rank] for x in pieces] + [x[:, rank:] for x in pieces], axis=1)
+        out_ref[part] = row
+        begin = 0
+        for part_ref in part_refs:
+            end = begin + part_ref.shape[1]
+            part_ref[part] = row[:, begin:end]
+            begin = end
+
+
+def project_kernel(local, nope_ref, rope_ref, w_ref, own_ref, wide_ref):
     heads, _, rank = w_ref.shape
     nope = nope_ref[...].astype(F32)
     width = nope.shape[1]
@@ -59,6 +65,9 @@
         own_ref[pl.ds(h * local, 4 * local), :rank] = jnp.concatenate(
             [pair(i) for i in (h, h + 2)], axis=0
         ).astype(BF16)
+    rows = own_ref.shape[0]
+    wide_ref[pl.ds(0, rows)] = own_ref[...]
+    wide_ref[pl.ds(rows, PAD)] = jnp.zeros((PAD, own_ref.shape[1]), BF16)
 
 
 def prefix_kernel(count, tiles, *refs):
@@ -67,7 +76,8 @@
     rank = acc_ref.shape[1]
     tile = keys_ref.shape[1] // tiles
     parts = [pl.ds(i * tile, tile) for i in range(tiles)]
-    queries = jnp.concatenate([ref[...] for ref in query_refs], axis=0)
+    rows = acc_ref.shape[0] // count
+    queries = jnp.concatenate([ref[pl.ds(0, rows)] for ref in query_refs], axis=0)
 
     def score(i):
         return jnp.dot(queries, keys_ref[:, parts[i]], preferred_element_type=F32) * SCALE2
@@ -101,9 +111,9 @@
         give_ref[0][...] = packed(acc[kept:] * (1.0 / running[kept:]), level)
 
 
-def prefix_attention(queries, keys, rank, give, tiles=4):
-    rows = sum(q.shape[0] for q in queries)
-    kept = queries[0].shape[0] if give else rows
+def prefix_attention(queries, keys, rank, give, each, tiles=4):
+    kept = queries[0].shape[0] if give else len(queries) * each
+    rows = len(queries) * each
     width, length = keys.shape
     out = [shape((kept, rank), F32)] + [shape((kept, LANES), F32)] * 2
     if give:
@@ -195,11 +205,10 @@
 
 def gather_kernel(line, chosen, names, *refs):
     block_refs, out_ref = refs[:-1], refs[-1]
-    if chosen:
-        block_refs = block_refs[:-1]
+    block_refs = block_refs[: len(chosen) or None]
     dom = lax.axis_index("dom")
     local = names.shape[0]
-    some = out_ref.shape[0] // local
+    piece = out_ref.shape[0] // local
     for p in range(local):
         owner, slot = lax.div(names[p], local), lax.rem(names[p], local)
         if line:
@@ -209,18 +218,18 @@
                 slot = jnp.where(at_end(dom), p, slot)
         else:
             which = lax.rem(dom - owner + len(block_refs), len(block_refs))
-        rows = pl.ds(pl.multiple_of(slot * some, some), some)
-        for k, block_ref in enumerate(block_refs):
+        rows = pl.ds(pl.multiple_of(slot * piece, piece), piece)
+        for k, (block_ref, begin) in enumerate(zip(block_refs, chosen or [0] * len(block_refs))):
 
             @pl.when(which == k)
             def _():
-                out_ref[pl.ds(p * some, some)] = block_ref[rows]
-
-
-def gathered(names, blocks, line, token=None):
+                out_ref[pl.ds(p * piece, piece)] = block_ref[rows, pl.ds(begin, out_ref.shape[1])]
+
+
+def gathered(names, blocks, line, begins=(), token=None):
     token = [] if token is None else [token]
     return pl.pallas_call(
-        functools.partial(gather_kernel, line, bool(token)),
+        functools.partial(gather_kernel, line, begins),
         out_shape=shape(blocks[0].shape),
         in_specs=[SMEM] + [VMEM] * len(blocks) + [ANY] * len(token),
         out_specs=VMEM,
@@ -235,48 +244,57 @@
     local = anc.shape[0]
     span, rank = keys.shape[0] // local, acc_ref.shape[1]
     ends = [lens[anc[p]] for p in range(local)]
-    seen = visible(query_ref.shape[0], ends, [lax.axis_index("seq") * span], span)
+    rows = acc_ref.shape[0] // 2
+    seen = visible(rows, ends, [lax.axis_index("seq") * span], span)
     known = [(column(max_ref[part]), column(sum_ref[part]), acc_ref[part])]
-    return packed(*attend(query_ref[...], keys, seen, rank, known))
+    return packed(*attend(query_ref[pl.ds(0, rows)], keys, seen, rank, known))
 
 
 def give_kernel(stages, line, anc, lens, *refs):
     stage_refs, refs = refs[: 4 * stages], refs[4 * stages :]
-    early_ref, late_ref, moved_ref, give_refs = refs[0], refs[1], refs[2], refs[3:]
+    give_refs = refs[len(refs) - stages :]
+    source_refs, moved_ref = refs[: len(refs) - stages - 1], refs[len(refs) - stages - 1]
     dom = lax.axis_index("dom")
     local = anc.shape[0]
-    some = early_ref.shape[0] // local
-    span, width = 2 * some, moved_ref.shape[1]
+    piece = source_refs[0].shape[0] // local
+    span, width = FOLD * piece, moved_ref.shape[1]
     rank = stage_refs[1].shape[1]
 
     def place(p, value):
-        for h in range(2):
-            rows, rope = pl.ds(p * span + h * some, some), 2 * rank + h * (width - rank)
-            moved_ref[rows, :rank] = value[:, h * rank : (h + 1) * rank]
+        for q in range(FOLD):
+            rows, rope = pl.ds(p * span + q * piece, piece), FOLD * rank + q * (width - rank)
+            moved_ref[rows, :rank] = value[:, q * rank : (q + 1) * rank]
             moved_ref[rows, rank:] = value[:, rope : rope + width - rank]
 
     for p in range(local):
+        own_rows = pl.ds(p * piece, piece)
         if line:
+            near_ref, middle_refs, late_refs = source_refs[0], source_refs[1:3], source_refs[3:5]
             owner, slot = lax.div(anc[p], local), lax.rem(anc[p], local)
             apart = jnp.bitwise_xor(owner, dom)
             late = jnp.where(at_end(dom), apart != 0, apart == 1)
+            middle = jnp.logical_not(at_end(dom)) & (apart == 2)
             slot = jnp.where(at_end(dom), p, slot)
-            rows = pl.ds(pl.multiple_of(slot * some, some), some)
+            rows = pl.ds(pl.multiple_of(slot * piece, piece), piece)
 
             @pl.when(late)
             def _():
-                place(p, late_ref[rows])
-
-            @pl.when(jnp.logical_not(late))
+                place(p, jnp.concatenate([ref[rows] for ref in late_refs], axis=1))
+
+            @pl.when(middle)
             def _():
-                place(p, early_ref[pl.ds(p * some, some)])
+                place(p, jnp.concatenate([ref[rows] for ref in middle_refs], axis=1))
+
+            @pl.when(jnp.logical_not(late | middle))
+            def _():
+                place(p, near_ref[own_rows])
 
         else:
-            place(p, early_ref[pl.ds(p * some, some)])
+            place(p, source_refs[0][own_rows])
 
     for k in range(stages):
         query_ref, *partial = stage_refs[4 * k : 4 * k + 4]
-        rows = query_ref.shape[0]
+        rows = partial[0].shape[0] // 2
         give_refs[k][...] = far_part(anc, lens, query_ref, partial, pl.ds(rows, rows), moved_ref[...])
 
 
@@ -285,7 +303,7 @@
     moved_ref, keep_refs = refs[0], refs[1:]
     for k in range(stages):
         query_ref, *partial = stage_refs[4 * k : 4 * k + 4]
-        rows = query_ref.shape[0]
+        rows = partial[0].shape[0] // 2
         keep_refs[k][...] = far_part(anc, lens, query_ref, partial, pl.ds(0, rows), moved_ref[...])
 
 
@@ -360,33 +378,38 @@
     seq_size, dom_size = lax.axis_size("seq"), lax.axis_size("dom")
     cores = 2
     chips = seq_size // cores
-    block = pl.pallas_call(
+    pack_rows, lanes = local * span // FOLD, FOLD * width
+    cut = (lanes // LANES // 2 + 1) * LANES
+    block, *halves = pl.pallas_call(
         functools.partial(pack_kernel, rank),
-        out_shape=shape((local * span // 2, 2 * width)),
+        out_shape=[shape((pack_rows, wide)) for wide in (lanes, cut, lanes - cut)],
         in_specs=[VMEM],
-        out_specs=VMEM,
+        out_specs=[VMEM] * 3,
         compiler_params=PARAMS,
         cost_estimate=pl.CostEstimate(flops=PACK, bytes_accessed=0, transcendentals=0),
         name="pack",
     )(private_caches)
+    block, q_nope, q_rope = lax.optimization_barrier((block, q_nope, q_rope))
+    if dom_size == 4:
+        theirs = lax.ppermute(ancestors, "dom", [(0, 1), (1, 0), (2, 3), (3, 2)])
+        theirs, q_nope = lax.optimization_barrier((theirs, q_nope))
     nope_rows, rope_rows = (jnp.swapaxes(q, 0, 1).reshape(rows, -1) for q in (q_nope, q_rope))
     line = dom_size == 4
     if line:
         swap = [(0, 1), (1, 0), (2, 3), (3, 2)]
-        middle = lax.ppermute(block, "dom", [(0, 2), (3, 1)])
+        middle = [lax.ppermute(halves[0], "dom", [(0, 2), (3, 1)])]
         far = lax.ppermute(block, "dom", [(1, 2), (2, 1)])
-        theirs = lax.ppermute(ancestors, "dom", [(0, 1), (3, 2)])
     else:
         blocks = [block] + [
             lax.ppermute(block, "dom", [(i, (i + k) % dom_size) for i in range(dom_size)])
             for k in range(1, dom_size)
         ]
 
-    own = pl.pallas_call(
+    own, wide = pl.pallas_call(
         functools.partial(project_kernel, local),
-        out_shape=shape((rows, width)),
+        out_shape=(shape((rows, width)), shape((rows + PAD, width))),
         in_specs=[VMEM] * 3,
-        out_specs=VMEM,
+        out_specs=[VMEM] * 2,
         compiler_params=PARAMS,
         cost_estimate=pl.CostEstimate(flops=PROJECT, bytes_accessed=0, transcendentals=0),
         name="project",
@@ -404,20 +427,28 @@
         return [(b, a) for a, b in pairs(turn, flip)]
 
     routes = [(t, f) for t in range(chips) for f in range(cores)]
-    queries = [own if r == (0, 0) else lax.ppermute(own, "seq", pairs(*r)) for r in routes]
+    queries = [own, lax.ppermute(own, "seq", pairs(0, 1))]
+    queries += [lax.ppermute(wide, "seq", pairs(*r)) for r in routes[2:]]
     stages = []
     for t in range(chips):
         asked = queries[2 * t : 2 * t + 2]
-        stage = [*asked, *prefix_attention(asked, keys, rank, t == 0)]
+        stage = [*asked, *prefix_attention(asked, keys, rank, t == 0, rows)]
         stages.append(stage)
         if t == 0:
             given = lax.ppermute(stage.pop(), "seq", pairs(0, 1))
         if line and t == 0:
-            chosen = gathered(theirs, [block, middle, far], line, stage[3])
-            late = lax.ppermute(chosen, "dom", swap)
-            early = gathered(ancestors, [block, middle, far], line)
-    if not line:
-        early = late = gathered(ancestors, blocks, line)
+            rest, stage[3] = lax.optimization_barrier((halves[1], stage[3]))
+            middle.append(lax.ppermute(rest, "dom", [(0, 2), (3, 1)]))
+            token, sent = stage[3], []
+            for h, begin in enumerate((0, cut)):
+                sources = [halves[h], middle[h], far]
+                token = gathered(theirs, sources, line, (0, 0, begin), token)
+                sent.append(lax.ppermute(token, "dom", swap))
+    if line:
+        early = gathered(ancestors, [block, block, far], line)
+        sources = [early, *middle, *sent]
+    else:
+        sources = [gathered(ancestors, blocks, line)]
 
     part = shape((rows, rank + LANES))
     others = chips - 1
@@ -426,11 +457,11 @@
     moved, *give = pl.pallas_call(
         functools.partial(give_kernel, others, line),
         out_shape=[shape((local * span, width))] + [part] * others,
-        in_specs=[SMEM] * 2 + [VMEM] * (len(giving) + 2),
+        in_specs=[SMEM] * 2 + [VMEM] * (len(giving) + len(sources)),
         out_specs=[VMEM] * (1 + others),
         compiler_params=PARAMS,
         name="suffix_give",
-    )(ancestors, lengths, *giving, early, late)
+    )(ancestors, lengths, *giving, *sources)
     keep = pl.pallas_call(
         functools.partial(keep_kernel, others),
         out_shape=[part] * others,

time: 39.7 us -> 42.4 us (1.068)
  starting transfers between devices: 18.9 us -> 23.1 us
  waiting for transfers between devices: 4.45 us -> 2.29 us
  Pallas kernels: 14.2 us -> 14.8 us
    ppermute x6 -> x8, starting transfers between devices: 15.3 us -> 19.6 us  [the longest x2 7.19 us: on_device(): sent.append(lax.ppermute(token, 'dom', swap))]
    ppermute x6 -> x8, waiting for transfers between devices: 2.19 us -> 0.02 us  [the longest x2 0.01 us: on_device(): queries += [lax.ppermute(wide, 'seq', pairs(*r)) for r in routes[2:]]]
    pallas_call x4 -> x5, Pallas kernels: 2.04 us -> 2.67 us  [the longest x3 1.95 us: gathered(): pl.pallas_call(functools.partial(gather_kernel, line, begins), out_shape=...]
  transfers between devices with their start and end apart: 12 -> 14, of which waited for: 3 -> 2; matrix products, arithmetic and copies ran while one was open for 0% -> 0% of each run, Pallas kernels for 29% -> 29%
where the time goes in v19:
time: 42.4 us; the launch traced here: 42.2 us
  starting transfers between devices  23.1 us (54%)
  Pallas kernels  14.8 us (35%)
  waiting for transfers between devices  2.29 us (5%)
  local copies, waits for them, and re-layouts  1.06 us (2%)
  between operations  0.91 us (2%)
    ppermute x2, starting transfers between devices, on_device(): sent.append(lax.ppermute(token, 'dom', swap))  7.19 us
    pallas_call x2, Pallas kernels, prefix_attention(): pl.pallas_call(functools.partial(prefix_kernel, len(queries), tiles), out...  6.58 us
    ppermute x1, starting transfers between devices, on_device(): middle = [lax.ppermute(halves[0], 'dom', [(0, 2), (3, 1)])]  5.86 us
    ppermute x1, starting transfers between devices, on_device(): theirs = lax.ppermute(ancestors, 'dom', [(0, 1), (1, 0), (2, 3), (3, 2)])  3.09 us
    ppermute x2, starting transfers between devices, on_device(): queries += [lax.ppermute(wide, 'seq', pairs(*r)) for r in routes[2:]]  2.14 us
    ppermute x2, starting transfers between devices, on_device(): lax.ppermute(s, 'seq', back(1 + i // 2, 0))  2.09 us
    ppermute x2, waiting for transfers between devices, on_device(): lax.ppermute(s, 'seq', back(1 + i // 2, 0))  2.03 us
    pallas_call x3, Pallas kernels, gathered(): pl.pallas_call(functools.partial(gather_kernel, line, begins), out_shape=...  1.95 us
  transfers between devices with their start and end apart: 14, of which 2 were waited for; matrix products, arithmetic and copies ran while one was open for 0% of the time, Pallas kernels for 29%

profile of v19, /device:TPU:0, one launch (start us, length us, event | category | flops | bytes accessed | tf_op | source)
XLA Modules:
  0.0 42.2 jit_solution(7499455685538949233)
XLA Ops:
  0.6 3.1 %collective-permute-start = (s32[4]{0:T(128)}, s32[4]{0:T(128)S(1)}, u32[]{:S(2)}, u32[]{:S(2)}) collective-permute-start(s32[4]{0:T(128)} %anc.5), channel_id=1, source_target_pairs={{0,1},{1,0},{2,3},{3,2},{4,5},{5,4},{6,7},{7,6},{8,9},{9,8},{10,11... | collective-permute-start | bytes 56 | tf_op jit(solution)/shard_map/ppermute | solution.py:394
  3.7 1.0 %copy-done.5 = bf16[4,64,576]{2,1,0:T(8,128)(2,1)S(1)} copy-done((bf16[4,64,576]{2,1,0:T(8,128)(2,1)S(1)}, bf16[4,64,576]{2,1,0:T(8,128)(2,1)}, u32[]{:S(2)}) %copy-start.5) | copy-done | bytes 294936
  4.8 0.8 %collective-permute-start.3 = (bf16[64,2304]{1,0:T(8,128)(2,1)S(1)}, bf16[64,2304]{1,0:T(8,128)(2,1)S(1)}, u32[]{:S(2)}, u32[]{:S(2)}) collective-permute-start(bf16[64,2304]{1,0:T(8,128)(2,1)S(1)} %get-tuple-element.37.refs_0_.refs_1_), channel_id=1, source_target_pairs={{1,2},{2,1},{5,6},{6,5},{9,10},{10,9},{13,14},{14,13},{17,18},{18,... | collective-permute-start | bytes 884744 | tf_op jit(solution)/shard_map/ppermute | solution.py:401
  5.7 0.6 %project.1 = (bf16[128,576]{1,0:T(8,128)(2,1)S(1)}, bf16[160,576]{1,0:T(8,128)(2,1)S(1)}) custom-call(bf16[128,128]{1,0:T(8,128)(2,1)S(1)} %bitcast.10, bf16[128,64]{1,0:T(8,128)(2,1)S(1)} %bitcast.9, bf16[32,128,512]{2,1,0:T(8,128)(2,1)S(1)} %copy-done.4), custom_call_target="tpu_custom_call" | custom-call | flops 8000000000 | tf_op jit(solution)/shard_map/project/pallas_call | solution.py:408
  6.4 1.8 %collective-permute-start.2 = (bf16[160,576]{1,0:T(8,128)(2,1)S(1)}, bf16[160,576]{1,0:T(8,128)(2,1)S(1)}, u32[]{:S(2)}, u32[]{:S(2)}) collective-permute-start(bf16[160,576]{1,0:T(8,128)(2,1)S(1)} %get-tuple-element.33), channel_id=1, source_target_pairs={{0,12},{4,8},{8,4},{12,0},{1,13},{5,9},{9,5},{13,1},{2,14},{6,10},... | collective-permute-start | bytes 552968 | tf_op jit(solution)/shard_map/ppermute | solution.py:431
  8.1 0.4 collective-permute-start.1
  8.5 5.9 %collective-permute-start.4 = (bf16[64,1280]{1,0:T(8,128)(2,1)S(1)}, bf16[64,1280]{1,0:T(8,128)(2,1)S(1)}, u32[]{:S(2)}, u32[]{:S(2)}) collective-permute-start(bf16[64,1280]{1,0:T(8,128)(2,1)S(1)} %get-tuple-element.38.refs_0_), channel_id=1, source_target_pairs={{0,2},{3,1},{4,6},{7,5},{8,10},{11,9},{12,14},{15,13},{16,18},{19,... | collective-permute-start | bytes 491528 | tf_op jit(solution)/shard_map/ppermute | solution.py:400
  14.4 3.3 %prefix_attention.3 = (f32[128,512]{1,0:T(8,128)S(1)}, f32[128,128]{1,0:T(8,128)S(1)}, f32[128,128]{1,0:T(8,128)S(1)}, bf16[128,640]{1,0:T(8,128)(2,1)S(1)}) custom-call(bf16[128,576]{1,0:T(8,128)(2,1)S(1)} %get-tuple-element.40.refs_0_, bf16[128,576]{1,0:T(8,128)(2,1)S(1)} %collective-permute-done.5.refs_1_, bf16[576,4096]{1,0:T(8,128)(2,1)S(1)} %bitcast.7), custom_call_target="tpu_custom_call" | custom-call | tf_op jit(solution)/shard_map/prefix_attention/pallas_call | solution.py:121
  17.8 1.3 %collective-permute-start.6 = (bf16[64,1024]{1,0:T(8,128)(2,1)S(1)}, bf16[64,1024]{1,0:T(8,128)(2,1)S(1)}, u32[]{:S(2)}, u32[]{:S(2)}) collective-permute-start(bf16[64,1024]{1,0:T(8,128)(2,1)S(1)} %get-tuple-element.42.refs_0_), channel_id=1, source_target_pairs={{0,2},{3,1},{4,6},{7,5},{8,10},{11,9},{12,14},{15,13},{16,18},{19,... | collective-permute-start | bytes 393224 | tf_op jit(solution)/shard_map/ppermute | solution.py:441
  19.1 0.6 %gather.4.refs_3_ = bf16[64,1280]{1,0:T(8,128)(2,1)S(1)} custom-call(s32[4]{0:T(128)S(1)} %collective-permute-done.names, bf16[64,1280]{1,0:T(8,128)(2,1)S(1)} %get-tuple-element.38.refs_0_, bf16[64,1280]{1,0:T(8,128)(2,1)S(1)} %collective-permute-done.4.refs_1_.refs_5_, bf16[64,2304]{1,0:T(8,128)(2,1)S(1)} %collective-permute-done.3.refs_2_, ...), custom_call_target="tpu_custom_call" | custom-call | tf_op jit(solution)/shard_map/gather/pallas_call | solution.py:231
  19.7 2.7 %collective-permute-start.7 = (bf16[64,1280]{1,0:T(8,128)(2,1)S(1)}, bf16[64,1280]{1,0:T(8,128)(2,1)S(1)}, u32[]{:S(2)}, u32[]{:S(2)}) collective-permute-start(bf16[64,1280]{1,0:T(8,128)(2,1)S(1)} %gather.4.refs_3_), channel_id=1, source_target_pairs={{0,1},{1,0},{2,3},{3,2},{4,5},{5,4},{6,7},{7,6},{8,9},{9,8},{10,11... | collective-permute-start | bytes 491528 | tf_op jit(solution)/shard_map/ppermute | solution.py:446
  22.4 0.6 %gather.5 = bf16[64,1024]{1,0:T(8,128)(2,1)S(1)} custom-call(s32[4]{0:T(128)S(1)} %collective-permute-done.names, bf16[64,1024]{1,0:T(8,128)(2,1)S(1)} %get-tuple-element.42.refs_0_, bf16[64,1024]{1,0:T(8,128)(2,1)S(1)} %collective-permute-done.6.refs_1_.refs_6_, bf16[64,2304]{1,0:T(8,128)(2,1)S(1)} %collective-permute-done.3.refs_2_, ...), custom_call_target="tpu_custom_call" | custom-call | tf_op jit(solution)/shard_map/gather/pallas_call | solution.py:231
  23.1 4.5 %collective-permute-start.8 = (bf16[64,1024]{1,0:T(8,128)(2,1)S(1)}, bf16[64,1024]{1,0:T(8,128)(2,1)S(1)}, u32[]{:S(2)}, u32[]{:S(2)}) collective-permute-start(bf16[64,1024]{1,0:T(8,128)(2,1)S(1)} %gather.5), channel_id=1, source_target_pairs={{0,1},{1,0},{2,3},{3,2},{4,5},{5,4},{6,7},{7,6},{8,9},{9,8},{10,11... | collective-permute-start | bytes 393224 | tf_op jit(solution)/shard_map/ppermute | solution.py:446
  27.6 3.3 %prefix_attention.2 = (f32[256,512]{1,0:T(8,128)S(1)}, f32[256,128]{1,0:T(8,128)S(1)}, f32[256,128]{1,0:T(8,128)S(1)}) custom-call(bf16[160,576]{1,0:T(8,128)(2,1)S(1)} %collective-permute-done.1.refs_0_, bf16[160,576]{1,0:T(8,128)(2,1)S(1)} %collective-permute-done.2.refs_1_.refs_0_, bf16[576,4096]{1,0:T(8,128)(2,1)S(1)} %bitcast.8), custom_call_target="tpu_custom_call" | custom-call | flops 2281701376 | bytes 4718592 | tf_op jit(solution)/shard_map/prefix_attention/pallas_call | solution.py:121
  30.9 0.7 %gather.3.refs_4_ = bf16[64,2304]{1,0:T(8,128)(2,1)S(1)} custom-call(s32[4]{0:T(128)S(1)} %copy-done.1, bf16[64,2304]{1,0:T(8,128)(2,1)S(1)} %get-tuple-element.37.refs_0_.refs_1_, bf16[64,2304]{1,0:T(8,128)(2,1)S(1)} %get-tuple-element.37.refs_0_.refs_1_, bf16[64,2304]{1,0:T(8,128)(2,1)S(1)} %collective-permute-done.3.refs_2_), custom_call_target="tpu_custom_call" | custom-call | tf_op jit(solution)/shard_map/gather/pallas_call | solution.py:231
  31.6 1.4 %suffix_give.1 = (bf16[256,576]{1,0:T(8,128)(2,1)S(1)}, bf16[128,640]{1,0:T(8,128)(2,1)S(1)}) custom-call(s32[4]{0:T(128)S(1)} %copy-done.1, s32[16]{0:T(128)S(1)} %copy-done.3, bf16[160,576]{1,0:T(8,128)(2,1)S(1)} %collective-permute-done.2.refs_1_.refs_0_, f32[256,512]{1,0:T(8,128)S(1)} %get-tuple-element.34.refs_1_, ...), custom_call_target="tpu_custom_call" | custom-call | tf_op jit(solution)/shard_map/suffix_give/pallas_call | solution.py:457
  33.1 0.5 %collective-permute-start.9 = (bf16[128,640]{1,0:T(8,128)(2,1)S(1)}, bf16[128,640]{1,0:T(8,128)(2,1)S(1)}, u32[]{:S(2)}, u32[]{:S(2)}) collective-permute-start(bf16[128,640]{1,0:T(8,128)(2,1)S(1)} %get-tuple-element.46), channel_id=1, source_target_pairs={{0,4},{4,0},{8,12},{12,8},{1,5},{5,1},{9,13},{13,9},{2,6},{6,2},{1... | collective-permute-start | bytes 491528 | tf_op jit(solution)/shard_map/ppermute | solution.py:473
  33.6 1.0 %suffix_keep.1.refs_0_ = bf16[128,640]{1,0:T(8,128)(2,1)S(1)} custom-call(s32[4]{0:T(128)S(1)} %copy-done.1, s32[16]{0:T(128)S(1)} %copy-done.3, bf16[160,576]{1,0:T(8,128)(2,1)S(1)} %collective-permute-done.1.refs_0_, f32[256,512]{1,0:T(8,128)S(1)} %get-tuple-element.34.refs_1_, f32[256,128]{1,0:T(8,128)S(1)} %get-tuple-element.35.refs_2_, ...), custom_call_target="tpu_custom_call" | custom-call | tf_op jit(solution)/shard_map/suffix_keep/pallas_call | solution.py:465
  34.7 0.2 collective-permute-done.9.refs_1_
  35.1 1.6 %collective-permute-start.10 = (bf16[128,512]{1,0:T(8,128)(2,1)S(1)}, bf16[128,512]{1,0:T(8,128)(2,1)S(1)}, u32[]{:S(2)}, u32[]{:S(2)}) collective-permute-start(bf16[128,512]{1,0:T(8,128)(2,1)S(1)} %get-tuple-element.47), channel_id=1, source_target_pairs={{8,0},{12,4},{0,8},{4,12},{9,1},{13,5},{1,9},{5,13},{10,2},{14,6},... | collective-permute-start | bytes 393224 | tf_op jit(solution)/shard_map/ppermute | solution.py:474
  36.7 0.5 %collective-permute-start.11 = (f32[8,128]{1,0:T(8,128)S(1)}, f32[8,128]{1,0:T(8,128)S(1)}, u32[]{:S(2)}, u32[]{:S(2)}) collective-permute-start(f32[8,128]{1,0:T(8,128)S(1)} %get-tuple-element.48), channel_id=1, source_target_pairs={{8,0},{12,4},{0,8},{4,12},{9,1},{13,5},{1,9},{5,13},{10,2},{14,6},... | collective-permute-start | bytes 12296 | tf_op jit(solution)/shard_map/ppermute | solution.py:474
  37.2 1.6 %suffix_near.1 = (bf16[4,64,576]{2,1,0:T(8,128)(2,1)}, bf16[128,512]{1,0:T(8,128)(2,1)S(1)}, f32[128,128]{1,0:T(8,128)S(1)}) custom-call(s32[4]{0:T(128)S(1)} %copy-done.1, s32[16]{0:T(128)S(1)} %copy-done.3, bf16[4,576]{1,0:T(4,128)(2,1)S(1)} %copy-done.2, bf16[128,576]{1,0:T(8,128)(2,1)S(1)} %get-tuple-element.40.refs_0_, ...), custom_call_target="tpu_custom_call" | custom-call | tf_op jit(solution)/shard_map/suffix_near/pallas_call | solution.py:479
  38.8 2.0 %collective-permute-done.11.refs_1_ = f32[8,128]{1,0:T(8,128)S(1)} collective-permute-done((f32[8,128]{1,0:T(8,128)S(1)}, f32[8,128]{1,0:T(8,128)S(1)}, u32[]{:S(2)}, u32[]{:S(2)}) %collective-permute-start.11) | collective-permute-done | bytes 4128 | tf_op jit(solution)/shard_map/ppermute | solution.py:474
  40.9 1.4 %final.1 = bf16[4,32,128]{2,1,0:T(8,128)(2,1)} custom-call(bf16[128,512]{1,0:T(8,128)(2,1)S(1)} %collective-permute-done.10.refs_0_, f32[8,128]{1,0:T(8,128)S(1)} %collective-permute-done.11.refs_1_, bf16[128,512]{1,0:T(8,128)(2,1)S(1)} %get-tuple-element.53.refs_2_, f32[128,128]{1,0:T(8,128)S(1)} %get-tuple-element.54.refs_3_, bf16[32,512,128]{2,1,0:T(8,128)(2,1)S(1)} %copy-done), custom_call_target="tpu_custom_call" | custom-call | tf_op jit(solution)/shard_map/final/pallas_call | solution.py:489
  (39 shorter events, 0.5 us)
Async XLA Ops:
  0.6 5.1 %copy-start.4 = (bf16[32,128,512]{2,1,0:T(8,128)(2,1)S(1)}, bf16[32,128,512]{2,1,0:T(8,128)(2,1)}, u32[]{:S(2)}) copy-start(bf16[32,128,512]{2,1,0:T(8,128)(2,1)} %w_ref.1) | copy-start | bytes 12582916
  0.6 5.0 %collective-permute-start = (s32[4]{0:T(128)}, s32[4]{0:T(128)S(1)}, u32[]{:S(2)}, u32[]{:S(2)}) collective-permute-start(s32[4]{0:T(128)} %anc.5), channel_id=1, source_target_pairs={{0,1},{1,0},{2,3},{3,2},{4,5},{5,4},{6,7},{7,6},{8,9},{9,8},{10,11... | collective-permute-start | bytes 56 | tf_op jit(solution)/shard_map/ppermute | solution.py:394
  3.7 1.0 %copy-start.5 = (bf16[4,64,576]{2,1,0:T(8,128)(2,1)S(1)}, bf16[4,64,576]{2,1,0:T(8,128)(2,1)}, u32[]{:S(2)}) copy-start(bf16[4,64,576]{2,1,0:T(8,128)(2,1)} %cache_ref.1) | copy-start | bytes 884740
  4.7 0.9 %copy-start.6 = (bf16[4,32,64]{2,1,0:T(8,128)(2,1)S(1)}, bf16[4,32,64]{2,1,0:T(8,128)(2,1)}, u32[]{:S(2)}) copy-start(bf16[4,32,64]{2,1,0:T(8,128)(2,1)} %param.10) | copy-start | bytes 49156
  4.7 0.9 %copy-start.7 = (bf16[4,32,128]{2,1,0:T(8,128)(2,1)S(1)}, bf16[4,32,128]{2,1,0:T(8,128)(2,1)}, u32[]{:S(2)}) copy-start(bf16[4,32,128]{2,1,0:T(8,128)(2,1)} %param.9) | copy-start | bytes 98308
  4.7 9.7 %slice-start = ((s8[4718592]{0:T(1024)(128)(4,1)}), s8[4194304]{0:T(1024)(128)(4,1)S(1)}, s32[]{:S(2)}) async-start(s8[4718592]{0:T(1024)(128)(4,1)} %bitcast.5), calls=%async_computation | async-start | bytes 8388608
  4.8 14.3 %collective-permute-start.3 = (bf16[64,2304]{1,0:T(8,128)(2,1)S(1)}, bf16[64,2304]{1,0:T(8,128)(2,1)S(1)}, u32[]{:S(2)}, u32[]{:S(2)}) collective-permute-start(bf16[64,2304]{1,0:T(8,128)(2,1)S(1)} %get-tuple-element.37.refs_0_.refs_1_), channel_id=1, source_target_pairs={{1,2},{2,1},{5,6},{6,5},{9,10},{10,9},{13,14},{14,13},{17,18},{18,... | collective-permute-start | bytes 884744 | tf_op jit(solution)/shard_map/ppermute | solution.py:401
  5.7 8.8 %slice-start.1 = ((s8[4718592]{0:T(1024)(128)(4,1)}), s8[524288]{0:T(1024)(128)(4,1)S(1)}, s32[]{:S(2)}) async-start(s8[4718592]{0:T(1024)(128)(4,1)} %bitcast.5), calls=%async_computation.1 | async-start | bytes 1048576
  6.3 8.0 %collective-permute-start.5 = (bf16[128,576]{1,0:T(8,128)(2,1)S(1)}, bf16[128,576]{1,0:T(8,128)(2,1)S(1)}, u32[]{:S(2)}, u32[]{:S(2)}) collective-permute-start(bf16[128,576]{1,0:T(8,128)(2,1)S(1)} %get-tuple-element.40.refs_0_), channel_id=1, source_target_pairs={{0,4},{4,0},{8,12},{12,8},{1,5},{5,1},{9,13},{13,9},{2,6},{6,2},{1... | collective-permute-start | bytes 442376 | tf_op jit(solution)/shard_map/ppermute | solution.py:430
  6.4 21.2 %collective-permute-start.2 = (bf16[160,576]{1,0:T(8,128)(2,1)S(1)}, bf16[160,576]{1,0:T(8,128)(2,1)S(1)}, u32[]{:S(2)}, u32[]{:S(2)}) collective-permute-start(bf16[160,576]{1,0:T(8,128)(2,1)S(1)} %get-tuple-element.33), channel_id=1, source_target_pairs={{0,12},{4,8},{8,4},{12,0},{1,13},{5,9},{9,5},{13,1},{2,14},{6,10},... | collective-permute-start | bytes 552968 | tf_op jit(solution)/shard_map/ppermute | solution.py:431
  8.1 19.5 %collective-permute-start.1 = (bf16[160,576]{1,0:T(8,128)(2,1)S(1)}, bf16[160,576]{1,0:T(8,128)(2,1)S(1)}, u32[]{:S(2)}, u32[]{:S(2)}) collective-permute-start(bf16[160,576]{1,0:T(8,128)(2,1)S(1)} %get-tuple-element.33), channel_id=1, source_target_pairs={{0,8},{4,12},{8,0},{12,4},{1,9},{5,13},{9,1},{13,5},{2,10},{6,14},... | collective-permute-start | bytes 552968 | tf_op jit(solution)/shard_map/ppermute | solution.py:431
  8.5 10.5 %collective-permute-start.4 = (bf16[64,1280]{1,0:T(8,128)(2,1)S(1)}, bf16[64,1280]{1,0:T(8,128)(2,1)S(1)}, u32[]{:S(2)}, u32[]{:S(2)}) collective-permute-start(bf16[64,1280]{1,0:T(8,128)(2,1)S(1)} %get-tuple-element.38.refs_0_), channel_id=1, source_target_pairs={{0,2},{3,1},{4,6},{7,5},{8,10},{11,9},{12,14},{15,13},{16,18},{19,... | collective-permute-start | bytes 491528 | tf_op jit(solution)/shard_map/ppermute | solution.py:400
  17.8 4.7 %collective-permute-start.6 = (bf16[64,1024]{1,0:T(8,128)(2,1)S(1)}, bf16[64,1024]{1,0:T(8,128)(2,1)S(1)}, u32[]{:S(2)}, u32[]{:S(2)}) collective-permute-start(bf16[64,1024]{1,0:T(8,128)(2,1)S(1)} %get-tuple-element.42.refs_0_), channel_id=1, source_target_pairs={{0,2},{3,1},{4,6},{7,5},{8,10},{11,9},{12,14},{15,13},{16,18},{19,... | collective-permute-start | bytes 393224 | tf_op jit(solution)/shard_map/ppermute | solution.py:441
  19.7 11.9 %collective-permute-start.7 = (bf16[64,1280]{1,0:T(8,128)(2,1)S(1)}, bf16[64,1280]{1,0:T(8,128)(2,1)S(1)}, u32[]{:S(2)}, u32[]{:S(2)}) collective-permute-start(bf16[64,1280]{1,0:T(8,128)(2,1)S(1)} %gather.4.refs_3_), channel_id=1, source_target_pairs={{0,1},{1,0},{2,3},{3,2},{4,5},{5,4},{6,7},{7,6},{8,9},{9,8},{10,11... | collective-permute-start | bytes 491528 | tf_op jit(solution)/shard_map/ppermute | solution.py:446
  23.1 7.8 %copy-start.1 = (s32[4]{0:T(128)S(1)}, s32[4]{0:T(128)}, u32[]{:S(2)}) copy-start(s32[4]{0:T(128)} %anc.5) | copy-start | bytes 52
  23.1 8.5 %copy-start.3 = (s32[16]{0:T(128)S(1)}, s32[16]{0:T(128)}, u32[]{:S(2)}) copy-start(s32[16]{0:T(128)} %lens.5) | copy-start | bytes 196
  23.1 8.5 %collective-permute-start.8 = (bf16[64,1024]{1,0:T(8,128)(2,1)S(1)}, bf16[64,1024]{1,0:T(8,128)(2,1)S(1)}, u32[]{:S(2)}, u32[]{:S(2)}) collective-permute-start(bf16[64,1024]{1,0:T(8,128)(2,1)S(1)} %gather.5), channel_id=1, source_target_pairs={{0,1},{1,0},{2,3},{3,2},{4,5},{5,4},{6,7},{7,6},{8,9},{9,8},{10,11... | collective-permute-start | bytes 393224 | tf_op jit(solution)/shard_map/ppermute | solution.py:446
  30.9 6.3 %copy-start.2 = (bf16[4,576]{1,0:T(4,128)(2,1)S(1)}, bf16[4,576]{1,0:T(4,128)(2,1)}, u32[]{:S(2)}) copy-start(bf16[4,576]{1,0:T(4,128)(2,1)} %fresh_ref.1) | copy-start | bytes 13828
  30.9 10.0 %copy-start = (bf16[32,512,128]{2,1,0:T(8,128)(2,1)S(1)}, bf16[32,512,128]{2,1,0:T(8,128)(2,1)}, u32[]{:S(2)}) copy-start(bf16[32,512,128]{2,1,0:T(8,128)(2,1)} %refs_4_.1) | copy-start | bytes 12582916
  33.0 4.2 %collective-permute-start.13 = (bf16[256,576]{1,0:T(8,128)(2,1)S(1)}, bf16[256,576]{1,0:T(8,128)(2,1)S(1)}, u32[]{:S(2)}, u32[]{:S(2)}) collective-permute-start(bf16[256,576]{1,0:T(8,128)(2,1)S(1)} %get-tuple-element.52.refs_4_.refs_5_), channel_id=1, source_target_pairs={{0,4},{4,0},{8,12},{12,8},{1,5},{5,1},{9,13},{13,9},{2,6},{6,2},{1... | collective-permute-start | bytes 884744 | tf_op jit(solution)/shard_map/ppermute | solution.py:475
  33.1 1.9 %collective-permute-start.9 = (bf16[128,640]{1,0:T(8,128)(2,1)S(1)}, bf16[128,640]{1,0:T(8,128)(2,1)S(1)}, u32[]{:S(2)}, u32[]{:S(2)}) collective-permute-start(bf16[128,640]{1,0:T(8,128)(2,1)S(1)} %get-tuple-element.46), channel_id=1, source_target_pairs={{0,4},{4,0},{8,12},{12,8},{1,5},{5,1},{9,13},{13,9},{2,6},{6,2},{1... | collective-permute-start | bytes 491528 | tf_op jit(solution)/shard_map/ppermute | solution.py:473
  33.6 3.6 %collective-permute-start.12 = (bf16[128,640]{1,0:T(8,128)(2,1)S(1)}, bf16[128,640]{1,0:T(8,128)(2,1)S(1)}, u32[]{:S(2)}, u32[]{:S(2)}) collective-permute-start(bf16[128,640]{1,0:T(8,128)(2,1)S(1)} %get-tuple-element.51), channel_id=1, source_target_pairs={{0,4},{4,0},{8,12},{12,8},{1,5},{5,1},{9,13},{13,9},{2,6},{6,2},{1... | collective-permute-start | bytes 491528 | tf_op jit(solution)/shard_map/ppermute | solution.py:438
  35.1 5.8 %collective-permute-start.10 = (bf16[128,512]{1,0:T(8,128)(2,1)S(1)}, bf16[128,512]{1,0:T(8,128)(2,1)S(1)}, u32[]{:S(2)}, u32[]{:S(2)}) collective-permute-start(bf16[128,512]{1,0:T(8,128)(2,1)S(1)} %get-tuple-element.47), channel_id=1, source_target_pairs={{8,0},{12,4},{0,8},{4,12},{9,1},{13,5},{1,9},{5,13},{10,2},{14,6},... | collective-permute-start | bytes 393224 | tf_op jit(solution)/shard_map/ppermute | solution.py:474
  36.7 4.2 %collective-permute-start.11 = (f32[8,128]{1,0:T(8,128)S(1)}, f32[8,128]{1,0:T(8,128)S(1)}, u32[]{:S(2)}, u32[]{:S(2)}) collective-permute-start(f32[8,128]{1,0:T(8,128)S(1)} %get-tuple-element.48), channel_id=1, source_target_pairs={{8,0},{12,4},{0,8},{4,12},{9,1},{13,5},{1,9},{5,13},{10,2},{14,6},... | collective-permute-start | bytes 12296 | tf_op jit(solution)/shard_map/ppermute | solution.py:474

commit v20 on v18

--- a/solution.py
+++ b/solution.py
@@ -282,7 +282,11 @@
 
 def keep_kernel(stages, anc, lens, *refs):
     stage_refs, refs = refs[: 4 * stages], refs[4 * stages :]
-    moved_ref, keep_refs = refs[0], refs[1:]
+    moved_ref, keep_refs, piece_refs = refs[0], refs[1 : 1 + stages], refs[1 + stages :]
+    begin = 0
+    for piece_ref in piece_refs:
+        piece_ref[...] = moved_ref[pl.ds(begin, piece_ref.shape[0])]
+        begin += piece_ref.shape[0]
     for k in range(stages):
         query_ref, *partial = stage_refs[4 * k : 4 * k + 4]
         rows = query_ref.shape[0]
@@ -291,12 +295,13 @@
 
 def near_kernel(anc, lens, fresh_ref, *refs):
     seq = lax.axis_index("seq")
-    query_ref, acc_ref, max_ref, sum_ref, got_ref, moved_ref, other_ref, cache_ref, value_ref, level_ref = refs
+    query_ref, acc_ref, max_ref, sum_ref, got_ref, moved_ref, *other_refs = refs[:-3]
+    cache_ref, value_ref, level_ref = refs[-3:]
     local, span, width = cache_ref.shape
     rank = acc_ref.shape[1]
     start, other = seq * span, jnp.bitwise_xor(seq, 1) * span
     ends = [lens[anc[p]] for p in range(local)]
-    keys = jnp.concatenate([moved_ref[...], other_ref[...]], axis=0)
+    keys = jnp.concatenate([ref[...] for ref in (moved_ref, *other_refs)], axis=0)
     seen = visible(query_ref.shape[0], ends, [start, other], span)
     level = jnp.sum(got_ref[:, rank:].astype(F32), axis=1, keepdims=True)
     known = [
@@ -421,6 +426,7 @@
 
     part = shape((rows, rank + LANES))
     others = chips - 1
+    given, early = lax.optimization_barrier((given, early))
     giving = [a for stage in stages[1:] for a in stage[1:]]
     keeping = [a for stage in stages[1:] for a in (stage[0], *stage[2:])]
     moved, *give = pl.pallas_call(
@@ -431,28 +437,32 @@
         compiler_params=PARAMS,
         name="suffix_give",
     )(ancestors, lengths, *giving, early, late)
-    keep = pl.pallas_call(
+    small = local * span // 48 * 16
+    cuts = (local * span - 2 * small, small, small)
+    keep_and_pieces = pl.pallas_call(
         functools.partial(keep_kernel, others),
-        out_shape=[part] * others,
+        out_shape=[part] * others + [shape((cut, width)) for cut in cuts],
         in_specs=[SMEM] * 2 + [VMEM] * (len(keeping) + 1),
-        out_specs=[VMEM] * others,
+        out_specs=[VMEM] * (others + len(cuts)),
         compiler_params=PARAMS,
         name="suffix_keep",
     )(ancestors, lengths, *keeping, moved)
+    keep, pieces = keep_and_pieces[:others], keep_and_pieces[others:]
     sums = chip_merge(keep, [lax.ppermute(g, "seq", pairs(0, 1)) for g in give])
     parts = [lax.ppermute(s, "seq", back(1 + i // 2, 0)) for i, s in enumerate(sums)]
-    other = lax.ppermute(moved, "seq", pairs(0, 1))
+    other = [lax.ppermute(piece, "seq", pairs(0, 1)) for piece in pieces]
 
     moved, _ = lax.optimization_barrier((moved, sums[0]))
     query, _, acc, level, mass = stages[0]
     new_caches, *own_part = pl.pallas_call(
         near_kernel,
         out_shape=[shape(private_caches.shape), shape((rows, rank)), shape((rows, LANES), F32)],
-        in_specs=[SMEM] * 2 + [VMEM] * 8,
+        in_specs=[SMEM] * 2 + [VMEM] * (7 + len(other)),
         out_specs=[VMEM] * 3,
         compiler_params=PARAMS,
+        cost_estimate=NO_COST,
         name="suffix_near",
-    )(ancestors, lengths, new_latent, query, acc, level, mass, given, moved, other)
+    )(ancestors, lengths, new_latent, query, acc, level, mass, given, moved, *other)
     parts += own_part
 
     head_values = pl.pallas_call(

time: 39.7 us -> 39.2 us (0.987)
  waiting for transfers between devices: 4.45 us -> 4.02 us
    ppermute x2, waiting for transfers between devices: 2.02 us -> 0.79 us  [on_device(): lax.ppermute(s, 'seq', back(1 + i // 2, 0))]
    ppermute x1 -> x3, waiting for transfers between devices: 0.01 us -> 0.77 us  [on_device(): other = [lax.ppermute(piece, 'seq', pairs(0, 1)) for piece in pieces]]
    ppermute x1 -> x3, starting transfers between devices: 0.07 us -> 0.51 us  [on_device(): other = [lax.ppermute(piece, 'seq', pairs(0, 1)) for piece in pieces]]
    ppermute x1, starting transfers between devices: 0.5 us -> 0.07 us  [on_device(): sums = chip_merge(keep, [lax.ppermute(g, 'seq', pairs(0, 1)) for g in give])]
  transfers between devices with their start and end apart: 12 -> 14, of which waited for: 3 -> 5; matrix products, arithmetic and copies ran while one was open for 0% -> 0% of each run, Pallas kernels for 29% -> 29%
where the time goes in v20:
time: 39.2 us; the launch traced here: 39.1 us
  starting transfers between devices  18.8 us (48%)
  Pallas kernels  14.2 us (36%)
  waiting for transfers between devices  4.02 us (10%)
  local copies, waits for them, and re-layouts  1.2 us (3%)
  between operations  0.88 us (2%)
    ppermute x1, starting transfers between devices, on_device(): middle = lax.ppermute(block, 'dom', [(0, 2), (3, 1)])  7.77 us
    pallas_call x2, Pallas kernels, prefix_attention(): pl.pallas_call(functools.partial(prefix_kernel, len(queries), tiles), out...  6.6 us
    ppermute x1, starting transfers between devices, on_device(): late = lax.ppermute(chosen, 'dom', swap)  4.03 us
    ppermute x3, starting transfers between devices, on_device(): lax.ppermute(own, 'seq', pairs(*r))  2.15 us
    ppermute x1, waiting for transfers between devices, on_device(): late = lax.ppermute(chosen, 'dom', swap)  2.13 us
    ppermute x2, starting transfers between devices, on_device(): lax.ppermute(s, 'seq', back(1 + i // 2, 0))  2.09 us
    pallas_call x1, Pallas kernels, on_device(): pl.pallas_call(near_kernel, out_shape=[shape(private_caches.shape), shape...  1.57 us
    ppermute x1, starting transfers between devices, on_device(): theirs = lax.ppermute(ancestors, 'dom', [(0, 1), (3, 2)])  1.38 us
  transfers between devices with their start and end apart: 14, of which 5 were waited for; matrix products, arithmetic and copies ran while one was open for 0% of the time, Pallas kernels for 29%

profile of v20, /device:TPU:0, one launch (start us, length us, event | category | flops | bytes accessed | tf_op | source)
XLA Modules:
  0.0 39.1 jit_solution(8397031326536939741)
XLA Ops:
  0.7 1.1 %copy-done.5 = bf16[4,64,576]{2,1,0:T(8,128)(2,1)S(1)} copy-done((bf16[4,64,576]{2,1,0:T(8,128)(2,1)S(1)}, bf16[4,64,576]{2,1,0:T(8,128)(2,1)}, u32[]{:S(2)}) %copy-start.5) | copy-done | bytes 294936
  1.8 0.8 %collective-permute-start.5 = (bf16[128,1152]{1,0:T(8,128)(2,1)S(1)}, bf16[128,1152]{1,0:T(8,128)(2,1)S(1)}, u32[]{:S(2)}, u32[]{:S(2)}) collective-permute-start(bf16[128,1152]{1,0:T(8,128)(2,1)S(1)} %pack.1.refs_0_), channel_id=1, source_target_pairs={{1,2},{2,1},{5,6},{6,5},{9,10},{10,9},{13,14},{14,13},{17,18},{18,... | collective-permute-start | bytes 884744 | tf_op jit(solution)/shard_map/ppermute | solution.py:382
  2.7 7.8 %collective-permute-start.4 = (bf16[128,1152]{1,0:T(8,128)(2,1)S(1)}, bf16[128,1152]{1,0:T(8,128)(2,1)S(1)}, u32[]{:S(2)}, u32[]{:S(2)}) collective-permute-start(bf16[128,1152]{1,0:T(8,128)(2,1)S(1)} %pack.1.refs_0_), channel_id=1, source_target_pairs={{0,2},{3,1},{4,6},{7,5},{8,10},{11,9},{12,14},{15,13},{16,18},{19,... | collective-permute-start | bytes 884744 | tf_op jit(solution)/shard_map/ppermute | solution.py:381
  10.5 0.6 %project.1.refs_0_ = bf16[128,576]{1,0:T(8,128)(2,1)S(1)} custom-call(bf16[128,128]{1,0:T(8,128)(2,1)S(1)} %bitcast.9, bf16[128,64]{1,0:T(8,128)(2,1)S(1)} %bitcast.10, bf16[32,128,512]{2,1,0:T(8,128)(2,1)S(1)} %copy-done.4), custom_call_target="tpu_custom_call" | custom-call | flops 8000000000 | tf_op jit(solution)/shard_map/project/pallas_call | solution.py:390
  11.2 1.6 %collective-permute-start.1 = (bf16[128,576]{1,0:T(8,128)(2,1)S(1)}, bf16[128,576]{1,0:T(8,128)(2,1)S(1)}, u32[]{:S(2)}, u32[]{:S(2)}) collective-permute-start(bf16[128,576]{1,0:T(8,128)(2,1)S(1)} %project.1.refs_0_), channel_id=1, source_target_pairs={{0,12},{4,8},{8,4},{12,0},{1,13},{5,9},{9,5},{13,1},{2,14},{6,10},... | collective-permute-start | bytes 442376 | tf_op jit(solution)/shard_map/ppermute | solution.py:412
  12.8 0.5 %collective-permute-start = (bf16[128,576]{1,0:T(8,128)(2,1)S(1)}, bf16[128,576]{1,0:T(8,128)(2,1)S(1)}, u32[]{:S(2)}, u32[]{:S(2)}) collective-permute-start(bf16[128,576]{1,0:T(8,128)(2,1)S(1)} %project.1.refs_0_), channel_id=1, source_target_pairs={{0,8},{4,12},{8,0},{12,4},{1,9},{5,13},{9,1},{13,5},{2,10},{6,14},... | collective-permute-start | bytes 442376 | tf_op jit(solution)/shard_map/ppermute | solution.py:412
  13.4 1.4 %collective-permute-start.6 = (s32[4]{0:T(128)S(1)}, s32[4]{0:T(128)S(1)}, u32[]{:S(2)}, u32[]{:S(2)}) collective-permute-start(s32[4]{0:T(128)S(1)} %copy-done.1), channel_id=1, source_target_pairs={{0,1},{3,2},{4,5},{7,6},{8,9},{11,10},{12,13},{15,14},{16,17},{19,... | collective-permute-start | bytes 56 | tf_op jit(solution)/shard_map/ppermute | solution.py:383
  14.8 3.3 %prefix_attention.3 = (f32[128,512]{1,0:T(8,128)S(1)}, f32[128,128]{1,0:T(8,128)S(1)}, f32[128,128]{1,0:T(8,128)S(1)}, bf16[128,640]{1,0:T(8,128)(2,1)S(1)}) custom-call(bf16[128,576]{1,0:T(8,128)(2,1)S(1)} %project.1.refs_0_, bf16[128,576]{1,0:T(8,128)(2,1)S(1)} %collective-permute-done.2.refs_1_, bf16[576,4096]{1,0:T(8,128)(2,1)S(1)} %bitcast.7), custom_call_target="tpu_custom_call" | custom-call | tf_op jit(solution)/shard_map/prefix_attention/pallas_call | solution.py:111
  18.1 0.7 %gather.3 = bf16[128,1152]{1,0:T(8,128)(2,1)S(1)} custom-call(s32[4]{0:T(128)S(1)} %collective-permute-done.6.names, bf16[128,1152]{1,0:T(8,128)(2,1)S(1)} %pack.1.refs_0_, bf16[128,1152]{1,0:T(8,128)(2,1)S(1)} %collective-permute-done.4.refs_1_, bf16[128,1152]{1,0:T(8,128)(2,1)S(1)} %collective-permute-done.5.refs_2_, ...), custom_call_target="tpu_custom_call" | custom-call | tf_op jit(solution)/shard_map/gather/pallas_call | solution.py:222
  18.8 4.0 %collective-permute-start.7 = (bf16[128,1152]{1,0:T(8,128)(2,1)S(1)}, bf16[128,1152]{1,0:T(8,128)(2,1)S(1)}, u32[]{:S(2)}, u32[]{:S(2)}) collective-permute-start(bf16[128,1152]{1,0:T(8,128)(2,1)S(1)} %gather.3), channel_id=1, source_target_pairs={{0,1},{1,0},{2,3},{3,2},{4,5},{5,4},{6,7},{7,6},{8,9},{9,8},{10,11... | collective-permute-start | bytes 884744 | tf_op jit(solution)/shard_map/ppermute | solution.py:422
  22.9 3.3 %prefix_attention.2 = (f32[256,512]{1,0:T(8,128)S(1)}, f32[256,128]{1,0:T(8,128)S(1)}, f32[256,128]{1,0:T(8,128)S(1)}) custom-call(bf16[128,576]{1,0:T(8,128)(2,1)S(1)} %collective-permute-done.refs_0_, bf16[128,576]{1,0:T(8,128)(2,1)S(1)} %collective-permute-done.1.refs_1_.refs_0_, bf16[576,4096]{1,0:T(8,128)(2,1)S(1)} %bitcast.8), custom_call_target="tpu_custom_call" | custom-call | flops 2281701376 | bytes 4718592 | tf_op jit(solution)/shard_map/prefix_attention/pallas_call | solution.py:111
  26.2 0.7 %gather.2.refs_4_ = bf16[128,1152]{1,0:T(8,128)(2,1)S(1)} custom-call(s32[4]{0:T(128)S(1)} %copy-done.1, bf16[128,1152]{1,0:T(8,128)(2,1)S(1)} %pack.1.refs_0_, bf16[128,1152]{1,0:T(8,128)(2,1)S(1)} %collective-permute-done.4.refs_1_, bf16[128,1152]{1,0:T(8,128)(2,1)S(1)} %collective-permute-done.5.refs_2_), custom_call_target="tpu_custom_call" | custom-call | tf_op jit(solution)/shard_map/gather/pallas_call | solution.py:222
  26.8 2.1 %collective-permute-done.7.refs_5_ = bf16[128,1152]{1,0:T(8,128)(2,1)S(1)} collective-permute-done((bf16[128,1152]{1,0:T(8,128)(2,1)S(1)}, bf16[128,1152]{1,0:T(8,128)(2,1)S(1)}, u32[]{:S(2)}, u32[]{:S(2)}) %collective-permute-start.7) | collective-permute-done | bytes 294944 | tf_op jit(solution)/shard_map/ppermute | solution.py:422
  29.0 1.4 %suffix_give.1 = (bf16[256,576]{1,0:T(8,128)(2,1)S(1)}, bf16[128,640]{1,0:T(8,128)(2,1)S(1)}) custom-call(s32[4]{0:T(128)S(1)} %copy-done.1, s32[16]{0:T(128)S(1)} %copy-done.3, bf16[128,576]{1,0:T(8,128)(2,1)S(1)} %collective-permute-done.1.refs_1_.refs_0_, f32[256,512]{1,0:T(8,128)S(1)} %get-tuple-element.23.refs_1_, ...), custom_call_target="tpu_custom_call" | custom-call | tf_op jit(solution)/shard_map/suffix_give/pallas_call | solution.py:432
  30.4 1.1 %suffix_keep.1 = (bf16[128,640]{1,0:T(8,128)(2,1)S(1)}, bf16[96,576]{1,0:T(8,128)(2,1)S(1)}, bf16[80,576]{1,0:T(8,128)(2,1)S(1)}, bf16[80,576]{1,0:T(8,128)(2,1)S(1)}) custom-call(s32[4]{0:T(128)S(1)} %copy-done.1, s32[16]{0:T(128)S(1)} %copy-done.3, bf16[128,576]{1,0:T(8,128)(2,1)S(1)} %collective-permute-done.refs_0_, ...), custom_call_target="tpu_custom_call" | custom-call | tf_op jit(solution)/shard_map/suffix_keep/pallas_call | solution.py:442
  31.5 0.3 collective-permute-done.8.refs_1_
  32.0 1.6 %collective-permute-start.9 = (bf16[128,512]{1,0:T(8,128)(2,1)S(1)}, bf16[128,512]{1,0:T(8,128)(2,1)S(1)}, u32[]{:S(2)}, u32[]{:S(2)}) collective-permute-start(bf16[128,512]{1,0:T(8,128)(2,1)S(1)} %get-tuple-element.32), channel_id=1, source_target_pairs={{8,0},{12,4},{0,8},{4,12},{9,1},{13,5},{1,9},{5,13},{10,2},{14,6},... | collective-permute-start | bytes 393224 | tf_op jit(solution)/shard_map/ppermute | solution.py:452
  33.5 0.5 %collective-permute-start.12 = (bf16[80,576]{1,0:T(8,128)(2,1)S(1)}, bf16[80,576]{1,0:T(8,128)(2,1)S(1)}, u32[]{:S(2)}, u32[]{:S(2)}) collective-permute-start(bf16[80,576]{1,0:T(8,128)(2,1)S(1)} %get-tuple-element.39), channel_id=1, source_target_pairs={{0,4},{4,0},{8,12},{12,8},{1,5},{5,1},{9,13},{13,9},{2,6},{6,2},{1... | collective-permute-start | bytes 276488 | tf_op jit(solution)/shard_map/ppermute | solution.py:453
  34.0 0.5 %collective-permute-start.10 = (f32[8,128]{1,0:T(8,128)S(1)}, f32[8,128]{1,0:T(8,128)S(1)}, u32[]{:S(2)}, u32[]{:S(2)}) collective-permute-start(f32[8,128]{1,0:T(8,128)S(1)} %get-tuple-element.33), channel_id=1, source_target_pairs={{8,0},{12,4},{0,8},{4,12},{9,1},{13,5},{1,9},{5,13},{10,2},{14,6},... | collective-permute-start | bytes 12296 | tf_op jit(solution)/shard_map/ppermute | solution.py:452
  34.6 0.4 %collective-permute-done.12.refs_7_ = bf16[80,576]{1,0:T(8,128)(2,1)S(1)} collective-permute-done((bf16[80,576]{1,0:T(8,128)(2,1)S(1)}, bf16[80,576]{1,0:T(8,128)(2,1)S(1)}, u32[]{:S(2)}, u32[]{:S(2)}) %collective-permute-start.12) | collective-permute-done | bytes 92192 | tf_op jit(solution)/shard_map/ppermute | solution.py:453
  35.0 0.3 collective-permute-done.13.refs_8_
  35.4 1.6 %suffix_near.1 = (bf16[4,64,576]{2,1,0:T(8,128)(2,1)}, bf16[128,512]{1,0:T(8,128)(2,1)S(1)}, f32[128,128]{1,0:T(8,128)S(1)}) custom-call(s32[4]{0:T(128)S(1)} %copy-done.1, s32[16]{0:T(128)S(1)} %copy-done.3, bf16[4,576]{1,0:T(4,128)(2,1)S(1)} %copy-done.2, bf16[128,576]{1,0:T(8,128)(2,1)S(1)} %project.1.refs_0_, f32[128,512]{1,0:T(8,128)S(1)} %get-tuple-element.34.refs_1_, ...), custom_call_target="tpu_custom_call" | custom-call | tf_op jit(solution)/shard_map/suffix_near/pallas_call | solution.py:457
  36.9 0.8 %collective-permute-done.10.refs_1_ = f32[8,128]{1,0:T(8,128)S(1)} collective-permute-done((f32[8,128]{1,0:T(8,128)S(1)}, f32[8,128]{1,0:T(8,128)S(1)}, u32[]{:S(2)}, u32[]{:S(2)}) %collective-permute-start.10) | collective-permute-done | bytes 4128 | tf_op jit(solution)/shard_map/ppermute | solution.py:452
  37.7 1.4 %final.1 = bf16[4,32,128]{2,1,0:T(8,128)(2,1)} custom-call(bf16[128,512]{1,0:T(8,128)(2,1)S(1)} %collective-permute-done.9.refs_0_, f32[8,128]{1,0:T(8,128)S(1)} %collective-permute-done.10.refs_1_, bf16[128,512]{1,0:T(8,128)(2,1)S(1)} %get-tuple-element.41.refs_2_, f32[128,128]{1,0:T(8,128)S(1)} %get-tuple-element.42.refs_3_, bf16[32,512,128]{2,1,0:T(8,128)(2,1)S(1)} %copy-done), custom_call_target="tpu_custom_call" | custom-call | tf_op jit(solution)/shard_map/final/pallas_call | solution.py:468
  (38 shorter events, 0.4 us)
Async XLA Ops:
  0.6 9.9 %copy-start.4 = (bf16[32,128,512]{2,1,0:T(8,128)(2,1)S(1)}, bf16[32,128,512]{2,1,0:T(8,128)(2,1)}, u32[]{:S(2)}) copy-start(bf16[32,128,512]{2,1,0:T(8,128)(2,1)} %w_ref.1) | copy-start | bytes 12582916
  0.6 1.1 %copy-start.5 = (bf16[4,64,576]{2,1,0:T(8,128)(2,1)S(1)}, bf16[4,64,576]{2,1,0:T(8,128)(2,1)}, u32[]{:S(2)}) copy-start(bf16[4,64,576]{2,1,0:T(8,128)(2,1)} %cache_ref.1) | copy-start | bytes 884740
  1.8 8.7 %copy-start.6 = (bf16[4,32,128]{2,1,0:T(8,128)(2,1)S(1)}, bf16[4,32,128]{2,1,0:T(8,128)(2,1)}, u32[]{:S(2)}) copy-start(bf16[4,32,128]{2,1,0:T(8,128)(2,1)} %param.9) | copy-start | bytes 98308
  1.8 8.7 %copy-start.7 = (bf16[4,32,64]{2,1,0:T(8,128)(2,1)S(1)}, bf16[4,32,64]{2,1,0:T(8,128)(2,1)}, u32[]{:S(2)}) copy-start(bf16[4,32,64]{2,1,0:T(8,128)(2,1)} %param.10) | copy-start | bytes 49156
  1.8 13.0 %slice-start = ((s8[4718592]{0:T(1024)(128)(4,1)}), s8[4194304]{0:T(1024)(128)(4,1)S(1)}, s32[]{:S(2)}) async-start(s8[4718592]{0:T(1024)(128)(4,1)} %bitcast.5), calls=%async_computation | async-start | bytes 8388608
  1.8 16.3 %collective-permute-start.5 = (bf16[128,1152]{1,0:T(8,128)(2,1)S(1)}, bf16[128,1152]{1,0:T(8,128)(2,1)S(1)}, u32[]{:S(2)}, u32[]{:S(2)}) collective-permute-start(bf16[128,1152]{1,0:T(8,128)(2,1)S(1)} %pack.1.refs_0_), channel_id=1, source_target_pairs={{1,2},{2,1},{5,6},{6,5},{9,10},{10,9},{13,14},{14,13},{17,18},{18,... | collective-permute-start | bytes 884744 | tf_op jit(solution)/shard_map/ppermute | solution.py:382
  2.7 15.5 %collective-permute-start.4 = (bf16[128,1152]{1,0:T(8,128)(2,1)S(1)}, bf16[128,1152]{1,0:T(8,128)(2,1)S(1)}, u32[]{:S(2)}, u32[]{:S(2)}) collective-permute-start(bf16[128,1152]{1,0:T(8,128)(2,1)S(1)} %pack.1.refs_0_), channel_id=1, source_target_pairs={{0,2},{3,1},{4,6},{7,5},{8,10},{11,9},{12,14},{15,13},{16,18},{19,... | collective-permute-start | bytes 884744 | tf_op jit(solution)/shard_map/ppermute | solution.py:381
  10.5 4.3 %slice-start.1 = ((s8[4718592]{0:T(1024)(128)(4,1)}), s8[524288]{0:T(1024)(128)(4,1)S(1)}, s32[]{:S(2)}) async-start(s8[4718592]{0:T(1024)(128)(4,1)} %bitcast.5), calls=%async_computation.1 | async-start | bytes 1048576
  10.5 2.8 %copy-start.1 = (s32[4]{0:T(128)S(1)}, s32[4]{0:T(128)}, u32[]{:S(2)}) copy-start(s32[4]{0:T(128)} %anc.5) | copy-start | bytes 52
  11.2 2.2 %collective-permute-start.2 = (bf16[128,576]{1,0:T(8,128)(2,1)S(1)}, bf16[128,576]{1,0:T(8,128)(2,1)S(1)}, u32[]{:S(2)}, u32[]{:S(2)}) collective-permute-start(bf16[128,576]{1,0:T(8,128)(2,1)S(1)} %project.1.refs_0_), channel_id=1, source_target_pairs={{0,4},{4,0},{8,12},{12,8},{1,5},{5,1},{9,13},{13,9},{2,6},{6,2},{1... | collective-permute-start | bytes 442376 | tf_op jit(solution)/shard_map/ppermute | solution.py:412
  11.2 11.6 %collective-permute-start.1 = (bf16[128,576]{1,0:T(8,128)(2,1)S(1)}, bf16[128,576]{1,0:T(8,128)(2,1)S(1)}, u32[]{:S(2)}, u32[]{:S(2)}) collective-permute-start(bf16[128,576]{1,0:T(8,128)(2,1)S(1)} %project.1.refs_0_), channel_id=1, source_target_pairs={{0,12},{4,8},{8,4},{12,0},{1,13},{5,9},{9,5},{13,1},{2,14},{6,10},... | collective-permute-start | bytes 442376 | tf_op jit(solution)/shard_map/ppermute | solution.py:412
  12.8 10.0 %collective-permute-start = (bf16[128,576]{1,0:T(8,128)(2,1)S(1)}, bf16[128,576]{1,0:T(8,128)(2,1)S(1)}, u32[]{:S(2)}, u32[]{:S(2)}) collective-permute-start(bf16[128,576]{1,0:T(8,128)(2,1)S(1)} %project.1.refs_0_), channel_id=1, source_target_pairs={{0,8},{4,12},{8,0},{12,4},{1,9},{5,13},{9,1},{13,5},{2,10},{6,14},... | collective-permute-start | bytes 442376 | tf_op jit(solution)/shard_map/ppermute | solution.py:412
  13.4 4.7 %collective-permute-start.6 = (s32[4]{0:T(128)S(1)}, s32[4]{0:T(128)S(1)}, u32[]{:S(2)}, u32[]{:S(2)}) collective-permute-start(s32[4]{0:T(128)S(1)} %copy-done.1), channel_id=1, source_target_pairs={{0,1},{3,2},{4,5},{7,6},{8,9},{11,10},{12,13},{15,14},{16,17},{19,... | collective-permute-start | bytes 56 | tf_op jit(solution)/shard_map/ppermute | solution.py:383
  18.8 10.2 %collective-permute-start.7 = (bf16[128,1152]{1,0:T(8,128)(2,1)S(1)}, bf16[128,1152]{1,0:T(8,128)(2,1)S(1)}, u32[]{:S(2)}, u32[]{:S(2)}) collective-permute-start(bf16[128,1152]{1,0:T(8,128)(2,1)S(1)} %gather.3), channel_id=1, source_target_pairs={{0,1},{1,0},{2,3},{3,2},{4,5},{5,4},{6,7},{7,6},{8,9},{9,8},{10,11... | collective-permute-start | bytes 884744 | tf_op jit(solution)/shard_map/ppermute | solution.py:422
  22.8 6.1 %copy-start.3 = (s32[16]{0:T(128)S(1)}, s32[16]{0:T(128)}, u32[]{:S(2)}) copy-start(s32[16]{0:T(128)} %lens.5) | copy-start | bytes 196
  22.8 4.0 %collective-permute-start.3 = (bf16[128,640]{1,0:T(8,128)(2,1)S(1)}, bf16[128,640]{1,0:T(8,128)(2,1)S(1)}, u32[]{:S(2)}, u32[]{:S(2)}) collective-permute-start(bf16[128,640]{1,0:T(8,128)(2,1)S(1)} %get-tuple-element.26), channel_id=1, source_target_pairs={{0,4},{4,0},{8,12},{12,8},{1,5},{5,1},{9,13},{13,9},{2,6},{6,2},{1... | collective-permute-start | bytes 491528 | tf_op jit(solution)/shard_map/ppermute | solution.py:419
  26.1 9.2 %copy-start.2 = (bf16[4,576]{1,0:T(4,128)(2,1)S(1)}, bf16[4,576]{1,0:T(4,128)(2,1)}, u32[]{:S(2)}) copy-start(bf16[4,576]{1,0:T(4,128)(2,1)} %fresh_ref.1) | copy-start | bytes 13828
  26.1 11.6 %copy-start = (bf16[32,512,128]{2,1,0:T(8,128)(2,1)S(1)}, bf16[32,512,128]{2,1,0:T(8,128)(2,1)}, u32[]{:S(2)}) copy-start(bf16[32,512,128]{2,1,0:T(8,128)(2,1)} %refs_4_.1) | copy-start | bytes 12582916
  30.3 1.5 %collective-permute-start.8 = (bf16[128,640]{1,0:T(8,128)(2,1)S(1)}, bf16[128,640]{1,0:T(8,128)(2,1)S(1)}, u32[]{:S(2)}, u32[]{:S(2)}) collective-permute-start(bf16[128,640]{1,0:T(8,128)(2,1)S(1)} %get-tuple-element.31), channel_id=1, source_target_pairs={{0,4},{4,0},{8,12},{12,8},{1,5},{5,1},{9,13},{13,9},{2,6},{6,2},{1... | collective-permute-start | bytes 491528 | tf_op jit(solution)/shard_map/ppermute | solution.py:451
  32.0 5.7 %collective-permute-start.9 = (bf16[128,512]{1,0:T(8,128)(2,1)S(1)}, bf16[128,512]{1,0:T(8,128)(2,1)S(1)}, u32[]{:S(2)}, u32[]{:S(2)}) collective-permute-start(bf16[128,512]{1,0:T(8,128)(2,1)S(1)} %get-tuple-element.32), channel_id=1, source_target_pairs={{8,0},{12,4},{0,8},{4,12},{9,1},{13,5},{1,9},{5,13},{10,2},{14,6},... | collective-permute-start | bytes 393224 | tf_op jit(solution)/shard_map/ppermute | solution.py:452
  33.5 1.8 %collective-permute-start.11 = (bf16[96,576]{1,0:T(8,128)(2,1)S(1)}, bf16[96,576]{1,0:T(8,128)(2,1)S(1)}, u32[]{:S(2)}, u32[]{:S(2)}) collective-permute-start(bf16[96,576]{1,0:T(8,128)(2,1)S(1)} %get-tuple-element.38), channel_id=1, source_target_pairs={{0,4},{4,0},{8,12},{12,8},{1,5},{5,1},{9,13},{13,9},{2,6},{6,2},{1... | collective-permute-start | bytes 331784 | tf_op jit(solution)/shard_map/ppermute | solution.py:453
  33.5 1.5 %collective-permute-start.12 = (bf16[80,576]{1,0:T(8,128)(2,1)S(1)}, bf16[80,576]{1,0:T(8,128)(2,1)S(1)}, u32[]{:S(2)}, u32[]{:S(2)}) collective-permute-start(bf16[80,576]{1,0:T(8,128)(2,1)S(1)} %get-tuple-element.39), channel_id=1, source_target_pairs={{0,4},{4,0},{8,12},{12,8},{1,5},{5,1},{9,13},{13,9},{2,6},{6,2},{1... | collective-permute-start | bytes 276488 | tf_op jit(solution)/shard_map/ppermute | solution.py:453
  34.0 1.3 %collective-permute-start.13 = (bf16[80,576]{1,0:T(8,128)(2,1)S(1)}, bf16[80,576]{1,0:T(8,128)(2,1)S(1)}, u32[]{:S(2)}, u32[]{:S(2)}) collective-permute-start(bf16[80,576]{1,0:T(8,128)(2,1)S(1)} %get-tuple-element.40), channel_id=1, source_target_pairs={{0,4},{4,0},{8,12},{12,8},{1,5},{5,1},{9,13},{13,9},{2,6},{6,2},{1... | collective-permute-start | bytes 276488 | tf_op jit(solution)/shard_map/ppermute | solution.py:453
  34.0 3.7 %collective-permute-start.10 = (f32[8,128]{1,0:T(8,128)S(1)}, f32[8,128]{1,0:T(8,128)S(1)}, u32[]{:S(2)}, u32[]{:S(2)}) collective-permute-start(f32[8,128]{1,0:T(8,128)S(1)} %get-tuple-element.33), channel_id=1, source_target_pairs={{8,0},{12,4},{0,8},{4,12},{9,1},{13,5},{1,9},{5,13},{10,2},{14,6},... | collective-permute-start | bytes 12296 | tf_op jit(solution)/shard_map/ppermute | solution.py:452

commit v21 on v20

--- a/solution.py
+++ b/solution.py
@@ -23,6 +23,7 @@
 HBM = pl.BlockSpec(memory_space=pltpu.HBM)
 PARAMS = pltpu.CompilerParams(vmem_limit_bytes=40 * 1024 * 1024)
 NO_COST = pl.CostEstimate(flops=0, bytes_accessed=0, transcendentals=0)
+EXTRA = 16
 PACK = 8_000_000_000
 PROJECT = 8_000_000_000
 
@@ -318,34 +319,45 @@
 
 def chip_kernel(count, *refs):
     for k in range(count):
-        value_ref, level_ref = refs[2 * count + 2 * k : 2 * count + 2 * k + 2]
+        out_ref = refs[2 * count + k]
         values, level = merged([unpacked(refs[k][...]), unpacked(refs[count + k][...])])
-        value_ref[...] = values.astype(BF16)
-        kept = jnp.where(diagonal(values.shape[0], level_ref.shape[1]), level, 0.0)
-        level_ref[...] = jnp.broadcast_to(jnp.sum(kept, axis=0, keepdims=True), level_ref.shape)
+        rows, rank = values.shape
+        lanes = max(rows, LANES)
+        level = jnp.sum(jnp.where(diagonal(rows, lanes), level, 0.0), axis=0, keepdims=True)
+        high = level.astype(BF16).astype(F32)
+        middle = (level - high).astype(BF16).astype(F32)
+        low = level - high - middle
+        row = lax.broadcasted_iota(jnp.int32, (EXTRA, lanes), 0)
+        stats = jnp.where(row == 0, high, jnp.where(row == 1, middle, jnp.where(row == 2, low, 0.0)))
+        out_ref[pl.ds(0, rows)] = values.astype(BF16)
+        out_ref[pl.ds(rows, EXTRA), :lanes] = stats.astype(BF16)
+        out_ref[pl.ds(rows, EXTRA), lanes:] = jnp.zeros((EXTRA, rank - lanes), BF16)
 
 
 def chip_merge(keep, got):
     rows, rank = keep[0].shape[0], keep[0].shape[1] - LANES
     return pl.pallas_call(
         functools.partial(chip_kernel, len(keep)),
-        out_shape=[shape((rows, rank)), shape((8, max(rows, LANES)), F32)] * len(keep),
+        out_shape=[shape((rows + EXTRA, rank))] * len(keep),
         in_specs=[VMEM] * (2 * len(keep)),
-        out_specs=[VMEM] * (2 * len(keep)),
+        out_specs=[VMEM] * len(keep),
         compiler_params=PARAMS,
         name="chip_merge",
     )(*keep, *got)
 
 
 def final_kernel(count, *refs):
-    part_refs, (value_ref, level_ref, w_ref, out_ref, values) = refs[: 2 * count], refs[2 * count :]
+    part_refs, (value_ref, level_ref, w_ref, out_ref, values) = refs[:count], refs[count:]
     heads, rank, reach = w_ref.shape
     local = out_ref.shape[0]
+    rows = value_ref.shape[0]
+    lanes = max(rows, LANES)
     parts = [(value_ref[...].astype(F32), column(level_ref[...]))]
-    for k in range(count):
-        row = part_refs[2 * k + 1][0:1]
-        kept = jnp.where(diagonal(value_ref.shape[0], row.shape[1]), row, 0.0)
-        parts.append((part_refs[2 * k][...].astype(F32), jnp.sum(kept, axis=1, keepdims=True)))
+    for part_ref in part_refs:
+        stats = part_ref[pl.ds(rows, EXTRA), :lanes].astype(F32)
+        level = jnp.sum(stats, axis=0, keepdims=True)
+        level = jnp.sum(jnp.where(diagonal(rows, lanes), level, 0.0), axis=1, keepdims=True)
+        parts.append((part_ref[pl.ds(0, rows)].astype(F32), level))
     latent = merged(parts)[0].astype(BF16)
     first = lax.broadcasted_iota(jnp.int32, (2 * local, reach), 0) < local
     for h in range(0, heads, 2):
@@ -449,7 +461,7 @@
     )(ancestors, lengths, *keeping, moved)
     keep, pieces = keep_and_pieces[:others], keep_and_pieces[others:]
     sums = chip_merge(keep, [lax.ppermute(g, "seq", pairs(0, 1)) for g in give])
-    parts = [lax.ppermute(s, "seq", back(1 + i // 2, 0)) for i, s in enumerate(sums)]
+    parts = [lax.ppermute(s, "seq", back(t, 0)) for t, s in enumerate(sums, 1)]
     other = [lax.ppermute(piece, "seq", pairs(0, 1)) for piece in pieces]
 
     moved, _ = lax.optimization_barrier((moved, sums[0]))
@@ -468,7 +480,7 @@
     head_values = pl.pallas_call(
         functools.partial(final_kernel, others),
         out_shape=shape((local, heads, reach)),
-        in_specs=[VMEM] * (2 * chips + 1),
+        in_specs=[VMEM] * (chips + 2),
         out_specs=VMEM,
         scratch_shapes=[pltpu.VMEM((rows, reach), F32)],
         compiler_params=PARAMS,

time: 39.2 us -> 39.5 us (level)
  waiting for transfers between devices: 4.02 us -> 4.82 us
  starting transfers between devices: 18.8 us -> 18.3 us
    ppermute x2 -> x1, starting transfers between devices: 2.09 us -> 1.56 us  [on_device(): parts = [lax.ppermute(s, 'seq', back(t, 0)) for t, s in enumerate(sums, 1)]]
    ppermute x3, waiting for transfers between devices: 0.77 us -> 1.31 us  [on_device(): other = [lax.ppermute(piece, 'seq', pairs(0, 1)) for piece in pieces]]
    ppermute x2 -> x1, waiting for transfers between devices: 0.79 us -> 1.05 us  [on_device(): parts = [lax.ppermute(s, 'seq', back(t, 0)) for t, s in enumerate(sums, 1)]]
  transfers between devices with their start and end apart: 14 -> 13, of which waited for: 5 -> 5; matrix products, arithmetic and copies ran while one was open for 0% -> 0% of each run, Pallas kernels for 29% -> 28%
where the time goes in v21:
time: 39.5 us; the launch traced here: 39.3 us
  starting transfers between devices  18.3 us (46%)
  Pallas kernels  14.2 us (36%)
  waiting for transfers between devices  4.82 us (12%)
  local copies, waits for them, and re-layouts  1.2 us (3%)
  between operations  0.88 us (2%)
    ppermute x1, starting transfers between devices, on_device(): middle = lax.ppermute(block, 'dom', [(0, 2), (3, 1)])  7.77 us
    pallas_call x2, Pallas kernels, prefix_attention(): pl.pallas_call(functools.partial(prefix_kernel, len(queries), tiles), out...  6.6 us
    ppermute x1, starting transfers between devices, on_device(): late = lax.ppermute(chosen, 'dom', swap)  4.03 us
    ppermute x3, starting transfers between devices, on_device(): lax.ppermute(own, 'seq', pairs(*r))  2.15 us
    ppermute x1, waiting for transfers between devices, on_device(): late = lax.ppermute(chosen, 'dom', swap)  2.13 us
    pallas_call x1, Pallas kernels, on_device(): pl.pallas_call(near_kernel, out_shape=[shape(private_caches.shape), shape...  1.57 us
    ppermute x1, starting transfers between devices, on_device(): parts = [lax.ppermute(s, 'seq', back(t, 0)) for t, s in enumerate(sums, 1)]  1.56 us
    ppermute x1, starting transfers between devices, on_device(): theirs = lax.ppermute(ancestors, 'dom', [(0, 1), (3, 2)])  1.38 us
  transfers between devices with their start and end apart: 13, of which 5 were waited for; matrix products, arithmetic and copies ran while one was open for 0% of the time, Pallas kernels for 28%

profile of v21, /device:TPU:0, one launch (start us, length us, event | category | flops | bytes accessed | tf_op | source)
XLA Modules:
  0.0 39.3 jit_solution(9158495969560167795)
XLA Ops:
  0.7 1.1 %copy-done.5 = bf16[4,64,576]{2,1,0:T(8,128)(2,1)S(1)} copy-done((bf16[4,64,576]{2,1,0:T(8,128)(2,1)S(1)}, bf16[4,64,576]{2,1,0:T(8,128)(2,1)}, u32[]{:S(2)}) %copy-start.5) | copy-done | bytes 294936
  1.8 0.8 %collective-permute-start.5 = (bf16[128,1152]{1,0:T(8,128)(2,1)S(1)}, bf16[128,1152]{1,0:T(8,128)(2,1)S(1)}, u32[]{:S(2)}, u32[]{:S(2)}) collective-permute-start(bf16[128,1152]{1,0:T(8,128)(2,1)S(1)} %pack.1.refs_0_), channel_id=1, source_target_pairs={{1,2},{2,1},{5,6},{6,5},{9,10},{10,9},{13,14},{14,13},{17,18},{18,... | collective-permute-start | bytes 884744 | tf_op jit(solution)/shard_map/ppermute | solution.py:394
  2.7 7.8 %collective-permute-start.4 = (bf16[128,1152]{1,0:T(8,128)(2,1)S(1)}, bf16[128,1152]{1,0:T(8,128)(2,1)S(1)}, u32[]{:S(2)}, u32[]{:S(2)}) collective-permute-start(bf16[128,1152]{1,0:T(8,128)(2,1)S(1)} %pack.1.refs_0_), channel_id=1, source_target_pairs={{0,2},{3,1},{4,6},{7,5},{8,10},{11,9},{12,14},{15,13},{16,18},{19,... | collective-permute-start | bytes 884744 | tf_op jit(solution)/shard_map/ppermute | solution.py:393
  10.5 0.6 %project.1.refs_0_ = bf16[128,576]{1,0:T(8,128)(2,1)S(1)} custom-call(bf16[128,128]{1,0:T(8,128)(2,1)S(1)} %bitcast.9, bf16[128,64]{1,0:T(8,128)(2,1)S(1)} %bitcast.10, bf16[32,128,512]{2,1,0:T(8,128)(2,1)S(1)} %copy-done.4), custom_call_target="tpu_custom_call" | custom-call | flops 8000000000 | tf_op jit(solution)/shard_map/project/pallas_call | solution.py:402
  11.2 1.6 %collective-permute-start.1 = (bf16[128,576]{1,0:T(8,128)(2,1)S(1)}, bf16[128,576]{1,0:T(8,128)(2,1)S(1)}, u32[]{:S(2)}, u32[]{:S(2)}) collective-permute-start(bf16[128,576]{1,0:T(8,128)(2,1)S(1)} %project.1.refs_0_), channel_id=1, source_target_pairs={{0,12},{4,8},{8,4},{12,0},{1,13},{5,9},{9,5},{13,1},{2,14},{6,10},... | collective-permute-start | bytes 442376 | tf_op jit(solution)/shard_map/ppermute | solution.py:424
  12.8 0.5 %collective-permute-start = (bf16[128,576]{1,0:T(8,128)(2,1)S(1)}, bf16[128,576]{1,0:T(8,128)(2,1)S(1)}, u32[]{:S(2)}, u32[]{:S(2)}) collective-permute-start(bf16[128,576]{1,0:T(8,128)(2,1)S(1)} %project.1.refs_0_), channel_id=1, source_target_pairs={{0,8},{4,12},{8,0},{12,4},{1,9},{5,13},{9,1},{13,5},{2,10},{6,14},... | collective-permute-start | bytes 442376 | tf_op jit(solution)/shard_map/ppermute | solution.py:424
  13.4 1.4 %collective-permute-start.6 = (s32[4]{0:T(128)S(1)}, s32[4]{0:T(128)S(1)}, u32[]{:S(2)}, u32[]{:S(2)}) collective-permute-start(s32[4]{0:T(128)S(1)} %copy-done.1), channel_id=1, source_target_pairs={{0,1},{3,2},{4,5},{7,6},{8,9},{11,10},{12,13},{15,14},{16,17},{19,... | collective-permute-start | bytes 56 | tf_op jit(solution)/shard_map/ppermute | solution.py:395
  14.8 3.3 %prefix_attention.3 = (f32[128,512]{1,0:T(8,128)S(1)}, f32[128,128]{1,0:T(8,128)S(1)}, f32[128,128]{1,0:T(8,128)S(1)}, bf16[128,640]{1,0:T(8,128)(2,1)S(1)}) custom-call(bf16[128,576]{1,0:T(8,128)(2,1)S(1)} %project.1.refs_0_, bf16[128,576]{1,0:T(8,128)(2,1)S(1)} %collective-permute-done.2.refs_1_, bf16[576,4096]{1,0:T(8,128)(2,1)S(1)} %bitcast.7), custom_call_target="tpu_custom_call" | custom-call | tf_op jit(solution)/shard_map/prefix_attention/pallas_call | solution.py:112
  18.1 0.7 %gather.3 = bf16[128,1152]{1,0:T(8,128)(2,1)S(1)} custom-call(s32[4]{0:T(128)S(1)} %collective-permute-done.6.names, bf16[128,1152]{1,0:T(8,128)(2,1)S(1)} %pack.1.refs_0_, bf16[128,1152]{1,0:T(8,128)(2,1)S(1)} %collective-permute-done.4.refs_1_, bf16[128,1152]{1,0:T(8,128)(2,1)S(1)} %collective-permute-done.5.refs_2_, ...), custom_call_target="tpu_custom_call" | custom-call | tf_op jit(solution)/shard_map/gather/pallas_call | solution.py:223
  18.8 4.0 %collective-permute-start.7 = (bf16[128,1152]{1,0:T(8,128)(2,1)S(1)}, bf16[128,1152]{1,0:T(8,128)(2,1)S(1)}, u32[]{:S(2)}, u32[]{:S(2)}) collective-permute-start(bf16[128,1152]{1,0:T(8,128)(2,1)S(1)} %gather.3), channel_id=1, source_target_pairs={{0,1},{1,0},{2,3},{3,2},{4,5},{5,4},{6,7},{7,6},{8,9},{9,8},{10,11... | collective-permute-start | bytes 884744 | tf_op jit(solution)/shard_map/ppermute | solution.py:434
  22.9 3.3 %prefix_attention.2 = (f32[256,512]{1,0:T(8,128)S(1)}, f32[256,128]{1,0:T(8,128)S(1)}, f32[256,128]{1,0:T(8,128)S(1)}) custom-call(bf16[128,576]{1,0:T(8,128)(2,1)S(1)} %collective-permute-done.refs_0_, bf16[128,576]{1,0:T(8,128)(2,1)S(1)} %collective-permute-done.1.refs_1_.refs_0_, bf16[576,4096]{1,0:T(8,128)(2,1)S(1)} %bitcast.8), custom_call_target="tpu_custom_call" | custom-call | flops 2281701376 | bytes 4718592 | tf_op jit(solution)/shard_map/prefix_attention/pallas_call | solution.py:112
  26.2 0.7 %gather.2.refs_4_ = bf16[128,1152]{1,0:T(8,128)(2,1)S(1)} custom-call(s32[4]{0:T(128)S(1)} %copy-done.1, bf16[128,1152]{1,0:T(8,128)(2,1)S(1)} %pack.1.refs_0_, bf16[128,1152]{1,0:T(8,128)(2,1)S(1)} %collective-permute-done.4.refs_1_, bf16[128,1152]{1,0:T(8,128)(2,1)S(1)} %collective-permute-done.5.refs_2_), custom_call_target="tpu_custom_call" | custom-call | tf_op jit(solution)/shard_map/gather/pallas_call | solution.py:223
  26.8 2.1 %collective-permute-done.7.refs_5_ = bf16[128,1152]{1,0:T(8,128)(2,1)S(1)} collective-permute-done((bf16[128,1152]{1,0:T(8,128)(2,1)S(1)}, bf16[128,1152]{1,0:T(8,128)(2,1)S(1)}, u32[]{:S(2)}, u32[]{:S(2)}) %collective-permute-start.7) | collective-permute-done | bytes 294944 | tf_op jit(solution)/shard_map/ppermute | solution.py:434
  29.0 1.4 %suffix_give.1 = (bf16[256,576]{1,0:T(8,128)(2,1)S(1)}, bf16[128,640]{1,0:T(8,128)(2,1)S(1)}) custom-call(s32[4]{0:T(128)S(1)} %copy-done.1, s32[16]{0:T(128)S(1)} %copy-done.3, bf16[128,576]{1,0:T(8,128)(2,1)S(1)} %collective-permute-done.1.refs_1_.refs_0_, f32[256,512]{1,0:T(8,128)S(1)} %get-tuple-element.21.refs_1_, ...), custom_call_target="tpu_custom_call" | custom-call | tf_op jit(solution)/shard_map/suffix_give/pallas_call | solution.py:444
  30.4 1.1 %suffix_keep.1 = (bf16[128,640]{1,0:T(8,128)(2,1)S(1)}, bf16[96,576]{1,0:T(8,128)(2,1)S(1)}, bf16[80,576]{1,0:T(8,128)(2,1)S(1)}, bf16[80,576]{1,0:T(8,128)(2,1)S(1)}) custom-call(s32[4]{0:T(128)S(1)} %copy-done.1, s32[16]{0:T(128)S(1)} %copy-done.3, bf16[128,576]{1,0:T(8,128)(2,1)S(1)} %collective-permute-done.refs_0_, ...), custom_call_target="tpu_custom_call" | custom-call | tf_op jit(solution)/shard_map/suffix_keep/pallas_call | solution.py:454
  31.5 0.3 collective-permute-done.8.refs_1_
  31.8 0.2 chip_merge.1
  32.0 1.6 %collective-permute-start.9 = (bf16[144,512]{1,0:T(8,128)(2,1)S(1)}, bf16[144,512]{1,0:T(8,128)(2,1)S(1)}, u32[]{:S(2)}, u32[]{:S(2)}) collective-permute-start(bf16[144,512]{1,0:T(8,128)(2,1)S(1)} %chip_merge.1), channel_id=1, source_target_pairs={{8,0},{12,4},{0,8},{4,12},{9,1},{13,5},{1,9},{5,13},{10,2},{14,6},... | collective-permute-start | bytes 442376 | tf_op jit(solution)/shard_map/ppermute | solution.py:464
  33.5 0.5 %collective-permute-start.11 = (bf16[80,576]{1,0:T(8,128)(2,1)S(1)}, bf16[80,576]{1,0:T(8,128)(2,1)S(1)}, u32[]{:S(2)}, u32[]{:S(2)}) collective-permute-start(bf16[80,576]{1,0:T(8,128)(2,1)S(1)} %get-tuple-element.35), channel_id=1, source_target_pairs={{0,4},{4,0},{8,12},{12,8},{1,5},{5,1},{9,13},{13,9},{2,6},{6,2},{1... | collective-permute-start | bytes 276488 | tf_op jit(solution)/shard_map/ppermute | solution.py:465
  34.0 1.0 %collective-permute-done.11.refs_7_ = bf16[80,576]{1,0:T(8,128)(2,1)S(1)} collective-permute-done((bf16[80,576]{1,0:T(8,128)(2,1)S(1)}, bf16[80,576]{1,0:T(8,128)(2,1)S(1)}, u32[]{:S(2)}, u32[]{:S(2)}) %collective-permute-start.11) | collective-permute-done | bytes 92192 | tf_op jit(solution)/shard_map/ppermute | solution.py:465
  35.0 0.3 collective-permute-done.12.refs_8_
  35.4 1.6 %suffix_near.1 = (bf16[4,64,576]{2,1,0:T(8,128)(2,1)}, bf16[128,512]{1,0:T(8,128)(2,1)S(1)}, f32[128,128]{1,0:T(8,128)S(1)}) custom-call(s32[4]{0:T(128)S(1)} %copy-done.1, s32[16]{0:T(128)S(1)} %copy-done.3, bf16[4,576]{1,0:T(4,128)(2,1)S(1)} %copy-done.2, bf16[128,576]{1,0:T(8,128)(2,1)S(1)} %project.1.refs_0_, f32[128,512]{1,0:T(8,128)S(1)} %get-tuple-element.30.refs_1_, ...), custom_call_target="tpu_custom_call" | custom-call | tf_op jit(solution)/shard_map/suffix_near/pallas_call | solution.py:469
  36.9 1.1 %collective-permute-done.9.refs_0_ = bf16[144,512]{1,0:T(8,128)(2,1)S(1)} collective-permute-done((bf16[144,512]{1,0:T(8,128)(2,1)S(1)}, bf16[144,512]{1,0:T(8,128)(2,1)S(1)}, u32[]{:S(2)}, u32[]{:S(2)}) %collective-permute-start.9) | collective-permute-done | bytes 147488 | tf_op jit(solution)/shard_map/ppermute | solution.py:464
  38.0 1.4 %final.1 = bf16[4,32,128]{2,1,0:T(8,128)(2,1)} custom-call(bf16[144,512]{1,0:T(8,128)(2,1)S(1)} %collective-permute-done.9.refs_0_, bf16[128,512]{1,0:T(8,128)(2,1)S(1)} %get-tuple-element.37.refs_1_, f32[128,128]{1,0:T(8,128)S(1)} %get-tuple-element.38.refs_2_, bf16[32,512,128]{2,1,0:T(8,128)(2,1)S(1)} %copy-done), custom_call_target="tpu_custom_call" | custom-call | tf_op jit(solution)/shard_map/final/pallas_call | solution.py:480
  (36 shorter events, 0.3 us)
Async XLA Ops:
  0.6 9.9 %copy-start.4 = (bf16[32,128,512]{2,1,0:T(8,128)(2,1)S(1)}, bf16[32,128,512]{2,1,0:T(8,128)(2,1)}, u32[]{:S(2)}) copy-start(bf16[32,128,512]{2,1,0:T(8,128)(2,1)} %w_ref.1) | copy-start | bytes 12582916
  0.6 1.1 %copy-start.5 = (bf16[4,64,576]{2,1,0:T(8,128)(2,1)S(1)}, bf16[4,64,576]{2,1,0:T(8,128)(2,1)}, u32[]{:S(2)}) copy-start(bf16[4,64,576]{2,1,0:T(8,128)(2,1)} %cache_ref.1) | copy-start | bytes 884740
  1.8 8.7 %copy-start.6 = (bf16[4,32,128]{2,1,0:T(8,128)(2,1)S(1)}, bf16[4,32,128]{2,1,0:T(8,128)(2,1)}, u32[]{:S(2)}) copy-start(bf16[4,32,128]{2,1,0:T(8,128)(2,1)} %param.9) | copy-start | bytes 98308
  1.8 8.7 %copy-start.7 = (bf16[4,32,64]{2,1,0:T(8,128)(2,1)S(1)}, bf16[4,32,64]{2,1,0:T(8,128)(2,1)}, u32[]{:S(2)}) copy-start(bf16[4,32,64]{2,1,0:T(8,128)(2,1)} %param.10) | copy-start | bytes 49156
  1.8 13.0 %slice-start = ((s8[4718592]{0:T(1024)(128)(4,1)}), s8[4194304]{0:T(1024)(128)(4,1)S(1)}, s32[]{:S(2)}) async-start(s8[4718592]{0:T(1024)(128)(4,1)} %bitcast.5), calls=%async_computation | async-start | bytes 8388608
  1.8 16.3 %collective-permute-start.5 = (bf16[128,1152]{1,0:T(8,128)(2,1)S(1)}, bf16[128,1152]{1,0:T(8,128)(2,1)S(1)}, u32[]{:S(2)}, u32[]{:S(2)}) collective-permute-start(bf16[128,1152]{1,0:T(8,128)(2,1)S(1)} %pack.1.refs_0_), channel_id=1, source_target_pairs={{1,2},{2,1},{5,6},{6,5},{9,10},{10,9},{13,14},{14,13},{17,18},{18,... | collective-permute-start | bytes 884744 | tf_op jit(solution)/shard_map/ppermute | solution.py:394
  2.7 15.5 %collective-permute-start.4 = (bf16[128,1152]{1,0:T(8,128)(2,1)S(1)}, bf16[128,1152]{1,0:T(8,128)(2,1)S(1)}, u32[]{:S(2)}, u32[]{:S(2)}) collective-permute-start(bf16[128,1152]{1,0:T(8,128)(2,1)S(1)} %pack.1.refs_0_), channel_id=1, source_target_pairs={{0,2},{3,1},{4,6},{7,5},{8,10},{11,9},{12,14},{15,13},{16,18},{19,... | collective-permute-start | bytes 884744 | tf_op jit(solution)/shard_map/ppermute | solution.py:393
  10.5 4.3 %slice-start.1 = ((s8[4718592]{0:T(1024)(128)(4,1)}), s8[524288]{0:T(1024)(128)(4,1)S(1)}, s32[]{:S(2)}) async-start(s8[4718592]{0:T(1024)(128)(4,1)} %bitcast.5), calls=%async_computation.1 | async-start | bytes 1048576
  10.5 2.8 %copy-start.1 = (s32[4]{0:T(128)S(1)}, s32[4]{0:T(128)}, u32[]{:S(2)}) copy-start(s32[4]{0:T(128)} %anc.5) | copy-start | bytes 52
  11.2 2.2 %collective-permute-start.2 = (bf16[128,576]{1,0:T(8,128)(2,1)S(1)}, bf16[128,576]{1,0:T(8,128)(2,1)S(1)}, u32[]{:S(2)}, u32[]{:S(2)}) collective-permute-start(bf16[128,576]{1,0:T(8,128)(2,1)S(1)} %project.1.refs_0_), channel_id=1, source_target_pairs={{0,4},{4,0},{8,12},{12,8},{1,5},{5,1},{9,13},{13,9},{2,6},{6,2},{1... | collective-permute-start | bytes 442376 | tf_op jit(solution)/shard_map/ppermute | solution.py:424
  11.2 11.6 %collective-permute-start.1 = (bf16[128,576]{1,0:T(8,128)(2,1)S(1)}, bf16[128,576]{1,0:T(8,128)(2,1)S(1)}, u32[]{:S(2)}, u32[]{:S(2)}) collective-permute-start(bf16[128,576]{1,0:T(8,128)(2,1)S(1)} %project.1.refs_0_), channel_id=1, source_target_pairs={{0,12},{4,8},{8,4},{12,0},{1,13},{5,9},{9,5},{13,1},{2,14},{6,10},... | collective-permute-start | bytes 442376 | tf_op jit(solution)/shard_map/ppermute | solution.py:424
  12.8 10.0 %collective-permute-start = (bf16[128,576]{1,0:T(8,128)(2,1)S(1)}, bf16[128,576]{1,0:T(8,128)(2,1)S(1)}, u32[]{:S(2)}, u32[]{:S(2)}) collective-permute-start(bf16[128,576]{1,0:T(8,128)(2,1)S(1)} %project.1.refs_0_), channel_id=1, source_target_pairs={{0,8},{4,12},{8,0},{12,4},{1,9},{5,13},{9,1},{13,5},{2,10},{6,14},... | collective-permute-start | bytes 442376 | tf_op jit(solution)/shard_map/ppermute | solution.py:424
  13.4 4.7 %collective-permute-start.6 = (s32[4]{0:T(128)S(1)}, s32[4]{0:T(128)S(1)}, u32[]{:S(2)}, u32[]{:S(2)}) collective-permute-start(s32[4]{0:T(128)S(1)} %copy-done.1), channel_id=1, source_target_pairs={{0,1},{3,2},{4,5},{7,6},{8,9},{11,10},{12,13},{15,14},{16,17},{19,... | collective-permute-start | bytes 56 | tf_op jit(solution)/shard_map/ppermute | solution.py:395
  18.8 10.2 %collective-permute-start.7 = (bf16[128,1152]{1,0:T(8,128)(2,1)S(1)}, bf16[128,1152]{1,0:T(8,128)(2,1)S(1)}, u32[]{:S(2)}, u32[]{:S(2)}) collective-permute-start(bf16[128,1152]{1,0:T(8,128)(2,1)S(1)} %gather.3), channel_id=1, source_target_pairs={{0,1},{1,0},{2,3},{3,2},{4,5},{5,4},{6,7},{7,6},{8,9},{9,8},{10,11... | collective-permute-start | bytes 884744 | tf_op jit(solution)/shard_map/ppermute | solution.py:434
  22.8 6.1 %copy-start.3 = (s32[16]{0:T(128)S(1)}, s32[16]{0:T(128)}, u32[]{:S(2)}) copy-start(s32[16]{0:T(128)} %lens.5) | copy-start | bytes 196
  22.8 4.0 %collective-permute-start.3 = (bf16[128,640]{1,0:T(8,128)(2,1)S(1)}, bf16[128,640]{1,0:T(8,128)(2,1)S(1)}, u32[]{:S(2)}, u32[]{:S(2)}) collective-permute-start(bf16[128,640]{1,0:T(8,128)(2,1)S(1)} %get-tuple-element.24), channel_id=1, source_target_pairs={{0,4},{4,0},{8,12},{12,8},{1,5},{5,1},{9,13},{13,9},{2,6},{6,2},{1... | collective-permute-start | bytes 491528 | tf_op jit(solution)/shard_map/ppermute | solution.py:431
  26.1 9.2 %copy-start.2 = (bf16[4,576]{1,0:T(4,128)(2,1)S(1)}, bf16[4,576]{1,0:T(4,128)(2,1)}, u32[]{:S(2)}) copy-start(bf16[4,576]{1,0:T(4,128)(2,1)} %fresh_ref.1) | copy-start | bytes 13828
  26.1 11.8 %copy-start = (bf16[32,512,128]{2,1,0:T(8,128)(2,1)S(1)}, bf16[32,512,128]{2,1,0:T(8,128)(2,1)}, u32[]{:S(2)}) copy-start(bf16[32,512,128]{2,1,0:T(8,128)(2,1)} %refs_3_.1) | copy-start | bytes 12582916
  30.3 1.5 %collective-permute-start.8 = (bf16[128,640]{1,0:T(8,128)(2,1)S(1)}, bf16[128,640]{1,0:T(8,128)(2,1)S(1)}, u32[]{:S(2)}, u32[]{:S(2)}) collective-permute-start(bf16[128,640]{1,0:T(8,128)(2,1)S(1)} %get-tuple-element.29), channel_id=1, source_target_pairs={{0,4},{4,0},{8,12},{12,8},{1,5},{5,1},{9,13},{13,9},{2,6},{6,2},{1... | collective-permute-start | bytes 491528 | tf_op jit(solution)/shard_map/ppermute | solution.py:463
  32.0 6.0 %collective-permute-start.9 = (bf16[144,512]{1,0:T(8,128)(2,1)S(1)}, bf16[144,512]{1,0:T(8,128)(2,1)S(1)}, u32[]{:S(2)}, u32[]{:S(2)}) collective-permute-start(bf16[144,512]{1,0:T(8,128)(2,1)S(1)} %chip_merge.1), channel_id=1, source_target_pairs={{8,0},{12,4},{0,8},{4,12},{9,1},{13,5},{1,9},{5,13},{10,2},{14,6},... | collective-permute-start | bytes 442376 | tf_op jit(solution)/shard_map/ppermute | solution.py:464
  33.5 1.8 %collective-permute-start.10 = (bf16[96,576]{1,0:T(8,128)(2,1)S(1)}, bf16[96,576]{1,0:T(8,128)(2,1)S(1)}, u32[]{:S(2)}, u32[]{:S(2)}) collective-permute-start(bf16[96,576]{1,0:T(8,128)(2,1)S(1)} %get-tuple-element.34), channel_id=1, source_target_pairs={{0,4},{4,0},{8,12},{12,8},{1,5},{5,1},{9,13},{13,9},{2,6},{6,2},{1... | collective-permute-start | bytes 331784 | tf_op jit(solution)/shard_map/ppermute | solution.py:465
  33.5 1.5 %collective-permute-start.11 = (bf16[80,576]{1,0:T(8,128)(2,1)S(1)}, bf16[80,576]{1,0:T(8,128)(2,1)S(1)}, u32[]{:S(2)}, u32[]{:S(2)}) collective-permute-start(bf16[80,576]{1,0:T(8,128)(2,1)S(1)} %get-tuple-element.35), channel_id=1, source_target_pairs={{0,4},{4,0},{8,12},{12,8},{1,5},{5,1},{9,13},{13,9},{2,6},{6,2},{1... | collective-permute-start | bytes 276488 | tf_op jit(solution)/shard_map/ppermute | solution.py:465
  34.0 1.3 %collective-permute-start.12 = (bf16[80,576]{1,0:T(8,128)(2,1)S(1)}, bf16[80,576]{1,0:T(8,128)(2,1)S(1)}, u32[]{:S(2)}, u32[]{:S(2)}) collective-permute-start(bf16[80,576]{1,0:T(8,128)(2,1)S(1)} %get-tuple-element.36), channel_id=1, source_target_pairs={{0,4},{4,0},{8,12},{12,8},{1,5},{5,1},{9,13},{13,9},{2,6},{6,2},{1... | collective-permute-start | bytes 276488 | tf_op jit(solution)/shard_map/ppermute | solution.py:465

commit v22 on v20

--- a/solution.py
+++ b/solution.py
@@ -31,15 +31,19 @@
     return jax.ShapeDtypeStruct(dims, dtype)
 
 
-def pack_kernel(rank, cache_ref, out_ref):
+def pack_slot(rows, out_ref, part):
+    some, width = rows.shape[0] // 2, rows.shape[1]
+    rank = width - ROPE
+    first, second = rows[:some], rows[some:]
+    out_ref[part, :rank] = first[:, :rank]
+    out_ref[part, rank : 2 * rank] = second[:, :rank]
+    out_ref[part, 2 * rank :] = jnp.concatenate([first[:, rank:], second[:, rank:]], axis=1)
+
+
+def pack_kernel(cache_ref, out_ref):
     local, span, _ = cache_ref.shape
-    some = span // 2
     for p in range(local):
-        part = pl.ds(p * some, some)
-        first, second = cache_ref[p, :some], cache_ref[p, some:]
-        out_ref[part, :rank] = first[:, :rank]
-        out_ref[part, rank : 2 * rank] = second[:, :rank]
-        out_ref[part, 2 * rank :] = jnp.concatenate([first[:, rank:], second[:, rank:]], axis=1)
+        pack_slot(cache_ref[p], out_ref, pl.ds(p * span // 2, span // 2))
 
 
 def project_kernel(local, nope_ref, rope_ref, w_ref, own_ref):
@@ -214,7 +218,11 @@
 
             @pl.when(which == k)
             def _():
-                out_ref[pl.ds(p * some, some)] = block_ref[rows]
+                part = pl.ds(p * some, some)
+                if len(block_ref.shape) == 2:
+                    out_ref[part] = block_ref[rows]
+                else:
+                    pack_slot(block_ref[slot], out_ref, part)
 
 
 def gathered(names, blocks, line, token=None):
@@ -366,7 +374,7 @@
     cores = 2
     chips = seq_size // cores
     block = pl.pallas_call(
-        functools.partial(pack_kernel, rank),
+        pack_kernel,
         out_shape=shape((local * span // 2, 2 * width)),
         in_specs=[VMEM],
         out_specs=VMEM,
@@ -379,7 +387,7 @@
     if line:
         swap = [(0, 1), (1, 0), (2, 3), (3, 2)]
         middle = lax.ppermute(block, "dom", [(0, 2), (3, 1)])
-        far = lax.ppermute(block, "dom", [(1, 2), (2, 1)])
+        far = lax.ppermute(private_caches, "dom", [(1, 2), (2, 1)])
         theirs = lax.ppermute(ancestors, "dom", [(0, 1), (3, 2)])
     else:
         blocks = [block] + [

time: 39.2 us -> 39 us (level)
  starting transfers between devices: 18.8 us -> 18.3 us
    ppermute x1, starting transfers between devices: 4.03 us -> 3.61 us  [on_device(): late = lax.ppermute(chosen, 'dom', swap)]
where the time goes in v22:
time: 39 us; the launch traced here: 38.8 us
  starting transfers between devices  18.3 us (47%)
  Pallas kernels  14.1 us (36%)
  waiting for transfers between devices  4.05 us (10%)
  local copies, waits for them, and re-layouts  1.46 us (4%)
  between operations  0.88 us (2%)
    ppermute x1, starting transfers between devices, on_device(): middle = lax.ppermute(block, 'dom', [(0, 2), (3, 1)])  7.63 us
    pallas_call x2, Pallas kernels, prefix_attention(): pl.pallas_call(functools.partial(prefix_kernel, len(queries), tiles), out...  6.58 us
    ppermute x1, starting transfers between devices, on_device(): late = lax.ppermute(chosen, 'dom', swap)  3.61 us
    ppermute x3, starting transfers between devices, on_device(): lax.ppermute(own, 'seq', pairs(*r))  2.15 us
    ppermute x1, waiting for transfers between devices, on_device(): late = lax.ppermute(chosen, 'dom', swap)  2.15 us
    ppermute x2, starting transfers between devices, on_device(): lax.ppermute(s, 'seq', back(1 + i // 2, 0))  2.09 us
    pallas_call x1, Pallas kernels, on_device(): pl.pallas_call(near_kernel, out_shape=[shape(private_caches.shape), shape...  1.57 us
    unnamed x20, local copies, waits for them, and re-layouts  1.42 us
  transfers between devices with their start and end apart: 14, of which 5 were waited for; matrix products, arithmetic and copies ran while one was open for 0% of the time, Pallas kernels for 29%

profile of v22, /device:TPU:0, one launch (start us, length us, event | category | flops | bytes accessed | tf_op | source)
XLA Modules:
  0.0 38.8 jit_solution(14956186743597588277)
XLA Ops:
  0.6 0.8 %collective-permute-start.5 = (bf16[4,64,576]{2,1,0:T(8,128)(2,1)}, bf16[4,64,576]{2,1,0:T(8,128)(2,1)S(1)}, u32[]{:S(2)}, u32[]{:S(2)}) collective-permute-start(bf16[4,64,576]{2,1,0:T(8,128)(2,1)} %cache_ref.1), channel_id=1, source_target_pairs={{1,2},{2,1},{5,6},{6,5},{9,10},{10,9},{13,14},{14,13},{17,18},{18,... | collective-permute-start | bytes 884744 | tf_op jit(solution)/shard_map/ppermute | solution.py:390
  1.5 1.4 %copy-done.5 = bf16[4,64,576]{2,1,0:T(8,128)(2,1)S(1)} copy-done((bf16[4,64,576]{2,1,0:T(8,128)(2,1)S(1)}, bf16[4,64,576]{2,1,0:T(8,128)(2,1)}, u32[]{:S(2)}) %copy-start.5) | copy-done | bytes 294936
  2.9 7.6 %collective-permute-start.4 = (bf16[128,1152]{1,0:T(8,128)(2,1)S(1)}, bf16[128,1152]{1,0:T(8,128)(2,1)S(1)}, u32[]{:S(2)}, u32[]{:S(2)}) collective-permute-start(bf16[128,1152]{1,0:T(8,128)(2,1)S(1)} %pack.1.refs_0_), channel_id=1, source_target_pairs={{0,2},{3,1},{4,6},{7,5},{8,10},{11,9},{12,14},{15,13},{16,18},{19,... | collective-permute-start | bytes 884744 | tf_op jit(solution)/shard_map/ppermute | solution.py:389
  10.7 0.6 %project.1.refs_0_ = bf16[128,576]{1,0:T(8,128)(2,1)S(1)} custom-call(bf16[128,128]{1,0:T(8,128)(2,1)S(1)} %bitcast.9, bf16[128,64]{1,0:T(8,128)(2,1)S(1)} %bitcast.10, bf16[32,128,512]{2,1,0:T(8,128)(2,1)S(1)} %copy-done.4), custom_call_target="tpu_custom_call" | custom-call | flops 8000000000 | tf_op jit(solution)/shard_map/project/pallas_call | solution.py:398
  11.3 1.6 %collective-permute-start.1 = (bf16[128,576]{1,0:T(8,128)(2,1)S(1)}, bf16[128,576]{1,0:T(8,128)(2,1)S(1)}, u32[]{:S(2)}, u32[]{:S(2)}) collective-permute-start(bf16[128,576]{1,0:T(8,128)(2,1)S(1)} %project.1.refs_0_), channel_id=1, source_target_pairs={{0,12},{4,8},{8,4},{12,0},{1,13},{5,9},{9,5},{13,1},{2,14},{6,10},... | collective-permute-start | bytes 442376 | tf_op jit(solution)/shard_map/ppermute | solution.py:420
  12.9 0.5 %collective-permute-start = (bf16[128,576]{1,0:T(8,128)(2,1)S(1)}, bf16[128,576]{1,0:T(8,128)(2,1)S(1)}, u32[]{:S(2)}, u32[]{:S(2)}) collective-permute-start(bf16[128,576]{1,0:T(8,128)(2,1)S(1)} %project.1.refs_0_), channel_id=1, source_target_pairs={{0,8},{4,12},{8,0},{12,4},{1,9},{5,13},{9,1},{13,5},{2,10},{6,14},... | collective-permute-start | bytes 442376 | tf_op jit(solution)/shard_map/ppermute | solution.py:420
  13.5 1.4 %collective-permute-start.6 = (s32[4]{0:T(128)S(1)}, s32[4]{0:T(128)S(1)}, u32[]{:S(2)}, u32[]{:S(2)}) collective-permute-start(s32[4]{0:T(128)S(1)} %copy-done.1), channel_id=1, source_target_pairs={{0,1},{3,2},{4,5},{7,6},{8,9},{11,10},{12,13},{15,14},{16,17},{19,... | collective-permute-start | bytes 56 | tf_op jit(solution)/shard_map/ppermute | solution.py:391
  14.9 3.3 %prefix_attention.3 = (f32[128,512]{1,0:T(8,128)S(1)}, f32[128,128]{1,0:T(8,128)S(1)}, f32[128,128]{1,0:T(8,128)S(1)}, bf16[128,640]{1,0:T(8,128)(2,1)S(1)}) custom-call(bf16[128,576]{1,0:T(8,128)(2,1)S(1)} %project.1.refs_0_, bf16[128,576]{1,0:T(8,128)(2,1)S(1)} %collective-permute-done.2.refs_1_, bf16[576,4096]{1,0:T(8,128)(2,1)S(1)} %bitcast.7), custom_call_target="tpu_custom_call" | custom-call | tf_op jit(solution)/shard_map/prefix_attention/pallas_call | solution.py:115
  18.3 0.7 %gather.3 = bf16[128,1152]{1,0:T(8,128)(2,1)S(1)} custom-call(s32[4]{0:T(128)S(1)} %collective-permute-done.6.names, bf16[128,1152]{1,0:T(8,128)(2,1)S(1)} %pack.1.refs_0_, bf16[128,1152]{1,0:T(8,128)(2,1)S(1)} %collective-permute-done.4.refs_1_, bf16[4,64,576]{2,1,0:T(8,128)(2,1)S(1)} %collective-permute-done.5.refs_2_, ...), custom_call_target="tpu_custom_call" | custom-call | tf_op jit(solution)/shard_map/gather/pallas_call | solution.py:230
  18.9 3.6 %collective-permute-start.7 = (bf16[128,1152]{1,0:T(8,128)(2,1)S(1)}, bf16[128,1152]{1,0:T(8,128)(2,1)S(1)}, u32[]{:S(2)}, u32[]{:S(2)}) collective-permute-start(bf16[128,1152]{1,0:T(8,128)(2,1)S(1)} %gather.3), channel_id=1, source_target_pairs={{0,1},{1,0},{2,3},{3,2},{4,5},{5,4},{6,7},{7,6},{8,9},{9,8},{10,11... | collective-permute-start | bytes 884744 | tf_op jit(solution)/shard_map/ppermute | solution.py:430
  22.6 3.3 %prefix_attention.2 = (f32[256,512]{1,0:T(8,128)S(1)}, f32[256,128]{1,0:T(8,128)S(1)}, f32[256,128]{1,0:T(8,128)S(1)}) custom-call(bf16[128,576]{1,0:T(8,128)(2,1)S(1)} %collective-permute-done.refs_0_, bf16[128,576]{1,0:T(8,128)(2,1)S(1)} %collective-permute-done.1.refs_1_.refs_0_, bf16[576,4096]{1,0:T(8,128)(2,1)S(1)} %bitcast.8), custom_call_target="tpu_custom_call" | custom-call | flops 2281701376 | bytes 4718592 | tf_op jit(solution)/shard_map/prefix_attention/pallas_call | solution.py:115
  25.8 0.7 %gather.2.refs_4_ = bf16[128,1152]{1,0:T(8,128)(2,1)S(1)} custom-call(s32[4]{0:T(128)S(1)} %copy-done.1, bf16[128,1152]{1,0:T(8,128)(2,1)S(1)} %pack.1.refs_0_, bf16[128,1152]{1,0:T(8,128)(2,1)S(1)} %collective-permute-done.4.refs_1_, bf16[4,64,576]{2,1,0:T(8,128)(2,1)S(1)} %collective-permute-done.5.refs_2_), custom_call_target="tpu_custom_call" | custom-call | tf_op jit(solution)/shard_map/gather/pallas_call | solution.py:230
  26.5 2.2 %collective-permute-done.7.refs_5_ = bf16[128,1152]{1,0:T(8,128)(2,1)S(1)} collective-permute-done((bf16[128,1152]{1,0:T(8,128)(2,1)S(1)}, bf16[128,1152]{1,0:T(8,128)(2,1)S(1)}, u32[]{:S(2)}, u32[]{:S(2)}) %collective-permute-start.7) | collective-permute-done | bytes 294944 | tf_op jit(solution)/shard_map/ppermute | solution.py:430
  28.7 1.4 %suffix_give.1 = (bf16[256,576]{1,0:T(8,128)(2,1)S(1)}, bf16[128,640]{1,0:T(8,128)(2,1)S(1)}) custom-call(s32[4]{0:T(128)S(1)} %copy-done.1, s32[16]{0:T(128)S(1)} %copy-done.3, bf16[128,576]{1,0:T(8,128)(2,1)S(1)} %collective-permute-done.1.refs_1_.refs_0_, f32[256,512]{1,0:T(8,128)S(1)} %get-tuple-element.23.refs_1_, ...), custom_call_target="tpu_custom_call" | custom-call | tf_op jit(solution)/shard_map/suffix_give/pallas_call | solution.py:440
  30.1 1.1 %suffix_keep.1 = (bf16[128,640]{1,0:T(8,128)(2,1)S(1)}, bf16[96,576]{1,0:T(8,128)(2,1)S(1)}, bf16[80,576]{1,0:T(8,128)(2,1)S(1)}, bf16[80,576]{1,0:T(8,128)(2,1)S(1)}) custom-call(s32[4]{0:T(128)S(1)} %copy-done.1, s32[16]{0:T(128)S(1)} %copy-done.3, bf16[128,576]{1,0:T(8,128)(2,1)S(1)} %collective-permute-done.refs_0_, ...), custom_call_target="tpu_custom_call" | custom-call | tf_op jit(solution)/shard_map/suffix_keep/pallas_call | solution.py:450
  31.2 0.3 collective-permute-done.8.refs_1_
  31.7 1.6 %collective-permute-start.9 = (bf16[128,512]{1,0:T(8,128)(2,1)S(1)}, bf16[128,512]{1,0:T(8,128)(2,1)S(1)}, u32[]{:S(2)}, u32[]{:S(2)}) collective-permute-start(bf16[128,512]{1,0:T(8,128)(2,1)S(1)} %get-tuple-element.32), channel_id=1, source_target_pairs={{8,0},{12,4},{0,8},{4,12},{9,1},{13,5},{1,9},{5,13},{10,2},{14,6},... | collective-permute-start | bytes 393224 | tf_op jit(solution)/shard_map/ppermute | solution.py:460
  33.2 0.5 %collective-permute-start.12 = (bf16[80,576]{1,0:T(8,128)(2,1)S(1)}, bf16[80,576]{1,0:T(8,128)(2,1)S(1)}, u32[]{:S(2)}, u32[]{:S(2)}) collective-permute-start(bf16[80,576]{1,0:T(8,128)(2,1)S(1)} %get-tuple-element.39), channel_id=1, source_target_pairs={{0,4},{4,0},{8,12},{12,8},{1,5},{5,1},{9,13},{13,9},{2,6},{6,2},{1... | collective-permute-start | bytes 276488 | tf_op jit(solution)/shard_map/ppermute | solution.py:461
  33.7 0.5 %collective-permute-start.10 = (f32[8,128]{1,0:T(8,128)S(1)}, f32[8,128]{1,0:T(8,128)S(1)}, u32[]{:S(2)}, u32[]{:S(2)}) collective-permute-start(f32[8,128]{1,0:T(8,128)S(1)} %get-tuple-element.33), channel_id=1, source_target_pairs={{8,0},{12,4},{0,8},{4,12},{9,1},{13,5},{1,9},{5,13},{10,2},{14,6},... | collective-permute-start | bytes 12296 | tf_op jit(solution)/shard_map/ppermute | solution.py:460
  34.3 0.4 %collective-permute-done.12.refs_7_ = bf16[80,576]{1,0:T(8,128)(2,1)S(1)} collective-permute-done((bf16[80,576]{1,0:T(8,128)(2,1)S(1)}, bf16[80,576]{1,0:T(8,128)(2,1)S(1)}, u32[]{:S(2)}, u32[]{:S(2)}) %collective-permute-start.12) | collective-permute-done | bytes 92192 | tf_op jit(solution)/shard_map/ppermute | solution.py:461
  34.7 0.3 collective-permute-done.13.refs_8_
  35.1 1.6 %suffix_near.1 = (bf16[4,64,576]{2,1,0:T(8,128)(2,1)}, bf16[128,512]{1,0:T(8,128)(2,1)S(1)}, f32[128,128]{1,0:T(8,128)S(1)}) custom-call(s32[4]{0:T(128)S(1)} %copy-done.1, s32[16]{0:T(128)S(1)} %copy-done.3, bf16[4,576]{1,0:T(4,128)(2,1)S(1)} %copy-done.2, bf16[128,576]{1,0:T(8,128)(2,1)S(1)} %project.1.refs_0_, f32[128,512]{1,0:T(8,128)S(1)} %get-tuple-element.34.refs_1_, ...), custom_call_target="tpu_custom_call" | custom-call | tf_op jit(solution)/shard_map/suffix_near/pallas_call | solution.py:465
  36.6 0.8 %collective-permute-done.10.refs_1_ = f32[8,128]{1,0:T(8,128)S(1)} collective-permute-done((f32[8,128]{1,0:T(8,128)S(1)}, f32[8,128]{1,0:T(8,128)S(1)}, u32[]{:S(2)}, u32[]{:S(2)}) %collective-permute-start.10) | collective-permute-done | bytes 4128 | tf_op jit(solution)/shard_map/ppermute | solution.py:460
  37.4 1.4 %final.1 = bf16[4,32,128]{2,1,0:T(8,128)(2,1)} custom-call(bf16[128,512]{1,0:T(8,128)(2,1)S(1)} %collective-permute-done.9.refs_0_, f32[8,128]{1,0:T(8,128)S(1)} %collective-permute-done.10.refs_1_, bf16[128,512]{1,0:T(8,128)(2,1)S(1)} %get-tuple-element.41.refs_2_, f32[128,128]{1,0:T(8,128)S(1)} %get-tuple-element.42.refs_3_, bf16[32,512,128]{2,1,0:T(8,128)(2,1)S(1)} %copy-done), custom_call_target="tpu_custom_call" | custom-call | tf_op jit(solution)/shard_map/final/pallas_call | solution.py:476
  (38 shorter events, 0.4 us)
Async XLA Ops:
  0.6 10.0 %copy-start.4 = (bf16[32,128,512]{2,1,0:T(8,128)(2,1)S(1)}, bf16[32,128,512]{2,1,0:T(8,128)(2,1)}, u32[]{:S(2)}) copy-start(bf16[32,128,512]{2,1,0:T(8,128)(2,1)} %w_ref.1) | copy-start | bytes 12582916
  0.6 17.6 %collective-permute-start.5 = (bf16[4,64,576]{2,1,0:T(8,128)(2,1)}, bf16[4,64,576]{2,1,0:T(8,128)(2,1)S(1)}, u32[]{:S(2)}, u32[]{:S(2)}) collective-permute-start(bf16[4,64,576]{2,1,0:T(8,128)(2,1)} %cache_ref.1), channel_id=1, source_target_pairs={{1,2},{2,1},{5,6},{6,5},{9,10},{10,9},{13,14},{14,13},{17,18},{18,... | collective-permute-start | bytes 884744 | tf_op jit(solution)/shard_map/ppermute | solution.py:390
  1.5 1.4 %copy-start.5 = (bf16[4,64,576]{2,1,0:T(8,128)(2,1)S(1)}, bf16[4,64,576]{2,1,0:T(8,128)(2,1)}, u32[]{:S(2)}) copy-start(bf16[4,64,576]{2,1,0:T(8,128)(2,1)} %cache_ref.1) | copy-start | bytes 884740
  2.8 7.7 %copy-start.6 = (bf16[4,32,128]{2,1,0:T(8,128)(2,1)S(1)}, bf16[4,32,128]{2,1,0:T(8,128)(2,1)}, u32[]{:S(2)}) copy-start(bf16[4,32,128]{2,1,0:T(8,128)(2,1)} %param.9) | copy-start | bytes 98308
  2.8 7.8 %copy-start.7 = (bf16[4,32,64]{2,1,0:T(8,128)(2,1)S(1)}, bf16[4,32,64]{2,1,0:T(8,128)(2,1)}, u32[]{:S(2)}) copy-start(bf16[4,32,64]{2,1,0:T(8,128)(2,1)} %param.10) | copy-start | bytes 49156
  2.8 12.0 %slice-start = ((s8[4718592]{0:T(1024)(128)(4,1)}), s8[4194304]{0:T(1024)(128)(4,1)S(1)}, s32[]{:S(2)}) async-start(s8[4718592]{0:T(1024)(128)(4,1)} %bitcast.5), calls=%async_computation | async-start | bytes 8388608
  2.9 15.3 %collective-permute-start.4 = (bf16[128,1152]{1,0:T(8,128)(2,1)S(1)}, bf16[128,1152]{1,0:T(8,128)(2,1)S(1)}, u32[]{:S(2)}, u32[]{:S(2)}) collective-permute-start(bf16[128,1152]{1,0:T(8,128)(2,1)S(1)} %pack.1.refs_0_), channel_id=1, source_target_pairs={{0,2},{3,1},{4,6},{7,5},{8,10},{11,9},{12,14},{15,13},{16,18},{19,... | collective-permute-start | bytes 884744 | tf_op jit(solution)/shard_map/ppermute | solution.py:389
  10.6 4.3 %slice-start.1 = ((s8[4718592]{0:T(1024)(128)(4,1)}), s8[524288]{0:T(1024)(128)(4,1)S(1)}, s32[]{:S(2)}) async-start(s8[4718592]{0:T(1024)(128)(4,1)} %bitcast.5), calls=%async_computation.1 | async-start | bytes 1048576
  10.7 2.8 %copy-start.1 = (s32[4]{0:T(128)S(1)}, s32[4]{0:T(128)}, u32[]{:S(2)}) copy-start(s32[4]{0:T(128)} %anc.5) | copy-start | bytes 52
  11.3 2.2 %collective-permute-start.2 = (bf16[128,576]{1,0:T(8,128)(2,1)S(1)}, bf16[128,576]{1,0:T(8,128)(2,1)S(1)}, u32[]{:S(2)}, u32[]{:S(2)}) collective-permute-start(bf16[128,576]{1,0:T(8,128)(2,1)S(1)} %project.1.refs_0_), channel_id=1, source_target_pairs={{0,4},{4,0},{8,12},{12,8},{1,5},{5,1},{9,13},{13,9},{2,6},{6,2},{1... | collective-permute-start | bytes 442376 | tf_op jit(solution)/shard_map/ppermute | solution.py:420
  11.3 11.2 %collective-permute-start.1 = (bf16[128,576]{1,0:T(8,128)(2,1)S(1)}, bf16[128,576]{1,0:T(8,128)(2,1)S(1)}, u32[]{:S(2)}, u32[]{:S(2)}) collective-permute-start(bf16[128,576]{1,0:T(8,128)(2,1)S(1)} %project.1.refs_0_), channel_id=1, source_target_pairs={{0,12},{4,8},{8,4},{12,0},{1,13},{5,9},{9,5},{13,1},{2,14},{6,10},... | collective-permute-start | bytes 442376 | tf_op jit(solution)/shard_map/ppermute | solution.py:420
  12.9 9.6 %collective-permute-start = (bf16[128,576]{1,0:T(8,128)(2,1)S(1)}, bf16[128,576]{1,0:T(8,128)(2,1)S(1)}, u32[]{:S(2)}, u32[]{:S(2)}) collective-permute-start(bf16[128,576]{1,0:T(8,128)(2,1)S(1)} %project.1.refs_0_), channel_id=1, source_target_pairs={{0,8},{4,12},{8,0},{12,4},{1,9},{5,13},{9,1},{13,5},{2,10},{6,14},... | collective-permute-start | bytes 442376 | tf_op jit(solution)/shard_map/ppermute | solution.py:420
  13.5 4.7 %collective-permute-start.6 = (s32[4]{0:T(128)S(1)}, s32[4]{0:T(128)S(1)}, u32[]{:S(2)}, u32[]{:S(2)}) collective-permute-start(s32[4]{0:T(128)S(1)} %copy-done.1), channel_id=1, source_target_pairs={{0,1},{3,2},{4,5},{7,6},{8,9},{11,10},{12,13},{15,14},{16,17},{19,... | collective-permute-start | bytes 56 | tf_op jit(solution)/shard_map/ppermute | solution.py:391
  18.9 9.7 %collective-permute-start.7 = (bf16[128,1152]{1,0:T(8,128)(2,1)S(1)}, bf16[128,1152]{1,0:T(8,128)(2,1)S(1)}, u32[]{:S(2)}, u32[]{:S(2)}) collective-permute-start(bf16[128,1152]{1,0:T(8,128)(2,1)S(1)} %gather.3), channel_id=1, source_target_pairs={{0,1},{1,0},{2,3},{3,2},{4,5},{5,4},{6,7},{7,6},{8,9},{9,8},{10,11... | collective-permute-start | bytes 884744 | tf_op jit(solution)/shard_map/ppermute | solution.py:430
  22.5 6.1 %copy-start.3 = (s32[16]{0:T(128)S(1)}, s32[16]{0:T(128)}, u32[]{:S(2)}) copy-start(s32[16]{0:T(128)} %lens.5) | copy-start | bytes 196
  22.5 4.0 %collective-permute-start.3 = (bf16[128,640]{1,0:T(8,128)(2,1)S(1)}, bf16[128,640]{1,0:T(8,128)(2,1)S(1)}, u32[]{:S(2)}, u32[]{:S(2)}) collective-permute-start(bf16[128,640]{1,0:T(8,128)(2,1)S(1)} %get-tuple-element.26), channel_id=1, source_target_pairs={{0,4},{4,0},{8,12},{12,8},{1,5},{5,1},{9,13},{13,9},{2,6},{6,2},{1... | collective-permute-start | bytes 491528 | tf_op jit(solution)/shard_map/ppermute | solution.py:427
  25.8 9.2 %copy-start.2 = (bf16[4,576]{1,0:T(4,128)(2,1)S(1)}, bf16[4,576]{1,0:T(4,128)(2,1)}, u32[]{:S(2)}) copy-start(bf16[4,576]{1,0:T(4,128)(2,1)} %fresh_ref.1) | copy-start | bytes 13828
  25.8 11.6 %copy-start = (bf16[32,512,128]{2,1,0:T(8,128)(2,1)S(1)}, bf16[32,512,128]{2,1,0:T(8,128)(2,1)}, u32[]{:S(2)}) copy-start(bf16[32,512,128]{2,1,0:T(8,128)(2,1)} %refs_4_.1) | copy-start | bytes 12582916
  30.0 1.5 %collective-permute-start.8 = (bf16[128,640]{1,0:T(8,128)(2,1)S(1)}, bf16[128,640]{1,0:T(8,128)(2,1)S(1)}, u32[]{:S(2)}, u32[]{:S(2)}) collective-permute-start(bf16[128,640]{1,0:T(8,128)(2,1)S(1)} %get-tuple-element.31), channel_id=1, source_target_pairs={{0,4},{4,0},{8,12},{12,8},{1,5},{5,1},{9,13},{13,9},{2,6},{6,2},{1... | collective-permute-start | bytes 491528 | tf_op jit(solution)/shard_map/ppermute | solution.py:459
  31.7 5.7 %collective-permute-start.9 = (bf16[128,512]{1,0:T(8,128)(2,1)S(1)}, bf16[128,512]{1,0:T(8,128)(2,1)S(1)}, u32[]{:S(2)}, u32[]{:S(2)}) collective-permute-start(bf16[128,512]{1,0:T(8,128)(2,1)S(1)} %get-tuple-element.32), channel_id=1, source_target_pairs={{8,0},{12,4},{0,8},{4,12},{9,1},{13,5},{1,9},{5,13},{10,2},{14,6},... | collective-permute-start | bytes 393224 | tf_op jit(solution)/shard_map/ppermute | solution.py:460
  33.2 1.8 %collective-permute-start.11 = (bf16[96,576]{1,0:T(8,128)(2,1)S(1)}, bf16[96,576]{1,0:T(8,128)(2,1)S(1)}, u32[]{:S(2)}, u32[]{:S(2)}) collective-permute-start(bf16[96,576]{1,0:T(8,128)(2,1)S(1)} %get-tuple-element.38), channel_id=1, source_target_pairs={{0,4},{4,0},{8,12},{12,8},{1,5},{5,1},{9,13},{13,9},{2,6},{6,2},{1... | collective-permute-start | bytes 331784 | tf_op jit(solution)/shard_map/ppermute | solution.py:461
  33.2 1.5 %collective-permute-start.12 = (bf16[80,576]{1,0:T(8,128)(2,1)S(1)}, bf16[80,576]{1,0:T(8,128)(2,1)S(1)}, u32[]{:S(2)}, u32[]{:S(2)}) collective-permute-start(bf16[80,576]{1,0:T(8,128)(2,1)S(1)} %get-tuple-element.39), channel_id=1, source_target_pairs={{0,4},{4,0},{8,12},{12,8},{1,5},{5,1},{9,13},{13,9},{2,6},{6,2},{1... | collective-permute-start | bytes 276488 | tf_op jit(solution)/shard_map/ppermute | solution.py:461
  33.7 1.3 %collective-permute-start.13 = (bf16[80,576]{1,0:T(8,128)(2,1)S(1)}, bf16[80,576]{1,0:T(8,128)(2,1)S(1)}, u32[]{:S(2)}, u32[]{:S(2)}) collective-permute-start(bf16[80,576]{1,0:T(8,128)(2,1)S(1)} %get-tuple-element.40), channel_id=1, source_target_pairs={{0,4},{4,0},{8,12},{12,8},{1,5},{5,1},{9,13},{13,9},{2,6},{6,2},{1... | collective-permute-start | bytes 276488 | tf_op jit(solution)/shard_map/ppermute | solution.py:461
  33.7 3.7 %collective-permute-start.10 = (f32[8,128]{1,0:T(8,128)S(1)}, f32[8,128]{1,0:T(8,128)S(1)}, u32[]{:S(2)}, u32[]{:S(2)}) collective-permute-start(f32[8,128]{1,0:T(8,128)S(1)} %get-tuple-element.33), channel_id=1, source_target_pairs={{8,0},{12,4},{0,8},{4,12},{9,1},{13,5},{1,9},{5,13},{10,2},{14,6},... | collective-permute-start | bytes 12296 | tf_op jit(solution)/shard_map/ppermute | solution.py:460

commit v23 on v22

--- a/solution.py
+++ b/solution.py
@@ -301,7 +301,18 @@
         keep_refs[k][...] = far_part(anc, lens, query_ref, partial, pl.ds(0, rows), moved_ref[...])
 
 
-def near_kernel(anc, lens, fresh_ref, *refs):
+def head_products(latent, w_ref, local):
+    heads, _, reach = w_ref.shape
+    first = lax.broadcasted_iota(jnp.int32, (2 * local, reach), 0) < local
+    products = []
+    for h in range(0, heads, 2):
+        weights = jnp.concatenate([w_ref[h], w_ref[h + 1]], axis=1)
+        both = jnp.dot(latent[h * local : (h + 2) * local], weights, preferred_element_type=F32)
+        products.append(jnp.where(first, both[:, :reach], both[:, reach:]))
+    return jnp.concatenate(products, axis=0)
+
+
+def near_kernel(anc, lens, fresh_ref, w_ref, *refs):
     seq = lax.axis_index("seq")
     query_ref, acc_ref, max_ref, sum_ref, got_ref, moved_ref, *other_refs = refs[:-3]
     cache_ref, value_ref, level_ref = refs[-3:]
@@ -317,7 +328,7 @@
         (level, 1.0, got_ref[:, :rank].astype(F32)),
     ]
     values, level = attend(query_ref[...], keys, seen, rank, known)
-    value_ref[...] = values.astype(BF16)
+    value_ref[...] = head_products(values.astype(BF16), w_ref, local)
     level_ref[...] = jnp.broadcast_to(level, level_ref.shape)
     for p in range(local):
         at = start + lax.broadcasted_iota(jnp.int32, (span, 1), 0) == ends[p]
@@ -349,18 +360,13 @@
     part_refs, (value_ref, level_ref, w_ref, out_ref, values) = refs[: 2 * count], refs[2 * count :]
     heads, rank, reach = w_ref.shape
     local = out_ref.shape[0]
-    parts = [(value_ref[...].astype(F32), column(level_ref[...]))]
+    parts = [(value_ref[...], column(level_ref[...]))]
     for k in range(count):
         row = part_refs[2 * k + 1][0:1]
         kept = jnp.where(diagonal(value_ref.shape[0], row.shape[1]), row, 0.0)
-        parts.append((part_refs[2 * k][...].astype(F32), jnp.sum(kept, axis=1, keepdims=True)))
-    latent = merged(parts)[0].astype(BF16)
-    first = lax.broadcasted_iota(jnp.int32, (2 * local, reach), 0) < local
-    for h in range(0, heads, 2):
-        two = latent[h * local : (h + 2) * local]
-        weights = jnp.concatenate([w_ref[h], w_ref[h + 1]], axis=1)
-        both = jnp.dot(two, weights, preferred_element_type=F32)
-        values[pl.ds(h * local, 2 * local), :] = jnp.where(first, both[:, :reach], both[:, reach:])
+        products = head_products(part_refs[2 * k][...], w_ref, local)
+        parts.append((products, jnp.sum(kept, axis=1, keepdims=True)))
+    values[...] = merged(parts)[0]
     for p in range(local):
         out_ref[p] = values[pl.ds(p, heads, stride=local), :].astype(BF16)
 
@@ -464,13 +470,13 @@
     query, _, acc, level, mass = stages[0]
     new_caches, *own_part = pl.pallas_call(
         near_kernel,
-        out_shape=[shape(private_caches.shape), shape((rows, rank)), shape((rows, LANES), F32)],
-        in_specs=[SMEM] * 2 + [VMEM] * (7 + len(other)),
+        out_shape=[shape(private_caches.shape), shape((rows, reach), F32), shape((rows, LANES), F32)],
+        in_specs=[SMEM] * 2 + [VMEM] * (8 + len(other)),
         out_specs=[VMEM] * 3,
         compiler_params=PARAMS,
         cost_estimate=NO_COST,
         name="suffix_near",
-    )(ancestors, lengths, new_latent, query, acc, level, mass, given, moved, *other)
+    )(ancestors, lengths, new_latent, w_uv, query, acc, level, mass, given, moved, *other)
     parts += own_part
 
     head_values = pl.pallas_call(

time: 39 us -> 38.9 us (level)
  no operation moved by 1% of the time
where the time goes in v23:
time: 38.9 us; the launch traced here: 38.8 us
  starting transfers between devices  18.3 us (47%)
  Pallas kernels  14.2 us (37%)
  waiting for transfers between devices  3.86 us (10%)
  local copies, waits for them, and re-layouts  1.46 us (4%)
  between operations  0.89 us (2%)
    ppermute x1, starting transfers between devices, on_device(): middle = lax.ppermute(block, 'dom', [(0, 2), (3, 1)])  7.63 us
    pallas_call x2, Pallas kernels, prefix_attention(): pl.pallas_call(functools.partial(prefix_kernel, len(queries), tiles), out...  6.57 us
    ppermute x1, starting transfers between devices, on_device(): late = lax.ppermute(chosen, 'dom', swap)  3.7 us
    ppermute x3, starting transfers between devices, on_device(): lax.ppermute(own, 'seq', pairs(*r))  2.15 us
    ppermute x1, waiting for transfers between devices, on_device(): late = lax.ppermute(chosen, 'dom', swap)  2.15 us
    ppermute x2, starting transfers between devices, on_device(): lax.ppermute(s, 'seq', back(1 + i // 2, 0))  2.09 us
    pallas_call x1, Pallas kernels, on_device(): pl.pallas_call(near_kernel, out_shape=[shape(private_caches.shape), shape...  1.76 us
    unnamed x20, local copies, waits for them, and re-layouts  1.42 us
  transfers between devices with their start and end apart: 14, of which 5 were waited for; matrix products, arithmetic and copies ran while one was open for 0% of the time, Pallas kernels for 29%

profile of v23, /device:TPU:0, one launch (start us, length us, event | category | flops | bytes accessed | tf_op | source)
XLA Modules:
  0.0 38.8 jit_solution(15489643235423812288)
XLA Ops:
  0.6 0.8 %collective-permute-start.5 = (bf16[4,64,576]{2,1,0:T(8,128)(2,1)}, bf16[4,64,576]{2,1,0:T(8,128)(2,1)S(1)}, u32[]{:S(2)}, u32[]{:S(2)}) collective-permute-start(bf16[4,64,576]{2,1,0:T(8,128)(2,1)} %cache_ref.1), channel_id=1, source_target_pairs={{1,2},{2,1},{5,6},{6,5},{9,10},{10,9},{13,14},{14,13},{17,18},{18,... | collective-permute-start | bytes 884744 | tf_op jit(solution)/shard_map/ppermute | solution.py:396
  1.5 1.4 %copy-done.5 = bf16[4,64,576]{2,1,0:T(8,128)(2,1)S(1)} copy-done((bf16[4,64,576]{2,1,0:T(8,128)(2,1)S(1)}, bf16[4,64,576]{2,1,0:T(8,128)(2,1)}, u32[]{:S(2)}) %copy-start.5) | copy-done | bytes 294936
  2.9 7.6 %collective-permute-start.4 = (bf16[128,1152]{1,0:T(8,128)(2,1)S(1)}, bf16[128,1152]{1,0:T(8,128)(2,1)S(1)}, u32[]{:S(2)}, u32[]{:S(2)}) collective-permute-start(bf16[128,1152]{1,0:T(8,128)(2,1)S(1)} %pack.1.refs_0_), channel_id=1, source_target_pairs={{0,2},{3,1},{4,6},{7,5},{8,10},{11,9},{12,14},{15,13},{16,18},{19,... | collective-permute-start | bytes 884744 | tf_op jit(solution)/shard_map/ppermute | solution.py:395
  10.7 0.6 %project.1.refs_0_ = bf16[128,576]{1,0:T(8,128)(2,1)S(1)} custom-call(bf16[128,128]{1,0:T(8,128)(2,1)S(1)} %bitcast.9, bf16[128,64]{1,0:T(8,128)(2,1)S(1)} %bitcast.10, bf16[32,128,512]{2,1,0:T(8,128)(2,1)S(1)} %copy-done.4), custom_call_target="tpu_custom_call" | custom-call | flops 8000000000 | tf_op jit(solution)/shard_map/project/pallas_call | solution.py:404
  11.3 1.6 %collective-permute-start.1 = (bf16[128,576]{1,0:T(8,128)(2,1)S(1)}, bf16[128,576]{1,0:T(8,128)(2,1)S(1)}, u32[]{:S(2)}, u32[]{:S(2)}) collective-permute-start(bf16[128,576]{1,0:T(8,128)(2,1)S(1)} %project.1.refs_0_), channel_id=1, source_target_pairs={{0,12},{4,8},{8,4},{12,0},{1,13},{5,9},{9,5},{13,1},{2,14},{6,10},... | collective-permute-start | bytes 442376 | tf_op jit(solution)/shard_map/ppermute | solution.py:426
  12.9 0.5 %collective-permute-start = (bf16[128,576]{1,0:T(8,128)(2,1)S(1)}, bf16[128,576]{1,0:T(8,128)(2,1)S(1)}, u32[]{:S(2)}, u32[]{:S(2)}) collective-permute-start(bf16[128,576]{1,0:T(8,128)(2,1)S(1)} %project.1.refs_0_), channel_id=1, source_target_pairs={{0,8},{4,12},{8,0},{12,4},{1,9},{5,13},{9,1},{13,5},{2,10},{6,14},... | collective-permute-start | bytes 442376 | tf_op jit(solution)/shard_map/ppermute | solution.py:426
  13.5 1.4 %collective-permute-start.6 = (s32[4]{0:T(128)S(1)}, s32[4]{0:T(128)S(1)}, u32[]{:S(2)}, u32[]{:S(2)}) collective-permute-start(s32[4]{0:T(128)S(1)} %copy-done.1), channel_id=1, source_target_pairs={{0,1},{3,2},{4,5},{7,6},{8,9},{11,10},{12,13},{15,14},{16,17},{19,... | collective-permute-start | bytes 56 | tf_op jit(solution)/shard_map/ppermute | solution.py:397
  14.9 3.3 %prefix_attention.3 = (f32[128,512]{1,0:T(8,128)S(1)}, f32[128,128]{1,0:T(8,128)S(1)}, f32[128,128]{1,0:T(8,128)S(1)}, bf16[128,640]{1,0:T(8,128)(2,1)S(1)}) custom-call(bf16[128,576]{1,0:T(8,128)(2,1)S(1)} %project.1.refs_0_, bf16[128,576]{1,0:T(8,128)(2,1)S(1)} %collective-permute-done.2.refs_1_, bf16[576,4096]{1,0:T(8,128)(2,1)S(1)} %bitcast.7), custom_call_target="tpu_custom_call" | custom-call | tf_op jit(solution)/shard_map/prefix_attention/pallas_call | solution.py:115
  18.3 0.7 %gather.3 = bf16[128,1152]{1,0:T(8,128)(2,1)S(1)} custom-call(s32[4]{0:T(128)S(1)} %collective-permute-done.6.names, bf16[128,1152]{1,0:T(8,128)(2,1)S(1)} %pack.1.refs_0_, bf16[128,1152]{1,0:T(8,128)(2,1)S(1)} %collective-permute-done.4.refs_1_, bf16[4,64,576]{2,1,0:T(8,128)(2,1)S(1)} %collective-permute-done.5.refs_2_, ...), custom_call_target="tpu_custom_call" | custom-call | tf_op jit(solution)/shard_map/gather/pallas_call | solution.py:230
  18.9 3.7 %collective-permute-start.7 = (bf16[128,1152]{1,0:T(8,128)(2,1)S(1)}, bf16[128,1152]{1,0:T(8,128)(2,1)S(1)}, u32[]{:S(2)}, u32[]{:S(2)}) collective-permute-start(bf16[128,1152]{1,0:T(8,128)(2,1)S(1)} %gather.3), channel_id=1, source_target_pairs={{0,1},{1,0},{2,3},{3,2},{4,5},{5,4},{6,7},{7,6},{8,9},{9,8},{10,11... | collective-permute-start | bytes 884744 | tf_op jit(solution)/shard_map/ppermute | solution.py:436
  22.6 3.3 %prefix_attention.2 = (f32[256,512]{1,0:T(8,128)S(1)}, f32[256,128]{1,0:T(8,128)S(1)}, f32[256,128]{1,0:T(8,128)S(1)}) custom-call(bf16[128,576]{1,0:T(8,128)(2,1)S(1)} %collective-permute-done.refs_0_, bf16[128,576]{1,0:T(8,128)(2,1)S(1)} %collective-permute-done.1.refs_1_.refs_0_, bf16[576,4096]{1,0:T(8,128)(2,1)S(1)} %bitcast.8), custom_call_target="tpu_custom_call" | custom-call | flops 2281701376 | bytes 4718592 | tf_op jit(solution)/shard_map/prefix_attention/pallas_call | solution.py:115
  25.9 0.7 %gather.2.refs_4_ = bf16[128,1152]{1,0:T(8,128)(2,1)S(1)} custom-call(s32[4]{0:T(128)S(1)} %copy-done.1, bf16[128,1152]{1,0:T(8,128)(2,1)S(1)} %pack.1.refs_0_, bf16[128,1152]{1,0:T(8,128)(2,1)S(1)} %collective-permute-done.4.refs_1_, bf16[4,64,576]{2,1,0:T(8,128)(2,1)S(1)} %collective-permute-done.5.refs_2_), custom_call_target="tpu_custom_call" | custom-call | tf_op jit(solution)/shard_map/gather/pallas_call | solution.py:230
  26.6 2.2 %collective-permute-done.7.refs_5_ = bf16[128,1152]{1,0:T(8,128)(2,1)S(1)} collective-permute-done((bf16[128,1152]{1,0:T(8,128)(2,1)S(1)}, bf16[128,1152]{1,0:T(8,128)(2,1)S(1)}, u32[]{:S(2)}, u32[]{:S(2)}) %collective-permute-start.7) | collective-permute-done | bytes 294944 | tf_op jit(solution)/shard_map/ppermute | solution.py:436
  28.8 1.4 %suffix_give.1 = (bf16[256,576]{1,0:T(8,128)(2,1)S(1)}, bf16[128,640]{1,0:T(8,128)(2,1)S(1)}) custom-call(s32[4]{0:T(128)S(1)} %copy-done.1, s32[16]{0:T(128)S(1)} %copy-done.3, bf16[128,576]{1,0:T(8,128)(2,1)S(1)} %collective-permute-done.1.refs_1_.refs_0_, f32[256,512]{1,0:T(8,128)S(1)} %get-tuple-element.23.refs_1_, ...), custom_call_target="tpu_custom_call" | custom-call | tf_op jit(solution)/shard_map/suffix_give/pallas_call | solution.py:446
  30.2 1.1 %suffix_keep.1 = (bf16[128,640]{1,0:T(8,128)(2,1)S(1)}, bf16[96,576]{1,0:T(8,128)(2,1)S(1)}, bf16[80,576]{1,0:T(8,128)(2,1)S(1)}, bf16[80,576]{1,0:T(8,128)(2,1)S(1)}) custom-call(s32[4]{0:T(128)S(1)} %copy-done.1, s32[16]{0:T(128)S(1)} %copy-done.3, bf16[128,576]{1,0:T(8,128)(2,1)S(1)} %collective-permute-done.refs_0_, ...), custom_call_target="tpu_custom_call" | custom-call | tf_op jit(solution)/shard_map/suffix_keep/pallas_call | solution.py:456
  31.3 0.3 collective-permute-done.8.refs_1_
  31.8 1.6 %collective-permute-start.9 = (bf16[128,512]{1,0:T(8,128)(2,1)S(1)}, bf16[128,512]{1,0:T(8,128)(2,1)S(1)}, u32[]{:S(2)}, u32[]{:S(2)}) collective-permute-start(bf16[128,512]{1,0:T(8,128)(2,1)S(1)} %get-tuple-element.32), channel_id=1, source_target_pairs={{8,0},{12,4},{0,8},{4,12},{9,1},{13,5},{1,9},{5,13},{10,2},{14,6},... | collective-permute-start | bytes 393224 | tf_op jit(solution)/shard_map/ppermute | solution.py:466
  33.3 0.5 %collective-permute-start.12 = (bf16[80,576]{1,0:T(8,128)(2,1)S(1)}, bf16[80,576]{1,0:T(8,128)(2,1)S(1)}, u32[]{:S(2)}, u32[]{:S(2)}) collective-permute-start(bf16[80,576]{1,0:T(8,128)(2,1)S(1)} %get-tuple-element.39), channel_id=1, source_target_pairs={{0,4},{4,0},{8,12},{12,8},{1,5},{5,1},{9,13},{13,9},{2,6},{6,2},{1... | collective-permute-start | bytes 276488 | tf_op jit(solution)/shard_map/ppermute | solution.py:467
  33.8 0.5 %collective-permute-start.10 = (f32[8,128]{1,0:T(8,128)S(1)}, f32[8,128]{1,0:T(8,128)S(1)}, u32[]{:S(2)}, u32[]{:S(2)}) collective-permute-start(f32[8,128]{1,0:T(8,128)S(1)} %get-tuple-element.33), channel_id=1, source_target_pairs={{8,0},{12,4},{0,8},{4,12},{9,1},{13,5},{1,9},{5,13},{10,2},{14,6},... | collective-permute-start | bytes 12296 | tf_op jit(solution)/shard_map/ppermute | solution.py:466
  34.4 0.4 %collective-permute-done.12.refs_7_ = bf16[80,576]{1,0:T(8,128)(2,1)S(1)} collective-permute-done((bf16[80,576]{1,0:T(8,128)(2,1)S(1)}, bf16[80,576]{1,0:T(8,128)(2,1)S(1)}, u32[]{:S(2)}, u32[]{:S(2)}) %collective-permute-start.12) | collective-permute-done | bytes 92192 | tf_op jit(solution)/shard_map/ppermute | solution.py:467
  34.8 0.3 collective-permute-done.13.refs_8_
  35.2 1.8 %suffix_near.1 = (bf16[4,64,576]{2,1,0:T(8,128)(2,1)}, f32[128,128]{1,0:T(8,128)S(1)}, f32[128,128]{1,0:T(8,128)S(1)}) custom-call(s32[4]{0:T(128)S(1)} %copy-done.1, s32[16]{0:T(128)S(1)} %copy-done.3, bf16[4,576]{1,0:T(4,128)(2,1)S(1)} %copy-done.2, bf16[32,512,128]{2,1,0:T(8,128)(2,1)S(1)} %copy-done, bf16[128,576]{1,0:T(8,128)(2,1)S(1)} %project.1.refs_0_, ...), custom_call_target="tpu_custom_call" | custom-call | tf_op jit(solution)/shard_map/suffix_near/pallas_call | solution.py:471
  36.9 0.6 %collective-permute-done.10.refs_1_ = f32[8,128]{1,0:T(8,128)S(1)} collective-permute-done((f32[8,128]{1,0:T(8,128)S(1)}, f32[8,128]{1,0:T(8,128)S(1)}, u32[]{:S(2)}, u32[]{:S(2)}) %collective-permute-start.10) | collective-permute-done | bytes 4128 | tf_op jit(solution)/shard_map/ppermute | solution.py:466
  37.5 1.3 %final.1 = bf16[4,32,128]{2,1,0:T(8,128)(2,1)} custom-call(bf16[128,512]{1,0:T(8,128)(2,1)S(1)} %collective-permute-done.9.refs_0_, f32[8,128]{1,0:T(8,128)S(1)} %collective-permute-done.10.refs_1_, f32[128,128]{1,0:T(8,128)S(1)} %get-tuple-element.41.refs_2_, f32[128,128]{1,0:T(8,128)S(1)} %get-tuple-element.42.refs_3_, bf16[32,512,128]{2,1,0:T(8,128)(2,1)S(1)} %copy-done), custom_call_target="tpu_custom_call" | custom-call | tf_op jit(solution)/shard_map/final/pallas_call | solution.py:482
  (38 shorter events, 0.4 us)
Async XLA Ops:
  0.6 10.0 %copy-start.4 = (bf16[32,128,512]{2,1,0:T(8,128)(2,1)S(1)}, bf16[32,128,512]{2,1,0:T(8,128)(2,1)}, u32[]{:S(2)}) copy-start(bf16[32,128,512]{2,1,0:T(8,128)(2,1)} %w_ref.2) | copy-start | bytes 12582916
  0.6 17.6 %collective-permute-start.5 = (bf16[4,64,576]{2,1,0:T(8,128)(2,1)}, bf16[4,64,576]{2,1,0:T(8,128)(2,1)S(1)}, u32[]{:S(2)}, u32[]{:S(2)}) collective-permute-start(bf16[4,64,576]{2,1,0:T(8,128)(2,1)} %cache_ref.1), channel_id=1, source_target_pairs={{1,2},{2,1},{5,6},{6,5},{9,10},{10,9},{13,14},{14,13},{17,18},{18,... | collective-permute-start | bytes 884744 | tf_op jit(solution)/shard_map/ppermute | solution.py:396
  1.5 1.4 %copy-start.5 = (bf16[4,64,576]{2,1,0:T(8,128)(2,1)S(1)}, bf16[4,64,576]{2,1,0:T(8,128)(2,1)}, u32[]{:S(2)}) copy-start(bf16[4,64,576]{2,1,0:T(8,128)(2,1)} %cache_ref.1) | copy-start | bytes 884740
  2.8 7.7 %copy-start.6 = (bf16[4,32,128]{2,1,0:T(8,128)(2,1)S(1)}, bf16[4,32,128]{2,1,0:T(8,128)(2,1)}, u32[]{:S(2)}) copy-start(bf16[4,32,128]{2,1,0:T(8,128)(2,1)} %param.9) | copy-start | bytes 98308
  2.8 7.8 %copy-start.7 = (bf16[4,32,64]{2,1,0:T(8,128)(2,1)S(1)}, bf16[4,32,64]{2,1,0:T(8,128)(2,1)}, u32[]{:S(2)}) copy-start(bf16[4,32,64]{2,1,0:T(8,128)(2,1)} %param.10) | copy-start | bytes 49156
  2.8 12.0 %slice-start = ((s8[4718592]{0:T(1024)(128)(4,1)}), s8[4194304]{0:T(1024)(128)(4,1)S(1)}, s32[]{:S(2)}) async-start(s8[4718592]{0:T(1024)(128)(4,1)} %bitcast.5), calls=%async_computation | async-start | bytes 8388608
  2.9 15.3 %collective-permute-start.4 = (bf16[128,1152]{1,0:T(8,128)(2,1)S(1)}, bf16[128,1152]{1,0:T(8,128)(2,1)S(1)}, u32[]{:S(2)}, u32[]{:S(2)}) collective-permute-start(bf16[128,1152]{1,0:T(8,128)(2,1)S(1)} %pack.1.refs_0_), channel_id=1, source_target_pairs={{0,2},{3,1},{4,6},{7,5},{8,10},{11,9},{12,14},{15,13},{16,18},{19,... | collective-permute-start | bytes 884744 | tf_op jit(solution)/shard_map/ppermute | solution.py:395
  10.6 4.3 %slice-start.1 = ((s8[4718592]{0:T(1024)(128)(4,1)}), s8[524288]{0:T(1024)(128)(4,1)S(1)}, s32[]{:S(2)}) async-start(s8[4718592]{0:T(1024)(128)(4,1)} %bitcast.5), calls=%async_computation.1 | async-start | bytes 1048576
  10.7 2.8 %copy-start.1 = (s32[4]{0:T(128)S(1)}, s32[4]{0:T(128)}, u32[]{:S(2)}) copy-start(s32[4]{0:T(128)} %anc.5) | copy-start | bytes 52
  11.3 2.2 %collective-permute-start.2 = (bf16[128,576]{1,0:T(8,128)(2,1)S(1)}, bf16[128,576]{1,0:T(8,128)(2,1)S(1)}, u32[]{:S(2)}, u32[]{:S(2)}) collective-permute-start(bf16[128,576]{1,0:T(8,128)(2,1)S(1)} %project.1.refs_0_), channel_id=1, source_target_pairs={{0,4},{4,0},{8,12},{12,8},{1,5},{5,1},{9,13},{13,9},{2,6},{6,2},{1... | collective-permute-start | bytes 442376 | tf_op jit(solution)/shard_map/ppermute | solution.py:426
  11.3 11.3 %collective-permute-start.1 = (bf16[128,576]{1,0:T(8,128)(2,1)S(1)}, bf16[128,576]{1,0:T(8,128)(2,1)S(1)}, u32[]{:S(2)}, u32[]{:S(2)}) collective-permute-start(bf16[128,576]{1,0:T(8,128)(2,1)S(1)} %project.1.refs_0_), channel_id=1, source_target_pairs={{0,12},{4,8},{8,4},{12,0},{1,13},{5,9},{9,5},{13,1},{2,14},{6,10},... | collective-permute-start | bytes 442376 | tf_op jit(solution)/shard_map/ppermute | solution.py:426
  12.9 9.7 %collective-permute-start = (bf16[128,576]{1,0:T(8,128)(2,1)S(1)}, bf16[128,576]{1,0:T(8,128)(2,1)S(1)}, u32[]{:S(2)}, u32[]{:S(2)}) collective-permute-start(bf16[128,576]{1,0:T(8,128)(2,1)S(1)} %project.1.refs_0_), channel_id=1, source_target_pairs={{0,8},{4,12},{8,0},{12,4},{1,9},{5,13},{9,1},{13,5},{2,10},{6,14},... | collective-permute-start | bytes 442376 | tf_op jit(solution)/shard_map/ppermute | solution.py:426
  13.5 4.7 %collective-permute-start.6 = (s32[4]{0:T(128)S(1)}, s32[4]{0:T(128)S(1)}, u32[]{:S(2)}, u32[]{:S(2)}) collective-permute-start(s32[4]{0:T(128)S(1)} %copy-done.1), channel_id=1, source_target_pairs={{0,1},{3,2},{4,5},{7,6},{8,9},{11,10},{12,13},{15,14},{16,17},{19,... | collective-permute-start | bytes 56 | tf_op jit(solution)/shard_map/ppermute | solution.py:397
  18.9 9.8 %collective-permute-start.7 = (bf16[128,1152]{1,0:T(8,128)(2,1)S(1)}, bf16[128,1152]{1,0:T(8,128)(2,1)S(1)}, u32[]{:S(2)}, u32[]{:S(2)}) collective-permute-start(bf16[128,1152]{1,0:T(8,128)(2,1)S(1)} %gather.3), channel_id=1, source_target_pairs={{0,1},{1,0},{2,3},{3,2},{4,5},{5,4},{6,7},{7,6},{8,9},{9,8},{10,11... | collective-permute-start | bytes 884744 | tf_op jit(solution)/shard_map/ppermute | solution.py:436
  22.6 6.1 %copy-start.3 = (s32[16]{0:T(128)S(1)}, s32[16]{0:T(128)}, u32[]{:S(2)}) copy-start(s32[16]{0:T(128)} %lens.5) | copy-start | bytes 196
  22.6 4.0 %collective-permute-start.3 = (bf16[128,640]{1,0:T(8,128)(2,1)S(1)}, bf16[128,640]{1,0:T(8,128)(2,1)S(1)}, u32[]{:S(2)}, u32[]{:S(2)}) collective-permute-start(bf16[128,640]{1,0:T(8,128)(2,1)S(1)} %get-tuple-element.26), channel_id=1, source_target_pairs={{0,4},{4,0},{8,12},{12,8},{1,5},{5,1},{9,13},{13,9},{2,6},{6,2},{1... | collective-permute-start | bytes 491528 | tf_op jit(solution)/shard_map/ppermute | solution.py:433
  25.9 9.2 %copy-start = (bf16[32,512,128]{2,1,0:T(8,128)(2,1)S(1)}, bf16[32,512,128]{2,1,0:T(8,128)(2,1)}, u32[]{:S(2)}) copy-start(bf16[32,512,128]{2,1,0:T(8,128)(2,1)} %refs_4_.1) | copy-start | bytes 12582916
  25.9 9.2 %copy-start.2 = (bf16[4,576]{1,0:T(4,128)(2,1)S(1)}, bf16[4,576]{1,0:T(4,128)(2,1)}, u32[]{:S(2)}) copy-start(bf16[4,576]{1,0:T(4,128)(2,1)} %fresh_ref.1) | copy-start | bytes 13828
  30.1 1.5 %collective-permute-start.8 = (bf16[128,640]{1,0:T(8,128)(2,1)S(1)}, bf16[128,640]{1,0:T(8,128)(2,1)S(1)}, u32[]{:S(2)}, u32[]{:S(2)}) collective-permute-start(bf16[128,640]{1,0:T(8,128)(2,1)S(1)} %get-tuple-element.31), channel_id=1, source_target_pairs={{0,4},{4,0},{8,12},{12,8},{1,5},{5,1},{9,13},{13,9},{2,6},{6,2},{1... | collective-permute-start | bytes 491528 | tf_op jit(solution)/shard_map/ppermute | solution.py:465
  31.8 5.7 %collective-permute-start.9 = (bf16[128,512]{1,0:T(8,128)(2,1)S(1)}, bf16[128,512]{1,0:T(8,128)(2,1)S(1)}, u32[]{:S(2)}, u32[]{:S(2)}) collective-permute-start(bf16[128,512]{1,0:T(8,128)(2,1)S(1)} %get-tuple-element.32), channel_id=1, source_target_pairs={{8,0},{12,4},{0,8},{4,12},{9,1},{13,5},{1,9},{5,13},{10,2},{14,6},... | collective-permute-start | bytes 393224 | tf_op jit(solution)/shard_map/ppermute | solution.py:466
  33.3 1.8 %collective-permute-start.11 = (bf16[96,576]{1,0:T(8,128)(2,1)S(1)}, bf16[96,576]{1,0:T(8,128)(2,1)S(1)}, u32[]{:S(2)}, u32[]{:S(2)}) collective-permute-start(bf16[96,576]{1,0:T(8,128)(2,1)S(1)} %get-tuple-element.38), channel_id=1, source_target_pairs={{0,4},{4,0},{8,12},{12,8},{1,5},{5,1},{9,13},{13,9},{2,6},{6,2},{1... | collective-permute-start | bytes 331784 | tf_op jit(solution)/shard_map/ppermute | solution.py:467
  33.3 1.5 %collective-permute-start.12 = (bf16[80,576]{1,0:T(8,128)(2,1)S(1)}, bf16[80,576]{1,0:T(8,128)(2,1)S(1)}, u32[]{:S(2)}, u32[]{:S(2)}) collective-permute-start(bf16[80,576]{1,0:T(8,128)(2,1)S(1)} %get-tuple-element.39), channel_id=1, source_target_pairs={{0,4},{4,0},{8,12},{12,8},{1,5},{5,1},{9,13},{13,9},{2,6},{6,2},{1... | collective-permute-start | bytes 276488 | tf_op jit(solution)/shard_map/ppermute | solution.py:467
  33.8 1.3 %collective-permute-start.13 = (bf16[80,576]{1,0:T(8,128)(2,1)S(1)}, bf16[80,576]{1,0:T(8,128)(2,1)S(1)}, u32[]{:S(2)}, u32[]{:S(2)}) collective-permute-start(bf16[80,576]{1,0:T(8,128)(2,1)S(1)} %get-tuple-element.40), channel_id=1, source_target_pairs={{0,4},{4,0},{8,12},{12,8},{1,5},{5,1},{9,13},{13,9},{2,6},{6,2},{1... | collective-permute-start | bytes 276488 | tf_op jit(solution)/shard_map/ppermute | solution.py:467
  33.8 3.7 %collective-permute-start.10 = (f32[8,128]{1,0:T(8,128)S(1)}, f32[8,128]{1,0:T(8,128)S(1)}, u32[]{:S(2)}, u32[]{:S(2)}) collective-permute-start(f32[8,128]{1,0:T(8,128)S(1)} %get-tuple-element.33), channel_id=1, source_target_pairs={{8,0},{12,4},{0,8},{4,12},{9,1},{13,5},{1,9},{5,13},{10,2},{14,6},... | collective-permute-start | bytes 12296 | tf_op jit(solution)/shard_map/ppermute | solution.py:466

commit v24 on v23

--- a/solution.py
+++ b/solution.py
@@ -197,12 +197,17 @@
     return (dom == 0) | (dom == 3)
 
 
-def gather_kernel(line, chosen, names, *refs):
+def picked(row, at):
+    lane = lax.broadcasted_iota(jnp.int32, row.shape, 1)
+    return jnp.sum(jnp.where(lane == at, row.astype(F32), 0.0)).astype(jnp.int32)
+
+
+def gather_kernel(line, chosen, local, names_ref, *refs):
     block_refs, out_ref = refs[:-1], refs[-1]
     if chosen:
         block_refs = block_refs[:-1]
     dom = lax.axis_index("dom")
-    local = names.shape[0]
+    names = [picked(names_ref[...], p) for p in range(local)]
     some = out_ref.shape[0] // local
     for p in range(local):
         owner, slot = lax.div(names[p], local), lax.rem(names[p], local)
@@ -225,12 +230,12 @@
                     pack_slot(block_ref[slot], out_ref, part)
 
 
-def gathered(names, blocks, line, token=None):
+def gathered(names, blocks, line, local, token=None):
     token = [] if token is None else [token]
     return pl.pallas_call(
-        functools.partial(gather_kernel, line, bool(token)),
+        functools.partial(gather_kernel, line, bool(token), local),
         out_shape=shape(blocks[0].shape),
-        in_specs=[SMEM] + [VMEM] * len(blocks) + [ANY] * len(token),
+        in_specs=[VMEM] * (1 + len(blocks)) + [ANY] * len(token),
         out_specs=VMEM,
         compiler_params=PARAMS,
         cost_estimate=NO_COST,
@@ -238,21 +243,19 @@
     )(names, *blocks, *token)
 
 
-def far_part(anc, lens, query_ref, stage_refs, part, keys):
+def far_part(ends, query_ref, stage_refs, part, keys):
     acc_ref, max_ref, sum_ref = stage_refs
-    local = anc.shape[0]
-    span, rank = keys.shape[0] // local, acc_ref.shape[1]
-    ends = [lens[anc[p]] for p in range(local)]
+    span, rank = keys.shape[0] // len(ends), acc_ref.shape[1]
     seen = visible(query_ref.shape[0], ends, [lax.axis_index("seq") * span], span)
     known = [(column(max_ref[part]), column(sum_ref[part]), acc_ref[part])]
     return packed(*attend(query_ref[...], keys, seen, rank, known))
 
 
-def give_kernel(stages, line, anc, lens, *refs):
+def give_kernel(stages, line, local, names_ref, lens_ref, *refs):
     stage_refs, refs = refs[: 4 * stages], refs[4 * stages :]
     early_ref, late_ref, moved_ref, give_refs = refs[0], refs[1], refs[2], refs[3:]
     dom = lax.axis_index("dom")
-    local = anc.shape[0]
+    anc = [picked(names_ref[...], p) for p in range(local)]
     some = early_ref.shape[0] // local
     span, width = 2 * some, moved_ref.shape[1]
     rank = stage_refs[1].shape[1]
@@ -285,7 +288,8 @@
     for k in range(stages):
         query_ref, *partial = stage_refs[4 * k : 4 * k + 4]
         rows = query_ref.shape[0]
-        give_refs[k][...] = far_part(anc, lens, query_ref, partial, pl.ds(rows, rows), moved_ref[...])
+        ends = [picked(lens_ref[...], anc[p]) for p in range(local)]
+        give_refs[k][...] = far_part(ends, query_ref, partial, pl.ds(rows, rows), moved_ref[...])
 
 
 def keep_kernel(stages, anc, lens, *refs):
@@ -298,7 +302,8 @@
     for k in range(stages):
         query_ref, *partial = stage_refs[4 * k : 4 * k + 4]
         rows = query_ref.shape[0]
-        keep_refs[k][...] = far_part(anc, lens, query_ref, partial, pl.ds(0, rows), moved_ref[...])
+        ends = [lens[anc[p]] for p in range(anc.shape[0])]
+        keep_refs[k][...] = far_part(ends, query_ref, partial, pl.ds(0, rows), moved_ref[...])
 
 
 def head_products(latent, w_ref, local):
@@ -389,12 +394,13 @@
         name="pack",
     )(private_caches)
     nope_rows, rope_rows = (jnp.swapaxes(q, 0, 1).reshape(rows, -1) for q in (q_nope, q_rope))
+    names = jnp.pad(ancestors, (0, LANES - local))[None]
     line = dom_size == 4
     if line:
         swap = [(0, 1), (1, 0), (2, 3), (3, 2)]
         middle = lax.ppermute(block, "dom", [(0, 2), (3, 1)])
         far = lax.ppermute(private_caches, "dom", [(1, 2), (2, 1)])
-        theirs = lax.ppermute(ancestors, "dom", [(0, 1), (3, 2)])
+        theirs = lax.ppermute(names, "dom", [(0, 1), (3, 2)])
     else:
         blocks = [block] + [
             lax.ppermute(block, "dom", [(i, (i + k) % dom_size) for i in range(dom_size)])
@@ -432,11 +438,11 @@
         if t == 0:
             given = lax.ppermute(stage.pop(), "seq", pairs(0, 1))
         if line and t == 0:
-            chosen = gathered(theirs, [block, middle, far], line, stage[3])
+            chosen = gathered(theirs, [block, middle, far], line, local, stage[3])
             late = lax.ppermute(chosen, "dom", swap)
-            early = gathered(ancestors, [block, middle, far], line)
+            early = gathered(names, [block, middle, far], line, local)
     if not line:
-        early = late = gathered(ancestors, blocks, line)
+        early = late = gathered(names, blocks, line, local)
 
     part = shape((rows, rank + LANES))
     others = chips - 1
@@ -444,13 +450,13 @@
     giving = [a for stage in stages[1:] for a in stage[1:]]
     keeping = [a for stage in stages[1:] for a in (stage[0], *stage[2:])]
     moved, *give = pl.pallas_call(
-        functools.partial(give_kernel, others, line),
+        functools.partial(give_kernel, others, line, local),
         out_shape=[shape((local * span, width))] + [part] * others,
-        in_specs=[SMEM] * 2 + [VMEM] * (len(giving) + 2),
+        in_specs=[VMEM] * (len(giving) + 4),
         out_specs=[VMEM] * (1 + others),
         compiler_params=PARAMS,
         name="suffix_give",
-    )(ancestors, lengths, *giving, early, late)
+    )(names, jnp.pad(lengths, (0, max(0, LANES - lengths.shape[0])))[None], *giving, early, late)
     small = local * span // 48 * 16
     cuts = (local * span - 2 * small, small, small)
     keep_and_pieces = pl.pallas_call(

time: 38.9 us -> 38 us (0.977)
  Pallas kernels: 14.2 us -> 12.9 us
  waiting for transfers between devices: 3.86 us -> 4.28 us
    pallas_call x3, Pallas kernels: 2.68 us -> 1.38 us  [the longest x1 0.92 us: on_device(): pl.pallas_call(functools.partial(give_kernel, others, line, local), out_s...]
    ppermute x1, waiting for transfers between devices: 2.15 us -> 2.57 us  [on_device(): late = lax.ppermute(chosen, 'dom', swap)]
  transfers between devices with their start and end apart: 14 -> 14, of which waited for: 5 -> 5; matrix products, arithmetic and copies ran while one was open for 0% -> 0% of each run, Pallas kernels for 29% -> 28%
where the time goes in v24:
time: 38 us; the launch traced here: 37.8 us
  starting transfers between devices  18.3 us (48%)
  Pallas kernels  12.9 us (34%)
  waiting for transfers between devices  4.28 us (11%)
  local copies, waits for them, and re-layouts  1.47 us (4%)
  between operations  0.9 us (2%)
    ppermute x1, starting transfers between devices, on_device(): middle = lax.ppermute(block, 'dom', [(0, 2), (3, 1)])  7.63 us
    pallas_call x2, Pallas kernels, prefix_attention(): pl.pallas_call(functools.partial(prefix_kernel, len(queries), tiles), out...  6.57 us
    ppermute x1, starting transfers between devices, on_device(): late = lax.ppermute(chosen, 'dom', swap)  3.58 us
    ppermute x1, waiting for transfers between devices, on_device(): late = lax.ppermute(chosen, 'dom', swap)  2.57 us
    ppermute x3, starting transfers between devices, on_device(): lax.ppermute(own, 'seq', pairs(*r))  2.17 us
    ppermute x2, starting transfers between devices, on_device(): lax.ppermute(s, 'seq', back(1 + i // 2, 0))  2.09 us
    pallas_call x1, Pallas kernels, on_device(): pl.pallas_call(near_kernel, out_shape=[shape(private_caches.shape), shape...  1.76 us
    unnamed x20, local copies, waits for them, and re-layouts  1.42 us
  transfers between devices with their start and end apart: 14, of which 5 were waited for; matrix products, arithmetic and copies ran while one was open for 0% of the time, Pallas kernels for 28%

profile of v24, /device:TPU:0, one launch (start us, length us, event | category | flops | bytes accessed | tf_op | source)
XLA Modules:
  0.0 37.8 jit_solution(1170840572674238970)
XLA Ops:
  0.6 0.8 %collective-permute-start.5 = (bf16[4,64,576]{2,1,0:T(8,128)(2,1)}, bf16[4,64,576]{2,1,0:T(8,128)(2,1)S(1)}, u32[]{:S(2)}, u32[]{:S(2)}) collective-permute-start(bf16[4,64,576]{2,1,0:T(8,128)(2,1)} %cache_ref.1), channel_id=1, source_target_pairs={{1,2},{2,1},{5,6},{6,5},{9,10},{10,9},{13,14},{14,13},{17,18},{18,... | collective-permute-start | bytes 884744 | tf_op jit(solution)/shard_map/ppermute | solution.py:402
  1.5 1.4 %copy-done.5 = bf16[4,64,576]{2,1,0:T(8,128)(2,1)S(1)} copy-done((bf16[4,64,576]{2,1,0:T(8,128)(2,1)S(1)}, bf16[4,64,576]{2,1,0:T(8,128)(2,1)}, u32[]{:S(2)}) %copy-start.5) | copy-done | bytes 294936
  2.9 7.6 %collective-permute-start.4 = (bf16[128,1152]{1,0:T(8,128)(2,1)S(1)}, bf16[128,1152]{1,0:T(8,128)(2,1)S(1)}, u32[]{:S(2)}, u32[]{:S(2)}) collective-permute-start(bf16[128,1152]{1,0:T(8,128)(2,1)S(1)} %pack.1.refs_0_), channel_id=1, source_target_pairs={{0,2},{3,1},{4,6},{7,5},{8,10},{11,9},{12,14},{15,13},{16,18},{19,... | collective-permute-start | bytes 884744 | tf_op jit(solution)/shard_map/ppermute | solution.py:401
  10.7 0.6 %project.1.refs_0_ = bf16[128,576]{1,0:T(8,128)(2,1)S(1)} custom-call(bf16[128,128]{1,0:T(8,128)(2,1)S(1)} %bitcast.13, bf16[128,64]{1,0:T(8,128)(2,1)S(1)} %bitcast.14, bf16[32,128,512]{2,1,0:T(8,128)(2,1)S(1)} %copy-done.4), custom_call_target="tpu_custom_call" | custom-call | flops 8000000000 | tf_op jit(solution)/shard_map/project/pallas_call | solution.py:410
  11.4 1.6 %collective-permute-start.1 = (bf16[128,576]{1,0:T(8,128)(2,1)S(1)}, bf16[128,576]{1,0:T(8,128)(2,1)S(1)}, u32[]{:S(2)}, u32[]{:S(2)}) collective-permute-start(bf16[128,576]{1,0:T(8,128)(2,1)S(1)} %project.1.refs_0_), channel_id=1, source_target_pairs={{0,12},{4,8},{8,4},{12,0},{1,13},{5,9},{9,5},{13,1},{2,14},{6,10},... | collective-permute-start | bytes 442376 | tf_op jit(solution)/shard_map/ppermute | solution.py:432
  13.0 0.5 %collective-permute-start = (bf16[128,576]{1,0:T(8,128)(2,1)S(1)}, bf16[128,576]{1,0:T(8,128)(2,1)S(1)}, u32[]{:S(2)}, u32[]{:S(2)}) collective-permute-start(bf16[128,576]{1,0:T(8,128)(2,1)S(1)} %project.1.refs_0_), channel_id=1, source_target_pairs={{0,8},{4,12},{8,0},{12,4},{1,9},{5,13},{9,1},{13,5},{2,10},{6,14},... | collective-permute-start | bytes 442376 | tf_op jit(solution)/shard_map/ppermute | solution.py:432
  13.5 1.4 %collective-permute-start.6 = (s32[1,128]{1,0:T(1,128)S(1)}, s32[1,128]{1,0:T(1,128)S(1)}, u32[]{:S(2)}, u32[]{:S(2)}) collective-permute-start(s32[1,128]{1,0:T(1,128)S(1)} %pad_bitcast_fusion.1.names_ref), channel_id=1, source_target_pairs={{0,1},{3,2},{4,5},{7,6},{8,9},{11,10},{12,13},{15,14},{16,17},{19,... | collective-permute-start | bytes 1544 | tf_op jit(solution)/shard_map/ppermute | solution.py:403
  14.9 3.3 %prefix_attention.3 = (f32[128,512]{1,0:T(8,128)S(1)}, f32[128,128]{1,0:T(8,128)S(1)}, f32[128,128]{1,0:T(8,128)S(1)}, bf16[128,640]{1,0:T(8,128)(2,1)S(1)}) custom-call(bf16[128,576]{1,0:T(8,128)(2,1)S(1)} %project.1.refs_0_, bf16[128,576]{1,0:T(8,128)(2,1)S(1)} %collective-permute-done.2.refs_1_, bf16[576,4096]{1,0:T(8,128)(2,1)S(1)} %bitcast.11), custom_call_target="tpu_custom_call" | custom-call | tf_op jit(solution)/shard_map/prefix_attention/pallas_call | solution.py:115
  18.3 0.2 gather.3
  18.5 3.6 %collective-permute-start.7 = (bf16[128,1152]{1,0:T(8,128)(2,1)S(1)}, bf16[128,1152]{1,0:T(8,128)(2,1)S(1)}, u32[]{:S(2)}, u32[]{:S(2)}) collective-permute-start(bf16[128,1152]{1,0:T(8,128)(2,1)S(1)} %gather.3), channel_id=1, source_target_pairs={{0,1},{1,0},{2,3},{3,2},{4,5},{5,4},{6,7},{7,6},{8,9},{9,8},{10,11... | collective-permute-start | bytes 884744 | tf_op jit(solution)/shard_map/ppermute | solution.py:442
  22.1 3.3 %prefix_attention.2 = (f32[256,512]{1,0:T(8,128)S(1)}, f32[256,128]{1,0:T(8,128)S(1)}, f32[256,128]{1,0:T(8,128)S(1)}) custom-call(bf16[128,576]{1,0:T(8,128)(2,1)S(1)} %collective-permute-done.refs_0_, bf16[128,576]{1,0:T(8,128)(2,1)S(1)} %collective-permute-done.1.refs_1_.refs_0_, bf16[576,4096]{1,0:T(8,128)(2,1)S(1)} %bitcast.12), custom_call_target="tpu_custom_call" | custom-call | flops 2281701376 | bytes 4718592 | tf_op jit(solution)/shard_map/prefix_attention/pallas_call | solution.py:115
  25.4 0.2 gather.2.refs_4_
  25.7 2.6 %collective-permute-done.7.refs_5_ = bf16[128,1152]{1,0:T(8,128)(2,1)S(1)} collective-permute-done((bf16[128,1152]{1,0:T(8,128)(2,1)S(1)}, bf16[128,1152]{1,0:T(8,128)(2,1)S(1)}, u32[]{:S(2)}, u32[]{:S(2)}) %collective-permute-start.7) | collective-permute-done | bytes 294944 | tf_op jit(solution)/shard_map/ppermute | solution.py:442
  28.2 0.9 %suffix_give.1 = (bf16[256,576]{1,0:T(8,128)(2,1)S(1)}, bf16[128,640]{1,0:T(8,128)(2,1)S(1)}) custom-call(s32[1,128]{1,0:T(1,128)S(1)} %pad_bitcast_fusion.1.names_ref, s32[1,128]{1,0:T(1,128)S(1)} %pad_bitcast_fusion.lens_ref, bf16[128,576]{1,0:T(8,128)(2,1)S(1)} %collective-permute-done.1.refs_1_.refs_0_, f32[256,512]{1,0:T(8,128)S(1)} %get-tuple-element.23.refs_1_, ...), custom_call_target="tpu_custom_call" | custom-call | tf_op jit(solution)/shard_map/suffix_give/pallas_call | solution.py:452
  29.2 1.1 %suffix_keep.1 = (bf16[128,640]{1,0:T(8,128)(2,1)S(1)}, bf16[96,576]{1,0:T(8,128)(2,1)S(1)}, bf16[80,576]{1,0:T(8,128)(2,1)S(1)}, bf16[80,576]{1,0:T(8,128)(2,1)S(1)}) custom-call(s32[4]{0:T(128)S(1)} %copy-done.2, s32[16]{0:T(128)S(1)} %copy-done.3, bf16[128,576]{1,0:T(8,128)(2,1)S(1)} %collective-permute-done.refs_0_, ...), custom_call_target="tpu_custom_call" | custom-call | tf_op jit(solution)/shard_map/suffix_keep/pallas_call | solution.py:462
  30.3 0.3 collective-permute-done.8.refs_1_
  30.8 1.6 %collective-permute-start.9 = (bf16[128,512]{1,0:T(8,128)(2,1)S(1)}, bf16[128,512]{1,0:T(8,128)(2,1)S(1)}, u32[]{:S(2)}, u32[]{:S(2)}) collective-permute-start(bf16[128,512]{1,0:T(8,128)(2,1)S(1)} %get-tuple-element.32), channel_id=1, source_target_pairs={{8,0},{12,4},{0,8},{4,12},{9,1},{13,5},{1,9},{5,13},{10,2},{14,6},... | collective-permute-start | bytes 393224 | tf_op jit(solution)/shard_map/ppermute | solution.py:472
  32.4 0.5 %collective-permute-start.12 = (bf16[80,576]{1,0:T(8,128)(2,1)S(1)}, bf16[80,576]{1,0:T(8,128)(2,1)S(1)}, u32[]{:S(2)}, u32[]{:S(2)}) collective-permute-start(bf16[80,576]{1,0:T(8,128)(2,1)S(1)} %get-tuple-element.39), channel_id=1, source_target_pairs={{0,4},{4,0},{8,12},{12,8},{1,5},{5,1},{9,13},{13,9},{2,6},{6,2},{1... | collective-permute-start | bytes 276488 | tf_op jit(solution)/shard_map/ppermute | solution.py:473
  32.9 0.5 %collective-permute-start.10 = (f32[8,128]{1,0:T(8,128)S(1)}, f32[8,128]{1,0:T(8,128)S(1)}, u32[]{:S(2)}, u32[]{:S(2)}) collective-permute-start(f32[8,128]{1,0:T(8,128)S(1)} %get-tuple-element.33), channel_id=1, source_target_pairs={{8,0},{12,4},{0,8},{4,12},{9,1},{13,5},{1,9},{5,13},{10,2},{14,6},... | collective-permute-start | bytes 12296 | tf_op jit(solution)/shard_map/ppermute | solution.py:472
  33.4 0.4 %collective-permute-done.12.refs_7_ = bf16[80,576]{1,0:T(8,128)(2,1)S(1)} collective-permute-done((bf16[80,576]{1,0:T(8,128)(2,1)S(1)}, bf16[80,576]{1,0:T(8,128)(2,1)S(1)}, u32[]{:S(2)}, u32[]{:S(2)}) %collective-permute-start.12) | collective-permute-done | bytes 92192 | tf_op jit(solution)/shard_map/ppermute | solution.py:473
  33.8 0.3 collective-permute-done.13.refs_8_
  34.2 1.8 %suffix_near.1 = (bf16[4,64,576]{2,1,0:T(8,128)(2,1)}, f32[128,128]{1,0:T(8,128)S(1)}, f32[128,128]{1,0:T(8,128)S(1)}) custom-call(s32[4]{0:T(128)S(1)} %copy-done.2, s32[16]{0:T(128)S(1)} %copy-done.3, bf16[4,576]{1,0:T(4,128)(2,1)S(1)} %copy-done.1, bf16[32,512,128]{2,1,0:T(8,128)(2,1)S(1)} %copy-done, bf16[128,576]{1,0:T(8,128)(2,1)S(1)} %project.1.refs_0_, ...), custom_call_target="tpu_custom_call" | custom-call | tf_op jit(solution)/shard_map/suffix_near/pallas_call | solution.py:477
  35.9 0.6 %collective-permute-done.10.refs_1_ = f32[8,128]{1,0:T(8,128)S(1)} collective-permute-done((f32[8,128]{1,0:T(8,128)S(1)}, f32[8,128]{1,0:T(8,128)S(1)}, u32[]{:S(2)}, u32[]{:S(2)}) %collective-permute-start.10) | collective-permute-done | bytes 4128 | tf_op jit(solution)/shard_map/ppermute | solution.py:472
  36.6 1.3 %final.1 = bf16[4,32,128]{2,1,0:T(8,128)(2,1)} custom-call(bf16[128,512]{1,0:T(8,128)(2,1)S(1)} %collective-permute-done.9.refs_0_, f32[8,128]{1,0:T(8,128)S(1)} %collective-permute-done.10.refs_1_, f32[128,128]{1,0:T(8,128)S(1)} %get-tuple-element.41.refs_2_, f32[128,128]{1,0:T(8,128)S(1)} %get-tuple-element.42.refs_3_, bf16[32,512,128]{2,1,0:T(8,128)(2,1)S(1)} %copy-done), custom_call_target="tpu_custom_call" | custom-call | tf_op jit(solution)/shard_map/final/pallas_call | solution.py:488
  (40 shorter events, 0.5 us)
Async XLA Ops:
  0.6 10.0 %copy-start.4 = (bf16[32,128,512]{2,1,0:T(8,128)(2,1)S(1)}, bf16[32,128,512]{2,1,0:T(8,128)(2,1)}, u32[]{:S(2)}) copy-start(bf16[32,128,512]{2,1,0:T(8,128)(2,1)} %w_ref.2) | copy-start | bytes 12582916
  0.6 17.6 %collective-permute-start.5 = (bf16[4,64,576]{2,1,0:T(8,128)(2,1)}, bf16[4,64,576]{2,1,0:T(8,128)(2,1)S(1)}, u32[]{:S(2)}, u32[]{:S(2)}) collective-permute-start(bf16[4,64,576]{2,1,0:T(8,128)(2,1)} %cache_ref.1), channel_id=1, source_target_pairs={{1,2},{2,1},{5,6},{6,5},{9,10},{10,9},{13,14},{14,13},{17,18},{18,... | collective-permute-start | bytes 884744 | tf_op jit(solution)/shard_map/ppermute | solution.py:402
  1.5 1.4 %copy-start.5 = (bf16[4,64,576]{2,1,0:T(8,128)(2,1)S(1)}, bf16[4,64,576]{2,1,0:T(8,128)(2,1)}, u32[]{:S(2)}) copy-start(bf16[4,64,576]{2,1,0:T(8,128)(2,1)} %cache_ref.1) | copy-start | bytes 884740
  2.8 7.7 %copy-start.6 = (bf16[4,32,128]{2,1,0:T(8,128)(2,1)S(1)}, bf16[4,32,128]{2,1,0:T(8,128)(2,1)}, u32[]{:S(2)}) copy-start(bf16[4,32,128]{2,1,0:T(8,128)(2,1)} %param.9) | copy-start | bytes 98308
  2.8 7.8 %copy-start.7 = (bf16[4,32,64]{2,1,0:T(8,128)(2,1)S(1)}, bf16[4,32,64]{2,1,0:T(8,128)(2,1)}, u32[]{:S(2)}) copy-start(bf16[4,32,64]{2,1,0:T(8,128)(2,1)} %param.10) | copy-start | bytes 49156
  2.8 12.1 %slice-start = ((s8[4718592]{0:T(1024)(128)(4,1)}), s8[4194304]{0:T(1024)(128)(4,1)S(1)}, s32[]{:S(2)}) async-start(s8[4718592]{0:T(1024)(128)(4,1)} %bitcast.9), calls=%async_computation | async-start | bytes 8388608
  2.9 15.3 %collective-permute-start.4 = (bf16[128,1152]{1,0:T(8,128)(2,1)S(1)}, bf16[128,1152]{1,0:T(8,128)(2,1)S(1)}, u32[]{:S(2)}, u32[]{:S(2)}) collective-permute-start(bf16[128,1152]{1,0:T(8,128)(2,1)S(1)} %pack.1.refs_0_), channel_id=1, source_target_pairs={{0,2},{3,1},{4,6},{7,5},{8,10},{11,9},{12,14},{15,13},{16,18},{19,... | collective-permute-start | bytes 884744 | tf_op jit(solution)/shard_map/ppermute | solution.py:401
  10.6 4.3 %slice-start.1 = ((s8[4718592]{0:T(1024)(128)(4,1)}), s8[524288]{0:T(1024)(128)(4,1)S(1)}, s32[]{:S(2)}) async-start(s8[4718592]{0:T(1024)(128)(4,1)} %bitcast.9), calls=%async_computation.1 | async-start | bytes 1048576
  10.7 2.8 %copy-start.2 = (s32[4]{0:T(128)S(1)}, s32[4]{0:T(128)}, u32[]{:S(2)}) copy-start(s32[4]{0:T(128)} %anc.3) | copy-start | bytes 52
  11.3 10.8 %copy-start.3 = (s32[16]{0:T(128)S(1)}, s32[16]{0:T(128)}, u32[]{:S(2)}) copy-start(s32[16]{0:T(128)} %lens.3) | copy-start | bytes 196
  11.3 2.2 %collective-permute-start.2 = (bf16[128,576]{1,0:T(8,128)(2,1)S(1)}, bf16[128,576]{1,0:T(8,128)(2,1)S(1)}, u32[]{:S(2)}, u32[]{:S(2)}) collective-permute-start(bf16[128,576]{1,0:T(8,128)(2,1)S(1)} %project.1.refs_0_), channel_id=1, source_target_pairs={{0,4},{4,0},{8,12},{12,8},{1,5},{5,1},{9,13},{13,9},{2,6},{6,2},{1... | collective-permute-start | bytes 442376 | tf_op jit(solution)/shard_map/ppermute | solution.py:432
  11.4 10.8 %collective-permute-start.1 = (bf16[128,576]{1,0:T(8,128)(2,1)S(1)}, bf16[128,576]{1,0:T(8,128)(2,1)S(1)}, u32[]{:S(2)}, u32[]{:S(2)}) collective-permute-start(bf16[128,576]{1,0:T(8,128)(2,1)S(1)} %project.1.refs_0_), channel_id=1, source_target_pairs={{0,12},{4,8},{8,4},{12,0},{1,13},{5,9},{9,5},{13,1},{2,14},{6,10},... | collective-permute-start | bytes 442376 | tf_op jit(solution)/shard_map/ppermute | solution.py:432
  13.0 9.2 %collective-permute-start = (bf16[128,576]{1,0:T(8,128)(2,1)S(1)}, bf16[128,576]{1,0:T(8,128)(2,1)S(1)}, u32[]{:S(2)}, u32[]{:S(2)}) collective-permute-start(bf16[128,576]{1,0:T(8,128)(2,1)S(1)} %project.1.refs_0_), channel_id=1, source_target_pairs={{0,8},{4,12},{8,0},{12,4},{1,9},{5,13},{9,1},{13,5},{2,10},{6,14},... | collective-permute-start | bytes 442376 | tf_op jit(solution)/shard_map/ppermute | solution.py:432
  13.5 4.8 %collective-permute-start.6 = (s32[1,128]{1,0:T(1,128)S(1)}, s32[1,128]{1,0:T(1,128)S(1)}, u32[]{:S(2)}, u32[]{:S(2)}) collective-permute-start(s32[1,128]{1,0:T(1,128)S(1)} %pad_bitcast_fusion.1.names_ref), channel_id=1, source_target_pairs={{0,1},{3,2},{4,5},{7,6},{8,9},{11,10},{12,13},{15,14},{16,17},{19,... | collective-permute-start | bytes 1544 | tf_op jit(solution)/shard_map/ppermute | solution.py:403
  18.5 9.7 %collective-permute-start.7 = (bf16[128,1152]{1,0:T(8,128)(2,1)S(1)}, bf16[128,1152]{1,0:T(8,128)(2,1)S(1)}, u32[]{:S(2)}, u32[]{:S(2)}) collective-permute-start(bf16[128,1152]{1,0:T(8,128)(2,1)S(1)} %gather.3), channel_id=1, source_target_pairs={{0,1},{1,0},{2,3},{3,2},{4,5},{5,4},{6,7},{7,6},{8,9},{9,8},{10,11... | collective-permute-start | bytes 884744 | tf_op jit(solution)/shard_map/ppermute | solution.py:442
  22.1 3.6 %collective-permute-start.3 = (bf16[128,640]{1,0:T(8,128)(2,1)S(1)}, bf16[128,640]{1,0:T(8,128)(2,1)S(1)}, u32[]{:S(2)}, u32[]{:S(2)}) collective-permute-start(bf16[128,640]{1,0:T(8,128)(2,1)S(1)} %get-tuple-element.26), channel_id=1, source_target_pairs={{0,4},{4,0},{8,12},{12,8},{1,5},{5,1},{9,13},{13,9},{2,6},{6,2},{1... | collective-permute-start | bytes 491528 | tf_op jit(solution)/shard_map/ppermute | solution.py:439
  25.4 8.8 %copy-start = (bf16[32,512,128]{2,1,0:T(8,128)(2,1)S(1)}, bf16[32,512,128]{2,1,0:T(8,128)(2,1)}, u32[]{:S(2)}) copy-start(bf16[32,512,128]{2,1,0:T(8,128)(2,1)} %refs_4_.1) | copy-start | bytes 12582916
  25.4 8.8 %copy-start.1 = (bf16[4,576]{1,0:T(4,128)(2,1)S(1)}, bf16[4,576]{1,0:T(4,128)(2,1)}, u32[]{:S(2)}) copy-start(bf16[4,576]{1,0:T(4,128)(2,1)} %fresh_ref.1) | copy-start | bytes 13828
  29.2 1.5 %collective-permute-start.8 = (bf16[128,640]{1,0:T(8,128)(2,1)S(1)}, bf16[128,640]{1,0:T(8,128)(2,1)S(1)}, u32[]{:S(2)}, u32[]{:S(2)}) collective-permute-start(bf16[128,640]{1,0:T(8,128)(2,1)S(1)} %get-tuple-element.31), channel_id=1, source_target_pairs={{0,4},{4,0},{8,12},{12,8},{1,5},{5,1},{9,13},{13,9},{2,6},{6,2},{1... | collective-permute-start | bytes 491528 | tf_op jit(solution)/shard_map/ppermute | solution.py:471
  30.8 5.8 %collective-permute-start.9 = (bf16[128,512]{1,0:T(8,128)(2,1)S(1)}, bf16[128,512]{1,0:T(8,128)(2,1)S(1)}, u32[]{:S(2)}, u32[]{:S(2)}) collective-permute-start(bf16[128,512]{1,0:T(8,128)(2,1)S(1)} %get-tuple-element.32), channel_id=1, source_target_pairs={{8,0},{12,4},{0,8},{4,12},{9,1},{13,5},{1,9},{5,13},{10,2},{14,6},... | collective-permute-start | bytes 393224 | tf_op jit(solution)/shard_map/ppermute | solution.py:472
  32.4 1.8 %collective-permute-start.11 = (bf16[96,576]{1,0:T(8,128)(2,1)S(1)}, bf16[96,576]{1,0:T(8,128)(2,1)S(1)}, u32[]{:S(2)}, u32[]{:S(2)}) collective-permute-start(bf16[96,576]{1,0:T(8,128)(2,1)S(1)} %get-tuple-element.38), channel_id=1, source_target_pairs={{0,4},{4,0},{8,12},{12,8},{1,5},{5,1},{9,13},{13,9},{2,6},{6,2},{1... | collective-permute-start | bytes 331784 | tf_op jit(solution)/shard_map/ppermute | solution.py:473
  32.4 1.5 %collective-permute-start.12 = (bf16[80,576]{1,0:T(8,128)(2,1)S(1)}, bf16[80,576]{1,0:T(8,128)(2,1)S(1)}, u32[]{:S(2)}, u32[]{:S(2)}) collective-permute-start(bf16[80,576]{1,0:T(8,128)(2,1)S(1)} %get-tuple-element.39), channel_id=1, source_target_pairs={{0,4},{4,0},{8,12},{12,8},{1,5},{5,1},{9,13},{13,9},{2,6},{6,2},{1... | collective-permute-start | bytes 276488 | tf_op jit(solution)/shard_map/ppermute | solution.py:473
  32.9 1.3 %collective-permute-start.13 = (bf16[80,576]{1,0:T(8,128)(2,1)S(1)}, bf16[80,576]{1,0:T(8,128)(2,1)S(1)}, u32[]{:S(2)}, u32[]{:S(2)}) collective-permute-start(bf16[80,576]{1,0:T(8,128)(2,1)S(1)} %get-tuple-element.40), channel_id=1, source_target_pairs={{0,4},{4,0},{8,12},{12,8},{1,5},{5,1},{9,13},{13,9},{2,6},{6,2},{1... | collective-permute-start | bytes 276488 | tf_op jit(solution)/shard_map/ppermute | solution.py:473
  32.9 3.7 %collective-permute-start.10 = (f32[8,128]{1,0:T(8,128)S(1)}, f32[8,128]{1,0:T(8,128)S(1)}, u32[]{:S(2)}, u32[]{:S(2)}) collective-permute-start(f32[8,128]{1,0:T(8,128)S(1)} %get-tuple-element.33), channel_id=1, source_target_pairs={{8,0},{12,4},{0,8},{4,12},{9,1},{13,5},{1,9},{5,13},{10,2},{14,6},... | collective-permute-start | bytes 12296 | tf_op jit(solution)/shard_map/ppermute | solution.py:472

commit v25 on v24

--- a/solution.py
+++ b/solution.py
@@ -292,7 +292,9 @@
         give_refs[k][...] = far_part(ends, query_ref, partial, pl.ds(rows, rows), moved_ref[...])
 
 
-def keep_kernel(stages, anc, lens, *refs):
+def keep_kernel(stages, local, names_ref, lens_ref, *refs):
+    anc = [picked(names_ref[...], p) for p in range(local)]
+    ends = [picked(lens_ref[...], at) for at in anc]
     stage_refs, refs = refs[: 4 * stages], refs[4 * stages :]
     moved_ref, keep_refs, piece_refs = refs[0], refs[1 : 1 + stages], refs[1 + stages :]
     begin = 0
@@ -302,7 +304,6 @@
     for k in range(stages):
         query_ref, *partial = stage_refs[4 * k : 4 * k + 4]
         rows = query_ref.shape[0]
-        ends = [lens[anc[p]] for p in range(anc.shape[0])]
         keep_refs[k][...] = far_part(ends, query_ref, partial, pl.ds(0, rows), moved_ref[...])
 
 
@@ -317,14 +318,14 @@
     return jnp.concatenate(products, axis=0)
 
 
-def near_kernel(anc, lens, fresh_ref, w_ref, *refs):
+def near_kernel(names_ref, lens_ref, fresh_ref, w_ref, *refs):
     seq = lax.axis_index("seq")
     query_ref, acc_ref, max_ref, sum_ref, got_ref, moved_ref, *other_refs = refs[:-3]
     cache_ref, value_ref, level_ref = refs[-3:]
     local, span, width = cache_ref.shape
     rank = acc_ref.shape[1]
     start, other = seq * span, jnp.bitwise_xor(seq, 1) * span
-    ends = [lens[anc[p]] for p in range(local)]
+    ends = [picked(lens_ref[...], picked(names_ref[...], p)) for p in range(local)]
     keys = jnp.concatenate([ref[...] for ref in (moved_ref, *other_refs)], axis=0)
     seen = visible(query_ref.shape[0], ends, [start, other], span)
     level = jnp.sum(got_ref[:, rank:].astype(F32), axis=1, keepdims=True)
@@ -395,6 +396,7 @@
     )(private_caches)
     nope_rows, rope_rows = (jnp.swapaxes(q, 0, 1).reshape(rows, -1) for q in (q_nope, q_rope))
     names = jnp.pad(ancestors, (0, LANES - local))[None]
+    limits = jnp.pad(lengths, (0, max(0, LANES - lengths.shape[0])))[None]
     line = dom_size == 4
     if line:
         swap = [(0, 1), (1, 0), (2, 3), (3, 2)]
@@ -456,17 +458,16 @@
         out_specs=[VMEM] * (1 + others),
         compiler_params=PARAMS,
         name="suffix_give",
-    )(names, jnp.pad(lengths, (0, max(0, LANES - lengths.shape[0])))[None], *giving, early, late)
-    small = local * span // 48 * 16
-    cuts = (local * span - 2 * small, small, small)
+    )(names, limits, *giving, early, late)
+    cuts = (local * span // 2,) * 2
     keep_and_pieces = pl.pallas_call(
-        functools.partial(keep_kernel, others),
+        functools.partial(keep_kernel, others, local),
         out_shape=[part] * others + [shape((cut, width)) for cut in cuts],
-        in_specs=[SMEM] * 2 + [VMEM] * (len(keeping) + 1),
+        in_specs=[VMEM] * (len(keeping) + 3),
         out_specs=[VMEM] * (others + len(cuts)),
         compiler_params=PARAMS,
         name="suffix_keep",
-    )(ancestors, lengths, *keeping, moved)
+    )(names, limits, *keeping, moved)
     keep, pieces = keep_and_pieces[:others], keep_and_pieces[others:]
     sums = chip_merge(keep, [lax.ppermute(g, "seq", pairs(0, 1)) for g in give])
     parts = [lax.ppermute(s, "seq", back(1 + i // 2, 0)) for i, s in enumerate(sums)]
@@ -477,12 +478,12 @@
     new_caches, *own_part = pl.pallas_call(
         near_kernel,
         out_shape=[shape(private_caches.shape), shape((rows, reach), F32), shape((rows, LANES), F32)],
-        in_specs=[SMEM] * 2 + [VMEM] * (8 + len(other)),
+        in_specs=[VMEM] * (10 + len(other)),
         out_specs=[VMEM] * 3,
         compiler_params=PARAMS,
         cost_estimate=NO_COST,
         name="suffix_near",
-    )(ancestors, lengths, new_latent, w_uv, query, acc, level, mass, given, moved, *other)
+    )(names, limits, new_latent, w_uv, query, acc, level, mass, given, moved, *other)
     parts += own_part
 
     head_values = pl.pallas_call(

time: 38 us -> 38.1 us (level)
  Pallas kernels: 12.9 us -> 12.2 us
  waiting for transfers between devices: 4.28 us -> 4.92 us
    ppermute x2, waiting for transfers between devices: 0.61 us -> 2.15 us  [on_device(): lax.ppermute(s, 'seq', back(1 + i // 2, 0))]
    ppermute x3 -> x2, waiting for transfers between devices: 0.77 us -> 0.01 us  [on_device(): other = [lax.ppermute(piece, 'seq', pairs(0, 1)) for piece in pieces]]
    pallas_call x1, Pallas kernels: 1.06 us -> 0.55 us  [on_device(): pl.pallas_call(functools.partial(keep_kernel, others, local), out_shape=[...]
  transfers between devices with their start and end apart: 14 -> 13, of which waited for: 5 -> 3; matrix products, arithmetic and copies ran while one was open for 0% -> 0% of each run, Pallas kernels for 28% -> 26%
where the time goes in v25:
time: 38.1 us; the launch traced here: 37.9 us
  starting transfers between devices  18.4 us (48%)
  Pallas kernels  12.2 us (32%)
  waiting for transfers between devices  4.92 us (13%)
  local copies, waits for them, and re-layouts  1.47 us (4%)
  between operations  0.91 us (2%)
    ppermute x1, starting transfers between devices, on_device(): middle = lax.ppermute(block, 'dom', [(0, 2), (3, 1)])  7.63 us
    pallas_call x2, Pallas kernels, prefix_attention(): pl.pallas_call(functools.partial(prefix_kernel, len(queries), tiles), out...  6.57 us
    ppermute x1, starting transfers between devices, on_device(): late = lax.ppermute(chosen, 'dom', swap)  3.58 us
    ppermute x1, waiting for transfers between devices, on_device(): late = lax.ppermute(chosen, 'dom', swap)  2.57 us
    ppermute x3, starting transfers between devices, on_device(): lax.ppermute(own, 'seq', pairs(*r))  2.17 us
    ppermute x2, waiting for transfers between devices, on_device(): lax.ppermute(s, 'seq', back(1 + i // 2, 0))  2.15 us
    ppermute x2, starting transfers between devices, on_device(): lax.ppermute(s, 'seq', back(1 + i // 2, 0))  2.09 us
    pallas_call x1, Pallas kernels, on_device(): pl.pallas_call(near_kernel, out_shape=[shape(private_caches.shape), shape...  1.55 us
  transfers between devices with their start and end apart: 13, of which 3 were waited for; matrix products, arithmetic and copies ran while one was open for 0% of the time, Pallas kernels for 26%

profile of v25, /device:TPU:0, one launch (start us, length us, event | category | flops | bytes accessed | tf_op | source)
XLA Modules:
  0.0 37.9 jit_solution(12468818209505593834)
XLA Ops:
  0.6 0.8 %collective-permute-start.5 = (bf16[4,64,576]{2,1,0:T(8,128)(2,1)}, bf16[4,64,576]{2,1,0:T(8,128)(2,1)S(1)}, u32[]{:S(2)}, u32[]{:S(2)}) collective-permute-start(bf16[4,64,576]{2,1,0:T(8,128)(2,1)} %cache_ref.1), channel_id=1, source_target_pairs={{1,2},{2,1},{5,6},{6,5},{9,10},{10,9},{13,14},{14,13},{17,18},{18,... | collective-permute-start | bytes 884744 | tf_op jit(solution)/shard_map/ppermute | solution.py:404
  1.5 1.4 %copy-done.3 = bf16[4,64,576]{2,1,0:T(8,128)(2,1)S(1)} copy-done((bf16[4,64,576]{2,1,0:T(8,128)(2,1)S(1)}, bf16[4,64,576]{2,1,0:T(8,128)(2,1)}, u32[]{:S(2)}) %copy-start.3) | copy-done | bytes 294936
  2.9 7.6 %collective-permute-start.4 = (bf16[128,1152]{1,0:T(8,128)(2,1)S(1)}, bf16[128,1152]{1,0:T(8,128)(2,1)S(1)}, u32[]{:S(2)}, u32[]{:S(2)}) collective-permute-start(bf16[128,1152]{1,0:T(8,128)(2,1)S(1)} %pack.1.refs_0_), channel_id=1, source_target_pairs={{0,2},{3,1},{4,6},{7,5},{8,10},{11,9},{12,14},{15,13},{16,18},{19,... | collective-permute-start | bytes 884744 | tf_op jit(solution)/shard_map/ppermute | solution.py:403
  10.7 0.6 %project.1.refs_0_ = bf16[128,576]{1,0:T(8,128)(2,1)S(1)} custom-call(bf16[128,128]{1,0:T(8,128)(2,1)S(1)} %bitcast.13, bf16[128,64]{1,0:T(8,128)(2,1)S(1)} %bitcast.14, bf16[32,128,512]{2,1,0:T(8,128)(2,1)S(1)} %copy-done.2), custom_call_target="tpu_custom_call" | custom-call | flops 8000000000 | tf_op jit(solution)/shard_map/project/pallas_call | solution.py:412
  11.4 1.6 %collective-permute-start.1 = (bf16[128,576]{1,0:T(8,128)(2,1)S(1)}, bf16[128,576]{1,0:T(8,128)(2,1)S(1)}, u32[]{:S(2)}, u32[]{:S(2)}) collective-permute-start(bf16[128,576]{1,0:T(8,128)(2,1)S(1)} %project.1.refs_0_), channel_id=1, source_target_pairs={{0,12},{4,8},{8,4},{12,0},{1,13},{5,9},{9,5},{13,1},{2,14},{6,10},... | collective-permute-start | bytes 442376 | tf_op jit(solution)/shard_map/ppermute | solution.py:434
  13.0 0.5 %collective-permute-start = (bf16[128,576]{1,0:T(8,128)(2,1)S(1)}, bf16[128,576]{1,0:T(8,128)(2,1)S(1)}, u32[]{:S(2)}, u32[]{:S(2)}) collective-permute-start(bf16[128,576]{1,0:T(8,128)(2,1)S(1)} %project.1.refs_0_), channel_id=1, source_target_pairs={{0,8},{4,12},{8,0},{12,4},{1,9},{5,13},{9,1},{13,5},{2,10},{6,14},... | collective-permute-start | bytes 442376 | tf_op jit(solution)/shard_map/ppermute | solution.py:434
  13.5 1.4 %collective-permute-start.6 = (s32[1,128]{1,0:T(1,128)S(1)}, s32[1,128]{1,0:T(1,128)S(1)}, u32[]{:S(2)}, u32[]{:S(2)}) collective-permute-start(s32[1,128]{1,0:T(1,128)S(1)} %pad_bitcast_fusion.1.names_ref), channel_id=1, source_target_pairs={{0,1},{3,2},{4,5},{7,6},{8,9},{11,10},{12,13},{15,14},{16,17},{19,... | collective-permute-start | bytes 1544 | tf_op jit(solution)/shard_map/ppermute | solution.py:405
  14.9 3.3 %prefix_attention.3 = (f32[128,512]{1,0:T(8,128)S(1)}, f32[128,128]{1,0:T(8,128)S(1)}, f32[128,128]{1,0:T(8,128)S(1)}, bf16[128,640]{1,0:T(8,128)(2,1)S(1)}) custom-call(bf16[128,576]{1,0:T(8,128)(2,1)S(1)} %project.1.refs_0_, bf16[128,576]{1,0:T(8,128)(2,1)S(1)} %collective-permute-done.2.refs_1_, bf16[576,4096]{1,0:T(8,128)(2,1)S(1)} %bitcast.11), custom_call_target="tpu_custom_call" | custom-call | tf_op jit(solution)/shard_map/prefix_attention/pallas_call | solution.py:115
  18.3 0.2 gather.3
  18.5 3.6 %collective-permute-start.7 = (bf16[128,1152]{1,0:T(8,128)(2,1)S(1)}, bf16[128,1152]{1,0:T(8,128)(2,1)S(1)}, u32[]{:S(2)}, u32[]{:S(2)}) collective-permute-start(bf16[128,1152]{1,0:T(8,128)(2,1)S(1)} %gather.3), channel_id=1, source_target_pairs={{0,1},{1,0},{2,3},{3,2},{4,5},{5,4},{6,7},{7,6},{8,9},{9,8},{10,11... | collective-permute-start | bytes 884744 | tf_op jit(solution)/shard_map/ppermute | solution.py:444
  22.1 3.3 %prefix_attention.2 = (f32[256,512]{1,0:T(8,128)S(1)}, f32[256,128]{1,0:T(8,128)S(1)}, f32[256,128]{1,0:T(8,128)S(1)}) custom-call(bf16[128,576]{1,0:T(8,128)(2,1)S(1)} %collective-permute-done.refs_0_, bf16[128,576]{1,0:T(8,128)(2,1)S(1)} %collective-permute-done.1.refs_1_.refs_0_, bf16[576,4096]{1,0:T(8,128)(2,1)S(1)} %bitcast.12), custom_call_target="tpu_custom_call" | custom-call | flops 2281701376 | bytes 4718592 | tf_op jit(solution)/shard_map/prefix_attention/pallas_call | solution.py:115
  25.4 0.2 gather.2.refs_4_
  25.7 2.6 %collective-permute-done.7.refs_5_ = bf16[128,1152]{1,0:T(8,128)(2,1)S(1)} collective-permute-done((bf16[128,1152]{1,0:T(8,128)(2,1)S(1)}, bf16[128,1152]{1,0:T(8,128)(2,1)S(1)}, u32[]{:S(2)}, u32[]{:S(2)}) %collective-permute-start.7) | collective-permute-done | bytes 294944 | tf_op jit(solution)/shard_map/ppermute | solution.py:444
  28.2 0.9 %suffix_give.1 = (bf16[256,576]{1,0:T(8,128)(2,1)S(1)}, bf16[128,640]{1,0:T(8,128)(2,1)S(1)}) custom-call(s32[1,128]{1,0:T(1,128)S(1)} %pad_bitcast_fusion.1.names_ref, s32[1,128]{1,0:T(1,128)S(1)} %pad_bitcast_fusion.lens_ref, bf16[128,576]{1,0:T(8,128)(2,1)S(1)} %collective-permute-done.1.refs_1_.refs_0_, f32[256,512]{1,0:T(8,128)S(1)} %get-tuple-element.22.refs_1_, ...), custom_call_target="tpu_custom_call" | custom-call | tf_op jit(solution)/shard_map/suffix_give/pallas_call | solution.py:454
  29.2 0.6 %suffix_keep.1 = (bf16[128,640]{1,0:T(8,128)(2,1)S(1)}, bf16[128,576]{1,0:T(8,128)(2,1)S(1)}, bf16[128,576]{1,0:T(8,128)(2,1)S(1)}) custom-call(s32[1,128]{1,0:T(1,128)S(1)} %pad_bitcast_fusion.1.names_ref, s32[1,128]{1,0:T(1,128)S(1)} %pad_bitcast_fusion.lens_ref, bf16[128,576]{1,0:T(8,128)(2,1)S(1)} %collective-permute-done.refs_0_, ...), custom_call_target="tpu_custom_call" | custom-call | tf_op jit(solution)/shard_map/suffix_keep/pallas_call | solution.py:463
  29.8 0.6 %collective-permute-start.11 = (bf16[128,576]{1,0:T(8,128)(2,1)S(1)}, bf16[128,576]{1,0:T(8,128)(2,1)S(1)}, u32[]{:S(2)}, u32[]{:S(2)}) collective-permute-start(bf16[128,576]{1,0:T(8,128)(2,1)S(1)} %get-tuple-element.37), channel_id=1, source_target_pairs={{0,4},{4,0},{8,12},{12,8},{1,5},{5,1},{9,13},{13,9},{2,6},{6,2},{1... | collective-permute-start | bytes 442376 | tf_op jit(solution)/shard_map/ppermute | solution.py:474
  30.4 0.1 collective-permute-start.12
  30.4 0.2 collective-permute-done.8.refs_1_
  30.6 0.2 chip_merge.1
  30.8 1.6 %collective-permute-start.9 = (bf16[128,512]{1,0:T(8,128)(2,1)S(1)}, bf16[128,512]{1,0:T(8,128)(2,1)S(1)}, u32[]{:S(2)}, u32[]{:S(2)}) collective-permute-start(bf16[128,512]{1,0:T(8,128)(2,1)S(1)} %get-tuple-element.31), channel_id=1, source_target_pairs={{8,0},{12,4},{0,8},{4,12},{9,1},{13,5},{1,9},{5,13},{10,2},{14,6},... | collective-permute-start | bytes 393224 | tf_op jit(solution)/shard_map/ppermute | solution.py:473
  32.4 0.5 %collective-permute-start.10 = (f32[8,128]{1,0:T(8,128)S(1)}, f32[8,128]{1,0:T(8,128)S(1)}, u32[]{:S(2)}, u32[]{:S(2)}) collective-permute-start(f32[8,128]{1,0:T(8,128)S(1)} %get-tuple-element.32), channel_id=1, source_target_pairs={{8,0},{12,4},{0,8},{4,12},{9,1},{13,5},{1,9},{5,13},{10,2},{14,6},... | collective-permute-start | bytes 12296 | tf_op jit(solution)/shard_map/ppermute | solution.py:473
  32.9 1.5 %suffix_near.1 = (bf16[4,64,576]{2,1,0:T(8,128)(2,1)}, f32[128,128]{1,0:T(8,128)S(1)}, f32[128,128]{1,0:T(8,128)S(1)}) custom-call(s32[1,128]{1,0:T(1,128)S(1)} %pad_bitcast_fusion.1.names_ref, s32[1,128]{1,0:T(1,128)S(1)} %pad_bitcast_fusion.lens_ref, bf16[4,576]{1,0:T(4,128)(2,1)S(1)} %copy-done.1, bf16[32,512,128]{2,1,0:T(8,128)(2,1)S(1)} %copy-done, ...), custom_call_target="tpu_custom_call" | custom-call | tf_op jit(solution)/shard_map/suffix_near/pallas_call | solution.py:478
  34.5 2.1 %collective-permute-done.10.refs_1_ = f32[8,128]{1,0:T(8,128)S(1)} collective-permute-done((f32[8,128]{1,0:T(8,128)S(1)}, f32[8,128]{1,0:T(8,128)S(1)}, u32[]{:S(2)}, u32[]{:S(2)}) %collective-permute-start.10) | collective-permute-done | bytes 4128 | tf_op jit(solution)/shard_map/ppermute | solution.py:473
  36.6 1.3 %final.1 = bf16[4,32,128]{2,1,0:T(8,128)(2,1)} custom-call(bf16[128,512]{1,0:T(8,128)(2,1)S(1)} %collective-permute-done.9.refs_0_, f32[8,128]{1,0:T(8,128)S(1)} %collective-permute-done.10.refs_1_, f32[128,128]{1,0:T(8,128)S(1)} %get-tuple-element.39.refs_2_, f32[128,128]{1,0:T(8,128)S(1)} %get-tuple-element.40.refs_3_, bf16[32,512,128]{2,1,0:T(8,128)(2,1)S(1)} %copy-done), custom_call_target="tpu_custom_call" | custom-call | tf_op jit(solution)/shard_map/final/pallas_call | solution.py:489
  (38 shorter events, 0.3 us)
Async XLA Ops:
  0.6 10.0 %copy-start.2 = (bf16[32,128,512]{2,1,0:T(8,128)(2,1)S(1)}, bf16[32,128,512]{2,1,0:T(8,128)(2,1)}, u32[]{:S(2)}) copy-start(bf16[32,128,512]{2,1,0:T(8,128)(2,1)} %w_ref.2) | copy-start | bytes 12582916
  0.6 17.6 %collective-permute-start.5 = (bf16[4,64,576]{2,1,0:T(8,128)(2,1)}, bf16[4,64,576]{2,1,0:T(8,128)(2,1)S(1)}, u32[]{:S(2)}, u32[]{:S(2)}) collective-permute-start(bf16[4,64,576]{2,1,0:T(8,128)(2,1)} %cache_ref.1), channel_id=1, source_target_pairs={{1,2},{2,1},{5,6},{6,5},{9,10},{10,9},{13,14},{14,13},{17,18},{18,... | collective-permute-start | bytes 884744 | tf_op jit(solution)/shard_map/ppermute | solution.py:404
  1.5 1.4 %copy-start.3 = (bf16[4,64,576]{2,1,0:T(8,128)(2,1)S(1)}, bf16[4,64,576]{2,1,0:T(8,128)(2,1)}, u32[]{:S(2)}) copy-start(bf16[4,64,576]{2,1,0:T(8,128)(2,1)} %cache_ref.1) | copy-start | bytes 884740
  2.8 7.7 %copy-start.4 = (bf16[4,32,128]{2,1,0:T(8,128)(2,1)S(1)}, bf16[4,32,128]{2,1,0:T(8,128)(2,1)}, u32[]{:S(2)}) copy-start(bf16[4,32,128]{2,1,0:T(8,128)(2,1)} %param.9) | copy-start | bytes 98308
  2.8 7.8 %copy-start.5 = (bf16[4,32,64]{2,1,0:T(8,128)(2,1)S(1)}, bf16[4,32,64]{2,1,0:T(8,128)(2,1)}, u32[]{:S(2)}) copy-start(bf16[4,32,64]{2,1,0:T(8,128)(2,1)} %param.10) | copy-start | bytes 49156
  2.8 12.1 %slice-start = ((s8[4718592]{0:T(1024)(128)(4,1)}), s8[4194304]{0:T(1024)(128)(4,1)S(1)}, s32[]{:S(2)}) async-start(s8[4718592]{0:T(1024)(128)(4,1)} %bitcast.9), calls=%async_computation | async-start | bytes 8388608
  2.9 15.3 %collective-permute-start.4 = (bf16[128,1152]{1,0:T(8,128)(2,1)S(1)}, bf16[128,1152]{1,0:T(8,128)(2,1)S(1)}, u32[]{:S(2)}, u32[]{:S(2)}) collective-permute-start(bf16[128,1152]{1,0:T(8,128)(2,1)S(1)} %pack.1.refs_0_), channel_id=1, source_target_pairs={{0,2},{3,1},{4,6},{7,5},{8,10},{11,9},{12,14},{15,13},{16,18},{19,... | collective-permute-start | bytes 884744 | tf_op jit(solution)/shard_map/ppermute | solution.py:403
  10.6 4.3 %slice-start.1 = ((s8[4718592]{0:T(1024)(128)(4,1)}), s8[524288]{0:T(1024)(128)(4,1)S(1)}, s32[]{:S(2)}) async-start(s8[4718592]{0:T(1024)(128)(4,1)} %bitcast.9), calls=%async_computation.1 | async-start | bytes 1048576
  10.7 2.8 %copy-start.6 = (s32[4]{0:T(128)S(1)}, s32[4]{0:T(128)}, u32[]{:S(2)}) copy-start(s32[4]{0:T(128)} %param.16) | copy-start | bytes 52
  11.3 10.8 %copy-start.7 = (s32[16]{0:T(128)S(1)}, s32[16]{0:T(128)}, u32[]{:S(2)}) copy-start(s32[16]{0:T(128)} %param.17) | copy-start | bytes 196
  11.3 2.2 %collective-permute-start.2 = (bf16[128,576]{1,0:T(8,128)(2,1)S(1)}, bf16[128,576]{1,0:T(8,128)(2,1)S(1)}, u32[]{:S(2)}, u32[]{:S(2)}) collective-permute-start(bf16[128,576]{1,0:T(8,128)(2,1)S(1)} %project.1.refs_0_), channel_id=1, source_target_pairs={{0,4},{4,0},{8,12},{12,8},{1,5},{5,1},{9,13},{13,9},{2,6},{6,2},{1... | collective-permute-start | bytes 442376 | tf_op jit(solution)/shard_map/ppermute | solution.py:434
  11.4 10.8 %collective-permute-start.1 = (bf16[128,576]{1,0:T(8,128)(2,1)S(1)}, bf16[128,576]{1,0:T(8,128)(2,1)S(1)}, u32[]{:S(2)}, u32[]{:S(2)}) collective-permute-start(bf16[128,576]{1,0:T(8,128)(2,1)S(1)} %project.1.refs_0_), channel_id=1, source_target_pairs={{0,12},{4,8},{8,4},{12,0},{1,13},{5,9},{9,5},{13,1},{2,14},{6,10},... | collective-permute-start | bytes 442376 | tf_op jit(solution)/shard_map/ppermute | solution.py:434
  13.0 9.2 %collective-permute-start = (bf16[128,576]{1,0:T(8,128)(2,1)S(1)}, bf16[128,576]{1,0:T(8,128)(2,1)S(1)}, u32[]{:S(2)}, u32[]{:S(2)}) collective-permute-start(bf16[128,576]{1,0:T(8,128)(2,1)S(1)} %project.1.refs_0_), channel_id=1, source_target_pairs={{0,8},{4,12},{8,0},{12,4},{1,9},{5,13},{9,1},{13,5},{2,10},{6,14},... | collective-permute-start | bytes 442376 | tf_op jit(solution)/shard_map/ppermute | solution.py:434
  13.5 4.8 %collective-permute-start.6 = (s32[1,128]{1,0:T(1,128)S(1)}, s32[1,128]{1,0:T(1,128)S(1)}, u32[]{:S(2)}, u32[]{:S(2)}) collective-permute-start(s32[1,128]{1,0:T(1,128)S(1)} %pad_bitcast_fusion.1.names_ref), channel_id=1, source_target_pairs={{0,1},{3,2},{4,5},{7,6},{8,9},{11,10},{12,13},{15,14},{16,17},{19,... | collective-permute-start | bytes 1544 | tf_op jit(solution)/shard_map/ppermute | solution.py:405
  18.5 9.7 %collective-permute-start.7 = (bf16[128,1152]{1,0:T(8,128)(2,1)S(1)}, bf16[128,1152]{1,0:T(8,128)(2,1)S(1)}, u32[]{:S(2)}, u32[]{:S(2)}) collective-permute-start(bf16[128,1152]{1,0:T(8,128)(2,1)S(1)} %gather.3), channel_id=1, source_target_pairs={{0,1},{1,0},{2,3},{3,2},{4,5},{5,4},{6,7},{7,6},{8,9},{9,8},{10,11... | collective-permute-start | bytes 884744 | tf_op jit(solution)/shard_map/ppermute | solution.py:444
  22.1 3.6 %collective-permute-start.3 = (bf16[128,640]{1,0:T(8,128)(2,1)S(1)}, bf16[128,640]{1,0:T(8,128)(2,1)S(1)}, u32[]{:S(2)}, u32[]{:S(2)}) collective-permute-start(bf16[128,640]{1,0:T(8,128)(2,1)S(1)} %get-tuple-element.25), channel_id=1, source_target_pairs={{0,4},{4,0},{8,12},{12,8},{1,5},{5,1},{9,13},{13,9},{2,6},{6,2},{1... | collective-permute-start | bytes 491528 | tf_op jit(solution)/shard_map/ppermute | solution.py:441
  25.4 7.5 %copy-start = (bf16[32,512,128]{2,1,0:T(8,128)(2,1)S(1)}, bf16[32,512,128]{2,1,0:T(8,128)(2,1)}, u32[]{:S(2)}) copy-start(bf16[32,512,128]{2,1,0:T(8,128)(2,1)} %refs_4_.1) | copy-start | bytes 12582916
  25.4 7.5 %copy-start.1 = (bf16[4,576]{1,0:T(4,128)(2,1)S(1)}, bf16[4,576]{1,0:T(4,128)(2,1)}, u32[]{:S(2)}) copy-start(bf16[4,576]{1,0:T(4,128)(2,1)} %fresh_ref.1) | copy-start | bytes 13828
  29.2 1.5 %collective-permute-start.8 = (bf16[128,640]{1,0:T(8,128)(2,1)S(1)}, bf16[128,640]{1,0:T(8,128)(2,1)S(1)}, u32[]{:S(2)}, u32[]{:S(2)}) collective-permute-start(bf16[128,640]{1,0:T(8,128)(2,1)S(1)} %get-tuple-element.30), channel_id=1, source_target_pairs={{0,4},{4,0},{8,12},{12,8},{1,5},{5,1},{9,13},{13,9},{2,6},{6,2},{1... | collective-permute-start | bytes 491528 | tf_op jit(solution)/shard_map/ppermute | solution.py:472
  29.8 3.1 %collective-permute-start.11 = (bf16[128,576]{1,0:T(8,128)(2,1)S(1)}, bf16[128,576]{1,0:T(8,128)(2,1)S(1)}, u32[]{:S(2)}, u32[]{:S(2)}) collective-permute-start(bf16[128,576]{1,0:T(8,128)(2,1)S(1)} %get-tuple-element.37), channel_id=1, source_target_pairs={{0,4},{4,0},{8,12},{12,8},{1,5},{5,1},{9,13},{13,9},{2,6},{6,2},{1... | collective-permute-start | bytes 442376 | tf_op jit(solution)/shard_map/ppermute | solution.py:474
  30.4 2.5 %collective-permute-start.12 = (bf16[128,576]{1,0:T(8,128)(2,1)S(1)}, bf16[128,576]{1,0:T(8,128)(2,1)S(1)}, u32[]{:S(2)}, u32[]{:S(2)}) collective-permute-start(bf16[128,576]{1,0:T(8,128)(2,1)S(1)} %get-tuple-element.38), channel_id=1, source_target_pairs={{0,4},{4,0},{8,12},{12,8},{1,5},{5,1},{9,13},{13,9},{2,6},{6,2},{1... | collective-permute-start | bytes 442376 | tf_op jit(solution)/shard_map/ppermute | solution.py:474
  30.8 5.8 %collective-permute-start.9 = (bf16[128,512]{1,0:T(8,128)(2,1)S(1)}, bf16[128,512]{1,0:T(8,128)(2,1)S(1)}, u32[]{:S(2)}, u32[]{:S(2)}) collective-permute-start(bf16[128,512]{1,0:T(8,128)(2,1)S(1)} %get-tuple-element.31), channel_id=1, source_target_pairs={{8,0},{12,4},{0,8},{4,12},{9,1},{13,5},{1,9},{5,13},{10,2},{14,6},... | collective-permute-start | bytes 393224 | tf_op jit(solution)/shard_map/ppermute | solution.py:473
  32.4 4.3 %collective-permute-start.10 = (f32[8,128]{1,0:T(8,128)S(1)}, f32[8,128]{1,0:T(8,128)S(1)}, u32[]{:S(2)}, u32[]{:S(2)}) collective-permute-start(f32[8,128]{1,0:T(8,128)S(1)} %get-tuple-element.32), channel_id=1, source_target_pairs={{8,0},{12,4},{0,8},{4,12},{9,1},{13,5},{1,9},{5,13},{10,2},{14,6},... | collective-permute-start | bytes 12296 | tf_op jit(solution)/shard_map/ppermute | solution.py:473

commit v26 on v25

--- a/solution.py
+++ b/solution.py
@@ -307,12 +307,12 @@
         keep_refs[k][...] = far_part(ends, query_ref, partial, pl.ds(0, rows), moved_ref[...])
 
 
-def head_products(latent, w_ref, local):
-    heads, _, reach = w_ref.shape
+def head_products(latent, w_ref, local, begin=0):
+    heads, reach = latent.shape[0] // local, w_ref.shape[2]
     first = lax.broadcasted_iota(jnp.int32, (2 * local, reach), 0) < local
     products = []
     for h in range(0, heads, 2):
-        weights = jnp.concatenate([w_ref[h], w_ref[h + 1]], axis=1)
+        weights = jnp.concatenate([w_ref[begin + h], w_ref[begin + h + 1]], axis=1)
         both = jnp.dot(latent[h * local : (h + 2) * local], weights, preferred_element_type=F32)
         products.append(jnp.where(first, both[:, :reach], both[:, reach:]))
     return jnp.concatenate(products, axis=0)
@@ -343,34 +343,54 @@
 
 def chip_kernel(count, *refs):
     for k in range(count):
-        value_ref, level_ref = refs[2 * count + 2 * k : 2 * count + 2 * k + 2]
+        first_ref, second_ref, level_ref = refs[2 * count + 3 * k : 2 * count + 3 * k + 3]
         values, level = merged([unpacked(refs[k][...]), unpacked(refs[count + k][...])])
-        value_ref[...] = values.astype(BF16)
+        half = first_ref.shape[0]
+        first_ref[...] = values[:half].astype(BF16)
+        second_ref[...] = values[half:].astype(BF16)
         kept = jnp.where(diagonal(values.shape[0], level_ref.shape[1]), level, 0.0)
         level_ref[...] = jnp.broadcast_to(jnp.sum(kept, axis=0, keepdims=True), level_ref.shape)
 
 
 def chip_merge(keep, got):
     rows, rank = keep[0].shape[0], keep[0].shape[1] - LANES
+    half = shape((rows // 2, rank))
     return pl.pallas_call(
         functools.partial(chip_kernel, len(keep)),
-        out_shape=[shape((rows, rank)), shape((8, max(rows, LANES)), F32)] * len(keep),
+        out_shape=[half, half, shape((8, max(rows, LANES)), F32)] * len(keep),
         in_specs=[VMEM] * (2 * len(keep)),
-        out_specs=[VMEM] * (2 * len(keep)),
+        out_specs=[VMEM] * (3 * len(keep)),
         compiler_params=PARAMS,
         name="chip_merge",
     )(*keep, *got)
 
 
+def half_kernel(local, part_ref, w_ref, out_ref):
+    out_ref[...] = head_products(part_ref[...], w_ref, local)
+
+
+def half_products(part, w_uv, local):
+    return pl.pallas_call(
+        functools.partial(half_kernel, local),
+        out_shape=shape((part.shape[0], w_uv.shape[2]), F32),
+        in_specs=[VMEM] * 2,
+        out_specs=VMEM,
+        compiler_params=PARAMS,
+        cost_estimate=NO_COST,
+        name="half",
+    )(part, w_uv)
+
+
 def final_kernel(count, *refs):
-    part_refs, (value_ref, level_ref, w_ref, out_ref, values) = refs[: 2 * count], refs[2 * count :]
+    part_refs, (value_ref, level_ref, w_ref, out_ref, values) = refs[: 3 * count], refs[3 * count :]
     heads, rank, reach = w_ref.shape
     local = out_ref.shape[0]
     parts = [(value_ref[...], column(level_ref[...]))]
     for k in range(count):
-        row = part_refs[2 * k + 1][0:1]
+        row = part_refs[3 * k + 2][0:1]
         kept = jnp.where(diagonal(value_ref.shape[0], row.shape[1]), row, 0.0)
-        products = head_products(part_refs[2 * k][...], w_ref, local)
+        rest = head_products(part_refs[3 * k + 1][...], w_ref, local, heads // 2)
+        products = jnp.concatenate([part_refs[3 * k][...], rest], axis=0)
         parts.append((products, jnp.sum(kept, axis=1, keepdims=True)))
     values[...] = merged(parts)[0]
     for p in range(local):
@@ -470,7 +490,8 @@
     )(names, limits, *keeping, moved)
     keep, pieces = keep_and_pieces[:others], keep_and_pieces[others:]
     sums = chip_merge(keep, [lax.ppermute(g, "seq", pairs(0, 1)) for g in give])
-    parts = [lax.ppermute(s, "seq", back(1 + i // 2, 0)) for i, s in enumerate(sums)]
+    parts = [lax.ppermute(s, "seq", back(1 + i // 3, 0)) for i, s in enumerate(sums)]
+    parts[::3] = [half_products(part, w_uv, local) for part in parts[::3]]
     other = [lax.ppermute(piece, "seq", pairs(0, 1)) for piece in pieces]
 
     moved, _ = lax.optimization_barrier((moved, sums[0]))
@@ -489,7 +510,7 @@
     head_values = pl.pallas_call(
         functools.partial(final_kernel, others),
         out_shape=shape((local, heads, reach)),
-        in_specs=[VMEM] * (2 * chips + 1),
+        in_specs=[VMEM] * (3 * others + 3),
         out_specs=VMEM,
         scratch_shapes=[pltpu.VMEM((rows, reach), F32)],
         compiler_params=PARAMS,

time: 38.1 us -> 37.9 us (level)
  waiting for transfers between devices: 4.92 us -> 3.1 us
  starting transfers between devices: 18.4 us -> 19.9 us
    ppermute x2 -> x3, waiting for transfers between devices: 2.15 us -> 0.32 us  [on_device(): lax.ppermute(s, 'seq', back(1 + i // 3, 0))]
    ppermute x2 -> x3, starting transfers between devices: 2.09 us -> 3.58 us  [on_device(): lax.ppermute(s, 'seq', back(1 + i // 3, 0))]
    pallas_call x1 -> x2, Pallas kernels: 0.17 us -> 0.57 us  [the longest x1 0.39 us: half_products(): pl.pallas_call(functools.partial(half_kernel, local), out_shape=shape((pa...]
  transfers between devices with their start and end apart: 13 -> 14, of which waited for: 3 -> 3; matrix products, arithmetic and copies ran while one was open for 0% -> 0% of each run, Pallas kernels for 26% -> 28%
where the time goes in v26:
time: 37.9 us; the launch traced here: 37.7 us
  starting transfers between devices  19.9 us (53%)
  Pallas kernels  12.3 us (32%)
  waiting for transfers between devices  3.1 us (8%)
  local copies, waits for them, and re-layouts  1.47 us (4%)
  between operations  0.91 us (2%)
    ppermute x1, starting transfers between devices, on_device(): middle = lax.ppermute(block, 'dom', [(0, 2), (3, 1)])  7.63 us
    pallas_call x2, Pallas kernels, prefix_attention(): pl.pallas_call(functools.partial(prefix_kernel, len(queries), tiles), out...  6.57 us
    ppermute x3, starting transfers between devices, on_device(): lax.ppermute(s, 'seq', back(1 + i // 3, 0))  3.58 us
    ppermute x1, starting transfers between devices, on_device(): late = lax.ppermute(chosen, 'dom', swap)  3.58 us
    ppermute x1, waiting for transfers between devices, on_device(): late = lax.ppermute(chosen, 'dom', swap)  2.57 us
    ppermute x3, starting transfers between devices, on_device(): lax.ppermute(own, 'seq', pairs(*r))  2.17 us
    pallas_call x1, Pallas kernels, on_device(): pl.pallas_call(near_kernel, out_shape=[shape(private_caches.shape), shape...  1.55 us
    unnamed x20, local copies, waits for them, and re-layouts  1.42 us
  transfers between devices with their start and end apart: 14, of which 3 were waited for; matrix products, arithmetic and copies ran while one was open for 0% of the time, Pallas kernels for 28%

profile of v26, /device:TPU:0, one launch (start us, length us, event | category | flops | bytes accessed | tf_op | source)
XLA Modules:
  0.0 37.7 jit_solution(4118381772410918501)
XLA Ops:
  0.6 0.8 %collective-permute-start.5 = (bf16[4,64,576]{2,1,0:T(8,128)(2,1)}, bf16[4,64,576]{2,1,0:T(8,128)(2,1)S(1)}, u32[]{:S(2)}, u32[]{:S(2)}) collective-permute-start(bf16[4,64,576]{2,1,0:T(8,128)(2,1)} %cache_ref.1), channel_id=1, source_target_pairs={{1,2},{2,1},{5,6},{6,5},{9,10},{10,9},{13,14},{14,13},{17,18},{18,... | collective-permute-start | bytes 884744 | tf_op jit(solution)/shard_map/ppermute | solution.py:424
  1.5 1.4 %copy-done.3 = bf16[4,64,576]{2,1,0:T(8,128)(2,1)S(1)} copy-done((bf16[4,64,576]{2,1,0:T(8,128)(2,1)S(1)}, bf16[4,64,576]{2,1,0:T(8,128)(2,1)}, u32[]{:S(2)}) %copy-start.3) | copy-done | bytes 294936
  2.9 7.6 %collective-permute-start.4 = (bf16[128,1152]{1,0:T(8,128)(2,1)S(1)}, bf16[128,1152]{1,0:T(8,128)(2,1)S(1)}, u32[]{:S(2)}, u32[]{:S(2)}) collective-permute-start(bf16[128,1152]{1,0:T(8,128)(2,1)S(1)} %pack.1.refs_0_), channel_id=1, source_target_pairs={{0,2},{3,1},{4,6},{7,5},{8,10},{11,9},{12,14},{15,13},{16,18},{19,... | collective-permute-start | bytes 884744 | tf_op jit(solution)/shard_map/ppermute | solution.py:423
  10.7 0.6 %project.1.refs_0_ = bf16[128,576]{1,0:T(8,128)(2,1)S(1)} custom-call(bf16[128,128]{1,0:T(8,128)(2,1)S(1)} %bitcast.13, bf16[128,64]{1,0:T(8,128)(2,1)S(1)} %bitcast.14, bf16[32,128,512]{2,1,0:T(8,128)(2,1)S(1)} %copy-done.2), custom_call_target="tpu_custom_call" | custom-call | flops 8000000000 | tf_op jit(solution)/shard_map/project/pallas_call | solution.py:432
  11.4 1.6 %collective-permute-start.1 = (bf16[128,576]{1,0:T(8,128)(2,1)S(1)}, bf16[128,576]{1,0:T(8,128)(2,1)S(1)}, u32[]{:S(2)}, u32[]{:S(2)}) collective-permute-start(bf16[128,576]{1,0:T(8,128)(2,1)S(1)} %project.1.refs_0_), channel_id=1, source_target_pairs={{0,12},{4,8},{8,4},{12,0},{1,13},{5,9},{9,5},{13,1},{2,14},{6,10},... | collective-permute-start | bytes 442376 | tf_op jit(solution)/shard_map/ppermute | solution.py:454
  13.0 0.5 %collective-permute-start = (bf16[128,576]{1,0:T(8,128)(2,1)S(1)}, bf16[128,576]{1,0:T(8,128)(2,1)S(1)}, u32[]{:S(2)}, u32[]{:S(2)}) collective-permute-start(bf16[128,576]{1,0:T(8,128)(2,1)S(1)} %project.1.refs_0_), channel_id=1, source_target_pairs={{0,8},{4,12},{8,0},{12,4},{1,9},{5,13},{9,1},{13,5},{2,10},{6,14},... | collective-permute-start | bytes 442376 | tf_op jit(solution)/shard_map/ppermute | solution.py:454
  13.5 1.4 %collective-permute-start.6 = (s32[1,128]{1,0:T(1,128)S(1)}, s32[1,128]{1,0:T(1,128)S(1)}, u32[]{:S(2)}, u32[]{:S(2)}) collective-permute-start(s32[1,128]{1,0:T(1,128)S(1)} %pad_bitcast_fusion.1.names_ref), channel_id=1, source_target_pairs={{0,1},{3,2},{4,5},{7,6},{8,9},{11,10},{12,13},{15,14},{16,17},{19,... | collective-permute-start | bytes 1544 | tf_op jit(solution)/shard_map/ppermute | solution.py:425
  14.9 3.3 %prefix_attention.3 = (f32[128,512]{1,0:T(8,128)S(1)}, f32[128,128]{1,0:T(8,128)S(1)}, f32[128,128]{1,0:T(8,128)S(1)}, bf16[128,640]{1,0:T(8,128)(2,1)S(1)}) custom-call(bf16[128,576]{1,0:T(8,128)(2,1)S(1)} %project.1.refs_0_, bf16[128,576]{1,0:T(8,128)(2,1)S(1)} %collective-permute-done.2.refs_1_, bf16[576,4096]{1,0:T(8,128)(2,1)S(1)} %bitcast.11), custom_call_target="tpu_custom_call" | custom-call | tf_op jit(solution)/shard_map/prefix_attention/pallas_call | solution.py:115
  18.3 0.2 gather.3
  18.5 3.6 %collective-permute-start.7 = (bf16[128,1152]{1,0:T(8,128)(2,1)S(1)}, bf16[128,1152]{1,0:T(8,128)(2,1)S(1)}, u32[]{:S(2)}, u32[]{:S(2)}) collective-permute-start(bf16[128,1152]{1,0:T(8,128)(2,1)S(1)} %gather.3), channel_id=1, source_target_pairs={{0,1},{1,0},{2,3},{3,2},{4,5},{5,4},{6,7},{7,6},{8,9},{9,8},{10,11... | collective-permute-start | bytes 884744 | tf_op jit(solution)/shard_map/ppermute | solution.py:464
  22.1 3.3 %prefix_attention.2 = (f32[256,512]{1,0:T(8,128)S(1)}, f32[256,128]{1,0:T(8,128)S(1)}, f32[256,128]{1,0:T(8,128)S(1)}) custom-call(bf16[128,576]{1,0:T(8,128)(2,1)S(1)} %collective-permute-done.refs_0_, bf16[128,576]{1,0:T(8,128)(2,1)S(1)} %collective-permute-done.1.refs_1_.refs_0_, bf16[576,4096]{1,0:T(8,128)(2,1)S(1)} %bitcast.12), custom_call_target="tpu_custom_call" | custom-call | flops 2281701376 | bytes 4718592 | tf_op jit(solution)/shard_map/prefix_attention/pallas_call | solution.py:115
  25.4 0.2 gather.2.refs_4_
  25.7 2.6 %collective-permute-done.7.refs_5_ = bf16[128,1152]{1,0:T(8,128)(2,1)S(1)} collective-permute-done((bf16[128,1152]{1,0:T(8,128)(2,1)S(1)}, bf16[128,1152]{1,0:T(8,128)(2,1)S(1)}, u32[]{:S(2)}, u32[]{:S(2)}) %collective-permute-start.7) | collective-permute-done | bytes 294944 | tf_op jit(solution)/shard_map/ppermute | solution.py:464
  28.2 0.9 %suffix_give.1 = (bf16[256,576]{1,0:T(8,128)(2,1)S(1)}, bf16[128,640]{1,0:T(8,128)(2,1)S(1)}) custom-call(s32[1,128]{1,0:T(1,128)S(1)} %pad_bitcast_fusion.1.names_ref, s32[1,128]{1,0:T(1,128)S(1)} %pad_bitcast_fusion.lens_ref, bf16[128,576]{1,0:T(8,128)(2,1)S(1)} %collective-permute-done.1.refs_1_.refs_0_, f32[256,512]{1,0:T(8,128)S(1)} %get-tuple-element.23.refs_1_, ...), custom_call_target="tpu_custom_call" | custom-call | tf_op jit(solution)/shard_map/suffix_give/pallas_call | solution.py:474
  29.2 0.6 %suffix_keep.1 = (bf16[128,640]{1,0:T(8,128)(2,1)S(1)}, bf16[128,576]{1,0:T(8,128)(2,1)S(1)}, bf16[128,576]{1,0:T(8,128)(2,1)S(1)}) custom-call(s32[1,128]{1,0:T(1,128)S(1)} %pad_bitcast_fusion.1.names_ref, s32[1,128]{1,0:T(1,128)S(1)} %pad_bitcast_fusion.lens_ref, bf16[128,576]{1,0:T(8,128)(2,1)S(1)} %collective-permute-done.refs_0_, ...), custom_call_target="tpu_custom_call" | custom-call | tf_op jit(solution)/shard_map/suffix_keep/pallas_call | solution.py:483
  29.8 0.6 %collective-permute-start.12 = (bf16[128,576]{1,0:T(8,128)(2,1)S(1)}, bf16[128,576]{1,0:T(8,128)(2,1)S(1)}, u32[]{:S(2)}, u32[]{:S(2)}) collective-permute-start(bf16[128,576]{1,0:T(8,128)(2,1)S(1)} %get-tuple-element.39), channel_id=1, source_target_pairs={{0,4},{4,0},{8,12},{12,8},{1,5},{5,1},{9,13},{13,9},{2,6},{6,2},{1... | collective-permute-start | bytes 442376 | tf_op jit(solution)/shard_map/ppermute | solution.py:495
  30.4 0.2 collective-permute-done.8.refs_1_
  30.8 1.6 %collective-permute-start.9 = (bf16[64,512]{1,0:T(8,128)(2,1)S(1)}, bf16[64,512]{1,0:T(8,128)(2,1)S(1)}, u32[]{:S(2)}, u32[]{:S(2)}) collective-permute-start(bf16[64,512]{1,0:T(8,128)(2,1)S(1)} %get-tuple-element.32), channel_id=1, source_target_pairs={{8,0},{12,4},{0,8},{4,12},{9,1},{13,5},{1,9},{5,13},{10,2},{14,6},... | collective-permute-start | bytes 196616 | tf_op jit(solution)/shard_map/ppermute | solution.py:493
  32.4 0.5 %collective-permute-start.10 = (bf16[64,512]{1,0:T(8,128)(2,1)S(1)}, bf16[64,512]{1,0:T(8,128)(2,1)S(1)}, u32[]{:S(2)}, u32[]{:S(2)}) collective-permute-start(bf16[64,512]{1,0:T(8,128)(2,1)S(1)} %get-tuple-element.33), channel_id=1, source_target_pairs={{8,0},{12,4},{0,8},{4,12},{9,1},{13,5},{1,9},{5,13},{10,2},{14,6},... | collective-permute-start | bytes 196616 | tf_op jit(solution)/shard_map/ppermute | solution.py:493
  32.9 1.5 %collective-permute-start.11 = (f32[8,128]{1,0:T(8,128)S(1)}, f32[8,128]{1,0:T(8,128)S(1)}, u32[]{:S(2)}, u32[]{:S(2)}) collective-permute-start(f32[8,128]{1,0:T(8,128)S(1)} %get-tuple-element.34), channel_id=1, source_target_pairs={{8,0},{12,4},{0,8},{4,12},{9,1},{13,5},{1,9},{5,13},{10,2},{14,6},... | collective-permute-start | bytes 12296 | tf_op jit(solution)/shard_map/ppermute | solution.py:493
  34.4 1.5 %suffix_near.1 = (bf16[4,64,576]{2,1,0:T(8,128)(2,1)}, f32[128,128]{1,0:T(8,128)S(1)}, f32[128,128]{1,0:T(8,128)S(1)}) custom-call(s32[1,128]{1,0:T(1,128)S(1)} %pad_bitcast_fusion.1.names_ref, s32[1,128]{1,0:T(1,128)S(1)} %pad_bitcast_fusion.lens_ref, bf16[4,576]{1,0:T(4,128)(2,1)S(1)} %copy-done.1, bf16[32,512,128]{2,1,0:T(8,128)(2,1)S(1)} %copy-done, ...), custom_call_target="tpu_custom_call" | custom-call | tf_op jit(solution)/shard_map/suffix_near/pallas_call | solution.py:499
  36.0 0.4 %half.1.refs_0_ = f32[64,128]{1,0:T(8,128)S(1)} custom-call(bf16[64,512]{1,0:T(8,128)(2,1)S(1)} %collective-permute-done.9.part_ref, bf16[32,512,128]{2,1,0:T(8,128)(2,1)S(1)} %copy-done), custom_call_target="tpu_custom_call" | custom-call | tf_op jit(solution)/shard_map/half/pallas_call | solution.py:373
  36.4 0.3 collective-permute-done.11.refs_2_
  36.7 1.0 %final.1 = bf16[4,32,128]{2,1,0:T(8,128)(2,1)} custom-call(f32[64,128]{1,0:T(8,128)S(1)} %half.1.refs_0_, bf16[64,512]{1,0:T(8,128)(2,1)S(1)} %collective-permute-done.10.refs_1_, f32[8,128]{1,0:T(8,128)S(1)} %collective-permute-done.11.refs_2_, f32[128,128]{1,0:T(8,128)S(1)} %get-tuple-element.41.refs_3_, f32[128,128]{1,0:T(8,128)S(1)} %get-tuple-element.42.refs_4_, ...), custom_call_target="tpu_custom_call" | custom-call | tf_op jit(solution)/shard_map/final/pallas_call | solution.py:510
  (41 shorter events, 0.6 us)
Async XLA Ops:
  0.6 10.0 %copy-start.2 = (bf16[32,128,512]{2,1,0:T(8,128)(2,1)S(1)}, bf16[32,128,512]{2,1,0:T(8,128)(2,1)}, u32[]{:S(2)}) copy-start(bf16[32,128,512]{2,1,0:T(8,128)(2,1)} %w_ref.3) | copy-start | bytes 12582916
  0.6 17.6 %collective-permute-start.5 = (bf16[4,64,576]{2,1,0:T(8,128)(2,1)}, bf16[4,64,576]{2,1,0:T(8,128)(2,1)S(1)}, u32[]{:S(2)}, u32[]{:S(2)}) collective-permute-start(bf16[4,64,576]{2,1,0:T(8,128)(2,1)} %cache_ref.1), channel_id=1, source_target_pairs={{1,2},{2,1},{5,6},{6,5},{9,10},{10,9},{13,14},{14,13},{17,18},{18,... | collective-permute-start | bytes 884744 | tf_op jit(solution)/shard_map/ppermute | solution.py:424
  1.5 1.4 %copy-start.3 = (bf16[4,64,576]{2,1,0:T(8,128)(2,1)S(1)}, bf16[4,64,576]{2,1,0:T(8,128)(2,1)}, u32[]{:S(2)}) copy-start(bf16[4,64,576]{2,1,0:T(8,128)(2,1)} %cache_ref.1) | copy-start | bytes 884740
  2.8 7.7 %copy-start.4 = (bf16[4,32,128]{2,1,0:T(8,128)(2,1)S(1)}, bf16[4,32,128]{2,1,0:T(8,128)(2,1)}, u32[]{:S(2)}) copy-start(bf16[4,32,128]{2,1,0:T(8,128)(2,1)} %param.9) | copy-start | bytes 98308
  2.8 7.8 %copy-start.5 = (bf16[4,32,64]{2,1,0:T(8,128)(2,1)S(1)}, bf16[4,32,64]{2,1,0:T(8,128)(2,1)}, u32[]{:S(2)}) copy-start(bf16[4,32,64]{2,1,0:T(8,128)(2,1)} %param.10) | copy-start | bytes 49156
  2.8 12.1 %slice-start = ((s8[4718592]{0:T(1024)(128)(4,1)}), s8[4194304]{0:T(1024)(128)(4,1)S(1)}, s32[]{:S(2)}) async-start(s8[4718592]{0:T(1024)(128)(4,1)} %bitcast.9), calls=%async_computation | async-start | bytes 8388608
  2.9 15.3 %collective-permute-start.4 = (bf16[128,1152]{1,0:T(8,128)(2,1)S(1)}, bf16[128,1152]{1,0:T(8,128)(2,1)S(1)}, u32[]{:S(2)}, u32[]{:S(2)}) collective-permute-start(bf16[128,1152]{1,0:T(8,128)(2,1)S(1)} %pack.1.refs_0_), channel_id=1, source_target_pairs={{0,2},{3,1},{4,6},{7,5},{8,10},{11,9},{12,14},{15,13},{16,18},{19,... | collective-permute-start | bytes 884744 | tf_op jit(solution)/shard_map/ppermute | solution.py:423
  10.6 4.3 %slice-start.1 = ((s8[4718592]{0:T(1024)(128)(4,1)}), s8[524288]{0:T(1024)(128)(4,1)S(1)}, s32[]{:S(2)}) async-start(s8[4718592]{0:T(1024)(128)(4,1)} %bitcast.9), calls=%async_computation.1 | async-start | bytes 1048576
  10.7 2.8 %copy-start.6 = (s32[4]{0:T(128)S(1)}, s32[4]{0:T(128)}, u32[]{:S(2)}) copy-start(s32[4]{0:T(128)} %param.16) | copy-start | bytes 52
  11.3 10.8 %copy-start.7 = (s32[16]{0:T(128)S(1)}, s32[16]{0:T(128)}, u32[]{:S(2)}) copy-start(s32[16]{0:T(128)} %param.17) | copy-start | bytes 196
  11.3 2.2 %collective-permute-start.2 = (bf16[128,576]{1,0:T(8,128)(2,1)S(1)}, bf16[128,576]{1,0:T(8,128)(2,1)S(1)}, u32[]{:S(2)}, u32[]{:S(2)}) collective-permute-start(bf16[128,576]{1,0:T(8,128)(2,1)S(1)} %project.1.refs_0_), channel_id=1, source_target_pairs={{0,4},{4,0},{8,12},{12,8},{1,5},{5,1},{9,13},{13,9},{2,6},{6,2},{1... | collective-permute-start | bytes 442376 | tf_op jit(solution)/shard_map/ppermute | solution.py:454
  11.4 10.8 %collective-permute-start.1 = (bf16[128,576]{1,0:T(8,128)(2,1)S(1)}, bf16[128,576]{1,0:T(8,128)(2,1)S(1)}, u32[]{:S(2)}, u32[]{:S(2)}) collective-permute-start(bf16[128,576]{1,0:T(8,128)(2,1)S(1)} %project.1.refs_0_), channel_id=1, source_target_pairs={{0,12},{4,8},{8,4},{12,0},{1,13},{5,9},{9,5},{13,1},{2,14},{6,10},... | collective-permute-start | bytes 442376 | tf_op jit(solution)/shard_map/ppermute | solution.py:454
  13.0 9.2 %collective-permute-start = (bf16[128,576]{1,0:T(8,128)(2,1)S(1)}, bf16[128,576]{1,0:T(8,128)(2,1)S(1)}, u32[]{:S(2)}, u32[]{:S(2)}) collective-permute-start(bf16[128,576]{1,0:T(8,128)(2,1)S(1)} %project.1.refs_0_), channel_id=1, source_target_pairs={{0,8},{4,12},{8,0},{12,4},{1,9},{5,13},{9,1},{13,5},{2,10},{6,14},... | collective-permute-start | bytes 442376 | tf_op jit(solution)/shard_map/ppermute | solution.py:454
  13.5 4.8 %collective-permute-start.6 = (s32[1,128]{1,0:T(1,128)S(1)}, s32[1,128]{1,0:T(1,128)S(1)}, u32[]{:S(2)}, u32[]{:S(2)}) collective-permute-start(s32[1,128]{1,0:T(1,128)S(1)} %pad_bitcast_fusion.1.names_ref), channel_id=1, source_target_pairs={{0,1},{3,2},{4,5},{7,6},{8,9},{11,10},{12,13},{15,14},{16,17},{19,... | collective-permute-start | bytes 1544 | tf_op jit(solution)/shard_map/ppermute | solution.py:425
  18.5 9.7 %collective-permute-start.7 = (bf16[128,1152]{1,0:T(8,128)(2,1)S(1)}, bf16[128,1152]{1,0:T(8,128)(2,1)S(1)}, u32[]{:S(2)}, u32[]{:S(2)}) collective-permute-start(bf16[128,1152]{1,0:T(8,128)(2,1)S(1)} %gather.3), channel_id=1, source_target_pairs={{0,1},{1,0},{2,3},{3,2},{4,5},{5,4},{6,7},{7,6},{8,9},{9,8},{10,11... | collective-permute-start | bytes 884744 | tf_op jit(solution)/shard_map/ppermute | solution.py:464
  22.1 3.6 %collective-permute-start.3 = (bf16[128,640]{1,0:T(8,128)(2,1)S(1)}, bf16[128,640]{1,0:T(8,128)(2,1)S(1)}, u32[]{:S(2)}, u32[]{:S(2)}) collective-permute-start(bf16[128,640]{1,0:T(8,128)(2,1)S(1)} %get-tuple-element.26), channel_id=1, source_target_pairs={{0,4},{4,0},{8,12},{12,8},{1,5},{5,1},{9,13},{13,9},{2,6},{6,2},{1... | collective-permute-start | bytes 491528 | tf_op jit(solution)/shard_map/ppermute | solution.py:461
  25.4 9.0 %copy-start = (bf16[32,512,128]{2,1,0:T(8,128)(2,1)S(1)}, bf16[32,512,128]{2,1,0:T(8,128)(2,1)}, u32[]{:S(2)}) copy-start(bf16[32,512,128]{2,1,0:T(8,128)(2,1)} %refs_5_.1) | copy-start | bytes 12582916
  25.4 9.0 %copy-start.1 = (bf16[4,576]{1,0:T(4,128)(2,1)S(1)}, bf16[4,576]{1,0:T(4,128)(2,1)}, u32[]{:S(2)}) copy-start(bf16[4,576]{1,0:T(4,128)(2,1)} %fresh_ref.1) | copy-start | bytes 13828
  29.2 1.5 %collective-permute-start.8 = (bf16[128,640]{1,0:T(8,128)(2,1)S(1)}, bf16[128,640]{1,0:T(8,128)(2,1)S(1)}, u32[]{:S(2)}, u32[]{:S(2)}) collective-permute-start(bf16[128,640]{1,0:T(8,128)(2,1)S(1)} %get-tuple-element.31), channel_id=1, source_target_pairs={{0,4},{4,0},{8,12},{12,8},{1,5},{5,1},{9,13},{13,9},{2,6},{6,2},{1... | collective-permute-start | bytes 491528 | tf_op jit(solution)/shard_map/ppermute | solution.py:492
  29.8 4.6 %collective-permute-start.12 = (bf16[128,576]{1,0:T(8,128)(2,1)S(1)}, bf16[128,576]{1,0:T(8,128)(2,1)S(1)}, u32[]{:S(2)}, u32[]{:S(2)}) collective-permute-start(bf16[128,576]{1,0:T(8,128)(2,1)S(1)} %get-tuple-element.39), channel_id=1, source_target_pairs={{0,4},{4,0},{8,12},{12,8},{1,5},{5,1},{9,13},{13,9},{2,6},{6,2},{1... | collective-permute-start | bytes 442376 | tf_op jit(solution)/shard_map/ppermute | solution.py:495
  30.4 4.0 %collective-permute-start.13 = (bf16[128,576]{1,0:T(8,128)(2,1)S(1)}, bf16[128,576]{1,0:T(8,128)(2,1)S(1)}, u32[]{:S(2)}, u32[]{:S(2)}) collective-permute-start(bf16[128,576]{1,0:T(8,128)(2,1)S(1)} %get-tuple-element.40), channel_id=1, source_target_pairs={{0,4},{4,0},{8,12},{12,8},{1,5},{5,1},{9,13},{13,9},{2,6},{6,2},{1... | collective-permute-start | bytes 442376 | tf_op jit(solution)/shard_map/ppermute | solution.py:495
  30.8 5.2 %collective-permute-start.9 = (bf16[64,512]{1,0:T(8,128)(2,1)S(1)}, bf16[64,512]{1,0:T(8,128)(2,1)S(1)}, u32[]{:S(2)}, u32[]{:S(2)}) collective-permute-start(bf16[64,512]{1,0:T(8,128)(2,1)S(1)} %get-tuple-element.32), channel_id=1, source_target_pairs={{8,0},{12,4},{0,8},{4,12},{9,1},{13,5},{1,9},{5,13},{10,2},{14,6},... | collective-permute-start | bytes 196616 | tf_op jit(solution)/shard_map/ppermute | solution.py:493
  32.4 4.3 %collective-permute-start.10 = (bf16[64,512]{1,0:T(8,128)(2,1)S(1)}, bf16[64,512]{1,0:T(8,128)(2,1)S(1)}, u32[]{:S(2)}, u32[]{:S(2)}) collective-permute-start(bf16[64,512]{1,0:T(8,128)(2,1)S(1)} %get-tuple-element.33), channel_id=1, source_target_pairs={{8,0},{12,4},{0,8},{4,12},{9,1},{13,5},{1,9},{5,13},{10,2},{14,6},... | collective-permute-start | bytes 196616 | tf_op jit(solution)/shard_map/ppermute | solution.py:493
  32.9 3.8 %collective-permute-start.11 = (f32[8,128]{1,0:T(8,128)S(1)}, f32[8,128]{1,0:T(8,128)S(1)}, u32[]{:S(2)}, u32[]{:S(2)}) collective-permute-start(f32[8,128]{1,0:T(8,128)S(1)} %get-tuple-element.34), channel_id=1, source_target_pairs={{8,0},{12,4},{0,8},{4,12},{9,1},{13,5},{1,9},{5,13},{10,2},{14,6},... | collective-permute-start | bytes 12296 | tf_op jit(solution)/shard_map/ppermute | solution.py:493

commit v27 on v26

--- a/solution.py
+++ b/solution.py
@@ -354,10 +354,11 @@
 
 def chip_merge(keep, got):
     rows, rank = keep[0].shape[0], keep[0].shape[1] - LANES
-    half = shape((rows // 2, rank))
+    cut = rows * 3 // 64 * 16
+    halves = [shape((cut, rank)), shape((rows - cut, rank))]
     return pl.pallas_call(
         functools.partial(chip_kernel, len(keep)),
-        out_shape=[half, half, shape((8, max(rows, LANES)), F32)] * len(keep),
+        out_shape=[*halves, shape((8, max(rows, LANES)), F32)] * len(keep),
         in_specs=[VMEM] * (2 * len(keep)),
         out_specs=[VMEM] * (3 * len(keep)),
         compiler_params=PARAMS,
@@ -389,7 +390,8 @@
     for k in range(count):
         row = part_refs[3 * k + 2][0:1]
         kept = jnp.where(diagonal(value_ref.shape[0], row.shape[1]), row, 0.0)
-        rest = head_products(part_refs[3 * k + 1][...], w_ref, local, heads // 2)
+        done = part_refs[3 * k].shape[0] // local
+        rest = head_products(part_refs[3 * k + 1][...], w_ref, local, done)
         products = jnp.concatenate([part_refs[3 * k][...], rest], axis=0)
         parts.append((products, jnp.sum(kept, axis=1, keepdims=True)))
     values[...] = merged(parts)[0]

time: 37.9 us -> 37.8 us (level)
  no operation moved by 1% of the time
where the time goes in v27:
time: 37.8 us; the launch traced here: 37.6 us
  starting transfers between devices  19.9 us (53%)
  Pallas kernels  12.3 us (33%)
  waiting for transfers between devices  3.04 us (8%)
  local copies, waits for them, and re-layouts  1.47 us (4%)
  between operations  0.91 us (2%)
    ppermute x1, starting transfers between devices, on_device(): middle = lax.ppermute(block, 'dom', [(0, 2), (3, 1)])  7.63 us
    pallas_call x2, Pallas kernels, prefix_attention(): pl.pallas_call(functools.partial(prefix_kernel, len(queries), tiles), out...  6.57 us
    ppermute x3, starting transfers between devices, on_device(): lax.ppermute(s, 'seq', back(1 + i // 3, 0))  3.58 us
    ppermute x1, starting transfers between devices, on_device(): late = lax.ppermute(chosen, 'dom', swap)  3.58 us
    ppermute x1, waiting for transfers between devices, on_device(): late = lax.ppermute(chosen, 'dom', swap)  2.57 us
    ppermute x3, starting transfers between devices, on_device(): lax.ppermute(own, 'seq', pairs(*r))  2.17 us
    pallas_call x1, Pallas kernels, on_device(): pl.pallas_call(near_kernel, out_shape=[shape(private_caches.shape), shape...  1.55 us
    unnamed x20, local copies, waits for them, and re-layouts  1.42 us
  transfers between devices with their start and end apart: 14, of which 3 were waited for; matrix products, arithmetic and copies ran while one was open for 0% of the time, Pallas kernels for 28%

profile of v27, /device:TPU:0, one launch (start us, length us, event | category | flops | bytes accessed | tf_op | source)
XLA Modules:
  0.0 37.6 jit_solution(17741228131442020776)
XLA Ops:
  0.6 0.8 %collective-permute-start.5 = (bf16[4,64,576]{2,1,0:T(8,128)(2,1)}, bf16[4,64,576]{2,1,0:T(8,128)(2,1)S(1)}, u32[]{:S(2)}, u32[]{:S(2)}) collective-permute-start(bf16[4,64,576]{2,1,0:T(8,128)(2,1)} %cache_ref.1), channel_id=1, source_target_pairs={{1,2},{2,1},{5,6},{6,5},{9,10},{10,9},{13,14},{14,13},{17,18},{18,... | collective-permute-start | bytes 884744 | tf_op jit(solution)/shard_map/ppermute | solution.py:426
  1.5 1.4 %copy-done.3 = bf16[4,64,576]{2,1,0:T(8,128)(2,1)S(1)} copy-done((bf16[4,64,576]{2,1,0:T(8,128)(2,1)S(1)}, bf16[4,64,576]{2,1,0:T(8,128)(2,1)}, u32[]{:S(2)}) %copy-start.3) | copy-done | bytes 294936
  2.9 7.6 %collective-permute-start.4 = (bf16[128,1152]{1,0:T(8,128)(2,1)S(1)}, bf16[128,1152]{1,0:T(8,128)(2,1)S(1)}, u32[]{:S(2)}, u32[]{:S(2)}) collective-permute-start(bf16[128,1152]{1,0:T(8,128)(2,1)S(1)} %pack.1.refs_0_), channel_id=1, source_target_pairs={{0,2},{3,1},{4,6},{7,5},{8,10},{11,9},{12,14},{15,13},{16,18},{19,... | collective-permute-start | bytes 884744 | tf_op jit(solution)/shard_map/ppermute | solution.py:425
  10.7 0.6 %project.1.refs_0_ = bf16[128,576]{1,0:T(8,128)(2,1)S(1)} custom-call(bf16[128,128]{1,0:T(8,128)(2,1)S(1)} %bitcast.13, bf16[128,64]{1,0:T(8,128)(2,1)S(1)} %bitcast.14, bf16[32,128,512]{2,1,0:T(8,128)(2,1)S(1)} %copy-done.2), custom_call_target="tpu_custom_call" | custom-call | flops 8000000000 | tf_op jit(solution)/shard_map/project/pallas_call | solution.py:434
  11.4 1.6 %collective-permute-start.1 = (bf16[128,576]{1,0:T(8,128)(2,1)S(1)}, bf16[128,576]{1,0:T(8,128)(2,1)S(1)}, u32[]{:S(2)}, u32[]{:S(2)}) collective-permute-start(bf16[128,576]{1,0:T(8,128)(2,1)S(1)} %project.1.refs_0_), channel_id=1, source_target_pairs={{0,12},{4,8},{8,4},{12,0},{1,13},{5,9},{9,5},{13,1},{2,14},{6,10},... | collective-permute-start | bytes 442376 | tf_op jit(solution)/shard_map/ppermute | solution.py:456
  13.0 0.5 %collective-permute-start = (bf16[128,576]{1,0:T(8,128)(2,1)S(1)}, bf16[128,576]{1,0:T(8,128)(2,1)S(1)}, u32[]{:S(2)}, u32[]{:S(2)}) collective-permute-start(bf16[128,576]{1,0:T(8,128)(2,1)S(1)} %project.1.refs_0_), channel_id=1, source_target_pairs={{0,8},{4,12},{8,0},{12,4},{1,9},{5,13},{9,1},{13,5},{2,10},{6,14},... | collective-permute-start | bytes 442376 | tf_op jit(solution)/shard_map/ppermute | solution.py:456
  13.5 1.4 %collective-permute-start.6 = (s32[1,128]{1,0:T(1,128)S(1)}, s32[1,128]{1,0:T(1,128)S(1)}, u32[]{:S(2)}, u32[]{:S(2)}) collective-permute-start(s32[1,128]{1,0:T(1,128)S(1)} %pad_bitcast_fusion.1.names_ref), channel_id=1, source_target_pairs={{0,1},{3,2},{4,5},{7,6},{8,9},{11,10},{12,13},{15,14},{16,17},{19,... | collective-permute-start | bytes 1544 | tf_op jit(solution)/shard_map/ppermute | solution.py:427
  14.9 3.3 %prefix_attention.3 = (f32[128,512]{1,0:T(8,128)S(1)}, f32[128,128]{1,0:T(8,128)S(1)}, f32[128,128]{1,0:T(8,128)S(1)}, bf16[128,640]{1,0:T(8,128)(2,1)S(1)}) custom-call(bf16[128,576]{1,0:T(8,128)(2,1)S(1)} %project.1.refs_0_, bf16[128,576]{1,0:T(8,128)(2,1)S(1)} %collective-permute-done.2.refs_1_, bf16[576,4096]{1,0:T(8,128)(2,1)S(1)} %bitcast.11), custom_call_target="tpu_custom_call" | custom-call | tf_op jit(solution)/shard_map/prefix_attention/pallas_call | solution.py:115
  18.3 0.2 gather.3
  18.5 3.6 %collective-permute-start.7 = (bf16[128,1152]{1,0:T(8,128)(2,1)S(1)}, bf16[128,1152]{1,0:T(8,128)(2,1)S(1)}, u32[]{:S(2)}, u32[]{:S(2)}) collective-permute-start(bf16[128,1152]{1,0:T(8,128)(2,1)S(1)} %gather.3), channel_id=1, source_target_pairs={{0,1},{1,0},{2,3},{3,2},{4,5},{5,4},{6,7},{7,6},{8,9},{9,8},{10,11... | collective-permute-start | bytes 884744 | tf_op jit(solution)/shard_map/ppermute | solution.py:466
  22.1 3.3 %prefix_attention.2 = (f32[256,512]{1,0:T(8,128)S(1)}, f32[256,128]{1,0:T(8,128)S(1)}, f32[256,128]{1,0:T(8,128)S(1)}) custom-call(bf16[128,576]{1,0:T(8,128)(2,1)S(1)} %collective-permute-done.refs_0_, bf16[128,576]{1,0:T(8,128)(2,1)S(1)} %collective-permute-done.1.refs_1_.refs_0_, bf16[576,4096]{1,0:T(8,128)(2,1)S(1)} %bitcast.12), custom_call_target="tpu_custom_call" | custom-call | flops 2281701376 | bytes 4718592 | tf_op jit(solution)/shard_map/prefix_attention/pallas_call | solution.py:115
  25.4 0.2 gather.2.refs_4_
  25.7 2.6 %collective-permute-done.7.refs_5_ = bf16[128,1152]{1,0:T(8,128)(2,1)S(1)} collective-permute-done((bf16[128,1152]{1,0:T(8,128)(2,1)S(1)}, bf16[128,1152]{1,0:T(8,128)(2,1)S(1)}, u32[]{:S(2)}, u32[]{:S(2)}) %collective-permute-start.7) | collective-permute-done | bytes 294944 | tf_op jit(solution)/shard_map/ppermute | solution.py:466
  28.2 0.9 %suffix_give.1 = (bf16[256,576]{1,0:T(8,128)(2,1)S(1)}, bf16[128,640]{1,0:T(8,128)(2,1)S(1)}) custom-call(s32[1,128]{1,0:T(1,128)S(1)} %pad_bitcast_fusion.1.names_ref, s32[1,128]{1,0:T(1,128)S(1)} %pad_bitcast_fusion.lens_ref, bf16[128,576]{1,0:T(8,128)(2,1)S(1)} %collective-permute-done.1.refs_1_.refs_0_, f32[256,512]{1,0:T(8,128)S(1)} %get-tuple-element.23.refs_1_, ...), custom_call_target="tpu_custom_call" | custom-call | tf_op jit(solution)/shard_map/suffix_give/pallas_call | solution.py:476
  29.2 0.6 %suffix_keep.1 = (bf16[128,640]{1,0:T(8,128)(2,1)S(1)}, bf16[128,576]{1,0:T(8,128)(2,1)S(1)}, bf16[128,576]{1,0:T(8,128)(2,1)S(1)}) custom-call(s32[1,128]{1,0:T(1,128)S(1)} %pad_bitcast_fusion.1.names_ref, s32[1,128]{1,0:T(1,128)S(1)} %pad_bitcast_fusion.lens_ref, bf16[128,576]{1,0:T(8,128)(2,1)S(1)} %collective-permute-done.refs_0_, ...), custom_call_target="tpu_custom_call" | custom-call | tf_op jit(solution)/shard_map/suffix_keep/pallas_call | solution.py:485
  29.8 0.6 %collective-permute-start.12 = (bf16[128,576]{1,0:T(8,128)(2,1)S(1)}, bf16[128,576]{1,0:T(8,128)(2,1)S(1)}, u32[]{:S(2)}, u32[]{:S(2)}) collective-permute-start(bf16[128,576]{1,0:T(8,128)(2,1)S(1)} %get-tuple-element.39), channel_id=1, source_target_pairs={{0,4},{4,0},{8,12},{12,8},{1,5},{5,1},{9,13},{13,9},{2,6},{6,2},{1... | collective-permute-start | bytes 442376 | tf_op jit(solution)/shard_map/ppermute | solution.py:497
  30.4 0.2 collective-permute-done.8.refs_1_
  30.8 1.6 %collective-permute-start.9 = (bf16[96,512]{1,0:T(8,128)(2,1)S(1)}, bf16[96,512]{1,0:T(8,128)(2,1)S(1)}, u32[]{:S(2)}, u32[]{:S(2)}) collective-permute-start(bf16[96,512]{1,0:T(8,128)(2,1)S(1)} %get-tuple-element.32), channel_id=1, source_target_pairs={{8,0},{12,4},{0,8},{4,12},{9,1},{13,5},{1,9},{5,13},{10,2},{14,6},... | collective-permute-start | bytes 294920 | tf_op jit(solution)/shard_map/ppermute | solution.py:495
  32.4 0.5 %collective-permute-start.10 = (bf16[32,512]{1,0:T(8,128)(2,1)S(1)}, bf16[32,512]{1,0:T(8,128)(2,1)S(1)}, u32[]{:S(2)}, u32[]{:S(2)}) collective-permute-start(bf16[32,512]{1,0:T(8,128)(2,1)S(1)} %get-tuple-element.33), channel_id=1, source_target_pairs={{8,0},{12,4},{0,8},{4,12},{9,1},{13,5},{1,9},{5,13},{10,2},{14,6},... | collective-permute-start | bytes 98312 | tf_op jit(solution)/shard_map/ppermute | solution.py:495
  32.9 1.5 %collective-permute-start.11 = (f32[8,128]{1,0:T(8,128)S(1)}, f32[8,128]{1,0:T(8,128)S(1)}, u32[]{:S(2)}, u32[]{:S(2)}) collective-permute-start(f32[8,128]{1,0:T(8,128)S(1)} %get-tuple-element.34), channel_id=1, source_target_pairs={{8,0},{12,4},{0,8},{4,12},{9,1},{13,5},{1,9},{5,13},{10,2},{14,6},... | collective-permute-start | bytes 12296 | tf_op jit(solution)/shard_map/ppermute | solution.py:495
  34.4 1.5 %suffix_near.1 = (bf16[4,64,576]{2,1,0:T(8,128)(2,1)}, f32[128,128]{1,0:T(8,128)S(1)}, f32[128,128]{1,0:T(8,128)S(1)}) custom-call(s32[1,128]{1,0:T(1,128)S(1)} %pad_bitcast_fusion.1.names_ref, s32[1,128]{1,0:T(1,128)S(1)} %pad_bitcast_fusion.lens_ref, bf16[4,576]{1,0:T(4,128)(2,1)S(1)} %copy-done.1, bf16[32,512,128]{2,1,0:T(8,128)(2,1)S(1)} %copy-done, ...), custom_call_target="tpu_custom_call" | custom-call | tf_op jit(solution)/shard_map/suffix_near/pallas_call | solution.py:501
  36.0 0.3 collective-permute-done.9.part_ref
  36.2 0.5 %half.1.refs_0_ = f32[96,128]{1,0:T(8,128)S(1)} custom-call(bf16[96,512]{1,0:T(8,128)(2,1)S(1)} %collective-permute-done.9.part_ref, bf16[32,512,128]{2,1,0:T(8,128)(2,1)S(1)} %copy-done), custom_call_target="tpu_custom_call" | custom-call | tf_op jit(solution)/shard_map/half/pallas_call | solution.py:374
  36.7 0.9 %final.1 = bf16[4,32,128]{2,1,0:T(8,128)(2,1)} custom-call(f32[96,128]{1,0:T(8,128)S(1)} %half.1.refs_0_, bf16[32,512]{1,0:T(8,128)(2,1)S(1)} %collective-permute-done.10.refs_1_, f32[8,128]{1,0:T(8,128)S(1)} %collective-permute-done.11.refs_2_, f32[128,128]{1,0:T(8,128)S(1)} %get-tuple-element.41.refs_3_, f32[128,128]{1,0:T(8,128)S(1)} %get-tuple-element.42.refs_4_, ...), custom_call_target="tpu_custom_call" | custom-call | tf_op jit(solution)/shard_map/final/pallas_call | solution.py:512
  (41 shorter events, 0.6 us)
Async XLA Ops:
  0.6 10.0 %copy-start.2 = (bf16[32,128,512]{2,1,0:T(8,128)(2,1)S(1)}, bf16[32,128,512]{2,1,0:T(8,128)(2,1)}, u32[]{:S(2)}) copy-start(bf16[32,128,512]{2,1,0:T(8,128)(2,1)} %w_ref.3) | copy-start | bytes 12582916
  0.6 17.6 %collective-permute-start.5 = (bf16[4,64,576]{2,1,0:T(8,128)(2,1)}, bf16[4,64,576]{2,1,0:T(8,128)(2,1)S(1)}, u32[]{:S(2)}, u32[]{:S(2)}) collective-permute-start(bf16[4,64,576]{2,1,0:T(8,128)(2,1)} %cache_ref.1), channel_id=1, source_target_pairs={{1,2},{2,1},{5,6},{6,5},{9,10},{10,9},{13,14},{14,13},{17,18},{18,... | collective-permute-start | bytes 884744 | tf_op jit(solution)/shard_map/ppermute | solution.py:426
  1.5 1.4 %copy-start.3 = (bf16[4,64,576]{2,1,0:T(8,128)(2,1)S(1)}, bf16[4,64,576]{2,1,0:T(8,128)(2,1)}, u32[]{:S(2)}) copy-start(bf16[4,64,576]{2,1,0:T(8,128)(2,1)} %cache_ref.1) | copy-start | bytes 884740
  2.8 7.7 %copy-start.4 = (bf16[4,32,128]{2,1,0:T(8,128)(2,1)S(1)}, bf16[4,32,128]{2,1,0:T(8,128)(2,1)}, u32[]{:S(2)}) copy-start(bf16[4,32,128]{2,1,0:T(8,128)(2,1)} %param.9) | copy-start | bytes 98308
  2.8 7.8 %copy-start.5 = (bf16[4,32,64]{2,1,0:T(8,128)(2,1)S(1)}, bf16[4,32,64]{2,1,0:T(8,128)(2,1)}, u32[]{:S(2)}) copy-start(bf16[4,32,64]{2,1,0:T(8,128)(2,1)} %param.10) | copy-start | bytes 49156
  2.8 12.1 %slice-start = ((s8[4718592]{0:T(1024)(128)(4,1)}), s8[4194304]{0:T(1024)(128)(4,1)S(1)}, s32[]{:S(2)}) async-start(s8[4718592]{0:T(1024)(128)(4,1)} %bitcast.9), calls=%async_computation | async-start | bytes 8388608
  2.9 15.3 %collective-permute-start.4 = (bf16[128,1152]{1,0:T(8,128)(2,1)S(1)}, bf16[128,1152]{1,0:T(8,128)(2,1)S(1)}, u32[]{:S(2)}, u32[]{:S(2)}) collective-permute-start(bf16[128,1152]{1,0:T(8,128)(2,1)S(1)} %pack.1.refs_0_), channel_id=1, source_target_pairs={{0,2},{3,1},{4,6},{7,5},{8,10},{11,9},{12,14},{15,13},{16,18},{19,... | collective-permute-start | bytes 884744 | tf_op jit(solution)/shard_map/ppermute | solution.py:425
  10.6 4.3 %slice-start.1 = ((s8[4718592]{0:T(1024)(128)(4,1)}), s8[524288]{0:T(1024)(128)(4,1)S(1)}, s32[]{:S(2)}) async-start(s8[4718592]{0:T(1024)(128)(4,1)} %bitcast.9), calls=%async_computation.1 | async-start | bytes 1048576
  10.7 2.8 %copy-start.6 = (s32[4]{0:T(128)S(1)}, s32[4]{0:T(128)}, u32[]{:S(2)}) copy-start(s32[4]{0:T(128)} %param.16) | copy-start | bytes 52
  11.3 10.8 %copy-start.7 = (s32[16]{0:T(128)S(1)}, s32[16]{0:T(128)}, u32[]{:S(2)}) copy-start(s32[16]{0:T(128)} %param.17) | copy-start | bytes 196
  11.3 2.2 %collective-permute-start.2 = (bf16[128,576]{1,0:T(8,128)(2,1)S(1)}, bf16[128,576]{1,0:T(8,128)(2,1)S(1)}, u32[]{:S(2)}, u32[]{:S(2)}) collective-permute-start(bf16[128,576]{1,0:T(8,128)(2,1)S(1)} %project.1.refs_0_), channel_id=1, source_target_pairs={{0,4},{4,0},{8,12},{12,8},{1,5},{5,1},{9,13},{13,9},{2,6},{6,2},{1... | collective-permute-start | bytes 442376 | tf_op jit(solution)/shard_map/ppermute | solution.py:456
  11.4 10.8 %collective-permute-start.1 = (bf16[128,576]{1,0:T(8,128)(2,1)S(1)}, bf16[128,576]{1,0:T(8,128)(2,1)S(1)}, u32[]{:S(2)}, u32[]{:S(2)}) collective-permute-start(bf16[128,576]{1,0:T(8,128)(2,1)S(1)} %project.1.refs_0_), channel_id=1, source_target_pairs={{0,12},{4,8},{8,4},{12,0},{1,13},{5,9},{9,5},{13,1},{2,14},{6,10},... | collective-permute-start | bytes 442376 | tf_op jit(solution)/shard_map/ppermute | solution.py:456
  13.0 9.2 %collective-permute-start = (bf16[128,576]{1,0:T(8,128)(2,1)S(1)}, bf16[128,576]{1,0:T(8,128)(2,1)S(1)}, u32[]{:S(2)}, u32[]{:S(2)}) collective-permute-start(bf16[128,576]{1,0:T(8,128)(2,1)S(1)} %project.1.refs_0_), channel_id=1, source_target_pairs={{0,8},{4,12},{8,0},{12,4},{1,9},{5,13},{9,1},{13,5},{2,10},{6,14},... | collective-permute-start | bytes 442376 | tf_op jit(solution)/shard_map/ppermute | solution.py:456
  13.5 4.8 %collective-permute-start.6 = (s32[1,128]{1,0:T(1,128)S(1)}, s32[1,128]{1,0:T(1,128)S(1)}, u32[]{:S(2)}, u32[]{:S(2)}) collective-permute-start(s32[1,128]{1,0:T(1,128)S(1)} %pad_bitcast_fusion.1.names_ref), channel_id=1, source_target_pairs={{0,1},{3,2},{4,5},{7,6},{8,9},{11,10},{12,13},{15,14},{16,17},{19,... | collective-permute-start | bytes 1544 | tf_op jit(solution)/shard_map/ppermute | solution.py:427
  18.5 9.7 %collective-permute-start.7 = (bf16[128,1152]{1,0:T(8,128)(2,1)S(1)}, bf16[128,1152]{1,0:T(8,128)(2,1)S(1)}, u32[]{:S(2)}, u32[]{:S(2)}) collective-permute-start(bf16[128,1152]{1,0:T(8,128)(2,1)S(1)} %gather.3), channel_id=1, source_target_pairs={{0,1},{1,0},{2,3},{3,2},{4,5},{5,4},{6,7},{7,6},{8,9},{9,8},{10,11... | collective-permute-start | bytes 884744 | tf_op jit(solution)/shard_map/ppermute | solution.py:466
  22.1 3.6 %collective-permute-start.3 = (bf16[128,640]{1,0:T(8,128)(2,1)S(1)}, bf16[128,640]{1,0:T(8,128)(2,1)S(1)}, u32[]{:S(2)}, u32[]{:S(2)}) collective-permute-start(bf16[128,640]{1,0:T(8,128)(2,1)S(1)} %get-tuple-element.26), channel_id=1, source_target_pairs={{0,4},{4,0},{8,12},{12,8},{1,5},{5,1},{9,13},{13,9},{2,6},{6,2},{1... | collective-permute-start | bytes 491528 | tf_op jit(solution)/shard_map/ppermute | solution.py:463
  25.4 9.0 %copy-start = (bf16[32,512,128]{2,1,0:T(8,128)(2,1)S(1)}, bf16[32,512,128]{2,1,0:T(8,128)(2,1)}, u32[]{:S(2)}) copy-start(bf16[32,512,128]{2,1,0:T(8,128)(2,1)} %refs_5_.1) | copy-start | bytes 12582916
  25.4 9.0 %copy-start.1 = (bf16[4,576]{1,0:T(4,128)(2,1)S(1)}, bf16[4,576]{1,0:T(4,128)(2,1)}, u32[]{:S(2)}) copy-start(bf16[4,576]{1,0:T(4,128)(2,1)} %fresh_ref.1) | copy-start | bytes 13828
  29.2 1.5 %collective-permute-start.8 = (bf16[128,640]{1,0:T(8,128)(2,1)S(1)}, bf16[128,640]{1,0:T(8,128)(2,1)S(1)}, u32[]{:S(2)}, u32[]{:S(2)}) collective-permute-start(bf16[128,640]{1,0:T(8,128)(2,1)S(1)} %get-tuple-element.31), channel_id=1, source_target_pairs={{0,4},{4,0},{8,12},{12,8},{1,5},{5,1},{9,13},{13,9},{2,6},{6,2},{1... | collective-permute-start | bytes 491528 | tf_op jit(solution)/shard_map/ppermute | solution.py:494
  29.8 4.6 %collective-permute-start.12 = (bf16[128,576]{1,0:T(8,128)(2,1)S(1)}, bf16[128,576]{1,0:T(8,128)(2,1)S(1)}, u32[]{:S(2)}, u32[]{:S(2)}) collective-permute-start(bf16[128,576]{1,0:T(8,128)(2,1)S(1)} %get-tuple-element.39), channel_id=1, source_target_pairs={{0,4},{4,0},{8,12},{12,8},{1,5},{5,1},{9,13},{13,9},{2,6},{6,2},{1... | collective-permute-start | bytes 442376 | tf_op jit(solution)/shard_map/ppermute | solution.py:497
  30.4 4.0 %collective-permute-start.13 = (bf16[128,576]{1,0:T(8,128)(2,1)S(1)}, bf16[128,576]{1,0:T(8,128)(2,1)S(1)}, u32[]{:S(2)}, u32[]{:S(2)}) collective-permute-start(bf16[128,576]{1,0:T(8,128)(2,1)S(1)} %get-tuple-element.40), channel_id=1, source_target_pairs={{0,4},{4,0},{8,12},{12,8},{1,5},{5,1},{9,13},{13,9},{2,6},{6,2},{1... | collective-permute-start | bytes 442376 | tf_op jit(solution)/shard_map/ppermute | solution.py:497
  30.8 5.4 %collective-permute-start.9 = (bf16[96,512]{1,0:T(8,128)(2,1)S(1)}, bf16[96,512]{1,0:T(8,128)(2,1)S(1)}, u32[]{:S(2)}, u32[]{:S(2)}) collective-permute-start(bf16[96,512]{1,0:T(8,128)(2,1)S(1)} %get-tuple-element.32), channel_id=1, source_target_pairs={{8,0},{12,4},{0,8},{4,12},{9,1},{13,5},{1,9},{5,13},{10,2},{14,6},... | collective-permute-start | bytes 294920 | tf_op jit(solution)/shard_map/ppermute | solution.py:495
  32.4 4.4 %collective-permute-start.10 = (bf16[32,512]{1,0:T(8,128)(2,1)S(1)}, bf16[32,512]{1,0:T(8,128)(2,1)S(1)}, u32[]{:S(2)}, u32[]{:S(2)}) collective-permute-start(bf16[32,512]{1,0:T(8,128)(2,1)S(1)} %get-tuple-element.33), channel_id=1, source_target_pairs={{8,0},{12,4},{0,8},{4,12},{9,1},{13,5},{1,9},{5,13},{10,2},{14,6},... | collective-permute-start | bytes 98312 | tf_op jit(solution)/shard_map/ppermute | solution.py:495
  32.9 3.8 %collective-permute-start.11 = (f32[8,128]{1,0:T(8,128)S(1)}, f32[8,128]{1,0:T(8,128)S(1)}, u32[]{:S(2)}, u32[]{:S(2)}) collective-permute-start(f32[8,128]{1,0:T(8,128)S(1)} %get-tuple-element.34), channel_id=1, source_target_pairs={{8,0},{12,4},{0,8},{4,12},{9,1},{13,5},{1,9},{5,13},{10,2},{14,6},... | collective-permute-start | bytes 12296 | tf_op jit(solution)/shard_map/ppermute | solution.py:495
